TPU v7x, 32 devices: a whole 2x2x4 slice. The times are simulated.
32 devices in a mesh: layer: 4 (over z), row: 2 (over core), col: 4 (over y, x).
Axes of the slice: x: 2, y: 2, z: 4, core: 2. Of those that a mesh axis runs over, the one named last changes fastest.
Arguments:
- lpanel: bfloat16 [4, 8, 3072, 256], P('layer', None, 'row', 'col'), may hold values from -6 to 6
- upanel: bfloat16 [4, 8, 256, 3072], P('layer', None, 'row', 'col'), may hold values from -0.09375 to 0.09375
- lpat: int32 [4, 8, 24], P('layer', None, 'row'), may hold values 0 or 1
- upat: int32 [4, 8, 24], P('layer', None, 'col'), may hold values 0 or 1
- ancestor_entries: float32 [3072, 3072], P('row', 'col'), may hold values from -2 to 64, as said below
Outputs:
- schur: float32 [3072, 3072], P(('row', 'layer'), 'col')
- diag_lu: float32 [24, 128, 128], P('col')
Inputs may be any that keep to these rules, and one draw needn't show every extreme that they name: `ancestor_entries`: entries on the diagonal lie in 32 to 64; all other entries in -2 to 2.
All inputs are finite; a program needn't handle non-finite values. No bound on the sum of `lpat` or of `upat` on one device may be relied on, other than what follows from the above.
Results may differ from a plain program's by a relative error of at most 0.0003.
Values may be sent and summed in bfloat16 or wider, within the bound.
No kernel may reach another device: no remote copies, remote signals or barrier semaphores. Data moves between devices by JAX's collectives and lax.ppermute only.
A program may use at most 64 MiB of HBM per device.

v0:
```python
import jax
import jax.numpy as jnp
from jax import lax
from jax.sharding import PartitionSpec as P

BLK = 128


panel_width = 16


def mask_rows(panel, pattern, block):
    count, length, inner = panel.shape
    shaped = panel.reshape(count, length // block, block, inner)
    return (shaped * pattern[:, :, None, None].astype(panel.dtype)).reshape(count, length, inner)


def mask_cols(panel, pattern, block):
    count, inner, length = panel.shape
    shaped = panel.reshape(count, inner, length // block, block)
    return (shaped * pattern[:, None, :, None].astype(panel.dtype)).reshape(count, inner, length)


def eliminate_tall(tile, steps):
    row_places = jnp.arange(tile.shape[1])
    col_places = jnp.arange(tile.shape[2])

    def eliminate_sweep(step, current):
        pivot = current[:, step, step]
        below = row_places > step
        column = jnp.where(below[None, :], current[:, :, step] / pivot[:, None], 0.0)
        right = col_places > step
        row_part = jnp.where(right[None, :], current[:, step, :], 0.0)
        current = current - column[:, :, None] * row_part[:, None, :]
        placed = below[None, :, None] & (col_places == step)[None, None, :]
        return jnp.where(placed, column[:, :, None], current)

    return lax.fori_loop(0, steps, eliminate_sweep, tile)


def forward_rows(unit, strip):
    places = jnp.arange(unit.shape[1])

    def forward_sweep(step, current):
        factors = jnp.where(places[None, :] > step, unit[:, :, step], 0.0)
        return current - factors[:, :, None] * current[:, step, :][:, None, :]

    return lax.fori_loop(0, unit.shape[1], forward_sweep, strip)


def factor(blocks):
    size = blocks.shape[-1]
    current = blocks
    for offset in range(0, size, panel_width):
        end = offset + panel_width
        panel = eliminate_tall(current[:, offset:, offset:end], panel_width)
        current = current.at[:, offset:, offset:end].set(panel)
        if end < size:
            strip = forward_rows(panel[:, :panel_width, :], current[:, offset:end, end:])
            current = current.at[:, offset:end, end:].set(strip)
            lower = panel[:, panel_width:, :]
            trailing = current[:, end:, end:] - jnp.einsum(
                "bik,bkj->bij",
                lower,
                strip,
                precision=lax.Precision.HIGHEST,
                preferred_element_type=jnp.float32,
            )
            current = current.at[:, end:, end:].set(trailing)
    return current


def candidates(matrix):
    width = matrix.shape[1]
    per_group = lax.axis_size("col") // lax.axis_size("row")
    column = lax.axis_index("col")
    valid = column // per_group == lax.axis_index("row")
    begin = column % per_group * width
    square = lax.dynamic_slice_in_dim(matrix, begin, width, 0)
    count = width // BLK
    blocks = jnp.stack(
        [square[j * BLK : (j + 1) * BLK, j * BLK : (j + 1) * BLK] for j in range(count)]
    )
    return (blocks, valid)


def pick_owned(gathered):
    per_group = lax.axis_size("col") // lax.axis_size("row")
    count = gathered.shape[0] // lax.axis_size("row")
    source = lax.axis_index("col") // per_group
    return lax.dynamic_slice_in_dim(gathered, source * count, count, 0)


def shards(lpanel, upanel, lpat, upat, ancestor_entries):
    left_masked = mask_rows(lpanel[0], lpat[0], BLK)
    right_masked = mask_cols(upanel[0], upat[0], BLK)
    right_full = lax.all_gather(right_masked, "row", axis=1, tiled=True)
    length = left_masked.shape[1]
    update = jnp.einsum(
        "kmw,kwn->mn",
        lax.all_gather(left_masked, "col", axis=2, tiled=True),
        right_full,
        preferred_element_type=jnp.float32,
    )
    share_rows = length // lax.axis_size("layer")
    offset = lax.axis_index("layer") * share_rows
    share = lax.psum_scatter(update, "layer", scatter_dimension=0, tiled=True)
    schur = lax.dynamic_slice_in_dim(ancestor_entries, offset, share_rows, 0) - share
    partial_blocks, valid = candidates(update)
    start_blocks, valid = candidates(ancestor_entries)
    pivots = start_blocks - lax.psum(partial_blocks, "layer")
    diag_lu = factor(pick_owned(lax.all_gather(pivots, "row", axis=0, tiled=True)))
    return (schur, diag_lu)


def solution(mesh):
    return jax.shard_map(
        shards,
        mesh=mesh,
        in_specs=(
            P("layer", None, "row", "col"),
            P("layer", None, "row", "col"),
            P("layer", None, "row"),
            P("layer", None, "col"),
            P("row", "col"),
        ),
        out_specs=(P(("row", "layer"), "col"), P("col", None, None)),
        check_vma=False,
    )
```

profile of v0, /device:TPU:2, one launch (start us, length us, event | category | flops | bytes accessed | tf_op | source)
XLA Modules:
  0.0 350.4 jit_solution(10777362637922583301)
XLA Ops:
  7.2 0.9 copy.122
  8.3 2.7 bitcast_multiply_fusion
  11.2 1.4 bitcast_multiply_fusion.1
  16.0 8.7 %all-gather.5.cloned.1.call-done = bf16[8,256,768]{2,1,0:T(8,128)(2,1)} async-done(((bf16[8,128,768]{2,1,0:T(8,128)(2,1)}), bf16[8,256,768]{2,1,0:T(8,128)(2,1)}) %all-gather.5.cloned.1.call-update) | async-done | bytes 3145744 | tf_op jit(solution)/shard_map/all_gather | solution.py:97
  24.7 72.9 %all-gather.3.cloned.1.call-done = bf16[8,1536,256]{1,2,0:T(8,128)(2,1)} async-done(((bf16[8,1536,64]{1,2,0:T(8,128)(2,1)}), bf16[8,1536,256]{1,2,0:T(8,128)(2,1)}) %all-gather.3.cloned.1.call-update) | async-done | bytes 6291472 | tf_op jit(solution)/shard_map/all_gather | solution.py:101
  97.7 9.7 %convolution_bitcast_fusion = f32[1536,768]{1,0:T(8,128)} fusion(bf16[8,1536,256]{1,2,0:T(8,128)(2,1)} %all-gather.3.cloned.1.call-done, bf16[8,256,768]{2,1,0:T(8,128)(2,1)} %all-gather.5.cloned.1.call-done), kind=kOutput, calls=%fused_computation.119 | convolution fusion | flops 4831838208 | bytes 14155776 | tf_op jit(solution)/shard_map/kmw,kwn->mn/dot_general | solution.py:99
  116.5 33.8 %all-reduce.2.cloned.1.call-done = f32[6,128,128]{2,1,0:T(8,128)} async-done(((f32[6,128,128]{2,1,0:T(8,128)}), f32[6,128,128]{2,1,0:T(8,128)}) %all-reduce.2.cloned.1.call-update) | async-done | bytes 393232 | tf_op jit(solution)/shard_map/psum | solution.py:111
  150.2 1.0 sub.138
  151.3 2.5 all_gather.11
  154.0 13.2 %while.248 = (s32[]{:T(128)}, f32[6,128,16]{1,0,2:T(8,128)S(1)}, s32[]{:T(128)}) while((s32[]{:T(128)}, f32[6,128,16]{1,0,2:T(8,128)S(1)}, s32[]{:T(128)}) %tuple.580), condition=%wide.region_3.4_spmd.clone.clone, body=%wide.region_2.3_spmd.clone.clone.sunk | while | flops 40706 | bytes 212433 | solution.py:38
  167.4 2.6 while.241
  170.1 2.0 dynamic-slice_select_fusion
  172.1 6.4 %scatter.75 = f32[6,128,128]{1,2,0:T(8,128)S(1)} dynamic-update-slice(f32[6,128,128]{1,2,0:T(8,128)S(1)} %get-tuple-element.1863, f32[6,16,112]{1,2,0:T(8,128)S(1)} %dynamic-slice_select_fusion, s32[]{:T(128)} %constant.1116.clone.1, s32[]{:T(128)} %bitcast.19, s32[]{:T(128)} %bitcast.20) | dynamic-update-slice | bytes 86020 | tf_op jit(solution)/shard_map/scatter | solution.py:60
  179.3 7.3 %scatter.76 = f32[6,128,128]{1,2,0:T(8,128)S(1)} dynamic-update-slice(f32[6,128,128]{1,2,0:T(8,128)S(1)} %scatter.75, f32[6,112,112]{1,2,0:T(8,128)S(1)} %convolution_subtract_fusion, s32[]{:T(128)} %constant.1116.clone.1, s32[]{:T(128)} %constant.1125.clone.1, s32[]{:T(128)} %constant.1125.clone.1) | dynamic-update-slice | bytes 602116 | tf_op jit(solution)/shard_map/scatter | solution.py:69
  186.7 12.9 %while.249 = (s32[]{:T(128)}, f32[6,112,16]{1,0,2:T(8,128)S(1)}, s32[]{:T(128)}) while((s32[]{:T(128)}, f32[6,112,16]{1,0,2:T(8,128)S(1)}, s32[]{:T(128)}) %tuple.586), condition=%wide.region_8.9_spmd.clone.clone, body=%wide.region_7.8_spmd.clone.clone.sunk | while | flops 35634 | bytes 186145 | solution.py:38
  199.6 2.3 scatter.79
  202.1 2.5 while.242
  204.8 3.2 scatter.80
  208.8 3.2 scatter.81
  212.0 12.5 %while.250 = (s32[]{:T(128)}, f32[6,96,16]{1,0,2:T(8,128)S(1)}, s32[]{:T(128)}) while((s32[]{:T(128)}, f32[6,96,16]{1,0,2:T(8,128)S(1)}, s32[]{:T(128)}) %tuple.592), condition=%wide.region_12.13_spmd.clone.clone, body=%wide.region_11.12_spmd.clone.clone.sunk | while | flops 30562 | bytes 159857 | solution.py:38
  224.6 2.3 scatter.84
  227.1 2.6 while.243
  229.8 3.0 scatter.85
  233.4 3.0 scatter.86
  236.5 12.1 %while.251 = (s32[]{:T(128)}, f32[6,80,16]{1,0,2:T(8,128)S(1)}, s32[]{:T(128)}) while((s32[]{:T(128)}, f32[6,80,16]{1,0,2:T(8,128)S(1)}, s32[]{:T(128)}) %tuple.598), condition=%wide.region_16.17_spmd.clone.clone, body=%wide.region_15.16_spmd.clone.clone.sunk | while | flops 25490 | bytes 133569 | solution.py:38
  248.7 2.3 scatter.89
  251.2 2.5 while.244
  253.8 3.0 scatter.90
  257.4 2.8 scatter.91
  260.3 11.8 %while.252 = (s32[]{:T(128)}, f32[6,64,16]{1,0,2:T(8,128)S(1)}, s32[]{:T(128)}) while((s32[]{:T(128)}, f32[6,64,16]{1,0,2:T(8,128)S(1)}, s32[]{:T(128)}) %tuple.604), condition=%wide.region_20.21_spmd.clone.clone, body=%wide.region_19.20_spmd.clone.clone.sunk | while | flops 20418 | bytes 107281 | solution.py:38
  272.1 2.3 scatter.94
  274.6 2.5 while.245
  277.2 2.6 scatter.95
  280.4 2.6 scatter.96
  283.0 11.5 %while.253 = (s32[]{:T(128)}, f32[6,48,16]{1,0,2:T(8,128)S(1)}, s32[]{:T(128)}) while((s32[]{:T(128)}, f32[6,48,16]{1,0,2:T(8,128)S(1)}, s32[]{:T(128)}) %tuple.610), condition=%wide.region_24.25_spmd.clone.clone, body=%wide.region_23.24_spmd.clone.clone.sunk | while | flops 15346 | bytes 80993 | solution.py:38
  294.5 2.3 scatter.99
  297.0 2.5 while.246
  299.6 2.4 scatter.100
  302.5 2.4 scatter.101
  305.0 11.1 %while.254 = (s32[]{:T(128)}, f32[6,32,16]{1,0,2:T(8,128)S(1)}, s32[]{:T(128)}) while((s32[]{:T(128)}, f32[6,32,16]{1,0,2:T(8,128)S(1)}, s32[]{:T(128)}) %tuple.616), condition=%wide.region_28.29_spmd.clone.clone, body=%wide.region_27.28_spmd.clone.clone.sunk | while | flops 10274 | bytes 54705 | solution.py:38
  316.3 2.3 scatter.104
  318.7 3.8 %while.247 = (s32[]{:T(128)}, f32[6,16,16]{2,0,1:T(8,128)S(1)}, f32[6,16,16]{1,0,2:T(8,128)S(1)}, s32[]{:T(128)}) while((s32[]{:T(128)}, f32[6,16,16]{2,0,1:T(8,128)S(1)}, f32[6,16,16]{1,0,2:T(8,128)S(1)}, s32[]{:T(128)}) %tuple.633), condition=%wide.region_30.31_spmd.clone, body=%wide.region_29.30_spmd.clone.sunk | while | flops 3186 | bytes 15465 | solution.py:48
  322.6 2.2 scatter.105
  325.0 2.2 scatter.106
  327.2 10.7 %while.255 = (s32[]{:T(128)}, f32[6,16,16]{1,0,2:T(8,128)S(1)}, s32[]{:T(128)}) while((s32[]{:T(128)}, f32[6,16,16]{1,0,2:T(8,128)S(1)}, s32[]{:T(128)}) %tuple.622), condition=%wide.region_32.33_spmd.clone.clone, body=%wide.region_31.32_spmd.clone.clone.sunk | while | flops 5186 | bytes 28397 | solution.py:38
  337.9 2.2 scatter.109
  340.2 0.9 copy.164
  341.1 2.8 dynamic-slice_subtract_fusion
  (1788 shorter events, 122.5 us)
Async XLA Ops:
  7.2 3.9 %copy-start.2 = (s32[1,8,12]{2,1,0:T(8,128)S(1)}, s32[1,8,12]{2,1,0:T(8,128)}, u32[]{:S(2)}) copy-start(s32[1,8,12]{2,1,0:T(8,128)} %param.81) | copy-start | bytes 1156
  7.2 4.1 %copy-start = (bf16[1,8,1536,64]{2,3,1,0:T(8,128)(2,1)S(1)}, bf16[1,8,1536,64]{2,3,1,0:T(8,128)(2,1)}, u32[]{:S(2)}) copy-start(bf16[1,8,1536,64]{2,3,1,0:T(8,128)(2,1)} %param.79) | copy-start | bytes 4718596
  7.2 17.6 %all-gather.5.cloned.1.call-start = ((), (), s32[]{:S(2)}) async-start(), calls=%async_computation.2 | async-start | bytes 4718592 | tf_op jit(solution)/shard_map/all_gather | solution.py:97
  8.3 4.4 %copy-start.3 = (s32[3]{0:T(128)S(1)}, s32[3]{0:T(128)}, u32[]{:S(2)}) copy-start(s32[3]{0:T(128)} %constant.1126.clone.1) | copy-start | bytes 40
  11.0 86.7 %all-gather.3.cloned.1.call-start = ((), (), s32[]{:S(2)}) async-start(), calls=%async_computation.1 | async-start | bytes 7864320 | tf_op jit(solution)/shard_map/all_gather | solution.py:101
  12.6 137.6 %all-reduce.2.cloned.1.call-start = ((), (), s32[]{:S(2)}) async-start(), calls=%async_computation.4 | async-start | bytes 786432 | tf_op jit(solution)/shard_map/psum | solution.py:111
  112.4 0.7 copy-start.1
  113.2 227.9 %reduce-scatter.2.cloned.1.call-start = ((), (), s32[]{:S(2)}) async-start(), calls=%async_computation.3 | async-start | bytes 5898240 | tf_op jit(solution)/shard_map/reduce_scatter | solution.py:107
Sparse Core Ops, SparseCore 0:
  11.1 13.6 all-gather.4
  26.6 71.0 all-gather.2
  113.3 36.8 all-reduce.1
  152.5 85.1 reduce-scatter.1
where the time goes:
time: 353 us; the launch traced here: 350 us
  local copies, waits for them, and re-layouts  137 us (39%)
  waiting for transfers between devices  116 us (33%)
  other arithmetic  55.1 us (16%)
  between operations  14.5 us (4%)
  matrix products  13.4 us (4%)
  loops' own time  11.6 us (3%)
    all_gather x1, waiting for transfers between devices, shards(): lax.all_gather(left_masked, 'col', axis=2, tiled=True)  72.9 us
    psum x1, waiting for transfers between devices, shards(): pivots = start_blocks - lax.psum(partial_blocks, 'layer')  33.8 us
    scatter x7, local copies, waits for them, and re-layouts, factor(): current = current.at[:, end:, end:].set(trailing)  23.7 us
    dynamic_slice x128, local copies, waits for them, and re-layouts, eliminate_sweep(): pivot = current[:, step, step]  23.6 us
    scatter x7, local copies, waits for them, and re-layouts, factor(): current = current.at[:, offset:end, end:].set(strip)  22.9 us
    while x224, local copies, waits for them, and re-layouts  22 us
    scatter x8, local copies, waits for them, and re-layouts, factor(): current = current.at[:, offset:, offset:end].set(panel)  16 us
    unnamed x36, local copies, waits for them, and re-layouts  12 us
  transfers between devices with their start and end apart: 4, of which 3 were waited for; matrix products, arithmetic and copies ran while one was open for 53% of the time, Pallas kernels for 0%

commit v1 on v0

v1 whole, which is shorter than its diff:
```python
import functools

import jax
import jax.numpy as jnp
from jax import lax
from jax.experimental import pallas as pl
from jax.experimental.pallas import tpu as pltpu
from jax.sharding import PartitionSpec as P

BLK = 128
VMEM_LIMIT = 48 * 1024 * 1024
SMEM = pl.BlockSpec(memory_space=pltpu.SMEM)
VMEM = pl.BlockSpec(memory_space=pltpu.VMEM)
ANY = pl.BlockSpec(memory_space=pl.ANY)


def lu_step(ref, j):
    size = ref.shape[1]
    top = j // 8 * 8
    row = ref[:, j : j + 1, :]
    inverse = 1.0 / row[:, :, j : j + 1]
    lanes = lax.broadcasted_iota(jnp.int32, (1, 1, size), 2)
    used = jnp.where(lanes > j, row, 0.0)
    if j % 8 != 7:
        head = ref[:, top : top + 8, :]
        rows = lax.broadcasted_iota(jnp.int32, (1, 8, 1), 1) + top
        factor = jnp.where(rows > j, head[:, :, j : j + 1] * inverse, 0.0)
        swept = head - factor * used
        ref[:, top : top + 8, :] = jnp.where((lanes == j) & (rows > j), factor, swept)
    if top + 8 < size:
        rest = ref[:, top + 8 :, :]
        factor = rest[:, :, j : j + 1] * inverse
        ref[:, top + 8 :, :] = jnp.where(lanes == j, factor, rest - factor * used)


def lu_kernel(where_ref, own_ref, other_ref, out_ref):
    held = where_ref[1] == where_ref[3]

    @pl.when(held)
    def _():
        out_ref[...] = own_ref[...]

    @pl.when(jnp.logical_not(held))
    def _():
        out_ref[...] = other_ref[...]

    for j in range(out_ref.shape[1]):
        lu_step(out_ref, j)


def factor(where, own, other):
    return pl.pallas_call(
        lu_kernel,
        out_shape=jax.ShapeDtypeStruct(own.shape, jnp.float32),
        in_specs=[SMEM, VMEM, VMEM],
        out_specs=VMEM,
        compiler_params=pltpu.CompilerParams(vmem_limit_bytes=VMEM_LIMIT),
        cost_estimate=pl.CostEstimate(flops=0, bytes_accessed=60_000_000, transcendentals=0),
        name="factor",
    )(where, own, other)


def pivot_kernel(chunks, layers, where_ref, anc_ref, *refs):
    parts, (out_ref, blocks, sems) = refs[:-3], refs[-3:]
    count = out_ref.shape[0]
    base = where_ref[4]
    copies = []
    for q in range(count):
        rows = pl.ds(pl.multiple_of(base + q * BLK, BLK), BLK)
        copies.append(
            pltpu.make_async_copy(
                anc_ref.at[rows, q * BLK : (q + 1) * BLK], blocks.at[q], sems.at[q]
            )
        )
    for copy in copies:
        copy.start()
    for copy in copies:
        copy.wait()
    for j in range(chunks):
        held = parts[j * layers : (j + 1) * layers]
        for i in range(count // chunks):
            terms = [ref[i] for ref in held]
            while len(terms) > 1:
                terms = [terms[n] + terms[n + 1] for n in range(0, len(terms), 2)]
            q = i * chunks + j
            out_ref[q] = blocks[q] - terms[0]


def pivots(where, anc, parts, chunks, layers):
    count = chunks * parts[0].shape[0]
    return pl.pallas_call(
        functools.partial(pivot_kernel, chunks, layers),
        out_shape=jax.ShapeDtypeStruct((count, BLK, BLK), jnp.float32),
        in_specs=[SMEM, ANY] + [VMEM] * len(parts),
        out_specs=VMEM,
        scratch_shapes=[
            pltpu.VMEM((count, BLK, BLK), jnp.float32),
            pltpu.SemaphoreType.DMA((count,)),
        ],
        compiler_params=pltpu.CompilerParams(vmem_limit_bytes=VMEM_LIMIT),
        name="pivots",
    )(where, anc, *parts)


def update_kernel(
    chunk, chunks, layers, where_ref, lpat_ref, upat_ref,
    own_ref, x_ref, y_ref, da_ref, db_ref, u_ref, uo_ref, *refs,
):
    kept_ref, diag_ref = refs[0], refs[1]
    sent_refs = refs[2 : 1 + layers]
    left, right, acc, sems = refs[1 + layers :]
    layer, row, col = where_ref[0], where_ref[1], where_ref[2]
    supers, depth, _ = own_ref.shape
    half = supers // 2
    wide = u_ref.shape[1]

    def slot(index, size):
        return pl.ds(pl.multiple_of(index * size, size), size)

    waits = []
    for h in range(2):
        ks = pl.ds(h * half, half)
        items = [
            (own_ref.at[ks], left.at[ks, slot(col, depth)]),
            (x_ref.at[ks], left.at[ks, slot(col ^ 1, depth)]),
            (y_ref.at[ks], left.at[ks, slot(col ^ 2, depth)]),
            ((da_ref, db_ref)[h], left.at[ks, slot(col ^ 3, depth)]),
            (u_ref.at[ks], right.at[ks, slot(row, wide)]),
            (uo_ref.at[ks], right.at[ks, slot(1 - row, wide)]),
        ]
        copies = [
            pltpu.make_async_copy(src, dst, sems.at[h, n]) for n, (src, dst) in enumerate(items)
        ]
        for copy in copies:
            copy.start()
        waits.append(copies)
    for h in range(2):
        for copy in waits[h]:
            copy.wait()
        for k in range(h * half, (h + 1) * half):
            for t in range(layers):

                @pl.when(lpat_ref[k, t * chunks + chunk] == 0)
                def _():
                    left[k, :, t * BLK : (t + 1) * BLK] = jnp.zeros(
                        (left.shape[1], BLK), left.dtype
                    )

            for n in range(right.shape[2] // BLK):

                @pl.when(upat_ref[k, n] == 0)
                def _():
                    right[k, :, n * BLK : (n + 1) * BLK] = jnp.zeros(
                        (right.shape[1], BLK), right.dtype
                    )

        product = lax.dot_general(
            left[h * half : (h + 1) * half].reshape(-1, left.shape[2]),
            right[h * half : (h + 1) * half].reshape(-1, right.shape[2]),
            (((0,), (0,)), ((), ())),
            preferred_element_type=jnp.float32,
        ).reshape(acc.shape)
        if h == 0:
            acc[...] = product
        else:
            acc[...] += product
    kept_ref[...] = acc[layer]
    for s in range(1, layers):
        sent_refs[s - 1][...] = acc[layer ^ s]
    per = diag_ref.shape[0]
    for i in range(per):
        q = i * chunks + chunk
        diag_ref[i] = acc[where_ref[5] + i, :, q * BLK : (q + 1) * BLK]


def chunk_update(where, lpat, upat, pieces, u, uo, chunk, chunks, layers):
    supers, depth, width = pieces[0].shape
    cols = u.shape[2]
    kdim = 2 * u.shape[1]
    per = cols // BLK // chunks
    one = jax.ShapeDtypeStruct((BLK, cols), jnp.float32)
    return pl.pallas_call(
        functools.partial(update_kernel, chunk, chunks, layers),
        out_shape=[one, jax.ShapeDtypeStruct((per, BLK, BLK), jnp.float32)] + [one] * (layers - 1),
        in_specs=[SMEM] * 3 + [ANY] * 7,
        out_specs=[VMEM] * (1 + layers),
        scratch_shapes=[
            pltpu.VMEM((supers, kdim, width), jnp.bfloat16),
            pltpu.VMEM((supers, kdim, cols), jnp.bfloat16),
            pltpu.VMEM((layers, BLK, cols), jnp.float32),
            pltpu.SemaphoreType.DMA((2, 6)),
        ],
        compiler_params=pltpu.CompilerParams(vmem_limit_bytes=VMEM_LIMIT),
        cost_estimate=pl.CostEstimate(
            flops=2 * supers * kdim * width * cols, bytes_accessed=8_000_000, transcendentals=0
        ),
        name="update",
    )(where, lpat, upat, *pieces, u, uo)


def xor_perm(size, bit):
    return [(i, i ^ bit) for i in range(size)]


def planned(lpanel, upanel, lpat, upat, anc):
    layers, rows, cols = (lax.axis_size(n) for n in ("layer", "row", "col"))
    layer, row, col = (lax.axis_index(n) for n in ("layer", "row", "col"))
    width = anc.shape[1]
    share = anc.shape[0] // layers
    chunks = share // BLK
    per_group = cols // rows
    where = jnp.stack(
        [
            layer,
            row,
            col,
            col // per_group,
            col % per_group * width,
            col % per_group * (width // share),
        ]
    ).astype(jnp.int32)
    lt = jnp.swapaxes(lpanel[0], 1, 2)
    u = upanel[0]
    supers, depth, length = lt.shape
    half = supers // 2
    cut = lt.reshape(supers, depth, layers, chunks, BLK)
    over_x, over_y = xor_perm(cols, 1), xor_perm(cols, 2)
    uo = lax.ppermute(u, "row", [(0, 1), (1, 0)])
    sends = [cut[:, :, :, j, :].reshape(supers, depth, layers * BLK) for j in range(chunks)]
    full = [(lax.ppermute(s, "col", over_x), lax.ppermute(s, "col", over_y)) for s in sends]
    kept, parts = [], []
    everyone = ("layer", "row", "col")
    index = lambda l, r, c: (l * rows + r) * cols + c
    for j in range(chunks):
        x, y = full[j]
        da = lax.ppermute(x[:half], "col", over_y)
        db = lax.ppermute(y[half:], "col", over_x)
        out = chunk_update(
            where, lpat[0], upat[0], (sends[j], x, y, da, db), u, uo, j, chunks, layers
        )
        diag = out[1]
        total = out[0]
        parts.append(diag)
        for s in range(1, layers):
            perm = [
                (index(l, c // per_group, c), index(l ^ s, c // per_group, c))
                for l in range(layers)
                for c in range(cols)
            ]
            parts.append(lax.ppermute(diag, everyone, perm))
        for s in range(1, layers):
            total = total + lax.ppermute(out[1 + s], "layer", xor_perm(layers, s))
        kept.append(total)
    own = pivots(where, anc, parts, chunks, layers)
    other = lax.ppermute(own, "row", [(0, 1), (1, 0)])
    diag_lu = factor(where, own, other)
    mine = lax.dynamic_slice_in_dim(anc, layer * share, share, 0)
    schur = mine - jnp.concatenate(kept, axis=0)
    return schur, diag_lu


def mask_rows(panel, pattern, block):
    count, length, inner = panel.shape
    shaped = panel.reshape(count, length // block, block, inner)
    return (shaped * pattern[:, :, None, None].astype(panel.dtype)).reshape(count, length, inner)


def mask_cols(panel, pattern, block):
    count, inner, length = panel.shape
    shaped = panel.reshape(count, inner, length // block, block)
    return (shaped * pattern[:, None, :, None].astype(panel.dtype)).reshape(count, inner, length)


def candidates(matrix):
    width = matrix.shape[1]
    per_group = lax.axis_size("col") // lax.axis_size("row")
    begin = lax.axis_index("col") % per_group * width
    square = lax.dynamic_slice_in_dim(matrix, begin, width, 0)
    count = width // BLK
    return jnp.stack(
        [square[j * BLK : (j + 1) * BLK, j * BLK : (j + 1) * BLK] for j in range(count)]
    )


def gathered(lpanel, upanel, lpat, upat, anc):
    left = mask_rows(lpanel[0], lpat[0], BLK)
    right = mask_cols(upanel[0], upat[0], BLK)
    update = jnp.einsum(
        "kmw,kwn->mn",
        lax.all_gather(left, "col", axis=2, tiled=True),
        lax.all_gather(right, "row", axis=1, tiled=True),
        preferred_element_type=jnp.float32,
    )
    rows = lax.axis_size("row")
    per_group = lax.axis_size("col") // rows
    share = anc.shape[0] // lax.axis_size("layer")
    pivot_blocks = candidates(anc) - lax.psum(candidates(update), "layer")
    both = lax.all_gather(pivot_blocks, "row", axis=0)
    chosen = lax.dynamic_index_in_dim(both, lax.axis_index("col") // per_group, 0, keepdims=False)
    where = jnp.zeros((6,), jnp.int32)
    diag_lu = factor(where, chosen, chosen)
    summed = lax.psum_scatter(update, "layer", scatter_dimension=0, tiled=True)
    mine = lax.dynamic_slice_in_dim(anc, lax.axis_index("layer") * share, share, 0)
    return mine - summed, diag_lu


def shards(lpanel, upanel, lpat, upat, anc):
    layers, rows, cols = (lax.axis_size(n) for n in ("layer", "row", "col"))
    fits = rows == 2 and cols == 4 and layers == 4
    if fits and anc.shape[0] % (layers * BLK) == 0 and lpanel.shape[1] % 2 == 0:
        return planned(lpanel, upanel, lpat, upat, anc)
    return gathered(lpanel, upanel, lpat, upat, anc)


def solution(mesh):
    return jax.shard_map(
        shards,
        mesh=mesh,
        in_specs=(
            P("layer", None, "row", "col"),
            P("layer", None, "row", "col"),
            P("layer", None, "row"),
            P("layer", None, "col"),
            P("row", "col"),
        ),
        out_specs=(P(("row", "layer"), "col"), P("col", None, None)),
        check_vma=False,
    )
```

time: 353 us -> 228 us (0.65)
  local copies, waits for them, and re-layouts: 137 us -> 26.4 us
  starting transfers between devices: 0.16 us -> 70 us
  other arithmetic: 55.1 us -> 5.1 us
  Pallas kernels: 0 us -> 33.6 us
  waiting for transfers between devices: 116 us -> 89.4 us
  between operations: 14.5 us -> 0.97 us
  matrix products: 13.4 us -> 0 us
  loops' own time: 11.6 us -> 0 us
    ppermute x0 -> x32, waiting for transfers between devices: none -> 89.4 us  [the longest x9 46.2 us: planned(): parts.append(lax.ppermute(diag, everyone, perm))]
    all_gather x2 -> x0, waiting for transfers between devices: 81.7 us -> none  [the longest x1 72.9 us: shards(): lax.all_gather(left_masked, 'col', axis=2, tiled=True)]
    ppermute x0 -> x32, starting transfers between devices: none -> 70 us  [the longest x9 39.6 us: planned(): parts.append(lax.ppermute(diag, everyone, perm))]
    scatter x22 -> x0, local copies, waits for them, and re-layouts: 62.5 us -> none  [the longest x7 23.7 us: factor(): current = current.at[:, end:, end:].set(trailing)]
    psum x1 -> x0, waiting for transfers between devices: 33.8 us -> none  [shards(): pivots = start_blocks - lax.psum(partial_blocks, 'layer')]
    pallas_call x0 -> x5, Pallas kernels: none -> 33.6 us  [the longest x3 17.9 us: chunk_update(): pl.pallas_call(functools.partial(update_kernel, chunk, chunks, layers), o...]
    dynamic_slice x225 -> x0, local copies, waits for them, and re-layouts: 24.6 us -> none  [the longest x128 23.6 us: eliminate_sweep(): pivot = current[:, step, step]]
    while x239 -> x0, local copies, waits for them, and re-layouts: 22.9 us -> none
  transfers between devices with their start and end apart: 4 -> 32, of which waited for: 3 -> 11; matrix products, arithmetic and copies ran while one was open for 53% -> 12% of each run, Pallas kernels for 0% -> 9%
where the time goes in v1:
time: 228 us; the launch traced here: 225 us
  waiting for transfers between devices  89.4 us (39%)
  starting transfers between devices  70 us (31%)
  Pallas kernels  33.6 us (15%)
  local copies, waits for them, and re-layouts  26.4 us (12%)
  other arithmetic  5.1 us (2%)
    ppermute x9, waiting for transfers between devices, planned(): parts.append(lax.ppermute(diag, everyone, perm))  46.2 us
    ppermute x9, starting transfers between devices, planned(): parts.append(lax.ppermute(diag, everyone, perm))  39.6 us
    ppermute x3, waiting for transfers between devices, planned(): lax.ppermute(s, 'col', over_x)  22.6 us
    pallas_call x3, Pallas kernels, chunk_update(): pl.pallas_call(functools.partial(update_kernel, chunk, chunks, layers), o...  17.9 us
    ppermute x9, waiting for transfers between devices, planned(): total = total + lax.ppermute(out[1 + s], 'layer', xor_perm(layers, s))  17 us
    ppermute x9, starting transfers between devices, planned(): total = total + lax.ppermute(out[1 + s], 'layer', xor_perm(layers, s))  16.3 us
    pallas_call x1, Pallas kernels, factor(): pl.pallas_call(lu_kernel, out_shape=jax.ShapeDtypeStruct(own.shape, jnp.f...  14 us
    slice x1, local copies, waits for them, and re-layouts, planned(): cut[:, :, :, j, :].reshape(supers, depth, layers * BLK)  9.45 us
  transfers between devices with their start and end apart: 32, of which 11 were waited for; matrix products, arithmetic and copies ran while one was open for 12% of the time, Pallas kernels for 9%

profile of v1, /device:TPU:2, one launch (start us, length us, event | category | flops | bytes accessed | tf_op | source)
XLA Modules:
  0.0 225.4 jit_solution(9774516398200312236)
XLA Ops:
  0.7 4.6 %reshape.7 = bf16[8,64,4,3,128]{4,3,2,1,0:T(4,128)(2,1)S(1)} reshape(bf16[8,64,1536]{2,1,0:T(8,128)(2,1)} %bitcast.22) | data formatting | bytes 3145728 | tf_op jit(solution)/shard_map/reshape | solution.py:226
  5.3 9.5 %slice_reduce_fusion.2 = (bf16[8,64,4,128]{3,2,1,0:T(4,128)(2,1)}, bf16[8,64,4,128]{3,2,1,0:T(4,128)(2,1)S(1)}, bf16[8,64,4,128]{3,2,1,0:T(4,128)(2,1)S(1)}) fusion(bf16[8,64,4,3,128]{4,3,2,1,0:T(4,128)(2,1)S(1)} %reshape.7), kind=kLoop, calls=%fused_computation.3 | loop fusion | bytes 3145728 | tf_op jit(solution)/shard_map/slice | solution.py:229
  14.8 1.2 reshape_squeeze.9.own_ref
  16.1 2.0 collective-permute-start.1
  18.3 1.6 collective-permute-start.8
  20.6 10.3 %collective-permute-done.x_ref = bf16[8,64,512]{2,1,0:T(8,128)(2,1)} collective-permute-done((bf16[8,64,512]{2,1,0:T(8,128)(2,1)S(1)}, bf16[8,64,512]{2,1,0:T(8,128)(2,1)}, u32[]{:S(2)}, u32[]{:S(2)}) %collective-permute-start) | collective-permute-done | bytes 524320 | tf_op jit(solution)/shard_map/ppermute | solution.py:230
  31.0 2.0 collective-permute-start.16
  33.0 1.7 slice.37
  34.7 1.7 slice.38
  36.4 5.7 %collective-permute-done.8.x_ref = bf16[8,64,512]{2,1,0:T(8,128)(2,1)S(1)} collective-permute-done((bf16[8,64,512]{2,1,0:T(8,128)(2,1)S(1)}, bf16[8,64,512]{2,1,0:T(8,128)(2,1)S(1)}, u32[]{:S(2)}, u32[]{:S(2)}) %collective-permute-start.8) | collective-permute-done | bytes 524320 | tf_op jit(solution)/shard_map/ppermute | solution.py:230
  42.0 1.5 collective-permute-start.2
  44.9 1.7 slice.41
  46.6 6.7 %collective-permute-done.15.x_ref = bf16[8,64,512]{2,1,0:T(8,128)(2,1)S(1)} collective-permute-done((bf16[8,64,512]{2,1,0:T(8,128)(2,1)S(1)}, bf16[8,64,512]{2,1,0:T(8,128)(2,1)S(1)}, u32[]{:S(2)}, u32[]{:S(2)}) %collective-permute-start.15) | collective-permute-done | bytes 524320 | tf_op jit(solution)/shard_map/ppermute | solution.py:230
  53.3 1.5 collective-permute-start.10
  55.6 3.5 %collective-permute-done.2.da_ref = bf16[4,64,512]{2,1,0:T(8,128)(2,1)} collective-permute-done((bf16[4,64,512]{2,1,0:T(8,128)(2,1)}, bf16[4,64,512]{2,1,0:T(8,128)(2,1)}, u32[]{:S(2)}, u32[]{:S(2)}) %collective-permute-start.2) | collective-permute-done | bytes 262176 | tf_op jit(solution)/shard_map/ppermute | solution.py:236
  59.1 2.0 collective-permute-start.17
  61.1 1.5 collective-permute-start.18
  62.6 1.4 copy-done.4
  64.0 5.3 %update.3 = (f32[128,768]{1,0:T(8,128)S(1)}, f32[2,128,128]{2,1,0:T(8,128)S(1)}, f32[128,768]{1,0:T(8,128)S(1)}, f32[128,768]{1,0:T(8,128)S(1)}, f32[128,768]{1,0:T(8,128)S(1)}) custom-call(s32[6]{0:T(128)S(1)} %stack.27.where_ref, s32[8,12]{1,0:T(8,128)S(1)} %bitcast.19, s32[8,6]{1,0:T(8,128)S(1)} %bitcast.12, ...), custom_call_target="tpu_custom_call" | custom-call | flops 1610612736 | bytes 8000000 | tf_op jit(solution)/shard_map/update/pallas_call | solution.py:182
  70.9 0.8 copy-done.10
  71.6 3.6 %collective-permute-start.22 = (f32[2,128,128]{2,1,0:T(8,128)S(1)}, f32[2,128,128]{2,1,0:T(8,128)S(1)}, u32[]{:S(2)}, u32[]{:S(2)}) collective-permute-start(f32[2,128,128]{2,1,0:T(8,128)S(1)} %get-tuple-element.29.refs_0_), channel_id=1, source_target_pairs={{0,8},{1,9},{6,14},{7,15},{8,0},{9,1},{14,6},{15,7},{16,24},{17,25... | collective-permute-start | bytes 393224 | tf_op jit(solution)/shard_map/ppermute | solution.py:250
  75.3 4.6 %collective-permute-start.23 = (f32[2,128,128]{2,1,0:T(8,128)S(1)}, f32[2,128,128]{2,1,0:T(8,128)S(1)}, u32[]{:S(2)}, u32[]{:S(2)}) collective-permute-start(f32[2,128,128]{2,1,0:T(8,128)S(1)} %get-tuple-element.29.refs_0_), channel_id=1, source_target_pairs={{0,16},{1,17},{6,22},{7,23},{8,24},{9,25},{14,30},{15,31},{16,0},{... | collective-permute-start | bytes 393224 | tf_op jit(solution)/shard_map/ppermute | solution.py:250
  79.9 2.0 collective-permute-start.24
  81.9 1.0 copy-done.3
  82.9 6.4 %update.4 = (f32[128,768]{1,0:T(8,128)S(1)}, f32[2,128,128]{2,1,0:T(8,128)S(1)}, f32[128,768]{1,0:T(8,128)}, f32[128,768]{1,0:T(8,128)}, f32[128,768]{1,0:T(8,128)}) custom-call(s32[6]{0:T(128)S(1)} %stack.27.where_ref, s32[8,12]{1,0:T(8,128)S(1)} %bitcast.20, s32[8,6]{1,0:T(8,128)S(1)} %bitcast.13, bf16[8,64,512]{2,1,0:T(8,128)(2,1)S(1)} %reshape_squeeze.10.own_ref, ...), custom_call_target="tpu_custom_call" | custom-call | flops 1610612736 | bytes 8000000 | tf_op jit(solution)/shard_map/update/pallas_call | solution.py:182
  89.4 2.6 %collective-permute-start.25 = (f32[2,128,128]{2,1,0:T(8,128)S(1)}, f32[2,128,128]{2,1,0:T(8,128)S(1)}, u32[]{:S(2)}, u32[]{:S(2)}) collective-permute-start(f32[2,128,128]{2,1,0:T(8,128)S(1)} %get-tuple-element.30.refs_4_), channel_id=1, source_target_pairs={{0,8},{1,9},{6,14},{7,15},{8,0},{9,1},{14,6},{15,7},{16,24},{17,25... | collective-permute-start | bytes 393224 | tf_op jit(solution)/shard_map/ppermute | solution.py:250
  92.0 5.5 %collective-permute-start.26 = (f32[2,128,128]{2,1,0:T(8,128)S(1)}, f32[2,128,128]{2,1,0:T(8,128)S(1)}, u32[]{:S(2)}, u32[]{:S(2)}) collective-permute-start(f32[2,128,128]{2,1,0:T(8,128)S(1)} %get-tuple-element.30.refs_4_), channel_id=1, source_target_pairs={{0,16},{1,17},{6,22},{7,23},{8,24},{9,25},{14,30},{15,31},{16,0},{... | collective-permute-start | bytes 393224 | tf_op jit(solution)/shard_map/ppermute | solution.py:250
  97.5 2.0 collective-permute-start.27
  99.6 6.1 %update.5 = (f32[128,768]{1,0:T(8,128)S(1)}, f32[2,128,128]{2,1,0:T(8,128)S(1)}, f32[128,768]{1,0:T(8,128)}, f32[128,768]{1,0:T(8,128)}, f32[128,768]{1,0:T(8,128)S(1)}) custom-call(s32[6]{0:T(128)S(1)} %stack.27.where_ref, s32[8,12]{1,0:T(8,128)S(1)} %bitcast.21, s32[8,6]{1,0:T(8,128)S(1)} %bitcast.14, bf16[8,64,512]{2,1,0:T(8,128)(2,1)S(1)} %reshape_squeeze.11.own_ref, ...), custom_call_target="tpu_custom_call" | custom-call | flops 1610612736 | bytes 8000000 | tf_op jit(solution)/shard_map/update/pallas_call | solution.py:182
  105.7 2.4 %collective-permute-start.28 = (f32[2,128,128]{2,1,0:T(8,128)S(1)}, f32[2,128,128]{2,1,0:T(8,128)S(1)}, u32[]{:S(2)}, u32[]{:S(2)}) collective-permute-start(f32[2,128,128]{2,1,0:T(8,128)S(1)} %get-tuple-element.31.refs_8_), channel_id=1, source_target_pairs={{0,8},{1,9},{6,14},{7,15},{8,0},{9,1},{14,6},{15,7},{16,24},{17,25... | collective-permute-start | bytes 393224 | tf_op jit(solution)/shard_map/ppermute | solution.py:250
  108.1 3.3 %collective-permute-start.21 = (f32[128,768]{1,0:T(8,128)S(1)}, f32[128,768]{1,0:T(8,128)S(1)}, u32[]{:S(2)}, u32[]{:S(2)}) collective-permute-start(f32[128,768]{1,0:T(8,128)S(1)} %get-tuple-element.28), channel_id=1, source_target_pairs={{0,24},{8,16},{16,8},{24,0},{1,25},{9,17},{17,9},{25,1},{2,26},{10... | collective-permute-start | bytes 1179656 | tf_op jit(solution)/shard_map/ppermute | solution.py:252
  112.6 3.2 %collective-permute-start.14 = (f32[128,768]{1,0:T(8,128)}, f32[128,768]{1,0:T(8,128)}, u32[]{:S(2)}, u32[]{:S(2)}) collective-permute-start(f32[128,768]{1,0:T(8,128)} %get-tuple-element.24), channel_id=1, source_target_pairs={{0,24},{8,16},{16,8},{24,0},{1,25},{9,17},{17,9},{25,1},{2,26},{10... | collective-permute-start | bytes 1179656 | tf_op jit(solution)/shard_map/ppermute | solution.py:252
  115.8 3.7 %collective-permute-done.28.refs_9_ = f32[2,128,128]{2,1,0:T(8,128)S(1)} collective-permute-done((f32[2,128,128]{2,1,0:T(8,128)S(1)}, f32[2,128,128]{2,1,0:T(8,128)S(1)}, u32[]{:S(2)}, u32[]{:S(2)}) %collective-permute-start.28) | collective-permute-done | bytes 131104 | tf_op jit(solution)/shard_map/ppermute | solution.py:250
  119.5 11.2 %collective-permute-start.29 = (f32[2,128,128]{2,1,0:T(8,128)S(1)}, f32[2,128,128]{2,1,0:T(8,128)S(1)}, u32[]{:S(2)}, u32[]{:S(2)}) collective-permute-start(f32[2,128,128]{2,1,0:T(8,128)S(1)} %get-tuple-element.31.refs_8_), channel_id=1, source_target_pairs={{0,16},{1,17},{6,22},{7,23},{8,24},{9,25},{14,30},{15,31},{16,0},{... | collective-permute-start | bytes 393224 | tf_op jit(solution)/shard_map/ppermute | solution.py:250
  130.7 39.4 %collective-permute-done.29.refs_10_ = f32[2,128,128]{2,1,0:T(8,128)S(1)} collective-permute-done((f32[2,128,128]{2,1,0:T(8,128)S(1)}, f32[2,128,128]{2,1,0:T(8,128)S(1)}, u32[]{:S(2)}, u32[]{:S(2)}) %collective-permute-start.29) | collective-permute-done | bytes 131104 | tf_op jit(solution)/shard_map/ppermute | solution.py:250
  170.1 5.6 %collective-permute-start.30 = (f32[2,128,128]{2,1,0:T(8,128)S(1)}, f32[2,128,128]{2,1,0:T(8,128)S(1)}, u32[]{:S(2)}, u32[]{:S(2)}) collective-permute-start(f32[2,128,128]{2,1,0:T(8,128)S(1)} %get-tuple-element.31.refs_8_), channel_id=1, source_target_pairs={{0,24},{1,25},{6,30},{7,31},{8,16},{9,17},{14,22},{15,23},{16,8},{... | collective-permute-start | bytes 393224 | tf_op jit(solution)/shard_map/ppermute | solution.py:250
  175.8 3.1 %collective-permute-done.30.refs_11_ = f32[2,128,128]{2,1,0:T(8,128)S(1)} collective-permute-done((f32[2,128,128]{2,1,0:T(8,128)S(1)}, f32[2,128,128]{2,1,0:T(8,128)S(1)}, u32[]{:S(2)}, u32[]{:S(2)}) %collective-permute-start.30) | collective-permute-done | bytes 131104 | tf_op jit(solution)/shard_map/ppermute | solution.py:250
  178.9 4.2 %collective-permute-start.12 = (f32[128,768]{1,0:T(8,128)}, f32[128,768]{1,0:T(8,128)}, u32[]{:S(2)}, u32[]{:S(2)}) collective-permute-start(f32[128,768]{1,0:T(8,128)} %get-tuple-element.22), channel_id=1, source_target_pairs={{0,8},{8,0},{16,24},{24,16},{1,9},{9,1},{17,25},{25,17},{2,10},{10... | collective-permute-start | bytes 1179656 | tf_op jit(solution)/shard_map/ppermute | solution.py:252
  183.1 1.7 pivots.1.own_ref
  185.1 2.0 collective-permute-start.6
  187.2 2.2 collective-permute-start.5
  189.3 1.2 add_add_fusion
  190.6 1.6 collective-permute-done.13
  192.6 1.3 add_add_fusion.1
  193.9 3.2 %collective-permute-done.7 = f32[128,768]{1,0:T(8,128)S(1)} collective-permute-done((f32[128,768]{1,0:T(8,128)S(1)}, f32[128,768]{1,0:T(8,128)S(1)}, u32[]{:S(2)}, u32[]{:S(2)}) %collective-permute-start.7) | collective-permute-done | bytes 393248 | tf_op jit(solution)/shard_map/ppermute | solution.py:252
  197.1 11.8 %collective-permute-done.6 = f32[128,768]{1,0:T(8,128)S(1)} collective-permute-done((f32[128,768]{1,0:T(8,128)S(1)}, f32[128,768]{1,0:T(8,128)S(1)}, u32[]{:S(2)}, u32[]{:S(2)}) %collective-permute-start.6) | collective-permute-done | bytes 393248 | tf_op jit(solution)/shard_map/ppermute | solution.py:252
  209.0 2.4 %maximum_subtract_fusion = f32[384,768]{1,0:T(8,128)} fusion(f32[128,768]{1,0:T(8,128)S(1)} %add_add_fusion, f32[128,768]{1,0:T(8,128)S(1)} %add_add_fusion.1, f32[128,768]{1,0:T(8,128)S(1)} %add_add_fusion.2, f32[1536,768]{1,0:T(8,128)} %anc_ref.1, s32[]{:T(128)S(6)} %select_n.16), kind=kLoop, calls=%fused_computation | loop fusion | flops 884736 | bytes 3538948 | tf_op jit(solution)/shard_map/sub | solution.py:258
  211.4 14.0 %factor.1 = f32[6,128,128]{2,1,0:T(8,128)} custom-call(s32[6]{0:T(128)S(1)} %stack.27.where_ref, f32[6,128,128]{2,1,0:T(8,128)S(1)} %pivots.1.own_ref, f32[6,128,128]{2,1,0:T(8,128)S(1)} %collective-permute-done.31.other_ref), custom_call_target="tpu_custom_call" | custom-call | bytes 60000000 | tf_op jit(solution)/shard_map/factor/pallas_call | solution.py:52
  (70 shorter events, 6.8 us)
Async XLA Ops:
  0.6 62.0 %collective-permute-start.4 = (bf16[8,128,768]{2,1,0:T(8,128)(2,1)}, bf16[8,128,768]{2,1,0:T(8,128)(2,1)}, u32[]{:S(2)}, u32[]{:S(2)}) collective-permute-start(bf16[8,128,768]{2,1,0:T(8,128)(2,1)} %bitcast.15), channel_id=1, source_target_pairs={{0,4},{4,0},{1,5},{5,1},{2,6},{6,2},{3,7},{7,3},{8,12},{12,8},{9,1... | collective-permute-start | bytes 4718600 | tf_op jit(solution)/shard_map/ppermute | solution.py:228
  16.0 14.9 %collective-permute-start = (bf16[8,64,512]{2,1,0:T(8,128)(2,1)S(1)}, bf16[8,64,512]{2,1,0:T(8,128)(2,1)}, u32[]{:S(2)}, u32[]{:S(2)}) collective-permute-start(bf16[8,64,512]{2,1,0:T(8,128)(2,1)S(1)} %reshape_squeeze.9.own_ref), channel_id=1, source_target_pairs={{0,1},{1,0},{2,3},{3,2},{4,5},{5,4},{6,7},{7,6},{8,9},{9,8},{10,11... | collective-permute-start | bytes 1572872 | tf_op jit(solution)/shard_map/ppermute | solution.py:230
  16.1 14.9 %collective-permute-start.1 = (bf16[8,64,512]{2,1,0:T(8,128)(2,1)S(1)}, bf16[8,64,512]{2,1,0:T(8,128)(2,1)}, u32[]{:S(2)}, u32[]{:S(2)}) collective-permute-start(bf16[8,64,512]{2,1,0:T(8,128)(2,1)S(1)} %reshape_squeeze.9.own_ref), channel_id=1, source_target_pairs={{0,2},{1,3},{2,0},{3,1},{4,6},{5,7},{6,4},{7,5},{8,10},{9,11},{10,... | collective-permute-start | bytes 1572872 | tf_op jit(solution)/shard_map/ppermute | solution.py:230
  18.3 23.7 %collective-permute-start.8 = (bf16[8,64,512]{2,1,0:T(8,128)(2,1)S(1)}, bf16[8,64,512]{2,1,0:T(8,128)(2,1)S(1)}, u32[]{:S(2)}, u32[]{:S(2)}) collective-permute-start(bf16[8,64,512]{2,1,0:T(8,128)(2,1)S(1)} %reshape_squeeze.10.own_ref), channel_id=1, source_target_pairs={{0,1},{1,0},{2,3},{3,2},{4,5},{5,4},{6,7},{7,6},{8,9},{9,8},{10,11... | collective-permute-start | bytes 1572872 | tf_op jit(solution)/shard_map/ppermute | solution.py:230
  19.9 23.7 %collective-permute-start.9 = (bf16[8,64,512]{2,1,0:T(8,128)(2,1)S(1)}, bf16[8,64,512]{2,1,0:T(8,128)(2,1)}, u32[]{:S(2)}, u32[]{:S(2)}) collective-permute-start(bf16[8,64,512]{2,1,0:T(8,128)(2,1)S(1)} %reshape_squeeze.10.own_ref), channel_id=1, source_target_pairs={{0,2},{1,3},{2,0},{3,1},{4,6},{5,7},{6,4},{7,5},{8,10},{9,11},{10,... | collective-permute-start | bytes 1572872 | tf_op jit(solution)/shard_map/ppermute | solution.py:230
  20.6 34.7 %copy-start.15 = (s32[1,8,6]{1,0,2:T(1,128)S(1)}, s32[1,8,6]{1,0,2:T(1,128)}, u32[]{:S(2)}) copy-start(s32[1,8,6]{1,0,2:T(1,128)} %param.8) | copy-start | bytes 580
  30.9 22.4 %collective-permute-start.15 = (bf16[8,64,512]{2,1,0:T(8,128)(2,1)S(1)}, bf16[8,64,512]{2,1,0:T(8,128)(2,1)S(1)}, u32[]{:S(2)}, u32[]{:S(2)}) collective-permute-start(bf16[8,64,512]{2,1,0:T(8,128)(2,1)S(1)} %reshape_squeeze.11.own_ref), channel_id=1, source_target_pairs={{0,1},{1,0},{2,3},{3,2},{4,5},{5,4},{6,7},{7,6},{8,9},{9,8},{10,11... | collective-permute-start | bytes 1572872 | tf_op jit(solution)/shard_map/ppermute | solution.py:230
  31.0 23.8 %collective-permute-start.16 = (bf16[8,64,512]{2,1,0:T(8,128)(2,1)S(1)}, bf16[8,64,512]{2,1,0:T(8,128)(2,1)S(1)}, u32[]{:S(2)}, u32[]{:S(2)}) collective-permute-start(bf16[8,64,512]{2,1,0:T(8,128)(2,1)S(1)} %reshape_squeeze.11.own_ref), channel_id=1, source_target_pairs={{0,2},{1,3},{2,0},{3,1},{4,6},{5,7},{6,4},{7,5},{8,10},{9,11},{10,... | collective-permute-start | bytes 1572872 | tf_op jit(solution)/shard_map/ppermute | solution.py:230
  36.4 26.2 %copy-start.12 = (s32[1,8,12]{2,1,0:T(8,128)S(1)}, s32[1,8,12]{2,1,0:T(8,128)}, u32[]{:S(2)}) copy-start(s32[1,8,12]{2,1,0:T(8,128)} %param.7) | copy-start | bytes 1156
  42.0 27.3 %copy-start.2 = (bf16[8,64,512]{2,1,0:T(8,128)(2,1)}, bf16[8,64,512]{2,1,0:T(8,128)(2,1)S(1)}, u32[]{:S(2)}) copy-start(bf16[8,64,512]{2,1,0:T(8,128)(2,1)S(1)} %collective-permute-done.8.x_ref) | copy-start | bytes 1572868
  42.0 17.0 %collective-permute-start.2 = (bf16[4,64,512]{2,1,0:T(8,128)(2,1)}, bf16[4,64,512]{2,1,0:T(8,128)(2,1)}, u32[]{:S(2)}, u32[]{:S(2)}) collective-permute-start(bf16[4,64,512]{2,1,0:T(8,128)(2,1)} %slice.37), channel_id=1, source_target_pairs={{0,2},{1,3},{2,0},{3,1},{4,6},{5,7},{6,4},{7,5},{8,10},{9,11},{10,... | collective-permute-start | bytes 786440 | tf_op jit(solution)/shard_map/ppermute | solution.py:236
  43.6 17.5 %collective-permute-start.3 = (bf16[4,64,512]{2,1,0:T(8,128)(2,1)}, bf16[4,64,512]{2,1,0:T(8,128)(2,1)}, u32[]{:S(2)}, u32[]{:S(2)}) collective-permute-start(bf16[4,64,512]{2,1,0:T(8,128)(2,1)} %slice.38), channel_id=1, source_target_pairs={{0,1},{1,0},{2,3},{3,2},{4,5},{5,4},{6,7},{7,6},{8,9},{9,8},{10,11... | collective-permute-start | bytes 786440 | tf_op jit(solution)/shard_map/ppermute | solution.py:237
  53.3 22.0 %collective-permute-start.10 = (bf16[4,64,512]{2,1,0:T(8,128)(2,1)}, bf16[4,64,512]{2,1,0:T(8,128)(2,1)S(1)}, u32[]{:S(2)}, u32[]{:S(2)}) collective-permute-start(bf16[4,64,512]{2,1,0:T(8,128)(2,1)} %slice.40), channel_id=1, source_target_pairs={{0,2},{1,3},{2,0},{3,1},{4,6},{5,7},{6,4},{7,5},{8,10},{9,11},{10,... | collective-permute-start | bytes 786440 | tf_op jit(solution)/shard_map/ppermute | solution.py:236
  54.8 7.8 %copy-start = (bf16[8,64,512]{2,1,0:T(8,128)(2,1)}, bf16[8,64,512]{2,1,0:T(8,128)(2,1)S(1)}, u32[]{:S(2)}) copy-start(bf16[8,64,512]{2,1,0:T(8,128)(2,1)S(1)} %collective-permute-done.16.y_ref) | copy-start | bytes 1572868
  54.8 25.1 %collective-permute-start.11 = (bf16[4,64,512]{2,1,0:T(8,128)(2,1)}, bf16[4,64,512]{2,1,0:T(8,128)(2,1)}, u32[]{:S(2)}, u32[]{:S(2)}) collective-permute-start(bf16[4,64,512]{2,1,0:T(8,128)(2,1)} %slice.41), channel_id=1, source_target_pairs={{0,1},{1,0},{2,3},{3,2},{4,5},{5,4},{6,7},{7,6},{8,9},{9,8},{10,11... | collective-permute-start | bytes 786440 | tf_op jit(solution)/shard_map/ppermute | solution.py:237
  59.1 30.3 %collective-permute-start.17 = (bf16[4,64,512]{2,1,0:T(8,128)(2,1)S(1)}, bf16[4,64,512]{2,1,0:T(8,128)(2,1)S(1)}, u32[]{:S(2)}, u32[]{:S(2)}) collective-permute-start(bf16[4,64,512]{2,1,0:T(8,128)(2,1)S(1)} %slice.43), channel_id=1, source_target_pairs={{0,2},{1,3},{2,0},{3,1},{4,6},{5,7},{6,4},{7,5},{8,10},{9,11},{10,... | collective-permute-start | bytes 786440 | tf_op jit(solution)/shard_map/ppermute | solution.py:236
  61.1 30.9 %collective-permute-start.18 = (bf16[4,64,512]{2,1,0:T(8,128)(2,1)S(1)}, bf16[4,64,512]{2,1,0:T(8,128)(2,1)S(1)}, u32[]{:S(2)}, u32[]{:S(2)}) collective-permute-start(bf16[4,64,512]{2,1,0:T(8,128)(2,1)S(1)} %slice.44), channel_id=1, source_target_pairs={{0,1},{1,0},{2,3},{3,2},{4,5},{5,4},{6,7},{7,6},{8,9},{9,8},{10,11... | collective-permute-start | bytes 786440 | tf_op jit(solution)/shard_map/ppermute | solution.py:237
  62.6 1.4 copy-start.4
  64.0 17.9 %copy-start.5 = (bf16[1,8,128,768]{3,2,1,0:T(8,128)(2,1)S(1)}, bf16[1,8,128,768]{3,2,1,0:T(8,128)(2,1)}, u32[]{:S(2)}) copy-start(bf16[1,8,128,768]{3,2,1,0:T(8,128)(2,1)} %param.6) | copy-start | bytes 4718596
  69.4 0.7 copy-start.6
  70.1 0.7 copy-start.8
  70.9 0.8 copy-start.10
  71.6 27.9 %copy-start.1 = (bf16[8,64,512]{2,1,0:T(8,128)(2,1)S(1)}, bf16[8,64,512]{2,1,0:T(8,128)(2,1)}, u32[]{:S(2)}) copy-start(bf16[8,64,512]{2,1,0:T(8,128)(2,1)} %copy-done) | copy-start | bytes 1572868
  71.6 25.9 %collective-permute-start.22 = (f32[2,128,128]{2,1,0:T(8,128)S(1)}, f32[2,128,128]{2,1,0:T(8,128)S(1)}, u32[]{:S(2)}, u32[]{:S(2)}) collective-permute-start(f32[2,128,128]{2,1,0:T(8,128)S(1)} %get-tuple-element.29.refs_0_), channel_id=1, source_target_pairs={{0,8},{1,9},{6,14},{7,15},{8,0},{9,1},{14,6},{15,7},{16,24},{17,25... | collective-permute-start | bytes 393224 | tf_op jit(solution)/shard_map/ppermute | solution.py:250
  75.3 30.4 %collective-permute-start.23 = (f32[2,128,128]{2,1,0:T(8,128)S(1)}, f32[2,128,128]{2,1,0:T(8,128)S(1)}, u32[]{:S(2)}, u32[]{:S(2)}) collective-permute-start(f32[2,128,128]{2,1,0:T(8,128)S(1)} %get-tuple-element.29.refs_0_), channel_id=1, source_target_pairs={{0,16},{1,17},{6,22},{7,23},{8,24},{9,25},{14,30},{15,31},{16,0},{... | collective-permute-start | bytes 393224 | tf_op jit(solution)/shard_map/ppermute | solution.py:250
  79.9 28.2 %collective-permute-start.24 = (f32[2,128,128]{2,1,0:T(8,128)S(1)}, f32[2,128,128]{2,1,0:T(8,128)S(1)}, u32[]{:S(2)}, u32[]{:S(2)}) collective-permute-start(f32[2,128,128]{2,1,0:T(8,128)S(1)} %get-tuple-element.29.refs_0_), channel_id=1, source_target_pairs={{0,24},{1,25},{6,30},{7,31},{8,16},{9,17},{14,22},{15,23},{16,8},{... | collective-permute-start | bytes 393224 | tf_op jit(solution)/shard_map/ppermute | solution.py:250
  81.9 1.0 copy-start.3
  89.4 22.0 %collective-permute-start.25 = (f32[2,128,128]{2,1,0:T(8,128)S(1)}, f32[2,128,128]{2,1,0:T(8,128)S(1)}, u32[]{:S(2)}, u32[]{:S(2)}) collective-permute-start(f32[2,128,128]{2,1,0:T(8,128)S(1)} %get-tuple-element.30.refs_4_), channel_id=1, source_target_pairs={{0,8},{1,9},{6,14},{7,15},{8,0},{9,1},{14,6},{15,7},{16,24},{17,25... | collective-permute-start | bytes 393224 | tf_op jit(solution)/shard_map/ppermute | solution.py:250
  92.0 20.0 %collective-permute-start.26 = (f32[2,128,128]{2,1,0:T(8,128)S(1)}, f32[2,128,128]{2,1,0:T(8,128)S(1)}, u32[]{:S(2)}, u32[]{:S(2)}) collective-permute-start(f32[2,128,128]{2,1,0:T(8,128)S(1)} %get-tuple-element.30.refs_4_), channel_id=1, source_target_pairs={{0,16},{1,17},{6,22},{7,23},{8,24},{9,25},{14,30},{15,31},{16,0},{... | collective-permute-start | bytes 393224 | tf_op jit(solution)/shard_map/ppermute | solution.py:250
  97.5 15.1 %collective-permute-start.27 = (f32[2,128,128]{2,1,0:T(8,128)S(1)}, f32[2,128,128]{2,1,0:T(8,128)S(1)}, u32[]{:S(2)}, u32[]{:S(2)}) collective-permute-start(f32[2,128,128]{2,1,0:T(8,128)S(1)} %get-tuple-element.30.refs_4_), channel_id=1, source_target_pairs={{0,24},{1,25},{6,30},{7,31},{8,16},{9,17},{14,22},{15,23},{16,8},{... | collective-permute-start | bytes 393224 | tf_op jit(solution)/shard_map/ppermute | solution.py:250
  105.7 13.8 %collective-permute-start.28 = (f32[2,128,128]{2,1,0:T(8,128)S(1)}, f32[2,128,128]{2,1,0:T(8,128)S(1)}, u32[]{:S(2)}, u32[]{:S(2)}) collective-permute-start(f32[2,128,128]{2,1,0:T(8,128)S(1)} %get-tuple-element.31.refs_8_), channel_id=1, source_target_pairs={{0,8},{1,9},{6,14},{7,15},{8,0},{9,1},{14,6},{15,7},{16,24},{17,25... | collective-permute-start | bytes 393224 | tf_op jit(solution)/shard_map/ppermute | solution.py:250
  108.1 70.8 %collective-permute-start.21 = (f32[128,768]{1,0:T(8,128)S(1)}, f32[128,768]{1,0:T(8,128)S(1)}, u32[]{:S(2)}, u32[]{:S(2)}) collective-permute-start(f32[128,768]{1,0:T(8,128)S(1)} %get-tuple-element.28), channel_id=1, source_target_pairs={{0,24},{8,16},{16,8},{24,0},{1,25},{9,17},{17,9},{25,1},{2,26},{10... | collective-permute-start | bytes 1179656 | tf_op jit(solution)/shard_map/ppermute | solution.py:252
  111.4 73.5 %collective-permute-start.20 = (f32[128,768]{1,0:T(8,128)}, f32[128,768]{1,0:T(8,128)}, u32[]{:S(2)}, u32[]{:S(2)}) collective-permute-start(f32[128,768]{1,0:T(8,128)} %get-tuple-element.27), channel_id=1, source_target_pairs={{0,16},{8,24},{16,0},{24,8},{1,17},{9,25},{17,1},{25,9},{2,18},{10... | collective-permute-start | bytes 1179656 | tf_op jit(solution)/shard_map/ppermute | solution.py:252
  112.0 73.1 %collective-permute-start.19 = (f32[128,768]{1,0:T(8,128)}, f32[128,768]{1,0:T(8,128)}, u32[]{:S(2)}, u32[]{:S(2)}) collective-permute-start(f32[128,768]{1,0:T(8,128)} %get-tuple-element.26), channel_id=1, source_target_pairs={{0,8},{8,0},{16,24},{24,16},{1,9},{9,1},{17,25},{25,17},{2,10},{10... | collective-permute-start | bytes 1179656 | tf_op jit(solution)/shard_map/ppermute | solution.py:252
  112.6 74.6 %collective-permute-start.14 = (f32[128,768]{1,0:T(8,128)}, f32[128,768]{1,0:T(8,128)}, u32[]{:S(2)}, u32[]{:S(2)}) collective-permute-start(f32[128,768]{1,0:T(8,128)} %get-tuple-element.24), channel_id=1, source_target_pairs={{0,24},{8,16},{16,8},{24,0},{1,25},{9,17},{17,9},{25,1},{2,26},{10... | collective-permute-start | bytes 1179656 | tf_op jit(solution)/shard_map/ppermute | solution.py:252
  119.5 50.7 %collective-permute-start.29 = (f32[2,128,128]{2,1,0:T(8,128)S(1)}, f32[2,128,128]{2,1,0:T(8,128)S(1)}, u32[]{:S(2)}, u32[]{:S(2)}) collective-permute-start(f32[2,128,128]{2,1,0:T(8,128)S(1)} %get-tuple-element.31.refs_8_), channel_id=1, source_target_pairs={{0,16},{1,17},{6,22},{7,23},{8,24},{9,25},{14,30},{15,31},{16,0},{... | collective-permute-start | bytes 393224 | tf_op jit(solution)/shard_map/ppermute | solution.py:250
  170.1 8.8 %collective-permute-start.30 = (f32[2,128,128]{2,1,0:T(8,128)S(1)}, f32[2,128,128]{2,1,0:T(8,128)S(1)}, u32[]{:S(2)}, u32[]{:S(2)}) collective-permute-start(f32[2,128,128]{2,1,0:T(8,128)S(1)} %get-tuple-element.31.refs_8_), channel_id=1, source_target_pairs={{0,24},{1,25},{6,30},{7,31},{8,16},{9,17},{14,22},{15,23},{16,8},{... | collective-permute-start | bytes 393224 | tf_op jit(solution)/shard_map/ppermute | solution.py:250
  178.9 13.3 %collective-permute-start.13 = (f32[128,768]{1,0:T(8,128)}, f32[128,768]{1,0:T(8,128)}, u32[]{:S(2)}, u32[]{:S(2)}) collective-permute-start(f32[128,768]{1,0:T(8,128)} %get-tuple-element.23), channel_id=1, source_target_pairs={{0,16},{8,24},{16,0},{24,8},{1,17},{9,25},{17,1},{25,9},{2,18},{10... | collective-permute-start | bytes 1179656 | tf_op jit(solution)/shard_map/ppermute | solution.py:252
  178.9 4.2 %copy-start.13 = (f32[128,768]{1,0:T(8,128)}, f32[128,768]{1,0:T(8,128)S(1)}, u32[]{:S(2)}) copy-start(f32[128,768]{1,0:T(8,128)S(1)} %collective-permute-done.21) | copy-start | bytes 1179652
  178.9 13.7 %collective-permute-start.12 = (f32[128,768]{1,0:T(8,128)}, f32[128,768]{1,0:T(8,128)}, u32[]{:S(2)}, u32[]{:S(2)}) collective-permute-start(f32[128,768]{1,0:T(8,128)} %get-tuple-element.22), channel_id=1, source_target_pairs={{0,8},{8,0},{16,24},{24,16},{1,9},{9,1},{17,25},{25,17},{2,10},{10... | collective-permute-start | bytes 1179656 | tf_op jit(solution)/shard_map/ppermute | solution.py:252
  183.1 1.8 copy-start.11
  183.1 2.1 copy-start.9
  183.1 4.1 %copy-start.7 = (f32[128,768]{1,0:T(8,128)S(1)}, f32[128,768]{1,0:T(8,128)}, u32[]{:S(2)}) copy-start(f32[128,768]{1,0:T(8,128)} %copy-done.6) | copy-start | bytes 1179652
  183.1 6.3 %copy-start.14 = (f32[128,768]{1,0:T(8,128)S(1)}, f32[128,768]{1,0:T(8,128)}, u32[]{:S(2)}) copy-start(f32[128,768]{1,0:T(8,128)} %copy-done.13) | copy-start | bytes 1179652
  184.9 12.2 %collective-permute-start.7 = (f32[128,768]{1,0:T(8,128)S(1)}, f32[128,768]{1,0:T(8,128)S(1)}, u32[]{:S(2)}, u32[]{:S(2)}) collective-permute-start(f32[128,768]{1,0:T(8,128)S(1)} %copy-done.11), channel_id=1, source_target_pairs={{0,24},{8,16},{16,8},{24,0},{1,25},{9,17},{17,9},{25,1},{2,26},{10... | collective-permute-start | bytes 1179656 | tf_op jit(solution)/shard_map/ppermute | solution.py:252
  185.1 23.7 %collective-permute-start.6 = (f32[128,768]{1,0:T(8,128)S(1)}, f32[128,768]{1,0:T(8,128)S(1)}, u32[]{:S(2)}, u32[]{:S(2)}) collective-permute-start(f32[128,768]{1,0:T(8,128)S(1)} %copy-done.9), channel_id=1, source_target_pairs={{0,16},{8,24},{16,0},{24,8},{1,17},{9,25},{17,1},{25,9},{2,18},{10... | collective-permute-start | bytes 1179656 | tf_op jit(solution)/shard_map/ppermute | solution.py:252
  187.2 21.7 %collective-permute-start.5 = (f32[128,768]{1,0:T(8,128)S(1)}, f32[128,768]{1,0:T(8,128)S(1)}, u32[]{:S(2)}, u32[]{:S(2)}) collective-permute-start(f32[128,768]{1,0:T(8,128)S(1)} %copy-done.7), channel_id=1, source_target_pairs={{0,8},{8,0},{16,24},{24,16},{1,9},{9,1},{17,25},{25,17},{2,10},{10... | collective-permute-start | bytes 1179656 | tf_op jit(solution)/shard_map/ppermute | solution.py:252
  192.2 19.3 %collective-permute-start.31 = (f32[6,128,128]{2,1,0:T(8,128)S(1)}, f32[6,128,128]{2,1,0:T(8,128)S(1)}, u32[]{:S(2)}, u32[]{:S(2)}) collective-permute-start(f32[6,128,128]{2,1,0:T(8,128)S(1)} %pivots.1.own_ref), channel_id=1, source_target_pairs={{0,4},{4,0},{1,5},{5,1},{2,6},{6,2},{3,7},{7,3},{8,12},{12,8},{9,1... | collective-permute-start | bytes 1179656 | tf_op jit(solution)/shard_map/ppermute | solution.py:255

commit v2 on v1

v2 whole, which is shorter than its diff:
```python
import functools

import jax
import jax.numpy as jnp
from jax import lax
from jax.experimental import pallas as pl
from jax.experimental.pallas import tpu as pltpu
from jax.sharding import PartitionSpec as P

BLK = 128
VMEM_LIMIT = 48 * 1024 * 1024
SMEM = pl.BlockSpec(memory_space=pltpu.SMEM)
VMEM = pl.BlockSpec(memory_space=pltpu.VMEM)
ANY = pl.BlockSpec(memory_space=pl.ANY)
CODE_TOP = 32500.0
EXP_STEPS = 128.0
EXP_ROWS = 16
WINDOW = 4
LARGE = pl.CostEstimate(flops=20_000_000_000, bytes_accessed=8_000_000, transcendentals=0)
SMALL = pl.CostEstimate(flops=1000, bytes_accessed=1000, transcendentals=0)


def params(**kwargs):
    return pltpu.CompilerParams(vmem_limit_bytes=VMEM_LIMIT, **kwargs)


def encode(block):
    top = jnp.max(jnp.abs(block), axis=0, keepdims=True)
    level = jnp.ceil(jnp.log2(jnp.maximum(top, 1e-30)) * EXP_STEPS) + 1.0
    codes = jnp.round(block * (CODE_TOP * jnp.exp2(level * (-1.0 / EXP_STEPS))))
    return codes.astype(jnp.int32).astype(jnp.int16), jnp.broadcast_to(
        level.astype(jnp.int32), (EXP_ROWS, block.shape[1])
    ).astype(jnp.int16)


def decode(codes, levels):
    level = levels.astype(jnp.int32).astype(jnp.float32)[:1]
    scale = jnp.exp2(level * (1.0 / EXP_STEPS)) * (1.0 / CODE_TOP)
    return codes.astype(jnp.int32).astype(jnp.float32) * scale


def lu_step(ref, j):
    size = ref.shape[1]
    top = j // 8 * 8
    row = ref[:, j : j + 1, :]
    inverse = 1.0 / row[:, :, j : j + 1]
    lanes = lax.broadcasted_iota(jnp.int32, (1, 1, size), 2)
    used = jnp.where(lanes > j, row, 0.0)
    if j % 8 != 7:
        head = ref[:, top : top + 8, :]
        rows = lax.broadcasted_iota(jnp.int32, (1, 8, 1), 1) + top
        factor = jnp.where(rows > j, head[:, :, j : j + 1] * inverse, 0.0)
        swept = head - factor * used
        ref[:, top : top + 8, :] = jnp.where((lanes == j) & (rows > j), factor, swept)
    if top + 8 < size:
        rest = ref[:, top + 8 :, :]
        factor = rest[:, :, j : j + 1] * inverse
        ref[:, top + 8 :, :] = jnp.where(lanes == j, factor, rest - factor * used)


def lu_kernel(where_ref, own_ref, other_ref, out_ref):
    held = where_ref[1] == where_ref[3]

    @pl.when(held)
    def _():
        out_ref[...] = own_ref[...]

    @pl.when(jnp.logical_not(held))
    def _():
        out_ref[...] = other_ref[...]

    for j in range(out_ref.shape[1]):
        lu_step(out_ref, j)


def factor(where, own, other):
    return pl.pallas_call(
        lu_kernel,
        out_shape=jax.ShapeDtypeStruct(own.shape, jnp.float32),
        in_specs=[SMEM, VMEM, VMEM],
        out_specs=VMEM,
        compiler_params=params(),
        cost_estimate=LARGE,
        name="factor",
    )(where, own, other)


def split_kernel(chunk, chunks, layers, lt_ref, *refs):
    outs, sems = refs[:-1], refs[-1]
    half = outs[0].shape[0]
    copies = []
    for h in range(len(outs)):
        for t in range(layers):
            begin = (t * chunks + chunk) * BLK
            copies.append(
                pltpu.make_async_copy(
                    lt_ref.at[h * half : (h + 1) * half, :, begin : begin + BLK],
                    outs[h].at[:, :, t * BLK : (t + 1) * BLK],
                    sems.at[h, t],
                )
            )
    for copy in copies:
        copy.start()
    for copy in copies:
        copy.wait()


def split(lt, chunk, chunks, layers):
    supers, depth, _ = lt.shape
    one = jax.ShapeDtypeStruct((supers // 2, depth, layers * BLK), lt.dtype)
    return pl.pallas_call(
        functools.partial(split_kernel, chunk, chunks, layers),
        out_shape=[one, one],
        in_specs=[ANY],
        out_specs=[ANY, ANY],
        scratch_shapes=[pltpu.SemaphoreType.DMA((2, layers))],
        compiler_params=params(),
        cost_estimate=SMALL,
        name="split",
    )(lt)


def right_kernel(where_ref, upat_ref, u_ref, uo_ref, out_ref, held, sems):
    row = where_ref[1]
    wide = u_ref.shape[1]
    copies = [
        pltpu.make_async_copy(
            ref, held.at[:, pl.ds(pl.multiple_of(spot * wide, wide), wide)], sems.at[n]
        )
        for n, (ref, spot) in enumerate(((u_ref, row), (uo_ref, 1 - row)))
    ]
    for copy in copies:
        copy.start()
    for copy in copies:
        copy.wait()
    for k in range(held.shape[0]):
        for n in range(held.shape[2] // BLK):

            @pl.when(upat_ref[k, n] == 0)
            def _():
                held[k, :, n * BLK : (n + 1) * BLK] = jnp.zeros((held.shape[1], BLK), held.dtype)

    back = pltpu.make_async_copy(held, out_ref, sems.at[2])
    back.start()
    back.wait()


def masked_right(where, upat, u, uo):
    supers, wide, cols = u.shape
    shape = (supers, 2 * wide, cols)
    return pl.pallas_call(
        right_kernel,
        out_shape=jax.ShapeDtypeStruct(shape, u.dtype),
        in_specs=[SMEM, SMEM, ANY, ANY],
        out_specs=ANY,
        scratch_shapes=[pltpu.VMEM(shape, u.dtype), pltpu.SemaphoreType.DMA((3,))],
        compiler_params=params(),
        cost_estimate=SMALL,
        name="masked_right",
    )(where, upat, u, uo)


def update_kernel(chunk, chunks, layers, last, where_ref, lpat_ref, *refs):
    pieces, right_ref = refs[:8], refs[8]
    kept_ref, diag_ref = refs[9:11]
    sent_refs, (left, right, acc, sems) = refs[11:-4], refs[-4:]
    layer, col = where_ref[0], where_ref[2]
    half, depth, _ = pieces[0].shape
    cols = right.shape[2]

    def slot(index):
        return pl.ds(pl.multiple_of(index * depth, depth), depth)

    waits = []
    for h in range(2):
        ks = pl.ds(h * half, half)
        items = [(right_ref.at[ks], right.at[ks])]
        items += [(pieces[2 * n + h], left.at[ks, slot(col ^ n)]) for n in range(4)]
        copies = [
            pltpu.make_async_copy(src, dst, sems.at[h, n]) for n, (src, dst) in enumerate(items)
        ]
        for copy in copies:
            copy.start()
        waits.append(copies)
    for h in range(2):
        for copy in waits[h]:
            copy.wait()
        for k in range(h * half, (h + 1) * half):
            for t in range(layers):

                @pl.when(lpat_ref[k, t * chunks + chunk] == 0)
                def _():
                    left[k, :, t * BLK : (t + 1) * BLK] = jnp.zeros(
                        (left.shape[1], BLK), left.dtype
                    )

        product = lax.dot_general(
            left[h * half : (h + 1) * half].reshape(-1, left.shape[2]),
            right[h * half : (h + 1) * half].reshape(-1, right.shape[2]),
            (((0,), (0,)), ((), ())),
            preferred_element_type=jnp.float32,
        ).reshape(acc.shape)
        if h == 0:
            acc[...] = product
        else:
            acc[...] += product
    for i in range(cols // BLK // chunks):
        q = i * chunks + chunk
        block = acc[where_ref[5] + i, :, q * BLK : (q + 1) * BLK]
        diag_ref[:BLK, i * BLK : (i + 1) * BLK], diag_ref[BLK:, i * BLK : (i + 1) * BLK] = encode(
            block
        )
    if last:
        for s in range(1, layers):
            sent_refs[s - 1][:BLK], sent_refs[s - 1][BLK:] = encode(acc[layer ^ s])
        kept_ref[...] = acc[layer]
    else:
        (sent_ref,) = sent_refs
        for n, s in enumerate((1, 3)):
            sent_ref[:BLK, n * cols : (n + 1) * cols], sent_ref[BLK:, n * cols : (n + 1) * cols] = (
                encode(acc[layer ^ s])
            )
        sent_ref[:, 2 * cols :] = diag_ref[...]
        kept_ref[0] = acc[layer]
        kept_ref[1] = acc[layer ^ 2]


def chunk_update(where, lpat, pieces, right, chunk, chunks, layers):
    half, _, width = pieces[0].shape
    supers, kdim, cols = right.shape
    beside = cols // chunks
    coded = BLK + EXP_ROWS
    last = chunk == chunks - 1
    if last:
        kept = (BLK, cols)
        sent = [(coded, cols)] * (layers - 1)
    else:
        kept = (2, BLK, cols)
        sent = [(coded, 2 * cols + beside)]
    return pl.pallas_call(
        functools.partial(update_kernel, chunk, chunks, layers, last),
        out_shape=[
            jax.ShapeDtypeStruct(kept, jnp.float32),
            jax.ShapeDtypeStruct((coded, beside), jnp.int16),
        ]
        + [jax.ShapeDtypeStruct(shape, jnp.int16) for shape in sent],
        in_specs=[SMEM] * 2 + [ANY] * 9,
        out_specs=[VMEM] * (2 + len(sent)),
        scratch_shapes=[
            pltpu.VMEM((supers, kdim, width), jnp.bfloat16),
            pltpu.VMEM((supers, kdim, cols), jnp.bfloat16),
            pltpu.VMEM((layers, BLK, cols), jnp.float32),
            pltpu.SemaphoreType.DMA((2, 5)),
        ],
        compiler_params=params(),
        cost_estimate=LARGE,
        name="update",
    )(where, lpat, *pieces, right)


def halve_kernel(kept_ref, diag_ref, got_ref, sum_ref, sent_ref):
    cols = sum_ref.shape[1]
    sum_ref[...] = kept_ref[0] + decode(got_ref[:BLK, :cols], got_ref[BLK:, :cols])
    other = kept_ref[1] + decode(got_ref[:BLK, cols : 2 * cols], got_ref[BLK:, cols : 2 * cols])
    sent_ref[:BLK, :cols], sent_ref[BLK:, :cols] = encode(other)
    diag = decode(diag_ref[:BLK], diag_ref[BLK:])
    diag += decode(got_ref[:BLK, 2 * cols :], got_ref[BLK:, 2 * cols :])
    sent_ref[:BLK, cols:], sent_ref[BLK:, cols:] = encode(diag)


def halve(kept, diag, got):
    cols = kept.shape[2]
    beside = diag.shape[1]
    return pl.pallas_call(
        halve_kernel,
        out_shape=[
            jax.ShapeDtypeStruct((BLK, cols), jnp.float32),
            jax.ShapeDtypeStruct((BLK + EXP_ROWS, cols + beside), jnp.int16),
        ],
        in_specs=[VMEM] * 3,
        out_specs=[VMEM] * 2,
        compiler_params=params(),
        cost_estimate=SMALL,
        name="halve",
    )(kept, diag, got)


def combine_kernel(chunk, codes, held, where_ref, anc_ref, kept_ref, *refs):
    got = refs[:codes]
    out_ref, start, result, sems = refs[codes + held :]
    cols = kept_ref.shape[1]
    share = out_ref.shape[0]
    begin = pl.multiple_of(where_ref[0] * share + chunk * BLK, BLK)
    fetch = pltpu.make_async_copy(anc_ref.at[pl.ds(begin, BLK)], start, sems.at[0])
    fetch.start()
    total = kept_ref[...]
    for ref in got:
        total += decode(ref[:BLK, :cols], ref[BLK:, :cols])
    fetch.wait()
    result[...] = start[...] - total
    back = pltpu.make_async_copy(
        result, out_ref.at[chunk * BLK : (chunk + 1) * BLK], sems.at[1]
    )
    back.start()
    back.wait()


def combine(where, anc, kept, got, held, share, chunk):
    cols = kept.shape[1]
    codes = len(got)
    return pl.pallas_call(
        functools.partial(combine_kernel, chunk, codes, len(held)),
        out_shape=jax.ShapeDtypeStruct((share, cols), jnp.float32),
        in_specs=[SMEM, ANY] + [VMEM] * (1 + codes) + [ANY] * len(held),
        out_specs=ANY,
        scratch_shapes=[
            pltpu.VMEM((BLK, cols), jnp.float32),
            pltpu.VMEM((BLK, cols), jnp.float32),
            pltpu.SemaphoreType.DMA((2,)),
        ],
        input_output_aliases={3 + codes: 0} if held else {},
        compiler_params=params(),
        cost_estimate=SMALL,
        name="combine",
    )(where, anc, kept, *got, *held)


def pivot_kernel(groups, where_ref, anc_ref, *refs):
    parts, (out_ref, blocks, sems) = refs[:-3], refs[-3:]
    copies = []
    for q in range(out_ref.shape[0]):
        rows = pl.ds(pl.multiple_of(where_ref[4] + q * BLK, BLK), BLK)
        copies.append(
            pltpu.make_async_copy(
                anc_ref.at[rows, q * BLK : (q + 1) * BLK], blocks.at[q], sems.at[q]
            )
        )
    for copy in copies:
        copy.start()
    for copy in copies:
        copy.wait()
    fresh = out_ref.shape[0] // len(groups)
    taken = 0
    for j, size in enumerate(groups):
        terms = []
        for ref in parts[taken : taken + size]:
            begin = ref.shape[1] - fresh * BLK
            terms.append(decode(ref[:BLK, begin:], ref[BLK:, begin:]))
        taken += size
        while len(terms) > 1:
            terms = [terms[i] + terms[i + 1] for i in range(0, len(terms), 2)]
        for i in range(fresh):
            q = i * len(groups) + j
            out_ref[q] = blocks[q] - terms[0][:, i * BLK : (i + 1) * BLK]


def pivots(where, anc, groups, count):
    parts = [part for group in groups for part in group]
    return pl.pallas_call(
        functools.partial(pivot_kernel, [len(group) for group in groups]),
        out_shape=jax.ShapeDtypeStruct((count, BLK, BLK), jnp.float32),
        in_specs=[SMEM, ANY] + [VMEM] * len(parts),
        out_specs=VMEM,
        scratch_shapes=[
            pltpu.VMEM((count, BLK, BLK), jnp.float32),
            pltpu.SemaphoreType.DMA((count,)),
        ],
        compiler_params=params(),
        cost_estimate=SMALL,
        name="pivots",
    )(where, anc, *parts)


def xor_perm(size, bit):
    return [(i, i ^ bit) for i in range(size)]


def after(value, *others):
    return lax.optimization_barrier((value, *others))[0]


def planned(lpanel, upanel, lpat, upat, anc):
    layers, rows, cols = (lax.axis_size(n) for n in ("layer", "row", "col"))
    layer, row, col = (lax.axis_index(n) for n in ("layer", "row", "col"))
    width = anc.shape[1]
    share = anc.shape[0] // layers
    chunks = share // BLK
    per_group = cols // rows
    where = jnp.stack(
        [
            layer,
            row,
            col,
            col // per_group,
            col % per_group * width,
            col % per_group * (width // share),
        ]
    ).astype(jnp.int32)
    everyone = ("layer", "row", "col")

    def index(l, r, c):
        return (l * rows + r) * cols + c

    def from_holders(value, target):
        perm = [
            (index(l, c // per_group, c), target(l, c // per_group, c))
            for l in range(layers)
            for c in range(cols)
        ]
        return lax.ppermute(value, everyone, perm)

    def over_layers(value, s):
        return lax.ppermute(value, "layer", xor_perm(layers, s))

    lt = jnp.swapaxes(lpanel[0], 1, 2)
    u = upanel[0]
    uo = lax.ppermute(u, "row", xor_perm(rows, 1))
    right = masked_right(where, upat[0], u, uo)
    moved = []
    gates = {}

    def over(value, bit):
        spot = len(moved)
        waits = list(gates.get(spot, ()))
        if spot >= WINDOW:
            waits.append(moved[spot - WINDOW])
        if waits:
            value = after(value, *waits)
        moved.append(lax.ppermute(value, "col", xor_perm(cols, bit)))
        return moved[-1]

    def gathered_chunk(j):
        a, b = split(lt, j, chunks, layers)
        xa = over(a, 1)
        yb = over(b, 2)
        xb = over(b, 1)
        ya = over(a, 2)
        da = over(xa, 2)
        db = over(yb, 1)
        return a, b, xa, xb, ya, yb, da, db

    pieces = gathered_chunk(0)
    held, groups, waits = [], [], []
    for j in range(chunks):
        out = chunk_update(where, lpat[0], pieces, after(right, *waits), j, chunks, layers)
        kept, diag = out[:2]
        if j < chunks - 1:
            gates[len(moved) + 4] = (kept,)
            pieces = gathered_chunk(j + 1)
            near = over_layers(out[2], 1)
            kept, sent = halve(kept, diag, near)
            got = [over_layers(sent, 2)]
            groups.append([sent, got[0]])
            waits = [sent] + held
            held = [combine(where, anc, kept, got, held, share, j)]
    steps = range(1, layers)
    parts = [from_holders(diag, lambda l, r, c, s=s: index(l ^ s, r, c)) for s in steps]
    got = [over_layers(after(out[1 + s], parts[-1]) if s > 1 else out[1 + s], s) for s in steps]
    groups.append([diag] + parts)
    own = pivots(where, anc, groups, width // BLK)
    other = from_holders(own, lambda l, r, c: index(l, 1 - r, c))
    diag_lu = factor(where, own, other)
    held = combine(where, anc, after(kept, diag_lu), got, held, share, chunks - 1)
    return held, diag_lu


def mask_rows(panel, pattern, block):
    count, length, inner = panel.shape
    shaped = panel.reshape(count, length // block, block, inner)
    return (shaped * pattern[:, :, None, None].astype(panel.dtype)).reshape(count, length, inner)


def mask_cols(panel, pattern, block):
    count, inner, length = panel.shape
    shaped = panel.reshape(count, inner, length // block, block)
    return (shaped * pattern[:, None, :, None].astype(panel.dtype)).reshape(count, inner, length)


def candidates(matrix):
    width = matrix.shape[1]
    per_group = lax.axis_size("col") // lax.axis_size("row")
    begin = lax.axis_index("col") % per_group * width
    square = lax.dynamic_slice_in_dim(matrix, begin, width, 0)
    count = width // BLK
    return jnp.stack(
        [square[j * BLK : (j + 1) * BLK, j * BLK : (j + 1) * BLK] for j in range(count)]
    )


def gathered(lpanel, upanel, lpat, upat, anc):
    left = mask_rows(lpanel[0], lpat[0], BLK)
    right = mask_cols(upanel[0], upat[0], BLK)
    update = jnp.einsum(
        "kmw,kwn->mn",
        lax.all_gather(left, "col", axis=2, tiled=True),
        lax.all_gather(right, "row", axis=1, tiled=True),
        preferred_element_type=jnp.float32,
    )
    rows = lax.axis_size("row")
    per_group = lax.axis_size("col") // rows
    share = anc.shape[0] // lax.axis_size("layer")
    pivot_blocks = candidates(anc) - lax.psum(candidates(update), "layer")
    both = lax.all_gather(pivot_blocks, "row", axis=0)
    chosen = lax.dynamic_index_in_dim(both, lax.axis_index("col") // per_group, 0, keepdims=False)
    where = jnp.zeros((6,), jnp.int32)
    diag_lu = factor(where, chosen, chosen)
    summed = lax.psum_scatter(update, "layer", scatter_dimension=0, tiled=True)
    mine = lax.dynamic_slice_in_dim(anc, lax.axis_index("layer") * share, share, 0)
    return mine - summed, diag_lu


def shards(lpanel, upanel, lpat, upat, anc):
    layers, rows, cols = (lax.axis_size(n) for n in ("layer", "row", "col"))
    fits = rows == 2 and cols == 4 and layers == 4
    share, extra = divmod(anc.shape[0], layers * BLK)
    blocks = anc.shape[1] // BLK
    if fits and extra == 0 and share > 1 and blocks % share == 0 and lpanel.shape[1] % 2 == 0:
        return planned(lpanel, upanel, lpat, upat, anc)
    return gathered(lpanel, upanel, lpat, upat, anc)


def solution(mesh):
    return jax.shard_map(
        shards,
        mesh=mesh,
        in_specs=(
            P("layer", None, "row", "col"),
            P("layer", None, "row", "col"),
            P("layer", None, "row"),
            P("layer", None, "col"),
            P("row", "col"),
        ),
        out_specs=(P(("row", "layer"), "col"), P("col", None, None)),
        check_vma=False,
    )
```

time: 228 us -> 115 us (0.50)
  waiting for transfers between devices: 89.4 us -> 27.4 us
  starting transfers between devices: 70 us -> 41.1 us
  local copies, waits for them, and re-layouts: 26.4 us -> 2.31 us
  Pallas kernels: 33.6 us -> 41 us
  other arithmetic: 5.1 us -> 0.01 us
    ppermute x32 -> x30, waiting for transfers between devices: 89.4 us -> 27.4 us  [the longest x18 14.6 us: over(): moved.append(lax.ppermute(value, 'col', xor_perm(cols, bit)))]
    ppermute x32 -> x30, starting transfers between devices: 70 us -> 41.1 us  [the longest x18 19.8 us: over(): moved.append(lax.ppermute(value, 'col', xor_perm(cols, bit)))]
    slice x7 -> x0, local copies, waits for them, and re-layouts: 15.3 us -> none  [the longest x1 9.45 us: planned(): cut[:, :, :, j, :].reshape(supers, depth, layers * BLK)]
    pallas_call x4 -> x13, Pallas kernels: 19.6 us -> 27.1 us  [the longest x3 15.5 us: chunk_update(): pl.pallas_call(functools.partial(update_kernel, chunk, chunks, layers, la...]
    reshape x1 -> x0, local copies, waits for them, and re-layouts: 4.6 us -> none  [planned(): cut = lt.reshape(supers, depth, layers, chunks, BLK)]
    add x3 -> x0, other arithmetic: 2.65 us -> none  [planned(): total = total + lax.ppermute(out[1 + s], 'layer', xor_perm(layers, s))]
    unnamed x33 -> x23, local copies, waits for them, and re-layouts: 4.8 us -> 2.23 us
    sub x1 -> x0, other arithmetic: 2.45 us -> none  [planned(): schur = mine - jnp.concatenate(kept, axis=0)]
  transfers between devices with their start and end apart: 32 -> 30, of which waited for: 11 -> 9; matrix products, arithmetic and copies ran while one was open for 12% -> 0% of each run, Pallas kernels for 9% -> 33%
where the time goes in v2:
time: 115 us; the launch traced here: 113 us
  starting transfers between devices  41.1 us (36%)
  Pallas kernels  41 us (36%)
  waiting for transfers between devices  27.4 us (24%)
  local copies, waits for them, and re-layouts  2.31 us (2%)
    ppermute x18, starting transfers between devices, over(): moved.append(lax.ppermute(value, 'col', xor_perm(cols, bit)))  19.8 us
    pallas_call x3, Pallas kernels, chunk_update(): pl.pallas_call(functools.partial(update_kernel, chunk, chunks, layers, la...  15.5 us
    ppermute x18, waiting for transfers between devices, over(): moved.append(lax.ppermute(value, 'col', xor_perm(cols, bit)))  14.6 us
    pallas_call x1, Pallas kernels, factor(): pl.pallas_call(lu_kernel, out_shape=jax.ShapeDtypeStruct(own.shape, jnp.f...  13.9 us
    ppermute x4, starting transfers between devices, from_holders(): return lax.ppermute(value, everyone, perm)  11.4 us
    ppermute x7, starting transfers between devices, over_layers(): return lax.ppermute(value, 'layer', xor_perm(layers, s))  9.83 us
    ppermute x7, waiting for transfers between devices, over_layers(): return lax.ppermute(value, 'layer', xor_perm(layers, s))  7.81 us
    pallas_call x3, Pallas kernels, combine(): pl.pallas_call(functools.partial(combine_kernel, chunk, codes, len(held))...  5.1 us
  transfers between devices with their start and end apart: 30, of which 9 were waited for; matrix products, arithmetic and copies ran while one was open for 0% of the time, Pallas kernels for 33%

profile of v2, /device:TPU:2, one launch (start us, length us, event | category | flops | bytes accessed | tf_op | source)
XLA Modules:
  0.0 112.9 jit_solution(9279101764267069376)
XLA Ops:
  0.7 1.4 %copy-done = bf16[1,8,1536,64]{2,3,1,0:T(8,128)(2,1)S(1)} copy-done((bf16[1,8,1536,64]{2,3,1,0:T(8,128)(2,1)S(1)}, bf16[1,8,1536,64]{2,3,1,0:T(8,128)(2,1)}, u32[]{:S(2)}) %copy-start) | copy-done | bytes 1572888
  2.1 0.9 split.5
  3.1 2.0 %collective-permute-start.7 = (bf16[4,64,512]{2,1,0:T(8,128)(2,1)}, bf16[4,64,512]{2,1,0:T(8,128)(2,1)}, u32[]{:S(2)}, u32[]{:S(2)}) collective-permute-start(bf16[4,64,512]{2,1,0:T(8,128)(2,1)} %get-tuple-element.50.refs_1_), channel_id=1, source_target_pairs={{0,2},{1,3},{2,0},{3,1},{4,6},{5,7},{6,4},{7,5},{8,10},{9,11},{10,... | collective-permute-start | bytes 786440 | tf_op jit(solution)/shard_map/ppermute | solution.py:429
  5.1 1.5 %collective-permute-start.4 = (bf16[4,64,512]{2,1,0:T(8,128)(2,1)}, bf16[4,64,512]{2,1,0:T(8,128)(2,1)}, u32[]{:S(2)}, u32[]{:S(2)}) collective-permute-start(bf16[4,64,512]{2,1,0:T(8,128)(2,1)} %get-tuple-element.50.refs_1_), channel_id=1, source_target_pairs={{0,1},{1,0},{2,3},{3,2},{4,5},{5,4},{6,7},{7,6},{8,9},{9,8},{10,11... | collective-permute-start | bytes 786440 | tf_op jit(solution)/shard_map/ppermute | solution.py:429
  6.6 0.5 collective-permute-start.6
  7.1 5.4 %collective-permute-done.refs_2_ = bf16[4,64,512]{2,1,0:T(8,128)(2,1)} collective-permute-done((bf16[4,64,512]{2,1,0:T(8,128)(2,1)}, bf16[4,64,512]{2,1,0:T(8,128)(2,1)}, u32[]{:S(2)}, u32[]{:S(2)}) %collective-permute-start) | collective-permute-done | bytes 262176 | tf_op jit(solution)/shard_map/ppermute | solution.py:429
  12.5 1.5 %collective-permute-start.1 = (bf16[4,64,512]{2,1,0:T(8,128)(2,1)}, bf16[4,64,512]{2,1,0:T(8,128)(2,1)}, u32[]{:S(2)}, u32[]{:S(2)}) collective-permute-start(bf16[4,64,512]{2,1,0:T(8,128)(2,1)} %collective-permute-done.refs_2_), channel_id=1, source_target_pairs={{0,2},{1,3},{2,0},{3,1},{4,6},{5,7},{6,4},{7,5},{8,10},{9,11},{10,... | collective-permute-start | bytes 786440 | tf_op jit(solution)/shard_map/ppermute | solution.py:429
  14.0 0.5 collective-permute-start.8
  14.7 0.7 copy-done.3
  15.6 2.5 %collective-permute-done.4.refs_3_ = bf16[4,64,512]{2,1,0:T(8,128)(2,1)} collective-permute-done((bf16[4,64,512]{2,1,0:T(8,128)(2,1)}, bf16[4,64,512]{2,1,0:T(8,128)(2,1)}, u32[]{:S(2)}, u32[]{:S(2)}) %collective-permute-start.4) | collective-permute-done | bytes 262176 | tf_op jit(solution)/shard_map/ppermute | solution.py:429
  18.2 2.0 %collective-permute-start.12 = (bf16[4,64,512]{2,1,0:T(8,128)(2,1)}, bf16[4,64,512]{2,1,0:T(8,128)(2,1)S(1)}, u32[]{:S(2)}, u32[]{:S(2)}) collective-permute-start(bf16[4,64,512]{2,1,0:T(8,128)(2,1)} %copy-done.3), channel_id=1, source_target_pairs={{0,2},{1,3},{2,0},{3,1},{4,6},{5,7},{6,4},{7,5},{8,10},{9,11},{10,... | collective-permute-start | bytes 786440 | tf_op jit(solution)/shard_map/ppermute | solution.py:429
  20.2 2.9 %masked_right.1.refs_8_ = bf16[8,256,768]{2,1,0:T(8,128)(2,1)} custom-call(s32[6]{0:T(128)S(1)} %stack.27.where_ref, s32[8,6]{1,0:T(8,128)S(1)} %bitcast.21, bf16[8,128,768]{2,1,0:T(8,128)(2,1)S(1)} %bitcast.20, bf16[8,128,768]{2,1,0:T(8,128)(2,1)S(1)} %collective-permute-done.9.uo_ref), custom_call_target="tpu_custom_call" | custom-call | flops 1000 | bytes 1000 | tf_op jit(solution)/shard_map/masked_right/pallas_call | solution.py:151
  23.1 0.7 collective-permute-done.1.refs_6_
  23.8 5.2 %update.3 = (f32[2,128,768]{2,1,0:T(8,128)S(1)}, s16[144,256]{1,0:T(8,128)(2,1)S(1)}, s16[144,1792]{1,0:T(8,128)(2,1)S(1)}) custom-call(s32[6]{0:T(128)S(1)} %stack.27.where_ref, s32[8,12]{1,0:T(8,128)S(1)} %bitcast.22, bf16[4,64,512]{2,1,0:T(8,128)(2,1)} %get-tuple-element.45.refs_0_, bf16[4,64,512]{2,1,0:T(8,128)(2,1)} %get-tuple-element.50.refs_1_, ...), custom_call_target="tpu_custom_call" | custom-call | flops 20000000000 | bytes 8000000 | tf_op jit(solution)/shard_map/update/pallas_call | solution.py:240
  29.0 2.2 %collective-permute-start.17 = (s16[144,1792]{1,0:T(8,128)(2,1)S(1)}, s16[144,1792]{1,0:T(8,128)(2,1)S(1)}, u32[]{:S(2)}, u32[]{:S(2)}) collective-permute-start(s16[144,1792]{1,0:T(8,128)(2,1)S(1)} %get-tuple-element.62), channel_id=1, source_target_pairs={{0,8},{8,0},{16,24},{24,16},{1,9},{9,1},{17,25},{25,17},{2,10},{10... | collective-permute-start | bytes 1548296 | tf_op jit(solution)/shard_map/ppermute | solution.py:413
  31.2 1.5 %collective-permute-start.2 = (bf16[4,64,512]{2,1,0:T(8,128)(2,1)S(1)}, bf16[4,64,512]{2,1,0:T(8,128)(2,1)S(1)}, u32[]{:S(2)}, u32[]{:S(2)}) collective-permute-start(bf16[4,64,512]{2,1,0:T(8,128)(2,1)S(1)} %copy-done.4), channel_id=1, source_target_pairs={{0,1},{1,0},{2,3},{3,2},{4,5},{5,4},{6,7},{7,6},{8,9},{9,8},{10,11... | collective-permute-start | bytes 786440 | tf_op jit(solution)/shard_map/ppermute | solution.py:429
  32.7 1.5 %collective-permute-start.15 = (bf16[4,64,512]{2,1,0:T(8,128)(2,1)S(1)}, bf16[4,64,512]{2,1,0:T(8,128)(2,1)S(1)}, u32[]{:S(2)}, u32[]{:S(2)}) collective-permute-start(bf16[4,64,512]{2,1,0:T(8,128)(2,1)S(1)} %get-tuple-element.59.refs_0_), channel_id=1, source_target_pairs={{0,2},{1,3},{2,0},{3,1},{4,6},{5,7},{6,4},{7,5},{8,10},{9,11},{10,... | collective-permute-start | bytes 786440 | tf_op jit(solution)/shard_map/ppermute | solution.py:429
  34.2 0.5 collective-permute-start.13
  34.7 0.5 collective-permute-start.10
  35.4 5.0 %collective-permute-done.2.refs_3_ = bf16[4,64,512]{2,1,0:T(8,128)(2,1)S(1)} collective-permute-done((bf16[4,64,512]{2,1,0:T(8,128)(2,1)S(1)}, bf16[4,64,512]{2,1,0:T(8,128)(2,1)S(1)}, u32[]{:S(2)}, u32[]{:S(2)}) %collective-permute-start.2) | collective-permute-done | bytes 262176 | tf_op jit(solution)/shard_map/ppermute | solution.py:429
  40.4 1.5 %collective-permute-start.3 = (bf16[4,64,512]{2,1,0:T(8,128)(2,1)S(1)}, bf16[4,64,512]{2,1,0:T(8,128)(2,1)S(1)}, u32[]{:S(2)}, u32[]{:S(2)}) collective-permute-start(bf16[4,64,512]{2,1,0:T(8,128)(2,1)S(1)} %get-tuple-element.58.refs_0_), channel_id=1, source_target_pairs={{0,1},{1,0},{2,3},{3,2},{4,5},{5,4},{6,7},{7,6},{8,9},{9,8},{10,11... | collective-permute-start | bytes 786440 | tf_op jit(solution)/shard_map/ppermute | solution.py:429
  41.9 1.5 %collective-permute-start.16 = (bf16[4,64,512]{2,1,0:T(8,128)(2,1)S(1)}, bf16[4,64,512]{2,1,0:T(8,128)(2,1)S(1)}, u32[]{:S(2)}, u32[]{:S(2)}) collective-permute-start(bf16[4,64,512]{2,1,0:T(8,128)(2,1)S(1)} %get-tuple-element.60.refs_1_), channel_id=1, source_target_pairs={{0,2},{1,3},{2,0},{3,1},{4,6},{5,7},{6,4},{7,5},{8,10},{9,11},{10,... | collective-permute-start | bytes 786440 | tf_op jit(solution)/shard_map/ppermute | solution.py:429
  43.5 0.3 halve.2
  43.8 2.6 %collective-permute-start.21 = (s16[144,1024]{1,0:T(8,128)(2,1)S(1)}, s16[144,1024]{1,0:T(8,128)(2,1)S(1)}, u32[]{:S(2)}, u32[]{:S(2)}) collective-permute-start(s16[144,1024]{1,0:T(8,128)(2,1)S(1)} %get-tuple-element.63.refs_0_), channel_id=1, source_target_pairs={{0,16},{8,24},{16,0},{24,8},{1,17},{9,25},{17,1},{25,9},{2,18},{10... | collective-permute-start | bytes 884744 | tf_op jit(solution)/shard_map/ppermute | solution.py:413
  46.4 1.0 collective-permute-done.10.refs_6_
  47.4 5.0 %update.4 = (f32[2,128,768]{2,1,0:T(8,128)S(1)}, s16[144,256]{1,0:T(8,128)(2,1)S(1)}, s16[144,1792]{1,0:T(8,128)(2,1)S(1)}) custom-call(s32[6]{0:T(128)S(1)} %stack.27.where_ref, s32[8,12]{1,0:T(8,128)S(1)} %bitcast.23, bf16[4,64,512]{2,1,0:T(8,128)(2,1)S(1)} %get-tuple-element.59.refs_0_, bf16[4,64,512]{2,1,0:T(8,128)(2,1)S(1)} %copy-done.4, ...), custom_call_target="tpu_custom_call" | custom-call | flops 20000000000 | bytes 8000000 | tf_op jit(solution)/shard_map/update/pallas_call | solution.py:240
  52.4 0.5 collective-permute-start.20
  52.9 1.5 %collective-permute-start.14 = (bf16[4,64,512]{2,1,0:T(8,128)(2,1)S(1)}, bf16[4,64,512]{2,1,0:T(8,128)(2,1)S(1)}, u32[]{:S(2)}, u32[]{:S(2)}) collective-permute-start(bf16[4,64,512]{2,1,0:T(8,128)(2,1)S(1)} %get-tuple-element.58.refs_0_), channel_id=1, source_target_pairs={{0,2},{1,3},{2,0},{3,1},{4,6},{5,7},{6,4},{7,5},{8,10},{9,11},{10,... | collective-permute-start | bytes 786440 | tf_op jit(solution)/shard_map/ppermute | solution.py:429
  54.4 0.6 collective-permute-start.19
  55.0 1.4 %collective-permute-start.11 = (bf16[4,64,512]{2,1,0:T(8,128)(2,1)S(1)}, bf16[4,64,512]{2,1,0:T(8,128)(2,1)S(1)}, u32[]{:S(2)}, u32[]{:S(2)}) collective-permute-start(bf16[4,64,512]{2,1,0:T(8,128)(2,1)S(1)} %get-tuple-element.60.refs_1_), channel_id=1, source_target_pairs={{0,1},{1,0},{2,3},{3,2},{4,5},{5,4},{6,7},{7,6},{8,9},{9,8},{10,11... | collective-permute-start | bytes 786440 | tf_op jit(solution)/shard_map/ppermute | solution.py:429
  56.5 0.6 collective-permute-done.21.refs_0_.refs_1_
  57.0 0.9 collective-permute-start.18
  57.9 1.6 %combine.3.refs_1_ = f32[384,768]{1,0:T(8,128)} custom-call(s32[6]{0:T(128)S(1)} %stack.27.where_ref, f32[1536,768]{1,0:T(8,128)S(1)} %bitcast.13, f32[128,768]{1,0:T(8,128)S(1)} %get-tuple-element.71.kept_ref, s16[144,1024]{1,0:T(8,128)(2,1)S(1)} %collective-permute-done.21.refs_0_.refs_1_), custom_call_target="tpu_custom_call" | custom-call | flops 1000 | bytes 1000 | tf_op jit(solution)/shard_map/combine/pallas_call | solution.py:311
  59.6 7.2 %collective-permute-done.20.got_ref = s16[144,1792]{1,0:T(8,128)(2,1)S(1)} collective-permute-done((s16[144,1792]{1,0:T(8,128)(2,1)S(1)}, s16[144,1792]{1,0:T(8,128)(2,1)S(1)}, u32[]{:S(2)}, u32[]{:S(2)}) %collective-permute-start.20) | collective-permute-done | bytes 516128 | tf_op jit(solution)/shard_map/ppermute | solution.py:413
  66.8 0.3 halve.3
  67.3 5.4 %update.5 = (f32[128,768]{1,0:T(8,128)S(1)}, s16[144,256]{1,0:T(8,128)(2,1)S(1)}, s16[144,768]{1,0:T(8,128)(2,1)S(1)}, s16[144,768]{1,0:T(8,128)(2,1)S(1)}, s16[144,768]{1,0:T(8,128)(2,1)S(1)}) custom-call(s32[6]{0:T(128)S(1)} %stack.27.where_ref, s32[8,12]{1,0:T(8,128)S(1)} %bitcast.24, bf16[4,64,512]{2,1,0:T(8,128)(2,1)S(1)} %get-tuple-element.58.refs_0_, ...), custom_call_target="tpu_custom_call" | custom-call | flops 20000000000 | bytes 8000000 | tf_op jit(solution)/shard_map/update/pallas_call | solution.py:240
  72.6 3.3 %collective-permute-start.23 = (s16[144,256]{1,0:T(8,128)(2,1)S(1)}, s16[144,256]{1,0:T(8,128)(2,1)S(1)}, u32[]{:S(2)}, u32[]{:S(2)}) collective-permute-start(s16[144,256]{1,0:T(8,128)(2,1)S(1)} %get-tuple-element.74.refs_4_), channel_id=1, source_target_pairs={{0,8},{1,9},{6,14},{7,15},{8,0},{9,1},{14,6},{15,7},{16,24},{17,25... | collective-permute-start | bytes 221192 | tf_op jit(solution)/shard_map/ppermute | solution.py:410
  75.9 3.1 %collective-permute-start.24 = (s16[144,256]{1,0:T(8,128)(2,1)S(1)}, s16[144,256]{1,0:T(8,128)(2,1)S(1)}, u32[]{:S(2)}, u32[]{:S(2)}) collective-permute-start(s16[144,256]{1,0:T(8,128)(2,1)S(1)} %get-tuple-element.74.refs_4_), channel_id=1, source_target_pairs={{0,16},{1,17},{6,22},{7,23},{8,24},{9,25},{14,30},{15,31},{16,0},{... | collective-permute-start | bytes 221192 | tf_op jit(solution)/shard_map/ppermute | solution.py:410
  79.0 3.7 %collective-permute-start.25 = (s16[144,256]{1,0:T(8,128)(2,1)S(1)}, s16[144,256]{1,0:T(8,128)(2,1)S(1)}, u32[]{:S(2)}, u32[]{:S(2)}) collective-permute-start(s16[144,256]{1,0:T(8,128)(2,1)S(1)} %get-tuple-element.74.refs_4_), channel_id=1, source_target_pairs={{0,24},{1,25},{6,30},{7,31},{8,16},{9,17},{14,22},{15,23},{16,8},{... | collective-permute-start | bytes 221192 | tf_op jit(solution)/shard_map/ppermute | solution.py:410
  82.8 1.1 collective-permute-done.24.refs_6_
  83.8 3.9 %collective-permute-done.25.refs_7_ = s16[144,256]{1,0:T(8,128)(2,1)S(1)} collective-permute-done((s16[144,256]{1,0:T(8,128)(2,1)S(1)}, s16[144,256]{1,0:T(8,128)(2,1)S(1)}, u32[]{:S(2)}, u32[]{:S(2)}) %collective-permute-start.25) | collective-permute-done | bytes 73760 | tf_op jit(solution)/shard_map/ppermute | solution.py:410
  87.8 1.8 %pivots.1.own_ref = f32[6,128,128]{2,1,0:T(8,128)S(1)} custom-call(s32[6]{0:T(128)S(1)} %stack.27.where_ref, f32[1536,768]{1,0:T(8,128)} %anc_ref.7, s16[144,1024]{1,0:T(8,128)(2,1)S(1)} %get-tuple-element.63.refs_0_, s16[144,1024]{1,0:T(8,128)(2,1)S(1)} %collective-permute-done.21.refs_0_.refs_1_, s16[144,1024]{1,0:T(8,128)(2,1)S(1)} %get-tuple-element.70.refs_2_, ...), custom_call_target="tpu_custom_call" | custom-call | flops 1000 | bytes 1000 | tf_op jit(solution)/shard_map/pivots/pallas_call | solution.py:359
  89.6 1.3 %collective-permute-start.26 = (f32[6,128,128]{2,1,0:T(8,128)S(1)}, f32[6,128,128]{2,1,0:T(8,128)S(1)}, u32[]{:S(2)}, u32[]{:S(2)}) collective-permute-start(f32[6,128,128]{2,1,0:T(8,128)S(1)} %pivots.1.own_ref), channel_id=1, source_target_pairs={{0,4},{1,5},{6,2},{7,3},{8,12},{9,13},{14,10},{15,11},{16,20},{17,... | collective-permute-start | bytes 1179656 | tf_op jit(solution)/shard_map/ppermute | solution.py:410
  91.0 1.7 %collective-permute-start.28 = (s16[144,768]{1,0:T(8,128)(2,1)S(1)}, s16[144,768]{1,0:T(8,128)(2,1)S(1)}, u32[]{:S(2)}, u32[]{:S(2)}) collective-permute-start(s16[144,768]{1,0:T(8,128)(2,1)S(1)} %get-tuple-element.78), channel_id=1, source_target_pairs={{0,16},{8,24},{16,0},{24,8},{1,17},{9,25},{17,1},{25,9},{2,18},{10... | collective-permute-start | bytes 663560 | tf_op jit(solution)/shard_map/ppermute | solution.py:413
  92.7 2.6 %collective-permute-start.29 = (s16[144,768]{1,0:T(8,128)(2,1)S(1)}, s16[144,768]{1,0:T(8,128)(2,1)S(1)}, u32[]{:S(2)}, u32[]{:S(2)}) collective-permute-start(s16[144,768]{1,0:T(8,128)(2,1)S(1)} %get-tuple-element.80), channel_id=1, source_target_pairs={{0,24},{8,16},{16,8},{24,0},{1,25},{9,17},{17,9},{25,1},{2,26},{10... | collective-permute-start | bytes 663560 | tf_op jit(solution)/shard_map/ppermute | solution.py:413
  95.3 1.6 %combine.4.refs_3_ = f32[384,768]{1,0:T(8,128)} custom-call(s32[6]{0:T(128)S(1)} %stack.27.where_ref, f32[1536,768]{1,0:T(8,128)S(1)} %bitcast.15, f32[128,768]{1,0:T(8,128)S(1)} %get-tuple-element.81.kept_ref, s16[144,1024]{1,0:T(8,128)(2,1)S(1)} %collective-permute-done.22.refs_3_.refs_0_, f32[384,768]{1,0:T(8,128)} %combine.3.refs_1_), custom_call_target="tpu_custom_call", output_to_operand_aliasing={{}: (4, {})} | custom-call | flops 1000 | bytes 1000 | tf_op jit(solution)/shard_map/combine/pallas_call | solution.py:311
  97.0 13.9 %factor.1 = f32[6,128,128]{2,1,0:T(8,128)} custom-call(s32[6]{0:T(128)S(1)} %stack.27.where_ref, f32[6,128,128]{2,1,0:T(8,128)S(1)} %pivots.1.own_ref, f32[6,128,128]{2,1,0:T(8,128)S(1)} %collective-permute-done.26.other_ref), custom_call_target="tpu_custom_call" | custom-call | flops 20000000000 | bytes 8000000 | tf_op jit(solution)/shard_map/factor/pallas_call | solution.py:77
  110.9 1.8 %combine.5 = f32[384,768]{1,0:T(8,128)} custom-call(s32[6]{0:T(128)S(1)} %stack.27.where_ref, f32[1536,768]{1,0:T(8,128)S(1)} %bitcast.15, f32[128,768]{1,0:T(8,128)S(1)} %get-tuple-element.75.kept_ref, s16[144,768]{1,0:T(8,128)(2,1)S(1)} %collective-permute-done.27.refs_0_, ...), custom_call_target="tpu_custom_call", output_to_operand_aliasing={{}: (6, {})} | custom-call | flops 1000 | bytes 1000 | tf_op jit(solution)/shard_map/combine/pallas_call | solution.py:311
  (52 shorter events, 1.0 us)
Async XLA Ops:
  0.6 19.6 %collective-permute-start.9 = (bf16[8,128,768]{2,1,0:T(8,128)(2,1)}, bf16[8,128,768]{2,1,0:T(8,128)(2,1)S(1)}, u32[]{:S(2)}, u32[]{:S(2)}) collective-permute-start(bf16[8,128,768]{2,1,0:T(8,128)(2,1)} %bitcast.19), channel_id=1, source_target_pairs={{0,4},{4,0},{1,5},{5,1},{2,6},{6,2},{3,7},{7,3},{8,12},{12,8},{9,1... | collective-permute-start | bytes 4718600 | tf_op jit(solution)/shard_map/ppermute | solution.py:417
  0.7 1.4 %copy-start = (bf16[1,8,1536,64]{2,3,1,0:T(8,128)(2,1)S(1)}, bf16[1,8,1536,64]{2,3,1,0:T(8,128)(2,1)}, u32[]{:S(2)}) copy-start(bf16[1,8,1536,64]{2,3,1,0:T(8,128)(2,1)} %param.5) | copy-start | bytes 4718596
  2.1 13.3 %copy-start.6 = (s32[1,8,6]{1,0,2:T(1,128)S(1)}, s32[1,8,6]{1,0,2:T(1,128)}, u32[]{:S(2)}) copy-start(s32[1,8,6]{1,0,2:T(1,128)} %param.8) | copy-start | bytes 580
  2.1 18.1 %copy-start.2 = (bf16[1,8,128,768]{3,2,1,0:T(8,128)(2,1)S(1)}, bf16[1,8,128,768]{3,2,1,0:T(8,128)(2,1)}, u32[]{:S(2)}) copy-start(bf16[1,8,128,768]{3,2,1,0:T(8,128)(2,1)} %param.6) | copy-start | bytes 4718596
  3.0 9.5 %collective-permute-start = (bf16[4,64,512]{2,1,0:T(8,128)(2,1)}, bf16[4,64,512]{2,1,0:T(8,128)(2,1)}, u32[]{:S(2)}, u32[]{:S(2)}) collective-permute-start(bf16[4,64,512]{2,1,0:T(8,128)(2,1)} %get-tuple-element.45.refs_0_), channel_id=1, source_target_pairs={{0,1},{1,0},{2,3},{3,2},{4,5},{5,4},{6,7},{7,6},{8,9},{9,8},{10,11... | collective-permute-start | bytes 786440 | tf_op jit(solution)/shard_map/ppermute | solution.py:429
  3.1 10.9 %collective-permute-start.7 = (bf16[4,64,512]{2,1,0:T(8,128)(2,1)}, bf16[4,64,512]{2,1,0:T(8,128)(2,1)}, u32[]{:S(2)}, u32[]{:S(2)}) collective-permute-start(bf16[4,64,512]{2,1,0:T(8,128)(2,1)} %get-tuple-element.50.refs_1_), channel_id=1, source_target_pairs={{0,2},{1,3},{2,0},{3,1},{4,6},{5,7},{6,4},{7,5},{8,10},{9,11},{10,... | collective-permute-start | bytes 786440 | tf_op jit(solution)/shard_map/ppermute | solution.py:429
  5.1 13.0 %collective-permute-start.4 = (bf16[4,64,512]{2,1,0:T(8,128)(2,1)}, bf16[4,64,512]{2,1,0:T(8,128)(2,1)}, u32[]{:S(2)}, u32[]{:S(2)}) collective-permute-start(bf16[4,64,512]{2,1,0:T(8,128)(2,1)} %get-tuple-element.50.refs_1_), channel_id=1, source_target_pairs={{0,1},{1,0},{2,3},{3,2},{4,5},{5,4},{6,7},{7,6},{8,9},{9,8},{10,11... | collective-permute-start | bytes 786440 | tf_op jit(solution)/shard_map/ppermute | solution.py:429
  6.6 11.6 %collective-permute-start.6 = (bf16[4,64,512]{2,1,0:T(8,128)(2,1)}, bf16[4,64,512]{2,1,0:T(8,128)(2,1)}, u32[]{:S(2)}, u32[]{:S(2)}) collective-permute-start(bf16[4,64,512]{2,1,0:T(8,128)(2,1)} %get-tuple-element.45.refs_0_), channel_id=1, source_target_pairs={{0,2},{1,3},{2,0},{3,1},{4,6},{5,7},{6,4},{7,5},{8,10},{9,11},{10,... | collective-permute-start | bytes 786440 | tf_op jit(solution)/shard_map/ppermute | solution.py:429
  12.5 11.3 %collective-permute-start.1 = (bf16[4,64,512]{2,1,0:T(8,128)(2,1)}, bf16[4,64,512]{2,1,0:T(8,128)(2,1)}, u32[]{:S(2)}, u32[]{:S(2)}) collective-permute-start(bf16[4,64,512]{2,1,0:T(8,128)(2,1)} %collective-permute-done.refs_2_), channel_id=1, source_target_pairs={{0,2},{1,3},{2,0},{3,1},{4,6},{5,7},{6,4},{7,5},{8,10},{9,11},{10,... | collective-permute-start | bytes 786440 | tf_op jit(solution)/shard_map/ppermute | solution.py:429
  14.0 9.8 %collective-permute-start.8 = (bf16[4,64,512]{2,1,0:T(8,128)(2,1)}, bf16[4,64,512]{2,1,0:T(8,128)(2,1)}, u32[]{:S(2)}, u32[]{:S(2)}) collective-permute-start(bf16[4,64,512]{2,1,0:T(8,128)(2,1)} %collective-permute-done.7.refs_5_), channel_id=1, source_target_pairs={{0,1},{1,0},{2,3},{3,2},{4,5},{5,4},{6,7},{7,6},{8,9},{9,8},{10,11... | collective-permute-start | bytes 786440 | tf_op jit(solution)/shard_map/ppermute | solution.py:429
  14.7 0.7 copy-start.3
  18.1 16.6 %collective-permute-start.5 = (bf16[4,64,512]{2,1,0:T(8,128)(2,1)S(1)}, bf16[4,64,512]{2,1,0:T(8,128)(2,1)S(1)}, u32[]{:S(2)}, u32[]{:S(2)}) collective-permute-start(bf16[4,64,512]{2,1,0:T(8,128)(2,1)S(1)} %get-tuple-element.59.refs_0_), channel_id=1, source_target_pairs={{0,1},{1,0},{2,3},{3,2},{4,5},{5,4},{6,7},{7,6},{8,9},{9,8},{10,11... | collective-permute-start | bytes 786440 | tf_op jit(solution)/shard_map/ppermute | solution.py:429
  18.2 16.0 %collective-permute-start.12 = (bf16[4,64,512]{2,1,0:T(8,128)(2,1)}, bf16[4,64,512]{2,1,0:T(8,128)(2,1)S(1)}, u32[]{:S(2)}, u32[]{:S(2)}) collective-permute-start(bf16[4,64,512]{2,1,0:T(8,128)(2,1)} %copy-done.3), channel_id=1, source_target_pairs={{0,2},{1,3},{2,0},{3,1},{4,6},{5,7},{6,4},{7,5},{8,10},{9,11},{10,... | collective-permute-start | bytes 786440 | tf_op jit(solution)/shard_map/ppermute | solution.py:429
  20.2 3.6 %copy-start.5 = (s32[1,8,12]{2,1,0:T(8,128)S(1)}, s32[1,8,12]{2,1,0:T(8,128)}, u32[]{:S(2)}) copy-start(s32[1,8,12]{2,1,0:T(8,128)} %param.7) | copy-start | bytes 1156
  23.8 7.4 %copy-start.4 = (bf16[4,64,512]{2,1,0:T(8,128)(2,1)S(1)}, bf16[4,64,512]{2,1,0:T(8,128)(2,1)}, u32[]{:S(2)}) copy-start(bf16[4,64,512]{2,1,0:T(8,128)(2,1)} %copy-done.3) | copy-start | bytes 786436
  23.8 11.4 %copy-start.1 = (bf16[1,8,1536,64]{2,3,1,0:T(8,128)(2,1)S(1)}, bf16[1,8,1536,64]{2,3,1,0:T(8,128)(2,1)}, u32[]{:S(2)}) copy-start(bf16[1,8,1536,64]{2,3,1,0:T(8,128)(2,1)} %param.5) | copy-start | bytes 4718596
  29.0 14.4 %collective-permute-start.17 = (s16[144,1792]{1,0:T(8,128)(2,1)S(1)}, s16[144,1792]{1,0:T(8,128)(2,1)S(1)}, u32[]{:S(2)}, u32[]{:S(2)}) collective-permute-start(s16[144,1792]{1,0:T(8,128)(2,1)S(1)} %get-tuple-element.62), channel_id=1, source_target_pairs={{0,8},{8,0},{16,24},{24,16},{1,9},{9,1},{17,25},{25,17},{2,10},{10... | collective-permute-start | bytes 1548296 | tf_op jit(solution)/shard_map/ppermute | solution.py:413
  31.2 9.2 %collective-permute-start.2 = (bf16[4,64,512]{2,1,0:T(8,128)(2,1)S(1)}, bf16[4,64,512]{2,1,0:T(8,128)(2,1)S(1)}, u32[]{:S(2)}, u32[]{:S(2)}) collective-permute-start(bf16[4,64,512]{2,1,0:T(8,128)(2,1)S(1)} %copy-done.4), channel_id=1, source_target_pairs={{0,1},{1,0},{2,3},{3,2},{4,5},{5,4},{6,7},{7,6},{8,9},{9,8},{10,11... | collective-permute-start | bytes 786440 | tf_op jit(solution)/shard_map/ppermute | solution.py:429
  32.7 9.2 %collective-permute-start.15 = (bf16[4,64,512]{2,1,0:T(8,128)(2,1)S(1)}, bf16[4,64,512]{2,1,0:T(8,128)(2,1)S(1)}, u32[]{:S(2)}, u32[]{:S(2)}) collective-permute-start(bf16[4,64,512]{2,1,0:T(8,128)(2,1)S(1)} %get-tuple-element.59.refs_0_), channel_id=1, source_target_pairs={{0,2},{1,3},{2,0},{3,1},{4,6},{5,7},{6,4},{7,5},{8,10},{9,11},{10,... | collective-permute-start | bytes 786440 | tf_op jit(solution)/shard_map/ppermute | solution.py:429
  34.2 12.2 %collective-permute-start.13 = (bf16[4,64,512]{2,1,0:T(8,128)(2,1)S(1)}, bf16[4,64,512]{2,1,0:T(8,128)(2,1)S(1)}, u32[]{:S(2)}, u32[]{:S(2)}) collective-permute-start(bf16[4,64,512]{2,1,0:T(8,128)(2,1)S(1)} %collective-permute-done.12.refs_5_), channel_id=1, source_target_pairs={{0,1},{1,0},{2,3},{3,2},{4,5},{5,4},{6,7},{7,6},{8,9},{9,8},{10,11... | collective-permute-start | bytes 786440 | tf_op jit(solution)/shard_map/ppermute | solution.py:429
  34.7 12.7 %collective-permute-start.10 = (bf16[4,64,512]{2,1,0:T(8,128)(2,1)S(1)}, bf16[4,64,512]{2,1,0:T(8,128)(2,1)S(1)}, u32[]{:S(2)}, u32[]{:S(2)}) collective-permute-start(bf16[4,64,512]{2,1,0:T(8,128)(2,1)S(1)} %collective-permute-done.5.refs_2_), channel_id=1, source_target_pairs={{0,2},{1,3},{2,0},{3,1},{4,6},{5,7},{6,4},{7,5},{8,10},{9,11},{10,... | collective-permute-start | bytes 786440 | tf_op jit(solution)/shard_map/ppermute | solution.py:429
  40.4 14.6 %collective-permute-start.3 = (bf16[4,64,512]{2,1,0:T(8,128)(2,1)S(1)}, bf16[4,64,512]{2,1,0:T(8,128)(2,1)S(1)}, u32[]{:S(2)}, u32[]{:S(2)}) collective-permute-start(bf16[4,64,512]{2,1,0:T(8,128)(2,1)S(1)} %get-tuple-element.58.refs_0_), channel_id=1, source_target_pairs={{0,1},{1,0},{2,3},{3,2},{4,5},{5,4},{6,7},{7,6},{8,9},{9,8},{10,11... | collective-permute-start | bytes 786440 | tf_op jit(solution)/shard_map/ppermute | solution.py:429
  41.9 12.5 %collective-permute-start.16 = (bf16[4,64,512]{2,1,0:T(8,128)(2,1)S(1)}, bf16[4,64,512]{2,1,0:T(8,128)(2,1)S(1)}, u32[]{:S(2)}, u32[]{:S(2)}) collective-permute-start(bf16[4,64,512]{2,1,0:T(8,128)(2,1)S(1)} %get-tuple-element.60.refs_1_), channel_id=1, source_target_pairs={{0,2},{1,3},{2,0},{3,1},{4,6},{5,7},{6,4},{7,5},{8,10},{9,11},{10,... | collective-permute-start | bytes 786440 | tf_op jit(solution)/shard_map/ppermute | solution.py:429
  43.8 14.2 %slice-start = ((s8[4718592]{0:T(1024)(128)(4,1)}), s8[4194304]{0:T(1024)(128)(4,1)S(1)}, s32[]{:S(2)}) async-start(s8[4718592]{0:T(1024)(128)(4,1)} %bitcast.12), calls=%async_computation | async-start | bytes 8388608
  43.8 14.2 %slice-start.1 = ((s8[4718592]{0:T(1024)(128)(4,1)}), s8[524288]{0:T(1024)(128)(4,1)S(1)}, s32[]{:S(2)}) async-start(s8[4718592]{0:T(1024)(128)(4,1)} %bitcast.12), calls=%async_computation.1 | async-start | bytes 1048576
  43.8 13.3 %collective-permute-start.21 = (s16[144,1024]{1,0:T(8,128)(2,1)S(1)}, s16[144,1024]{1,0:T(8,128)(2,1)S(1)}, u32[]{:S(2)}, u32[]{:S(2)}) collective-permute-start(s16[144,1024]{1,0:T(8,128)(2,1)S(1)} %get-tuple-element.63.refs_0_), channel_id=1, source_target_pairs={{0,16},{8,24},{16,0},{24,8},{1,17},{9,25},{17,1},{25,9},{2,18},{10... | collective-permute-start | bytes 884744 | tf_op jit(solution)/shard_map/ppermute | solution.py:413
  52.4 14.4 %collective-permute-start.20 = (s16[144,1792]{1,0:T(8,128)(2,1)S(1)}, s16[144,1792]{1,0:T(8,128)(2,1)S(1)}, u32[]{:S(2)}, u32[]{:S(2)}) collective-permute-start(s16[144,1792]{1,0:T(8,128)(2,1)S(1)} %get-tuple-element.69), channel_id=1, source_target_pairs={{0,8},{8,0},{16,24},{24,16},{1,9},{9,1},{17,25},{25,17},{2,10},{10... | collective-permute-start | bytes 1548296 | tf_op jit(solution)/shard_map/ppermute | solution.py:413
  52.9 14.3 %collective-permute-start.14 = (bf16[4,64,512]{2,1,0:T(8,128)(2,1)S(1)}, bf16[4,64,512]{2,1,0:T(8,128)(2,1)S(1)}, u32[]{:S(2)}, u32[]{:S(2)}) collective-permute-start(bf16[4,64,512]{2,1,0:T(8,128)(2,1)S(1)} %get-tuple-element.58.refs_0_), channel_id=1, source_target_pairs={{0,2},{1,3},{2,0},{3,1},{4,6},{5,7},{6,4},{7,5},{8,10},{9,11},{10,... | collective-permute-start | bytes 786440 | tf_op jit(solution)/shard_map/ppermute | solution.py:429
  54.4 12.8 %collective-permute-start.19 = (bf16[4,64,512]{2,1,0:T(8,128)(2,1)S(1)}, bf16[4,64,512]{2,1,0:T(8,128)(2,1)S(1)}, u32[]{:S(2)}, u32[]{:S(2)}) collective-permute-start(bf16[4,64,512]{2,1,0:T(8,128)(2,1)S(1)} %collective-permute-done.16.refs_5_), channel_id=1, source_target_pairs={{0,1},{1,0},{2,3},{3,2},{4,5},{5,4},{6,7},{7,6},{8,9},{9,8},{10,11... | collective-permute-start | bytes 786440 | tf_op jit(solution)/shard_map/ppermute | solution.py:429
  55.0 12.2 %collective-permute-start.11 = (bf16[4,64,512]{2,1,0:T(8,128)(2,1)S(1)}, bf16[4,64,512]{2,1,0:T(8,128)(2,1)S(1)}, u32[]{:S(2)}, u32[]{:S(2)}) collective-permute-start(bf16[4,64,512]{2,1,0:T(8,128)(2,1)S(1)} %get-tuple-element.60.refs_1_), channel_id=1, source_target_pairs={{0,1},{1,0},{2,3},{3,2},{4,5},{5,4},{6,7},{7,6},{8,9},{9,8},{10,11... | collective-permute-start | bytes 786440 | tf_op jit(solution)/shard_map/ppermute | solution.py:429
  57.0 10.2 %collective-permute-start.18 = (bf16[4,64,512]{2,1,0:T(8,128)(2,1)S(1)}, bf16[4,64,512]{2,1,0:T(8,128)(2,1)S(1)}, u32[]{:S(2)}, u32[]{:S(2)}) collective-permute-start(bf16[4,64,512]{2,1,0:T(8,128)(2,1)S(1)} %collective-permute-done.3.refs_2_), channel_id=1, source_target_pairs={{0,2},{1,3},{2,0},{3,1},{4,6},{5,7},{6,4},{7,5},{8,10},{9,11},{10,... | collective-permute-start | bytes 786440 | tf_op jit(solution)/shard_map/ppermute | solution.py:429
  57.9 37.4 %slice-start.2 = ((s8[4718592]{0:T(1024)(128)(4,1)}), s8[524288]{0:T(1024)(128)(4,1)S(1)}, s32[]{:S(2)}) async-start(s8[4718592]{0:T(1024)(128)(4,1)} %bitcast.14), calls=%async_computation.2 | async-start | bytes 1048576
  67.1 28.2 %slice-start.3 = ((s8[4718592]{0:T(1024)(128)(4,1)}), s8[4194304]{0:T(1024)(128)(4,1)S(1)}, s32[]{:S(2)}) async-start(s8[4718592]{0:T(1024)(128)(4,1)} %bitcast.14), calls=%async_computation.3 | async-start | bytes 8388608
  67.1 20.6 %collective-permute-start.22 = (s16[144,1024]{1,0:T(8,128)(2,1)S(1)}, s16[144,1024]{1,0:T(8,128)(2,1)S(1)}, u32[]{:S(2)}, u32[]{:S(2)}) collective-permute-start(s16[144,1024]{1,0:T(8,128)(2,1)S(1)} %get-tuple-element.70.refs_2_), channel_id=1, source_target_pairs={{0,16},{8,24},{16,0},{24,8},{1,17},{9,25},{17,1},{25,9},{2,18},{10... | collective-permute-start | bytes 884744 | tf_op jit(solution)/shard_map/ppermute | solution.py:413
  72.6 10.1 %collective-permute-start.23 = (s16[144,256]{1,0:T(8,128)(2,1)S(1)}, s16[144,256]{1,0:T(8,128)(2,1)S(1)}, u32[]{:S(2)}, u32[]{:S(2)}) collective-permute-start(s16[144,256]{1,0:T(8,128)(2,1)S(1)} %get-tuple-element.74.refs_4_), channel_id=1, source_target_pairs={{0,8},{1,9},{6,14},{7,15},{8,0},{9,1},{14,6},{15,7},{16,24},{17,25... | collective-permute-start | bytes 221192 | tf_op jit(solution)/shard_map/ppermute | solution.py:410
  75.9 7.9 %collective-permute-start.24 = (s16[144,256]{1,0:T(8,128)(2,1)S(1)}, s16[144,256]{1,0:T(8,128)(2,1)S(1)}, u32[]{:S(2)}, u32[]{:S(2)}) collective-permute-start(s16[144,256]{1,0:T(8,128)(2,1)S(1)} %get-tuple-element.74.refs_4_), channel_id=1, source_target_pairs={{0,16},{1,17},{6,22},{7,23},{8,24},{9,25},{14,30},{15,31},{16,0},{... | collective-permute-start | bytes 221192 | tf_op jit(solution)/shard_map/ppermute | solution.py:410
  79.0 8.8 %collective-permute-start.25 = (s16[144,256]{1,0:T(8,128)(2,1)S(1)}, s16[144,256]{1,0:T(8,128)(2,1)S(1)}, u32[]{:S(2)}, u32[]{:S(2)}) collective-permute-start(s16[144,256]{1,0:T(8,128)(2,1)S(1)} %get-tuple-element.74.refs_4_), channel_id=1, source_target_pairs={{0,24},{1,25},{6,30},{7,31},{8,16},{9,17},{14,22},{15,23},{16,8},{... | collective-permute-start | bytes 221192 | tf_op jit(solution)/shard_map/ppermute | solution.py:410
  89.6 7.4 %collective-permute-start.26 = (f32[6,128,128]{2,1,0:T(8,128)S(1)}, f32[6,128,128]{2,1,0:T(8,128)S(1)}, u32[]{:S(2)}, u32[]{:S(2)}) collective-permute-start(f32[6,128,128]{2,1,0:T(8,128)S(1)} %pivots.1.own_ref), channel_id=1, source_target_pairs={{0,4},{1,5},{6,2},{7,3},{8,12},{9,13},{14,10},{15,11},{16,20},{17,... | collective-permute-start | bytes 1179656 | tf_op jit(solution)/shard_map/ppermute | solution.py:410
  90.9 20.0 %collective-permute-start.27 = (s16[144,768]{1,0:T(8,128)(2,1)S(1)}, s16[144,768]{1,0:T(8,128)(2,1)S(1)}, u32[]{:S(2)}, u32[]{:S(2)}) collective-permute-start(s16[144,768]{1,0:T(8,128)(2,1)S(1)} %get-tuple-element.76), channel_id=1, source_target_pairs={{0,8},{8,0},{16,24},{24,16},{1,9},{9,1},{17,25},{25,17},{2,10},{10... | collective-permute-start | bytes 663560 | tf_op jit(solution)/shard_map/ppermute | solution.py:413
  91.0 19.9 %collective-permute-start.28 = (s16[144,768]{1,0:T(8,128)(2,1)S(1)}, s16[144,768]{1,0:T(8,128)(2,1)S(1)}, u32[]{:S(2)}, u32[]{:S(2)}) collective-permute-start(s16[144,768]{1,0:T(8,128)(2,1)S(1)} %get-tuple-element.78), channel_id=1, source_target_pairs={{0,16},{8,24},{16,0},{24,8},{1,17},{9,25},{17,1},{25,9},{2,18},{10... | collective-permute-start | bytes 663560 | tf_op jit(solution)/shard_map/ppermute | solution.py:413
  92.7 18.2 %collective-permute-start.29 = (s16[144,768]{1,0:T(8,128)(2,1)S(1)}, s16[144,768]{1,0:T(8,128)(2,1)S(1)}, u32[]{:S(2)}, u32[]{:S(2)}) collective-permute-start(s16[144,768]{1,0:T(8,128)(2,1)S(1)} %get-tuple-element.80), channel_id=1, source_target_pairs={{0,24},{8,16},{16,8},{24,0},{1,25},{9,17},{17,9},{25,1},{2,26},{10... | collective-permute-start | bytes 663560 | tf_op jit(solution)/shard_map/ppermute | solution.py:413

commit v3 on v2

--- a/solution.py
+++ b/solution.py
@@ -8,7 +8,7 @@
 from jax.sharding import PartitionSpec as P
 
 BLK = 128
-VMEM_LIMIT = 48 * 1024 * 1024
+VMEM_LIMIT = 24 * 1024 * 1024
 SMEM = pl.BlockSpec(memory_space=pltpu.SMEM)
 VMEM = pl.BlockSpec(memory_space=pltpu.VMEM)
 ANY = pl.BlockSpec(memory_space=pl.ANY)
@@ -16,8 +16,14 @@
 EXP_STEPS = 128.0
 EXP_ROWS = 16
 WINDOW = 4
-LARGE = pl.CostEstimate(flops=20_000_000_000, bytes_accessed=8_000_000, transcendentals=0)
-SMALL = pl.CostEstimate(flops=1000, bytes_accessed=1000, transcendentals=0)
+NEAR = 10
+FAR = 4
+
+
+def cost(micros):
+    return pl.CostEstimate(
+        flops=1_000_000_000 * micros + 1000, bytes_accessed=1000, transcendentals=0
+    )
 
 
 def params(**kwargs):
@@ -39,23 +45,34 @@
     return codes.astype(jnp.int32).astype(jnp.float32) * scale
 
 
-def lu_step(ref, j):
+def lu_pair(ref, j):
     size = ref.shape[1]
     top = j // 8 * 8
-    row = ref[:, j : j + 1, :]
-    inverse = 1.0 / row[:, :, j : j + 1]
+    first = ref[:, j : j + 1, :]
+    second = ref[:, j + 1 : j + 2, :]
     lanes = lax.broadcasted_iota(jnp.int32, (1, 1, size), 2)
-    used = jnp.where(lanes > j, row, 0.0)
-    if j % 8 != 7:
+    above = first[:, :, j + 1 : j + 2]
+    inverse = 1.0 / first[:, :, j : j + 1]
+    under = second[:, :, j : j + 1] * inverse
+    later = 1.0 / (second[:, :, j + 1 : j + 2] - under * above)
+    first = jnp.where(lanes > j, first, 0.0)
+    swept = second - under * first
+    ref[:, j + 1 : j + 2, :] = jnp.where(lanes == j, under, swept)
+    second = jnp.where(lanes > j + 1, swept, 0.0)
+
+    def sweep(block, keep):
+        one = block[:, :, j : j + 1] * inverse
+        two = (block[:, :, j + 1 : j + 2] - one * above) * later
+        result = block - one * first - two * second
+        result = jnp.where(lanes == j, one, jnp.where(lanes == j + 1, two, result))
+        return result if keep is None else jnp.where(keep, result, block)
+
+    if j % 8 != 6:
+        rows = lax.broadcasted_iota(jnp.int32, (1, 8, 1), 1) + top
         head = ref[:, top : top + 8, :]
-        rows = lax.broadcasted_iota(jnp.int32, (1, 8, 1), 1) + top
-        factor = jnp.where(rows > j, head[:, :, j : j + 1] * inverse, 0.0)
-        swept = head - factor * used
-        ref[:, top : top + 8, :] = jnp.where((lanes == j) & (rows > j), factor, swept)
+        ref[:, top : top + 8, :] = sweep(head, rows > j + 1)
     if top + 8 < size:
-        rest = ref[:, top + 8 :, :]
-        factor = rest[:, :, j : j + 1] * inverse
-        ref[:, top + 8 :, :] = jnp.where(lanes == j, factor, rest - factor * used)
+        ref[:, top + 8 :, :] = sweep(ref[:, top + 8 :, :], None)
 
 
 def lu_kernel(where_ref, own_ref, other_ref, out_ref):
@@ -69,8 +86,8 @@
     def _():
         out_ref[...] = other_ref[...]
 
-    for j in range(out_ref.shape[1]):
-        lu_step(out_ref, j)
+    for j in range(0, out_ref.shape[1], 2):
+        lu_pair(out_ref, j)
 
 
 def factor(where, own, other):
@@ -80,7 +97,7 @@
         in_specs=[SMEM, VMEM, VMEM],
         out_specs=VMEM,
         compiler_params=params(),
-        cost_estimate=LARGE,
+        cost_estimate=cost(20),
         name="factor",
     )(where, own, other)
 
@@ -115,100 +132,111 @@
         out_specs=[ANY, ANY],
         scratch_shapes=[pltpu.SemaphoreType.DMA((2, layers))],
         compiler_params=params(),
-        cost_estimate=SMALL,
+        cost_estimate=cost(0),
         name="split",
     )(lt)
 
 
-def right_kernel(where_ref, upat_ref, u_ref, uo_ref, out_ref, held, sems):
-    row = where_ref[1]
-    wide = u_ref.shape[1]
-    copies = [
-        pltpu.make_async_copy(
-            ref, held.at[:, pl.ds(pl.multiple_of(spot * wide, wide), wide)], sems.at[n]
-        )
-        for n, (ref, spot) in enumerate(((u_ref, row), (uo_ref, 1 - row)))
-    ]
-    for copy in copies:
-        copy.start()
-    for copy in copies:
-        copy.wait()
-    for k in range(held.shape[0]):
-        for n in range(held.shape[2] // BLK):
-
-            @pl.when(upat_ref[k, n] == 0)
-            def _():
-                held[k, :, n * BLK : (n + 1) * BLK] = jnp.zeros((held.shape[1], BLK), held.dtype)
-
-    back = pltpu.make_async_copy(held, out_ref, sems.at[2])
-    back.start()
-    back.wait()
-
-
-def masked_right(where, upat, u, uo):
-    supers, wide, cols = u.shape
-    shape = (supers, 2 * wide, cols)
+def right_kernel(where_ref, upat_ref, u_ref, uo_ref, near_ref, far_ref):
+    _, wide, cols = u_ref.shape
+    depth = far_ref.shape[1]
+    begin = where_ref[6] * depth
+    mine = where_ref[1] == where_ref[3]
+
+    def fill(close_ref, away_ref):
+        for n, ref in enumerate((close_ref, close_ref, away_ref, away_ref)):
+            spot = begin if n % 2 == 0 else wide - depth - begin
+            rows = pl.ds(pl.multiple_of(spot, depth), depth)
+            for k in range(u_ref.shape[0]):
+                for m in range(cols // BLK):
+                    lanes = slice(m * BLK, (m + 1) * BLK)
+                    block = ref[k, rows, lanes]
+                    block = jnp.where(upat_ref[k, m] != 0, block, jnp.zeros_like(block))
+                    if n < 3:
+                        near_ref[k, n * depth : (n + 1) * depth, lanes] = block
+                    else:
+                        far_ref[k, :, lanes] = block
+
+    @pl.when(mine)
+    def _():
+        fill(u_ref, uo_ref)
+
+    @pl.when(jnp.logical_not(mine))
+    def _():
+        fill(uo_ref, u_ref)
+
+
+def masked_right(where, upat, u, uo, depth):
+    supers, _, cols = u.shape
     return pl.pallas_call(
         right_kernel,
-        out_shape=jax.ShapeDtypeStruct(shape, u.dtype),
-        in_specs=[SMEM, SMEM, ANY, ANY],
-        out_specs=ANY,
-        scratch_shapes=[pltpu.VMEM(shape, u.dtype), pltpu.SemaphoreType.DMA((3,))],
-        compiler_params=params(),
-        cost_estimate=SMALL,
+        out_shape=[
+            jax.ShapeDtypeStruct((supers, 3 * depth, cols), u.dtype),
+            jax.ShapeDtypeStruct((supers, depth, cols), u.dtype),
+        ],
+        in_specs=[SMEM, SMEM, VMEM, VMEM],
+        out_specs=[VMEM, VMEM],
+        compiler_params=params(),
+        cost_estimate=cost(0),
         name="masked_right",
     )(where, upat, u, uo)
 
 
-def update_kernel(chunk, chunks, layers, last, where_ref, lpat_ref, *refs):
-    pieces, right_ref = refs[:8], refs[8]
-    kept_ref, diag_ref = refs[9:11]
-    sent_refs, (left, right, acc, sems) = refs[11:-4], refs[-4:]
-    layer, col = where_ref[0], where_ref[2]
-    half, depth, _ = pieces[0].shape
-    cols = right.shape[2]
-
-    def slot(index):
-        return pl.ds(pl.multiple_of(index * depth, depth), depth)
-
-    waits = []
-    for h in range(2):
-        ks = pl.ds(h * half, half)
-        items = [(right_ref.at[ks], right.at[ks])]
-        items += [(pieces[2 * n + h], left.at[ks, slot(col ^ n)]) for n in range(4)]
-        copies = [
-            pltpu.make_async_copy(src, dst, sems.at[h, n]) for n, (src, dst) in enumerate(items)
-        ]
-        for copy in copies:
-            copy.start()
-        waits.append(copies)
-    for h in range(2):
-        for copy in waits[h]:
-            copy.wait()
-        for k in range(h * half, (h + 1) * half):
-            for t in range(layers):
-
-                @pl.when(lpat_ref[k, t * chunks + chunk] == 0)
-                def _():
-                    left[k, :, t * BLK : (t + 1) * BLK] = jnp.zeros(
-                        (left.shape[1], BLK), left.dtype
+def product(chunk, chunks, layers, lpat_ref, groups, right_ref, left):
+    half, depth, _ = groups[0][0].shape
+    for n, group in enumerate(groups):
+        for h in range(2):
+            for i in range(half):
+                k = h * half + i
+                for t in range(layers):
+                    lanes = slice(t * BLK, (t + 1) * BLK)
+                    block = group[h][i, :, lanes]
+                    kept = lpat_ref[k, t * chunks + chunk] != 0
+                    left[k, n * depth : (n + 1) * depth, lanes] = jnp.where(
+                        kept, block, jnp.zeros_like(block)
                     )
-
-        product = lax.dot_general(
-            left[h * half : (h + 1) * half].reshape(-1, left.shape[2]),
-            right[h * half : (h + 1) * half].reshape(-1, right.shape[2]),
-            (((0,), (0,)), ((), ())),
-            preferred_element_type=jnp.float32,
-        ).reshape(acc.shape)
-        if h == 0:
-            acc[...] = product
-        else:
-            acc[...] += product
+    return lax.dot_general(
+        left[...].reshape(-1, left.shape[2]),
+        right_ref[...].reshape(-1, right_ref.shape[2]),
+        (((0,), (0,)), ((), ())),
+        preferred_element_type=jnp.float32,
+    )
+
+
+def near_kernel(chunk, chunks, layers, lpat_ref, *refs):
+    pieces, (right_ref, acc_ref, left) = refs[:6], refs[6:]
+    groups = [pieces[2 * n : 2 * n + 2] for n in range(3)]
+    total = product(chunk, chunks, layers, lpat_ref, groups, right_ref, left)
+    acc_ref[...] = total.reshape(acc_ref.shape)
+
+
+def near_update(lpat, pieces, right, chunk, chunks, layers):
+    half, _, width = pieces[0].shape
+    supers, kdim, cols = right.shape
+    return pl.pallas_call(
+        functools.partial(near_kernel, chunk, chunks, layers),
+        out_shape=jax.ShapeDtypeStruct((layers, BLK, cols), jnp.float32),
+        in_specs=[SMEM] + [VMEM] * 7,
+        out_specs=VMEM,
+        scratch_shapes=[pltpu.VMEM((supers, kdim, width), jnp.bfloat16)],
+        compiler_params=params(),
+        cost_estimate=cost(NEAR),
+        name="near_update",
+    )(lpat, *pieces, right)
+
+
+def far_kernel(chunk, chunks, layers, last, where_ref, lpat_ref, da_ref, db_ref, *refs):
+    right_ref, before_ref, kept_ref, diag_ref = refs[:4]
+    sent_refs, (left, acc) = refs[4:-2], refs[-2:]
+    layer = where_ref[0]
+    cols = right_ref.shape[2]
+    total = product(chunk, chunks, layers, lpat_ref, [(da_ref, db_ref)], right_ref, left)
+    acc[...] = before_ref[...] + total.reshape(acc.shape)
     for i in range(cols // BLK // chunks):
         q = i * chunks + chunk
-        block = acc[where_ref[5] + i, :, q * BLK : (q + 1) * BLK]
-        diag_ref[:BLK, i * BLK : (i + 1) * BLK], diag_ref[BLK:, i * BLK : (i + 1) * BLK] = encode(
-            block
+        lanes = slice(i * BLK, (i + 1) * BLK)
+        diag_ref[:BLK, lanes], diag_ref[BLK:, lanes] = encode(
+            acc[where_ref[5] + i, :, q * BLK : (q + 1) * BLK]
         )
     if last:
         for s in range(1, layers):
@@ -217,17 +245,16 @@
     else:
         (sent_ref,) = sent_refs
         for n, s in enumerate((1, 3)):
-            sent_ref[:BLK, n * cols : (n + 1) * cols], sent_ref[BLK:, n * cols : (n + 1) * cols] = (
-                encode(acc[layer ^ s])
-            )
+            lanes = slice(n * cols, (n + 1) * cols)
+            sent_ref[:BLK, lanes], sent_ref[BLK:, lanes] = encode(acc[layer ^ s])
         sent_ref[:, 2 * cols :] = diag_ref[...]
         kept_ref[0] = acc[layer]
         kept_ref[1] = acc[layer ^ 2]
 
 
-def chunk_update(where, lpat, pieces, right, chunk, chunks, layers):
-    half, _, width = pieces[0].shape
-    supers, kdim, cols = right.shape
+def far_update(where, lpat, pieces, right, before, chunk, chunks, layers):
+    half, depth, width = pieces[0].shape
+    supers, _, cols = right.shape
     beside = cols // chunks
     coded = BLK + EXP_ROWS
     last = chunk == chunks - 1
@@ -238,24 +265,22 @@
         kept = (2, BLK, cols)
         sent = [(coded, 2 * cols + beside)]
     return pl.pallas_call(
-        functools.partial(update_kernel, chunk, chunks, layers, last),
+        functools.partial(far_kernel, chunk, chunks, layers, last),
         out_shape=[
             jax.ShapeDtypeStruct(kept, jnp.float32),
             jax.ShapeDtypeStruct((coded, beside), jnp.int16),
         ]
         + [jax.ShapeDtypeStruct(shape, jnp.int16) for shape in sent],
-        in_specs=[SMEM] * 2 + [ANY] * 9,
+        in_specs=[SMEM] * 2 + [VMEM] * 4,
         out_specs=[VMEM] * (2 + len(sent)),
         scratch_shapes=[
-            pltpu.VMEM((supers, kdim, width), jnp.bfloat16),
-            pltpu.VMEM((supers, kdim, cols), jnp.bfloat16),
+            pltpu.VMEM((supers, depth, width), jnp.bfloat16),
             pltpu.VMEM((layers, BLK, cols), jnp.float32),
-            pltpu.SemaphoreType.DMA((2, 5)),
         ],
         compiler_params=params(),
-        cost_estimate=LARGE,
-        name="update",
-    )(where, lpat, *pieces, right)
+        cost_estimate=cost(FAR),
+        name="far_update",
+    )(where, lpat, *pieces, right, before)
 
 
 def halve_kernel(kept_ref, diag_ref, got_ref, sum_ref, sent_ref):
@@ -280,9 +305,26 @@
         in_specs=[VMEM] * 3,
         out_specs=[VMEM] * 2,
         compiler_params=params(),
-        cost_estimate=SMALL,
+        cost_estimate=cost(0),
         name="halve",
     )(kept, diag, got)
+
+
+def add_kernel(mine_ref, got_ref, out_ref):
+    total = decode(mine_ref[:BLK], mine_ref[BLK:]) + decode(got_ref[:BLK], got_ref[BLK:])
+    out_ref[:BLK], out_ref[BLK:] = encode(total)
+
+
+def add_coded(mine, got):
+    return pl.pallas_call(
+        add_kernel,
+        out_shape=jax.ShapeDtypeStruct(mine.shape, mine.dtype),
+        in_specs=[VMEM] * 2,
+        out_specs=VMEM,
+        compiler_params=params(),
+        cost_estimate=cost(0),
+        name="add_coded",
+    )(mine, got)
 
 
 def combine_kernel(chunk, codes, held, where_ref, anc_ref, kept_ref, *refs):
@@ -320,7 +362,7 @@
         ],
         input_output_aliases={3 + codes: 0} if held else {},
         compiler_params=params(),
-        cost_estimate=SMALL,
+        cost_estimate=cost(0),
         name="combine",
     )(where, anc, kept, *got, *held)
 
@@ -366,7 +408,7 @@
             pltpu.SemaphoreType.DMA((count,)),
         ],
         compiler_params=params(),
-        cost_estimate=SMALL,
+        cost_estimate=cost(0),
         name="pivots",
     )(where, anc, *parts)
 
@@ -394,6 +436,7 @@
             col // per_group,
             col % per_group * width,
             col % per_group * (width // share),
+            col % per_group,
         ]
     ).astype(jnp.int32)
     everyone = ("layer", "row", "col")
@@ -415,7 +458,7 @@
     lt = jnp.swapaxes(lpanel[0], 1, 2)
     u = upanel[0]
     uo = lax.ppermute(u, "row", xor_perm(rows, 1))
-    right = masked_right(where, upat[0], u, uo)
+    near_right, far_right = masked_right(where, upat[0], u, uo, lt.shape[1])
     moved = []
     gates = {}
 
@@ -437,26 +480,27 @@
         ya = over(a, 2)
         da = over(xa, 2)
         db = over(yb, 1)
-        return a, b, xa, xb, ya, yb, da, db
-
-    pieces = gathered_chunk(0)
+        return (a, b, xa, xb, ya, yb), (da, db)
+
+    near, far = gathered_chunk(0)
     held, groups, waits = [], [], []
     for j in range(chunks):
-        out = chunk_update(where, lpat[0], pieces, after(right, *waits), j, chunks, layers)
+        part = near_update(lpat[0], near, after(near_right, *waits), j, chunks, layers)
+        out = far_update(where, lpat[0], far, far_right, part, j, chunks, layers)
         kept, diag = out[:2]
         if j < chunks - 1:
-            gates[len(moved) + 4] = (kept,)
-            pieces = gathered_chunk(j + 1)
-            near = over_layers(out[2], 1)
-            kept, sent = halve(kept, diag, near)
+            near, far = gathered_chunk(j + 1)
+            kept, sent = halve(kept, diag, over_layers(out[2], 1))
             got = [over_layers(sent, 2)]
             groups.append([sent, got[0]])
-            waits = [sent] + held
+            waits = [sent] if j == 0 else held
             held = [combine(where, anc, kept, got, held, share, j)]
+    near = from_holders(diag, lambda l, r, c: index(l ^ 1, r, c))
+    near = add_coded(diag, near)
+    far = from_holders(near, lambda l, r, c: index(l ^ 2, r, c))
     steps = range(1, layers)
-    parts = [from_holders(diag, lambda l, r, c, s=s: index(l ^ s, r, c)) for s in steps]
-    got = [over_layers(after(out[1 + s], parts[-1]) if s > 1 else out[1 + s], s) for s in steps]
-    groups.append([diag] + parts)
+    got = [over_layers(after(out[1 + s], far) if s > 1 else out[1 + s], s) for s in steps]
+    groups.append([near, far])
     own = pivots(where, anc, groups, width // BLK)
     other = from_holders(own, lambda l, r, c: index(l, 1 - r, c))
     diag_lu = factor(where, own, other)

time: 115 us -> 135 us (1.17)
  waiting for transfers between devices: 27.4 us -> 46.1 us
  Pallas kernels: 41 us -> 46.7 us
  starting transfers between devices: 41.1 us -> 36.2 us
    pallas_call x1, Pallas kernels: 13.9 us -> 24.9 us  [factor(): pl.pallas_call(lu_kernel, out_shape=jax.ShapeDtypeStruct(own.shape, jnp.f...]
    ppermute x4 -> x3, waiting for transfers between devices: 5.02 us -> 13.1 us  [from_holders(): return lax.ppermute(value, everyone, perm)]
    ppermute x4 -> x3, starting transfers between devices: 11.4 us -> 5.16 us  [from_holders(): return lax.ppermute(value, everyone, perm)]
    ppermute x18, waiting for transfers between devices: 14.6 us -> 20.8 us  [over(): moved.append(lax.ppermute(value, 'col', xor_perm(cols, bit)))]
    ppermute x7, waiting for transfers between devices: 7.81 us -> 12.3 us  [over_layers(): return lax.ppermute(value, 'layer', xor_perm(layers, s))]
    pallas_call x4 -> x8, Pallas kernels: 18.4 us -> 14.1 us  [the longest x3 7.46 us: near_update(): pl.pallas_call(functools.partial(near_kernel, chunk, chunks, layers), out...]
  transfers between devices with their start and end apart: 30 -> 29, of which waited for: 9 -> 9; matrix products, arithmetic and copies ran while one was open for 0% -> 0% of each run, Pallas kernels for 33% -> 33%
where the time goes in v3:
time: 135 us; the launch traced here: 132 us
  Pallas kernels  46.7 us (35%)
  waiting for transfers between devices  46.1 us (34%)
  starting transfers between devices  36.2 us (27%)
  local copies, waits for them, and re-layouts  2.3 us (2%)
    pallas_call x1, Pallas kernels, factor(): pl.pallas_call(lu_kernel, out_shape=jax.ShapeDtypeStruct(own.shape, jnp.f...  24.9 us
    ppermute x18, waiting for transfers between devices, over(): moved.append(lax.ppermute(value, 'col', xor_perm(cols, bit)))  20.8 us
    ppermute x18, starting transfers between devices, over(): moved.append(lax.ppermute(value, 'col', xor_perm(cols, bit)))  20 us
    ppermute x3, waiting for transfers between devices, from_holders(): return lax.ppermute(value, everyone, perm)  13.1 us
    ppermute x7, waiting for transfers between devices, over_layers(): return lax.ppermute(value, 'layer', xor_perm(layers, s))  12.3 us
    ppermute x7, starting transfers between devices, over_layers(): return lax.ppermute(value, 'layer', xor_perm(layers, s))  11 us
    pallas_call x3, Pallas kernels, near_update(): pl.pallas_call(functools.partial(near_kernel, chunk, chunks, layers), out...  7.46 us
    ppermute x3, starting transfers between devices, from_holders(): return lax.ppermute(value, everyone, perm)  5.16 us
  transfers between devices with their start and end apart: 29, of which 9 were waited for; matrix products, arithmetic and copies ran while one was open for 0% of the time, Pallas kernels for 33%

profile of v3, /device:TPU:2, one launch (start us, length us, event | category | flops | bytes accessed | tf_op | source)
XLA Modules:
  0.0 132.3 jit_solution(2055833823072614316)
XLA Ops:
  0.7 1.4 %copy-done = bf16[1,8,1536,64]{2,3,1,0:T(8,128)(2,1)S(1)} copy-done((bf16[1,8,1536,64]{2,3,1,0:T(8,128)(2,1)S(1)}, bf16[1,8,1536,64]{2,3,1,0:T(8,128)(2,1)}, u32[]{:S(2)}) %copy-start) | copy-done | bytes 1572888
  2.1 0.9 split.5
  3.1 2.0 %collective-permute-start.5 = (bf16[4,64,512]{2,1,0:T(8,128)(2,1)}, bf16[4,64,512]{2,1,0:T(8,128)(2,1)}, u32[]{:S(2)}, u32[]{:S(2)}) collective-permute-start(bf16[4,64,512]{2,1,0:T(8,128)(2,1)} %get-tuple-element.53.refs_1_), channel_id=1, source_target_pairs={{0,2},{1,3},{2,0},{3,1},{4,6},{5,7},{6,4},{7,5},{8,10},{9,11},{10,... | collective-permute-start | bytes 786440 | tf_op jit(solution)/shard_map/ppermute | solution.py:472
  5.1 1.5 %collective-permute-start.11 = (bf16[4,64,512]{2,1,0:T(8,128)(2,1)}, bf16[4,64,512]{2,1,0:T(8,128)(2,1)}, u32[]{:S(2)}, u32[]{:S(2)}) collective-permute-start(bf16[4,64,512]{2,1,0:T(8,128)(2,1)} %get-tuple-element.53.refs_1_), channel_id=1, source_target_pairs={{0,1},{1,0},{2,3},{3,2},{4,5},{5,4},{6,7},{7,6},{8,9},{9,8},{10,11... | collective-permute-start | bytes 786440 | tf_op jit(solution)/shard_map/ppermute | solution.py:472
  6.6 0.5 collective-permute-start.15
  7.1 5.4 %collective-permute-done.refs_2_ = bf16[4,64,512]{2,1,0:T(8,128)(2,1)} collective-permute-done((bf16[4,64,512]{2,1,0:T(8,128)(2,1)}, bf16[4,64,512]{2,1,0:T(8,128)(2,1)}, u32[]{:S(2)}, u32[]{:S(2)}) %collective-permute-start) | collective-permute-done | bytes 262176 | tf_op jit(solution)/shard_map/ppermute | solution.py:472
  12.5 1.5 %collective-permute-start.1 = (bf16[4,64,512]{2,1,0:T(8,128)(2,1)}, bf16[4,64,512]{2,1,0:T(8,128)(2,1)}, u32[]{:S(2)}, u32[]{:S(2)}) collective-permute-start(bf16[4,64,512]{2,1,0:T(8,128)(2,1)} %collective-permute-done.refs_2_), channel_id=1, source_target_pairs={{0,2},{1,3},{2,0},{3,1},{4,6},{5,7},{6,4},{7,5},{8,10},{9,11},{10,... | collective-permute-start | bytes 786440 | tf_op jit(solution)/shard_map/ppermute | solution.py:472
  14.0 0.5 collective-permute-start.6
  14.7 0.7 copy-done.3
  15.6 2.5 %collective-permute-done.11.refs_3_ = bf16[4,64,512]{2,1,0:T(8,128)(2,1)} collective-permute-done((bf16[4,64,512]{2,1,0:T(8,128)(2,1)}, bf16[4,64,512]{2,1,0:T(8,128)(2,1)}, u32[]{:S(2)}, u32[]{:S(2)}) %collective-permute-start.11) | collective-permute-done | bytes 262176 | tf_op jit(solution)/shard_map/ppermute | solution.py:472
  18.2 2.0 %collective-permute-start.16 = (bf16[4,64,512]{2,1,0:T(8,128)(2,1)}, bf16[4,64,512]{2,1,0:T(8,128)(2,1)S(1)}, u32[]{:S(2)}, u32[]{:S(2)}) collective-permute-start(bf16[4,64,512]{2,1,0:T(8,128)(2,1)} %copy-done.3), channel_id=1, source_target_pairs={{0,2},{1,3},{2,0},{3,1},{4,6},{5,7},{6,4},{7,5},{8,10},{9,11},{10,... | collective-permute-start | bytes 786440 | tf_op jit(solution)/shard_map/ppermute | solution.py:472
  20.2 3.6 %collective-permute-done.1.da_ref = bf16[4,64,512]{2,1,0:T(8,128)(2,1)} collective-permute-done((bf16[4,64,512]{2,1,0:T(8,128)(2,1)}, bf16[4,64,512]{2,1,0:T(8,128)(2,1)}, u32[]{:S(2)}, u32[]{:S(2)}) %collective-permute-start.1) | collective-permute-done | bytes 262176 | tf_op jit(solution)/shard_map/ppermute | solution.py:472
  23.8 2.0 %collective-permute-start.2 = (bf16[4,64,512]{2,1,0:T(8,128)(2,1)}, bf16[4,64,512]{2,1,0:T(8,128)(2,1)S(1)}, u32[]{:S(2)}, u32[]{:S(2)}) collective-permute-start(bf16[4,64,512]{2,1,0:T(8,128)(2,1)} %copy-done.3), channel_id=1, source_target_pairs={{0,1},{1,0},{2,3},{3,2},{4,5},{5,4},{6,7},{7,6},{8,9},{9,8},{10,11... | collective-permute-start | bytes 786440 | tf_op jit(solution)/shard_map/ppermute | solution.py:472
  25.8 1.5 %collective-permute-start.7 = (bf16[4,64,512]{2,1,0:T(8,128)(2,1)S(1)}, bf16[4,64,512]{2,1,0:T(8,128)(2,1)S(1)}, u32[]{:S(2)}, u32[]{:S(2)}) collective-permute-start(bf16[4,64,512]{2,1,0:T(8,128)(2,1)S(1)} %get-tuple-element.59.refs_0_), channel_id=1, source_target_pairs={{0,2},{1,3},{2,0},{3,1},{4,6},{5,7},{6,4},{7,5},{8,10},{9,11},{10,... | collective-permute-start | bytes 786440 | tf_op jit(solution)/shard_map/ppermute | solution.py:472
  27.3 1.4 %masked_right.1 = (bf16[8,192,768]{2,1,0:T(8,128)(2,1)S(1)}, bf16[8,64,768]{2,1,0:T(8,128)(2,1)S(1)}) custom-call(s32[7]{0:T(128)S(1)} %stack.31.where_ref, s32[8,6]{1,0:T(8,128)S(1)} %bitcast.20, bf16[8,128,768]{2,1,0:T(8,128)(2,1)S(1)} %bitcast.19, bf16[8,128,768]{2,1,0:T(8,128)(2,1)S(1)} %collective-permute-done.10.uo_ref), custom_call_target="tpu_custom_call" | custom-call | flops 1000 | bytes 1000 | tf_op jit(solution)/shard_map/masked_right/pallas_call | solution.py:171
  28.7 3.0 %near_update.3.refs_1_ = f32[4,128,768]{2,1,0:T(8,128)S(1)} custom-call(s32[8,12]{1,0:T(8,128)S(1)} %bitcast.21, bf16[4,64,512]{2,1,0:T(8,128)(2,1)} %get-tuple-element.46.refs_0_, bf16[4,64,512]{2,1,0:T(8,128)(2,1)} %get-tuple-element.53.refs_1_, bf16[4,64,512]{2,1,0:T(8,128)(2,1)} %collective-permute-done.refs_2_, ...), custom_call_target="tpu_custom_call" | custom-call | flops 10000001024 | bytes 1000 | tf_op jit(solution)/shard_map/near_update/pallas_call | solution.py:216
  31.7 2.1 %far_update.3 = (f32[2,128,768]{2,1,0:T(8,128)S(1)}, s16[144,256]{1,0:T(8,128)(2,1)S(1)}, s16[144,1792]{1,0:T(8,128)(2,1)S(1)}) custom-call(s32[7]{0:T(128)S(1)} %stack.31.where_ref, s32[8,12]{1,0:T(8,128)S(1)} %bitcast.22, bf16[4,64,512]{2,1,0:T(8,128)(2,1)} %collective-permute-done.1.da_ref, bf16[4,64,512]{2,1,0:T(8,128)(2,1)} %collective-permute-done.6.db_ref, ...), custom_call_target="tpu_custom_call" | custom-call | flops 4000001024 | bytes 1000 | tf_op jit(solution)/shard_map/far_update/pallas_call | solution.py:267
  33.8 1.6 %collective-permute-start.19 = (s16[144,1792]{1,0:T(8,128)(2,1)S(1)}, s16[144,1792]{1,0:T(8,128)(2,1)S(1)}, u32[]{:S(2)}, u32[]{:S(2)}) collective-permute-start(s16[144,1792]{1,0:T(8,128)(2,1)S(1)} %get-tuple-element.68), channel_id=1, source_target_pairs={{0,8},{8,0},{16,24},{24,16},{1,9},{9,1},{17,25},{25,17},{2,10},{10... | collective-permute-start | bytes 1548296 | tf_op jit(solution)/shard_map/ppermute | solution.py:456
  35.6 0.6 collective-permute-start.13
  36.2 0.5 collective-permute-start.17
  36.7 1.5 %collective-permute-start.3 = (bf16[4,64,512]{2,1,0:T(8,128)(2,1)S(1)}, bf16[4,64,512]{2,1,0:T(8,128)(2,1)S(1)}, u32[]{:S(2)}, u32[]{:S(2)}) collective-permute-start(bf16[4,64,512]{2,1,0:T(8,128)(2,1)S(1)} %get-tuple-element.64.refs_0_), channel_id=1, source_target_pairs={{0,1},{1,0},{2,3},{3,2},{4,5},{5,4},{6,7},{7,6},{8,9},{9,8},{10,11... | collective-permute-start | bytes 786440 | tf_op jit(solution)/shard_map/ppermute | solution.py:472
  38.2 1.5 %collective-permute-start.8 = (bf16[4,64,512]{2,1,0:T(8,128)(2,1)S(1)}, bf16[4,64,512]{2,1,0:T(8,128)(2,1)S(1)}, u32[]{:S(2)}, u32[]{:S(2)}) collective-permute-start(bf16[4,64,512]{2,1,0:T(8,128)(2,1)S(1)} %get-tuple-element.61.refs_1_), channel_id=1, source_target_pairs={{0,2},{1,3},{2,0},{3,1},{4,6},{5,7},{6,4},{7,5},{8,10},{9,11},{10,... | collective-permute-start | bytes 786440 | tf_op jit(solution)/shard_map/ppermute | solution.py:472
  39.8 5.2 %collective-permute-done.13.da_ref = bf16[4,64,512]{2,1,0:T(8,128)(2,1)S(1)} collective-permute-done((bf16[4,64,512]{2,1,0:T(8,128)(2,1)S(1)}, bf16[4,64,512]{2,1,0:T(8,128)(2,1)S(1)}, u32[]{:S(2)}, u32[]{:S(2)}) %collective-permute-start.13) | collective-permute-done | bytes 262176 | tf_op jit(solution)/shard_map/ppermute | solution.py:472
  44.9 0.5 collective-permute-start.14
  45.5 1.5 %collective-permute-start.18 = (bf16[4,64,512]{2,1,0:T(8,128)(2,1)S(1)}, bf16[4,64,512]{2,1,0:T(8,128)(2,1)S(1)}, u32[]{:S(2)}, u32[]{:S(2)}) collective-permute-start(bf16[4,64,512]{2,1,0:T(8,128)(2,1)S(1)} %get-tuple-element.64.refs_0_), channel_id=1, source_target_pairs={{0,2},{1,3},{2,0},{3,1},{4,6},{5,7},{6,4},{7,5},{8,10},{9,11},{10,... | collective-permute-start | bytes 786440 | tf_op jit(solution)/shard_map/ppermute | solution.py:472
  47.0 4.1 %collective-permute-done.3.refs_2_ = bf16[4,64,512]{2,1,0:T(8,128)(2,1)S(1)} collective-permute-done((bf16[4,64,512]{2,1,0:T(8,128)(2,1)S(1)}, bf16[4,64,512]{2,1,0:T(8,128)(2,1)S(1)}, u32[]{:S(2)}, u32[]{:S(2)}) %collective-permute-start.3) | collective-permute-done | bytes 262176 | tf_op jit(solution)/shard_map/ppermute | solution.py:472
  51.1 1.5 %collective-permute-start.4 = (bf16[4,64,512]{2,1,0:T(8,128)(2,1)S(1)}, bf16[4,64,512]{2,1,0:T(8,128)(2,1)S(1)}, u32[]{:S(2)}, u32[]{:S(2)}) collective-permute-start(bf16[4,64,512]{2,1,0:T(8,128)(2,1)S(1)} %collective-permute-done.3.refs_2_), channel_id=1, source_target_pairs={{0,2},{1,3},{2,0},{3,1},{4,6},{5,7},{6,4},{7,5},{8,10},{9,11},{10,... | collective-permute-start | bytes 786440 | tf_op jit(solution)/shard_map/ppermute | solution.py:472
  52.6 0.5 collective-permute-start.9
  53.4 2.7 %collective-permute-start.20 = (s16[144,1024]{1,0:T(8,128)(2,1)S(1)}, s16[144,1024]{1,0:T(8,128)(2,1)S(1)}, u32[]{:S(2)}, u32[]{:S(2)}) collective-permute-start(s16[144,1024]{1,0:T(8,128)(2,1)S(1)} %get-tuple-element.70.refs_0_), channel_id=1, source_target_pairs={{0,16},{8,24},{16,0},{24,8},{1,17},{9,25},{17,1},{25,9},{2,18},{10... | collective-permute-start | bytes 884744 | tf_op jit(solution)/shard_map/ppermute | solution.py:456
  56.1 2.2 %near_update.5.refs_1_ = f32[4,128,768]{2,1,0:T(8,128)S(1)} custom-call(s32[8,12]{1,0:T(8,128)S(1)} %bitcast.23, bf16[4,64,512]{2,1,0:T(8,128)(2,1)S(1)} %get-tuple-element.59.refs_0_, bf16[4,64,512]{2,1,0:T(8,128)(2,1)S(1)} %copy-done.4, bf16[4,64,512]{2,1,0:T(8,128)(2,1)S(1)} %collective-permute-done.12.refs_2_, ...), custom_call_target="tpu_custom_call" | custom-call | flops 10000001024 | bytes 1000 | tf_op jit(solution)/shard_map/near_update/pallas_call | solution.py:216
  58.3 1.5 %far_update.5 = (f32[2,128,768]{2,1,0:T(8,128)S(1)}, s16[144,256]{1,0:T(8,128)(2,1)S(1)}, s16[144,1792]{1,0:T(8,128)(2,1)S(1)}) custom-call(s32[7]{0:T(128)S(1)} %stack.31.where_ref, s32[8,12]{1,0:T(8,128)S(1)} %bitcast.24, bf16[4,64,512]{2,1,0:T(8,128)(2,1)S(1)} %collective-permute-done.13.da_ref, bf16[4,64,512]{2,1,0:T(8,128)(2,1)S(1)} %collective-permute-done.17.db_ref, ...), custom_call_target="tpu_custom_call" | custom-call | flops 4000001024 | bytes 1000 | tf_op jit(solution)/shard_map/far_update/pallas_call | solution.py:267
  59.9 4.4 %collective-permute-done.20.refs_0_.refs_1_ = s16[144,1024]{1,0:T(8,128)(2,1)S(1)} collective-permute-done((s16[144,1024]{1,0:T(8,128)(2,1)S(1)}, s16[144,1024]{1,0:T(8,128)(2,1)S(1)}, u32[]{:S(2)}, u32[]{:S(2)}) %collective-permute-start.20) | collective-permute-done | bytes 294944 | tf_op jit(solution)/shard_map/ppermute | solution.py:456
  64.3 1.6 %combine.3.refs_1_ = f32[384,768]{1,0:T(8,128)} custom-call(s32[7]{0:T(128)S(1)} %stack.31.where_ref, f32[1536,768]{1,0:T(8,128)S(1)} %bitcast.14, f32[128,768]{1,0:T(8,128)S(1)} %get-tuple-element.69.kept_ref, s16[144,1024]{1,0:T(8,128)(2,1)S(1)} %collective-permute-done.20.refs_0_.refs_1_), custom_call_target="tpu_custom_call" | custom-call | flops 1000 | bytes 1000 | tf_op jit(solution)/shard_map/combine/pallas_call | solution.py:353
  66.0 2.3 %near_update.4.refs_1_ = f32[4,128,768]{2,1,0:T(8,128)S(1)} custom-call(s32[8,12]{1,0:T(8,128)S(1)} %bitcast.25, bf16[4,64,512]{2,1,0:T(8,128)(2,1)S(1)} %get-tuple-element.64.refs_0_, bf16[4,64,512]{2,1,0:T(8,128)(2,1)S(1)} %get-tuple-element.61.refs_1_, bf16[4,64,512]{2,1,0:T(8,128)(2,1)S(1)} %collective-permute-done.3.refs_2_, ...), custom_call_target="tpu_custom_call" | custom-call | flops 10000001024 | bytes 1000 | tf_op jit(solution)/shard_map/near_update/pallas_call | solution.py:216
  68.2 7.8 %collective-permute-done.21.got_ref = s16[144,1792]{1,0:T(8,128)(2,1)S(1)} collective-permute-done((s16[144,1792]{1,0:T(8,128)(2,1)S(1)}, s16[144,1792]{1,0:T(8,128)(2,1)S(1)}, u32[]{:S(2)}, u32[]{:S(2)}) %collective-permute-start.21) | collective-permute-done | bytes 516128 | tf_op jit(solution)/shard_map/ppermute | solution.py:456
  76.4 3.1 %collective-permute-start.22 = (s16[144,1024]{1,0:T(8,128)(2,1)S(1)}, s16[144,1024]{1,0:T(8,128)(2,1)S(1)}, u32[]{:S(2)}, u32[]{:S(2)}) collective-permute-start(s16[144,1024]{1,0:T(8,128)(2,1)S(1)} %get-tuple-element.77.refs_2_), channel_id=1, source_target_pairs={{0,16},{8,24},{16,0},{24,8},{1,17},{9,25},{17,1},{25,9},{2,18},{10... | collective-permute-start | bytes 884744 | tf_op jit(solution)/shard_map/ppermute | solution.py:456
  79.5 1.6 %far_update.4 = (f32[128,768]{1,0:T(8,128)S(1)}, s16[144,256]{1,0:T(8,128)(2,1)S(1)}, s16[144,768]{1,0:T(8,128)(2,1)S(1)}, s16[144,768]{1,0:T(8,128)(2,1)S(1)}, s16[144,768]{1,0:T(8,128)(2,1)S(1)}) custom-call(s32[7]{0:T(128)S(1)} %stack.31.where_ref, s32[8,12]{1,0:T(8,128)S(1)} %bitcast.26, bf16[4,64,512]{2,1,0:T(8,128)(2,1)S(1)} %collective-permute-done.4.da_ref, ...), custom_call_target="tpu_custom_call" | custom-call | flops 4000001024 | bytes 1000 | tf_op jit(solution)/shard_map/far_update/pallas_call | solution.py:267
  81.1 1.9 %collective-permute-start.23 = (s16[144,256]{1,0:T(8,128)(2,1)S(1)}, s16[144,256]{1,0:T(8,128)(2,1)S(1)}, u32[]{:S(2)}, u32[]{:S(2)}) collective-permute-start(s16[144,256]{1,0:T(8,128)(2,1)S(1)} %get-tuple-element.78.mine_ref), channel_id=1, source_target_pairs={{0,8},{1,9},{6,14},{7,15},{8,0},{9,1},{14,6},{15,7},{16,24},{17,25... | collective-permute-start | bytes 221192 | tf_op jit(solution)/shard_map/ppermute | solution.py:453
  83.0 6.9 %collective-permute-done.23.got_ref = s16[144,256]{1,0:T(8,128)(2,1)S(1)} collective-permute-done((s16[144,256]{1,0:T(8,128)(2,1)S(1)}, s16[144,256]{1,0:T(8,128)(2,1)S(1)}, u32[]{:S(2)}, u32[]{:S(2)}) %collective-permute-start.23) | collective-permute-done | bytes 73760 | tf_op jit(solution)/shard_map/ppermute | solution.py:453
  90.0 1.9 %collective-permute-start.24 = (s16[144,256]{1,0:T(8,128)(2,1)S(1)}, s16[144,256]{1,0:T(8,128)(2,1)S(1)}, u32[]{:S(2)}, u32[]{:S(2)}) collective-permute-start(s16[144,256]{1,0:T(8,128)(2,1)S(1)} %add_coded.1.refs_4_), channel_id=1, source_target_pairs={{0,16},{1,17},{6,22},{7,23},{8,24},{9,25},{14,30},{15,31},{16,0},{... | collective-permute-start | bytes 221192 | tf_op jit(solution)/shard_map/ppermute | solution.py:453
  91.9 6.2 %collective-permute-done.24.refs_5_ = s16[144,256]{1,0:T(8,128)(2,1)S(1)} collective-permute-done((s16[144,256]{1,0:T(8,128)(2,1)S(1)}, s16[144,256]{1,0:T(8,128)(2,1)S(1)}, u32[]{:S(2)}, u32[]{:S(2)}) %collective-permute-start.24) | collective-permute-done | bytes 73760 | tf_op jit(solution)/shard_map/ppermute | solution.py:453
  98.0 0.8 pivots.1.own_ref
  98.8 1.3 collective-permute-start.25
  100.5 1.1 collective-permute-start.28
  101.6 2.1 %collective-permute-start.27 = (s16[144,768]{1,0:T(8,128)(2,1)S(1)}, s16[144,768]{1,0:T(8,128)(2,1)S(1)}, u32[]{:S(2)}, u32[]{:S(2)}) collective-permute-start(s16[144,768]{1,0:T(8,128)(2,1)S(1)} %get-tuple-element.82), channel_id=1, source_target_pairs={{0,16},{8,24},{16,0},{24,8},{1,17},{9,25},{17,1},{25,9},{2,18},{10... | collective-permute-start | bytes 663560 | tf_op jit(solution)/shard_map/ppermute | solution.py:456
  103.7 1.6 %combine.4.refs_3_ = f32[384,768]{1,0:T(8,128)} custom-call(s32[7]{0:T(128)S(1)} %stack.31.where_ref, f32[1536,768]{1,0:T(8,128)S(1)} %bitcast.14, f32[128,768]{1,0:T(8,128)S(1)} %get-tuple-element.85.kept_ref, s16[144,1024]{1,0:T(8,128)(2,1)S(1)} %collective-permute-done.22.refs_3_.refs_0_, f32[384,768]{1,0:T(8,128)} %combine.3.refs_1_), custom_call_target="tpu_custom_call", output_to_operand_aliasing={{}: (4, {})} | custom-call | flops 1000 | bytes 1000 | tf_op jit(solution)/shard_map/combine/pallas_call | solution.py:353
  105.4 24.9 %factor.1 = f32[6,128,128]{2,1,0:T(8,128)} custom-call(s32[7]{0:T(128)S(1)} %stack.31.where_ref, f32[6,128,128]{2,1,0:T(8,128)S(1)} %pivots.1.own_ref, f32[6,128,128]{2,1,0:T(8,128)S(1)} %collective-permute-done.25.other_ref), custom_call_target="tpu_custom_call" | custom-call | flops 20000000000 | bytes 1000 | tf_op jit(solution)/shard_map/factor/pallas_call | solution.py:94
  130.3 1.8 %combine.5 = f32[384,768]{1,0:T(8,128)} custom-call(s32[7]{0:T(128)S(1)} %stack.31.where_ref, f32[1536,768]{1,0:T(8,128)S(1)} %bitcast.14, f32[128,768]{1,0:T(8,128)S(1)} %get-tuple-element.79.kept_ref, s16[144,768]{1,0:T(8,128)(2,1)S(1)} %collective-permute-done.26.refs_0_, ...), custom_call_target="tpu_custom_call", output_to_operand_aliasing={{}: (6, {})} | custom-call | flops 1000 | bytes 1000 | tf_op jit(solution)/shard_map/combine/pallas_call | solution.py:353
  (49 shorter events, 1.9 us)
Async XLA Ops:
  0.6 26.7 %collective-permute-start.10 = (bf16[8,128,768]{2,1,0:T(8,128)(2,1)}, bf16[8,128,768]{2,1,0:T(8,128)(2,1)S(1)}, u32[]{:S(2)}, u32[]{:S(2)}) collective-permute-start(bf16[8,128,768]{2,1,0:T(8,128)(2,1)} %bitcast.18), channel_id=1, source_target_pairs={{0,4},{4,0},{1,5},{5,1},{2,6},{6,2},{3,7},{7,3},{8,12},{12,8},{9,1... | collective-permute-start | bytes 4718600 | tf_op jit(solution)/shard_map/ppermute | solution.py:460
  0.7 1.4 %copy-start = (bf16[1,8,1536,64]{2,3,1,0:T(8,128)(2,1)S(1)}, bf16[1,8,1536,64]{2,3,1,0:T(8,128)(2,1)}, u32[]{:S(2)}) copy-start(bf16[1,8,1536,64]{2,3,1,0:T(8,128)(2,1)} %param.5) | copy-start | bytes 4718596
  2.1 13.3 %copy-start.6 = (s32[1,8,6]{1,0,2:T(1,128)S(1)}, s32[1,8,6]{1,0,2:T(1,128)}, u32[]{:S(2)}) copy-start(s32[1,8,6]{1,0,2:T(1,128)} %param.8) | copy-start | bytes 580
  2.1 25.2 %copy-start.2 = (bf16[1,8,128,768]{3,2,1,0:T(8,128)(2,1)S(1)}, bf16[1,8,128,768]{3,2,1,0:T(8,128)(2,1)}, u32[]{:S(2)}) copy-start(bf16[1,8,128,768]{3,2,1,0:T(8,128)(2,1)} %param.6) | copy-start | bytes 4718596
  3.0 9.5 %collective-permute-start = (bf16[4,64,512]{2,1,0:T(8,128)(2,1)}, bf16[4,64,512]{2,1,0:T(8,128)(2,1)}, u32[]{:S(2)}, u32[]{:S(2)}) collective-permute-start(bf16[4,64,512]{2,1,0:T(8,128)(2,1)} %get-tuple-element.46.refs_0_), channel_id=1, source_target_pairs={{0,1},{1,0},{2,3},{3,2},{4,5},{5,4},{6,7},{7,6},{8,9},{9,8},{10,11... | collective-permute-start | bytes 786440 | tf_op jit(solution)/shard_map/ppermute | solution.py:472
  3.1 10.9 %collective-permute-start.5 = (bf16[4,64,512]{2,1,0:T(8,128)(2,1)}, bf16[4,64,512]{2,1,0:T(8,128)(2,1)}, u32[]{:S(2)}, u32[]{:S(2)}) collective-permute-start(bf16[4,64,512]{2,1,0:T(8,128)(2,1)} %get-tuple-element.53.refs_1_), channel_id=1, source_target_pairs={{0,2},{1,3},{2,0},{3,1},{4,6},{5,7},{6,4},{7,5},{8,10},{9,11},{10,... | collective-permute-start | bytes 786440 | tf_op jit(solution)/shard_map/ppermute | solution.py:472
  5.1 13.0 %collective-permute-start.11 = (bf16[4,64,512]{2,1,0:T(8,128)(2,1)}, bf16[4,64,512]{2,1,0:T(8,128)(2,1)}, u32[]{:S(2)}, u32[]{:S(2)}) collective-permute-start(bf16[4,64,512]{2,1,0:T(8,128)(2,1)} %get-tuple-element.53.refs_1_), channel_id=1, source_target_pairs={{0,1},{1,0},{2,3},{3,2},{4,5},{5,4},{6,7},{7,6},{8,9},{9,8},{10,11... | collective-permute-start | bytes 786440 | tf_op jit(solution)/shard_map/ppermute | solution.py:472
  6.6 11.6 %collective-permute-start.15 = (bf16[4,64,512]{2,1,0:T(8,128)(2,1)}, bf16[4,64,512]{2,1,0:T(8,128)(2,1)}, u32[]{:S(2)}, u32[]{:S(2)}) collective-permute-start(bf16[4,64,512]{2,1,0:T(8,128)(2,1)} %get-tuple-element.46.refs_0_), channel_id=1, source_target_pairs={{0,2},{1,3},{2,0},{3,1},{4,6},{5,7},{6,4},{7,5},{8,10},{9,11},{10,... | collective-permute-start | bytes 786440 | tf_op jit(solution)/shard_map/ppermute | solution.py:472
  12.5 11.3 %collective-permute-start.1 = (bf16[4,64,512]{2,1,0:T(8,128)(2,1)}, bf16[4,64,512]{2,1,0:T(8,128)(2,1)}, u32[]{:S(2)}, u32[]{:S(2)}) collective-permute-start(bf16[4,64,512]{2,1,0:T(8,128)(2,1)} %collective-permute-done.refs_2_), channel_id=1, source_target_pairs={{0,2},{1,3},{2,0},{3,1},{4,6},{5,7},{6,4},{7,5},{8,10},{9,11},{10,... | collective-permute-start | bytes 786440 | tf_op jit(solution)/shard_map/ppermute | solution.py:472
  14.0 11.8 %collective-permute-start.6 = (bf16[4,64,512]{2,1,0:T(8,128)(2,1)}, bf16[4,64,512]{2,1,0:T(8,128)(2,1)}, u32[]{:S(2)}, u32[]{:S(2)}) collective-permute-start(bf16[4,64,512]{2,1,0:T(8,128)(2,1)} %collective-permute-done.5.refs_5_), channel_id=1, source_target_pairs={{0,1},{1,0},{2,3},{3,2},{4,5},{5,4},{6,7},{7,6},{8,9},{9,8},{10,11... | collective-permute-start | bytes 786440 | tf_op jit(solution)/shard_map/ppermute | solution.py:472
  14.7 0.7 copy-start.3
  18.1 17.5 %collective-permute-start.12 = (bf16[4,64,512]{2,1,0:T(8,128)(2,1)S(1)}, bf16[4,64,512]{2,1,0:T(8,128)(2,1)S(1)}, u32[]{:S(2)}, u32[]{:S(2)}) collective-permute-start(bf16[4,64,512]{2,1,0:T(8,128)(2,1)S(1)} %get-tuple-element.59.refs_0_), channel_id=1, source_target_pairs={{0,1},{1,0},{2,3},{3,2},{4,5},{5,4},{6,7},{7,6},{8,9},{9,8},{10,11... | collective-permute-start | bytes 786440 | tf_op jit(solution)/shard_map/ppermute | solution.py:472
  18.2 18.0 %collective-permute-start.16 = (bf16[4,64,512]{2,1,0:T(8,128)(2,1)}, bf16[4,64,512]{2,1,0:T(8,128)(2,1)S(1)}, u32[]{:S(2)}, u32[]{:S(2)}) collective-permute-start(bf16[4,64,512]{2,1,0:T(8,128)(2,1)} %copy-done.3), channel_id=1, source_target_pairs={{0,2},{1,3},{2,0},{3,1},{4,6},{5,7},{6,4},{7,5},{8,10},{9,11},{10,... | collective-permute-start | bytes 786440 | tf_op jit(solution)/shard_map/ppermute | solution.py:472
  23.8 12.9 %collective-permute-start.2 = (bf16[4,64,512]{2,1,0:T(8,128)(2,1)}, bf16[4,64,512]{2,1,0:T(8,128)(2,1)S(1)}, u32[]{:S(2)}, u32[]{:S(2)}) collective-permute-start(bf16[4,64,512]{2,1,0:T(8,128)(2,1)} %copy-done.3), channel_id=1, source_target_pairs={{0,1},{1,0},{2,3},{3,2},{4,5},{5,4},{6,7},{7,6},{8,9},{9,8},{10,11... | collective-permute-start | bytes 786440 | tf_op jit(solution)/shard_map/ppermute | solution.py:472
  25.8 12.5 %collective-permute-start.7 = (bf16[4,64,512]{2,1,0:T(8,128)(2,1)S(1)}, bf16[4,64,512]{2,1,0:T(8,128)(2,1)S(1)}, u32[]{:S(2)}, u32[]{:S(2)}) collective-permute-start(bf16[4,64,512]{2,1,0:T(8,128)(2,1)S(1)} %get-tuple-element.59.refs_0_), channel_id=1, source_target_pairs={{0,2},{1,3},{2,0},{3,1},{4,6},{5,7},{6,4},{7,5},{8,10},{9,11},{10,... | collective-permute-start | bytes 786440 | tf_op jit(solution)/shard_map/ppermute | solution.py:472
  27.3 1.4 %copy-start.5 = (s32[1,8,12]{2,1,0:T(8,128)S(1)}, s32[1,8,12]{2,1,0:T(8,128)}, u32[]{:S(2)}) copy-start(s32[1,8,12]{2,1,0:T(8,128)} %param.7) | copy-start | bytes 1156
  31.7 3.7 %copy-start.1 = (bf16[1,8,1536,64]{2,3,1,0:T(8,128)(2,1)S(1)}, bf16[1,8,1536,64]{2,3,1,0:T(8,128)(2,1)}, u32[]{:S(2)}) copy-start(bf16[1,8,1536,64]{2,3,1,0:T(8,128)(2,1)} %param.5) | copy-start | bytes 4718596
  33.8 22.3 %copy-start.4 = (bf16[4,64,512]{2,1,0:T(8,128)(2,1)S(1)}, bf16[4,64,512]{2,1,0:T(8,128)(2,1)}, u32[]{:S(2)}) copy-start(bf16[4,64,512]{2,1,0:T(8,128)(2,1)} %copy-done.3) | copy-start | bytes 786436
  33.8 19.3 %collective-permute-start.19 = (s16[144,1792]{1,0:T(8,128)(2,1)S(1)}, s16[144,1792]{1,0:T(8,128)(2,1)S(1)}, u32[]{:S(2)}, u32[]{:S(2)}) collective-permute-start(s16[144,1792]{1,0:T(8,128)(2,1)S(1)} %get-tuple-element.68), channel_id=1, source_target_pairs={{0,8},{8,0},{16,24},{24,16},{1,9},{9,1},{17,25},{25,17},{2,10},{10... | collective-permute-start | bytes 1548296 | tf_op jit(solution)/shard_map/ppermute | solution.py:456
  35.6 9.3 %collective-permute-start.13 = (bf16[4,64,512]{2,1,0:T(8,128)(2,1)S(1)}, bf16[4,64,512]{2,1,0:T(8,128)(2,1)S(1)}, u32[]{:S(2)}, u32[]{:S(2)}) collective-permute-start(bf16[4,64,512]{2,1,0:T(8,128)(2,1)S(1)} %collective-permute-done.12.refs_2_), channel_id=1, source_target_pairs={{0,2},{1,3},{2,0},{3,1},{4,6},{5,7},{6,4},{7,5},{8,10},{9,11},{10,... | collective-permute-start | bytes 786440 | tf_op jit(solution)/shard_map/ppermute | solution.py:472
  36.2 9.3 %collective-permute-start.17 = (bf16[4,64,512]{2,1,0:T(8,128)(2,1)S(1)}, bf16[4,64,512]{2,1,0:T(8,128)(2,1)S(1)}, u32[]{:S(2)}, u32[]{:S(2)}) collective-permute-start(bf16[4,64,512]{2,1,0:T(8,128)(2,1)S(1)} %collective-permute-done.16.refs_5_), channel_id=1, source_target_pairs={{0,1},{1,0},{2,3},{3,2},{4,5},{5,4},{6,7},{7,6},{8,9},{9,8},{10,11... | collective-permute-start | bytes 786440 | tf_op jit(solution)/shard_map/ppermute | solution.py:472
  36.7 14.3 %collective-permute-start.3 = (bf16[4,64,512]{2,1,0:T(8,128)(2,1)S(1)}, bf16[4,64,512]{2,1,0:T(8,128)(2,1)S(1)}, u32[]{:S(2)}, u32[]{:S(2)}) collective-permute-start(bf16[4,64,512]{2,1,0:T(8,128)(2,1)S(1)} %get-tuple-element.64.refs_0_), channel_id=1, source_target_pairs={{0,1},{1,0},{2,3},{3,2},{4,5},{5,4},{6,7},{7,6},{8,9},{9,8},{10,11... | collective-permute-start | bytes 786440 | tf_op jit(solution)/shard_map/ppermute | solution.py:472
  38.2 14.3 %collective-permute-start.8 = (bf16[4,64,512]{2,1,0:T(8,128)(2,1)S(1)}, bf16[4,64,512]{2,1,0:T(8,128)(2,1)S(1)}, u32[]{:S(2)}, u32[]{:S(2)}) collective-permute-start(bf16[4,64,512]{2,1,0:T(8,128)(2,1)S(1)} %get-tuple-element.61.refs_1_), channel_id=1, source_target_pairs={{0,2},{1,3},{2,0},{3,1},{4,6},{5,7},{6,4},{7,5},{8,10},{9,11},{10,... | collective-permute-start | bytes 786440 | tf_op jit(solution)/shard_map/ppermute | solution.py:472
  44.9 21.0 %collective-permute-start.14 = (bf16[4,64,512]{2,1,0:T(8,128)(2,1)S(1)}, bf16[4,64,512]{2,1,0:T(8,128)(2,1)S(1)}, u32[]{:S(2)}, u32[]{:S(2)}) collective-permute-start(bf16[4,64,512]{2,1,0:T(8,128)(2,1)S(1)} %get-tuple-element.61.refs_1_), channel_id=1, source_target_pairs={{0,1},{1,0},{2,3},{3,2},{4,5},{5,4},{6,7},{7,6},{8,9},{9,8},{10,11... | collective-permute-start | bytes 786440 | tf_op jit(solution)/shard_map/ppermute | solution.py:472
  45.5 20.5 %collective-permute-start.18 = (bf16[4,64,512]{2,1,0:T(8,128)(2,1)S(1)}, bf16[4,64,512]{2,1,0:T(8,128)(2,1)S(1)}, u32[]{:S(2)}, u32[]{:S(2)}) collective-permute-start(bf16[4,64,512]{2,1,0:T(8,128)(2,1)S(1)} %get-tuple-element.64.refs_0_), channel_id=1, source_target_pairs={{0,2},{1,3},{2,0},{3,1},{4,6},{5,7},{6,4},{7,5},{8,10},{9,11},{10,... | collective-permute-start | bytes 786440 | tf_op jit(solution)/shard_map/ppermute | solution.py:472
  51.1 28.4 %collective-permute-start.4 = (bf16[4,64,512]{2,1,0:T(8,128)(2,1)S(1)}, bf16[4,64,512]{2,1,0:T(8,128)(2,1)S(1)}, u32[]{:S(2)}, u32[]{:S(2)}) collective-permute-start(bf16[4,64,512]{2,1,0:T(8,128)(2,1)S(1)} %collective-permute-done.3.refs_2_), channel_id=1, source_target_pairs={{0,2},{1,3},{2,0},{3,1},{4,6},{5,7},{6,4},{7,5},{8,10},{9,11},{10,... | collective-permute-start | bytes 786440 | tf_op jit(solution)/shard_map/ppermute | solution.py:472
  52.6 26.9 %collective-permute-start.9 = (bf16[4,64,512]{2,1,0:T(8,128)(2,1)S(1)}, bf16[4,64,512]{2,1,0:T(8,128)(2,1)S(1)}, u32[]{:S(2)}, u32[]{:S(2)}) collective-permute-start(bf16[4,64,512]{2,1,0:T(8,128)(2,1)S(1)} %collective-permute-done.8.refs_5_), channel_id=1, source_target_pairs={{0,1},{1,0},{2,3},{3,2},{4,5},{5,4},{6,7},{7,6},{8,9},{9,8},{10,11... | collective-permute-start | bytes 786440 | tf_op jit(solution)/shard_map/ppermute | solution.py:472
  53.4 10.9 %slice-start = ((s8[4718592]{0:T(1024)(128)(4,1)}), s8[4194304]{0:T(1024)(128)(4,1)S(1)}, s32[]{:S(2)}) async-start(s8[4718592]{0:T(1024)(128)(4,1)} %bitcast.13), calls=%async_computation | async-start | bytes 8388608
  53.4 10.9 %slice-start.1 = ((s8[4718592]{0:T(1024)(128)(4,1)}), s8[524288]{0:T(1024)(128)(4,1)S(1)}, s32[]{:S(2)}) async-start(s8[4718592]{0:T(1024)(128)(4,1)} %bitcast.13), calls=%async_computation.1 | async-start | bytes 1048576
  53.4 10.8 %collective-permute-start.20 = (s16[144,1024]{1,0:T(8,128)(2,1)S(1)}, s16[144,1024]{1,0:T(8,128)(2,1)S(1)}, u32[]{:S(2)}, u32[]{:S(2)}) collective-permute-start(s16[144,1024]{1,0:T(8,128)(2,1)S(1)} %get-tuple-element.70.refs_0_), channel_id=1, source_target_pairs={{0,16},{8,24},{16,0},{24,8},{1,17},{9,25},{17,1},{25,9},{2,18},{10... | collective-permute-start | bytes 884744 | tf_op jit(solution)/shard_map/ppermute | solution.py:456
  64.3 11.8 %collective-permute-start.21 = (s16[144,1792]{1,0:T(8,128)(2,1)S(1)}, s16[144,1792]{1,0:T(8,128)(2,1)S(1)}, u32[]{:S(2)}, u32[]{:S(2)}) collective-permute-start(s16[144,1792]{1,0:T(8,128)(2,1)S(1)} %get-tuple-element.76), channel_id=1, source_target_pairs={{0,8},{8,0},{16,24},{24,16},{1,9},{9,1},{17,25},{25,17},{2,10},{10... | collective-permute-start | bytes 1548296 | tf_op jit(solution)/shard_map/ppermute | solution.py:456
  76.4 21.7 %collective-permute-start.22 = (s16[144,1024]{1,0:T(8,128)(2,1)S(1)}, s16[144,1024]{1,0:T(8,128)(2,1)S(1)}, u32[]{:S(2)}, u32[]{:S(2)}) collective-permute-start(s16[144,1024]{1,0:T(8,128)(2,1)S(1)} %get-tuple-element.77.refs_2_), channel_id=1, source_target_pairs={{0,16},{8,24},{16,0},{24,8},{1,17},{9,25},{17,1},{25,9},{2,18},{10... | collective-permute-start | bytes 884744 | tf_op jit(solution)/shard_map/ppermute | solution.py:456
  81.1 8.8 %collective-permute-start.23 = (s16[144,256]{1,0:T(8,128)(2,1)S(1)}, s16[144,256]{1,0:T(8,128)(2,1)S(1)}, u32[]{:S(2)}, u32[]{:S(2)}) collective-permute-start(s16[144,256]{1,0:T(8,128)(2,1)S(1)} %get-tuple-element.78.mine_ref), channel_id=1, source_target_pairs={{0,8},{1,9},{6,14},{7,15},{8,0},{9,1},{14,6},{15,7},{16,24},{17,25... | collective-permute-start | bytes 221192 | tf_op jit(solution)/shard_map/ppermute | solution.py:453
  90.0 8.1 %collective-permute-start.24 = (s16[144,256]{1,0:T(8,128)(2,1)S(1)}, s16[144,256]{1,0:T(8,128)(2,1)S(1)}, u32[]{:S(2)}, u32[]{:S(2)}) collective-permute-start(s16[144,256]{1,0:T(8,128)(2,1)S(1)} %add_coded.1.refs_4_), channel_id=1, source_target_pairs={{0,16},{1,17},{6,22},{7,23},{8,24},{9,25},{14,30},{15,31},{16,0},{... | collective-permute-start | bytes 221192 | tf_op jit(solution)/shard_map/ppermute | solution.py:453
  98.8 6.5 %collective-permute-start.25 = (f32[6,128,128]{2,1,0:T(8,128)S(1)}, f32[6,128,128]{2,1,0:T(8,128)S(1)}, u32[]{:S(2)}, u32[]{:S(2)}) collective-permute-start(f32[6,128,128]{2,1,0:T(8,128)S(1)} %pivots.1.own_ref), channel_id=1, source_target_pairs={{0,4},{1,5},{6,2},{7,3},{8,12},{9,13},{14,10},{15,11},{16,20},{17,... | collective-permute-start | bytes 1179656 | tf_op jit(solution)/shard_map/ppermute | solution.py:453
  100.2 30.1 %collective-permute-start.26 = (s16[144,768]{1,0:T(8,128)(2,1)S(1)}, s16[144,768]{1,0:T(8,128)(2,1)S(1)}, u32[]{:S(2)}, u32[]{:S(2)}) collective-permute-start(s16[144,768]{1,0:T(8,128)(2,1)S(1)} %get-tuple-element.80), channel_id=1, source_target_pairs={{0,8},{8,0},{16,24},{24,16},{1,9},{9,1},{17,25},{25,17},{2,10},{10... | collective-permute-start | bytes 663560 | tf_op jit(solution)/shard_map/ppermute | solution.py:456
  100.5 29.8 %collective-permute-start.28 = (s16[144,768]{1,0:T(8,128)(2,1)S(1)}, s16[144,768]{1,0:T(8,128)(2,1)S(1)}, u32[]{:S(2)}, u32[]{:S(2)}) collective-permute-start(s16[144,768]{1,0:T(8,128)(2,1)S(1)} %get-tuple-element.84), channel_id=1, source_target_pairs={{0,24},{8,16},{16,8},{24,0},{1,25},{9,17},{17,9},{25,1},{2,26},{10... | collective-permute-start | bytes 663560 | tf_op jit(solution)/shard_map/ppermute | solution.py:456
  101.6 28.7 %collective-permute-start.27 = (s16[144,768]{1,0:T(8,128)(2,1)S(1)}, s16[144,768]{1,0:T(8,128)(2,1)S(1)}, u32[]{:S(2)}, u32[]{:S(2)}) collective-permute-start(s16[144,768]{1,0:T(8,128)(2,1)S(1)} %get-tuple-element.82), channel_id=1, source_target_pairs={{0,16},{8,24},{16,0},{24,8},{1,17},{9,25},{17,1},{25,9},{2,18},{10... | collective-permute-start | bytes 663560 | tf_op jit(solution)/shard_map/ppermute | solution.py:456

commit v4 on v3

--- a/solution.py
+++ b/solution.py
@@ -45,34 +45,23 @@
     return codes.astype(jnp.int32).astype(jnp.float32) * scale
 
 
-def lu_pair(ref, j):
+def lu_step(ref, j):
     size = ref.shape[1]
     top = j // 8 * 8
-    first = ref[:, j : j + 1, :]
-    second = ref[:, j + 1 : j + 2, :]
+    row = ref[:, j : j + 1, :]
+    inverse = 1.0 / row[:, :, j : j + 1]
     lanes = lax.broadcasted_iota(jnp.int32, (1, 1, size), 2)
-    above = first[:, :, j + 1 : j + 2]
-    inverse = 1.0 / first[:, :, j : j + 1]
-    under = second[:, :, j : j + 1] * inverse
-    later = 1.0 / (second[:, :, j + 1 : j + 2] - under * above)
-    first = jnp.where(lanes > j, first, 0.0)
-    swept = second - under * first
-    ref[:, j + 1 : j + 2, :] = jnp.where(lanes == j, under, swept)
-    second = jnp.where(lanes > j + 1, swept, 0.0)
-
-    def sweep(block, keep):
-        one = block[:, :, j : j + 1] * inverse
-        two = (block[:, :, j + 1 : j + 2] - one * above) * later
-        result = block - one * first - two * second
-        result = jnp.where(lanes == j, one, jnp.where(lanes == j + 1, two, result))
-        return result if keep is None else jnp.where(keep, result, block)
-
-    if j % 8 != 6:
+    used = jnp.where(lanes > j, row, 0.0)
+    if j % 8 != 7:
+        head = ref[:, top : top + 8, :]
         rows = lax.broadcasted_iota(jnp.int32, (1, 8, 1), 1) + top
-        head = ref[:, top : top + 8, :]
-        ref[:, top : top + 8, :] = sweep(head, rows > j + 1)
+        factor = jnp.where(rows > j, head[:, :, j : j + 1] * inverse, 0.0)
+        swept = head - factor * used
+        ref[:, top : top + 8, :] = jnp.where((lanes == j) & (rows > j), factor, swept)
     if top + 8 < size:
-        ref[:, top + 8 :, :] = sweep(ref[:, top + 8 :, :], None)
+        rest = ref[:, top + 8 :, :]
+        factor = rest[:, :, j : j + 1] * inverse
+        ref[:, top + 8 :, :] = jnp.where(lanes == j, factor, rest - factor * used)
 
 
 def lu_kernel(where_ref, own_ref, other_ref, out_ref):
@@ -86,8 +75,8 @@
     def _():
         out_ref[...] = other_ref[...]
 
-    for j in range(0, out_ref.shape[1], 2):
-        lu_pair(out_ref, j)
+    for j in range(out_ref.shape[1]):
+        lu_step(out_ref, j)
 
 
 def factor(where, own, other):
@@ -225,20 +214,28 @@
     )(lpat, *pieces, right)
 
 
-def far_kernel(chunk, chunks, layers, last, where_ref, lpat_ref, da_ref, db_ref, *refs):
-    right_ref, before_ref, kept_ref, diag_ref = refs[:4]
-    sent_refs, (left, acc) = refs[4:-2], refs[-2:]
+def far_kernel(chunk, chunks, layers, earlier, where_ref, lpat_ref, da_ref, db_ref, *refs):
+    right_ref, before_ref = refs[:2]
+    refs = refs[2:]
+    if earlier:
+        old_ref, refs = refs[0], refs[1:]
+    kept_ref, diag_ref = refs[:2]
+    sent_refs, (left, acc) = refs[2:-2], refs[-2:]
     layer = where_ref[0]
     cols = right_ref.shape[2]
     total = product(chunk, chunks, layers, lpat_ref, [(da_ref, db_ref)], right_ref, left)
     acc[...] = before_ref[...] + total.reshape(acc.shape)
+    begin = 0
+    if earlier:
+        begin = old_ref.shape[1]
+        diag_ref[:, :begin] = old_ref[...]
     for i in range(cols // BLK // chunks):
         q = i * chunks + chunk
-        lanes = slice(i * BLK, (i + 1) * BLK)
+        lanes = slice(begin + i * BLK, begin + (i + 1) * BLK)
         diag_ref[:BLK, lanes], diag_ref[BLK:, lanes] = encode(
             acc[where_ref[5] + i, :, q * BLK : (q + 1) * BLK]
         )
-    if last:
+    if chunk == chunks - 1:
         for s in range(1, layers):
             sent_refs[s - 1][:BLK], sent_refs[s - 1][BLK:] = encode(acc[layer ^ s])
         kept_ref[...] = acc[layer]
@@ -247,31 +244,32 @@
         for n, s in enumerate((1, 3)):
             lanes = slice(n * cols, (n + 1) * cols)
             sent_ref[:BLK, lanes], sent_ref[BLK:, lanes] = encode(acc[layer ^ s])
-        sent_ref[:, 2 * cols :] = diag_ref[...]
+        if sent_ref.shape[1] > 2 * cols:
+            sent_ref[:, 2 * cols :] = diag_ref[...]
         kept_ref[0] = acc[layer]
         kept_ref[1] = acc[layer ^ 2]
 
 
-def far_update(where, lpat, pieces, right, before, chunk, chunks, layers):
+def far_update(where, lpat, pieces, right, before, earlier, chunk, chunks, layers):
     half, depth, width = pieces[0].shape
     supers, _, cols = right.shape
     beside = cols // chunks
     coded = BLK + EXP_ROWS
-    last = chunk == chunks - 1
-    if last:
+    if chunk == chunks - 1:
         kept = (BLK, cols)
         sent = [(coded, cols)] * (layers - 1)
     else:
         kept = (2, BLK, cols)
-        sent = [(coded, 2 * cols + beside)]
-    return pl.pallas_call(
-        functools.partial(far_kernel, chunk, chunks, layers, last),
+        sent = [(coded, 2 * cols + (beside if chunk == 0 else 0))]
+    known = sum(part.shape[1] for part in earlier)
+    return pl.pallas_call(
+        functools.partial(far_kernel, chunk, chunks, layers, len(earlier)),
         out_shape=[
             jax.ShapeDtypeStruct(kept, jnp.float32),
-            jax.ShapeDtypeStruct((coded, beside), jnp.int16),
+            jax.ShapeDtypeStruct((coded, known + beside), jnp.int16),
         ]
         + [jax.ShapeDtypeStruct(shape, jnp.int16) for shape in sent],
-        in_specs=[SMEM] * 2 + [VMEM] * 4,
+        in_specs=[SMEM] * 2 + [VMEM] * (4 + len(earlier)),
         out_specs=[VMEM] * (2 + len(sent)),
         scratch_shapes=[
             pltpu.VMEM((supers, depth, width), jnp.bfloat16),
@@ -280,7 +278,7 @@
         compiler_params=params(),
         cost_estimate=cost(FAR),
         name="far_update",
-    )(where, lpat, *pieces, right, before)
+    )(where, lpat, *pieces, right, before, *earlier)
 
 
 def halve_kernel(kept_ref, diag_ref, got_ref, sum_ref, sent_ref):
@@ -288,19 +286,19 @@
     sum_ref[...] = kept_ref[0] + decode(got_ref[:BLK, :cols], got_ref[BLK:, :cols])
     other = kept_ref[1] + decode(got_ref[:BLK, cols : 2 * cols], got_ref[BLK:, cols : 2 * cols])
     sent_ref[:BLK, :cols], sent_ref[BLK:, :cols] = encode(other)
-    diag = decode(diag_ref[:BLK], diag_ref[BLK:])
-    diag += decode(got_ref[:BLK, 2 * cols :], got_ref[BLK:, 2 * cols :])
-    sent_ref[:BLK, cols:], sent_ref[BLK:, cols:] = encode(diag)
+    if sent_ref.shape[1] > cols:
+        diag = decode(diag_ref[:BLK], diag_ref[BLK:])
+        diag += decode(got_ref[:BLK, 2 * cols :], got_ref[BLK:, 2 * cols :])
+        sent_ref[:BLK, cols:], sent_ref[BLK:, cols:] = encode(diag)
 
 
 def halve(kept, diag, got):
     cols = kept.shape[2]
-    beside = diag.shape[1]
     return pl.pallas_call(
         halve_kernel,
         out_shape=[
             jax.ShapeDtypeStruct((BLK, cols), jnp.float32),
-            jax.ShapeDtypeStruct((BLK + EXP_ROWS, cols + beside), jnp.int16),
+            jax.ShapeDtypeStruct((BLK + EXP_ROWS, got.shape[1] - cols), jnp.int16),
         ],
         in_specs=[VMEM] * 3,
         out_specs=[VMEM] * 2,
@@ -367,7 +365,7 @@
     )(where, anc, kept, *got, *held)
 
 
-def pivot_kernel(groups, where_ref, anc_ref, *refs):
+def pivot_kernel(rounds, chunks, where_ref, anc_ref, *refs):
     parts, (out_ref, blocks, sems) = refs[:-3], refs[-3:]
     copies = []
     for q in range(out_ref.shape[0]):
@@ -381,25 +379,25 @@
         copy.start()
     for copy in copies:
         copy.wait()
-    fresh = out_ref.shape[0] // len(groups)
-    taken = 0
-    for j, size in enumerate(groups):
-        terms = []
-        for ref in parts[taken : taken + size]:
-            begin = ref.shape[1] - fresh * BLK
-            terms.append(decode(ref[:BLK, begin:], ref[BLK:, begin:]))
-        taken += size
-        while len(terms) > 1:
-            terms = [terms[i] + terms[i + 1] for i in range(0, len(terms), 2)]
-        for i in range(fresh):
-            q = i * len(groups) + j
-            out_ref[q] = blocks[q] - terms[0][:, i * BLK : (i + 1) * BLK]
-
-
-def pivots(where, anc, groups, count):
+    fresh = out_ref.shape[0] // chunks
+    chunk = 0
+    for n, count in enumerate(rounds):
+        one, two = parts[2 * n : 2 * n + 2]
+        begin = one.shape[1] - count * fresh * BLK
+        total = decode(one[:BLK, begin:], one[BLK:, begin:])
+        total += decode(two[:BLK, begin:], two[BLK:, begin:])
+        for m in range(count):
+            for i in range(fresh):
+                q = i * chunks + chunk
+                at = (m * fresh + i) * BLK
+                out_ref[q] = blocks[q] - total[:, at : at + BLK]
+            chunk += 1
+
+
+def pivots(where, anc, groups, rounds, chunks, count):
     parts = [part for group in groups for part in group]
     return pl.pallas_call(
-        functools.partial(pivot_kernel, [len(group) for group in groups]),
+        functools.partial(pivot_kernel, rounds, chunks),
         out_shape=jax.ShapeDtypeStruct((count, BLK, BLK), jnp.float32),
         in_specs=[SMEM, ANY] + [VMEM] * len(parts),
         out_specs=VMEM,
@@ -483,29 +481,43 @@
         return (a, b, xa, xb, ya, yb), (da, db)
 
     near, far = gathered_chunk(0)
-    held, groups, waits = [], [], []
+    finished, groups, earlier, sent = [], [], [], None
     for j in range(chunks):
+        waits = [sent] if j == 1 else []
         part = near_update(lpat[0], near, after(near_right, *waits), j, chunks, layers)
-        out = far_update(where, lpat[0], far, far_right, part, j, chunks, layers)
+        if j > 1:
+            part = after(part, *first)
+        out = far_update(where, lpat[0], far, far_right, part, earlier, j, chunks, layers)
         kept, diag = out[:2]
         if j < chunks - 1:
+            spot = len(moved)
+            if j > 0:
+                gates.update({spot + n: (kept,) for n in (4,)})
             near, far = gathered_chunk(j + 1)
             kept, sent = halve(kept, diag, over_layers(out[2], 1))
             got = [over_layers(sent, 2)]
-            groups.append([sent, got[0]])
-            waits = [sent] if j == 0 else held
-            held = [combine(where, anc, kept, got, held, share, j)]
+            if j == 0:
+                groups.append([sent, got[0]])
+                first = got
+            else:
+                earlier = [diag]
+            finished.append((kept, got))
     near = from_holders(diag, lambda l, r, c: index(l ^ 1, r, c))
-    near = add_coded(diag, near)
+    near = add_coded(after(diag, sent), near)
     far = from_holders(near, lambda l, r, c: index(l ^ 2, r, c))
     steps = range(1, layers)
     got = [over_layers(after(out[1 + s], far) if s > 1 else out[1 + s], s) for s in steps]
     groups.append([near, far])
-    own = pivots(where, anc, groups, width // BLK)
+    own = pivots(where, anc, groups, [1, chunks - 1], chunks, width // BLK)
     other = from_holders(own, lambda l, r, c: index(l, 1 - r, c))
     diag_lu = factor(where, own, other)
-    held = combine(where, anc, after(kept, diag_lu), got, held, share, chunks - 1)
-    return held, diag_lu
+    finished.append((kept, got))
+    held = []
+    for j, (kept, got) in enumerate(finished):
+        if j > 0:
+            kept = after(kept, diag_lu)
+        held = [combine(where, anc, kept, got, held, share, j)]
+    return held[0], diag_lu
 
 
 def mask_rows(panel, pattern, block):

time: 135 us -> 118 us (0.87)
  Pallas kernels: 46.7 us -> 35.3 us
  starting transfers between devices: 36.2 us -> 33.1 us
  waiting for transfers between devices: 46.1 us -> 43.9 us
    pallas_call x1, Pallas kernels: 24.9 us -> 13.7 us  [factor(): pl.pallas_call(lu_kernel, out_shape=jax.ShapeDtypeStruct(own.shape, jnp.f...]
    ppermute x7, waiting for transfers between devices: 12.3 us -> 3.39 us  [over_layers(): return lax.ppermute(value, 'layer', xor_perm(layers, s))]
    ppermute x18, waiting for transfers between devices: 20.8 us -> 26.4 us  [over(): moved.append(lax.ppermute(value, 'col', xor_perm(cols, bit)))]
    ppermute x18, starting transfers between devices: 20 us -> 15.7 us  [over(): moved.append(lax.ppermute(value, 'col', xor_perm(cols, bit)))]
    ppermute x3, starting transfers between devices: 5.16 us -> 7.59 us  [from_holders(): return lax.ppermute(value, everyone, perm)]
  transfers between devices with their start and end apart: 29 -> 29, of which waited for: 9 -> 11; matrix products, arithmetic and copies ran while one was open for 0% -> 0% of each run, Pallas kernels for 33% -> 28%
where the time goes in v4:
time: 118 us; the launch traced here: 116 us
  waiting for transfers between devices  43.9 us (37%)
  Pallas kernels  35.3 us (30%)
  starting transfers between devices  33.1 us (28%)
  local copies, waits for them, and re-layouts  2.3 us (2%)
    ppermute x18, waiting for transfers between devices, over(): moved.append(lax.ppermute(value, 'col', xor_perm(cols, bit)))  26.4 us
    ppermute x18, starting transfers between devices, over(): moved.append(lax.ppermute(value, 'col', xor_perm(cols, bit)))  15.7 us
    ppermute x3, waiting for transfers between devices, from_holders(): return lax.ppermute(value, everyone, perm)  14.1 us
    pallas_call x1, Pallas kernels, factor(): pl.pallas_call(lu_kernel, out_shape=jax.ShapeDtypeStruct(own.shape, jnp.f...  13.7 us
    ppermute x7, starting transfers between devices, over_layers(): return lax.ppermute(value, 'layer', xor_perm(layers, s))  9.73 us
    ppermute x3, starting transfers between devices, from_holders(): return lax.ppermute(value, everyone, perm)  7.59 us
    pallas_call x3, Pallas kernels, near_update(): pl.pallas_call(functools.partial(near_kernel, chunk, chunks, layers), out...  7.44 us
    pallas_call x3, Pallas kernels, combine(): pl.pallas_call(functools.partial(combine_kernel, chunk, codes, len(held))...  5.07 us
  transfers between devices with their start and end apart: 29, of which 11 were waited for; matrix products, arithmetic and copies ran while one was open for 0% of the time, Pallas kernels for 28%

profile of v4, /device:TPU:2, one launch (start us, length us, event | category | flops | bytes accessed | tf_op | source)
XLA Modules:
  0.0 115.7 jit_solution(3498009957836568996)
XLA Ops:
  0.7 1.4 %copy-done = bf16[1,8,1536,64]{2,3,1,0:T(8,128)(2,1)S(1)} copy-done((bf16[1,8,1536,64]{2,3,1,0:T(8,128)(2,1)S(1)}, bf16[1,8,1536,64]{2,3,1,0:T(8,128)(2,1)}, u32[]{:S(2)}) %copy-start) | copy-done | bytes 1572888
  2.1 0.8 split.5
  3.0 1.6 %collective-permute-start.11 = (bf16[4,64,512]{2,1,0:T(8,128)(2,1)}, bf16[4,64,512]{2,1,0:T(8,128)(2,1)}, u32[]{:S(2)}, u32[]{:S(2)}) collective-permute-start(bf16[4,64,512]{2,1,0:T(8,128)(2,1)} %get-tuple-element.53.refs_1_), channel_id=1, source_target_pairs={{0,2},{1,3},{2,0},{3,1},{4,6},{5,7},{6,4},{7,5},{8,10},{9,11},{10,... | collective-permute-start | bytes 786440 | tf_op jit(solution)/shard_map/ppermute | solution.py:470
  4.6 0.5 collective-permute-start
  5.1 1.5 %collective-permute-start.4 = (bf16[4,64,512]{2,1,0:T(8,128)(2,1)}, bf16[4,64,512]{2,1,0:T(8,128)(2,1)}, u32[]{:S(2)}, u32[]{:S(2)}) collective-permute-start(bf16[4,64,512]{2,1,0:T(8,128)(2,1)} %get-tuple-element.53.refs_1_), channel_id=1, source_target_pairs={{0,1},{1,0},{2,3},{3,2},{4,5},{5,4},{6,7},{7,6},{8,9},{9,8},{10,11... | collective-permute-start | bytes 786440 | tf_op jit(solution)/shard_map/ppermute | solution.py:470
  6.6 0.5 collective-permute-start.7
  7.1 5.4 %collective-permute-done.11.refs_5_ = bf16[4,64,512]{2,1,0:T(8,128)(2,1)} collective-permute-done((bf16[4,64,512]{2,1,0:T(8,128)(2,1)}, bf16[4,64,512]{2,1,0:T(8,128)(2,1)}, u32[]{:S(2)}, u32[]{:S(2)}) %collective-permute-start.11) | collective-permute-done | bytes 262176 | tf_op jit(solution)/shard_map/ppermute | solution.py:470
  12.8 0.7 copy-done.3
  14.0 1.6 %collective-permute-start.1 = (bf16[4,64,512]{2,1,0:T(8,128)(2,1)}, bf16[4,64,512]{2,1,0:T(8,128)(2,1)S(1)}, u32[]{:S(2)}, u32[]{:S(2)}) collective-permute-start(bf16[4,64,512]{2,1,0:T(8,128)(2,1)} %collective-permute-done.refs_2_), channel_id=1, source_target_pairs={{0,2},{1,3},{2,0},{3,1},{4,6},{5,7},{6,4},{7,5},{8,10},{9,11},{10,... | collective-permute-start | bytes 786440 | tf_op jit(solution)/shard_map/ppermute | solution.py:470
  15.6 4.0 %collective-permute-done.4.refs_3_ = bf16[4,64,512]{2,1,0:T(8,128)(2,1)} collective-permute-done((bf16[4,64,512]{2,1,0:T(8,128)(2,1)}, bf16[4,64,512]{2,1,0:T(8,128)(2,1)}, u32[]{:S(2)}, u32[]{:S(2)}) %collective-permute-start.4) | collective-permute-done | bytes 262176 | tf_op jit(solution)/shard_map/ppermute | solution.py:470
  19.6 0.5 collective-permute-start.5
  20.2 5.0 %collective-permute-done.12.db_ref = bf16[4,64,512]{2,1,0:T(8,128)(2,1)} collective-permute-done((bf16[4,64,512]{2,1,0:T(8,128)(2,1)}, bf16[4,64,512]{2,1,0:T(8,128)(2,1)}, u32[]{:S(2)}, u32[]{:S(2)}) %collective-permute-start.12) | collective-permute-done | bytes 262176 | tf_op jit(solution)/shard_map/ppermute | solution.py:470
  25.3 0.5 collective-permute-start.13
  25.8 1.4 %masked_right.1 = (bf16[8,192,768]{2,1,0:T(8,128)(2,1)S(1)}, bf16[8,64,768]{2,1,0:T(8,128)(2,1)S(1)}) custom-call(s32[7]{0:T(128)S(1)} %stack.31.where_ref, s32[8,6]{1,0:T(8,128)S(1)} %bitcast.20, bf16[8,128,768]{2,1,0:T(8,128)(2,1)S(1)} %bitcast.19, bf16[8,128,768]{2,1,0:T(8,128)(2,1)S(1)} %collective-permute-done.10.uo_ref), custom_call_target="tpu_custom_call" | custom-call | flops 1000 | bytes 1000 | tf_op jit(solution)/shard_map/masked_right/pallas_call | solution.py:160
  27.2 3.0 %near_update.3.refs_1_ = f32[4,128,768]{2,1,0:T(8,128)S(1)} custom-call(s32[8,12]{1,0:T(8,128)S(1)} %bitcast.21, bf16[4,64,512]{2,1,0:T(8,128)(2,1)} %get-tuple-element.48.refs_0_, bf16[4,64,512]{2,1,0:T(8,128)(2,1)} %get-tuple-element.53.refs_1_, bf16[4,64,512]{2,1,0:T(8,128)(2,1)} %collective-permute-done.refs_2_, ...), custom_call_target="tpu_custom_call" | custom-call | flops 10000001024 | bytes 1000 | tf_op jit(solution)/shard_map/near_update/pallas_call | solution.py:205
  30.2 2.0 %far_update.3 = (f32[2,128,768]{2,1,0:T(8,128)S(1)}, s16[144,256]{1,0:T(8,128)(2,1)S(1)}, s16[144,1792]{1,0:T(8,128)(2,1)S(1)}) custom-call(s32[7]{0:T(128)S(1)} %stack.31.where_ref, s32[8,12]{1,0:T(8,128)S(1)} %bitcast.22, bf16[4,64,512]{2,1,0:T(8,128)(2,1)S(1)} %collective-permute-done.1.da_ref, bf16[4,64,512]{2,1,0:T(8,128)(2,1)} %collective-permute-done.12.db_ref, ...), custom_call_target="tpu_custom_call" | custom-call | flops 4000001024 | bytes 1000 | tf_op jit(solution)/shard_map/far_update/pallas_call | solution.py:265
  32.2 1.6 %collective-permute-start.14 = (s16[144,1792]{1,0:T(8,128)(2,1)S(1)}, s16[144,1792]{1,0:T(8,128)(2,1)S(1)}, u32[]{:S(2)}, u32[]{:S(2)}) collective-permute-start(s16[144,1792]{1,0:T(8,128)(2,1)S(1)} %get-tuple-element.64), channel_id=1, source_target_pairs={{0,8},{8,0},{16,24},{24,16},{1,9},{9,1},{17,25},{25,17},{2,10},{10... | collective-permute-start | bytes 1548296 | tf_op jit(solution)/shard_map/ppermute | solution.py:454
  34.0 0.6 collective-permute-start.2
  34.6 1.5 %collective-permute-start.6 = (bf16[4,64,512]{2,1,0:T(8,128)(2,1)S(1)}, bf16[4,64,512]{2,1,0:T(8,128)(2,1)S(1)}, u32[]{:S(2)}, u32[]{:S(2)}) collective-permute-start(bf16[4,64,512]{2,1,0:T(8,128)(2,1)S(1)} %collective-permute-done.5.refs_2_), channel_id=1, source_target_pairs={{0,2},{1,3},{2,0},{3,1},{4,6},{5,7},{6,4},{7,5},{8,10},{9,11},{10,... | collective-permute-start | bytes 786440 | tf_op jit(solution)/shard_map/ppermute | solution.py:470
  36.2 1.5 %collective-permute-start.9 = (bf16[4,64,512]{2,1,0:T(8,128)(2,1)S(1)}, bf16[4,64,512]{2,1,0:T(8,128)(2,1)S(1)}, u32[]{:S(2)}, u32[]{:S(2)}) collective-permute-start(bf16[4,64,512]{2,1,0:T(8,128)(2,1)S(1)} %collective-permute-done.8.refs_5_), channel_id=1, source_target_pairs={{0,1},{1,0},{2,3},{3,2},{4,5},{5,4},{6,7},{7,6},{8,9},{9,8},{10,11... | collective-permute-start | bytes 786440 | tf_op jit(solution)/shard_map/ppermute | solution.py:470
  38.2 5.2 %collective-permute-done.2.refs_3_ = bf16[4,64,512]{2,1,0:T(8,128)(2,1)S(1)} collective-permute-done((bf16[4,64,512]{2,1,0:T(8,128)(2,1)S(1)}, bf16[4,64,512]{2,1,0:T(8,128)(2,1)S(1)}, u32[]{:S(2)}, u32[]{:S(2)}) %collective-permute-start.2) | collective-permute-done | bytes 262176 | tf_op jit(solution)/shard_map/ppermute | solution.py:470
  43.3 0.5 collective-permute-start.3
  43.9 1.5 %collective-permute-start.18 = (bf16[4,64,512]{2,1,0:T(8,128)(2,1)S(1)}, bf16[4,64,512]{2,1,0:T(8,128)(2,1)S(1)}, u32[]{:S(2)}, u32[]{:S(2)}) collective-permute-start(bf16[4,64,512]{2,1,0:T(8,128)(2,1)S(1)} %get-tuple-element.72.refs_1_), channel_id=1, source_target_pairs={{0,1},{1,0},{2,3},{3,2},{4,5},{5,4},{6,7},{7,6},{8,9},{9,8},{10,11... | collective-permute-start | bytes 786440 | tf_op jit(solution)/shard_map/ppermute | solution.py:470
  45.4 3.6 %collective-permute-done.9.db_ref = bf16[4,64,512]{2,1,0:T(8,128)(2,1)S(1)} collective-permute-done((bf16[4,64,512]{2,1,0:T(8,128)(2,1)S(1)}, bf16[4,64,512]{2,1,0:T(8,128)(2,1)S(1)}, u32[]{:S(2)}, u32[]{:S(2)}) %collective-permute-start.9) | collective-permute-done | bytes 262176 | tf_op jit(solution)/shard_map/ppermute | solution.py:470
  49.0 1.5 %collective-permute-start.19 = (bf16[4,64,512]{2,1,0:T(8,128)(2,1)S(1)}, bf16[4,64,512]{2,1,0:T(8,128)(2,1)S(1)}, u32[]{:S(2)}, u32[]{:S(2)}) collective-permute-start(bf16[4,64,512]{2,1,0:T(8,128)(2,1)S(1)} %get-tuple-element.73.refs_0_), channel_id=1, source_target_pairs={{0,2},{1,3},{2,0},{3,1},{4,6},{5,7},{6,4},{7,5},{8,10},{9,11},{10,... | collective-permute-start | bytes 786440 | tf_op jit(solution)/shard_map/ppermute | solution.py:470
  50.5 0.5 collective-permute-start.17
  51.3 2.7 %collective-permute-start.20 = (s16[144,1024]{1,0:T(8,128)(2,1)S(1)}, s16[144,1024]{1,0:T(8,128)(2,1)S(1)}, u32[]{:S(2)}, u32[]{:S(2)}) collective-permute-start(s16[144,1024]{1,0:T(8,128)(2,1)S(1)} %get-tuple-element.65.refs_0_), channel_id=1, source_target_pairs={{0,16},{8,24},{16,0},{24,8},{1,17},{9,25},{17,1},{25,9},{2,18},{10... | collective-permute-start | bytes 884744 | tf_op jit(solution)/shard_map/ppermute | solution.py:454
  54.0 2.2 %near_update.4.refs_1_ = f32[4,128,768]{2,1,0:T(8,128)S(1)} custom-call(s32[8,12]{1,0:T(8,128)S(1)} %bitcast.23, bf16[4,64,512]{2,1,0:T(8,128)(2,1)S(1)} %get-tuple-element.60.refs_0_, bf16[4,64,512]{2,1,0:T(8,128)(2,1)S(1)} %copy-done.4, bf16[4,64,512]{2,1,0:T(8,128)(2,1)S(1)} %collective-permute-done.5.refs_2_, ...), custom_call_target="tpu_custom_call" | custom-call | flops 10000001024 | bytes 1000 | tf_op jit(solution)/shard_map/near_update/pallas_call | solution.py:205
  56.2 1.5 %far_update.4 = (f32[2,128,768]{2,1,0:T(8,128)S(1)}, s16[144,256]{1,0:T(8,128)(2,1)S(1)}, s16[144,1536]{1,0:T(8,128)(2,1)S(1)}) custom-call(s32[7]{0:T(128)S(1)} %stack.31.where_ref, s32[8,12]{1,0:T(8,128)S(1)} %bitcast.24, bf16[4,64,512]{2,1,0:T(8,128)(2,1)S(1)} %collective-permute-done.6.da_ref, bf16[4,64,512]{2,1,0:T(8,128)(2,1)S(1)} %collective-permute-done.9.db_ref, ...), custom_call_target="tpu_custom_call" | custom-call | flops 4000001024 | bytes 1000 | tf_op jit(solution)/shard_map/far_update/pallas_call | solution.py:265
  57.7 0.6 collective-permute-start.15
  58.3 1.8 %collective-permute-done.18.refs_3_ = bf16[4,64,512]{2,1,0:T(8,128)(2,1)S(1)} collective-permute-done((bf16[4,64,512]{2,1,0:T(8,128)(2,1)S(1)}, bf16[4,64,512]{2,1,0:T(8,128)(2,1)S(1)}, u32[]{:S(2)}, u32[]{:S(2)}) %collective-permute-start.18) | collective-permute-done | bytes 262176 | tf_op jit(solution)/shard_map/ppermute | solution.py:470
  60.1 2.2 %near_update.5.refs_1_ = f32[4,128,768]{2,1,0:T(8,128)S(1)} custom-call(s32[8,12]{1,0:T(8,128)S(1)} %bitcast.25, bf16[4,64,512]{2,1,0:T(8,128)(2,1)S(1)} %get-tuple-element.73.refs_0_, bf16[4,64,512]{2,1,0:T(8,128)(2,1)S(1)} %get-tuple-element.72.refs_1_, bf16[4,64,512]{2,1,0:T(8,128)(2,1)S(1)} %collective-permute-done.3.refs_2_, ...), custom_call_target="tpu_custom_call" | custom-call | flops 10000001024 | bytes 1000 | tf_op jit(solution)/shard_map/near_update/pallas_call | solution.py:205
  62.3 0.8 collective-permute-start.21
  63.1 1.1 collective-permute-done.15.da_ref
  64.2 1.5 %far_update.5 = (f32[128,768]{1,0:T(8,128)S(1)}, s16[144,512]{1,0:T(8,128)(2,1)S(1)}, s16[144,768]{1,0:T(8,128)(2,1)S(1)}, s16[144,768]{1,0:T(8,128)(2,1)S(1)}, s16[144,768]{1,0:T(8,128)(2,1)S(1)}) custom-call(s32[7]{0:T(128)S(1)} %stack.31.where_ref, s32[8,12]{1,0:T(8,128)S(1)} %bitcast.26, bf16[4,64,512]{2,1,0:T(8,128)(2,1)S(1)} %collective-permute-done.15.da_ref, ...), custom_call_target="tpu_custom_call" | custom-call | flops 4000001024 | bytes 1000 | tf_op jit(solution)/shard_map/far_update/pallas_call | solution.py:265
  65.7 2.5 %collective-permute-start.22 = (s16[144,512]{1,0:T(8,128)(2,1)S(1)}, s16[144,512]{1,0:T(8,128)(2,1)S(1)}, u32[]{:S(2)}, u32[]{:S(2)}) collective-permute-start(s16[144,512]{1,0:T(8,128)(2,1)S(1)} %get-tuple-element.80.mine_ref), channel_id=1, source_target_pairs={{0,8},{1,9},{6,14},{7,15},{8,0},{9,1},{14,6},{15,7},{16,24},{17,25... | collective-permute-start | bytes 442376 | tf_op jit(solution)/shard_map/ppermute | solution.py:451
  68.3 3.4 %collective-permute-done.21.got_ref = s16[144,1536]{1,0:T(8,128)(2,1)S(1)} collective-permute-done((s16[144,1536]{1,0:T(8,128)(2,1)S(1)}, s16[144,1536]{1,0:T(8,128)(2,1)S(1)}, u32[]{:S(2)}, u32[]{:S(2)}) %collective-permute-start.21) | collective-permute-done | bytes 442400 | tf_op jit(solution)/shard_map/ppermute | solution.py:454
  71.9 1.3 %collective-permute-done.22.got_ref = s16[144,512]{1,0:T(8,128)(2,1)S(1)} collective-permute-done((s16[144,512]{1,0:T(8,128)(2,1)S(1)}, s16[144,512]{1,0:T(8,128)(2,1)S(1)}, u32[]{:S(2)}, u32[]{:S(2)}) %collective-permute-start.22) | collective-permute-done | bytes 147488 | tf_op jit(solution)/shard_map/ppermute | solution.py:451
  73.3 3.6 %collective-permute-start.23 = (s16[144,512]{1,0:T(8,128)(2,1)S(1)}, s16[144,512]{1,0:T(8,128)(2,1)S(1)}, u32[]{:S(2)}, u32[]{:S(2)}) collective-permute-start(s16[144,512]{1,0:T(8,128)(2,1)S(1)} %add_coded.1.refs_2_), channel_id=1, source_target_pairs={{0,16},{1,17},{6,22},{7,23},{8,24},{9,25},{14,30},{15,31},{16,0},{... | collective-permute-start | bytes 442376 | tf_op jit(solution)/shard_map/ppermute | solution.py:451
  76.9 12.8 %collective-permute-done.23.refs_3_ = s16[144,512]{1,0:T(8,128)(2,1)S(1)} collective-permute-done((s16[144,512]{1,0:T(8,128)(2,1)S(1)}, s16[144,512]{1,0:T(8,128)(2,1)S(1)}, u32[]{:S(2)}, u32[]{:S(2)}) %collective-permute-start.23) | collective-permute-done | bytes 147488 | tf_op jit(solution)/shard_map/ppermute | solution.py:451
  89.7 0.8 pivots.1.own_ref
  90.5 1.5 %collective-permute-start.24 = (f32[6,128,128]{2,1,0:T(8,128)S(1)}, f32[6,128,128]{2,1,0:T(8,128)S(1)}, u32[]{:S(2)}, u32[]{:S(2)}) collective-permute-start(f32[6,128,128]{2,1,0:T(8,128)S(1)} %pivots.1.own_ref), channel_id=1, source_target_pairs={{0,4},{1,5},{6,2},{7,3},{8,12},{9,13},{14,10},{15,11},{16,20},{17,... | collective-permute-start | bytes 1179656 | tf_op jit(solution)/shard_map/ppermute | solution.py:451
  92.1 1.6 %combine.3.refs_1_ = f32[384,768]{1,0:T(8,128)} custom-call(s32[7]{0:T(128)S(1)} %stack.31.where_ref, f32[1536,768]{1,0:T(8,128)S(1)} %bitcast.14, f32[128,768]{1,0:T(8,128)S(1)} %get-tuple-element.89.kept_ref, s16[144,1024]{1,0:T(8,128)(2,1)S(1)} %collective-permute-done.20.refs_1_.refs_0_), custom_call_target="tpu_custom_call" | custom-call | flops 1000 | bytes 1000 | tf_op jit(solution)/shard_map/combine/pallas_call | solution.py:351
  93.7 3.1 %collective-permute-start.28 = (s16[144,768]{1,0:T(8,128)(2,1)S(1)}, s16[144,768]{1,0:T(8,128)(2,1)S(1)}, u32[]{:S(2)}, u32[]{:S(2)}) collective-permute-start(s16[144,768]{1,0:T(8,128)(2,1)S(1)} %get-tuple-element.79), channel_id=1, source_target_pairs={{0,16},{8,24},{16,0},{24,8},{1,17},{9,25},{17,1},{25,9},{2,18},{10... | collective-permute-start | bytes 663560 | tf_op jit(solution)/shard_map/ppermute | solution.py:454
  96.8 1.3 %collective-permute-start.27 = (s16[144,768]{1,0:T(8,128)(2,1)S(1)}, s16[144,768]{1,0:T(8,128)(2,1)S(1)}, u32[]{:S(2)}, u32[]{:S(2)}) collective-permute-start(s16[144,768]{1,0:T(8,128)(2,1)S(1)} %get-tuple-element.86), channel_id=1, source_target_pairs={{0,24},{8,16},{16,8},{24,0},{1,25},{9,17},{17,9},{25,1},{2,26},{10... | collective-permute-start | bytes 663560 | tf_op jit(solution)/shard_map/ppermute | solution.py:454
  98.3 13.7 %factor.1 = f32[6,128,128]{2,1,0:T(8,128)} custom-call(s32[7]{0:T(128)S(1)} %stack.31.where_ref, f32[6,128,128]{2,1,0:T(8,128)S(1)} %pivots.1.own_ref, f32[6,128,128]{2,1,0:T(8,128)S(1)} %collective-permute-done.24.other_ref), custom_call_target="tpu_custom_call" | custom-call | flops 20000000000 | bytes 1000 | tf_op jit(solution)/shard_map/factor/pallas_call | solution.py:83
  112.0 1.6 %combine.4.refs_3_ = f32[384,768]{1,0:T(8,128)} custom-call(s32[7]{0:T(128)S(1)} %stack.31.where_ref, f32[1536,768]{1,0:T(8,128)S(1)} %bitcast.14, f32[128,768]{1,0:T(8,128)S(1)} %get-tuple-element.88.kept_ref, s16[144,768]{1,0:T(8,128)(2,1)S(1)} %collective-permute-done.28.refs_0_, f32[384,768]{1,0:T(8,128)} %combine.3.refs_1_), custom_call_target="tpu_custom_call", output_to_operand_aliasing={{}: (4, {})} | custom-call | flops 1000 | bytes 1000 | tf_op jit(solution)/shard_map/combine/pallas_call | solution.py:351
  113.7 1.8 %combine.5 = f32[384,768]{1,0:T(8,128)} custom-call(s32[7]{0:T(128)S(1)} %stack.31.where_ref, f32[1536,768]{1,0:T(8,128)S(1)} %bitcast.14, f32[128,768]{1,0:T(8,128)S(1)} %get-tuple-element.81.kept_ref, s16[144,768]{1,0:T(8,128)(2,1)S(1)} %collective-permute-done.25.refs_0_, ...), custom_call_target="tpu_custom_call", output_to_operand_aliasing={{}: (6, {})} | custom-call | flops 1000 | bytes 1000 | tf_op jit(solution)/shard_map/combine/pallas_call | solution.py:351
  (49 shorter events, 2.6 us)
Async XLA Ops:
  0.6 25.1 %collective-permute-start.10 = (bf16[8,128,768]{2,1,0:T(8,128)(2,1)}, bf16[8,128,768]{2,1,0:T(8,128)(2,1)S(1)}, u32[]{:S(2)}, u32[]{:S(2)}) collective-permute-start(bf16[8,128,768]{2,1,0:T(8,128)(2,1)} %bitcast.18), channel_id=1, source_target_pairs={{0,4},{4,0},{1,5},{5,1},{2,6},{6,2},{3,7},{7,3},{8,12},{12,8},{9,1... | collective-permute-start | bytes 4718600 | tf_op jit(solution)/shard_map/ppermute | solution.py:458
  0.7 1.4 %copy-start = (bf16[1,8,1536,64]{2,3,1,0:T(8,128)(2,1)S(1)}, bf16[1,8,1536,64]{2,3,1,0:T(8,128)(2,1)}, u32[]{:S(2)}) copy-start(bf16[1,8,1536,64]{2,3,1,0:T(8,128)(2,1)} %param.5) | copy-start | bytes 4718596
  2.1 11.3 %copy-start.6 = (s32[1,8,6]{1,0,2:T(1,128)S(1)}, s32[1,8,6]{1,0,2:T(1,128)}, u32[]{:S(2)}) copy-start(s32[1,8,6]{1,0,2:T(1,128)} %param.8) | copy-start | bytes 580
  2.1 23.6 %copy-start.2 = (bf16[1,8,128,768]{3,2,1,0:T(8,128)(2,1)S(1)}, bf16[1,8,128,768]{3,2,1,0:T(8,128)(2,1)}, u32[]{:S(2)}) copy-start(bf16[1,8,128,768]{3,2,1,0:T(8,128)(2,1)} %param.6) | copy-start | bytes 4718596
  3.0 9.5 %collective-permute-start.11 = (bf16[4,64,512]{2,1,0:T(8,128)(2,1)}, bf16[4,64,512]{2,1,0:T(8,128)(2,1)}, u32[]{:S(2)}, u32[]{:S(2)}) collective-permute-start(bf16[4,64,512]{2,1,0:T(8,128)(2,1)} %get-tuple-element.53.refs_1_), channel_id=1, source_target_pairs={{0,2},{1,3},{2,0},{3,1},{4,6},{5,7},{6,4},{7,5},{8,10},{9,11},{10,... | collective-permute-start | bytes 786440 | tf_op jit(solution)/shard_map/ppermute | solution.py:470
  4.6 9.5 %collective-permute-start = (bf16[4,64,512]{2,1,0:T(8,128)(2,1)}, bf16[4,64,512]{2,1,0:T(8,128)(2,1)}, u32[]{:S(2)}, u32[]{:S(2)}) collective-permute-start(bf16[4,64,512]{2,1,0:T(8,128)(2,1)} %get-tuple-element.48.refs_0_), channel_id=1, source_target_pairs={{0,1},{1,0},{2,3},{3,2},{4,5},{5,4},{6,7},{7,6},{8,9},{9,8},{10,11... | collective-permute-start | bytes 786440 | tf_op jit(solution)/shard_map/ppermute | solution.py:470
  5.1 14.5 %collective-permute-start.4 = (bf16[4,64,512]{2,1,0:T(8,128)(2,1)}, bf16[4,64,512]{2,1,0:T(8,128)(2,1)}, u32[]{:S(2)}, u32[]{:S(2)}) collective-permute-start(bf16[4,64,512]{2,1,0:T(8,128)(2,1)} %get-tuple-element.53.refs_1_), channel_id=1, source_target_pairs={{0,1},{1,0},{2,3},{3,2},{4,5},{5,4},{6,7},{7,6},{8,9},{9,8},{10,11... | collective-permute-start | bytes 786440 | tf_op jit(solution)/shard_map/ppermute | solution.py:470
  6.6 13.6 %collective-permute-start.7 = (bf16[4,64,512]{2,1,0:T(8,128)(2,1)}, bf16[4,64,512]{2,1,0:T(8,128)(2,1)}, u32[]{:S(2)}, u32[]{:S(2)}) collective-permute-start(bf16[4,64,512]{2,1,0:T(8,128)(2,1)} %get-tuple-element.48.refs_0_), channel_id=1, source_target_pairs={{0,2},{1,3},{2,0},{3,1},{4,6},{5,7},{6,4},{7,5},{8,10},{9,11},{10,... | collective-permute-start | bytes 786440 | tf_op jit(solution)/shard_map/ppermute | solution.py:470
  12.5 12.8 %collective-permute-start.12 = (bf16[4,64,512]{2,1,0:T(8,128)(2,1)}, bf16[4,64,512]{2,1,0:T(8,128)(2,1)}, u32[]{:S(2)}, u32[]{:S(2)}) collective-permute-start(bf16[4,64,512]{2,1,0:T(8,128)(2,1)} %collective-permute-done.11.refs_5_), channel_id=1, source_target_pairs={{0,1},{1,0},{2,3},{3,2},{4,5},{5,4},{6,7},{7,6},{8,9},{9,8},{10,11... | collective-permute-start | bytes 786440 | tf_op jit(solution)/shard_map/ppermute | solution.py:470
  12.8 0.7 copy-start.3
  14.0 16.1 %collective-permute-start.1 = (bf16[4,64,512]{2,1,0:T(8,128)(2,1)}, bf16[4,64,512]{2,1,0:T(8,128)(2,1)S(1)}, u32[]{:S(2)}, u32[]{:S(2)}) collective-permute-start(bf16[4,64,512]{2,1,0:T(8,128)(2,1)} %collective-permute-done.refs_2_), channel_id=1, source_target_pairs={{0,2},{1,3},{2,0},{3,1},{4,6},{5,7},{6,4},{7,5},{8,10},{9,11},{10,... | collective-permute-start | bytes 786440 | tf_op jit(solution)/shard_map/ppermute | solution.py:470
  19.6 15.0 %collective-permute-start.5 = (bf16[4,64,512]{2,1,0:T(8,128)(2,1)S(1)}, bf16[4,64,512]{2,1,0:T(8,128)(2,1)S(1)}, u32[]{:S(2)}, u32[]{:S(2)}) collective-permute-start(bf16[4,64,512]{2,1,0:T(8,128)(2,1)S(1)} %get-tuple-element.60.refs_0_), channel_id=1, source_target_pairs={{0,1},{1,0},{2,3},{3,2},{4,5},{5,4},{6,7},{7,6},{8,9},{9,8},{10,11... | collective-permute-start | bytes 786440 | tf_op jit(solution)/shard_map/ppermute | solution.py:470
  20.2 16.0 %collective-permute-start.8 = (bf16[4,64,512]{2,1,0:T(8,128)(2,1)}, bf16[4,64,512]{2,1,0:T(8,128)(2,1)S(1)}, u32[]{:S(2)}, u32[]{:S(2)}) collective-permute-start(bf16[4,64,512]{2,1,0:T(8,128)(2,1)} %copy-done.3), channel_id=1, source_target_pairs={{0,2},{1,3},{2,0},{3,1},{4,6},{5,7},{6,4},{7,5},{8,10},{9,11},{10,... | collective-permute-start | bytes 786440 | tf_op jit(solution)/shard_map/ppermute | solution.py:470
  25.3 12.4 %collective-permute-start.13 = (bf16[4,64,512]{2,1,0:T(8,128)(2,1)S(1)}, bf16[4,64,512]{2,1,0:T(8,128)(2,1)S(1)}, u32[]{:S(2)}, u32[]{:S(2)}) collective-permute-start(bf16[4,64,512]{2,1,0:T(8,128)(2,1)S(1)} %get-tuple-element.60.refs_0_), channel_id=1, source_target_pairs={{0,2},{1,3},{2,0},{3,1},{4,6},{5,7},{6,4},{7,5},{8,10},{9,11},{10,... | collective-permute-start | bytes 786440 | tf_op jit(solution)/shard_map/ppermute | solution.py:470
  25.8 1.4 %copy-start.5 = (s32[1,8,12]{2,1,0:T(8,128)S(1)}, s32[1,8,12]{2,1,0:T(8,128)}, u32[]{:S(2)}) copy-start(s32[1,8,12]{2,1,0:T(8,128)} %param.7) | copy-start | bytes 1156
  30.2 3.7 %copy-start.1 = (bf16[1,8,1536,64]{2,3,1,0:T(8,128)(2,1)S(1)}, bf16[1,8,1536,64]{2,3,1,0:T(8,128)(2,1)}, u32[]{:S(2)}) copy-start(bf16[1,8,1536,64]{2,3,1,0:T(8,128)(2,1)} %param.5) | copy-start | bytes 4718596
  32.2 1.8 %copy-start.4 = (bf16[4,64,512]{2,1,0:T(8,128)(2,1)S(1)}, bf16[4,64,512]{2,1,0:T(8,128)(2,1)}, u32[]{:S(2)}) copy-start(bf16[4,64,512]{2,1,0:T(8,128)(2,1)} %copy-done.3) | copy-start | bytes 786436
  32.2 18.8 %collective-permute-start.14 = (s16[144,1792]{1,0:T(8,128)(2,1)S(1)}, s16[144,1792]{1,0:T(8,128)(2,1)S(1)}, u32[]{:S(2)}, u32[]{:S(2)}) collective-permute-start(s16[144,1792]{1,0:T(8,128)(2,1)S(1)} %get-tuple-element.64), channel_id=1, source_target_pairs={{0,8},{8,0},{16,24},{24,16},{1,9},{9,1},{17,25},{25,17},{2,10},{10... | collective-permute-start | bytes 1548296 | tf_op jit(solution)/shard_map/ppermute | solution.py:454
  34.0 9.3 %collective-permute-start.2 = (bf16[4,64,512]{2,1,0:T(8,128)(2,1)S(1)}, bf16[4,64,512]{2,1,0:T(8,128)(2,1)S(1)}, u32[]{:S(2)}, u32[]{:S(2)}) collective-permute-start(bf16[4,64,512]{2,1,0:T(8,128)(2,1)S(1)} %copy-done.4), channel_id=1, source_target_pairs={{0,1},{1,0},{2,3},{3,2},{4,5},{5,4},{6,7},{7,6},{8,9},{9,8},{10,11... | collective-permute-start | bytes 786440 | tf_op jit(solution)/shard_map/ppermute | solution.py:470
  34.6 9.2 %collective-permute-start.6 = (bf16[4,64,512]{2,1,0:T(8,128)(2,1)S(1)}, bf16[4,64,512]{2,1,0:T(8,128)(2,1)S(1)}, u32[]{:S(2)}, u32[]{:S(2)}) collective-permute-start(bf16[4,64,512]{2,1,0:T(8,128)(2,1)S(1)} %collective-permute-done.5.refs_2_), channel_id=1, source_target_pairs={{0,2},{1,3},{2,0},{3,1},{4,6},{5,7},{6,4},{7,5},{8,10},{9,11},{10,... | collective-permute-start | bytes 786440 | tf_op jit(solution)/shard_map/ppermute | solution.py:470
  36.2 12.8 %collective-permute-start.9 = (bf16[4,64,512]{2,1,0:T(8,128)(2,1)S(1)}, bf16[4,64,512]{2,1,0:T(8,128)(2,1)S(1)}, u32[]{:S(2)}, u32[]{:S(2)}) collective-permute-start(bf16[4,64,512]{2,1,0:T(8,128)(2,1)S(1)} %collective-permute-done.8.refs_5_), channel_id=1, source_target_pairs={{0,1},{1,0},{2,3},{3,2},{4,5},{5,4},{6,7},{7,6},{8,9},{9,8},{10,11... | collective-permute-start | bytes 786440 | tf_op jit(solution)/shard_map/ppermute | solution.py:470
  37.7 12.8 %collective-permute-start.16 = (bf16[4,64,512]{2,1,0:T(8,128)(2,1)S(1)}, bf16[4,64,512]{2,1,0:T(8,128)(2,1)S(1)}, u32[]{:S(2)}, u32[]{:S(2)}) collective-permute-start(bf16[4,64,512]{2,1,0:T(8,128)(2,1)S(1)} %get-tuple-element.72.refs_1_), channel_id=1, source_target_pairs={{0,2},{1,3},{2,0},{3,1},{4,6},{5,7},{6,4},{7,5},{8,10},{9,11},{10,... | collective-permute-start | bytes 786440 | tf_op jit(solution)/shard_map/ppermute | solution.py:470
  43.3 14.4 %collective-permute-start.3 = (bf16[4,64,512]{2,1,0:T(8,128)(2,1)S(1)}, bf16[4,64,512]{2,1,0:T(8,128)(2,1)S(1)}, u32[]{:S(2)}, u32[]{:S(2)}) collective-permute-start(bf16[4,64,512]{2,1,0:T(8,128)(2,1)S(1)} %get-tuple-element.73.refs_0_), channel_id=1, source_target_pairs={{0,1},{1,0},{2,3},{3,2},{4,5},{5,4},{6,7},{7,6},{8,9},{9,8},{10,11... | collective-permute-start | bytes 786440 | tf_op jit(solution)/shard_map/ppermute | solution.py:470
  43.9 16.2 %collective-permute-start.18 = (bf16[4,64,512]{2,1,0:T(8,128)(2,1)S(1)}, bf16[4,64,512]{2,1,0:T(8,128)(2,1)S(1)}, u32[]{:S(2)}, u32[]{:S(2)}) collective-permute-start(bf16[4,64,512]{2,1,0:T(8,128)(2,1)S(1)} %get-tuple-element.72.refs_1_), channel_id=1, source_target_pairs={{0,1},{1,0},{2,3},{3,2},{4,5},{5,4},{6,7},{7,6},{8,9},{9,8},{10,11... | collective-permute-start | bytes 786440 | tf_op jit(solution)/shard_map/ppermute | solution.py:470
  49.0 11.1 %collective-permute-start.19 = (bf16[4,64,512]{2,1,0:T(8,128)(2,1)S(1)}, bf16[4,64,512]{2,1,0:T(8,128)(2,1)S(1)}, u32[]{:S(2)}, u32[]{:S(2)}) collective-permute-start(bf16[4,64,512]{2,1,0:T(8,128)(2,1)S(1)} %get-tuple-element.73.refs_0_), channel_id=1, source_target_pairs={{0,2},{1,3},{2,0},{3,1},{4,6},{5,7},{6,4},{7,5},{8,10},{9,11},{10,... | collective-permute-start | bytes 786440 | tf_op jit(solution)/shard_map/ppermute | solution.py:470
  50.5 12.6 %collective-permute-start.17 = (bf16[4,64,512]{2,1,0:T(8,128)(2,1)S(1)}, bf16[4,64,512]{2,1,0:T(8,128)(2,1)S(1)}, u32[]{:S(2)}, u32[]{:S(2)}) collective-permute-start(bf16[4,64,512]{2,1,0:T(8,128)(2,1)S(1)} %collective-permute-done.16.refs_5_), channel_id=1, source_target_pairs={{0,1},{1,0},{2,3},{3,2},{4,5},{5,4},{6,7},{7,6},{8,9},{9,8},{10,11... | collective-permute-start | bytes 786440 | tf_op jit(solution)/shard_map/ppermute | solution.py:470
  51.3 11.8 %collective-permute-start.20 = (s16[144,1024]{1,0:T(8,128)(2,1)S(1)}, s16[144,1024]{1,0:T(8,128)(2,1)S(1)}, u32[]{:S(2)}, u32[]{:S(2)}) collective-permute-start(s16[144,1024]{1,0:T(8,128)(2,1)S(1)} %get-tuple-element.65.refs_0_), channel_id=1, source_target_pairs={{0,16},{8,24},{16,0},{24,8},{1,17},{9,25},{17,1},{25,9},{2,18},{10... | collective-permute-start | bytes 884744 | tf_op jit(solution)/shard_map/ppermute | solution.py:454
  57.7 6.4 %collective-permute-start.15 = (bf16[4,64,512]{2,1,0:T(8,128)(2,1)S(1)}, bf16[4,64,512]{2,1,0:T(8,128)(2,1)S(1)}, u32[]{:S(2)}, u32[]{:S(2)}) collective-permute-start(bf16[4,64,512]{2,1,0:T(8,128)(2,1)S(1)} %collective-permute-done.3.refs_2_), channel_id=1, source_target_pairs={{0,2},{1,3},{2,0},{3,1},{4,6},{5,7},{6,4},{7,5},{8,10},{9,11},{10,... | collective-permute-start | bytes 786440 | tf_op jit(solution)/shard_map/ppermute | solution.py:470
  62.3 9.3 %collective-permute-start.21 = (s16[144,1536]{1,0:T(8,128)(2,1)S(1)}, s16[144,1536]{1,0:T(8,128)(2,1)S(1)}, u32[]{:S(2)}, u32[]{:S(2)}) collective-permute-start(s16[144,1536]{1,0:T(8,128)(2,1)S(1)} %get-tuple-element.78), channel_id=1, source_target_pairs={{0,8},{8,0},{16,24},{24,16},{1,9},{9,1},{17,25},{25,17},{2,10},{10... | collective-permute-start | bytes 1327112 | tf_op jit(solution)/shard_map/ppermute | solution.py:454
  64.2 25.5 %slice-start = ((s8[4718592]{0:T(1024)(128)(4,1)}), s8[4194304]{0:T(1024)(128)(4,1)S(1)}, s32[]{:S(2)}) async-start(s8[4718592]{0:T(1024)(128)(4,1)} %bitcast.13), calls=%async_computation | async-start | bytes 8388608
  64.2 25.5 %slice-start.1 = ((s8[4718592]{0:T(1024)(128)(4,1)}), s8[524288]{0:T(1024)(128)(4,1)S(1)}, s32[]{:S(2)}) async-start(s8[4718592]{0:T(1024)(128)(4,1)} %bitcast.13), calls=%async_computation.1 | async-start | bytes 1048576
  65.7 7.5 %collective-permute-start.22 = (s16[144,512]{1,0:T(8,128)(2,1)S(1)}, s16[144,512]{1,0:T(8,128)(2,1)S(1)}, u32[]{:S(2)}, u32[]{:S(2)}) collective-permute-start(s16[144,512]{1,0:T(8,128)(2,1)S(1)} %get-tuple-element.80.mine_ref), channel_id=1, source_target_pairs={{0,8},{1,9},{6,14},{7,15},{8,0},{9,1},{14,6},{15,7},{16,24},{17,25... | collective-permute-start | bytes 442376 | tf_op jit(solution)/shard_map/ppermute | solution.py:451
  73.3 16.3 %collective-permute-start.23 = (s16[144,512]{1,0:T(8,128)(2,1)S(1)}, s16[144,512]{1,0:T(8,128)(2,1)S(1)}, u32[]{:S(2)}, u32[]{:S(2)}) collective-permute-start(s16[144,512]{1,0:T(8,128)(2,1)S(1)} %add_coded.1.refs_2_), channel_id=1, source_target_pairs={{0,16},{1,17},{6,22},{7,23},{8,24},{9,25},{14,30},{15,31},{16,0},{... | collective-permute-start | bytes 442376 | tf_op jit(solution)/shard_map/ppermute | solution.py:451
  90.5 7.8 %collective-permute-start.24 = (f32[6,128,128]{2,1,0:T(8,128)S(1)}, f32[6,128,128]{2,1,0:T(8,128)S(1)}, u32[]{:S(2)}, u32[]{:S(2)}) collective-permute-start(f32[6,128,128]{2,1,0:T(8,128)S(1)} %pivots.1.own_ref), channel_id=1, source_target_pairs={{0,4},{1,5},{6,2},{7,3},{8,12},{9,13},{14,10},{15,11},{16,20},{17,... | collective-permute-start | bytes 1179656 | tf_op jit(solution)/shard_map/ppermute | solution.py:451
  92.0 21.7 %collective-permute-start.25 = (s16[144,768]{1,0:T(8,128)(2,1)S(1)}, s16[144,768]{1,0:T(8,128)(2,1)S(1)}, u32[]{:S(2)}, u32[]{:S(2)}) collective-permute-start(s16[144,768]{1,0:T(8,128)(2,1)S(1)} %get-tuple-element.82), channel_id=1, source_target_pairs={{0,8},{8,0},{16,24},{24,16},{1,9},{9,1},{17,25},{25,17},{2,10},{10... | collective-permute-start | bytes 663560 | tf_op jit(solution)/shard_map/ppermute | solution.py:454
  93.7 18.3 %collective-permute-start.28 = (s16[144,768]{1,0:T(8,128)(2,1)S(1)}, s16[144,768]{1,0:T(8,128)(2,1)S(1)}, u32[]{:S(2)}, u32[]{:S(2)}) collective-permute-start(s16[144,768]{1,0:T(8,128)(2,1)S(1)} %get-tuple-element.79), channel_id=1, source_target_pairs={{0,16},{8,24},{16,0},{24,8},{1,17},{9,25},{17,1},{25,9},{2,18},{10... | collective-permute-start | bytes 663560 | tf_op jit(solution)/shard_map/ppermute | solution.py:454
  96.8 16.9 %collective-permute-start.27 = (s16[144,768]{1,0:T(8,128)(2,1)S(1)}, s16[144,768]{1,0:T(8,128)(2,1)S(1)}, u32[]{:S(2)}, u32[]{:S(2)}) collective-permute-start(s16[144,768]{1,0:T(8,128)(2,1)S(1)} %get-tuple-element.86), channel_id=1, source_target_pairs={{0,24},{8,16},{16,8},{24,0},{1,25},{9,17},{17,9},{25,1},{2,26},{10... | collective-permute-start | bytes 663560 | tf_op jit(solution)/shard_map/ppermute | solution.py:454
  98.1 15.5 %collective-permute-start.26 = (s16[144,768]{1,0:T(8,128)(2,1)S(1)}, s16[144,768]{1,0:T(8,128)(2,1)S(1)}, u32[]{:S(2)}, u32[]{:S(2)}) collective-permute-start(s16[144,768]{1,0:T(8,128)(2,1)S(1)} %get-tuple-element.84), channel_id=1, source_target_pairs={{0,16},{8,24},{16,0},{24,8},{1,17},{9,25},{17,1},{25,9},{2,18},{10... | collective-permute-start | bytes 663560 | tf_op jit(solution)/shard_map/ppermute | solution.py:454

commit v5 on v4

--- a/solution.py
+++ b/solution.py
@@ -15,7 +15,6 @@
 CODE_TOP = 32500.0
 EXP_STEPS = 128.0
 EXP_ROWS = 16
-WINDOW = 4
 NEAR = 10
 FAR = 4
 
@@ -91,18 +90,44 @@
     )(where, own, other)
 
 
-def split_kernel(chunk, chunks, layers, lt_ref, *refs):
-    outs, sems = refs[:-1], refs[-1]
-    half = outs[0].shape[0]
+def halves_kernel(lt_ref, one_ref, two_ref, sems):
+    half = one_ref.shape[0]
+    copies = [
+        pltpu.make_async_copy(lt_ref.at[:half], one_ref, sems.at[0]),
+        pltpu.make_async_copy(lt_ref.at[half:], two_ref, sems.at[1]),
+    ]
+    for copy in copies:
+        copy.start()
+    for copy in copies:
+        copy.wait()
+
+
+def halves(lt):
+    supers, depth, length = lt.shape
+    one = jax.ShapeDtypeStruct((supers // 2, depth, length), lt.dtype)
+    return pl.pallas_call(
+        halves_kernel,
+        out_shape=[one, one],
+        in_specs=[ANY],
+        out_specs=[ANY, ANY],
+        scratch_shapes=[pltpu.SemaphoreType.DMA((2,))],
+        compiler_params=params(),
+        cost_estimate=cost(0),
+        name="halves",
+    )(lt)
+
+
+def split_kernel(chunk, chunks, layers, *refs):
+    sources, outs, sems = refs[:4], refs[4:6], refs[6]
     copies = []
-    for h in range(len(outs)):
+    for n, ref in enumerate(sources):
         for t in range(layers):
             begin = (t * chunks + chunk) * BLK
             copies.append(
                 pltpu.make_async_copy(
-                    lt_ref.at[h * half : (h + 1) * half, :, begin : begin + BLK],
-                    outs[h].at[:, :, t * BLK : (t + 1) * BLK],
-                    sems.at[h, t],
+                    ref.at[:, :, begin : begin + BLK],
+                    outs[n // 2].at[n % 2, :, :, t * BLK : (t + 1) * BLK],
+                    sems.at[n, t],
                 )
             )
     for copy in copies:
@@ -111,40 +136,41 @@
         copy.wait()
 
 
-def split(lt, chunk, chunks, layers):
-    supers, depth, _ = lt.shape
-    one = jax.ShapeDtypeStruct((supers // 2, depth, layers * BLK), lt.dtype)
+def split(sources, chunk, chunks, layers):
+    half, depth, _ = sources[0].shape
+    one = jax.ShapeDtypeStruct((2, half, depth, layers * BLK), sources[0].dtype)
     return pl.pallas_call(
         functools.partial(split_kernel, chunk, chunks, layers),
         out_shape=[one, one],
-        in_specs=[ANY],
+        in_specs=[ANY] * 4,
         out_specs=[ANY, ANY],
-        scratch_shapes=[pltpu.SemaphoreType.DMA((2, layers))],
+        scratch_shapes=[pltpu.SemaphoreType.DMA((4, layers))],
         compiler_params=params(),
         cost_estimate=cost(0),
         name="split",
-    )(lt)
+    )(*sources)
 
 
 def right_kernel(where_ref, upat_ref, u_ref, uo_ref, near_ref, far_ref):
-    _, wide, cols = u_ref.shape
-    depth = far_ref.shape[1]
+    supers, wide, cols = u_ref.shape
+    depth = wide // 2
     begin = where_ref[6] * depth
     mine = where_ref[1] == where_ref[3]
 
     def fill(close_ref, away_ref):
         for n, ref in enumerate((close_ref, close_ref, away_ref, away_ref)):
-            spot = begin if n % 2 == 0 else wide - depth - begin
+            spot = begin if n % 2 == 0 else depth - begin
             rows = pl.ds(pl.multiple_of(spot, depth), depth)
-            for k in range(u_ref.shape[0]):
+            for k in range(supers):
+                first = (0, 1) if k < supers // 2 else (0, 2)
+                out_ref = near_ref if n in first else far_ref
+                at = 0 if n in (0, 3 - first[1]) else depth
                 for m in range(cols // BLK):
                     lanes = slice(m * BLK, (m + 1) * BLK)
                     block = ref[k, rows, lanes]
-                    block = jnp.where(upat_ref[k, m] != 0, block, jnp.zeros_like(block))
-                    if n < 3:
-                        near_ref[k, n * depth : (n + 1) * depth, lanes] = block
-                    else:
-                        far_ref[k, :, lanes] = block
+                    out_ref[k, at : at + depth, lanes] = jnp.where(
+                        upat_ref[k, m] != 0, block, jnp.zeros_like(block)
+                    )
 
     @pl.when(mine)
     def _():
@@ -155,14 +181,11 @@
         fill(uo_ref, u_ref)
 
 
-def masked_right(where, upat, u, uo, depth):
-    supers, _, cols = u.shape
+def masked_right(where, upat, u, uo):
+    shape = jax.ShapeDtypeStruct(u.shape, u.dtype)
     return pl.pallas_call(
         right_kernel,
-        out_shape=[
-            jax.ShapeDtypeStruct((supers, 3 * depth, cols), u.dtype),
-            jax.ShapeDtypeStruct((supers, depth, cols), u.dtype),
-        ],
+        out_shape=[shape, shape],
         in_specs=[SMEM, SMEM, VMEM, VMEM],
         out_specs=[VMEM, VMEM],
         compiler_params=params(),
@@ -172,14 +195,14 @@
 
 
 def product(chunk, chunks, layers, lpat_ref, groups, right_ref, left):
-    half, depth, _ = groups[0][0].shape
-    for n, group in enumerate(groups):
-        for h in range(2):
+    pieces, half, depth, _ = groups[0].shape
+    for h, group in enumerate(groups):
+        for n in range(pieces):
             for i in range(half):
                 k = h * half + i
                 for t in range(layers):
                     lanes = slice(t * BLK, (t + 1) * BLK)
-                    block = group[h][i, :, lanes]
+                    block = group[n, i, :, lanes]
                     kept = lpat_ref[k, t * chunks + chunk] != 0
                     left[k, n * depth : (n + 1) * depth, lanes] = jnp.where(
                         kept, block, jnp.zeros_like(block)
@@ -192,20 +215,18 @@
     )
 
 
-def near_kernel(chunk, chunks, layers, lpat_ref, *refs):
-    pieces, (right_ref, acc_ref, left) = refs[:6], refs[6:]
-    groups = [pieces[2 * n : 2 * n + 2] for n in range(3)]
-    total = product(chunk, chunks, layers, lpat_ref, groups, right_ref, left)
+def near_kernel(chunk, chunks, layers, lpat_ref, a_ref, b_ref, right_ref, acc_ref, left):
+    total = product(chunk, chunks, layers, lpat_ref, (a_ref, b_ref), right_ref, left)
     acc_ref[...] = total.reshape(acc_ref.shape)
 
 
 def near_update(lpat, pieces, right, chunk, chunks, layers):
-    half, _, width = pieces[0].shape
+    width = pieces[0].shape[3]
     supers, kdim, cols = right.shape
     return pl.pallas_call(
         functools.partial(near_kernel, chunk, chunks, layers),
         out_shape=jax.ShapeDtypeStruct((layers, BLK, cols), jnp.float32),
-        in_specs=[SMEM] + [VMEM] * 7,
+        in_specs=[SMEM] + [VMEM] * 3,
         out_specs=VMEM,
         scratch_shapes=[pltpu.VMEM((supers, kdim, width), jnp.bfloat16)],
         compiler_params=params(),
@@ -214,16 +235,15 @@
     )(lpat, *pieces, right)
 
 
-def far_kernel(chunk, chunks, layers, earlier, where_ref, lpat_ref, da_ref, db_ref, *refs):
+def far_kernel(chunk, chunks, layers, earlier, where_ref, lpat_ref, a_ref, b_ref, *refs):
     right_ref, before_ref = refs[:2]
     refs = refs[2:]
     if earlier:
         old_ref, refs = refs[0], refs[1:]
-    kept_ref, diag_ref = refs[:2]
-    sent_refs, (left, acc) = refs[2:-2], refs[-2:]
+    kept_ref, sent_ref, diag_ref, left, acc = refs
     layer = where_ref[0]
     cols = right_ref.shape[2]
-    total = product(chunk, chunks, layers, lpat_ref, [(da_ref, db_ref)], right_ref, left)
+    total = product(chunk, chunks, layers, lpat_ref, (a_ref, b_ref), right_ref, left)
     acc[...] = before_ref[...] + total.reshape(acc.shape)
     begin = 0
     if earlier:
@@ -235,44 +255,33 @@
         diag_ref[:BLK, lanes], diag_ref[BLK:, lanes] = encode(
             acc[where_ref[5] + i, :, q * BLK : (q + 1) * BLK]
         )
-    if chunk == chunks - 1:
-        for s in range(1, layers):
-            sent_refs[s - 1][:BLK], sent_refs[s - 1][BLK:] = encode(acc[layer ^ s])
-        kept_ref[...] = acc[layer]
-    else:
-        (sent_ref,) = sent_refs
-        for n, s in enumerate((1, 3)):
-            lanes = slice(n * cols, (n + 1) * cols)
-            sent_ref[:BLK, lanes], sent_ref[BLK:, lanes] = encode(acc[layer ^ s])
-        if sent_ref.shape[1] > 2 * cols:
-            sent_ref[:, 2 * cols :] = diag_ref[...]
-        kept_ref[0] = acc[layer]
-        kept_ref[1] = acc[layer ^ 2]
+    for n, s in enumerate((1, 3)):
+        lanes = slice(n * cols, (n + 1) * cols)
+        sent_ref[:BLK, lanes], sent_ref[BLK:, lanes] = encode(acc[layer ^ s])
+    if sent_ref.shape[1] > 2 * cols:
+        sent_ref[:, 2 * cols :] = diag_ref[...]
+    kept_ref[0] = acc[layer]
+    kept_ref[1] = acc[layer ^ 2]
 
 
 def far_update(where, lpat, pieces, right, before, earlier, chunk, chunks, layers):
-    half, depth, width = pieces[0].shape
-    supers, _, cols = right.shape
+    width = pieces[0].shape[3]
+    supers, kdim, cols = right.shape
     beside = cols // chunks
     coded = BLK + EXP_ROWS
-    if chunk == chunks - 1:
-        kept = (BLK, cols)
-        sent = [(coded, cols)] * (layers - 1)
-    else:
-        kept = (2, BLK, cols)
-        sent = [(coded, 2 * cols + (beside if chunk == 0 else 0))]
     known = sum(part.shape[1] for part in earlier)
+    ride = beside if chunk == 0 else 0
     return pl.pallas_call(
         functools.partial(far_kernel, chunk, chunks, layers, len(earlier)),
         out_shape=[
-            jax.ShapeDtypeStruct(kept, jnp.float32),
+            jax.ShapeDtypeStruct((2, BLK, cols), jnp.float32),
+            jax.ShapeDtypeStruct((coded, 2 * cols + ride), jnp.int16),
             jax.ShapeDtypeStruct((coded, known + beside), jnp.int16),
-        ]
-        + [jax.ShapeDtypeStruct(shape, jnp.int16) for shape in sent],
+        ],
         in_specs=[SMEM] * 2 + [VMEM] * (4 + len(earlier)),
-        out_specs=[VMEM] * (2 + len(sent)),
+        out_specs=[VMEM] * 3,
         scratch_shapes=[
-            pltpu.VMEM((supers, depth, width), jnp.bfloat16),
+            pltpu.VMEM((supers, kdim, width), jnp.bfloat16),
             pltpu.VMEM((layers, BLK, cols), jnp.float32),
         ],
         compiler_params=params(),
@@ -453,70 +462,52 @@
     def over_layers(value, s):
         return lax.ppermute(value, "layer", xor_perm(layers, s))
 
+    def over(value, bit):
+        return lax.ppermute(value, "col", xor_perm(cols, bit))
+
     lt = jnp.swapaxes(lpanel[0], 1, 2)
     u = upanel[0]
+    a, b = halves(lt)
+    xa, yb = over(a, 1), over(b, 2)
     uo = lax.ppermute(u, "row", xor_perm(rows, 1))
-    near_right, far_right = masked_right(where, upat[0], u, uo, lt.shape[1])
-    moved = []
-    gates = {}
-
-    def over(value, bit):
-        spot = len(moved)
-        waits = list(gates.get(spot, ()))
-        if spot >= WINDOW:
-            waits.append(moved[spot - WINDOW])
-        if waits:
-            value = after(value, *waits)
-        moved.append(lax.ppermute(value, "col", xor_perm(cols, bit)))
-        return moved[-1]
-
-    def gathered_chunk(j):
-        a, b = split(lt, j, chunks, layers)
-        xa = over(a, 1)
-        yb = over(b, 2)
-        xb = over(b, 1)
-        ya = over(a, 2)
-        da = over(xa, 2)
-        db = over(yb, 1)
-        return (a, b, xa, xb, ya, yb), (da, db)
-
-    near, far = gathered_chunk(0)
-    finished, groups, earlier, sent = [], [], [], None
+    near_right, far_right = masked_right(where, upat[0], u, uo)
+    sides = []
     for j in range(chunks):
-        waits = [sent] if j == 1 else []
-        part = near_update(lpat[0], near, after(near_right, *waits), j, chunks, layers)
-        if j > 1:
-            part = after(part, *first)
-        out = far_update(where, lpat[0], far, far_right, part, earlier, j, chunks, layers)
-        kept, diag = out[:2]
-        if j < chunks - 1:
-            spot = len(moved)
-            if j > 0:
-                gates.update({spot + n: (kept,) for n in (4,)})
-            near, far = gathered_chunk(j + 1)
-            kept, sent = halve(kept, diag, over_layers(out[2], 1))
-            got = [over_layers(sent, 2)]
-            if j == 0:
-                groups.append([sent, got[0]])
-                first = got
-            else:
-                earlier = [diag]
-            finished.append((kept, got))
+        whole = (after(a, *sides[-1]) if j else a, xa, b, yb)
+        sides.append(split(whole, j, chunks, layers))
+    others = [(over(one, 2), over(two, 1)) for one, two in sides]
+    finished, riding, alone = [], [], []
+    for j in range(chunks):
+        right = after(near_right, finished[0][1]) if j > 1 else near_right
+        part = near_update(lpat[0], sides[j], right, j, chunks, layers)
+        if j > 0:
+            part = after(part, kept)
+        if j > 0:
+            part = after(part, finished[0][1])
+        if j == chunks - 1:
+            part = after(part, *[sent for _, sent in finished])
+        kept, coded, diag = far_update(
+            where, lpat[0], others[j], far_right, part, alone, j, chunks, layers
+        )
+        total, sent = halve(kept, diag, over_layers(coded, 1))
+        finished.append((total, sent))
+        if j == 0:
+            riding = [sent, over_layers(sent, 2)]
+        else:
+            alone = [diag]
     near = from_holders(diag, lambda l, r, c: index(l ^ 1, r, c))
-    near = add_coded(after(diag, sent), near)
+    near = add_coded(after(diag, riding[1]), near)
     far = from_holders(near, lambda l, r, c: index(l ^ 2, r, c))
-    steps = range(1, layers)
-    got = [over_layers(after(out[1 + s], far) if s > 1 else out[1 + s], s) for s in steps]
-    groups.append([near, far])
+    groups = [riding, [near, far]]
     own = pivots(where, anc, groups, [1, chunks - 1], chunks, width // BLK)
     other = from_holders(own, lambda l, r, c: index(l, 1 - r, c))
+    got = [riding[1]] + [over_layers(after(sent, other), 2) for _, sent in finished[1:]]
     diag_lu = factor(where, own, other)
-    finished.append((kept, got))
     held = []
-    for j, (kept, got) in enumerate(finished):
+    for j, (total, _) in enumerate(finished):
         if j > 0:
-            kept = after(kept, diag_lu)
-        held = [combine(where, anc, kept, got, held, share, j)]
+            total = after(total, diag_lu)
+        held = [combine(where, anc, total, [got[j]], held, share, j)]
     return held[0], diag_lu
 
 

time: 118 us -> 119 us (level)
  waiting for transfers between devices: 43.9 us -> 50.6 us
  starting transfers between devices: 33.1 us -> 28.4 us
    ppermute x7 -> x6, waiting for transfers between devices: 3.39 us -> 21.4 us  [over_layers(): return lax.ppermute(value, 'layer', xor_perm(layers, s))]
    ppermute x3, waiting for transfers between devices: 14.1 us -> 7.13 us  [from_holders(): return lax.ppermute(value, everyone, perm)]
    ppermute x18 -> x8, starting transfers between devices: 15.7 us -> 9.76 us  [over(): return lax.ppermute(value, 'col', xor_perm(cols, bit))]
    ppermute x18 -> x8, waiting for transfers between devices: 26.4 us -> 22 us  [over(): return lax.ppermute(value, 'col', xor_perm(cols, bit))]
    pallas_call x3, Pallas kernels: 7.44 us -> 5.3 us  [near_update(): pl.pallas_call(functools.partial(near_kernel, chunk, chunks, layers), out...]
    ppermute x3, starting transfers between devices: 7.59 us -> 9.01 us  [from_holders(): return lax.ppermute(value, everyone, perm)]
    ppermute x7 -> x6, starting transfers between devices: 9.73 us -> 9.59 us  [over_layers(): return lax.ppermute(value, 'layer', xor_perm(layers, s))]
  transfers between devices with their start and end apart: 29 -> 18, of which waited for: 11 -> 9; matrix products, arithmetic and copies ran while one was open for 0% -> 0% of each run, Pallas kernels for 28% -> 29%
where the time goes in v5:
time: 119 us; the launch traced here: 117 us
  waiting for transfers between devices  50.6 us (43%)
  Pallas kernels  35.1 us (29%)
  starting transfers between devices  28.4 us (24%)
  local copies, waits for them, and re-layouts  1.59 us (1%)
    ppermute x8, waiting for transfers between devices, over(): return lax.ppermute(value, 'col', xor_perm(cols, bit))  22 us
    ppermute x6, waiting for transfers between devices, over_layers(): return lax.ppermute(value, 'layer', xor_perm(layers, s))  21.4 us
    pallas_call x1, Pallas kernels, factor(): pl.pallas_call(lu_kernel, out_shape=jax.ShapeDtypeStruct(own.shape, jnp.f...  13.9 us
    ppermute x8, starting transfers between devices, over(): return lax.ppermute(value, 'col', xor_perm(cols, bit))  9.76 us
    ppermute x6, starting transfers between devices, over_layers(): return lax.ppermute(value, 'layer', xor_perm(layers, s))  9.59 us
    ppermute x3, starting transfers between devices, from_holders(): return lax.ppermute(value, everyone, perm)  9.01 us
    ppermute x3, waiting for transfers between devices, from_holders(): return lax.ppermute(value, everyone, perm)  7.13 us
    pallas_call x3, Pallas kernels, far_update(): pl.pallas_call(functools.partial(far_kernel, chunk, chunks, layers, len(e...  5.94 us
  transfers between devices with their start and end apart: 18, of which 9 were waited for; matrix products, arithmetic and copies ran while one was open for 0% of the time, Pallas kernels for 29%

profile of v5, /device:TPU:2, one launch (start us, length us, event | category | flops | bytes accessed | tf_op | source)
XLA Modules:
  0.0 116.8 jit_solution(5150198070868378970)
XLA Ops:
  0.7 1.4 %copy-done = bf16[1,8,1536,64]{2,3,1,0:T(8,128)(2,1)S(1)} copy-done((bf16[1,8,1536,64]{2,3,1,0:T(8,128)(2,1)S(1)}, bf16[1,8,1536,64]{2,3,1,0:T(8,128)(2,1)}, u32[]{:S(2)}) %copy-start) | copy-done | bytes 1572888
  2.1 0.1 halves.1
  2.3 2.0 %collective-permute-start.1 = (bf16[4,64,1536]{2,1,0:T(8,128)(2,1)S(1)}, bf16[4,64,1536]{2,1,0:T(8,128)(2,1)S(1)}, u32[]{:S(2)}, u32[]{:S(2)}) collective-permute-start(bf16[4,64,1536]{2,1,0:T(8,128)(2,1)S(1)} %get-tuple-element.41.refs_2_), channel_id=1, source_target_pairs={{0,2},{1,3},{2,0},{3,1},{4,6},{5,7},{6,4},{7,5},{8,10},{9,11},{10,... | collective-permute-start | bytes 2359304 | tf_op jit(solution)/shard_map/ppermute | solution.py:466
  4.4 0.1 copy.9
  4.5 0.1 stack.31.where_ref
  4.6 17.7 %collective-permute-done.refs_1_ = bf16[4,64,1536]{2,1,0:T(8,128)(2,1)S(1)} collective-permute-done((bf16[4,64,1536]{2,1,0:T(8,128)(2,1)S(1)}, bf16[4,64,1536]{2,1,0:T(8,128)(2,1)S(1)}, u32[]{:S(2)}, u32[]{:S(2)}) %collective-permute-start) | collective-permute-done | bytes 786464 | tf_op jit(solution)/shard_map/ppermute | solution.py:466
  22.3 0.1 collective-permute-done.1.refs_3_
  22.3 0.4 split.3
  22.7 1.8 %collective-permute-start.5 = (bf16[2,4,64,512]{3,2,1,0:T(8,128)(2,1)S(1)}, bf16[2,4,64,512]{3,2,1,0:T(8,128)(2,1)S(1)}, u32[]{:S(2)}, u32[]{:S(2)}) collective-permute-start(bf16[2,4,64,512]{3,2,1,0:T(8,128)(2,1)S(1)} %get-tuple-element.42.a_ref), channel_id=1, source_target_pairs={{0,2},{1,3},{2,0},{3,1},{4,6},{5,7},{6,4},{7,5},{8,10},{9,11},{10,... | collective-permute-start | bytes 1572872 | tf_op jit(solution)/shard_map/ppermute | solution.py:466
  24.5 1.5 %collective-permute-start.6 = (bf16[2,4,64,512]{3,2,1,0:T(8,128)(2,1)S(1)}, bf16[2,4,64,512]{3,2,1,0:T(8,128)(2,1)S(1)}, u32[]{:S(2)}, u32[]{:S(2)}) collective-permute-start(bf16[2,4,64,512]{3,2,1,0:T(8,128)(2,1)S(1)} %get-tuple-element.43.b_ref), channel_id=1, source_target_pairs={{0,1},{1,0},{2,3},{3,2},{4,5},{5,4},{6,7},{7,6},{8,9},{9,8},{10,11... | collective-permute-start | bytes 1572872 | tf_op jit(solution)/shard_map/ppermute | solution.py:466
  26.0 0.4 split.4
  26.3 0.6 collective-permute-start.8
  26.9 0.4 collective-permute-start.9
  27.3 0.4 split.5
  27.6 1.8 %collective-permute-start.2 = (bf16[2,4,64,512]{3,2,1,0:T(8,128)(2,1)S(1)}, bf16[2,4,64,512]{3,2,1,0:T(8,128)(2,1)S(1)}, u32[]{:S(2)}, u32[]{:S(2)}) collective-permute-start(bf16[2,4,64,512]{3,2,1,0:T(8,128)(2,1)S(1)} %get-tuple-element.48.a_ref), channel_id=1, source_target_pairs={{0,2},{1,3},{2,0},{3,1},{4,6},{5,7},{6,4},{7,5},{8,10},{9,11},{10,... | collective-permute-start | bytes 1572872 | tf_op jit(solution)/shard_map/ppermute | solution.py:466
  29.4 2.2 %masked_right.1 = (bf16[8,128,768]{2,1,0:T(8,128)(2,1)S(1)}, bf16[8,128,768]{2,1,0:T(8,128)(2,1)S(1)}) custom-call(s32[7]{0:T(128)S(1)} %stack.31.where_ref, s32[8,6]{1,0:T(8,128)S(1)} %bitcast.18, bf16[8,128,768]{2,1,0:T(8,128)(2,1)S(1)} %bitcast.17, bf16[8,128,768]{2,1,0:T(8,128)(2,1)} %collective-permute-done.4.uo_ref), custom_call_target="tpu_custom_call" | custom-call | flops 1000 | bytes 1000 | tf_op jit(solution)/shard_map/masked_right/pallas_call | solution.py:186
  31.6 1.8 %near_update.3.refs_1_ = f32[4,128,768]{2,1,0:T(8,128)S(1)} custom-call(s32[8,12]{1,0:T(8,128)S(1)} %bitcast.19, bf16[2,4,64,512]{3,2,1,0:T(8,128)(2,1)S(1)} %get-tuple-element.42.a_ref, bf16[2,4,64,512]{3,2,1,0:T(8,128)(2,1)S(1)} %get-tuple-element.43.b_ref, bf16[8,128,768]{2,1,0:T(8,128)(2,1)S(1)} %get-tuple-element.56.right_ref), custom_call_target="tpu_custom_call" | custom-call | flops 10000001024 | bytes 1000 | tf_op jit(solution)/shard_map/near_update/pallas_call | solution.py:226
  33.4 4.2 %collective-permute-done.5.a_ref = bf16[2,4,64,512]{3,2,1,0:T(8,128)(2,1)S(1)} collective-permute-done((bf16[2,4,64,512]{3,2,1,0:T(8,128)(2,1)S(1)}, bf16[2,4,64,512]{3,2,1,0:T(8,128)(2,1)S(1)}, u32[]{:S(2)}, u32[]{:S(2)}) %collective-permute-start.5) | collective-permute-done | bytes 524320 | tf_op jit(solution)/shard_map/ppermute | solution.py:466
  37.6 1.7 %collective-permute-start.3 = (bf16[2,4,64,512]{3,2,1,0:T(8,128)(2,1)S(1)}, bf16[2,4,64,512]{3,2,1,0:T(8,128)(2,1)S(1)}, u32[]{:S(2)}, u32[]{:S(2)}) collective-permute-start(bf16[2,4,64,512]{3,2,1,0:T(8,128)(2,1)S(1)} %get-tuple-element.49.b_ref), channel_id=1, source_target_pairs={{0,1},{1,0},{2,3},{3,2},{4,5},{5,4},{6,7},{7,6},{8,9},{9,8},{10,11... | collective-permute-start | bytes 1572872 | tf_op jit(solution)/shard_map/ppermute | solution.py:466
  39.3 2.0 %far_update.3 = (f32[2,128,768]{2,1,0:T(8,128)S(1)}, s16[144,1792]{1,0:T(8,128)(2,1)S(1)}, s16[144,256]{1,0:T(8,128)(2,1)S(1)}) custom-call(s32[7]{0:T(128)S(1)} %stack.31.where_ref, s32[8,12]{1,0:T(8,128)S(1)} %bitcast.20, bf16[2,4,64,512]{3,2,1,0:T(8,128)(2,1)S(1)} %collective-permute-done.5.a_ref, ...), custom_call_target="tpu_custom_call" | custom-call | flops 4000001024 | bytes 1000 | tf_op jit(solution)/shard_map/far_update/pallas_call | solution.py:274
  41.3 1.6 %collective-permute-start.7 = (s16[144,1792]{1,0:T(8,128)(2,1)S(1)}, s16[144,1792]{1,0:T(8,128)(2,1)S(1)}, u32[]{:S(2)}, u32[]{:S(2)}) collective-permute-start(s16[144,1792]{1,0:T(8,128)(2,1)S(1)} %get-tuple-element.54), channel_id=1, source_target_pairs={{0,8},{8,0},{16,24},{24,16},{1,9},{9,1},{17,25},{25,17},{2,10},{10... | collective-permute-start | bytes 1548296 | tf_op jit(solution)/shard_map/ppermute | solution.py:463
  43.0 1.8 %near_update.5.refs_1_ = f32[4,128,768]{2,1,0:T(8,128)S(1)} custom-call(s32[8,12]{1,0:T(8,128)S(1)} %bitcast.21, bf16[2,4,64,512]{3,2,1,0:T(8,128)(2,1)S(1)} %get-tuple-element.45.a_ref, bf16[2,4,64,512]{3,2,1,0:T(8,128)(2,1)S(1)} %get-tuple-element.46.b_ref, bf16[8,128,768]{2,1,0:T(8,128)(2,1)S(1)} %get-tuple-element.56.right_ref), custom_call_target="tpu_custom_call" | custom-call | flops 10000001024 | bytes 1000 | tf_op jit(solution)/shard_map/near_update/pallas_call | solution.py:226
  44.7 8.4 %collective-permute-done.7.got_ref = s16[144,1792]{1,0:T(8,128)(2,1)S(1)} collective-permute-done((s16[144,1792]{1,0:T(8,128)(2,1)S(1)}, s16[144,1792]{1,0:T(8,128)(2,1)S(1)}, u32[]{:S(2)}, u32[]{:S(2)}) %collective-permute-start.7) | collective-permute-done | bytes 516128 | tf_op jit(solution)/shard_map/ppermute | solution.py:463
  53.1 0.3 halve.3
  53.4 2.6 %collective-permute-start.12 = (s16[144,1024]{1,0:T(8,128)(2,1)S(1)}, s16[144,1024]{1,0:T(8,128)(2,1)S(1)}, u32[]{:S(2)}, u32[]{:S(2)}) collective-permute-start(s16[144,1024]{1,0:T(8,128)(2,1)S(1)} %get-tuple-element.55.refs_0_), channel_id=1, source_target_pairs={{0,16},{8,24},{16,0},{24,8},{1,17},{9,25},{17,1},{25,9},{2,18},{10... | collective-permute-start | bytes 884744 | tf_op jit(solution)/shard_map/ppermute | solution.py:463
  56.0 2.0 %far_update.4 = (f32[2,128,768]{2,1,0:T(8,128)S(1)}, s16[144,1536]{1,0:T(8,128)(2,1)S(1)}, s16[144,256]{1,0:T(8,128)(2,1)S(1)}) custom-call(s32[7]{0:T(128)S(1)} %stack.31.where_ref, s32[8,12]{1,0:T(8,128)S(1)} %bitcast.22, bf16[2,4,64,512]{3,2,1,0:T(8,128)(2,1)S(1)} %collective-permute-done.8.a_ref, ...), custom_call_target="tpu_custom_call" | custom-call | flops 4000001024 | bytes 1000 | tf_op jit(solution)/shard_map/far_update/pallas_call | solution.py:274
  58.0 0.6 collective-permute-start.10
  58.6 1.8 %near_update.4.refs_1_ = f32[4,128,768]{2,1,0:T(8,128)S(1)} custom-call(s32[8,12]{1,0:T(8,128)S(1)} %bitcast.23, bf16[2,4,64,512]{3,2,1,0:T(8,128)(2,1)S(1)} %get-tuple-element.48.a_ref, bf16[2,4,64,512]{3,2,1,0:T(8,128)(2,1)S(1)} %get-tuple-element.49.b_ref, bf16[8,128,768]{2,1,0:T(8,128)(2,1)S(1)} %get-tuple-element.56.right_ref), custom_call_target="tpu_custom_call" | custom-call | flops 10000001024 | bytes 1000 | tf_op jit(solution)/shard_map/near_update/pallas_call | solution.py:226
  60.4 7.7 %collective-permute-done.10.got_ref = s16[144,1536]{1,0:T(8,128)(2,1)S(1)} collective-permute-done((s16[144,1536]{1,0:T(8,128)(2,1)S(1)}, s16[144,1536]{1,0:T(8,128)(2,1)S(1)}, u32[]{:S(2)}, u32[]{:S(2)}) %collective-permute-start.10) | collective-permute-done | bytes 442400 | tf_op jit(solution)/shard_map/ppermute | solution.py:463
  68.1 0.2 halve.4
  68.3 2.0 %far_update.5 = (f32[2,128,768]{2,1,0:T(8,128)S(1)}, s16[144,1536]{1,0:T(8,128)(2,1)S(1)}, s16[144,512]{1,0:T(8,128)(2,1)S(1)}) custom-call(s32[7]{0:T(128)S(1)} %stack.31.where_ref, s32[8,12]{1,0:T(8,128)S(1)} %bitcast.24, bf16[2,4,64,512]{3,2,1,0:T(8,128)(2,1)S(1)} %collective-permute-done.2.a_ref, ...), custom_call_target="tpu_custom_call" | custom-call | flops 4000001024 | bytes 1000 | tf_op jit(solution)/shard_map/far_update/pallas_call | solution.py:274
  70.3 2.9 %collective-permute-start.13 = (s16[144,512]{1,0:T(8,128)(2,1)S(1)}, s16[144,512]{1,0:T(8,128)(2,1)S(1)}, u32[]{:S(2)}, u32[]{:S(2)}) collective-permute-start(s16[144,512]{1,0:T(8,128)(2,1)S(1)} %get-tuple-element.70.diag_ref.mine_ref), channel_id=1, source_target_pairs={{0,8},{1,9},{6,14},{7,15},{8,0},{9,1},{14,6},{15,7},{16,24},{17,25... | collective-permute-start | bytes 442376 | tf_op jit(solution)/shard_map/ppermute | solution.py:460
  73.2 4.1 %collective-permute-done.13.got_ref = s16[144,512]{1,0:T(8,128)(2,1)S(1)} collective-permute-done((s16[144,512]{1,0:T(8,128)(2,1)S(1)}, s16[144,512]{1,0:T(8,128)(2,1)S(1)}, u32[]{:S(2)}, u32[]{:S(2)}) %collective-permute-start.13) | collective-permute-done | bytes 147488 | tf_op jit(solution)/shard_map/ppermute | solution.py:460
  77.4 0.1 add_coded.1.refs_2_
  77.5 4.8 %collective-permute-start.14 = (s16[144,512]{1,0:T(8,128)(2,1)S(1)}, s16[144,512]{1,0:T(8,128)(2,1)S(1)}, u32[]{:S(2)}, u32[]{:S(2)}) collective-permute-start(s16[144,512]{1,0:T(8,128)(2,1)S(1)} %add_coded.1.refs_2_), channel_id=1, source_target_pairs={{0,16},{1,17},{6,22},{7,23},{8,24},{9,25},{14,30},{15,31},{16,0},{... | collective-permute-start | bytes 442376 | tf_op jit(solution)/shard_map/ppermute | solution.py:460
  82.3 1.8 %collective-permute-start.11 = (s16[144,1536]{1,0:T(8,128)(2,1)S(1)}, s16[144,1536]{1,0:T(8,128)(2,1)S(1)}, u32[]{:S(2)}, u32[]{:S(2)}) collective-permute-start(s16[144,1536]{1,0:T(8,128)(2,1)S(1)} %get-tuple-element.68), channel_id=1, source_target_pairs={{0,8},{8,0},{16,24},{24,16},{1,9},{9,1},{17,25},{25,17},{2,10},{10... | collective-permute-start | bytes 1327112 | tf_op jit(solution)/shard_map/ppermute | solution.py:463
  84.1 3.0 %collective-permute-done.14.refs_3_ = s16[144,512]{1,0:T(8,128)(2,1)S(1)} collective-permute-done((s16[144,512]{1,0:T(8,128)(2,1)S(1)}, s16[144,512]{1,0:T(8,128)(2,1)S(1)}, u32[]{:S(2)}, u32[]{:S(2)}) %collective-permute-start.14) | collective-permute-done | bytes 147488 | tf_op jit(solution)/shard_map/ppermute | solution.py:460
  87.1 0.8 pivots.1.own_ref
  87.9 1.3 %collective-permute-start.15 = (f32[6,128,128]{2,1,0:T(8,128)S(1)}, f32[6,128,128]{2,1,0:T(8,128)S(1)}, u32[]{:S(2)}, u32[]{:S(2)}) collective-permute-start(f32[6,128,128]{2,1,0:T(8,128)S(1)} %pivots.1.own_ref), channel_id=1, source_target_pairs={{0,4},{1,5},{6,2},{7,3},{8,12},{9,13},{14,10},{15,11},{16,20},{17,... | collective-permute-start | bytes 1179656 | tf_op jit(solution)/shard_map/ppermute | solution.py:460
  89.2 1.6 %combine.3.refs_1_ = f32[384,768]{1,0:T(8,128)} custom-call(s32[7]{0:T(128)S(1)} %stack.31.where_ref, f32[1536,768]{1,0:T(8,128)S(1)} %bitcast.14, f32[128,768]{1,0:T(8,128)S(1)} %get-tuple-element.77.kept_ref, s16[144,1024]{1,0:T(8,128)(2,1)S(1)} %collective-permute-done.12.refs_1_.refs_0_), custom_call_target="tpu_custom_call" | custom-call | flops 1000 | bytes 1000 | tf_op jit(solution)/shard_map/combine/pallas_call | solution.py:360
  90.9 0.1 collective-permute-done.11.got_ref
  91.0 0.2 halve.5
  91.2 1.3 %collective-permute-start.16 = (s16[144,768]{1,0:T(8,128)(2,1)S(1)}, s16[144,768]{1,0:T(8,128)(2,1)S(1)}, u32[]{:S(2)}, u32[]{:S(2)}) collective-permute-start(s16[144,768]{1,0:T(8,128)(2,1)S(1)} %get-tuple-element.73), channel_id=1, source_target_pairs={{0,16},{8,24},{16,0},{24,8},{1,17},{9,25},{17,1},{25,9},{2,18},{10... | collective-permute-start | bytes 663560 | tf_op jit(solution)/shard_map/ppermute | solution.py:463
  92.5 1.7 %collective-permute-start.17 = (s16[144,768]{1,0:T(8,128)(2,1)S(1)}, s16[144,768]{1,0:T(8,128)(2,1)S(1)}, u32[]{:S(2)}, u32[]{:S(2)}) collective-permute-start(s16[144,768]{1,0:T(8,128)(2,1)S(1)} %get-tuple-element.76), channel_id=1, source_target_pairs={{0,16},{8,24},{16,0},{24,8},{1,17},{9,25},{17,1},{25,9},{2,18},{10... | collective-permute-start | bytes 663560 | tf_op jit(solution)/shard_map/ppermute | solution.py:463
  94.2 13.9 %factor.1 = f32[6,128,128]{2,1,0:T(8,128)} custom-call(s32[7]{0:T(128)S(1)} %stack.31.where_ref, f32[6,128,128]{2,1,0:T(8,128)S(1)} %pivots.1.own_ref, f32[6,128,128]{2,1,0:T(8,128)S(1)} %collective-permute-done.15.other_ref), custom_call_target="tpu_custom_call" | custom-call | flops 20000000000 | bytes 1000 | tf_op jit(solution)/shard_map/factor/pallas_call | solution.py:82
  108.1 5.2 %collective-permute-done.17.refs_0_ = s16[144,768]{1,0:T(8,128)(2,1)S(1)} collective-permute-done((s16[144,768]{1,0:T(8,128)(2,1)S(1)}, s16[144,768]{1,0:T(8,128)(2,1)S(1)}, u32[]{:S(2)}, u32[]{:S(2)}) %collective-permute-start.17) | collective-permute-done | bytes 221216 | tf_op jit(solution)/shard_map/ppermute | solution.py:463
  113.3 1.6 %combine.4.refs_1_ = f32[384,768]{1,0:T(8,128)} custom-call(s32[7]{0:T(128)S(1)} %stack.31.where_ref, f32[1536,768]{1,0:T(8,128)S(1)} %bitcast.14, f32[128,768]{1,0:T(8,128)S(1)} %get-tuple-element.75.kept_ref, s16[144,768]{1,0:T(8,128)(2,1)S(1)} %collective-permute-done.17.refs_0_, f32[384,768]{1,0:T(8,128)} %combine.3.refs_1_), custom_call_target="tpu_custom_call", output_to_operand_aliasing={{}: (4, {})} | custom-call | flops 1000 | bytes 1000 | tf_op jit(solution)/shard_map/combine/pallas_call | solution.py:360
  115.0 1.6 %combine.5 = f32[384,768]{1,0:T(8,128)} custom-call(s32[7]{0:T(128)S(1)} %stack.31.where_ref, f32[1536,768]{1,0:T(8,128)S(1)} %bitcast.14, f32[128,768]{1,0:T(8,128)S(1)} %get-tuple-element.71.kept_ref, s16[144,768]{1,0:T(8,128)(2,1)S(1)} %collective-permute-done.16.refs_0_, f32[384,768]{1,0:T(8,128)} %combine.4.refs_1_), custom_call_target="tpu_custom_call", output_to_operand_aliasing={{}: (4, {})} | custom-call | flops 1000 | bytes 1000 | tf_op jit(solution)/shard_map/combine/pallas_call | solution.py:360
  (23 shorter events, 0.2 us)
Async XLA Ops:
  0.6 3.8 %copy-start.3 = (s32[1,8,6]{1,0,2:T(1,128)S(1)}, s32[1,8,6]{1,0,2:T(1,128)}, u32[]{:S(2)}) copy-start(s32[1,8,6]{1,0,2:T(1,128)} %param.8) | copy-start | bytes 580
  0.6 27.0 %collective-permute-start.4 = (bf16[8,128,768]{2,1,0:T(8,128)(2,1)}, bf16[8,128,768]{2,1,0:T(8,128)(2,1)}, u32[]{:S(2)}, u32[]{:S(2)}) collective-permute-start(bf16[8,128,768]{2,1,0:T(8,128)(2,1)} %bitcast.16), channel_id=1, source_target_pairs={{0,4},{4,0},{1,5},{5,1},{2,6},{6,2},{3,7},{7,3},{8,12},{12,8},{9,1... | collective-permute-start | bytes 4718600 | tf_op jit(solution)/shard_map/ppermute | solution.py:472
  0.7 1.4 %copy-start = (bf16[1,8,1536,64]{2,3,1,0:T(8,128)(2,1)S(1)}, bf16[1,8,1536,64]{2,3,1,0:T(8,128)(2,1)}, u32[]{:S(2)}) copy-start(bf16[1,8,1536,64]{2,3,1,0:T(8,128)(2,1)} %param.5) | copy-start | bytes 4718596
  2.3 20.0 %collective-permute-start = (bf16[4,64,1536]{2,1,0:T(8,128)(2,1)S(1)}, bf16[4,64,1536]{2,1,0:T(8,128)(2,1)S(1)}, u32[]{:S(2)}, u32[]{:S(2)}) collective-permute-start(bf16[4,64,1536]{2,1,0:T(8,128)(2,1)S(1)} %get-tuple-element.47.refs_0_), channel_id=1, source_target_pairs={{0,1},{1,0},{2,3},{3,2},{4,5},{5,4},{6,7},{7,6},{8,9},{9,8},{10,11... | collective-permute-start | bytes 2359304 | tf_op jit(solution)/shard_map/ppermute | solution.py:466
  2.3 20.0 %collective-permute-start.1 = (bf16[4,64,1536]{2,1,0:T(8,128)(2,1)S(1)}, bf16[4,64,1536]{2,1,0:T(8,128)(2,1)S(1)}, u32[]{:S(2)}, u32[]{:S(2)}) collective-permute-start(bf16[4,64,1536]{2,1,0:T(8,128)(2,1)S(1)} %get-tuple-element.41.refs_2_), channel_id=1, source_target_pairs={{0,2},{1,3},{2,0},{3,1},{4,6},{5,7},{6,4},{7,5},{8,10},{9,11},{10,... | collective-permute-start | bytes 2359304 | tf_op jit(solution)/shard_map/ppermute | solution.py:466
  22.7 14.9 %collective-permute-start.5 = (bf16[2,4,64,512]{3,2,1,0:T(8,128)(2,1)S(1)}, bf16[2,4,64,512]{3,2,1,0:T(8,128)(2,1)S(1)}, u32[]{:S(2)}, u32[]{:S(2)}) collective-permute-start(bf16[2,4,64,512]{3,2,1,0:T(8,128)(2,1)S(1)} %get-tuple-element.42.a_ref), channel_id=1, source_target_pairs={{0,2},{1,3},{2,0},{3,1},{4,6},{5,7},{6,4},{7,5},{8,10},{9,11},{10,... | collective-permute-start | bytes 1572872 | tf_op jit(solution)/shard_map/ppermute | solution.py:466
  24.5 14.9 %collective-permute-start.6 = (bf16[2,4,64,512]{3,2,1,0:T(8,128)(2,1)S(1)}, bf16[2,4,64,512]{3,2,1,0:T(8,128)(2,1)S(1)}, u32[]{:S(2)}, u32[]{:S(2)}) collective-permute-start(bf16[2,4,64,512]{3,2,1,0:T(8,128)(2,1)S(1)} %get-tuple-element.43.b_ref), channel_id=1, source_target_pairs={{0,1},{1,0},{2,3},{3,2},{4,5},{5,4},{6,7},{7,6},{8,9},{9,8},{10,11... | collective-permute-start | bytes 1572872 | tf_op jit(solution)/shard_map/ppermute | solution.py:466
  26.3 29.7 %collective-permute-start.8 = (bf16[2,4,64,512]{3,2,1,0:T(8,128)(2,1)S(1)}, bf16[2,4,64,512]{3,2,1,0:T(8,128)(2,1)S(1)}, u32[]{:S(2)}, u32[]{:S(2)}) collective-permute-start(bf16[2,4,64,512]{3,2,1,0:T(8,128)(2,1)S(1)} %get-tuple-element.45.a_ref), channel_id=1, source_target_pairs={{0,2},{1,3},{2,0},{3,1},{4,6},{5,7},{6,4},{7,5},{8,10},{9,11},{10,... | collective-permute-start | bytes 1572872 | tf_op jit(solution)/shard_map/ppermute | solution.py:466
  26.9 2.5 %copy-start.1 = (bf16[1,8,128,768]{3,2,1,0:T(8,128)(2,1)S(1)}, bf16[1,8,128,768]{3,2,1,0:T(8,128)(2,1)}, u32[]{:S(2)}) copy-start(bf16[1,8,128,768]{3,2,1,0:T(8,128)(2,1)} %param.6) | copy-start | bytes 4718596
  26.9 29.1 %collective-permute-start.9 = (bf16[2,4,64,512]{3,2,1,0:T(8,128)(2,1)S(1)}, bf16[2,4,64,512]{3,2,1,0:T(8,128)(2,1)S(1)}, u32[]{:S(2)}, u32[]{:S(2)}) collective-permute-start(bf16[2,4,64,512]{3,2,1,0:T(8,128)(2,1)S(1)} %get-tuple-element.46.b_ref), channel_id=1, source_target_pairs={{0,1},{1,0},{2,3},{3,2},{4,5},{5,4},{6,7},{7,6},{8,9},{9,8},{10,11... | collective-permute-start | bytes 1572872 | tf_op jit(solution)/shard_map/ppermute | solution.py:466
  27.6 40.7 %collective-permute-start.2 = (bf16[2,4,64,512]{3,2,1,0:T(8,128)(2,1)S(1)}, bf16[2,4,64,512]{3,2,1,0:T(8,128)(2,1)S(1)}, u32[]{:S(2)}, u32[]{:S(2)}) collective-permute-start(bf16[2,4,64,512]{3,2,1,0:T(8,128)(2,1)S(1)} %get-tuple-element.48.a_ref), channel_id=1, source_target_pairs={{0,2},{1,3},{2,0},{3,1},{4,6},{5,7},{6,4},{7,5},{8,10},{9,11},{10,... | collective-permute-start | bytes 1572872 | tf_op jit(solution)/shard_map/ppermute | solution.py:466
  29.4 2.2 %copy-start.2 = (s32[1,8,12]{2,1,0:T(8,128)S(1)}, s32[1,8,12]{2,1,0:T(8,128)}, u32[]{:S(2)}) copy-start(s32[1,8,12]{2,1,0:T(8,128)} %param.7) | copy-start | bytes 1156
  37.6 30.7 %collective-permute-start.3 = (bf16[2,4,64,512]{3,2,1,0:T(8,128)(2,1)S(1)}, bf16[2,4,64,512]{3,2,1,0:T(8,128)(2,1)S(1)}, u32[]{:S(2)}, u32[]{:S(2)}) collective-permute-start(bf16[2,4,64,512]{3,2,1,0:T(8,128)(2,1)S(1)} %get-tuple-element.49.b_ref), channel_id=1, source_target_pairs={{0,1},{1,0},{2,3},{3,2},{4,5},{5,4},{6,7},{7,6},{8,9},{9,8},{10,11... | collective-permute-start | bytes 1572872 | tf_op jit(solution)/shard_map/ppermute | solution.py:466
  41.3 11.8 %collective-permute-start.7 = (s16[144,1792]{1,0:T(8,128)(2,1)S(1)}, s16[144,1792]{1,0:T(8,128)(2,1)S(1)}, u32[]{:S(2)}, u32[]{:S(2)}) collective-permute-start(s16[144,1792]{1,0:T(8,128)(2,1)S(1)} %get-tuple-element.54), channel_id=1, source_target_pairs={{0,8},{8,0},{16,24},{24,16},{1,9},{9,1},{17,25},{25,17},{2,10},{10... | collective-permute-start | bytes 1548296 | tf_op jit(solution)/shard_map/ppermute | solution.py:463
  53.4 19.8 %collective-permute-start.12 = (s16[144,1024]{1,0:T(8,128)(2,1)S(1)}, s16[144,1024]{1,0:T(8,128)(2,1)S(1)}, u32[]{:S(2)}, u32[]{:S(2)}) collective-permute-start(s16[144,1024]{1,0:T(8,128)(2,1)S(1)} %get-tuple-element.55.refs_0_), channel_id=1, source_target_pairs={{0,16},{8,24},{16,0},{24,8},{1,17},{9,25},{17,1},{25,9},{2,18},{10... | collective-permute-start | bytes 884744 | tf_op jit(solution)/shard_map/ppermute | solution.py:463
  58.0 10.0 %collective-permute-start.10 = (s16[144,1536]{1,0:T(8,128)(2,1)S(1)}, s16[144,1536]{1,0:T(8,128)(2,1)S(1)}, u32[]{:S(2)}, u32[]{:S(2)}) collective-permute-start(s16[144,1536]{1,0:T(8,128)(2,1)S(1)} %get-tuple-element.63), channel_id=1, source_target_pairs={{0,8},{8,0},{16,24},{24,16},{1,9},{9,1},{17,25},{25,17},{2,10},{10... | collective-permute-start | bytes 1327112 | tf_op jit(solution)/shard_map/ppermute | solution.py:463
  68.3 18.8 %slice-start = ((s8[4718592]{0:T(1024)(128)(4,1)}), s8[4194304]{0:T(1024)(128)(4,1)S(1)}, s32[]{:S(2)}) async-start(s8[4718592]{0:T(1024)(128)(4,1)} %bitcast.13), calls=%async_computation | async-start | bytes 8388608
  68.3 18.8 %slice-start.1 = ((s8[4718592]{0:T(1024)(128)(4,1)}), s8[524288]{0:T(1024)(128)(4,1)S(1)}, s32[]{:S(2)}) async-start(s8[4718592]{0:T(1024)(128)(4,1)} %bitcast.13), calls=%async_computation.1 | async-start | bytes 1048576
  70.3 7.0 %collective-permute-start.13 = (s16[144,512]{1,0:T(8,128)(2,1)S(1)}, s16[144,512]{1,0:T(8,128)(2,1)S(1)}, u32[]{:S(2)}, u32[]{:S(2)}) collective-permute-start(s16[144,512]{1,0:T(8,128)(2,1)S(1)} %get-tuple-element.70.diag_ref.mine_ref), channel_id=1, source_target_pairs={{0,8},{1,9},{6,14},{7,15},{8,0},{9,1},{14,6},{15,7},{16,24},{17,25... | collective-permute-start | bytes 442376 | tf_op jit(solution)/shard_map/ppermute | solution.py:460
  77.5 9.6 %collective-permute-start.14 = (s16[144,512]{1,0:T(8,128)(2,1)S(1)}, s16[144,512]{1,0:T(8,128)(2,1)S(1)}, u32[]{:S(2)}, u32[]{:S(2)}) collective-permute-start(s16[144,512]{1,0:T(8,128)(2,1)S(1)} %add_coded.1.refs_2_), channel_id=1, source_target_pairs={{0,16},{1,17},{6,22},{7,23},{8,24},{9,25},{14,30},{15,31},{16,0},{... | collective-permute-start | bytes 442376 | tf_op jit(solution)/shard_map/ppermute | solution.py:460
  82.3 8.7 %collective-permute-start.11 = (s16[144,1536]{1,0:T(8,128)(2,1)S(1)}, s16[144,1536]{1,0:T(8,128)(2,1)S(1)}, u32[]{:S(2)}, u32[]{:S(2)}) collective-permute-start(s16[144,1536]{1,0:T(8,128)(2,1)S(1)} %get-tuple-element.68), channel_id=1, source_target_pairs={{0,8},{8,0},{16,24},{24,16},{1,9},{9,1},{17,25},{25,17},{2,10},{10... | collective-permute-start | bytes 1327112 | tf_op jit(solution)/shard_map/ppermute | solution.py:463
  87.9 3.3 %collective-permute-start.15 = (f32[6,128,128]{2,1,0:T(8,128)S(1)}, f32[6,128,128]{2,1,0:T(8,128)S(1)}, u32[]{:S(2)}, u32[]{:S(2)}) collective-permute-start(f32[6,128,128]{2,1,0:T(8,128)S(1)} %pivots.1.own_ref), channel_id=1, source_target_pairs={{0,4},{1,5},{6,2},{7,3},{8,12},{9,13},{14,10},{15,11},{16,20},{17,... | collective-permute-start | bytes 1179656 | tf_op jit(solution)/shard_map/ppermute | solution.py:460
  91.2 23.8 %collective-permute-start.16 = (s16[144,768]{1,0:T(8,128)(2,1)S(1)}, s16[144,768]{1,0:T(8,128)(2,1)S(1)}, u32[]{:S(2)}, u32[]{:S(2)}) collective-permute-start(s16[144,768]{1,0:T(8,128)(2,1)S(1)} %get-tuple-element.73), channel_id=1, source_target_pairs={{0,16},{8,24},{16,0},{24,8},{1,17},{9,25},{17,1},{25,9},{2,18},{10... | collective-permute-start | bytes 663560 | tf_op jit(solution)/shard_map/ppermute | solution.py:463
  92.5 20.9 %collective-permute-start.17 = (s16[144,768]{1,0:T(8,128)(2,1)S(1)}, s16[144,768]{1,0:T(8,128)(2,1)S(1)}, u32[]{:S(2)}, u32[]{:S(2)}) collective-permute-start(s16[144,768]{1,0:T(8,128)(2,1)S(1)} %get-tuple-element.76), channel_id=1, source_target_pairs={{0,16},{8,24},{16,0},{24,8},{1,17},{9,25},{17,1},{25,9},{2,18},{10... | collective-permute-start | bytes 663560 | tf_op jit(solution)/shard_map/ppermute | solution.py:463

commit v6 on v5

v6 whole, which is shorter than its diff:
```python
import functools

import jax
import jax.numpy as jnp
from jax import lax
from jax.experimental import pallas as pl
from jax.experimental.pallas import tpu as pltpu
from jax.sharding import PartitionSpec as P

BLK = 128
VMEM_LIMIT = 24 * 1024 * 1024
SMEM = pl.BlockSpec(memory_space=pltpu.SMEM)
VMEM = pl.BlockSpec(memory_space=pltpu.VMEM)
ANY = pl.BlockSpec(memory_space=pl.ANY)
CODE_TOP = 32500.0
EXP_STEPS = 128.0
EXP_ROWS = 16
HALF_STEPS = 48
NEAR = 10
FAR = 4


def cost(micros):
    return pl.CostEstimate(
        flops=1_000_000_000 * micros + 1000, bytes_accessed=1000, transcendentals=0
    )


def params(**kwargs):
    return pltpu.CompilerParams(vmem_limit_bytes=VMEM_LIMIT, **kwargs)


def encode(block):
    top = jnp.max(jnp.abs(block), axis=0, keepdims=True)
    level = jnp.ceil(jnp.log2(jnp.maximum(top, 1e-30)) * EXP_STEPS) + 1.0
    codes = jnp.round(block * (CODE_TOP * jnp.exp2(level * (-1.0 / EXP_STEPS))))
    return codes.astype(jnp.int32).astype(jnp.int16), jnp.broadcast_to(
        level.astype(jnp.int32), (EXP_ROWS, block.shape[1])
    ).astype(jnp.int16)


def decode(codes, levels):
    level = levels.astype(jnp.int32).astype(jnp.float32)[:1]
    scale = jnp.exp2(level * (1.0 / EXP_STEPS)) * (1.0 / CODE_TOP)
    return codes.astype(jnp.int32).astype(jnp.float32) * scale


def lu_step(ref, j):
    size = ref.shape[1]
    top = j // 8 * 8
    row = ref[:, j : j + 1, :]
    inverse = 1.0 / row[:, :, j : j + 1]
    lanes = lax.broadcasted_iota(jnp.int32, (1, 1, size), 2)
    used = jnp.where(lanes > j, row, 0.0)
    if j % 8 != 7:
        head = ref[:, top : top + 8, :]
        rows = lax.broadcasted_iota(jnp.int32, (1, 8, 1), 1) + top
        factor = jnp.where(rows > j, head[:, :, j : j + 1] * inverse, 0.0)
        swept = head - factor * used
        ref[:, top : top + 8, :] = jnp.where((lanes == j) & (rows > j), factor, swept)
    if top + 8 < size:
        rest = ref[:, top + 8 :, :]
        factor = rest[:, :, j : j + 1] * inverse
        ref[:, top + 8 :, :] = jnp.where(lanes == j, factor, rest - factor * used)


def lu_kernel(until, where_ref, own_ref, other_ref, out_ref):
    held = where_ref[1] == where_ref[3]

    @pl.when(held)
    def _():
        out_ref[...] = own_ref[...]

    @pl.when(jnp.logical_not(held))
    def _():
        out_ref[...] = other_ref[...]

    for j in range(until):
        lu_step(out_ref, j)


def factor(where, own, other, until):
    return pl.pallas_call(
        functools.partial(lu_kernel, until),
        out_shape=jax.ShapeDtypeStruct(own.shape, jnp.float32),
        in_specs=[SMEM, VMEM, VMEM],
        out_specs=VMEM,
        compiler_params=params(),
        cost_estimate=cost(10),
        name="factor",
    )(where, own, other)


def rest_kernel(begin, in_ref, out_ref):
    out_ref[...] = in_ref[...]
    for j in range(begin, out_ref.shape[1]):
        lu_step(out_ref, j)


def factor_rest(blocks, begin):
    return pl.pallas_call(
        functools.partial(rest_kernel, begin),
        out_shape=jax.ShapeDtypeStruct(blocks.shape, jnp.float32),
        in_specs=[VMEM],
        out_specs=VMEM,
        compiler_params=params(),
        cost_estimate=cost(10),
        name="factor_rest",
    )(blocks)


def halves_kernel(lt_ref, one_ref, two_ref, sems):
    half = one_ref.shape[0]
    copies = [
        pltpu.make_async_copy(lt_ref.at[:half], one_ref, sems.at[0]),
        pltpu.make_async_copy(lt_ref.at[half:], two_ref, sems.at[1]),
    ]
    for copy in copies:
        copy.start()
    for copy in copies:
        copy.wait()


def halves(lt):
    supers, depth, length = lt.shape
    one = jax.ShapeDtypeStruct((supers // 2, depth, length), lt.dtype)
    return pl.pallas_call(
        halves_kernel,
        out_shape=[one, one],
        in_specs=[ANY],
        out_specs=[ANY, ANY],
        scratch_shapes=[pltpu.SemaphoreType.DMA((2,))],
        compiler_params=params(),
        cost_estimate=cost(0),
        name="halves",
    )(lt)


def first_block(where_ref, phase, part, start, blocks):
    half = where_ref[7] if phase == 0 else 1 - where_ref[7]
    return (2 * half + part) * blocks + start


def split_kernel(phase, start, count, blocks, where_ref, *refs):
    sources, outs, sems = refs[:4], refs[4:6], refs[6]
    size = count * BLK
    copies = []
    for n, ref in enumerate(sources):
        for part in range(2):
            begin = first_block(where_ref, 1 - phase, part, start, blocks) * BLK
            copies.append(
                pltpu.make_async_copy(
                    ref.at[:, :, pl.ds(pl.multiple_of(begin, BLK), size)],
                    outs[n // 2].at[n % 2, :, :, part * size : (part + 1) * size],
                    sems.at[n, part],
                )
            )
    for copy in copies:
        copy.start()
    for copy in copies:
        copy.wait()


def split(where, sources, chunk, blocks):
    phase, start, count = chunk
    half, depth, _ = sources[0].shape
    one = jax.ShapeDtypeStruct((2, half, depth, 2 * count * BLK), sources[0].dtype)
    return pl.pallas_call(
        functools.partial(split_kernel, phase, start, count, blocks),
        out_shape=[one, one],
        in_specs=[SMEM] + [ANY] * 4,
        out_specs=[ANY, ANY],
        scratch_shapes=[pltpu.SemaphoreType.DMA((4, 2))],
        compiler_params=params(),
        cost_estimate=cost(0),
        name="split",
    )(where, *sources)


def right_kernel(where_ref, upat_ref, u_ref, uo_ref, near_ref, far_ref):
    supers, wide, cols = u_ref.shape
    depth = wide // 2
    begin = where_ref[6] * depth
    mine = where_ref[1] == where_ref[3]

    def fill(close_ref, away_ref):
        for n, ref in enumerate((close_ref, close_ref, away_ref, away_ref)):
            spot = begin if n % 2 == 0 else depth - begin
            rows = pl.ds(pl.multiple_of(spot, depth), depth)
            for k in range(supers):
                first = (0, 1) if k < supers // 2 else (0, 2)
                out_ref = near_ref if n in first else far_ref
                at = 0 if n in (0, 3 - first[1]) else depth
                for m in range(cols // BLK):
                    lanes = slice(m * BLK, (m + 1) * BLK)
                    block = ref[k, rows, lanes]
                    out_ref[k, at : at + depth, lanes] = jnp.where(
                        upat_ref[k, m] != 0, block, jnp.zeros_like(block)
                    )

    @pl.when(mine)
    def _():
        fill(u_ref, uo_ref)

    @pl.when(jnp.logical_not(mine))
    def _():
        fill(uo_ref, u_ref)


def masked_right(where, upat, u, uo):
    shape = jax.ShapeDtypeStruct(u.shape, u.dtype)
    return pl.pallas_call(
        right_kernel,
        out_shape=[shape, shape],
        in_specs=[SMEM, SMEM, VMEM, VMEM],
        out_specs=[VMEM, VMEM],
        compiler_params=params(),
        cost_estimate=cost(0),
        name="masked_right",
    )(where, upat, u, uo)


def product(chunk, blocks, where_ref, lpat_ref, whole, groups, right_ref, left):
    phase, start, count = chunk
    pieces, half, depth = 2, left.shape[0] // 2, left.shape[1] // 2
    for part in range(2):
        first = first_block(where_ref, phase, part, start, blocks)
        for h, group in enumerate(groups):
            for n in range(pieces):
                for i in range(half):
                    k = h * half + i
                    for m in range(count):
                        at = (part * count + m) * BLK
                        if whole:
                            begin = pl.multiple_of((first + m) * BLK, BLK)
                            block = group[n][i, :, pl.ds(begin, BLK)]
                        else:
                            block = group[n, i, :, at : at + BLK]
                        kept = lpat_ref[k, first + m] != 0
                        left[k, n * depth : (n + 1) * depth, at : at + BLK] = jnp.where(
                            kept, block, jnp.zeros_like(block)
                        )
    return lax.dot_general(
        left[...].reshape(-1, left.shape[2]),
        right_ref[...].reshape(-1, right_ref.shape[2]),
        (((0,), (0,)), ((), ())),
        preferred_element_type=jnp.float32,
    )


def near_kernel(chunk, blocks, where_ref, lpat_ref, *refs):
    right_ref, acc_ref, left = refs[4:]
    groups = (refs[:2], refs[2:4])
    total = product(chunk, blocks, where_ref, lpat_ref, True, groups, right_ref, left)
    acc_ref[...] = total.reshape(acc_ref.shape)


def near_update(where, lpat, sources, right, chunk, blocks):
    supers, kdim, cols = right.shape
    count = 2 * chunk[2]
    return pl.pallas_call(
        functools.partial(near_kernel, chunk, blocks),
        out_shape=jax.ShapeDtypeStruct((count, BLK, cols), jnp.float32),
        in_specs=[SMEM] * 2 + [VMEM] * 5,
        out_specs=VMEM,
        scratch_shapes=[pltpu.VMEM((supers, kdim, count * BLK), jnp.bfloat16)],
        compiler_params=params(),
        cost_estimate=cost(NEAR),
        name="near_update",
    )(where, lpat, *sources, right)


def far_kernel(chunk, blocks, where_ref, lpat_ref, a_ref, b_ref, right_ref, before_ref, *refs):
    kept_ref, sent_ref = refs[:2]
    left, acc = refs[-2:]
    count = chunk[2]
    groups = (a_ref, b_ref)
    total = product(chunk, blocks, where_ref, lpat_ref, False, groups, right_ref, left)
    acc[...] = (before_ref[...] + total.reshape(before_ref.shape)).reshape(acc.shape)
    if chunk[0] == 0:
        diag_ref = refs[2]
        for q in range(2 * count):
            lanes = slice(q * BLK, (q + 1) * BLK)
            diag_ref[:BLK, lanes], diag_ref[BLK:, lanes] = encode(
                acc[q // count, q % count, :, lanes]
            )
    mine = where_ref[0] & 1
    for m in range(count):
        kept_ref[m] = acc[mine, m]
        sent_ref[m, :BLK], sent_ref[m, BLK:] = encode(acc[1 - mine, m])


def far_update(where, lpat, pieces, right, before, chunk, blocks):
    supers, kdim, cols = right.shape
    count = chunk[2]
    coded = BLK + EXP_ROWS
    shapes = [
        jax.ShapeDtypeStruct((count, BLK, cols), jnp.float32),
        jax.ShapeDtypeStruct((count, coded, cols), jnp.int16),
    ]
    if chunk[0] == 0:
        shapes.append(jax.ShapeDtypeStruct((coded, 2 * count * BLK), jnp.int16))
    return pl.pallas_call(
        functools.partial(far_kernel, chunk, blocks),
        out_shape=shapes,
        in_specs=[SMEM] * 2 + [VMEM] * 4,
        out_specs=[VMEM] * len(shapes),
        scratch_shapes=[
            pltpu.VMEM((supers, kdim, 2 * count * BLK), jnp.bfloat16),
            pltpu.VMEM((2, count, BLK, cols), jnp.float32),
        ],
        compiler_params=params(),
        cost_estimate=cost(FAR),
        name="far_update",
    )(where, lpat, *pieces, right, before)


def halve_kernel(kept_ref, got_ref, sum_ref, sent_ref):
    for m in range(kept_ref.shape[0]):
        total = kept_ref[m] + decode(got_ref[m, :BLK], got_ref[m, BLK:])
        sum_ref[m] = total
        sent_ref[m, :BLK], sent_ref[m, BLK:] = encode(total)


def halve(kept, got):
    return pl.pallas_call(
        halve_kernel,
        out_shape=[
            jax.ShapeDtypeStruct(kept.shape, kept.dtype),
            jax.ShapeDtypeStruct(got.shape, got.dtype),
        ],
        in_specs=[VMEM] * 2,
        out_specs=[VMEM] * 2,
        compiler_params=params(),
        cost_estimate=cost(0),
        name="halve",
    )(kept, got)


def add_kernel(mine_ref, got_ref, out_ref):
    total = decode(mine_ref[:BLK], mine_ref[BLK:]) + decode(got_ref[:BLK], got_ref[BLK:])
    out_ref[:BLK], out_ref[BLK:] = encode(total)


def add_coded(mine, got):
    return pl.pallas_call(
        add_kernel,
        out_shape=jax.ShapeDtypeStruct(mine.shape, mine.dtype),
        in_specs=[VMEM] * 2,
        out_specs=VMEM,
        compiler_params=params(),
        cost_estimate=cost(0),
        name="add_coded",
    )(mine, got)


def combine_kernel(counts, where_ref, anc_ref, *refs):
    out_ref, start, sem = refs[-3:]
    share = out_ref.shape[0]
    begin = pl.multiple_of(where_ref[0] * share, BLK)
    fetch = pltpu.make_async_copy(anc_ref.at[pl.ds(begin, share)], start, sem)
    fetch.start()
    fetch.wait()

    def fill(spots):
        row = 0
        for n in spots:
            kept_ref, got_ref = refs[2 * n : 2 * n + 2]
            for m in range(counts[n]):
                total = kept_ref[m] + decode(got_ref[m, :BLK], got_ref[m, BLK:])
                out_ref[row : row + BLK] = start[row : row + BLK] - total
                row += BLK

    first = where_ref[0] // 2 == where_ref[7]

    @pl.when(first)
    def _():
        fill([0])

    @pl.when(jnp.logical_not(first))
    def _():
        fill(range(1, len(counts)))


def combine(where, anc, pairs, share):
    parts = [part for pair in pairs for part in pair]
    cols = anc.shape[1]
    return pl.pallas_call(
        functools.partial(combine_kernel, [kept.shape[0] for kept, _ in pairs]),
        out_shape=jax.ShapeDtypeStruct((share, cols), jnp.float32),
        in_specs=[SMEM, ANY] + [VMEM] * len(parts),
        out_specs=VMEM,
        scratch_shapes=[pltpu.VMEM((share, cols), jnp.float32), pltpu.SemaphoreType.DMA],
        compiler_params=params(),
        cost_estimate=cost(0),
        name="combine",
    )(where, anc, *parts)


def pivot_kernel(where_ref, anc_ref, one_ref, two_ref, out_ref, blocks, sems):
    count = out_ref.shape[0]
    copies = []
    for q in range(count):
        rows = pl.ds(pl.multiple_of(where_ref[4] + q * BLK, BLK), BLK)
        copies.append(
            pltpu.make_async_copy(
                anc_ref.at[rows, q * BLK : (q + 1) * BLK], blocks.at[q], sems.at[q]
            )
        )
    for copy in copies:
        copy.start()
    total = decode(one_ref[:BLK], one_ref[BLK:]) + decode(two_ref[:BLK], two_ref[BLK:])
    for copy in copies:
        copy.wait()
    for q in range(count):
        out_ref[q] = blocks[q] - total[:, q * BLK : (q + 1) * BLK]


def pivots(where, anc, one, two):
    count = one.shape[1] // BLK
    return pl.pallas_call(
        pivot_kernel,
        out_shape=jax.ShapeDtypeStruct((count, BLK, BLK), jnp.float32),
        in_specs=[SMEM, ANY, VMEM, VMEM],
        out_specs=VMEM,
        scratch_shapes=[
            pltpu.VMEM((count, BLK, BLK), jnp.float32),
            pltpu.SemaphoreType.DMA((count,)),
        ],
        compiler_params=params(),
        cost_estimate=cost(0),
        name="pivots",
    )(where, anc, one, two)


def xor_perm(size, bit):
    return [(i, i ^ bit) for i in range(size)]


def after(value, *others):
    return lax.optimization_barrier((value, *others))[0]


def planned(lpanel, upanel, lpat, upat, anc):
    layers, rows, cols = (lax.axis_size(n) for n in ("layer", "row", "col"))
    layer, row, col = (lax.axis_index(n) for n in ("layer", "row", "col"))
    width = anc.shape[1]
    share = anc.shape[0] // layers
    blocks = share // BLK
    per_group = cols // rows
    owner, side = col // per_group, col % per_group
    first = jnp.where(owner == row, side, 1 - side)
    where = jnp.stack(
        [layer, row, col, owner, side * width, side * (width // share), side, first]
    ).astype(jnp.int32)
    everyone = ("layer", "row", "col")
    spots = [(l, r, c) for l in range(layers) for r in range(rows) for c in range(cols)]

    def index(l, r, c):
        return (l * rows + r) * cols + c

    def holders(value, target):
        perm = [(index(*p), index(*target(*p))) for p in spots if p[1] == p[2] // per_group]
        return lax.ppermute(value, everyone, perm)

    def near_layers(value):
        return lax.ppermute(value, "layer", xor_perm(layers, 1))

    def far_layers(value, phase):
        perm = []
        for l, r, c in spots:
            half = c % per_group if r == c // per_group else 1 - c % per_group
            if phase == 1:
                half = 1 - half
            if l // 2 != half:
                perm.append((index(l, r, c), index(l ^ 2, r, c)))
        return lax.ppermute(value, everyone, perm)

    def over(value, bit):
        return lax.ppermute(value, "col", xor_perm(cols, bit))

    lt = jnp.swapaxes(lpanel[0], 1, 2)
    u = upanel[0]
    a, b = halves(lt)
    xa, yb = over(a, 1), over(b, 2)
    uo = lax.ppermute(u, "row", xor_perm(rows, 1))
    near_right, far_right = masked_right(where, upat[0], u, uo)
    whole = (a, xa, b, yb)
    chunks = [(0, 0, blocks), (1, 0, blocks - 1), (1, blocks - 1, 1)]
    sides, others = [], []

    def send_rows(chunk, *waits):
        if sides:
            waits += tuple(sides[-1])
        ready = (after(a, *waits) if waits else a, xa, b, yb)
        sides.append(split(where, ready, chunk, blocks))
        others.append((over(sides[-1][0], 2), over(sides[-1][1], 1)))

    send_rows(chunks[0])
    send_rows(chunks[1])
    masks = lpat[0]
    parts = [near_update(where, masks, whole, near_right, chunk, blocks) for chunk in chunks]

    def far_part(j, *waits):
        return far_update(
            where, masks, others[j], far_right, after(parts[j], *waits), chunks[j], blocks
        )

    kept0, coded0, diag = far_part(0)
    near = add_coded(diag, holders(diag, lambda l, r, c: (l ^ 1, r, c)))
    far = holders(near, lambda l, r, c: (l ^ 2, r, c))
    send_rows(chunks[2], near)
    own = pivots(where, anc, near, far)
    other = holders(own, lambda l, r, c: (l, 1 - r, c))
    kept1, coded1 = far_part(1, near)
    kept2, coded2 = far_part(2, own)
    sum0, sent0 = halve(kept0, near_layers(coded0))
    half_lu = factor(where, after(own, sent0, coded2), other, HALF_STEPS)
    sum1, sent1 = halve(after(kept1, half_lu), near_layers(coded1))
    diag_lu = factor_rest(after(half_lu, sent1), HALF_STEPS)
    sum2, sent2 = halve(after(kept2, half_lu), near_layers(coded2))
    pairs = [
        (sum0, far_layers(sent0, 0)),
        (sum1, far_layers(sent1, 1)),
        (after(sum2, diag_lu), far_layers(sent2, 1)),
    ]
    return combine(where, anc, pairs, share), diag_lu


def mask_rows(panel, pattern, block):
    count, length, inner = panel.shape
    shaped = panel.reshape(count, length // block, block, inner)
    return (shaped * pattern[:, :, None, None].astype(panel.dtype)).reshape(count, length, inner)


def mask_cols(panel, pattern, block):
    count, inner, length = panel.shape
    shaped = panel.reshape(count, inner, length // block, block)
    return (shaped * pattern[:, None, :, None].astype(panel.dtype)).reshape(count, inner, length)


def candidates(matrix):
    width = matrix.shape[1]
    per_group = lax.axis_size("col") // lax.axis_size("row")
    begin = lax.axis_index("col") % per_group * width
    square = lax.dynamic_slice_in_dim(matrix, begin, width, 0)
    count = width // BLK
    return jnp.stack(
        [square[j * BLK : (j + 1) * BLK, j * BLK : (j + 1) * BLK] for j in range(count)]
    )


def gathered(lpanel, upanel, lpat, upat, anc):
    left = mask_rows(lpanel[0], lpat[0], BLK)
    right = mask_cols(upanel[0], upat[0], BLK)
    update = jnp.einsum(
        "kmw,kwn->mn",
        lax.all_gather(left, "col", axis=2, tiled=True),
        lax.all_gather(right, "row", axis=1, tiled=True),
        preferred_element_type=jnp.float32,
    )
    rows = lax.axis_size("row")
    per_group = lax.axis_size("col") // rows
    share = anc.shape[0] // lax.axis_size("layer")
    pivot_blocks = candidates(anc) - lax.psum(candidates(update), "layer")
    both = lax.all_gather(pivot_blocks, "row", axis=0)
    chosen = lax.dynamic_index_in_dim(both, lax.axis_index("col") // per_group, 0, keepdims=False)
    where = jnp.zeros((6,), jnp.int32)
    diag_lu = factor(where, chosen, chosen, BLK)
    summed = lax.psum_scatter(update, "layer", scatter_dimension=0, tiled=True)
    mine = lax.dynamic_slice_in_dim(anc, lax.axis_index("layer") * share, share, 0)
    return mine - summed, diag_lu


def shards(lpanel, upanel, lpat, upat, anc):
    layers, rows, cols = (lax.axis_size(n) for n in ("layer", "row", "col"))
    fits = rows == 2 and cols == 4 and layers == 4
    share, extra = divmod(anc.shape[0], layers * BLK)
    square = anc.shape[1] == 2 * share * BLK
    if fits and square and extra == 0 and share > 1 and lpanel.shape[1] % 2 == 0:
        return planned(lpanel, upanel, lpat, upat, anc)
    return gathered(lpanel, upanel, lpat, upat, anc)


def solution(mesh):
    return jax.shard_map(
        shards,
        mesh=mesh,
        in_specs=(
            P("layer", None, "row", "col"),
            P("layer", None, "row", "col"),
            P("layer", None, "row"),
            P("layer", None, "col"),
            P("row", "col"),
        ),
        out_specs=(P(("row", "layer"), "col"), P("col", None, None)),
        check_vma=False,
    )
```

time: 119 us -> 116 us (0.975)
  the two profiles are of different devices: /device:TPU:2 before, /device:TPU:0 now
where the time goes in v6:
time: 116 us
  waiting for transfers between devices  44.8 us (39%)
  Pallas kernels  34.5 us (30%)
  starting transfers between devices  34.1 us (29%)
  local copies, waits for them, and re-layouts  1.6 us (1%)
    ppermute x8, waiting for transfers between devices, over(): return lax.ppermute(value, 'col', xor_perm(cols, bit))  30.6 us
    ppermute x8, starting transfers between devices, over(): return lax.ppermute(value, 'col', xor_perm(cols, bit))  9.62 us
    ppermute x3, starting transfers between devices, holders(): return lax.ppermute(value, everyone, perm)  9.59 us
    ppermute x3, waiting for transfers between devices, far_layers(): return lax.ppermute(value, everyone, perm)  8.72 us
    pallas_call x1, Pallas kernels, factor_rest(): pl.pallas_call(functools.partial(rest_kernel, begin), out_shape=jax.Shape...  8.67 us
    ppermute x3, starting transfers between devices, far_layers(): return lax.ppermute(value, everyone, perm)  8.11 us
    pallas_call x3, Pallas kernels, far_update(): pl.pallas_call(functools.partial(far_kernel, chunk, blocks), out_shape=sh...  6.37 us
    ppermute x3, starting transfers between devices, near_layers(): return lax.ppermute(value, 'layer', xor_perm(layers, 1))  6.25 us
  transfers between devices with their start and end apart: 18, of which 7 were waited for; matrix products, arithmetic and copies ran while one was open for 0% of the time, Pallas kernels for 28%

profile of v6, /device:TPU:0, one launch (start us, length us, event | category | flops | bytes accessed | tf_op | source)
XLA Modules:
  0.0 116.0 jit_solution(17579009654171576501)
XLA Ops:
  0.6 0.5 collective-permute-start.4
  1.2 1.4 %copy-done = bf16[1,8,1536,64]{2,3,1,0:T(8,128)(2,1)S(1)} copy-done((bf16[1,8,1536,64]{2,3,1,0:T(8,128)(2,1)S(1)}, bf16[1,8,1536,64]{2,3,1,0:T(8,128)(2,1)}, u32[]{:S(2)}) %copy-start) | copy-done | bytes 1572888
  2.6 0.1 halves.1
  2.7 2.6 %collective-permute-start = (bf16[4,64,1536]{2,1,0:T(8,128)(2,1)S(1)}, bf16[4,64,1536]{2,1,0:T(8,128)(2,1)S(1)}, u32[]{:S(2)}, u32[]{:S(2)}) collective-permute-start(bf16[4,64,1536]{2,1,0:T(8,128)(2,1)S(1)} %get-tuple-element.50.refs_0_), channel_id=1, source_target_pairs={{0,1},{1,0},{2,3},{3,2},{4,5},{5,4},{6,7},{7,6},{8,9},{9,8},{10,11... | collective-permute-start | bytes 2359304 | tf_op jit(solution)/shard_map/ppermute | solution.py:480
  5.3 1.5 %collective-permute-start.1 = (bf16[4,64,1536]{2,1,0:T(8,128)(2,1)S(1)}, bf16[4,64,1536]{2,1,0:T(8,128)(2,1)S(1)}, u32[]{:S(2)}, u32[]{:S(2)}) collective-permute-start(bf16[4,64,1536]{2,1,0:T(8,128)(2,1)S(1)} %get-tuple-element.35.refs_2_), channel_id=1, source_target_pairs={{0,2},{1,3},{2,0},{3,1},{4,6},{5,7},{6,4},{7,5},{8,10},{9,11},{10,... | collective-permute-start | bytes 2359304 | tf_op jit(solution)/shard_map/ppermute | solution.py:480
  6.8 0.1 copy.7
  6.9 0.1 stack.35.where_ref
  7.0 16.5 %collective-permute-done.refs_1_ = bf16[4,64,1536]{2,1,0:T(8,128)(2,1)S(1)} collective-permute-done((bf16[4,64,1536]{2,1,0:T(8,128)(2,1)S(1)}, bf16[4,64,1536]{2,1,0:T(8,128)(2,1)S(1)}, u32[]{:S(2)}, u32[]{:S(2)}) %collective-permute-start) | collective-permute-done | bytes 786464 | tf_op jit(solution)/shard_map/ppermute | solution.py:480
  23.5 1.5 %collective-permute-done.1.refs_3_ = bf16[4,64,1536]{2,1,0:T(8,128)(2,1)S(1)} collective-permute-done((bf16[4,64,1536]{2,1,0:T(8,128)(2,1)S(1)}, bf16[4,64,1536]{2,1,0:T(8,128)(2,1)S(1)}, u32[]{:S(2)}, u32[]{:S(2)}) %collective-permute-start.1) | collective-permute-done | bytes 786464 | tf_op jit(solution)/shard_map/ppermute | solution.py:480
  24.9 0.8 split.3
  25.7 1.6 %collective-permute-start.2 = (bf16[2,4,64,768]{3,2,1,0:T(8,128)(2,1)S(1)}, bf16[2,4,64,768]{3,2,1,0:T(8,128)(2,1)S(1)}, u32[]{:S(2)}, u32[]{:S(2)}) collective-permute-start(bf16[2,4,64,768]{3,2,1,0:T(8,128)(2,1)S(1)} %get-tuple-element.36), channel_id=1, source_target_pairs={{0,2},{1,3},{2,0},{3,1},{4,6},{5,7},{6,4},{7,5},{8,10},{9,11},{10,... | collective-permute-start | bytes 2359304 | tf_op jit(solution)/shard_map/ppermute | solution.py:480
  27.3 0.5 collective-permute-start.3
  27.9 0.7 split.4
  28.6 0.4 collective-permute-start.7
  29.0 1.7 %collective-permute-start.8 = (bf16[2,4,64,512]{3,2,1,0:T(8,128)(2,1)S(1)}, bf16[2,4,64,512]{3,2,1,0:T(8,128)(2,1)S(1)}, u32[]{:S(2)}, u32[]{:S(2)}) collective-permute-start(bf16[2,4,64,512]{3,2,1,0:T(8,128)(2,1)S(1)} %get-tuple-element.46), channel_id=1, source_target_pairs={{0,1},{1,0},{2,3},{3,2},{4,5},{5,4},{6,7},{7,6},{8,9},{9,8},{10,11... | collective-permute-start | bytes 1572872 | tf_op jit(solution)/shard_map/ppermute | solution.py:480
  30.7 2.2 %masked_right.1 = (bf16[8,128,768]{2,1,0:T(8,128)(2,1)S(1)}, bf16[8,128,768]{2,1,0:T(8,128)(2,1)S(1)}) custom-call(s32[8]{0:T(128)S(1)} %stack.35.where_ref, s32[8,6]{1,0:T(8,128)S(1)} %bitcast.19, bf16[8,128,768]{2,1,0:T(8,128)(2,1)S(1)} %bitcast.18, bf16[8,128,768]{2,1,0:T(8,128)(2,1)} %collective-permute-done.4.uo_ref), custom_call_target="tpu_custom_call" | custom-call | flops 1000 | bytes 1000 | tf_op jit(solution)/shard_map/masked_right/pallas_call | solution.py:212
  32.9 2.3 %near_update.3.before_ref = f32[6,128,768]{2,1,0:T(8,128)S(1)} custom-call(s32[8]{0:T(128)S(1)} %stack.35.where_ref, s32[8,12]{1,0:T(8,128)S(1)} %bitcast.20, bf16[4,64,1536]{2,1,0:T(8,128)(2,1)S(1)} %get-tuple-element.50.refs_0_, bf16[4,64,1536]{2,1,0:T(8,128)(2,1)S(1)} %collective-permute-done.refs_1_, bf16[4,64,1536]{2,1,0:T(8,128)(2,1)S(1)} %get-tuple-element.35.refs_2_, ...), custom_call_target="tpu_custom_call" | custom-call | flops 10000001024 | bytes 1000 | tf_op jit(solution)/shard_map/near_update/pallas_call | solution.py:261
  35.2 11.1 %collective-permute-done.2.a_ref = bf16[2,4,64,768]{3,2,1,0:T(8,128)(2,1)S(1)} collective-permute-done((bf16[2,4,64,768]{3,2,1,0:T(8,128)(2,1)S(1)}, bf16[2,4,64,768]{3,2,1,0:T(8,128)(2,1)S(1)}, u32[]{:S(2)}, u32[]{:S(2)}) %collective-permute-start.2) | collective-permute-done | bytes 786464 | tf_op jit(solution)/shard_map/ppermute | solution.py:480
  46.3 1.5 %collective-permute-done.3.b_ref = bf16[2,4,64,768]{3,2,1,0:T(8,128)(2,1)S(1)} collective-permute-done((bf16[2,4,64,768]{3,2,1,0:T(8,128)(2,1)S(1)}, bf16[2,4,64,768]{3,2,1,0:T(8,128)(2,1)S(1)}, u32[]{:S(2)}, u32[]{:S(2)}) %collective-permute-start.3) | collective-permute-done | bytes 786464 | tf_op jit(solution)/shard_map/ppermute | solution.py:480
  47.8 2.7 %far_update.3 = (f32[3,128,768]{2,1,0:T(8,128)S(1)}, s16[3,144,768]{2,1,0:T(8,128)(2,1)S(1)}, s16[144,768]{1,0:T(8,128)(2,1)S(1)}) custom-call(s32[8]{0:T(128)S(1)} %stack.35.where_ref, s32[8,12]{1,0:T(8,128)S(1)} %bitcast.21, bf16[2,4,64,768]{3,2,1,0:T(8,128)(2,1)S(1)} %collective-permute-done.2.a_ref, ...), custom_call_target="tpu_custom_call" | custom-call | flops 4000001024 | bytes 1000 | tf_op jit(solution)/shard_map/far_update/pallas_call | solution.py:303
  50.5 3.5 %collective-permute-start.9 = (s16[144,768]{1,0:T(8,128)(2,1)S(1)}, s16[144,768]{1,0:T(8,128)(2,1)S(1)}, u32[]{:S(2)}, u32[]{:S(2)}) collective-permute-start(s16[144,768]{1,0:T(8,128)(2,1)S(1)} %get-tuple-element.47.mine_ref), channel_id=1, source_target_pairs={{0,8},{1,9},{6,14},{7,15},{8,0},{9,1},{14,6},{15,7},{16,24},{17,25... | collective-permute-start | bytes 663560 | tf_op jit(solution)/shard_map/ppermute | solution.py:464
  54.0 0.5 collective-permute-start.5
  54.5 1.3 %near_update.5.before_ref = f32[2,128,768]{2,1,0:T(8,128)S(1)} custom-call(s32[8]{0:T(128)S(1)} %stack.35.where_ref, s32[8,12]{1,0:T(8,128)S(1)} %bitcast.22, bf16[4,64,1536]{2,1,0:T(8,128)(2,1)S(1)} %get-tuple-element.50.refs_0_, bf16[4,64,1536]{2,1,0:T(8,128)(2,1)S(1)} %collective-permute-done.refs_1_, bf16[4,64,1536]{2,1,0:T(8,128)(2,1)S(1)} %get-tuple-element.35.refs_2_, ...), custom_call_target="tpu_custom_call" | custom-call | flops 10000001024 | bytes 1000 | tf_op jit(solution)/shard_map/near_update/pallas_call | solution.py:261
  55.8 3.8 %collective-permute-done.9.got_ref = s16[144,768]{1,0:T(8,128)(2,1)S(1)} collective-permute-done((s16[144,768]{1,0:T(8,128)(2,1)S(1)}, s16[144,768]{1,0:T(8,128)(2,1)S(1)}, u32[]{:S(2)}, u32[]{:S(2)}) %collective-permute-start.9) | collective-permute-done | bytes 221216 | tf_op jit(solution)/shard_map/ppermute | solution.py:464
  59.6 0.2 add_coded.1.one_ref
  59.8 0.0 slice-start.1
  59.8 4.8 %collective-permute-start.10 = (s16[144,768]{1,0:T(8,128)(2,1)S(1)}, s16[144,768]{1,0:T(8,128)(2,1)S(1)}, u32[]{:S(2)}, u32[]{:S(2)}) collective-permute-start(s16[144,768]{1,0:T(8,128)(2,1)S(1)} %add_coded.1.one_ref), channel_id=1, source_target_pairs={{0,16},{1,17},{6,22},{7,23},{8,24},{9,25},{14,30},{15,31},{16,0},{... | collective-permute-start | bytes 663560 | tf_op jit(solution)/shard_map/ppermute | solution.py:464
  64.5 1.8 %near_update.4.before_ref = f32[4,128,768]{2,1,0:T(8,128)S(1)} custom-call(s32[8]{0:T(128)S(1)} %stack.35.where_ref, s32[8,12]{1,0:T(8,128)S(1)} %bitcast.23, bf16[4,64,1536]{2,1,0:T(8,128)(2,1)S(1)} %get-tuple-element.50.refs_0_, bf16[4,64,1536]{2,1,0:T(8,128)(2,1)S(1)} %collective-permute-done.refs_1_, bf16[4,64,1536]{2,1,0:T(8,128)(2,1)S(1)} %get-tuple-element.35.refs_2_, ...), custom_call_target="tpu_custom_call" | custom-call | flops 10000001024 | bytes 1000 | tf_op jit(solution)/shard_map/near_update/pallas_call | solution.py:261
  66.4 0.7 split.5
  67.1 0.1 collective-permute-start.11
  67.2 1.7 %collective-permute-done.10.two_ref = s16[144,768]{1,0:T(8,128)(2,1)S(1)} collective-permute-done((s16[144,768]{1,0:T(8,128)(2,1)S(1)}, s16[144,768]{1,0:T(8,128)(2,1)S(1)}, u32[]{:S(2)}, u32[]{:S(2)}) %collective-permute-start.10) | collective-permute-done | bytes 221216 | tf_op jit(solution)/shard_map/ppermute | solution.py:464
  68.9 1.3 %collective-permute-start.12 = (bf16[2,4,64,256]{3,2,1,0:T(8,128)(2,1)S(1)}, bf16[2,4,64,256]{3,2,1,0:T(8,128)(2,1)S(1)}, u32[]{:S(2)}, u32[]{:S(2)}) collective-permute-start(bf16[2,4,64,256]{3,2,1,0:T(8,128)(2,1)S(1)} %get-tuple-element.52), channel_id=1, source_target_pairs={{0,1},{1,0},{2,3},{3,2},{4,5},{5,4},{6,7},{7,6},{8,9},{9,8},{10,11... | collective-permute-start | bytes 786440 | tf_op jit(solution)/shard_map/ppermute | solution.py:480
  70.2 0.9 pivots.1.own_ref
  71.0 1.3 %collective-permute-start.13 = (f32[6,128,128]{2,1,0:T(8,128)S(1)}, f32[6,128,128]{2,1,0:T(8,128)S(1)}, u32[]{:S(2)}, u32[]{:S(2)}) collective-permute-start(f32[6,128,128]{2,1,0:T(8,128)S(1)} %pivots.1.own_ref), channel_id=1, source_target_pairs={{0,4},{1,5},{6,2},{7,3},{8,12},{9,13},{14,10},{15,11},{16,20},{17,... | collective-permute-start | bytes 1179656 | tf_op jit(solution)/shard_map/ppermute | solution.py:464
  72.4 2.2 %far_update.4 = (f32[2,128,768]{2,1,0:T(8,128)S(1)}, s16[2,144,768]{2,1,0:T(8,128)(2,1)S(1)}) custom-call(s32[8]{0:T(128)S(1)} %stack.35.where_ref, s32[8,12]{1,0:T(8,128)S(1)} %bitcast.24, bf16[2,4,64,512]{3,2,1,0:T(8,128)(2,1)S(1)} %collective-permute-done.7.a_ref, bf16[2,4,64,512]{3,2,1,0:T(8,128)(2,1)S(1)} %collective-permute-done.8.b_ref, ...), custom_call_target="tpu_custom_call" | custom-call | flops 4000001024 | bytes 1000 | tf_op jit(solution)/shard_map/far_update/pallas_call | solution.py:303
  74.5 4.0 %collective-permute-start.14 = (s16[2,144,768]{2,1,0:T(8,128)(2,1)S(1)}, s16[2,144,768]{2,1,0:T(8,128)(2,1)S(1)}, u32[]{:S(2)}, u32[]{:S(2)}) collective-permute-start(s16[2,144,768]{2,1,0:T(8,128)(2,1)S(1)} %get-tuple-element.57), channel_id=1, source_target_pairs={{0,8},{8,0},{16,24},{24,16},{1,9},{9,1},{17,25},{25,17},{2,10},{10... | collective-permute-start | bytes 1327112 | tf_op jit(solution)/shard_map/ppermute | solution.py:467
  78.6 1.5 %far_update.5 = (f32[1,128,768]{2,1,0:T(8,128)S(1)}, s16[1,144,768]{2,1,0:T(8,128)(2,1)S(1)}) custom-call(s32[8]{0:T(128)S(1)} %stack.35.where_ref, s32[8,12]{1,0:T(8,128)S(1)} %bitcast.25, bf16[2,4,64,256]{3,2,1,0:T(8,128)(2,1)S(1)} %collective-permute-done.11.a_ref, bf16[2,4,64,256]{3,2,1,0:T(8,128)(2,1)S(1)} %collective-permute-done.12.b_ref, ...), custom_call_target="tpu_custom_call" | custom-call | flops 4000001024 | bytes 1000 | tf_op jit(solution)/shard_map/far_update/pallas_call | solution.py:303
  80.1 1.7 %collective-permute-start.16 = (s16[1,144,768]{2,1,0:T(8,128)(2,1)S(1)}, s16[1,144,768]{2,1,0:T(8,128)(2,1)S(1)}, u32[]{:S(2)}, u32[]{:S(2)}) collective-permute-start(s16[1,144,768]{2,1,0:T(8,128)(2,1)S(1)} %get-tuple-element.54), channel_id=1, source_target_pairs={{0,8},{8,0},{16,24},{24,16},{1,9},{9,1},{17,25},{25,17},{2,10},{10... | collective-permute-start | bytes 663560 | tf_op jit(solution)/shard_map/ppermute | solution.py:467
  81.8 0.4 halve.3
  82.2 1.3 %collective-permute-start.6 = (s16[3,144,768]{2,1,0:T(8,128)(2,1)S(1)}, s16[3,144,768]{2,1,0:T(8,128)(2,1)S(1)}, u32[]{:S(2)}, u32[]{:S(2)}) collective-permute-start(s16[3,144,768]{2,1,0:T(8,128)(2,1)S(1)} %get-tuple-element.43), channel_id=1, source_target_pairs={{1,17},{2,18},{4,20},{7,23},{9,25},{10,26},{12,28},{15,31},{16,0},... | collective-permute-start | bytes 1990664 | tf_op jit(solution)/shard_map/ppermute | solution.py:477
  83.5 5.6 %factor.1.in_ref = f32[6,128,128]{2,1,0:T(8,128)S(1)} custom-call(s32[8]{0:T(128)S(1)} %stack.35.where_ref, f32[6,128,128]{2,1,0:T(8,128)S(1)} %pivots.1.own_ref, f32[6,128,128]{2,1,0:T(8,128)S(1)} %collective-permute-done.13.other_ref), custom_call_target="tpu_custom_call" | custom-call | flops 10000001024 | bytes 1000 | tf_op jit(solution)/shard_map/factor/pallas_call | solution.py:83
  89.1 0.3 halve.4
  89.4 5.5 %collective-permute-start.15 = (s16[2,144,768]{2,1,0:T(8,128)(2,1)S(1)}, s16[2,144,768]{2,1,0:T(8,128)(2,1)S(1)}, u32[]{:S(2)}, u32[]{:S(2)}) collective-permute-start(s16[2,144,768]{2,1,0:T(8,128)(2,1)S(1)} %get-tuple-element.59), channel_id=1, source_target_pairs={{0,16},{3,19},{5,21},{6,22},{8,24},{11,27},{13,29},{14,30},{17,1},... | collective-permute-start | bytes 1327112 | tf_op jit(solution)/shard_map/ppermute | solution.py:477
  94.9 0.1 halve.5
  95.1 1.3 %collective-permute-start.17 = (s16[1,144,768]{2,1,0:T(8,128)(2,1)S(1)}, s16[1,144,768]{2,1,0:T(8,128)(2,1)S(1)}, u32[]{:S(2)}, u32[]{:S(2)}) collective-permute-start(s16[1,144,768]{2,1,0:T(8,128)(2,1)S(1)} %get-tuple-element.65), channel_id=1, source_target_pairs={{0,16},{3,19},{5,21},{6,22},{8,24},{11,27},{13,29},{14,30},{17,1},... | collective-permute-start | bytes 663560 | tf_op jit(solution)/shard_map/ppermute | solution.py:477
  96.4 8.7 %factor_rest.1 = f32[6,128,128]{2,1,0:T(8,128)} custom-call(f32[6,128,128]{2,1,0:T(8,128)S(1)} %factor.1.in_ref), custom_call_target="tpu_custom_call" | custom-call | flops 10000001024 | bytes 1000 | tf_op jit(solution)/shard_map/factor_rest/pallas_call | solution.py:101
  105.0 8.7 %collective-permute-done.6.refs_1_ = s16[3,144,768]{2,1,0:T(8,128)(2,1)S(1)} collective-permute-done((s16[3,144,768]{2,1,0:T(8,128)(2,1)S(1)}, s16[3,144,768]{2,1,0:T(8,128)(2,1)S(1)}, u32[]{:S(2)}, u32[]{:S(2)}) %collective-permute-start.6) | collective-permute-done | bytes 663584 | tf_op jit(solution)/shard_map/ppermute | solution.py:477
  113.8 2.0 %combine.1 = f32[384,768]{1,0:T(8,128)} custom-call(s32[8]{0:T(128)S(1)} %stack.35.where_ref, f32[1536,768]{1,0:T(8,128)S(1)} %bitcast.15, f32[3,128,768]{2,1,0:T(8,128)S(1)} %get-tuple-element.42.refs_0_, s16[3,144,768]{2,1,0:T(8,128)(2,1)S(1)} %collective-permute-done.6.refs_1_, f32[2,128,768]{2,1,0:T(8,128)S(1)} %get-tuple-element.58.refs_2_, ...), custom_call_target="tpu_custom_call" | custom-call | flops 1000 | bytes 1000 | tf_op jit(solution)/shard_map/combine/pallas_call | solution.py:388
  (22 shorter events, 0.0 us)
Async XLA Ops:
  0.6 6.2 %copy-start.3 = (s32[1,8,6]{1,0,2:T(1,128)S(1)}, s32[1,8,6]{1,0,2:T(1,128)}, u32[]{:S(2)}) copy-start(s32[1,8,6]{1,0,2:T(1,128)} %param.8) | copy-start | bytes 580
  0.6 30.0 %collective-permute-start.4 = (bf16[8,128,768]{2,1,0:T(8,128)(2,1)}, bf16[8,128,768]{2,1,0:T(8,128)(2,1)}, u32[]{:S(2)}, u32[]{:S(2)}) collective-permute-start(bf16[8,128,768]{2,1,0:T(8,128)(2,1)} %bitcast.17), channel_id=1, source_target_pairs={{0,4},{4,0},{1,5},{5,1},{2,6},{6,2},{3,7},{7,3},{8,12},{12,8},{9,1... | collective-permute-start | bytes 4718600 | tf_op jit(solution)/shard_map/ppermute | solution.py:486
  1.2 1.4 %copy-start = (bf16[1,8,1536,64]{2,3,1,0:T(8,128)(2,1)S(1)}, bf16[1,8,1536,64]{2,3,1,0:T(8,128)(2,1)}, u32[]{:S(2)}) copy-start(bf16[1,8,1536,64]{2,3,1,0:T(8,128)(2,1)} %param.5) | copy-start | bytes 4718596
  2.7 20.8 %collective-permute-start = (bf16[4,64,1536]{2,1,0:T(8,128)(2,1)S(1)}, bf16[4,64,1536]{2,1,0:T(8,128)(2,1)S(1)}, u32[]{:S(2)}, u32[]{:S(2)}) collective-permute-start(bf16[4,64,1536]{2,1,0:T(8,128)(2,1)S(1)} %get-tuple-element.50.refs_0_), channel_id=1, source_target_pairs={{0,1},{1,0},{2,3},{3,2},{4,5},{5,4},{6,7},{7,6},{8,9},{9,8},{10,11... | collective-permute-start | bytes 2359304 | tf_op jit(solution)/shard_map/ppermute | solution.py:480
  5.3 19.7 %collective-permute-start.1 = (bf16[4,64,1536]{2,1,0:T(8,128)(2,1)S(1)}, bf16[4,64,1536]{2,1,0:T(8,128)(2,1)S(1)}, u32[]{:S(2)}, u32[]{:S(2)}) collective-permute-start(bf16[4,64,1536]{2,1,0:T(8,128)(2,1)S(1)} %get-tuple-element.35.refs_2_), channel_id=1, source_target_pairs={{0,2},{1,3},{2,0},{3,1},{4,6},{5,7},{6,4},{7,5},{8,10},{9,11},{10,... | collective-permute-start | bytes 2359304 | tf_op jit(solution)/shard_map/ppermute | solution.py:480
  25.7 20.5 %collective-permute-start.2 = (bf16[2,4,64,768]{3,2,1,0:T(8,128)(2,1)S(1)}, bf16[2,4,64,768]{3,2,1,0:T(8,128)(2,1)S(1)}, u32[]{:S(2)}, u32[]{:S(2)}) collective-permute-start(bf16[2,4,64,768]{3,2,1,0:T(8,128)(2,1)S(1)} %get-tuple-element.36), channel_id=1, source_target_pairs={{0,2},{1,3},{2,0},{3,1},{4,6},{5,7},{6,4},{7,5},{8,10},{9,11},{10,... | collective-permute-start | bytes 2359304 | tf_op jit(solution)/shard_map/ppermute | solution.py:480
  27.3 3.3 %copy-start.1 = (bf16[1,8,128,768]{3,2,1,0:T(8,128)(2,1)S(1)}, bf16[1,8,128,768]{3,2,1,0:T(8,128)(2,1)}, u32[]{:S(2)}) copy-start(bf16[1,8,128,768]{3,2,1,0:T(8,128)(2,1)} %param.6) | copy-start | bytes 4718596
  27.3 20.5 %collective-permute-start.3 = (bf16[2,4,64,768]{3,2,1,0:T(8,128)(2,1)S(1)}, bf16[2,4,64,768]{3,2,1,0:T(8,128)(2,1)S(1)}, u32[]{:S(2)}, u32[]{:S(2)}) collective-permute-start(bf16[2,4,64,768]{3,2,1,0:T(8,128)(2,1)S(1)} %get-tuple-element.37), channel_id=1, source_target_pairs={{0,1},{1,0},{2,3},{3,2},{4,5},{5,4},{6,7},{7,6},{8,9},{9,8},{10,11... | collective-permute-start | bytes 2359304 | tf_op jit(solution)/shard_map/ppermute | solution.py:480
  28.6 42.4 %collective-permute-start.7 = (bf16[2,4,64,512]{3,2,1,0:T(8,128)(2,1)S(1)}, bf16[2,4,64,512]{3,2,1,0:T(8,128)(2,1)S(1)}, u32[]{:S(2)}, u32[]{:S(2)}) collective-permute-start(bf16[2,4,64,512]{3,2,1,0:T(8,128)(2,1)S(1)} %get-tuple-element.45), channel_id=1, source_target_pairs={{0,2},{1,3},{2,0},{3,1},{4,6},{5,7},{6,4},{7,5},{8,10},{9,11},{10,... | collective-permute-start | bytes 1572872 | tf_op jit(solution)/shard_map/ppermute | solution.py:480
  29.0 43.4 %collective-permute-start.8 = (bf16[2,4,64,512]{3,2,1,0:T(8,128)(2,1)S(1)}, bf16[2,4,64,512]{3,2,1,0:T(8,128)(2,1)S(1)}, u32[]{:S(2)}, u32[]{:S(2)}) collective-permute-start(bf16[2,4,64,512]{3,2,1,0:T(8,128)(2,1)S(1)} %get-tuple-element.46), channel_id=1, source_target_pairs={{0,1},{1,0},{2,3},{3,2},{4,5},{5,4},{6,7},{7,6},{8,9},{9,8},{10,11... | collective-permute-start | bytes 1572872 | tf_op jit(solution)/shard_map/ppermute | solution.py:480
  30.7 2.2 %copy-start.2 = (s32[1,8,12]{2,1,0:T(8,128)S(1)}, s32[1,8,12]{2,1,0:T(8,128)}, u32[]{:S(2)}) copy-start(s32[1,8,12]{2,1,0:T(8,128)} %param.7) | copy-start | bytes 1156
  50.5 9.1 %collective-permute-start.9 = (s16[144,768]{1,0:T(8,128)(2,1)S(1)}, s16[144,768]{1,0:T(8,128)(2,1)S(1)}, u32[]{:S(2)}, u32[]{:S(2)}) collective-permute-start(s16[144,768]{1,0:T(8,128)(2,1)S(1)} %get-tuple-element.47.mine_ref), channel_id=1, source_target_pairs={{0,8},{1,9},{6,14},{7,15},{8,0},{9,1},{14,6},{15,7},{16,24},{17,25... | collective-permute-start | bytes 663560 | tf_op jit(solution)/shard_map/ppermute | solution.py:464
  54.0 27.8 %collective-permute-start.5 = (s16[3,144,768]{2,1,0:T(8,128)(2,1)S(1)}, s16[3,144,768]{2,1,0:T(8,128)(2,1)S(1)}, u32[]{:S(2)}, u32[]{:S(2)}) collective-permute-start(s16[3,144,768]{2,1,0:T(8,128)(2,1)S(1)} %get-tuple-element.41), channel_id=1, source_target_pairs={{0,8},{8,0},{16,24},{24,16},{1,9},{9,1},{17,25},{25,17},{2,10},{10... | collective-permute-start | bytes 1990664 | tf_op jit(solution)/shard_map/ppermute | solution.py:467
  59.6 10.6 %slice-start = ((s8[4718592]{0:T(1024)(128)(4,1)}), s8[4194304]{0:T(1024)(128)(4,1)S(1)}, s32[]{:S(2)}) async-start(s8[4718592]{0:T(1024)(128)(4,1)} %bitcast.14), calls=%async_computation | async-start | bytes 8388608
  59.8 10.4 %slice-start.1 = ((s8[4718592]{0:T(1024)(128)(4,1)}), s8[524288]{0:T(1024)(128)(4,1)S(1)}, s32[]{:S(2)}) async-start(s8[4718592]{0:T(1024)(128)(4,1)} %bitcast.14), calls=%async_computation.1 | async-start | bytes 1048576
  59.8 9.1 %collective-permute-start.10 = (s16[144,768]{1,0:T(8,128)(2,1)S(1)}, s16[144,768]{1,0:T(8,128)(2,1)S(1)}, u32[]{:S(2)}, u32[]{:S(2)}) collective-permute-start(s16[144,768]{1,0:T(8,128)(2,1)S(1)} %add_coded.1.one_ref), channel_id=1, source_target_pairs={{0,16},{1,17},{6,22},{7,23},{8,24},{9,25},{14,30},{15,31},{16,0},{... | collective-permute-start | bytes 663560 | tf_op jit(solution)/shard_map/ppermute | solution.py:464
  67.1 11.4 %collective-permute-start.11 = (bf16[2,4,64,256]{3,2,1,0:T(8,128)(2,1)S(1)}, bf16[2,4,64,256]{3,2,1,0:T(8,128)(2,1)S(1)}, u32[]{:S(2)}, u32[]{:S(2)}) collective-permute-start(bf16[2,4,64,256]{3,2,1,0:T(8,128)(2,1)S(1)} %get-tuple-element.51), channel_id=1, source_target_pairs={{0,2},{1,3},{2,0},{3,1},{4,6},{5,7},{6,4},{7,5},{8,10},{9,11},{10,... | collective-permute-start | bytes 786440 | tf_op jit(solution)/shard_map/ppermute | solution.py:480
  68.9 9.7 %collective-permute-start.12 = (bf16[2,4,64,256]{3,2,1,0:T(8,128)(2,1)S(1)}, bf16[2,4,64,256]{3,2,1,0:T(8,128)(2,1)S(1)}, u32[]{:S(2)}, u32[]{:S(2)}) collective-permute-start(bf16[2,4,64,256]{3,2,1,0:T(8,128)(2,1)S(1)} %get-tuple-element.52), channel_id=1, source_target_pairs={{0,1},{1,0},{2,3},{3,2},{4,5},{5,4},{6,7},{7,6},{8,9},{9,8},{10,11... | collective-permute-start | bytes 786440 | tf_op jit(solution)/shard_map/ppermute | solution.py:480
  71.0 12.5 %collective-permute-start.13 = (f32[6,128,128]{2,1,0:T(8,128)S(1)}, f32[6,128,128]{2,1,0:T(8,128)S(1)}, u32[]{:S(2)}, u32[]{:S(2)}) collective-permute-start(f32[6,128,128]{2,1,0:T(8,128)S(1)} %pivots.1.own_ref), channel_id=1, source_target_pairs={{0,4},{1,5},{6,2},{7,3},{8,12},{9,13},{14,10},{15,11},{16,20},{17,... | collective-permute-start | bytes 1179656 | tf_op jit(solution)/shard_map/ppermute | solution.py:464
  74.5 14.6 %collective-permute-start.14 = (s16[2,144,768]{2,1,0:T(8,128)(2,1)S(1)}, s16[2,144,768]{2,1,0:T(8,128)(2,1)S(1)}, u32[]{:S(2)}, u32[]{:S(2)}) collective-permute-start(s16[2,144,768]{2,1,0:T(8,128)(2,1)S(1)} %get-tuple-element.57), channel_id=1, source_target_pairs={{0,8},{8,0},{16,24},{24,16},{1,9},{9,1},{17,25},{25,17},{2,10},{10... | collective-permute-start | bytes 1327112 | tf_op jit(solution)/shard_map/ppermute | solution.py:467
  80.1 14.8 %collective-permute-start.16 = (s16[1,144,768]{2,1,0:T(8,128)(2,1)S(1)}, s16[1,144,768]{2,1,0:T(8,128)(2,1)S(1)}, u32[]{:S(2)}, u32[]{:S(2)}) collective-permute-start(s16[1,144,768]{2,1,0:T(8,128)(2,1)S(1)} %get-tuple-element.54), channel_id=1, source_target_pairs={{0,8},{8,0},{16,24},{24,16},{1,9},{9,1},{17,25},{25,17},{2,10},{10... | collective-permute-start | bytes 663560 | tf_op jit(solution)/shard_map/ppermute | solution.py:467
  82.2 31.5 %collective-permute-start.6 = (s16[3,144,768]{2,1,0:T(8,128)(2,1)S(1)}, s16[3,144,768]{2,1,0:T(8,128)(2,1)S(1)}, u32[]{:S(2)}, u32[]{:S(2)}) collective-permute-start(s16[3,144,768]{2,1,0:T(8,128)(2,1)S(1)} %get-tuple-element.43), channel_id=1, source_target_pairs={{1,17},{2,18},{4,20},{7,23},{9,25},{10,26},{12,28},{15,31},{16,0},... | collective-permute-start | bytes 1990664 | tf_op jit(solution)/shard_map/ppermute | solution.py:477
  89.4 15.7 %collective-permute-start.15 = (s16[2,144,768]{2,1,0:T(8,128)(2,1)S(1)}, s16[2,144,768]{2,1,0:T(8,128)(2,1)S(1)}, u32[]{:S(2)}, u32[]{:S(2)}) collective-permute-start(s16[2,144,768]{2,1,0:T(8,128)(2,1)S(1)} %get-tuple-element.59), channel_id=1, source_target_pairs={{0,16},{3,19},{5,21},{6,22},{8,24},{11,27},{13,29},{14,30},{17,1},... | collective-permute-start | bytes 1327112 | tf_op jit(solution)/shard_map/ppermute | solution.py:477
  95.1 10.0 %collective-permute-start.17 = (s16[1,144,768]{2,1,0:T(8,128)(2,1)S(1)}, s16[1,144,768]{2,1,0:T(8,128)(2,1)S(1)}, u32[]{:S(2)}, u32[]{:S(2)}) collective-permute-start(s16[1,144,768]{2,1,0:T(8,128)(2,1)S(1)} %get-tuple-element.65), channel_id=1, source_target_pairs={{0,16},{3,19},{5,21},{6,22},{8,24},{11,27},{13,29},{14,30},{17,1},... | collective-permute-start | bytes 663560 | tf_op jit(solution)/shard_map/ppermute | solution.py:477

commit v7 on v6

--- a/solution.py
+++ b/solution.py
@@ -17,7 +17,7 @@
 EXP_ROWS = 16
 HALF_STEPS = 48
 NEAR = 10
-FAR = 4
+FAR = 10
 
 
 def cost(micros):
@@ -30,19 +30,26 @@
     return pltpu.CompilerParams(vmem_limit_bytes=VMEM_LIMIT, **kwargs)
 
 
-def encode(block):
+def levels_of(block):
     top = jnp.max(jnp.abs(block), axis=0, keepdims=True)
-    level = jnp.ceil(jnp.log2(jnp.maximum(top, 1e-30)) * EXP_STEPS) + 1.0
-    codes = jnp.round(block * (CODE_TOP * jnp.exp2(level * (-1.0 / EXP_STEPS))))
-    return codes.astype(jnp.int32).astype(jnp.int16), jnp.broadcast_to(
-        level.astype(jnp.int32), (EXP_ROWS, block.shape[1])
-    ).astype(jnp.int16)
-
-
-def decode(codes, levels):
-    level = levels.astype(jnp.int32).astype(jnp.float32)[:1]
-    scale = jnp.exp2(level * (1.0 / EXP_STEPS)) * (1.0 / CODE_TOP)
-    return codes.astype(jnp.int32).astype(jnp.float32) * scale
+    return jnp.ceil(jnp.log2(jnp.maximum(top, 1e-30)) * EXP_STEPS) + 1.0
+
+
+def encode(ref, blocks):
+    rows = lax.broadcasted_iota(jnp.int32, (EXP_ROWS, ref.shape[1]), 0)
+    packed = jnp.zeros(rows.shape, jnp.int32)
+    for n, block in enumerate(blocks):
+        level = levels_of(block)
+        codes = jnp.round(block * (CODE_TOP * jnp.exp2(level * (-1.0 / EXP_STEPS))))
+        ref[n * BLK : (n + 1) * BLK] = codes.astype(jnp.int32).astype(jnp.int16)
+        packed = jnp.where(rows == n, level.astype(jnp.int32), packed)
+    ref[len(blocks) * BLK :] = packed.astype(jnp.int16)
+
+
+def decode(ref, n=0):
+    levels = ref[ref.shape[0] - EXP_ROWS :].astype(jnp.int32).astype(jnp.float32)[n : n + 1]
+    scale = jnp.exp2(levels * (1.0 / EXP_STEPS)) * (1.0 / CODE_TOP)
+    return ref[n * BLK : (n + 1) * BLK].astype(jnp.int32).astype(jnp.float32) * scale
 
 
 def lu_step(ref, j):
@@ -136,25 +143,27 @@
     )(lt)
 
 
-def first_block(where_ref, phase, part, start, blocks):
-    half = where_ref[7] if phase == 0 else 1 - where_ref[7]
-    return (2 * half + part) * blocks + start
-
-
-def split_kernel(phase, start, count, blocks, where_ref, *refs):
+def block_at(where_ref, spot, part, blocks, flip=0):
+    phase, number = spot
+    half = where_ref[7] if phase == flip else 1 - where_ref[7]
+    return (2 * half + part) * blocks + number
+
+
+def split_kernel(chunk, blocks, where_ref, *refs):
     sources, outs, sems = refs[:4], refs[4:6], refs[6]
-    size = count * BLK
     copies = []
     for n, ref in enumerate(sources):
         for part in range(2):
-            begin = first_block(where_ref, 1 - phase, part, start, blocks) * BLK
-            copies.append(
-                pltpu.make_async_copy(
-                    ref.at[:, :, pl.ds(pl.multiple_of(begin, BLK), size)],
-                    outs[n // 2].at[n % 2, :, :, part * size : (part + 1) * size],
-                    sems.at[n, part],
+            for m, spot in enumerate(chunk):
+                begin = block_at(where_ref, spot, part, blocks, flip=1) * BLK
+                at = (part * len(chunk) + m) * BLK
+                copies.append(
+                    pltpu.make_async_copy(
+                        ref.at[:, :, pl.ds(pl.multiple_of(begin, BLK), BLK)],
+                        outs[n // 2].at[n % 2, :, :, at : at + BLK],
+                        sems.at[n, part, m],
+                    )
                 )
-            )
     for copy in copies:
         copy.start()
     for copy in copies:
@@ -162,15 +171,15 @@
 
 
 def split(where, sources, chunk, blocks):
-    phase, start, count = chunk
     half, depth, _ = sources[0].shape
+    count = len(chunk)
     one = jax.ShapeDtypeStruct((2, half, depth, 2 * count * BLK), sources[0].dtype)
     return pl.pallas_call(
-        functools.partial(split_kernel, phase, start, count, blocks),
+        functools.partial(split_kernel, chunk, blocks),
         out_shape=[one, one],
         in_specs=[SMEM] + [ANY] * 4,
         out_specs=[ANY, ANY],
-        scratch_shapes=[pltpu.SemaphoreType.DMA((4, 2))],
+        scratch_shapes=[pltpu.SemaphoreType.DMA((4, 2, count))],
         compiler_params=params(),
         cost_estimate=cost(0),
         name="split",
@@ -221,25 +230,23 @@
 
 
 def product(chunk, blocks, where_ref, lpat_ref, whole, groups, right_ref, left):
-    phase, start, count = chunk
-    pieces, half, depth = 2, left.shape[0] // 2, left.shape[1] // 2
+    half, depth = left.shape[0] // 2, left.shape[1] // 2
     for part in range(2):
-        first = first_block(where_ref, phase, part, start, blocks)
-        for h, group in enumerate(groups):
-            for n in range(pieces):
-                for i in range(half):
-                    k = h * half + i
-                    for m in range(count):
-                        at = (part * count + m) * BLK
-                        if whole:
-                            begin = pl.multiple_of((first + m) * BLK, BLK)
-                            block = group[n][i, :, pl.ds(begin, BLK)]
-                        else:
-                            block = group[n, i, :, at : at + BLK]
-                        kept = lpat_ref[k, first + m] != 0
-                        left[k, n * depth : (n + 1) * depth, at : at + BLK] = jnp.where(
-                            kept, block, jnp.zeros_like(block)
-                        )
+        for m, spot in enumerate(chunk):
+            number = block_at(where_ref, spot, part, blocks)
+            at = (part * len(chunk) + m) * BLK
+            for k in range(2 * half):
+                kept = lpat_ref[k, number] != 0
+                for n in range(2):
+                    group, i = groups[k // half], k % half
+                    if whole:
+                        begin = pl.multiple_of(number * BLK, BLK)
+                        block = group[n][i, :, pl.ds(begin, BLK)]
+                    else:
+                        block = group[n, i, :, at : at + BLK]
+                    left[k, n * depth : (n + 1) * depth, at : at + BLK] = jnp.where(
+                        kept, block, jnp.zeros_like(block)
+                    )
     return lax.dot_general(
         left[...].reshape(-1, left.shape[2]),
         right_ref[...].reshape(-1, right_ref.shape[2]),
@@ -257,7 +264,7 @@
 
 def near_update(where, lpat, sources, right, chunk, blocks):
     supers, kdim, cols = right.shape
-    count = 2 * chunk[2]
+    count = 2 * len(chunk)
     return pl.pallas_call(
         functools.partial(near_kernel, chunk, blocks),
         out_shape=jax.ShapeDtypeStruct((count, BLK, cols), jnp.float32),
@@ -270,40 +277,43 @@
     )(where, lpat, *sources, right)
 
 
-def far_kernel(chunk, blocks, where_ref, lpat_ref, a_ref, b_ref, right_ref, before_ref, *refs):
-    kept_ref, sent_ref = refs[:2]
+def far_kernel(chunk, blocks, earlier, where_ref, lpat_ref, a_ref, b_ref, *refs):
+    right_ref, before_ref = refs[:2]
+    kept_ref, sent_ref = refs[2 + earlier : 4 + earlier]
     left, acc = refs[-2:]
-    count = chunk[2]
+    count = len(chunk)
     groups = (a_ref, b_ref)
     total = product(chunk, blocks, where_ref, lpat_ref, False, groups, right_ref, left)
     acc[...] = (before_ref[...] + total.reshape(before_ref.shape)).reshape(acc.shape)
-    if chunk[0] == 0:
-        diag_ref = refs[2]
-        for q in range(2 * count):
-            lanes = slice(q * BLK, (q + 1) * BLK)
-            diag_ref[:BLK, lanes], diag_ref[BLK:, lanes] = encode(
-                acc[q // count, q % count, :, lanes]
-            )
+    first = [(m, number) for m, (phase, number) in enumerate(chunk) if phase == 0]
+    if first:
+        diag_ref = refs[4 + earlier]
+        if earlier:
+            diag_ref[...] = refs[2][...]
+        for part in range(2):
+            for m, number in first:
+                q = part * blocks + number
+                lanes = slice(q * BLK, (q + 1) * BLK)
+                encode(diag_ref.at[:, lanes], [acc[part, m, :, lanes]])
     mine = where_ref[0] & 1
     for m in range(count):
         kept_ref[m] = acc[mine, m]
-        sent_ref[m, :BLK], sent_ref[m, BLK:] = encode(acc[1 - mine, m])
-
-
-def far_update(where, lpat, pieces, right, before, chunk, blocks):
+    encode(sent_ref, [acc[1 - mine, m] for m in range(count)])
+
+
+def far_update(where, lpat, pieces, right, before, earlier, chunk, blocks):
     supers, kdim, cols = right.shape
-    count = chunk[2]
-    coded = BLK + EXP_ROWS
+    count = len(chunk)
     shapes = [
         jax.ShapeDtypeStruct((count, BLK, cols), jnp.float32),
-        jax.ShapeDtypeStruct((count, coded, cols), jnp.int16),
+        jax.ShapeDtypeStruct((count * BLK + EXP_ROWS, cols), jnp.int16),
     ]
-    if chunk[0] == 0:
-        shapes.append(jax.ShapeDtypeStruct((coded, 2 * count * BLK), jnp.int16))
-    return pl.pallas_call(
-        functools.partial(far_kernel, chunk, blocks),
+    if any(phase == 0 for phase, _ in chunk):
+        shapes.append(jax.ShapeDtypeStruct((BLK + EXP_ROWS, cols), jnp.int16))
+    return pl.pallas_call(
+        functools.partial(far_kernel, chunk, blocks, len(earlier)),
         out_shape=shapes,
-        in_specs=[SMEM] * 2 + [VMEM] * 4,
+        in_specs=[SMEM] * 2 + [VMEM] * (4 + len(earlier)),
         out_specs=[VMEM] * len(shapes),
         scratch_shapes=[
             pltpu.VMEM((supers, kdim, 2 * count * BLK), jnp.bfloat16),
@@ -312,34 +322,47 @@
         compiler_params=params(),
         cost_estimate=cost(FAR),
         name="far_update",
-    )(where, lpat, *pieces, right, before)
-
-
-def halve_kernel(kept_ref, got_ref, sum_ref, sent_ref):
-    for m in range(kept_ref.shape[0]):
-        total = kept_ref[m] + decode(got_ref[m, :BLK], got_ref[m, BLK:])
+    )(where, lpat, *pieces, right, before, *earlier)
+
+
+def halve_kernel(chunk, where_ref, kept_ref, got_ref, sum_ref, sent_ref):
+    totals = [kept_ref[m] + decode(got_ref, m) for m in range(len(chunk))]
+    for m, total in enumerate(totals):
         sum_ref[m] = total
-        sent_ref[m, :BLK], sent_ref[m, BLK:] = encode(total)
-
-
-def halve(kept, got):
-    return pl.pallas_call(
-        halve_kernel,
+    early = [total for total, (phase, _) in zip(totals, chunk) if phase == 0]
+    late = [total for total, (phase, _) in zip(totals, chunk) if phase == 1]
+    if early and late:
+        keeps_early = where_ref[0] // 2 == where_ref[7]
+
+        @pl.when(keeps_early)
+        def _():
+            encode(sent_ref, late)
+
+        @pl.when(jnp.logical_not(keeps_early))
+        def _():
+            encode(sent_ref, early)
+    else:
+        encode(sent_ref, totals)
+
+
+def halve(where, kept, got, chunk):
+    count = max(sum(phase == p for phase, _ in chunk) for p in range(2))
+    return pl.pallas_call(
+        functools.partial(halve_kernel, chunk),
         out_shape=[
             jax.ShapeDtypeStruct(kept.shape, kept.dtype),
-            jax.ShapeDtypeStruct(got.shape, got.dtype),
+            jax.ShapeDtypeStruct((count * BLK + EXP_ROWS, kept.shape[2]), got.dtype),
         ],
-        in_specs=[VMEM] * 2,
+        in_specs=[SMEM] + [VMEM] * 2,
         out_specs=[VMEM] * 2,
         compiler_params=params(),
         cost_estimate=cost(0),
         name="halve",
-    )(kept, got)
+    )(where, kept, got)
 
 
 def add_kernel(mine_ref, got_ref, out_ref):
-    total = decode(mine_ref[:BLK], mine_ref[BLK:]) + decode(got_ref[:BLK], got_ref[BLK:])
-    out_ref[:BLK], out_ref[BLK:] = encode(total)
+    encode(out_ref, [decode(mine_ref) + decode(got_ref)])
 
 
 def add_coded(mine, got):
@@ -354,7 +377,7 @@
     )(mine, got)
 
 
-def combine_kernel(counts, where_ref, anc_ref, *refs):
+def combine_kernel(chunks, where_ref, anc_ref, *refs):
     out_ref, start, sem = refs[-3:]
     share = out_ref.shape[0]
     begin = pl.multiple_of(where_ref[0] * share, BLK)
@@ -362,31 +385,30 @@
     fetch.start()
     fetch.wait()
 
-    def fill(spots):
-        row = 0
-        for n in spots:
+    def fill(wanted):
+        for n, chunk in enumerate(chunks):
             kept_ref, got_ref = refs[2 * n : 2 * n + 2]
-            for m in range(counts[n]):
-                total = kept_ref[m] + decode(got_ref[m, :BLK], got_ref[m, BLK:])
-                out_ref[row : row + BLK] = start[row : row + BLK] - total
-                row += BLK
-
-    first = where_ref[0] // 2 == where_ref[7]
-
-    @pl.when(first)
+            spots = [(m, number) for m, (phase, number) in enumerate(chunk) if phase == wanted]
+            for i, (m, number) in enumerate(spots):
+                rows = slice(number * BLK, (number + 1) * BLK)
+                out_ref[rows] = start[rows] - (kept_ref[m] + decode(got_ref, i))
+
+    early = where_ref[0] // 2 == where_ref[7]
+
+    @pl.when(early)
     def _():
-        fill([0])
-
-    @pl.when(jnp.logical_not(first))
+        fill(0)
+
+    @pl.when(jnp.logical_not(early))
     def _():
-        fill(range(1, len(counts)))
-
-
-def combine(where, anc, pairs, share):
+        fill(1)
+
+
+def combine(where, anc, pairs, chunks, share):
     parts = [part for pair in pairs for part in pair]
     cols = anc.shape[1]
     return pl.pallas_call(
-        functools.partial(combine_kernel, [kept.shape[0] for kept, _ in pairs]),
+        functools.partial(combine_kernel, chunks),
         out_shape=jax.ShapeDtypeStruct((share, cols), jnp.float32),
         in_specs=[SMEM, ANY] + [VMEM] * len(parts),
         out_specs=VMEM,
@@ -409,7 +431,7 @@
         )
     for copy in copies:
         copy.start()
-    total = decode(one_ref[:BLK], one_ref[BLK:]) + decode(two_ref[:BLK], two_ref[BLK:])
+    total = decode(one_ref) + decode(two_ref)
     for copy in copies:
         copy.wait()
     for q in range(count):
@@ -466,13 +488,13 @@
     def near_layers(value):
         return lax.ppermute(value, "layer", xor_perm(layers, 1))
 
-    def far_layers(value, phase):
+    def far_layers(value, chunk):
+        phases = {phase for phase, _ in chunk}
         perm = []
         for l, r, c in spots:
             half = c % per_group if r == c // per_group else 1 - c % per_group
-            if phase == 1:
-                half = 1 - half
-            if l // 2 != half:
+            sends = 1 if l // 2 == half else 0
+            if sends in phases:
                 perm.append((index(l, r, c), index(l ^ 2, r, c)))
         return lax.ppermute(value, everyone, perm)
 
@@ -486,45 +508,41 @@
     uo = lax.ppermute(u, "row", xor_perm(rows, 1))
     near_right, far_right = masked_right(where, upat[0], u, uo)
     whole = (a, xa, b, yb)
-    chunks = [(0, 0, blocks), (1, 0, blocks - 1), (1, blocks - 1, 1)]
-    sides, others = [], []
-
-    def send_rows(chunk, *waits):
-        if sides:
-            waits += tuple(sides[-1])
-        ready = (after(a, *waits) if waits else a, xa, b, yb)
+    rounds = [(phase, number) for phase in range(2) for number in range(blocks)]
+    chunks = [rounds[n : n + 2] for n in range(0, len(rounds), 2)]
+    sides = []
+    for chunk in chunks:
+        ready = (after(a, *sides[-1]) if sides else a, xa, b, yb)
         sides.append(split(where, ready, chunk, blocks))
-        others.append((over(sides[-1][0], 2), over(sides[-1][1], 1)))
-
-    send_rows(chunks[0])
-    send_rows(chunks[1])
+    others = [(over(one, 2), over(two, 1)) for one, two in sides]
     masks = lpat[0]
     parts = [near_update(where, masks, whole, near_right, chunk, blocks) for chunk in chunks]
+    known = []
 
     def far_part(j, *waits):
-        return far_update(
-            where, masks, others[j], far_right, after(parts[j], *waits), chunks[j], blocks
-        )
+        part = after(parts[j], *waits) if waits else parts[j]
+        return far_update(where, masks, others[j], far_right, part, known, chunks[j], blocks)
 
     kept0, coded0, diag = far_part(0)
-    near = add_coded(diag, holders(diag, lambda l, r, c: (l ^ 1, r, c)))
+    known = [diag]
+    sum0, sent0 = halve(where, kept0, near_layers(coded0), chunks[0])
+    kept1, coded1, diag = far_part(1, kept0, parts[2])
+    known = []
+    near = add_coded(after(diag, sent0), holders(diag, lambda l, r, c: (l ^ 1, r, c)))
     far = holders(near, lambda l, r, c: (l ^ 2, r, c))
-    send_rows(chunks[2], near)
     own = pivots(where, anc, near, far)
     other = holders(own, lambda l, r, c: (l, 1 - r, c))
-    kept1, coded1 = far_part(1, near)
-    kept2, coded2 = far_part(2, own)
-    sum0, sent0 = halve(kept0, near_layers(coded0))
-    half_lu = factor(where, after(own, sent0, coded2), other, HALF_STEPS)
-    sum1, sent1 = halve(after(kept1, half_lu), near_layers(coded1))
-    diag_lu = factor_rest(after(half_lu, sent1), HALF_STEPS)
-    sum2, sent2 = halve(after(kept2, half_lu), near_layers(coded2))
+    kept2, coded2 = far_part(2, near, sent0)
+    sum1, sent1 = halve(where, kept1, near_layers(coded1), chunks[1])
+    half_lu = factor(where, after(own, sent1, coded2), other, HALF_STEPS)
+    sum2, sent2 = halve(where, after(kept2, half_lu), near_layers(coded2), chunks[2])
+    diag_lu = factor_rest(after(half_lu, sent2), HALF_STEPS)
     pairs = [
-        (sum0, far_layers(sent0, 0)),
-        (sum1, far_layers(sent1, 1)),
-        (after(sum2, diag_lu), far_layers(sent2, 1)),
+        (sum0, far_layers(sent0, chunks[0])),
+        (sum1, far_layers(sent1, chunks[1])),
+        (after(sum2, diag_lu), far_layers(sent2, chunks[2])),
     ]
-    return combine(where, anc, pairs, share), diag_lu
+    return combine(where, anc, pairs, chunks, share), diag_lu
 
 
 def mask_rows(panel, pattern, block):
@@ -577,7 +595,7 @@
     fits = rows == 2 and cols == 4 and layers == 4
     share, extra = divmod(anc.shape[0], layers * BLK)
     square = anc.shape[1] == 2 * share * BLK
-    if fits and square and extra == 0 and share > 1 and lpanel.shape[1] % 2 == 0:
+    if fits and square and extra == 0 and share == 3 and lpanel.shape[1] % 2 == 0:
         return planned(lpanel, upanel, lpat, upat, anc)
     return gathered(lpanel, upanel, lpat, upat, anc)
 

time: 116 us -> 112 us (0.966)
  the two profiles are of different devices: /device:TPU:0 before, /device:TPU:2 now
where the time goes in v7:
time: 112 us; the launch traced here: 111 us
  waiting for transfers between devices  47.7 us (43%)
  Pallas kernels  36.5 us (33%)
  starting transfers between devices  24.5 us (22%)
  local copies, waits for them, and re-layouts  1.58 us (1%)
    ppermute x8, waiting for transfers between devices, over(): return lax.ppermute(value, 'col', xor_perm(cols, bit))  24.9 us
    ppermute x3, waiting for transfers between devices, holders(): return lax.ppermute(value, everyone, perm)  15.1 us
    ppermute x8, starting transfers between devices, over(): return lax.ppermute(value, 'col', xor_perm(cols, bit))  9.62 us
    pallas_call x1, Pallas kernels, factor_rest(): pl.pallas_call(functools.partial(rest_kernel, begin), out_shape=jax.Shape...  8.67 us
    ppermute x3, starting transfers between devices, holders(): return lax.ppermute(value, everyone, perm)  6.74 us
    pallas_call x3, Pallas kernels, far_update(): pl.pallas_call(functools.partial(far_kernel, chunk, blocks, len(earlier))...  6.35 us
    ppermute x3, starting transfers between devices, far_layers(): return lax.ppermute(value, everyone, perm)  6.21 us
    pallas_call x3, Pallas kernels, near_update(): pl.pallas_call(functools.partial(near_kernel, chunk, blocks), out_shape=j...  5.41 us
  transfers between devices with their start and end apart: 18, of which 8 were waited for; matrix products, arithmetic and copies ran while one was open for 0% of the time, Pallas kernels for 31%

profile of v7, /device:TPU:2, one launch (start us, length us, event | category | flops | bytes accessed | tf_op | source)
XLA Modules:
  0.0 111.3 jit_solution(6354217955971498562)
XLA Ops:
  0.6 0.1 collective-permute-start.4
  0.7 1.4 %copy-done = bf16[1,8,1536,64]{2,3,1,0:T(8,128)(2,1)S(1)} copy-done((bf16[1,8,1536,64]{2,3,1,0:T(8,128)(2,1)S(1)}, bf16[1,8,1536,64]{2,3,1,0:T(8,128)(2,1)}, u32[]{:S(2)}) %copy-start) | copy-done | bytes 1572888
  2.1 0.1 halves.1
  2.3 0.1 collective-permute-start
  2.3 2.0 %collective-permute-start.1 = (bf16[4,64,1536]{2,1,0:T(8,128)(2,1)S(1)}, bf16[4,64,1536]{2,1,0:T(8,128)(2,1)S(1)}, u32[]{:S(2)}, u32[]{:S(2)}) collective-permute-start(bf16[4,64,1536]{2,1,0:T(8,128)(2,1)S(1)} %get-tuple-element.36.refs_2_), channel_id=1, source_target_pairs={{0,2},{1,3},{2,0},{3,1},{4,6},{5,7},{6,4},{7,5},{8,10},{9,11},{10,... | collective-permute-start | bytes 2359304 | tf_op jit(solution)/shard_map/ppermute | solution.py:502
  4.4 0.1 copy.7
  4.5 0.1 stack.35.where_ref
  4.6 17.7 %collective-permute-done.refs_1_ = bf16[4,64,1536]{2,1,0:T(8,128)(2,1)S(1)} collective-permute-done((bf16[4,64,1536]{2,1,0:T(8,128)(2,1)S(1)}, bf16[4,64,1536]{2,1,0:T(8,128)(2,1)S(1)}, u32[]{:S(2)}, u32[]{:S(2)}) %collective-permute-start) | collective-permute-done | bytes 786464 | tf_op jit(solution)/shard_map/ppermute | solution.py:502
  22.3 0.1 collective-permute-done.1.refs_3_
  22.3 0.9 split.3
  23.3 1.8 %collective-permute-start.2 = (bf16[2,4,64,512]{3,2,1,0:T(8,128)(2,1)S(1)}, bf16[2,4,64,512]{3,2,1,0:T(8,128)(2,1)S(1)}, u32[]{:S(2)}, u32[]{:S(2)}) collective-permute-start(bf16[2,4,64,512]{3,2,1,0:T(8,128)(2,1)S(1)} %get-tuple-element.37), channel_id=1, source_target_pairs={{0,2},{1,3},{2,0},{3,1},{4,6},{5,7},{6,4},{7,5},{8,10},{9,11},{10,... | collective-permute-start | bytes 1572872 | tf_op jit(solution)/shard_map/ppermute | solution.py:502
  25.0 1.5 %collective-permute-start.3 = (bf16[2,4,64,512]{3,2,1,0:T(8,128)(2,1)S(1)}, bf16[2,4,64,512]{3,2,1,0:T(8,128)(2,1)S(1)}, u32[]{:S(2)}, u32[]{:S(2)}) collective-permute-start(bf16[2,4,64,512]{3,2,1,0:T(8,128)(2,1)S(1)} %get-tuple-element.38), channel_id=1, source_target_pairs={{0,1},{1,0},{2,3},{3,2},{4,5},{5,4},{6,7},{7,6},{8,9},{9,8},{10,11... | collective-permute-start | bytes 1572872 | tf_op jit(solution)/shard_map/ppermute | solution.py:502
  26.5 0.9 split.4
  27.4 0.6 collective-permute-start.7
  28.0 0.4 collective-permute-start.8
  28.4 0.9 split.5
  29.3 1.8 %collective-permute-start.11 = (bf16[2,4,64,512]{3,2,1,0:T(8,128)(2,1)S(1)}, bf16[2,4,64,512]{3,2,1,0:T(8,128)(2,1)S(1)}, u32[]{:S(2)}, u32[]{:S(2)}) collective-permute-start(bf16[2,4,64,512]{3,2,1,0:T(8,128)(2,1)S(1)} %get-tuple-element.55), channel_id=1, source_target_pairs={{0,2},{1,3},{2,0},{3,1},{4,6},{5,7},{6,4},{7,5},{8,10},{9,11},{10,... | collective-permute-start | bytes 1572872 | tf_op jit(solution)/shard_map/ppermute | solution.py:502
  31.1 2.2 %masked_right.1 = (bf16[8,128,768]{2,1,0:T(8,128)(2,1)S(1)}, bf16[8,128,768]{2,1,0:T(8,128)(2,1)S(1)}) custom-call(s32[8]{0:T(128)S(1)} %stack.35.where_ref, s32[8,6]{1,0:T(8,128)S(1)} %bitcast.19, bf16[8,128,768]{2,1,0:T(8,128)(2,1)S(1)} %bitcast.18, bf16[8,128,768]{2,1,0:T(8,128)(2,1)} %collective-permute-done.4.uo_ref), custom_call_target="tpu_custom_call" | custom-call | flops 1000 | bytes 1000 | tf_op jit(solution)/shard_map/masked_right/pallas_call | solution.py:221
  33.3 1.8 %near_update.4.refs_1_ = f32[4,128,768]{2,1,0:T(8,128)S(1)} custom-call(s32[8]{0:T(128)S(1)} %stack.35.where_ref, s32[8,12]{1,0:T(8,128)S(1)} %bitcast.20, bf16[4,64,1536]{2,1,0:T(8,128)(2,1)S(1)} %get-tuple-element.54.refs_0_, bf16[4,64,1536]{2,1,0:T(8,128)(2,1)S(1)} %collective-permute-done.refs_1_, bf16[4,64,1536]{2,1,0:T(8,128)(2,1)S(1)} %get-tuple-element.36.refs_2_, ...), custom_call_target="tpu_custom_call" | custom-call | flops 10000001024 | bytes 1000 | tf_op jit(solution)/shard_map/near_update/pallas_call | solution.py:268
  35.1 1.8 %near_update.5.refs_1_ = f32[4,128,768]{2,1,0:T(8,128)S(1)} custom-call(s32[8]{0:T(128)S(1)} %stack.35.where_ref, s32[8,12]{1,0:T(8,128)S(1)} %bitcast.21, bf16[4,64,1536]{2,1,0:T(8,128)(2,1)S(1)} %get-tuple-element.54.refs_0_, bf16[4,64,1536]{2,1,0:T(8,128)(2,1)S(1)} %collective-permute-done.refs_1_, bf16[4,64,1536]{2,1,0:T(8,128)(2,1)S(1)} %get-tuple-element.36.refs_2_, ...), custom_call_target="tpu_custom_call" | custom-call | flops 10000001024 | bytes 1000 | tf_op jit(solution)/shard_map/near_update/pallas_call | solution.py:268
  36.9 1.8 %near_update.3.refs_1_ = f32[4,128,768]{2,1,0:T(8,128)S(1)} custom-call(s32[8]{0:T(128)S(1)} %stack.35.where_ref, s32[8,12]{1,0:T(8,128)S(1)} %bitcast.22, bf16[4,64,1536]{2,1,0:T(8,128)(2,1)S(1)} %get-tuple-element.54.refs_0_, bf16[4,64,1536]{2,1,0:T(8,128)(2,1)S(1)} %collective-permute-done.refs_1_, bf16[4,64,1536]{2,1,0:T(8,128)(2,1)S(1)} %get-tuple-element.36.refs_2_, ...), custom_call_target="tpu_custom_call" | custom-call | flops 10000001024 | bytes 1000 | tf_op jit(solution)/shard_map/near_update/pallas_call | solution.py:268
  38.7 1.6 %collective-permute-start.12 = (bf16[2,4,64,512]{3,2,1,0:T(8,128)(2,1)S(1)}, bf16[2,4,64,512]{3,2,1,0:T(8,128)(2,1)S(1)}, u32[]{:S(2)}, u32[]{:S(2)}) collective-permute-start(bf16[2,4,64,512]{3,2,1,0:T(8,128)(2,1)S(1)} %get-tuple-element.56), channel_id=1, source_target_pairs={{0,1},{1,0},{2,3},{3,2},{4,5},{5,4},{6,7},{7,6},{8,9},{9,8},{10,11... | collective-permute-start | bytes 1572872 | tf_op jit(solution)/shard_map/ppermute | solution.py:502
  40.3 2.1 %far_update.3 = (f32[2,128,768]{2,1,0:T(8,128)S(1)}, s16[272,768]{1,0:T(8,128)(2,1)S(1)}, s16[144,768]{1,0:T(8,128)(2,1)S(1)}) custom-call(s32[8]{0:T(128)S(1)} %stack.35.where_ref, s32[8,12]{1,0:T(8,128)S(1)} %bitcast.23, bf16[2,4,64,512]{3,2,1,0:T(8,128)(2,1)S(1)} %collective-permute-done.2.a_ref, ...), custom_call_target="tpu_custom_call" | custom-call | flops 10000001024 | bytes 1000 | tf_op jit(solution)/shard_map/far_update/pallas_call | solution.py:313
  42.4 1.7 %collective-permute-start.5 = (s16[272,768]{1,0:T(8,128)(2,1)S(1)}, s16[272,768]{1,0:T(8,128)(2,1)S(1)}, u32[]{:S(2)}, u32[]{:S(2)}) collective-permute-start(s16[272,768]{1,0:T(8,128)(2,1)S(1)} %get-tuple-element.42), channel_id=1, source_target_pairs={{0,8},{8,0},{16,24},{24,16},{1,9},{9,1},{17,25},{25,17},{2,10},{10... | collective-permute-start | bytes 1253384 | tf_op jit(solution)/shard_map/ppermute | solution.py:489
  44.1 5.3 %collective-permute-done.7.a_ref = bf16[2,4,64,512]{3,2,1,0:T(8,128)(2,1)S(1)} collective-permute-done((bf16[2,4,64,512]{3,2,1,0:T(8,128)(2,1)S(1)}, bf16[2,4,64,512]{3,2,1,0:T(8,128)(2,1)S(1)}, u32[]{:S(2)}, u32[]{:S(2)}) %collective-permute-start.7) | collective-permute-done | bytes 524320 | tf_op jit(solution)/shard_map/ppermute | solution.py:502
  49.4 1.7 %collective-permute-done.8.b_ref = bf16[2,4,64,512]{3,2,1,0:T(8,128)(2,1)S(1)} collective-permute-done((bf16[2,4,64,512]{3,2,1,0:T(8,128)(2,1)S(1)}, bf16[2,4,64,512]{3,2,1,0:T(8,128)(2,1)S(1)}, u32[]{:S(2)}, u32[]{:S(2)}) %collective-permute-start.8) | collective-permute-done | bytes 524320 | tf_op jit(solution)/shard_map/ppermute | solution.py:502
  51.1 2.1 %far_update.4 = (f32[2,128,768]{2,1,0:T(8,128)S(1)}, s16[272,768]{1,0:T(8,128)(2,1)S(1)}, s16[144,768]{1,0:T(8,128)(2,1)S(1)}) custom-call(s32[8]{0:T(128)S(1)} %stack.35.where_ref, s32[8,12]{1,0:T(8,128)S(1)} %bitcast.24, bf16[2,4,64,512]{3,2,1,0:T(8,128)(2,1)S(1)} %collective-permute-done.7.a_ref, ...), custom_call_target="tpu_custom_call" | custom-call | flops 10000001024 | bytes 1000 | tf_op jit(solution)/shard_map/far_update/pallas_call | solution.py:313
  53.3 3.5 %collective-permute-start.13 = (s16[144,768]{1,0:T(8,128)(2,1)S(1)}, s16[144,768]{1,0:T(8,128)(2,1)S(1)}, u32[]{:S(2)}, u32[]{:S(2)}) collective-permute-start(s16[144,768]{1,0:T(8,128)(2,1)S(1)} %get-tuple-element.58.mine_ref), channel_id=1, source_target_pairs={{0,8},{1,9},{6,14},{7,15},{8,0},{9,1},{14,6},{15,7},{16,24},{17,25... | collective-permute-start | bytes 663560 | tf_op jit(solution)/shard_map/ppermute | solution.py:486
  56.8 0.8 halve.3
  57.6 10.1 %collective-permute-done.13.got_ref = s16[144,768]{1,0:T(8,128)(2,1)S(1)} collective-permute-done((s16[144,768]{1,0:T(8,128)(2,1)S(1)}, s16[144,768]{1,0:T(8,128)(2,1)S(1)}, u32[]{:S(2)}, u32[]{:S(2)}) %collective-permute-start.13) | collective-permute-done | bytes 221216 | tf_op jit(solution)/shard_map/ppermute | solution.py:486
  67.7 0.2 add_coded.1.one_ref
  67.9 1.9 %collective-permute-start.14 = (s16[144,768]{1,0:T(8,128)(2,1)S(1)}, s16[144,768]{1,0:T(8,128)(2,1)S(1)}, u32[]{:S(2)}, u32[]{:S(2)}) collective-permute-start(s16[144,768]{1,0:T(8,128)(2,1)S(1)} %add_coded.1.one_ref), channel_id=1, source_target_pairs={{0,16},{1,17},{6,22},{7,23},{8,24},{9,25},{14,30},{15,31},{16,0},{... | collective-permute-start | bytes 663560 | tf_op jit(solution)/shard_map/ppermute | solution.py:486
  69.8 0.1 collective-permute-start.9
  69.9 4.8 %collective-permute-start.6 = (s16[272,768]{1,0:T(8,128)(2,1)S(1)}, s16[272,768]{1,0:T(8,128)(2,1)S(1)}, u32[]{:S(2)}, u32[]{:S(2)}) collective-permute-start(s16[272,768]{1,0:T(8,128)(2,1)S(1)} %get-tuple-element.44), channel_id=1, source_target_pairs={{1,17},{2,18},{4,20},{7,23},{9,25},{10,26},{12,28},{15,31},{16,0},... | collective-permute-start | bytes 1253384 | tf_op jit(solution)/shard_map/ppermute | solution.py:499
  74.7 5.0 %collective-permute-done.14.two_ref = s16[144,768]{1,0:T(8,128)(2,1)S(1)} collective-permute-done((s16[144,768]{1,0:T(8,128)(2,1)S(1)}, s16[144,768]{1,0:T(8,128)(2,1)S(1)}, u32[]{:S(2)}, u32[]{:S(2)}) %collective-permute-start.14) | collective-permute-done | bytes 221216 | tf_op jit(solution)/shard_map/ppermute | solution.py:486
  79.8 0.8 pivots.1.own_ref
  80.6 1.3 %collective-permute-start.15 = (f32[6,128,128]{2,1,0:T(8,128)S(1)}, f32[6,128,128]{2,1,0:T(8,128)S(1)}, u32[]{:S(2)}, u32[]{:S(2)}) collective-permute-start(f32[6,128,128]{2,1,0:T(8,128)S(1)} %pivots.1.own_ref), channel_id=1, source_target_pairs={{0,4},{1,5},{6,2},{7,3},{8,12},{9,13},{14,10},{15,11},{16,20},{17,... | collective-permute-start | bytes 1179656 | tf_op jit(solution)/shard_map/ppermute | solution.py:486
  81.9 2.1 %far_update.5 = (f32[2,128,768]{2,1,0:T(8,128)S(1)}, s16[272,768]{1,0:T(8,128)(2,1)S(1)}) custom-call(s32[8]{0:T(128)S(1)} %stack.35.where_ref, s32[8,12]{1,0:T(8,128)S(1)} %bitcast.25, bf16[2,4,64,512]{3,2,1,0:T(8,128)(2,1)S(1)} %collective-permute-done.11.a_ref, bf16[2,4,64,512]{3,2,1,0:T(8,128)(2,1)S(1)} %collective-permute-done.12.b_ref, ...), custom_call_target="tpu_custom_call" | custom-call | flops 10000001024 | bytes 1000 | tf_op jit(solution)/shard_map/far_update/pallas_call | solution.py:313
  84.1 0.1 collective-permute-start.16
  84.2 0.9 halve.4
  85.1 0.1 collective-permute-start.10
  85.2 5.4 %factor.1.in_ref = f32[6,128,128]{2,1,0:T(8,128)S(1)} custom-call(s32[8]{0:T(128)S(1)} %stack.35.where_ref, f32[6,128,128]{2,1,0:T(8,128)S(1)} %pivots.1.own_ref, f32[6,128,128]{2,1,0:T(8,128)S(1)} %collective-permute-done.15.other_ref), custom_call_target="tpu_custom_call" | custom-call | flops 10000001024 | bytes 1000 | tf_op jit(solution)/shard_map/factor/pallas_call | solution.py:90
  90.6 4.0 %collective-permute-done.16.got_ref = s16[272,768]{1,0:T(8,128)(2,1)S(1)} collective-permute-done((s16[272,768]{1,0:T(8,128)(2,1)S(1)}, s16[272,768]{1,0:T(8,128)(2,1)S(1)}, u32[]{:S(2)}, u32[]{:S(2)}) %collective-permute-start.16) | collective-permute-done | bytes 417824 | tf_op jit(solution)/shard_map/ppermute | solution.py:489
  94.6 0.8 halve.5
  95.4 1.3 %collective-permute-start.17 = (s16[272,768]{1,0:T(8,128)(2,1)S(1)}, s16[272,768]{1,0:T(8,128)(2,1)S(1)}, u32[]{:S(2)}, u32[]{:S(2)}) collective-permute-start(s16[272,768]{1,0:T(8,128)(2,1)S(1)} %get-tuple-element.65), channel_id=1, source_target_pairs={{0,16},{3,19},{5,21},{6,22},{8,24},{11,27},{13,29},{14,30},{17,1},... | collective-permute-start | bytes 1253384 | tf_op jit(solution)/shard_map/ppermute | solution.py:499
  96.7 8.7 %factor_rest.1 = f32[6,128,128]{2,1,0:T(8,128)} custom-call(f32[6,128,128]{2,1,0:T(8,128)S(1)} %factor.1.in_ref), custom_call_target="tpu_custom_call" | custom-call | flops 10000001024 | bytes 1000 | tf_op jit(solution)/shard_map/factor_rest/pallas_call | solution.py:108
  105.3 3.7 %collective-permute-done.17.refs_5_ = s16[272,768]{1,0:T(8,128)(2,1)S(1)} collective-permute-done((s16[272,768]{1,0:T(8,128)(2,1)S(1)}, s16[272,768]{1,0:T(8,128)(2,1)S(1)}, u32[]{:S(2)}, u32[]{:S(2)}) %collective-permute-start.17) | collective-permute-done | bytes 417824 | tf_op jit(solution)/shard_map/ppermute | solution.py:499
  109.1 2.1 %combine.1 = f32[384,768]{1,0:T(8,128)} custom-call(s32[8]{0:T(128)S(1)} %stack.35.where_ref, f32[1536,768]{1,0:T(8,128)S(1)} %bitcast.15, f32[2,128,768]{2,1,0:T(8,128)S(1)} %get-tuple-element.43.refs_0_, s16[272,768]{1,0:T(8,128)(2,1)S(1)} %collective-permute-done.6.refs_1_, f32[2,128,768]{2,1,0:T(8,128)S(1)} %get-tuple-element.52.refs_2_, ...), custom_call_target="tpu_custom_call" | custom-call | flops 1000 | bytes 1000 | tf_op jit(solution)/shard_map/combine/pallas_call | solution.py:410
  (22 shorter events, 0.0 us)
Async XLA Ops:
  0.6 3.8 %copy-start.3 = (s32[1,8,6]{1,0,2:T(1,128)S(1)}, s32[1,8,6]{1,0,2:T(1,128)}, u32[]{:S(2)}) copy-start(s32[1,8,6]{1,0,2:T(1,128)} %param.8) | copy-start | bytes 580
  0.6 28.7 %collective-permute-start.4 = (bf16[8,128,768]{2,1,0:T(8,128)(2,1)}, bf16[8,128,768]{2,1,0:T(8,128)(2,1)}, u32[]{:S(2)}, u32[]{:S(2)}) collective-permute-start(bf16[8,128,768]{2,1,0:T(8,128)(2,1)} %bitcast.17), channel_id=1, source_target_pairs={{0,4},{4,0},{1,5},{5,1},{2,6},{6,2},{3,7},{7,3},{8,12},{12,8},{9,1... | collective-permute-start | bytes 4718600 | tf_op jit(solution)/shard_map/ppermute | solution.py:508
  0.7 1.4 %copy-start = (bf16[1,8,1536,64]{2,3,1,0:T(8,128)(2,1)S(1)}, bf16[1,8,1536,64]{2,3,1,0:T(8,128)(2,1)}, u32[]{:S(2)}) copy-start(bf16[1,8,1536,64]{2,3,1,0:T(8,128)(2,1)} %param.5) | copy-start | bytes 4718596
  2.3 20.0 %collective-permute-start = (bf16[4,64,1536]{2,1,0:T(8,128)(2,1)S(1)}, bf16[4,64,1536]{2,1,0:T(8,128)(2,1)S(1)}, u32[]{:S(2)}, u32[]{:S(2)}) collective-permute-start(bf16[4,64,1536]{2,1,0:T(8,128)(2,1)S(1)} %get-tuple-element.54.refs_0_), channel_id=1, source_target_pairs={{0,1},{1,0},{2,3},{3,2},{4,5},{5,4},{6,7},{7,6},{8,9},{9,8},{10,11... | collective-permute-start | bytes 2359304 | tf_op jit(solution)/shard_map/ppermute | solution.py:502
  2.3 20.0 %collective-permute-start.1 = (bf16[4,64,1536]{2,1,0:T(8,128)(2,1)S(1)}, bf16[4,64,1536]{2,1,0:T(8,128)(2,1)S(1)}, u32[]{:S(2)}, u32[]{:S(2)}) collective-permute-start(bf16[4,64,1536]{2,1,0:T(8,128)(2,1)S(1)} %get-tuple-element.36.refs_2_), channel_id=1, source_target_pairs={{0,2},{1,3},{2,0},{3,1},{4,6},{5,7},{6,4},{7,5},{8,10},{9,11},{10,... | collective-permute-start | bytes 2359304 | tf_op jit(solution)/shard_map/ppermute | solution.py:502
  23.3 15.5 %collective-permute-start.2 = (bf16[2,4,64,512]{3,2,1,0:T(8,128)(2,1)S(1)}, bf16[2,4,64,512]{3,2,1,0:T(8,128)(2,1)S(1)}, u32[]{:S(2)}, u32[]{:S(2)}) collective-permute-start(bf16[2,4,64,512]{3,2,1,0:T(8,128)(2,1)S(1)} %get-tuple-element.37), channel_id=1, source_target_pairs={{0,2},{1,3},{2,0},{3,1},{4,6},{5,7},{6,4},{7,5},{8,10},{9,11},{10,... | collective-permute-start | bytes 1572872 | tf_op jit(solution)/shard_map/ppermute | solution.py:502
  25.0 15.3 %collective-permute-start.3 = (bf16[2,4,64,512]{3,2,1,0:T(8,128)(2,1)S(1)}, bf16[2,4,64,512]{3,2,1,0:T(8,128)(2,1)S(1)}, u32[]{:S(2)}, u32[]{:S(2)}) collective-permute-start(bf16[2,4,64,512]{3,2,1,0:T(8,128)(2,1)S(1)} %get-tuple-element.38), channel_id=1, source_target_pairs={{0,1},{1,0},{2,3},{3,2},{4,5},{5,4},{6,7},{7,6},{8,9},{9,8},{10,11... | collective-permute-start | bytes 1572872 | tf_op jit(solution)/shard_map/ppermute | solution.py:502
  27.4 22.0 %collective-permute-start.7 = (bf16[2,4,64,512]{3,2,1,0:T(8,128)(2,1)S(1)}, bf16[2,4,64,512]{3,2,1,0:T(8,128)(2,1)S(1)}, u32[]{:S(2)}, u32[]{:S(2)}) collective-permute-start(bf16[2,4,64,512]{3,2,1,0:T(8,128)(2,1)S(1)} %get-tuple-element.46), channel_id=1, source_target_pairs={{0,2},{1,3},{2,0},{3,1},{4,6},{5,7},{6,4},{7,5},{8,10},{9,11},{10,... | collective-permute-start | bytes 1572872 | tf_op jit(solution)/shard_map/ppermute | solution.py:502
  28.0 3.1 %copy-start.1 = (bf16[1,8,128,768]{3,2,1,0:T(8,128)(2,1)S(1)}, bf16[1,8,128,768]{3,2,1,0:T(8,128)(2,1)}, u32[]{:S(2)}) copy-start(bf16[1,8,128,768]{3,2,1,0:T(8,128)(2,1)} %param.6) | copy-start | bytes 4718596
  28.0 23.1 %collective-permute-start.8 = (bf16[2,4,64,512]{3,2,1,0:T(8,128)(2,1)S(1)}, bf16[2,4,64,512]{3,2,1,0:T(8,128)(2,1)S(1)}, u32[]{:S(2)}, u32[]{:S(2)}) collective-permute-start(bf16[2,4,64,512]{3,2,1,0:T(8,128)(2,1)S(1)} %get-tuple-element.47), channel_id=1, source_target_pairs={{0,1},{1,0},{2,3},{3,2},{4,5},{5,4},{6,7},{7,6},{8,9},{9,8},{10,11... | collective-permute-start | bytes 1572872 | tf_op jit(solution)/shard_map/ppermute | solution.py:502
  29.3 52.6 %collective-permute-start.11 = (bf16[2,4,64,512]{3,2,1,0:T(8,128)(2,1)S(1)}, bf16[2,4,64,512]{3,2,1,0:T(8,128)(2,1)S(1)}, u32[]{:S(2)}, u32[]{:S(2)}) collective-permute-start(bf16[2,4,64,512]{3,2,1,0:T(8,128)(2,1)S(1)} %get-tuple-element.55), channel_id=1, source_target_pairs={{0,2},{1,3},{2,0},{3,1},{4,6},{5,7},{6,4},{7,5},{8,10},{9,11},{10,... | collective-permute-start | bytes 1572872 | tf_op jit(solution)/shard_map/ppermute | solution.py:502
  31.1 2.2 %copy-start.2 = (s32[1,8,12]{2,1,0:T(8,128)S(1)}, s32[1,8,12]{2,1,0:T(8,128)}, u32[]{:S(2)}) copy-start(s32[1,8,12]{2,1,0:T(8,128)} %param.7) | copy-start | bytes 1156
  38.7 43.2 %collective-permute-start.12 = (bf16[2,4,64,512]{3,2,1,0:T(8,128)(2,1)S(1)}, bf16[2,4,64,512]{3,2,1,0:T(8,128)(2,1)S(1)}, u32[]{:S(2)}, u32[]{:S(2)}) collective-permute-start(bf16[2,4,64,512]{3,2,1,0:T(8,128)(2,1)S(1)} %get-tuple-element.56), channel_id=1, source_target_pairs={{0,1},{1,0},{2,3},{3,2},{4,5},{5,4},{6,7},{7,6},{8,9},{9,8},{10,11... | collective-permute-start | bytes 1572872 | tf_op jit(solution)/shard_map/ppermute | solution.py:502
  42.4 14.4 %collective-permute-start.5 = (s16[272,768]{1,0:T(8,128)(2,1)S(1)}, s16[272,768]{1,0:T(8,128)(2,1)S(1)}, u32[]{:S(2)}, u32[]{:S(2)}) collective-permute-start(s16[272,768]{1,0:T(8,128)(2,1)S(1)} %get-tuple-element.42), channel_id=1, source_target_pairs={{0,8},{8,0},{16,24},{24,16},{1,9},{9,1},{17,25},{25,17},{2,10},{10... | collective-permute-start | bytes 1253384 | tf_op jit(solution)/shard_map/ppermute | solution.py:489
  51.1 28.6 %slice-start = ((s8[4718592]{0:T(1024)(128)(4,1)}), s8[4194304]{0:T(1024)(128)(4,1)S(1)}, s32[]{:S(2)}) async-start(s8[4718592]{0:T(1024)(128)(4,1)} %bitcast.14), calls=%async_computation | async-start | bytes 8388608
  51.1 28.6 %slice-start.1 = ((s8[4718592]{0:T(1024)(128)(4,1)}), s8[524288]{0:T(1024)(128)(4,1)S(1)}, s32[]{:S(2)}) async-start(s8[4718592]{0:T(1024)(128)(4,1)} %bitcast.14), calls=%async_computation.1 | async-start | bytes 1048576
  53.3 14.4 %collective-permute-start.13 = (s16[144,768]{1,0:T(8,128)(2,1)S(1)}, s16[144,768]{1,0:T(8,128)(2,1)S(1)}, u32[]{:S(2)}, u32[]{:S(2)}) collective-permute-start(s16[144,768]{1,0:T(8,128)(2,1)S(1)} %get-tuple-element.58.mine_ref), channel_id=1, source_target_pairs={{0,8},{1,9},{6,14},{7,15},{8,0},{9,1},{14,6},{15,7},{16,24},{17,25... | collective-permute-start | bytes 663560 | tf_op jit(solution)/shard_map/ppermute | solution.py:486
  67.9 11.9 %collective-permute-start.14 = (s16[144,768]{1,0:T(8,128)(2,1)S(1)}, s16[144,768]{1,0:T(8,128)(2,1)S(1)}, u32[]{:S(2)}, u32[]{:S(2)}) collective-permute-start(s16[144,768]{1,0:T(8,128)(2,1)S(1)} %add_coded.1.one_ref), channel_id=1, source_target_pairs={{0,16},{1,17},{6,22},{7,23},{8,24},{9,25},{14,30},{15,31},{16,0},{... | collective-permute-start | bytes 663560 | tf_op jit(solution)/shard_map/ppermute | solution.py:486
  69.8 14.4 %collective-permute-start.9 = (s16[272,768]{1,0:T(8,128)(2,1)S(1)}, s16[272,768]{1,0:T(8,128)(2,1)S(1)}, u32[]{:S(2)}, u32[]{:S(2)}) collective-permute-start(s16[272,768]{1,0:T(8,128)(2,1)S(1)} %get-tuple-element.51), channel_id=1, source_target_pairs={{0,8},{8,0},{16,24},{24,16},{1,9},{9,1},{17,25},{25,17},{2,10},{10... | collective-permute-start | bytes 1253384 | tf_op jit(solution)/shard_map/ppermute | solution.py:489
  69.9 35.5 %collective-permute-start.6 = (s16[272,768]{1,0:T(8,128)(2,1)S(1)}, s16[272,768]{1,0:T(8,128)(2,1)S(1)}, u32[]{:S(2)}, u32[]{:S(2)}) collective-permute-start(s16[272,768]{1,0:T(8,128)(2,1)S(1)} %get-tuple-element.44), channel_id=1, source_target_pairs={{1,17},{2,18},{4,20},{7,23},{9,25},{10,26},{12,28},{15,31},{16,0},... | collective-permute-start | bytes 1253384 | tf_op jit(solution)/shard_map/ppermute | solution.py:499
  80.6 4.6 %collective-permute-start.15 = (f32[6,128,128]{2,1,0:T(8,128)S(1)}, f32[6,128,128]{2,1,0:T(8,128)S(1)}, u32[]{:S(2)}, u32[]{:S(2)}) collective-permute-start(f32[6,128,128]{2,1,0:T(8,128)S(1)} %pivots.1.own_ref), channel_id=1, source_target_pairs={{0,4},{1,5},{6,2},{7,3},{8,12},{9,13},{14,10},{15,11},{16,20},{17,... | collective-permute-start | bytes 1179656 | tf_op jit(solution)/shard_map/ppermute | solution.py:486
  84.1 10.5 %collective-permute-start.16 = (s16[272,768]{1,0:T(8,128)(2,1)S(1)}, s16[272,768]{1,0:T(8,128)(2,1)S(1)}, u32[]{:S(2)}, u32[]{:S(2)}) collective-permute-start(s16[272,768]{1,0:T(8,128)(2,1)S(1)} %get-tuple-element.61), channel_id=1, source_target_pairs={{0,8},{8,0},{16,24},{24,16},{1,9},{9,1},{17,25},{25,17},{2,10},{10... | collective-permute-start | bytes 1253384 | tf_op jit(solution)/shard_map/ppermute | solution.py:489
  85.1 20.2 %collective-permute-start.10 = (s16[144,768]{1,0:T(8,128)(2,1)S(1)}, s16[144,768]{1,0:T(8,128)(2,1)S(1)}, u32[]{:S(2)}, u32[]{:S(2)}) collective-permute-start(s16[144,768]{1,0:T(8,128)(2,1)S(1)} %get-tuple-element.53), channel_id=1, source_target_pairs={{0,16},{1,17},{2,18},{3,19},{4,20},{5,21},{6,22},{7,23},{8,24},{9,... | collective-permute-start | bytes 663560 | tf_op jit(solution)/shard_map/ppermute | solution.py:499
  95.4 13.7 %collective-permute-start.17 = (s16[272,768]{1,0:T(8,128)(2,1)S(1)}, s16[272,768]{1,0:T(8,128)(2,1)S(1)}, u32[]{:S(2)}, u32[]{:S(2)}) collective-permute-start(s16[272,768]{1,0:T(8,128)(2,1)S(1)} %get-tuple-element.65), channel_id=1, source_target_pairs={{0,16},{3,19},{5,21},{6,22},{8,24},{11,27},{13,29},{14,30},{17,1},... | collective-permute-start | bytes 1253384 | tf_op jit(solution)/shard_map/ppermute | solution.py:499

commit v8 on v7

--- a/solution.py
+++ b/solution.py
@@ -16,6 +16,7 @@
 EXP_STEPS = 128.0
 EXP_ROWS = 16
 HALF_STEPS = 48
+LU = 10
 NEAR = 10
 FAR = 10
 
@@ -71,48 +72,21 @@
         ref[:, top + 8 :, :] = jnp.where(lanes == j, factor, rest - factor * used)
 
 
-def lu_kernel(until, where_ref, own_ref, other_ref, out_ref):
-    held = where_ref[1] == where_ref[3]
-
-    @pl.when(held)
-    def _():
-        out_ref[...] = own_ref[...]
-
-    @pl.when(jnp.logical_not(held))
-    def _():
-        out_ref[...] = other_ref[...]
-
-    for j in range(until):
+def lu_kernel(begin, end, in_ref, out_ref):
+    out_ref[...] = in_ref[...]
+    for j in range(begin, end):
         lu_step(out_ref, j)
 
 
-def factor(where, own, other, until):
-    return pl.pallas_call(
-        functools.partial(lu_kernel, until),
-        out_shape=jax.ShapeDtypeStruct(own.shape, jnp.float32),
-        in_specs=[SMEM, VMEM, VMEM],
-        out_specs=VMEM,
-        compiler_params=params(),
-        cost_estimate=cost(10),
-        name="factor",
-    )(where, own, other)
-
-
-def rest_kernel(begin, in_ref, out_ref):
-    out_ref[...] = in_ref[...]
-    for j in range(begin, out_ref.shape[1]):
-        lu_step(out_ref, j)
-
-
-def factor_rest(blocks, begin):
-    return pl.pallas_call(
-        functools.partial(rest_kernel, begin),
+def factor(blocks, begin, end):
+    return pl.pallas_call(
+        functools.partial(lu_kernel, begin, end),
         out_shape=jax.ShapeDtypeStruct(blocks.shape, jnp.float32),
         in_specs=[VMEM],
         out_specs=VMEM,
         compiler_params=params(),
-        cost_estimate=cost(10),
-        name="factor_rest",
+        cost_estimate=cost(LU),
+        name="factor",
     )(blocks)
 
 
@@ -287,14 +261,14 @@
     acc[...] = (before_ref[...] + total.reshape(before_ref.shape)).reshape(acc.shape)
     first = [(m, number) for m, (phase, number) in enumerate(chunk) if phase == 0]
     if first:
-        diag_ref = refs[4 + earlier]
-        if earlier:
-            diag_ref[...] = refs[2][...]
         for part in range(2):
+            diag_ref = refs[4 + earlier + part]
+            if earlier:
+                diag_ref[...] = refs[2 + part][...]
             for m, number in first:
                 q = part * blocks + number
-                lanes = slice(q * BLK, (q + 1) * BLK)
-                encode(diag_ref.at[:, lanes], [acc[part, m, :, lanes]])
+                at = slice(number * BLK, (number + 1) * BLK)
+                encode(diag_ref.at[:, at], [acc[part, m, :, q * BLK : (q + 1) * BLK]])
     mine = where_ref[0] & 1
     for m in range(count):
         kept_ref[m] = acc[mine, m]
@@ -309,7 +283,7 @@
         jax.ShapeDtypeStruct((count * BLK + EXP_ROWS, cols), jnp.int16),
     ]
     if any(phase == 0 for phase, _ in chunk):
-        shapes.append(jax.ShapeDtypeStruct((BLK + EXP_ROWS, cols), jnp.int16))
+        shapes += [jax.ShapeDtypeStruct((BLK + EXP_ROWS, cols // 2), jnp.int16)] * 2
     return pl.pallas_call(
         functools.partial(far_kernel, chunk, blocks, len(earlier)),
         out_shape=shapes,
@@ -361,6 +335,30 @@
     )(where, kept, got)
 
 
+def pick_kernel(where_ref, mine_ref, got_ref, out_ref):
+    held = where_ref[1] == where_ref[3]
+
+    @pl.when(held)
+    def _():
+        out_ref[...] = mine_ref[...]
+
+    @pl.when(jnp.logical_not(held))
+    def _():
+        out_ref[...] = got_ref[...]
+
+
+def pick(where, mine, got):
+    return pl.pallas_call(
+        pick_kernel,
+        out_shape=jax.ShapeDtypeStruct(mine.shape, mine.dtype),
+        in_specs=[SMEM] + [VMEM] * 2,
+        out_specs=VMEM,
+        compiler_params=params(),
+        cost_estimate=cost(0),
+        name="pick",
+    )(where, mine, got)
+
+
 def add_kernel(mine_ref, got_ref, out_ref):
     encode(out_ref, [decode(mine_ref) + decode(got_ref)])
 
@@ -378,11 +376,25 @@
 
 
 def combine_kernel(chunks, where_ref, anc_ref, *refs):
-    out_ref, start, sem = refs[-3:]
+    lu_ref, lu_got_ref = refs[2 * len(chunks) : 2 * len(chunks) + 2]
+    out_ref, diag_ref, start, sem = refs[-4:]
     share = out_ref.shape[0]
     begin = pl.multiple_of(where_ref[0] * share, BLK)
     fetch = pltpu.make_async_copy(anc_ref.at[pl.ds(begin, share)], start, sem)
     fetch.start()
+    held = where_ref[1] == where_ref[3]
+    size = lu_ref.shape[0]
+
+    @pl.when(held)
+    def _():
+        diag_ref[:size] = lu_ref[...]
+        diag_ref[size:] = lu_got_ref[...]
+
+    @pl.when(jnp.logical_not(held))
+    def _():
+        diag_ref[:size] = lu_got_ref[...]
+        diag_ref[size:] = lu_ref[...]
+
     fetch.wait()
 
     def fill(wanted):
@@ -404,14 +416,17 @@
         fill(1)
 
 
-def combine(where, anc, pairs, chunks, share):
-    parts = [part for pair in pairs for part in pair]
+def combine(where, anc, pairs, lu, lu_got, chunks, share):
+    parts = [part for pair in pairs for part in pair] + [lu, lu_got]
     cols = anc.shape[1]
     return pl.pallas_call(
         functools.partial(combine_kernel, chunks),
-        out_shape=jax.ShapeDtypeStruct((share, cols), jnp.float32),
+        out_shape=[
+            jax.ShapeDtypeStruct((share, cols), jnp.float32),
+            jax.ShapeDtypeStruct((2 * lu.shape[0], BLK, BLK), jnp.float32),
+        ],
         in_specs=[SMEM, ANY] + [VMEM] * len(parts),
-        out_specs=VMEM,
+        out_specs=[VMEM] * 2,
         scratch_shapes=[pltpu.VMEM((share, cols), jnp.float32), pltpu.SemaphoreType.DMA],
         compiler_params=params(),
         cost_estimate=cost(0),
@@ -419,31 +434,59 @@
     )(where, anc, *parts)
 
 
-def pivot_kernel(where_ref, anc_ref, one_ref, two_ref, out_ref, blocks, sems):
-    count = out_ref.shape[0]
+def diagonal_copies(where_ref, anc_ref, out_ref, sems, first):
     copies = []
-    for q in range(count):
+    for i in range(out_ref.shape[0]):
+        q = first + i
         rows = pl.ds(pl.multiple_of(where_ref[4] + q * BLK, BLK), BLK)
         copies.append(
             pltpu.make_async_copy(
-                anc_ref.at[rows, q * BLK : (q + 1) * BLK], blocks.at[q], sems.at[q]
+                anc_ref.at[rows, q * BLK : (q + 1) * BLK], out_ref.at[i], sems.at[i]
             )
         )
+    return copies
+
+
+def later_kernel(where_ref, anc_ref, out_ref, sems):
+    copies = diagonal_copies(where_ref, anc_ref, out_ref, sems, out_ref.shape[0])
+    for copy in copies:
+        copy.start()
+    for copy in copies:
+        copy.wait()
+
+
+def later_blocks(where, anc, count):
+    return pl.pallas_call(
+        later_kernel,
+        out_shape=jax.ShapeDtypeStruct((count, BLK, BLK), jnp.float32),
+        in_specs=[SMEM, ANY],
+        out_specs=VMEM,
+        scratch_shapes=[pltpu.SemaphoreType.DMA((count,))],
+        compiler_params=params(),
+        cost_estimate=cost(0),
+        name="later_blocks",
+    )(where, anc)
+
+
+def pivot_kernel(where_ref, anc_ref, given_ref, one_ref, two_ref, out_ref, blocks, sems):
+    copies = diagonal_copies(where_ref, anc_ref, blocks, sems, 0)
     for copy in copies:
         copy.start()
     total = decode(one_ref) + decode(two_ref)
     for copy in copies:
         copy.wait()
-    for q in range(count):
-        out_ref[q] = blocks[q] - total[:, q * BLK : (q + 1) * BLK]
-
-
-def pivots(where, anc, one, two):
-    count = one.shape[1] // BLK
+    held = where_ref[1] == where_ref[3]
+    for q in range(out_ref.shape[0]):
+        block = jnp.where(held, blocks[q], given_ref[q])
+        out_ref[q] = block - total[:, q * BLK : (q + 1) * BLK]
+
+
+def pivots(where, anc, given, one, two):
+    count = given.shape[0]
     return pl.pallas_call(
         pivot_kernel,
         out_shape=jax.ShapeDtypeStruct((count, BLK, BLK), jnp.float32),
-        in_specs=[SMEM, ANY, VMEM, VMEM],
+        in_specs=[SMEM, ANY] + [VMEM] * 3,
         out_specs=VMEM,
         scratch_shapes=[
             pltpu.VMEM((count, BLK, BLK), jnp.float32),
@@ -452,7 +495,7 @@
         compiler_params=params(),
         cost_estimate=cost(0),
         name="pivots",
-    )(where, anc, one, two)
+    )(where, anc, given, one, two)
 
 
 def xor_perm(size, bit):
@@ -481,12 +524,14 @@
     def index(l, r, c):
         return (l * rows + r) * cols + c
 
-    def holders(value, target):
-        perm = [(index(*p), index(*target(*p))) for p in spots if p[1] == p[2] // per_group]
+    def to_other_core(value):
+        perm = [
+            (index(l, r, c), index(l, 1 - r, c)) for l, r, c in spots if r == c // per_group
+        ]
         return lax.ppermute(value, everyone, perm)
 
-    def near_layers(value):
-        return lax.ppermute(value, "layer", xor_perm(layers, 1))
+    def over_layers(value, bit):
+        return lax.ppermute(value, "layer", xor_perm(layers, bit))
 
     def far_layers(value, chunk):
         phases = {phase for phase, _ in chunk}
@@ -510,9 +555,10 @@
     whole = (a, xa, b, yb)
     rounds = [(phase, number) for phase in range(2) for number in range(blocks)]
     chunks = [rounds[n : n + 2] for n in range(0, len(rounds), 2)]
+    given = to_other_core(later_blocks(where, after(anc, a), blocks))
     sides = []
     for chunk in chunks:
-        ready = (after(a, *sides[-1]) if sides else a, xa, b, yb)
+        ready = (after(a, *(sides[-1] if sides else [given, near_right])), xa, b, yb)
         sides.append(split(where, ready, chunk, blocks))
     others = [(over(one, 2), over(two, 1)) for one, two in sides]
     masks = lpat[0]
@@ -523,26 +569,27 @@
         part = after(parts[j], *waits) if waits else parts[j]
         return far_update(where, masks, others[j], far_right, part, known, chunks[j], blocks)
 
-    kept0, coded0, diag = far_part(0)
-    known = [diag]
-    sum0, sent0 = halve(where, kept0, near_layers(coded0), chunks[0])
-    kept1, coded1, diag = far_part(1, kept0, parts[2])
+    kept0, coded0, *diag = far_part(0)
+    known = diag
+    sum0, sent0 = halve(where, kept0, over_layers(coded0, 1), chunks[0])
+    kept1, coded1, *diag = far_part(1, kept0, parts[2])
     known = []
-    near = add_coded(after(diag, sent0), holders(diag, lambda l, r, c: (l ^ 1, r, c)))
-    far = holders(near, lambda l, r, c: (l ^ 2, r, c))
-    own = pivots(where, anc, near, far)
-    other = holders(own, lambda l, r, c: (l, 1 - r, c))
+    mine = pick(where, diag[0], to_other_core(diag[1]))
+    near = add_coded(after(mine, sent0), over_layers(mine, 1))
+    far = over_layers(near, 2)
+    own = pivots(where, anc, given, near, far)
     kept2, coded2 = far_part(2, near, sent0)
-    sum1, sent1 = halve(where, kept1, near_layers(coded1), chunks[1])
-    half_lu = factor(where, after(own, sent1, coded2), other, HALF_STEPS)
-    sum2, sent2 = halve(where, after(kept2, half_lu), near_layers(coded2), chunks[2])
-    diag_lu = factor_rest(after(half_lu, sent2), HALF_STEPS)
+    sum1, sent1 = halve(where, kept1, over_layers(coded1, 1), chunks[1])
+    half_lu = factor(after(own, sent1, coded2), 0, HALF_STEPS)
+    sum2, sent2 = halve(where, after(kept2, half_lu), over_layers(coded2, 1), chunks[2])
+    lu = factor(after(half_lu, sent2), HALF_STEPS, BLK)
+    lu_got = lax.ppermute(lu, "row", xor_perm(rows, 1))
     pairs = [
         (sum0, far_layers(sent0, chunks[0])),
         (sum1, far_layers(sent1, chunks[1])),
-        (after(sum2, diag_lu), far_layers(sent2, chunks[2])),
+        (sum2, far_layers(sent2, chunks[2])),
     ]
-    return combine(where, anc, pairs, chunks, share), diag_lu
+    return tuple(combine(where, anc, pairs, lu, lu_got, chunks, share))
 
 
 def mask_rows(panel, pattern, block):
@@ -583,8 +630,7 @@
     pivot_blocks = candidates(anc) - lax.psum(candidates(update), "layer")
     both = lax.all_gather(pivot_blocks, "row", axis=0)
     chosen = lax.dynamic_index_in_dim(both, lax.axis_index("col") // per_group, 0, keepdims=False)
-    where = jnp.zeros((6,), jnp.int32)
-    diag_lu = factor(where, chosen, chosen, BLK)
+    diag_lu = factor(chosen, 0, BLK)
     summed = lax.psum_scatter(update, "layer", scatter_dimension=0, tiled=True)
     mine = lax.dynamic_slice_in_dim(anc, lax.axis_index("layer") * share, share, 0)
     return mine - summed, diag_lu

time: 112 us -> 110 us (0.982)
  waiting for transfers between devices: 47.7 us -> 41.5 us
  local copies, waits for them, and re-layouts: 1.58 us -> 5.33 us
  starting transfers between devices: 24.5 us -> 26.7 us
  Pallas kernels: 36.5 us -> 34.8 us
    ppermute x8, waiting for transfers between devices: 24.9 us -> 18.6 us  [over(): return lax.ppermute(value, 'col', xor_perm(cols, bit))]
    ppermute x6 -> x8, starting transfers between devices: 8.56 us -> 12.8 us  [the longest x5 8.08 us: over_layers(): return lax.ppermute(value, 'layer', xor_perm(layers, bit))]
    unnamed x13 -> x15, local copies, waits for them, and re-layouts: 1.5 us -> 5.25 us
    ppermute x3, starting transfers between devices: 6.21 us -> 4.07 us  [far_layers(): return lax.ppermute(value, everyone, perm)]
    pallas_call x3 -> x5, Pallas kernels: 16.1 us -> 14.8 us  [the longest x2 11.4 us: factor(): pl.pallas_call(functools.partial(lu_kernel, begin, end), out_shape=jax.Sh...]
    ppermute x6 -> x8, waiting for transfers between devices: 19.1 us -> 18.4 us  [the longest x5 16.4 us: over_layers(): return lax.ppermute(value, 'layer', xor_perm(layers, bit))]
  transfers between devices with their start and end apart: 18 -> 20, of which waited for: 8 -> 11; matrix products, arithmetic and copies ran while one was open for 0% -> 0% of each run, Pallas kernels for 31% -> 29%
where the time goes in v8:
time: 110 us; the launch traced here: 109 us
  waiting for transfers between devices  41.5 us (38%)
  Pallas kernels  34.8 us (32%)
  starting transfers between devices  26.7 us (24%)
  local copies, waits for them, and re-layouts  5.33 us (5%)
    ppermute x8, waiting for transfers between devices, over(): return lax.ppermute(value, 'col', xor_perm(cols, bit))  18.6 us
    ppermute x5, waiting for transfers between devices, over_layers(): return lax.ppermute(value, 'layer', xor_perm(layers, bit))  16.4 us
    pallas_call x2, Pallas kernels, factor(): pl.pallas_call(functools.partial(lu_kernel, begin, end), out_shape=jax.Sh...  11.4 us
    ppermute x8, starting transfers between devices, over(): return lax.ppermute(value, 'col', xor_perm(cols, bit))  9.76 us
    ppermute x5, starting transfers between devices, over_layers(): return lax.ppermute(value, 'layer', xor_perm(layers, bit))  8.08 us
    pallas_call x3, Pallas kernels, far_update(): pl.pallas_call(functools.partial(far_kernel, chunk, blocks, len(earlier))...  6.34 us
    pallas_call x3, Pallas kernels, near_update(): pl.pallas_call(functools.partial(near_kernel, chunk, blocks), out_shape=j...  5.4 us
    unnamed x15, local copies, waits for them, and re-layouts  5.25 us
  transfers between devices with their start and end apart: 20, of which 11 were waited for; matrix products, arithmetic and copies ran while one was open for 0% of the time, Pallas kernels for 29%

profile of v8, /device:TPU:2, one launch (start us, length us, event | category | flops | bytes accessed | tf_op | source)
XLA Modules:
  0.0 109.5 jit_solution(14632659163263390566)
XLA Ops:
  0.7 1.4 %copy-done.1 = bf16[1,8,1536,64]{2,3,1,0:T(8,128)(2,1)S(1)} copy-done((bf16[1,8,1536,64]{2,3,1,0:T(8,128)(2,1)S(1)}, bf16[1,8,1536,64]{2,3,1,0:T(8,128)(2,1)}, u32[]{:S(2)}) %copy-start.1) | copy-done | bytes 1572888
  2.3 2.0 %collective-permute-start.3 = (bf16[4,64,1536]{2,1,0:T(8,128)(2,1)S(1)}, bf16[4,64,1536]{2,1,0:T(8,128)(2,1)S(1)}, u32[]{:S(2)}, u32[]{:S(2)}) collective-permute-start(bf16[4,64,1536]{2,1,0:T(8,128)(2,1)S(1)} %get-tuple-element.42.refs_2_), channel_id=1, source_target_pairs={{0,2},{1,3},{2,0},{3,1},{4,6},{5,7},{6,4},{7,5},{8,10},{9,11},{10,... | collective-permute-start | bytes 2359304 | tf_op jit(solution)/shard_map/ppermute | solution.py:547
  4.5 2.3 %copy-done = f32[1536,768]{1,0:T(8,128)S(1)} copy-done((f32[1536,768]{1,0:T(8,128)S(1)}, f32[1536,768]{1,0:T(8,128)}, u32[]{:S(2)}) %copy-start) | copy-done | bytes 4718616
  6.8 0.6 later_blocks.1
  7.4 1.8 %collective-permute-start = (f32[3,128,128]{2,1,0:T(8,128)S(1)}, f32[3,128,128]{2,1,0:T(8,128)S(1)}, u32[]{:S(2)}, u32[]{:S(2)}) collective-permute-start(f32[3,128,128]{2,1,0:T(8,128)S(1)} %later_blocks.1), channel_id=1, source_target_pairs={{0,4},{1,5},{6,2},{7,3},{8,12},{9,13},{14,10},{15,11},{16,20},{17,... | collective-permute-start | bytes 589832 | tf_op jit(solution)/shard_map/ppermute | solution.py:531
  9.4 1.4 %copy-done.2 = bf16[1,8,128,768]{3,2,1,0:T(8,128)(2,1)S(1)} copy-done((bf16[1,8,128,768]{3,2,1,0:T(8,128)(2,1)S(1)}, bf16[1,8,128,768]{3,2,1,0:T(8,128)(2,1)}, u32[]{:S(2)}) %copy-start.2) | copy-done | bytes 1572888
  10.8 2.2 %masked_right.1 = (bf16[8,128,768]{2,1,0:T(8,128)(2,1)S(1)}, bf16[8,128,768]{2,1,0:T(8,128)(2,1)S(1)}) custom-call(s32[8]{0:T(128)S(1)} %stack.35.where_ref, s32[8,6]{1,0:T(8,128)S(1)} %bitcast.19, bf16[8,128,768]{2,1,0:T(8,128)(2,1)S(1)} %bitcast.18, bf16[8,128,768]{2,1,0:T(8,128)(2,1)} %collective-permute-done.1.uo_ref), custom_call_target="tpu_custom_call" | custom-call | flops 1000 | bytes 1000 | tf_op jit(solution)/shard_map/masked_right/pallas_call | solution.py:195
  13.0 9.3 %collective-permute-done.2.refs_1_ = bf16[4,64,1536]{2,1,0:T(8,128)(2,1)S(1)} collective-permute-done((bf16[4,64,1536]{2,1,0:T(8,128)(2,1)S(1)}, bf16[4,64,1536]{2,1,0:T(8,128)(2,1)S(1)}, u32[]{:S(2)}, u32[]{:S(2)}) %collective-permute-start.2) | collective-permute-done | bytes 786464 | tf_op jit(solution)/shard_map/ppermute | solution.py:547
  22.3 0.9 split.3
  23.3 1.8 %collective-permute-start.4 = (bf16[2,4,64,512]{3,2,1,0:T(8,128)(2,1)S(1)}, bf16[2,4,64,512]{3,2,1,0:T(8,128)(2,1)S(1)}, u32[]{:S(2)}, u32[]{:S(2)}) collective-permute-start(bf16[2,4,64,512]{3,2,1,0:T(8,128)(2,1)S(1)} %get-tuple-element.43), channel_id=1, source_target_pairs={{0,2},{1,3},{2,0},{3,1},{4,6},{5,7},{6,4},{7,5},{8,10},{9,11},{10,... | collective-permute-start | bytes 1572872 | tf_op jit(solution)/shard_map/ppermute | solution.py:547
  25.0 1.5 %collective-permute-start.5 = (bf16[2,4,64,512]{3,2,1,0:T(8,128)(2,1)S(1)}, bf16[2,4,64,512]{3,2,1,0:T(8,128)(2,1)S(1)}, u32[]{:S(2)}, u32[]{:S(2)}) collective-permute-start(bf16[2,4,64,512]{3,2,1,0:T(8,128)(2,1)S(1)} %get-tuple-element.44), channel_id=1, source_target_pairs={{0,1},{1,0},{2,3},{3,2},{4,5},{5,4},{6,7},{7,6},{8,9},{9,8},{10,11... | collective-permute-start | bytes 1572872 | tf_op jit(solution)/shard_map/ppermute | solution.py:547
  26.5 0.9 split.4
  27.4 0.6 collective-permute-start.8
  28.4 0.9 split.5
  29.3 1.8 %collective-permute-start.12 = (bf16[2,4,64,512]{3,2,1,0:T(8,128)(2,1)S(1)}, bf16[2,4,64,512]{3,2,1,0:T(8,128)(2,1)S(1)}, u32[]{:S(2)}, u32[]{:S(2)}) collective-permute-start(bf16[2,4,64,512]{3,2,1,0:T(8,128)(2,1)S(1)} %get-tuple-element.61), channel_id=1, source_target_pairs={{0,2},{1,3},{2,0},{3,1},{4,6},{5,7},{6,4},{7,5},{8,10},{9,11},{10,... | collective-permute-start | bytes 1572872 | tf_op jit(solution)/shard_map/ppermute | solution.py:547
  31.0 1.8 %near_update.4.refs_1_ = f32[4,128,768]{2,1,0:T(8,128)S(1)} custom-call(s32[8]{0:T(128)S(1)} %stack.35.where_ref, s32[8,12]{1,0:T(8,128)S(1)} %bitcast.20, bf16[4,64,1536]{2,1,0:T(8,128)(2,1)S(1)} %get-tuple-element.60.refs_0_, bf16[4,64,1536]{2,1,0:T(8,128)(2,1)S(1)} %collective-permute-done.2.refs_1_, bf16[4,64,1536]{2,1,0:T(8,128)(2,1)S(1)} %get-tuple-element.42.refs_2_, ...), custom_call_target="tpu_custom_call" | custom-call | flops 10000001024 | bytes 1000 | tf_op jit(solution)/shard_map/near_update/pallas_call | solution.py:242
  32.8 1.8 %near_update.5.refs_1_ = f32[4,128,768]{2,1,0:T(8,128)S(1)} custom-call(s32[8]{0:T(128)S(1)} %stack.35.where_ref, s32[8,12]{1,0:T(8,128)S(1)} %bitcast.21, bf16[4,64,1536]{2,1,0:T(8,128)(2,1)S(1)} %get-tuple-element.60.refs_0_, bf16[4,64,1536]{2,1,0:T(8,128)(2,1)S(1)} %collective-permute-done.2.refs_1_, bf16[4,64,1536]{2,1,0:T(8,128)(2,1)S(1)} %get-tuple-element.42.refs_2_, ...), custom_call_target="tpu_custom_call" | custom-call | flops 10000001024 | bytes 1000 | tf_op jit(solution)/shard_map/near_update/pallas_call | solution.py:242
  34.7 1.8 %near_update.3.refs_1_ = f32[4,128,768]{2,1,0:T(8,128)S(1)} custom-call(s32[8]{0:T(128)S(1)} %stack.35.where_ref, s32[8,12]{1,0:T(8,128)S(1)} %bitcast.22, bf16[4,64,1536]{2,1,0:T(8,128)(2,1)S(1)} %get-tuple-element.60.refs_0_, bf16[4,64,1536]{2,1,0:T(8,128)(2,1)S(1)} %collective-permute-done.2.refs_1_, bf16[4,64,1536]{2,1,0:T(8,128)(2,1)S(1)} %get-tuple-element.42.refs_2_, ...), custom_call_target="tpu_custom_call" | custom-call | flops 10000001024 | bytes 1000 | tf_op jit(solution)/shard_map/near_update/pallas_call | solution.py:242
  36.5 1.7 %collective-permute-done.4.a_ref = bf16[2,4,64,512]{3,2,1,0:T(8,128)(2,1)S(1)} collective-permute-done((bf16[2,4,64,512]{3,2,1,0:T(8,128)(2,1)S(1)}, bf16[2,4,64,512]{3,2,1,0:T(8,128)(2,1)S(1)}, u32[]{:S(2)}, u32[]{:S(2)}) %collective-permute-start.4) | collective-permute-done | bytes 524320 | tf_op jit(solution)/shard_map/ppermute | solution.py:547
  38.2 1.7 %collective-permute-start.13 = (bf16[2,4,64,512]{3,2,1,0:T(8,128)(2,1)S(1)}, bf16[2,4,64,512]{3,2,1,0:T(8,128)(2,1)S(1)}, u32[]{:S(2)}, u32[]{:S(2)}) collective-permute-start(bf16[2,4,64,512]{3,2,1,0:T(8,128)(2,1)S(1)} %get-tuple-element.62), channel_id=1, source_target_pairs={{0,1},{1,0},{2,3},{3,2},{4,5},{5,4},{6,7},{7,6},{8,9},{9,8},{10,11... | collective-permute-start | bytes 1572872 | tf_op jit(solution)/shard_map/ppermute | solution.py:547
  39.9 2.1 %far_update.3 = (f32[2,128,768]{2,1,0:T(8,128)S(1)}, s16[272,768]{1,0:T(8,128)(2,1)S(1)}, s16[144,384]{1,0:T(8,128)(2,1)S(1)}, s16[144,384]{1,0:T(8,128)(2,1)S(1)}) custom-call(s32[8]{0:T(128)S(1)} %stack.35.where_ref, s32[8,12]{1,0:T(8,128)S(1)} %bitcast.23, bf16[2,4,64,512]{3,2,1,0:T(8,128)(2,1)S(1)} %collective-permute-done.4.a_ref, ...), custom_call_target="tpu_custom_call" | custom-call | flops 10000001024 | bytes 1000 | tf_op jit(solution)/shard_map/far_update/pallas_call | solution.py:287
  42.0 1.7 %collective-permute-start.6 = (s16[272,768]{1,0:T(8,128)(2,1)S(1)}, s16[272,768]{1,0:T(8,128)(2,1)S(1)}, u32[]{:S(2)}, u32[]{:S(2)}) collective-permute-start(s16[272,768]{1,0:T(8,128)(2,1)S(1)} %get-tuple-element.47), channel_id=1, source_target_pairs={{0,8},{8,0},{16,24},{24,16},{1,9},{9,1},{17,25},{25,17},{2,10},{10... | collective-permute-start | bytes 1253384 | tf_op jit(solution)/shard_map/ppermute | solution.py:534
  43.6 5.8 %collective-permute-done.8.a_ref = bf16[2,4,64,512]{3,2,1,0:T(8,128)(2,1)S(1)} collective-permute-done((bf16[2,4,64,512]{3,2,1,0:T(8,128)(2,1)S(1)}, bf16[2,4,64,512]{3,2,1,0:T(8,128)(2,1)S(1)}, u32[]{:S(2)}, u32[]{:S(2)}) %collective-permute-start.8) | collective-permute-done | bytes 524320 | tf_op jit(solution)/shard_map/ppermute | solution.py:547
  49.4 1.7 %collective-permute-done.9.b_ref = bf16[2,4,64,512]{3,2,1,0:T(8,128)(2,1)S(1)} collective-permute-done((bf16[2,4,64,512]{3,2,1,0:T(8,128)(2,1)S(1)}, bf16[2,4,64,512]{3,2,1,0:T(8,128)(2,1)S(1)}, u32[]{:S(2)}, u32[]{:S(2)}) %collective-permute-start.9) | collective-permute-done | bytes 524320 | tf_op jit(solution)/shard_map/ppermute | solution.py:547
  51.1 2.1 %far_update.4 = (f32[2,128,768]{2,1,0:T(8,128)S(1)}, s16[272,768]{1,0:T(8,128)(2,1)S(1)}, s16[144,384]{1,0:T(8,128)(2,1)S(1)}, s16[144,384]{1,0:T(8,128)(2,1)S(1)}) custom-call(s32[8]{0:T(128)S(1)} %stack.35.where_ref, s32[8,12]{1,0:T(8,128)S(1)} %bitcast.24, bf16[2,4,64,512]{3,2,1,0:T(8,128)(2,1)S(1)} %collective-permute-done.8.a_ref, ...), custom_call_target="tpu_custom_call" | custom-call | flops 10000001024 | bytes 1000 | tf_op jit(solution)/shard_map/far_update/pallas_call | solution.py:287
  53.3 1.3 %collective-permute-start.14 = (s16[144,384]{1,0:T(8,128)(2,1)S(1)}, s16[144,384]{1,0:T(8,128)(2,1)S(1)}, u32[]{:S(2)}, u32[]{:S(2)}) collective-permute-start(s16[144,384]{1,0:T(8,128)(2,1)S(1)} %get-tuple-element.64), channel_id=1, source_target_pairs={{0,4},{1,5},{6,2},{7,3},{8,12},{9,13},{14,10},{15,11},{16,20},{17,... | collective-permute-start | bytes 331784 | tf_op jit(solution)/shard_map/ppermute | solution.py:531
  54.6 0.9 collective-permute-done.14.got_ref
  55.5 0.6 pick.1.mine_ref
  56.1 1.7 %collective-permute-start.15 = (s16[144,384]{1,0:T(8,128)(2,1)S(1)}, s16[144,384]{1,0:T(8,128)(2,1)S(1)}, u32[]{:S(2)}, u32[]{:S(2)}) collective-permute-start(s16[144,384]{1,0:T(8,128)(2,1)S(1)} %pick.1.mine_ref), channel_id=1, source_target_pairs={{0,8},{8,0},{16,24},{24,16},{1,9},{9,1},{17,25},{25,17},{2,10},{10... | collective-permute-start | bytes 331784 | tf_op jit(solution)/shard_map/ppermute | solution.py:534
  57.7 0.4 collective-permute-start.10
  58.2 0.8 halve.3
  59.0 3.0 %collective-permute-done.15.got_ref = s16[144,384]{1,0:T(8,128)(2,1)S(1)} collective-permute-done((s16[144,384]{1,0:T(8,128)(2,1)S(1)}, s16[144,384]{1,0:T(8,128)(2,1)S(1)}, u32[]{:S(2)}, u32[]{:S(2)}) %collective-permute-start.15) | collective-permute-done | bytes 110624 | tf_op jit(solution)/shard_map/ppermute | solution.py:534
  62.1 2.6 %collective-permute-start.16 = (s16[144,384]{1,0:T(8,128)(2,1)S(1)}, s16[144,384]{1,0:T(8,128)(2,1)S(1)}, u32[]{:S(2)}, u32[]{:S(2)}) collective-permute-start(s16[144,384]{1,0:T(8,128)(2,1)S(1)} %add_coded.1.one_ref), channel_id=1, source_target_pairs={{0,16},{8,24},{16,0},{24,8},{1,17},{9,25},{17,1},{25,9},{2,18},{10... | collective-permute-start | bytes 331784 | tf_op jit(solution)/shard_map/ppermute | solution.py:534
  64.8 2.5 %collective-permute-start.7 = (s16[272,768]{1,0:T(8,128)(2,1)S(1)}, s16[272,768]{1,0:T(8,128)(2,1)S(1)}, u32[]{:S(2)}, u32[]{:S(2)}) collective-permute-start(s16[272,768]{1,0:T(8,128)(2,1)S(1)} %get-tuple-element.49), channel_id=1, source_target_pairs={{1,17},{2,18},{4,20},{7,23},{9,25},{10,26},{12,28},{15,31},{16,0},... | collective-permute-start | bytes 1253384 | tf_op jit(solution)/shard_map/ppermute | solution.py:544
  67.3 2.1 %far_update.5 = (f32[2,128,768]{2,1,0:T(8,128)S(1)}, s16[272,768]{1,0:T(8,128)(2,1)S(1)}) custom-call(s32[8]{0:T(128)S(1)} %stack.35.where_ref, s32[8,12]{1,0:T(8,128)S(1)} %bitcast.25, bf16[2,4,64,512]{3,2,1,0:T(8,128)(2,1)S(1)} %collective-permute-done.12.a_ref, bf16[2,4,64,512]{3,2,1,0:T(8,128)(2,1)S(1)} %collective-permute-done.13.b_ref, ...), custom_call_target="tpu_custom_call" | custom-call | flops 10000001024 | bytes 1000 | tf_op jit(solution)/shard_map/far_update/pallas_call | solution.py:287
  69.5 1.7 %collective-permute-start.17 = (s16[272,768]{1,0:T(8,128)(2,1)S(1)}, s16[272,768]{1,0:T(8,128)(2,1)S(1)}, u32[]{:S(2)}, u32[]{:S(2)}) collective-permute-start(s16[272,768]{1,0:T(8,128)(2,1)S(1)} %get-tuple-element.68), channel_id=1, source_target_pairs={{0,8},{8,0},{16,24},{24,16},{1,9},{9,1},{17,25},{25,17},{2,10},{10... | collective-permute-start | bytes 1253384 | tf_op jit(solution)/shard_map/ppermute | solution.py:534
  71.1 6.7 %collective-permute-done.10.got_ref = s16[272,768]{1,0:T(8,128)(2,1)S(1)} collective-permute-done((s16[272,768]{1,0:T(8,128)(2,1)S(1)}, s16[272,768]{1,0:T(8,128)(2,1)S(1)}, u32[]{:S(2)}, u32[]{:S(2)}) %collective-permute-start.10) | collective-permute-done | bytes 417824 | tf_op jit(solution)/shard_map/ppermute | solution.py:534
  77.8 0.9 halve.4
  79.0 0.7 pivots.1.in_ref
  79.7 4.6 %factor.2.in_ref = f32[3,128,128]{2,1,0:T(8,128)S(1)} custom-call(f32[3,128,128]{2,1,0:T(8,128)S(1)} %pivots.1.in_ref), custom_call_target="tpu_custom_call" | custom-call | flops 10000001024 | bytes 1000 | tf_op jit(solution)/shard_map/factor/pallas_call | solution.py:82
  84.3 6.7 %collective-permute-done.17.got_ref = s16[272,768]{1,0:T(8,128)(2,1)S(1)} collective-permute-done((s16[272,768]{1,0:T(8,128)(2,1)S(1)}, s16[272,768]{1,0:T(8,128)(2,1)S(1)}, u32[]{:S(2)}, u32[]{:S(2)}) %collective-permute-start.17) | collective-permute-done | bytes 417824 | tf_op jit(solution)/shard_map/ppermute | solution.py:534
  91.0 0.8 halve.5
  91.8 1.3 %collective-permute-start.18 = (s16[272,768]{1,0:T(8,128)(2,1)S(1)}, s16[272,768]{1,0:T(8,128)(2,1)S(1)}, u32[]{:S(2)}, u32[]{:S(2)}) collective-permute-start(s16[272,768]{1,0:T(8,128)(2,1)S(1)} %get-tuple-element.72), channel_id=1, source_target_pairs={{0,16},{3,19},{5,21},{6,22},{8,24},{11,27},{13,29},{14,30},{17,1},... | collective-permute-start | bytes 1253384 | tf_op jit(solution)/shard_map/ppermute | solution.py:544
  93.1 6.8 %factor.3.refs_6_ = f32[3,128,128]{2,1,0:T(8,128)S(1)} custom-call(f32[3,128,128]{2,1,0:T(8,128)S(1)} %factor.2.in_ref), custom_call_target="tpu_custom_call" | custom-call | flops 10000001024 | bytes 1000 | tf_op jit(solution)/shard_map/factor/pallas_call | solution.py:82
  99.9 1.6 %collective-permute-start.19 = (f32[3,128,128]{2,1,0:T(8,128)S(1)}, f32[3,128,128]{2,1,0:T(8,128)S(1)}, u32[]{:S(2)}, u32[]{:S(2)}) collective-permute-start(f32[3,128,128]{2,1,0:T(8,128)S(1)} %factor.3.refs_6_), channel_id=1, source_target_pairs={{0,4},{4,0},{1,5},{5,1},{2,6},{6,2},{3,7},{7,3},{8,12},{12,8},{9,1... | collective-permute-start | bytes 589832 | tf_op jit(solution)/shard_map/ppermute | solution.py:586
  101.5 1.1 collective-permute-done.19.refs_7_
  102.6 4.5 %collective-permute-done.18.refs_5_ = s16[272,768]{1,0:T(8,128)(2,1)S(1)} collective-permute-done((s16[272,768]{1,0:T(8,128)(2,1)S(1)}, s16[272,768]{1,0:T(8,128)(2,1)S(1)}, u32[]{:S(2)}, u32[]{:S(2)}) %collective-permute-start.18) | collective-permute-done | bytes 417824 | tf_op jit(solution)/shard_map/ppermute | solution.py:544
  107.1 2.2 %combine.1 = (f32[384,768]{1,0:T(8,128)}, f32[6,128,128]{2,1,0:T(8,128)}) custom-call(s32[8]{0:T(128)S(1)} %stack.35.where_ref, f32[1536,768]{1,0:T(8,128)S(1)} %bitcast.15, f32[2,128,768]{2,1,0:T(8,128)S(1)} %get-tuple-element.48.refs_0_, s16[272,768]{1,0:T(8,128)(2,1)S(1)} %collective-permute-done.7.refs_1_, f32[2,128,768]{2,1,0:T(8,128)S(1)} %get-tuple-element.58.refs_2_, ...), custom_call_target="tpu_custom_call" | custom-call | flops 1000 | bytes 1000 | tf_op jit(solution)/shard_map/combine/pallas_call | solution.py:422
  (30 shorter events, 1.3 us)
Async XLA Ops:
  0.6 8.7 %collective-permute-start.1 = (bf16[8,128,768]{2,1,0:T(8,128)(2,1)}, bf16[8,128,768]{2,1,0:T(8,128)(2,1)}, u32[]{:S(2)}, u32[]{:S(2)}) collective-permute-start(bf16[8,128,768]{2,1,0:T(8,128)(2,1)} %bitcast.17), channel_id=1, source_target_pairs={{0,4},{4,0},{1,5},{5,1},{2,6},{6,2},{3,7},{7,3},{8,12},{12,8},{9,1... | collective-permute-start | bytes 4718600 | tf_op jit(solution)/shard_map/ppermute | solution.py:553
  0.7 1.4 %copy-start.1 = (bf16[1,8,1536,64]{2,3,1,0:T(8,128)(2,1)S(1)}, bf16[1,8,1536,64]{2,3,1,0:T(8,128)(2,1)}, u32[]{:S(2)}) copy-start(bf16[1,8,1536,64]{2,3,1,0:T(8,128)(2,1)} %param.5) | copy-start | bytes 4718596
  2.3 20.0 %collective-permute-start.2 = (bf16[4,64,1536]{2,1,0:T(8,128)(2,1)S(1)}, bf16[4,64,1536]{2,1,0:T(8,128)(2,1)S(1)}, u32[]{:S(2)}, u32[]{:S(2)}) collective-permute-start(bf16[4,64,1536]{2,1,0:T(8,128)(2,1)S(1)} %get-tuple-element.60.refs_0_), channel_id=1, source_target_pairs={{0,1},{1,0},{2,3},{3,2},{4,5},{5,4},{6,7},{7,6},{8,9},{9,8},{10,11... | collective-permute-start | bytes 2359304 | tf_op jit(solution)/shard_map/ppermute | solution.py:547
  2.3 20.0 %collective-permute-start.3 = (bf16[4,64,1536]{2,1,0:T(8,128)(2,1)S(1)}, bf16[4,64,1536]{2,1,0:T(8,128)(2,1)S(1)}, u32[]{:S(2)}, u32[]{:S(2)}) collective-permute-start(bf16[4,64,1536]{2,1,0:T(8,128)(2,1)S(1)} %get-tuple-element.42.refs_2_), channel_id=1, source_target_pairs={{0,2},{1,3},{2,0},{3,1},{4,6},{5,7},{6,4},{7,5},{8,10},{9,11},{10,... | collective-permute-start | bytes 2359304 | tf_op jit(solution)/shard_map/ppermute | solution.py:547
  4.5 2.3 %copy-start = (f32[1536,768]{1,0:T(8,128)S(1)}, f32[1536,768]{1,0:T(8,128)}, u32[]{:S(2)}) copy-start(f32[1536,768]{1,0:T(8,128)} %anc_ref.4) | copy-start | bytes 14155780
  6.8 2.5 %copy-start.4 = (s32[1,8,6]{1,0,2:T(1,128)S(1)}, s32[1,8,6]{1,0,2:T(1,128)}, u32[]{:S(2)}) copy-start(s32[1,8,6]{1,0,2:T(1,128)} %param.8) | copy-start | bytes 580
  7.4 5.6 %collective-permute-start = (f32[3,128,128]{2,1,0:T(8,128)S(1)}, f32[3,128,128]{2,1,0:T(8,128)S(1)}, u32[]{:S(2)}, u32[]{:S(2)}) collective-permute-start(f32[3,128,128]{2,1,0:T(8,128)S(1)} %later_blocks.1), channel_id=1, source_target_pairs={{0,4},{1,5},{6,2},{7,3},{8,12},{9,13},{14,10},{15,11},{16,20},{17,... | collective-permute-start | bytes 589832 | tf_op jit(solution)/shard_map/ppermute | solution.py:531
  9.4 1.4 %copy-start.2 = (bf16[1,8,128,768]{3,2,1,0:T(8,128)(2,1)S(1)}, bf16[1,8,128,768]{3,2,1,0:T(8,128)(2,1)}, u32[]{:S(2)}) copy-start(bf16[1,8,128,768]{3,2,1,0:T(8,128)(2,1)} %param.6) | copy-start | bytes 4718596
  23.3 14.9 %collective-permute-start.4 = (bf16[2,4,64,512]{3,2,1,0:T(8,128)(2,1)S(1)}, bf16[2,4,64,512]{3,2,1,0:T(8,128)(2,1)S(1)}, u32[]{:S(2)}, u32[]{:S(2)}) collective-permute-start(bf16[2,4,64,512]{3,2,1,0:T(8,128)(2,1)S(1)} %get-tuple-element.43), channel_id=1, source_target_pairs={{0,2},{1,3},{2,0},{3,1},{4,6},{5,7},{6,4},{7,5},{8,10},{9,11},{10,... | collective-permute-start | bytes 1572872 | tf_op jit(solution)/shard_map/ppermute | solution.py:547
  25.0 14.9 %collective-permute-start.5 = (bf16[2,4,64,512]{3,2,1,0:T(8,128)(2,1)S(1)}, bf16[2,4,64,512]{3,2,1,0:T(8,128)(2,1)S(1)}, u32[]{:S(2)}, u32[]{:S(2)}) collective-permute-start(bf16[2,4,64,512]{3,2,1,0:T(8,128)(2,1)S(1)} %get-tuple-element.44), channel_id=1, source_target_pairs={{0,1},{1,0},{2,3},{3,2},{4,5},{5,4},{6,7},{7,6},{8,9},{9,8},{10,11... | collective-permute-start | bytes 1572872 | tf_op jit(solution)/shard_map/ppermute | solution.py:547
  27.4 22.0 %collective-permute-start.8 = (bf16[2,4,64,512]{3,2,1,0:T(8,128)(2,1)S(1)}, bf16[2,4,64,512]{3,2,1,0:T(8,128)(2,1)S(1)}, u32[]{:S(2)}, u32[]{:S(2)}) collective-permute-start(bf16[2,4,64,512]{3,2,1,0:T(8,128)(2,1)S(1)} %get-tuple-element.51), channel_id=1, source_target_pairs={{0,2},{1,3},{2,0},{3,1},{4,6},{5,7},{6,4},{7,5},{8,10},{9,11},{10,... | collective-permute-start | bytes 1572872 | tf_op jit(solution)/shard_map/ppermute | solution.py:547
  28.0 3.0 %copy-start.3 = (s32[1,8,12]{2,1,0:T(8,128)S(1)}, s32[1,8,12]{2,1,0:T(8,128)}, u32[]{:S(2)}) copy-start(s32[1,8,12]{2,1,0:T(8,128)} %param.7) | copy-start | bytes 1156
  28.0 23.1 %collective-permute-start.9 = (bf16[2,4,64,512]{3,2,1,0:T(8,128)(2,1)S(1)}, bf16[2,4,64,512]{3,2,1,0:T(8,128)(2,1)S(1)}, u32[]{:S(2)}, u32[]{:S(2)}) collective-permute-start(bf16[2,4,64,512]{3,2,1,0:T(8,128)(2,1)S(1)} %get-tuple-element.52), channel_id=1, source_target_pairs={{0,1},{1,0},{2,3},{3,2},{4,5},{5,4},{6,7},{7,6},{8,9},{9,8},{10,11... | collective-permute-start | bytes 1572872 | tf_op jit(solution)/shard_map/ppermute | solution.py:547
  29.3 38.0 %collective-permute-start.12 = (bf16[2,4,64,512]{3,2,1,0:T(8,128)(2,1)S(1)}, bf16[2,4,64,512]{3,2,1,0:T(8,128)(2,1)S(1)}, u32[]{:S(2)}, u32[]{:S(2)}) collective-permute-start(bf16[2,4,64,512]{3,2,1,0:T(8,128)(2,1)S(1)} %get-tuple-element.61), channel_id=1, source_target_pairs={{0,2},{1,3},{2,0},{3,1},{4,6},{5,7},{6,4},{7,5},{8,10},{9,11},{10,... | collective-permute-start | bytes 1572872 | tf_op jit(solution)/shard_map/ppermute | solution.py:547
  38.2 29.2 %collective-permute-start.13 = (bf16[2,4,64,512]{3,2,1,0:T(8,128)(2,1)S(1)}, bf16[2,4,64,512]{3,2,1,0:T(8,128)(2,1)S(1)}, u32[]{:S(2)}, u32[]{:S(2)}) collective-permute-start(bf16[2,4,64,512]{3,2,1,0:T(8,128)(2,1)S(1)} %get-tuple-element.62), channel_id=1, source_target_pairs={{0,1},{1,0},{2,3},{3,2},{4,5},{5,4},{6,7},{7,6},{8,9},{9,8},{10,11... | collective-permute-start | bytes 1572872 | tf_op jit(solution)/shard_map/ppermute | solution.py:547
  42.0 16.2 %collective-permute-start.6 = (s16[272,768]{1,0:T(8,128)(2,1)S(1)}, s16[272,768]{1,0:T(8,128)(2,1)S(1)}, u32[]{:S(2)}, u32[]{:S(2)}) collective-permute-start(s16[272,768]{1,0:T(8,128)(2,1)S(1)} %get-tuple-element.47), channel_id=1, source_target_pairs={{0,8},{8,0},{16,24},{24,16},{1,9},{9,1},{17,25},{25,17},{2,10},{10... | collective-permute-start | bytes 1253384 | tf_op jit(solution)/shard_map/ppermute | solution.py:534
  53.3 2.2 %collective-permute-start.14 = (s16[144,384]{1,0:T(8,128)(2,1)S(1)}, s16[144,384]{1,0:T(8,128)(2,1)S(1)}, u32[]{:S(2)}, u32[]{:S(2)}) collective-permute-start(s16[144,384]{1,0:T(8,128)(2,1)S(1)} %get-tuple-element.64), channel_id=1, source_target_pairs={{0,4},{1,5},{6,2},{7,3},{8,12},{9,13},{14,10},{15,11},{16,20},{17,... | collective-permute-start | bytes 331784 | tf_op jit(solution)/shard_map/ppermute | solution.py:531
  56.1 6.0 %collective-permute-start.15 = (s16[144,384]{1,0:T(8,128)(2,1)S(1)}, s16[144,384]{1,0:T(8,128)(2,1)S(1)}, u32[]{:S(2)}, u32[]{:S(2)}) collective-permute-start(s16[144,384]{1,0:T(8,128)(2,1)S(1)} %pick.1.mine_ref), channel_id=1, source_target_pairs={{0,8},{8,0},{16,24},{24,16},{1,9},{9,1},{17,25},{25,17},{2,10},{10... | collective-permute-start | bytes 331784 | tf_op jit(solution)/shard_map/ppermute | solution.py:534
  57.7 20.1 %collective-permute-start.10 = (s16[272,768]{1,0:T(8,128)(2,1)S(1)}, s16[272,768]{1,0:T(8,128)(2,1)S(1)}, u32[]{:S(2)}, u32[]{:S(2)}) collective-permute-start(s16[272,768]{1,0:T(8,128)(2,1)S(1)} %get-tuple-element.57), channel_id=1, source_target_pairs={{0,8},{8,0},{16,24},{24,16},{1,9},{9,1},{17,25},{25,17},{2,10},{10... | collective-permute-start | bytes 1253384 | tf_op jit(solution)/shard_map/ppermute | solution.py:534
  62.0 17.0 %slice-start = ((s8[4718592]{0:T(1024)(128)(4,1)}), s8[4194304]{0:T(1024)(128)(4,1)S(1)}, s32[]{:S(2)}) async-start(s8[4718592]{0:T(1024)(128)(4,1)} %bitcast.14), calls=%async_computation | async-start | bytes 8388608
  62.1 16.9 %slice-start.1 = ((s8[4718592]{0:T(1024)(128)(4,1)}), s8[524288]{0:T(1024)(128)(4,1)S(1)}, s32[]{:S(2)}) async-start(s8[4718592]{0:T(1024)(128)(4,1)} %bitcast.14), calls=%async_computation.1 | async-start | bytes 1048576
  62.1 16.9 %collective-permute-start.16 = (s16[144,384]{1,0:T(8,128)(2,1)S(1)}, s16[144,384]{1,0:T(8,128)(2,1)S(1)}, u32[]{:S(2)}, u32[]{:S(2)}) collective-permute-start(s16[144,384]{1,0:T(8,128)(2,1)S(1)} %add_coded.1.one_ref), channel_id=1, source_target_pairs={{0,16},{8,24},{16,0},{24,8},{1,17},{9,25},{17,1},{25,9},{2,18},{10... | collective-permute-start | bytes 331784 | tf_op jit(solution)/shard_map/ppermute | solution.py:534
  64.8 36.7 %collective-permute-start.7 = (s16[272,768]{1,0:T(8,128)(2,1)S(1)}, s16[272,768]{1,0:T(8,128)(2,1)S(1)}, u32[]{:S(2)}, u32[]{:S(2)}) collective-permute-start(s16[272,768]{1,0:T(8,128)(2,1)S(1)} %get-tuple-element.49), channel_id=1, source_target_pairs={{1,17},{2,18},{4,20},{7,23},{9,25},{10,26},{12,28},{15,31},{16,0},... | collective-permute-start | bytes 1253384 | tf_op jit(solution)/shard_map/ppermute | solution.py:544
  69.5 21.5 %collective-permute-start.17 = (s16[272,768]{1,0:T(8,128)(2,1)S(1)}, s16[272,768]{1,0:T(8,128)(2,1)S(1)}, u32[]{:S(2)}, u32[]{:S(2)}) collective-permute-start(s16[272,768]{1,0:T(8,128)(2,1)S(1)} %get-tuple-element.68), channel_id=1, source_target_pairs={{0,8},{8,0},{16,24},{24,16},{1,9},{9,1},{17,25},{25,17},{2,10},{10... | collective-permute-start | bytes 1253384 | tf_op jit(solution)/shard_map/ppermute | solution.py:534
  78.7 22.7 %collective-permute-start.11 = (s16[144,768]{1,0:T(8,128)(2,1)S(1)}, s16[144,768]{1,0:T(8,128)(2,1)S(1)}, u32[]{:S(2)}, u32[]{:S(2)}) collective-permute-start(s16[144,768]{1,0:T(8,128)(2,1)S(1)} %get-tuple-element.59), channel_id=1, source_target_pairs={{0,16},{1,17},{2,18},{3,19},{4,20},{5,21},{6,22},{7,23},{8,24},{9,... | collective-permute-start | bytes 663560 | tf_op jit(solution)/shard_map/ppermute | solution.py:544
  91.8 15.3 %collective-permute-start.18 = (s16[272,768]{1,0:T(8,128)(2,1)S(1)}, s16[272,768]{1,0:T(8,128)(2,1)S(1)}, u32[]{:S(2)}, u32[]{:S(2)}) collective-permute-start(s16[272,768]{1,0:T(8,128)(2,1)S(1)} %get-tuple-element.72), channel_id=1, source_target_pairs={{0,16},{3,19},{5,21},{6,22},{8,24},{11,27},{13,29},{14,30},{17,1},... | collective-permute-start | bytes 1253384 | tf_op jit(solution)/shard_map/ppermute | solution.py:544
  99.9 2.7 %collective-permute-start.19 = (f32[3,128,128]{2,1,0:T(8,128)S(1)}, f32[3,128,128]{2,1,0:T(8,128)S(1)}, u32[]{:S(2)}, u32[]{:S(2)}) collective-permute-start(f32[3,128,128]{2,1,0:T(8,128)S(1)} %factor.3.refs_6_), channel_id=1, source_target_pairs={{0,4},{4,0},{1,5},{5,1},{2,6},{6,2},{3,7},{7,3},{8,12},{12,8},{9,1... | collective-permute-start | bytes 589832 | tf_op jit(solution)/shard_map/ppermute | solution.py:586

commit v9 on v8

--- a/solution.py
+++ b/solution.py
@@ -90,51 +90,81 @@
     )(blocks)
 
 
-def halves_kernel(lt_ref, one_ref, two_ref, sems):
+def set_numbers(group, blocks):
+    return range(blocks - 1) if group == 0 else range(blocks - 1, blocks)
+
+
+def halves_kernel(group, layers, blocks, lt_ref, one_ref, two_ref, sems):
     half = one_ref.shape[0]
-    copies = [
-        pltpu.make_async_copy(lt_ref.at[:half], one_ref, sems.at[0]),
-        pltpu.make_async_copy(lt_ref.at[half:], two_ref, sems.at[1]),
-    ]
+    numbers = set_numbers(group, blocks)
+    size = len(numbers) * BLK
+    copies = []
+    for h, ref in enumerate((one_ref, two_ref)):
+        for t in range(layers):
+            begin = (t * blocks + numbers[0]) * BLK
+            copies.append(
+                pltpu.make_async_copy(
+                    lt_ref.at[h * half : (h + 1) * half, :, begin : begin + size],
+                    ref.at[:, :, t * size : (t + 1) * size],
+                    sems.at[h, t],
+                )
+            )
     for copy in copies:
         copy.start()
     for copy in copies:
         copy.wait()
 
 
-def halves(lt):
-    supers, depth, length = lt.shape
-    one = jax.ShapeDtypeStruct((supers // 2, depth, length), lt.dtype)
-    return pl.pallas_call(
-        halves_kernel,
+def halves(lt, group, layers, blocks):
+    supers, depth, _ = lt.shape
+    size = layers * len(set_numbers(group, blocks)) * BLK
+    one = jax.ShapeDtypeStruct((supers // 2, depth, size), lt.dtype)
+    return pl.pallas_call(
+        functools.partial(halves_kernel, group, layers, blocks),
         out_shape=[one, one],
         in_specs=[ANY],
         out_specs=[ANY, ANY],
-        scratch_shapes=[pltpu.SemaphoreType.DMA((2,))],
+        scratch_shapes=[pltpu.SemaphoreType.DMA((2, layers))],
         compiler_params=params(),
         cost_estimate=cost(0),
         name="halves",
     )(lt)
 
 
-def block_at(where_ref, spot, part, blocks, flip=0):
-    phase, number = spot
-    half = where_ref[7] if phase == flip else 1 - where_ref[7]
-    return (2 * half + part) * blocks + number
+def share_at(where_ref, spot, part, flip=0):
+    half = where_ref[7] if spot[0] == flip else 1 - where_ref[7]
+    return 2 * half + part
+
+
+def group_of(spot, blocks):
+    return 0 if spot[1] < blocks - 1 else 1
+
+
+def used_sets(sets, chunk, blocks):
+    groups = sorted({group_of(spot, blocks) for spot in chunk})
+    return [ref for group in groups for ref in sets[group]]
+
+
+def place(where_ref, chunk, spot, part, blocks, flip=0):
+    groups = sorted({group_of(other, blocks) for other in chunk})
+    group = group_of(spot, blocks)
+    numbers = set_numbers(group, blocks)
+    begin = share_at(where_ref, spot, part, flip) * len(numbers) + spot[1] - numbers[0]
+    return 4 * groups.index(group), pl.ds(pl.multiple_of(begin * BLK, BLK), BLK)
 
 
 def split_kernel(chunk, blocks, where_ref, *refs):
-    sources, outs, sems = refs[:4], refs[4:6], refs[6]
+    sources, (one_ref, two_ref, sems) = refs[:-3], refs[-3:]
     copies = []
-    for n, ref in enumerate(sources):
-        for part in range(2):
-            for m, spot in enumerate(chunk):
-                begin = block_at(where_ref, spot, part, blocks, flip=1) * BLK
-                at = (part * len(chunk) + m) * BLK
+    for part in range(2):
+        for m, spot in enumerate(chunk):
+            first, lanes = place(where_ref, chunk, spot, part, blocks, flip=1)
+            at = (part * len(chunk) + m) * BLK
+            for n in range(4):
                 copies.append(
                     pltpu.make_async_copy(
-                        ref.at[:, :, pl.ds(pl.multiple_of(begin, BLK), BLK)],
-                        outs[n // 2].at[n % 2, :, :, at : at + BLK],
+                        sources[first + n].at[:, :, lanes],
+                        (one_ref, two_ref)[n // 2].at[n % 2, :, :, at : at + BLK],
                         sems.at[n, part, m],
                     )
                 )
@@ -144,14 +174,15 @@
         copy.wait()
 
 
-def split(where, sources, chunk, blocks):
+def split(where, sets, chunk, blocks):
+    sources = used_sets(sets, chunk, blocks)
     half, depth, _ = sources[0].shape
     count = len(chunk)
     one = jax.ShapeDtypeStruct((2, half, depth, 2 * count * BLK), sources[0].dtype)
     return pl.pallas_call(
         functools.partial(split_kernel, chunk, blocks),
         out_shape=[one, one],
-        in_specs=[SMEM] + [ANY] * 4,
+        in_specs=[SMEM] + [ANY] * len(sources),
         out_specs=[ANY, ANY],
         scratch_shapes=[pltpu.SemaphoreType.DMA((4, 2, count))],
         compiler_params=params(),
@@ -203,21 +234,16 @@
     )(where, upat, u, uo)
 
 
-def product(chunk, blocks, where_ref, lpat_ref, whole, groups, right_ref, left):
+def product(chunk, blocks, where_ref, lpat_ref, pieces, right_ref, left):
     half, depth = left.shape[0] // 2, left.shape[1] // 2
     for part in range(2):
         for m, spot in enumerate(chunk):
-            number = block_at(where_ref, spot, part, blocks)
+            number = share_at(where_ref, spot, part) * blocks + spot[1]
             at = (part * len(chunk) + m) * BLK
             for k in range(2 * half):
                 kept = lpat_ref[k, number] != 0
                 for n in range(2):
-                    group, i = groups[k // half], k % half
-                    if whole:
-                        begin = pl.multiple_of(number * BLK, BLK)
-                        block = group[n][i, :, pl.ds(begin, BLK)]
-                    else:
-                        block = group[n, i, :, at : at + BLK]
+                    block = pieces(part, m, k // half, n, k % half)
                     left[k, n * depth : (n + 1) * depth, at : at + BLK] = jnp.where(
                         kept, block, jnp.zeros_like(block)
                     )
@@ -230,19 +256,24 @@
 
 
 def near_kernel(chunk, blocks, where_ref, lpat_ref, *refs):
-    right_ref, acc_ref, left = refs[4:]
-    groups = (refs[:2], refs[2:4])
-    total = product(chunk, blocks, where_ref, lpat_ref, True, groups, right_ref, left)
+    sources, (right_ref, acc_ref, left) = refs[:-3], refs[-3:]
+
+    def pieces(part, m, h, n, i):
+        first, lanes = place(where_ref, chunk, chunk[m], part, blocks)
+        return sources[first + 2 * h + n][i, :, lanes]
+
+    total = product(chunk, blocks, where_ref, lpat_ref, pieces, right_ref, left)
     acc_ref[...] = total.reshape(acc_ref.shape)
 
 
-def near_update(where, lpat, sources, right, chunk, blocks):
+def near_update(where, lpat, sets, right, chunk, blocks):
+    sources = used_sets(sets, chunk, blocks)
     supers, kdim, cols = right.shape
     count = 2 * len(chunk)
     return pl.pallas_call(
         functools.partial(near_kernel, chunk, blocks),
         out_shape=jax.ShapeDtypeStruct((count, BLK, cols), jnp.float32),
-        in_specs=[SMEM] * 2 + [VMEM] * 5,
+        in_specs=[SMEM] * 2 + [VMEM] * (len(sources) + 1),
         out_specs=VMEM,
         scratch_shapes=[pltpu.VMEM((supers, kdim, count * BLK), jnp.bfloat16)],
         compiler_params=params(),
@@ -256,8 +287,12 @@
     kept_ref, sent_ref = refs[2 + earlier : 4 + earlier]
     left, acc = refs[-2:]
     count = len(chunk)
-    groups = (a_ref, b_ref)
-    total = product(chunk, blocks, where_ref, lpat_ref, False, groups, right_ref, left)
+
+    def pieces(part, m, h, n, i):
+        at = (part * count + m) * BLK
+        return (a_ref, b_ref)[h][n, i, :, at : at + BLK]
+
+    total = product(chunk, blocks, where_ref, lpat_ref, pieces, right_ref, left)
     acc[...] = (before_ref[...] + total.reshape(before_ref.shape)).reshape(acc.shape)
     first = [(m, number) for m, (phase, number) in enumerate(chunk) if phase == 0]
     if first:
@@ -548,21 +583,22 @@
 
     lt = jnp.swapaxes(lpanel[0], 1, 2)
     u = upanel[0]
-    a, b = halves(lt)
-    xa, yb = over(a, 1), over(b, 2)
+    a, b = halves(lt, 0, layers, blocks)
     uo = lax.ppermute(u, "row", xor_perm(rows, 1))
+    sets = [(a, over(a, 1), b, over(b, 2))]
+    a, b = halves(after(lt, a), 1, layers, blocks)
+    sets.append((a, over(a, 1), b, over(b, 2)))
     near_right, far_right = masked_right(where, upat[0], u, uo)
-    whole = (a, xa, b, yb)
     rounds = [(phase, number) for phase in range(2) for number in range(blocks)]
     chunks = [rounds[n : n + 2] for n in range(0, len(rounds), 2)]
     given = to_other_core(later_blocks(where, after(anc, a), blocks))
     sides = []
     for chunk in chunks:
-        ready = (after(a, *(sides[-1] if sides else [given, near_right])), xa, b, yb)
-        sides.append(split(where, ready, chunk, blocks))
+        before = sides[-1] if sides else [given, near_right]
+        sides.append(split(after(where, *before), sets, chunk, blocks))
     others = [(over(one, 2), over(two, 1)) for one, two in sides]
     masks = lpat[0]
-    parts = [near_update(where, masks, whole, near_right, chunk, blocks) for chunk in chunks]
+    parts = [near_update(where, masks, sets, near_right, chunk, blocks) for chunk in chunks]
     known = []
 
     def far_part(j, *waits):
@@ -571,21 +607,22 @@
 
     kept0, coded0, *diag = far_part(0)
     known = diag
-    sum0, sent0 = halve(where, kept0, over_layers(coded0, 1), chunks[0])
     kept1, coded1, *diag = far_part(1, kept0, parts[2])
+    sum0, sent0 = halve(where, after(kept0, kept1), over_layers(coded0, 1), chunks[0])
     known = []
     mine = pick(where, diag[0], to_other_core(diag[1]))
-    near = add_coded(after(mine, sent0), over_layers(mine, 1))
+    got0 = far_layers(sent0, chunks[0])
+    near = add_coded(after(mine, got0), over_layers(mine, 1))
     far = over_layers(near, 2)
     own = pivots(where, anc, given, near, far)
-    kept2, coded2 = far_part(2, near, sent0)
+    kept2, coded2 = far_part(2, mine, sent0)
     sum1, sent1 = halve(where, kept1, over_layers(coded1, 1), chunks[1])
     half_lu = factor(after(own, sent1, coded2), 0, HALF_STEPS)
     sum2, sent2 = halve(where, after(kept2, half_lu), over_layers(coded2, 1), chunks[2])
     lu = factor(after(half_lu, sent2), HALF_STEPS, BLK)
     lu_got = lax.ppermute(lu, "row", xor_perm(rows, 1))
     pairs = [
-        (sum0, far_layers(sent0, chunks[0])),
+        (sum0, got0),
         (sum1, far_layers(sent1, chunks[1])),
         (sum2, far_layers(sent2, chunks[2])),
     ]

time: 110 us -> 107 us (0.973); the launches traced: 109 us -> 105 us
  waiting for transfers between devices: 41.5 us -> 27.4 us
  starting transfers between devices: 26.7 us -> 35.9 us
    ppermute x8 -> x10, waiting for transfers between devices: 18.6 us -> 10.1 us  [over(): return lax.ppermute(value, 'col', xor_perm(cols, bit))]
    ppermute x5, waiting for transfers between devices: 16.4 us -> 11.2 us  [over_layers(): return lax.ppermute(value, 'layer', xor_perm(layers, bit))]
    ppermute x8 -> x10, starting transfers between devices: 9.76 us -> 13.5 us  [over(): return lax.ppermute(value, 'col', xor_perm(cols, bit))]
    ppermute x3, starting transfers between devices: 4.07 us -> 7.2 us  [far_layers(): return lax.ppermute(value, everyone, perm)]
    ppermute x1, starting transfers between devices: 1.61 us -> 3.45 us  [planned(): lu_got = lax.ppermute(lu, 'row', xor_perm(rows, 1))]
  transfers between devices with their start and end apart: 20 -> 22, of which waited for: 11 -> 13; matrix products, arithmetic and copies ran while one was open for 0% -> 0% of each run, Pallas kernels for 29% -> 32%
where the time goes in v9:
time: 107 us; the launch traced here: 105 us
  starting transfers between devices  35.9 us (34%)
  Pallas kernels  35.4 us (33%)
  waiting for transfers between devices  27.4 us (26%)
  local copies, waits for them, and re-layouts  5.33 us (5%)
  between operations  1.09 us (1%)
    ppermute x10, starting transfers between devices, over(): return lax.ppermute(value, 'col', xor_perm(cols, bit))  13.5 us
    pallas_call x2, Pallas kernels, factor(): pl.pallas_call(functools.partial(lu_kernel, begin, end), out_shape=jax.Sh...  11.4 us
    ppermute x5, waiting for transfers between devices, over_layers(): return lax.ppermute(value, 'layer', xor_perm(layers, bit))  11.2 us
    ppermute x10, waiting for transfers between devices, over(): return lax.ppermute(value, 'col', xor_perm(cols, bit))  10.1 us
    ppermute x5, starting transfers between devices, over_layers(): return lax.ppermute(value, 'layer', xor_perm(layers, bit))  9.07 us
    ppermute x3, starting transfers between devices, far_layers(): return lax.ppermute(value, everyone, perm)  7.2 us
    pallas_call x3, Pallas kernels, far_update(): pl.pallas_call(functools.partial(far_kernel, chunk, blocks, len(earlier))...  6.34 us
    pallas_call x3, Pallas kernels, near_update(): pl.pallas_call(functools.partial(near_kernel, chunk, blocks), out_shape=j...  5.49 us
  transfers between devices with their start and end apart: 22, of which 13 were waited for; matrix products, arithmetic and copies ran while one was open for 0% of the time, Pallas kernels for 32%

profile of v9, /device:TPU:2, one launch (start us, length us, event | category | flops | bytes accessed | tf_op | source)
XLA Modules:
  0.0 105.1 jit_solution(1997980765860052798)
XLA Ops:
  0.7 1.4 %copy-done.1 = bf16[1,8,1536,64]{2,3,1,0:T(8,128)(2,1)S(1)} copy-done((bf16[1,8,1536,64]{2,3,1,0:T(8,128)(2,1)S(1)}, bf16[1,8,1536,64]{2,3,1,0:T(8,128)(2,1)}, u32[]{:S(2)}) %copy-start.1) | copy-done | bytes 1572888
  2.4 2.0 %collective-permute-start.3 = (bf16[4,64,1024]{2,1,0:T(8,128)(2,1)S(1)}, bf16[4,64,1024]{2,1,0:T(8,128)(2,1)S(1)}, u32[]{:S(2)}, u32[]{:S(2)}) collective-permute-start(bf16[4,64,1024]{2,1,0:T(8,128)(2,1)S(1)} %get-tuple-element.48.refs_2_), channel_id=1, source_target_pairs={{0,2},{1,3},{2,0},{3,1},{4,6},{5,7},{6,4},{7,5},{8,10},{9,11},{10,... | collective-permute-start | bytes 1572872 | tf_op jit(solution)/shard_map/ppermute | solution.py:582
  4.7 1.6 %collective-permute-start.6 = (bf16[4,64,512]{2,1,0:T(8,128)(2,1)S(1)}, bf16[4,64,512]{2,1,0:T(8,128)(2,1)S(1)}, u32[]{:S(2)}, u32[]{:S(2)}) collective-permute-start(bf16[4,64,512]{2,1,0:T(8,128)(2,1)S(1)} %get-tuple-element.44.refs_4_), channel_id=1, source_target_pairs={{0,1},{1,0},{2,3},{3,2},{4,5},{5,4},{6,7},{7,6},{8,9},{9,8},{10,11... | collective-permute-start | bytes 786440 | tf_op jit(solution)/shard_map/ppermute | solution.py:582
  6.8 2.3 %copy-done = f32[1536,768]{1,0:T(8,128)S(1)} copy-done((f32[1536,768]{1,0:T(8,128)S(1)}, f32[1536,768]{1,0:T(8,128)}, u32[]{:S(2)}) %copy-start) | copy-done | bytes 4718616
  9.8 1.3 %collective-permute-start = (f32[3,128,128]{2,1,0:T(8,128)S(1)}, f32[3,128,128]{2,1,0:T(8,128)S(1)}, u32[]{:S(2)}, u32[]{:S(2)}) collective-permute-start(f32[3,128,128]{2,1,0:T(8,128)S(1)} %later_blocks.1), channel_id=1, source_target_pairs={{0,4},{1,5},{6,2},{7,3},{8,12},{9,13},{14,10},{15,11},{16,20},{17,... | collective-permute-start | bytes 589832 | tf_op jit(solution)/shard_map/ppermute | solution.py:566
  11.2 1.4 %copy-done.2 = bf16[1,8,128,768]{3,2,1,0:T(8,128)(2,1)S(1)} copy-done((bf16[1,8,128,768]{3,2,1,0:T(8,128)(2,1)S(1)}, bf16[1,8,128,768]{3,2,1,0:T(8,128)(2,1)}, u32[]{:S(2)}) %copy-start.2) | copy-done | bytes 1572888
  12.6 2.2 %masked_right.1 = (bf16[8,128,768]{2,1,0:T(8,128)(2,1)S(1)}, bf16[8,128,768]{2,1,0:T(8,128)(2,1)S(1)}) custom-call(s32[8]{0:T(128)S(1)} %stack.35.where_ref, s32[8,6]{1,0:T(8,128)S(1)} %bitcast.20, bf16[8,128,768]{2,1,0:T(8,128)(2,1)S(1)} %bitcast.19, bf16[8,128,768]{2,1,0:T(8,128)(2,1)} %collective-permute-done.1.uo_ref), custom_call_target="tpu_custom_call" | custom-call | flops 1000 | bytes 1000 | tf_op jit(solution)/shard_map/masked_right/pallas_call | solution.py:226
  14.8 2.4 %collective-permute-done.2.refs_1_ = bf16[4,64,1024]{2,1,0:T(8,128)(2,1)S(1)} collective-permute-done((bf16[4,64,1024]{2,1,0:T(8,128)(2,1)S(1)}, bf16[4,64,1024]{2,1,0:T(8,128)(2,1)S(1)}, u32[]{:S(2)}, u32[]{:S(2)}) %collective-permute-start.2) | collective-permute-done | bytes 524320 | tf_op jit(solution)/shard_map/ppermute | solution.py:582
  17.2 1.0 split.3
  18.2 2.1 %collective-permute-start.4 = (bf16[2,4,64,512]{3,2,1,0:T(8,128)(2,1)S(1)}, bf16[2,4,64,512]{3,2,1,0:T(8,128)(2,1)S(1)}, u32[]{:S(2)}, u32[]{:S(2)}) collective-permute-start(bf16[2,4,64,512]{3,2,1,0:T(8,128)(2,1)S(1)} %get-tuple-element.49), channel_id=1, source_target_pairs={{0,2},{1,3},{2,0},{3,1},{4,6},{5,7},{6,4},{7,5},{8,10},{9,11},{10,... | collective-permute-start | bytes 1572872 | tf_op jit(solution)/shard_map/ppermute | solution.py:582
  20.3 1.5 %collective-permute-start.5 = (bf16[2,4,64,512]{3,2,1,0:T(8,128)(2,1)S(1)}, bf16[2,4,64,512]{3,2,1,0:T(8,128)(2,1)S(1)}, u32[]{:S(2)}, u32[]{:S(2)}) collective-permute-start(bf16[2,4,64,512]{3,2,1,0:T(8,128)(2,1)S(1)} %get-tuple-element.50), channel_id=1, source_target_pairs={{0,1},{1,0},{2,3},{3,2},{4,5},{5,4},{6,7},{7,6},{8,9},{9,8},{10,11... | collective-permute-start | bytes 1572872 | tf_op jit(solution)/shard_map/ppermute | solution.py:582
  21.8 1.0 collective-permute-done.6.refs_5_
  22.8 1.0 split.4
  23.8 2.1 %collective-permute-start.8 = (bf16[2,4,64,512]{3,2,1,0:T(8,128)(2,1)S(1)}, bf16[2,4,64,512]{3,2,1,0:T(8,128)(2,1)S(1)}, u32[]{:S(2)}, u32[]{:S(2)}) collective-permute-start(bf16[2,4,64,512]{3,2,1,0:T(8,128)(2,1)S(1)} %get-tuple-element.55), channel_id=1, source_target_pairs={{0,2},{1,3},{2,0},{3,1},{4,6},{5,7},{6,4},{7,5},{8,10},{9,11},{10,... | collective-permute-start | bytes 1572872 | tf_op jit(solution)/shard_map/ppermute | solution.py:582
  25.9 1.5 %collective-permute-start.9 = (bf16[2,4,64,512]{3,2,1,0:T(8,128)(2,1)S(1)}, bf16[2,4,64,512]{3,2,1,0:T(8,128)(2,1)S(1)}, u32[]{:S(2)}, u32[]{:S(2)}) collective-permute-start(bf16[2,4,64,512]{3,2,1,0:T(8,128)(2,1)S(1)} %get-tuple-element.56), channel_id=1, source_target_pairs={{0,1},{1,0},{2,3},{3,2},{4,5},{5,4},{6,7},{7,6},{8,9},{9,8},{10,11... | collective-permute-start | bytes 1572872 | tf_op jit(solution)/shard_map/ppermute | solution.py:582
  27.4 1.0 split.5
  28.9 1.8 %near_update.5.refs_1_ = f32[4,128,768]{2,1,0:T(8,128)S(1)} custom-call(s32[8]{0:T(128)S(1)} %stack.35.where_ref, s32[8,12]{1,0:T(8,128)S(1)} %bitcast.21, bf16[4,64,1024]{2,1,0:T(8,128)(2,1)S(1)} %get-tuple-element.42.refs_0_, bf16[4,64,1024]{2,1,0:T(8,128)(2,1)S(1)} %collective-permute-done.2.refs_1_, bf16[4,64,1024]{2,1,0:T(8,128)(2,1)S(1)} %get-tuple-element.48.refs_2_, ...), custom_call_target="tpu_custom_call" | custom-call | flops 10000001024 | bytes 1000 | tf_op jit(solution)/shard_map/near_update/pallas_call | solution.py:273
  30.7 1.8 %near_update.4.refs_1_ = f32[4,128,768]{2,1,0:T(8,128)S(1)} custom-call(s32[8]{0:T(128)S(1)} %stack.35.where_ref, s32[8,12]{1,0:T(8,128)S(1)} %bitcast.22, bf16[4,64,1024]{2,1,0:T(8,128)(2,1)S(1)} %get-tuple-element.42.refs_0_, bf16[4,64,1024]{2,1,0:T(8,128)(2,1)S(1)} %collective-permute-done.2.refs_1_, bf16[4,64,1024]{2,1,0:T(8,128)(2,1)S(1)} %get-tuple-element.48.refs_2_, ...), custom_call_target="tpu_custom_call" | custom-call | flops 10000001024 | bytes 1000 | tf_op jit(solution)/shard_map/near_update/pallas_call | solution.py:273
  32.6 1.9 %near_update.3.refs_1_ = f32[4,128,768]{2,1,0:T(8,128)S(1)} custom-call(s32[8]{0:T(128)S(1)} %stack.35.where_ref, s32[8,12]{1,0:T(8,128)S(1)} %bitcast.23, bf16[4,64,1024]{2,1,0:T(8,128)(2,1)S(1)} %get-tuple-element.42.refs_0_, bf16[4,64,1024]{2,1,0:T(8,128)(2,1)S(1)} %collective-permute-done.2.refs_1_, bf16[4,64,1024]{2,1,0:T(8,128)(2,1)S(1)} %get-tuple-element.48.refs_2_, ...), custom_call_target="tpu_custom_call" | custom-call | flops 10000001024 | bytes 1000 | tf_op jit(solution)/shard_map/near_update/pallas_call | solution.py:273
  34.4 1.6 %collective-permute-start.15 = (bf16[2,4,64,512]{3,2,1,0:T(8,128)(2,1)S(1)}, bf16[2,4,64,512]{3,2,1,0:T(8,128)(2,1)S(1)}, u32[]{:S(2)}, u32[]{:S(2)}) collective-permute-start(bf16[2,4,64,512]{3,2,1,0:T(8,128)(2,1)S(1)} %get-tuple-element.70), channel_id=1, source_target_pairs={{0,1},{1,0},{2,3},{3,2},{4,5},{5,4},{6,7},{7,6},{8,9},{9,8},{10,11... | collective-permute-start | bytes 1572872 | tf_op jit(solution)/shard_map/ppermute | solution.py:582
  36.1 2.1 %far_update.3 = (f32[2,128,768]{2,1,0:T(8,128)S(1)}, s16[272,768]{1,0:T(8,128)(2,1)S(1)}, s16[144,384]{1,0:T(8,128)(2,1)S(1)}, s16[144,384]{1,0:T(8,128)(2,1)S(1)}) custom-call(s32[8]{0:T(128)S(1)} %stack.35.where_ref, s32[8,12]{1,0:T(8,128)S(1)} %bitcast.24, bf16[2,4,64,512]{3,2,1,0:T(8,128)(2,1)S(1)} %collective-permute-done.4.a_ref, ...), custom_call_target="tpu_custom_call" | custom-call | flops 10000001024 | bytes 1000 | tf_op jit(solution)/shard_map/far_update/pallas_call | solution.py:322
  38.1 1.7 %collective-permute-start.10 = (s16[272,768]{1,0:T(8,128)(2,1)S(1)}, s16[272,768]{1,0:T(8,128)(2,1)S(1)}, u32[]{:S(2)}, u32[]{:S(2)}) collective-permute-start(s16[272,768]{1,0:T(8,128)(2,1)S(1)} %get-tuple-element.62), channel_id=1, source_target_pairs={{0,8},{8,0},{16,24},{24,16},{1,9},{9,1},{17,25},{25,17},{2,10},{10... | collective-permute-start | bytes 1253384 | tf_op jit(solution)/shard_map/ppermute | solution.py:569
  39.8 5.5 %collective-permute-done.8.a_ref = bf16[2,4,64,512]{3,2,1,0:T(8,128)(2,1)S(1)} collective-permute-done((bf16[2,4,64,512]{3,2,1,0:T(8,128)(2,1)S(1)}, bf16[2,4,64,512]{3,2,1,0:T(8,128)(2,1)S(1)}, u32[]{:S(2)}, u32[]{:S(2)}) %collective-permute-start.8) | collective-permute-done | bytes 524320 | tf_op jit(solution)/shard_map/ppermute | solution.py:582
  45.3 1.1 %collective-permute-done.9.b_ref = bf16[2,4,64,512]{3,2,1,0:T(8,128)(2,1)S(1)} collective-permute-done((bf16[2,4,64,512]{3,2,1,0:T(8,128)(2,1)S(1)}, bf16[2,4,64,512]{3,2,1,0:T(8,128)(2,1)S(1)}, u32[]{:S(2)}, u32[]{:S(2)}) %collective-permute-start.9) | collective-permute-done | bytes 524320 | tf_op jit(solution)/shard_map/ppermute | solution.py:582
  46.4 2.1 %far_update.4 = (f32[2,128,768]{2,1,0:T(8,128)S(1)}, s16[272,768]{1,0:T(8,128)(2,1)S(1)}, s16[144,384]{1,0:T(8,128)(2,1)S(1)}, s16[144,384]{1,0:T(8,128)(2,1)S(1)}) custom-call(s32[8]{0:T(128)S(1)} %stack.35.where_ref, s32[8,12]{1,0:T(8,128)S(1)} %bitcast.25, bf16[2,4,64,512]{3,2,1,0:T(8,128)(2,1)S(1)} %collective-permute-done.8.a_ref, ...), custom_call_target="tpu_custom_call" | custom-call | flops 10000001024 | bytes 1000 | tf_op jit(solution)/shard_map/far_update/pallas_call | solution.py:322
  48.6 0.8 halve.3
  49.4 4.5 %collective-permute-start.11 = (s16[272,768]{1,0:T(8,128)(2,1)S(1)}, s16[272,768]{1,0:T(8,128)(2,1)S(1)}, u32[]{:S(2)}, u32[]{:S(2)}) collective-permute-start(s16[272,768]{1,0:T(8,128)(2,1)S(1)} %get-tuple-element.64), channel_id=1, source_target_pairs={{1,17},{2,18},{4,20},{7,23},{9,25},{10,26},{12,28},{15,31},{16,0},... | collective-permute-start | bytes 1253384 | tf_op jit(solution)/shard_map/ppermute | solution.py:579
  53.9 1.3 %collective-permute-start.16 = (s16[144,384]{1,0:T(8,128)(2,1)S(1)}, s16[144,384]{1,0:T(8,128)(2,1)S(1)}, u32[]{:S(2)}, u32[]{:S(2)}) collective-permute-start(s16[144,384]{1,0:T(8,128)(2,1)S(1)} %get-tuple-element.72), channel_id=1, source_target_pairs={{0,4},{1,5},{6,2},{7,3},{8,12},{9,13},{14,10},{15,11},{16,20},{17,... | collective-permute-start | bytes 331784 | tf_op jit(solution)/shard_map/ppermute | solution.py:566
  55.2 0.9 collective-permute-done.16.got_ref
  56.1 0.7 pick.1.mine_ref
  56.9 1.7 %collective-permute-start.17 = (s16[144,384]{1,0:T(8,128)(2,1)S(1)}, s16[144,384]{1,0:T(8,128)(2,1)S(1)}, u32[]{:S(2)}, u32[]{:S(2)}) collective-permute-start(s16[144,384]{1,0:T(8,128)(2,1)S(1)} %pick.1.mine_ref), channel_id=1, source_target_pairs={{0,8},{8,0},{16,24},{24,16},{1,9},{9,1},{17,25},{25,17},{2,10},{10... | collective-permute-start | bytes 331784 | tf_op jit(solution)/shard_map/ppermute | solution.py:569
  59.0 0.8 collective-permute-done.11.refs_1_
  59.8 4.5 %collective-permute-done.17.got_ref = s16[144,384]{1,0:T(8,128)(2,1)S(1)} collective-permute-done((s16[144,384]{1,0:T(8,128)(2,1)S(1)}, s16[144,384]{1,0:T(8,128)(2,1)S(1)}, u32[]{:S(2)}, u32[]{:S(2)}) %collective-permute-start.17) | collective-permute-done | bytes 110624 | tf_op jit(solution)/shard_map/ppermute | solution.py:569
  64.6 2.1 %far_update.5 = (f32[2,128,768]{2,1,0:T(8,128)S(1)}, s16[272,768]{1,0:T(8,128)(2,1)S(1)}) custom-call(s32[8]{0:T(128)S(1)} %stack.35.where_ref, s32[8,12]{1,0:T(8,128)S(1)} %bitcast.26, bf16[2,4,64,512]{3,2,1,0:T(8,128)(2,1)S(1)} %collective-permute-done.14.a_ref, bf16[2,4,64,512]{3,2,1,0:T(8,128)(2,1)S(1)} %collective-permute-done.15.b_ref, ...), custom_call_target="tpu_custom_call" | custom-call | flops 10000001024 | bytes 1000 | tf_op jit(solution)/shard_map/far_update/pallas_call | solution.py:322
  66.7 5.2 %collective-permute-start.19 = (s16[272,768]{1,0:T(8,128)(2,1)S(1)}, s16[272,768]{1,0:T(8,128)(2,1)S(1)}, u32[]{:S(2)}, u32[]{:S(2)}) collective-permute-start(s16[272,768]{1,0:T(8,128)(2,1)S(1)} %get-tuple-element.76), channel_id=1, source_target_pairs={{0,8},{8,0},{16,24},{24,16},{1,9},{9,1},{17,25},{25,17},{2,10},{10... | collective-permute-start | bytes 1253384 | tf_op jit(solution)/shard_map/ppermute | solution.py:569
  71.9 3.7 %collective-permute-done.12.got_ref = s16[272,768]{1,0:T(8,128)(2,1)S(1)} collective-permute-done((s16[272,768]{1,0:T(8,128)(2,1)S(1)}, s16[272,768]{1,0:T(8,128)(2,1)S(1)}, u32[]{:S(2)}, u32[]{:S(2)}) %collective-permute-start.12) | collective-permute-done | bytes 417824 | tf_op jit(solution)/shard_map/ppermute | solution.py:569
  75.7 0.7 halve.4
  76.4 1.4 %collective-permute-start.13 = (s16[144,768]{1,0:T(8,128)(2,1)S(1)}, s16[144,768]{1,0:T(8,128)(2,1)S(1)}, u32[]{:S(2)}, u32[]{:S(2)}) collective-permute-start(s16[144,768]{1,0:T(8,128)(2,1)S(1)} %get-tuple-element.67), channel_id=1, source_target_pairs={{0,16},{1,17},{2,18},{3,19},{4,20},{5,21},{6,22},{7,23},{8,24},{9,... | collective-permute-start | bytes 663560 | tf_op jit(solution)/shard_map/ppermute | solution.py:579
  77.8 0.7 pivots.1.in_ref
  78.5 4.6 %factor.2.in_ref = f32[3,128,128]{2,1,0:T(8,128)S(1)} custom-call(f32[3,128,128]{2,1,0:T(8,128)S(1)} %pivots.1.in_ref), custom_call_target="tpu_custom_call" | custom-call | flops 10000001024 | bytes 1000 | tf_op jit(solution)/shard_map/factor/pallas_call | solution.py:82
  83.1 3.0 %collective-permute-done.19.got_ref = s16[272,768]{1,0:T(8,128)(2,1)S(1)} collective-permute-done((s16[272,768]{1,0:T(8,128)(2,1)S(1)}, s16[272,768]{1,0:T(8,128)(2,1)S(1)}, u32[]{:S(2)}, u32[]{:S(2)}) %collective-permute-start.19) | collective-permute-done | bytes 417824 | tf_op jit(solution)/shard_map/ppermute | solution.py:569
  86.1 0.8 halve.5
  86.9 1.3 %collective-permute-start.20 = (s16[272,768]{1,0:T(8,128)(2,1)S(1)}, s16[272,768]{1,0:T(8,128)(2,1)S(1)}, u32[]{:S(2)}, u32[]{:S(2)}) collective-permute-start(s16[272,768]{1,0:T(8,128)(2,1)S(1)} %get-tuple-element.80), channel_id=1, source_target_pairs={{0,16},{3,19},{5,21},{6,22},{8,24},{11,27},{13,29},{14,30},{17,1},... | collective-permute-start | bytes 1253384 | tf_op jit(solution)/shard_map/ppermute | solution.py:579
  88.2 6.8 %factor.3.refs_6_ = f32[3,128,128]{2,1,0:T(8,128)S(1)} custom-call(f32[3,128,128]{2,1,0:T(8,128)S(1)} %factor.2.in_ref), custom_call_target="tpu_custom_call" | custom-call | flops 10000001024 | bytes 1000 | tf_op jit(solution)/shard_map/factor/pallas_call | solution.py:82
  95.0 3.5 %collective-permute-start.21 = (f32[3,128,128]{2,1,0:T(8,128)S(1)}, f32[3,128,128]{2,1,0:T(8,128)S(1)}, u32[]{:S(2)}, u32[]{:S(2)}) collective-permute-start(f32[3,128,128]{2,1,0:T(8,128)S(1)} %factor.3.refs_6_), channel_id=1, source_target_pairs={{0,4},{4,0},{1,5},{5,1},{2,6},{6,2},{3,7},{7,3},{8,12},{12,8},{9,1... | collective-permute-start | bytes 589832 | tf_op jit(solution)/shard_map/ppermute | solution.py:623
  98.5 1.1 %collective-permute-done.21.refs_7_ = f32[3,128,128]{2,1,0:T(8,128)S(1)} collective-permute-done((f32[3,128,128]{2,1,0:T(8,128)S(1)}, f32[3,128,128]{2,1,0:T(8,128)S(1)}, u32[]{:S(2)}, u32[]{:S(2)}) %collective-permute-start.21) | collective-permute-done | bytes 196640 | tf_op jit(solution)/shard_map/ppermute | solution.py:623
  99.5 3.2 %collective-permute-done.20.refs_5_ = s16[272,768]{1,0:T(8,128)(2,1)S(1)} collective-permute-done((s16[272,768]{1,0:T(8,128)(2,1)S(1)}, s16[272,768]{1,0:T(8,128)(2,1)S(1)}, u32[]{:S(2)}, u32[]{:S(2)}) %collective-permute-start.20) | collective-permute-done | bytes 417824 | tf_op jit(solution)/shard_map/ppermute | solution.py:579
  102.7 2.2 %combine.1 = (f32[384,768]{1,0:T(8,128)}, f32[6,128,128]{2,1,0:T(8,128)}) custom-call(s32[8]{0:T(128)S(1)} %stack.35.where_ref, f32[1536,768]{1,0:T(8,128)S(1)} %bitcast.15, f32[2,128,768]{2,1,0:T(8,128)S(1)} %get-tuple-element.63.refs_0_, s16[272,768]{1,0:T(8,128)(2,1)S(1)} %collective-permute-done.11.refs_1_, ...), custom_call_target="tpu_custom_call" | custom-call | flops 1000 | bytes 1000 | tf_op jit(solution)/shard_map/combine/pallas_call | solution.py:457
  (35 shorter events, 3.2 us)
Async XLA Ops:
  0.6 9.1 %collective-permute-start.1 = (bf16[8,128,768]{2,1,0:T(8,128)(2,1)}, bf16[8,128,768]{2,1,0:T(8,128)(2,1)}, u32[]{:S(2)}, u32[]{:S(2)}) collective-permute-start(bf16[8,128,768]{2,1,0:T(8,128)(2,1)} %bitcast.18), channel_id=1, source_target_pairs={{0,4},{4,0},{1,5},{5,1},{2,6},{6,2},{3,7},{7,3},{8,12},{12,8},{9,1... | collective-permute-start | bytes 4718600 | tf_op jit(solution)/shard_map/ppermute | solution.py:587
  0.7 1.4 %copy-start.1 = (bf16[1,8,1536,64]{2,3,1,0:T(8,128)(2,1)S(1)}, bf16[1,8,1536,64]{2,3,1,0:T(8,128)(2,1)}, u32[]{:S(2)}) copy-start(bf16[1,8,1536,64]{2,3,1,0:T(8,128)(2,1)} %param.5) | copy-start | bytes 4718596
  2.4 14.8 %collective-permute-start.2 = (bf16[4,64,1024]{2,1,0:T(8,128)(2,1)S(1)}, bf16[4,64,1024]{2,1,0:T(8,128)(2,1)S(1)}, u32[]{:S(2)}, u32[]{:S(2)}) collective-permute-start(bf16[4,64,1024]{2,1,0:T(8,128)(2,1)S(1)} %get-tuple-element.42.refs_0_), channel_id=1, source_target_pairs={{0,1},{1,0},{2,3},{3,2},{4,5},{5,4},{6,7},{7,6},{8,9},{9,8},{10,11... | collective-permute-start | bytes 1572872 | tf_op jit(solution)/shard_map/ppermute | solution.py:582
  2.4 14.8 %collective-permute-start.3 = (bf16[4,64,1024]{2,1,0:T(8,128)(2,1)S(1)}, bf16[4,64,1024]{2,1,0:T(8,128)(2,1)S(1)}, u32[]{:S(2)}, u32[]{:S(2)}) collective-permute-start(bf16[4,64,1024]{2,1,0:T(8,128)(2,1)S(1)} %get-tuple-element.48.refs_2_), channel_id=1, source_target_pairs={{0,2},{1,3},{2,0},{3,1},{4,6},{5,7},{6,4},{7,5},{8,10},{9,11},{10,... | collective-permute-start | bytes 1572872 | tf_op jit(solution)/shard_map/ppermute | solution.py:582
  4.7 18.1 %collective-permute-start.6 = (bf16[4,64,512]{2,1,0:T(8,128)(2,1)S(1)}, bf16[4,64,512]{2,1,0:T(8,128)(2,1)S(1)}, u32[]{:S(2)}, u32[]{:S(2)}) collective-permute-start(bf16[4,64,512]{2,1,0:T(8,128)(2,1)S(1)} %get-tuple-element.44.refs_4_), channel_id=1, source_target_pairs={{0,1},{1,0},{2,3},{3,2},{4,5},{5,4},{6,7},{7,6},{8,9},{9,8},{10,11... | collective-permute-start | bytes 786440 | tf_op jit(solution)/shard_map/ppermute | solution.py:582
  6.2 16.6 %collective-permute-start.7 = (bf16[4,64,512]{2,1,0:T(8,128)(2,1)S(1)}, bf16[4,64,512]{2,1,0:T(8,128)(2,1)S(1)}, u32[]{:S(2)}, u32[]{:S(2)}) collective-permute-start(bf16[4,64,512]{2,1,0:T(8,128)(2,1)S(1)} %get-tuple-element.54.refs_6_), channel_id=1, source_target_pairs={{0,2},{1,3},{2,0},{3,1},{4,6},{5,7},{6,4},{7,5},{8,10},{9,11},{10,... | collective-permute-start | bytes 786440 | tf_op jit(solution)/shard_map/ppermute | solution.py:582
  6.8 2.3 %copy-start = (f32[1536,768]{1,0:T(8,128)S(1)}, f32[1536,768]{1,0:T(8,128)}, u32[]{:S(2)}) copy-start(f32[1536,768]{1,0:T(8,128)} %anc_ref.4) | copy-start | bytes 14155780
  9.1 1.9 %copy-start.4 = (s32[1,8,6]{1,0,2:T(1,128)S(1)}, s32[1,8,6]{1,0,2:T(1,128)}, u32[]{:S(2)}) copy-start(s32[1,8,6]{1,0,2:T(1,128)} %param.8) | copy-start | bytes 580
  9.8 5.0 %collective-permute-start = (f32[3,128,128]{2,1,0:T(8,128)S(1)}, f32[3,128,128]{2,1,0:T(8,128)S(1)}, u32[]{:S(2)}, u32[]{:S(2)}) collective-permute-start(f32[3,128,128]{2,1,0:T(8,128)S(1)} %later_blocks.1), channel_id=1, source_target_pairs={{0,4},{1,5},{6,2},{7,3},{8,12},{9,13},{14,10},{15,11},{16,20},{17,... | collective-permute-start | bytes 589832 | tf_op jit(solution)/shard_map/ppermute | solution.py:566
  11.2 1.4 %copy-start.2 = (bf16[1,8,128,768]{3,2,1,0:T(8,128)(2,1)S(1)}, bf16[1,8,128,768]{3,2,1,0:T(8,128)(2,1)}, u32[]{:S(2)}) copy-start(bf16[1,8,128,768]{3,2,1,0:T(8,128)(2,1)} %param.6) | copy-start | bytes 4718596
  18.2 16.2 %collective-permute-start.4 = (bf16[2,4,64,512]{3,2,1,0:T(8,128)(2,1)S(1)}, bf16[2,4,64,512]{3,2,1,0:T(8,128)(2,1)S(1)}, u32[]{:S(2)}, u32[]{:S(2)}) collective-permute-start(bf16[2,4,64,512]{3,2,1,0:T(8,128)(2,1)S(1)} %get-tuple-element.49), channel_id=1, source_target_pairs={{0,2},{1,3},{2,0},{3,1},{4,6},{5,7},{6,4},{7,5},{8,10},{9,11},{10,... | collective-permute-start | bytes 1572872 | tf_op jit(solution)/shard_map/ppermute | solution.py:582
  20.3 15.8 %collective-permute-start.5 = (bf16[2,4,64,512]{3,2,1,0:T(8,128)(2,1)S(1)}, bf16[2,4,64,512]{3,2,1,0:T(8,128)(2,1)S(1)}, u32[]{:S(2)}, u32[]{:S(2)}) collective-permute-start(bf16[2,4,64,512]{3,2,1,0:T(8,128)(2,1)S(1)} %get-tuple-element.50), channel_id=1, source_target_pairs={{0,1},{1,0},{2,3},{3,2},{4,5},{5,4},{6,7},{7,6},{8,9},{9,8},{10,11... | collective-permute-start | bytes 1572872 | tf_op jit(solution)/shard_map/ppermute | solution.py:582
  23.8 21.5 %collective-permute-start.8 = (bf16[2,4,64,512]{3,2,1,0:T(8,128)(2,1)S(1)}, bf16[2,4,64,512]{3,2,1,0:T(8,128)(2,1)S(1)}, u32[]{:S(2)}, u32[]{:S(2)}) collective-permute-start(bf16[2,4,64,512]{3,2,1,0:T(8,128)(2,1)S(1)} %get-tuple-element.55), channel_id=1, source_target_pairs={{0,2},{1,3},{2,0},{3,1},{4,6},{5,7},{6,4},{7,5},{8,10},{9,11},{10,... | collective-permute-start | bytes 1572872 | tf_op jit(solution)/shard_map/ppermute | solution.py:582
  25.9 3.0 %copy-start.3 = (s32[1,8,12]{2,1,0:T(8,128)S(1)}, s32[1,8,12]{2,1,0:T(8,128)}, u32[]{:S(2)}) copy-start(s32[1,8,12]{2,1,0:T(8,128)} %param.7) | copy-start | bytes 1156
  25.9 20.5 %collective-permute-start.9 = (bf16[2,4,64,512]{3,2,1,0:T(8,128)(2,1)S(1)}, bf16[2,4,64,512]{3,2,1,0:T(8,128)(2,1)S(1)}, u32[]{:S(2)}, u32[]{:S(2)}) collective-permute-start(bf16[2,4,64,512]{3,2,1,0:T(8,128)(2,1)S(1)} %get-tuple-element.56), channel_id=1, source_target_pairs={{0,1},{1,0},{2,3},{3,2},{4,5},{5,4},{6,7},{7,6},{8,9},{9,8},{10,11... | collective-permute-start | bytes 1572872 | tf_op jit(solution)/shard_map/ppermute | solution.py:582
  28.3 36.2 %collective-permute-start.14 = (bf16[2,4,64,512]{3,2,1,0:T(8,128)(2,1)S(1)}, bf16[2,4,64,512]{3,2,1,0:T(8,128)(2,1)S(1)}, u32[]{:S(2)}, u32[]{:S(2)}) collective-permute-start(bf16[2,4,64,512]{3,2,1,0:T(8,128)(2,1)S(1)} %get-tuple-element.69), channel_id=1, source_target_pairs={{0,2},{1,3},{2,0},{3,1},{4,6},{5,7},{6,4},{7,5},{8,10},{9,11},{10,... | collective-permute-start | bytes 1572872 | tf_op jit(solution)/shard_map/ppermute | solution.py:582
  34.4 30.1 %collective-permute-start.15 = (bf16[2,4,64,512]{3,2,1,0:T(8,128)(2,1)S(1)}, bf16[2,4,64,512]{3,2,1,0:T(8,128)(2,1)S(1)}, u32[]{:S(2)}, u32[]{:S(2)}) collective-permute-start(bf16[2,4,64,512]{3,2,1,0:T(8,128)(2,1)S(1)} %get-tuple-element.70), channel_id=1, source_target_pairs={{0,1},{1,0},{2,3},{3,2},{4,5},{5,4},{6,7},{7,6},{8,9},{9,8},{10,11... | collective-permute-start | bytes 1572872 | tf_op jit(solution)/shard_map/ppermute | solution.py:582
  38.1 10.4 %collective-permute-start.10 = (s16[272,768]{1,0:T(8,128)(2,1)S(1)}, s16[272,768]{1,0:T(8,128)(2,1)S(1)}, u32[]{:S(2)}, u32[]{:S(2)}) collective-permute-start(s16[272,768]{1,0:T(8,128)(2,1)S(1)} %get-tuple-element.62), channel_id=1, source_target_pairs={{0,8},{8,0},{16,24},{24,16},{1,9},{9,1},{17,25},{25,17},{2,10},{10... | collective-permute-start | bytes 1253384 | tf_op jit(solution)/shard_map/ppermute | solution.py:569
  49.4 10.5 %collective-permute-start.11 = (s16[272,768]{1,0:T(8,128)(2,1)S(1)}, s16[272,768]{1,0:T(8,128)(2,1)S(1)}, u32[]{:S(2)}, u32[]{:S(2)}) collective-permute-start(s16[272,768]{1,0:T(8,128)(2,1)S(1)} %get-tuple-element.64), channel_id=1, source_target_pairs={{1,17},{2,18},{4,20},{7,23},{9,25},{10,26},{12,28},{15,31},{16,0},... | collective-permute-start | bytes 1253384 | tf_op jit(solution)/shard_map/ppermute | solution.py:579
  53.9 2.2 %collective-permute-start.16 = (s16[144,384]{1,0:T(8,128)(2,1)S(1)}, s16[144,384]{1,0:T(8,128)(2,1)S(1)}, u32[]{:S(2)}, u32[]{:S(2)}) collective-permute-start(s16[144,384]{1,0:T(8,128)(2,1)S(1)} %get-tuple-element.72), channel_id=1, source_target_pairs={{0,4},{1,5},{6,2},{7,3},{8,12},{9,13},{14,10},{15,11},{16,20},{17,... | collective-permute-start | bytes 331784 | tf_op jit(solution)/shard_map/ppermute | solution.py:566
  56.9 7.5 %collective-permute-start.17 = (s16[144,384]{1,0:T(8,128)(2,1)S(1)}, s16[144,384]{1,0:T(8,128)(2,1)S(1)}, u32[]{:S(2)}, u32[]{:S(2)}) collective-permute-start(s16[144,384]{1,0:T(8,128)(2,1)S(1)} %pick.1.mine_ref), channel_id=1, source_target_pairs={{0,8},{8,0},{16,24},{24,16},{1,9},{9,1},{17,25},{25,17},{2,10},{10... | collective-permute-start | bytes 331784 | tf_op jit(solution)/shard_map/ppermute | solution.py:569
  58.5 17.1 %collective-permute-start.12 = (s16[272,768]{1,0:T(8,128)(2,1)S(1)}, s16[272,768]{1,0:T(8,128)(2,1)S(1)}, u32[]{:S(2)}, u32[]{:S(2)}) collective-permute-start(s16[272,768]{1,0:T(8,128)(2,1)S(1)} %get-tuple-element.65), channel_id=1, source_target_pairs={{0,8},{8,0},{16,24},{24,16},{1,9},{9,1},{17,25},{25,17},{2,10},{10... | collective-permute-start | bytes 1253384 | tf_op jit(solution)/shard_map/ppermute | solution.py:569
  64.3 13.5 %slice-start = ((s8[4718592]{0:T(1024)(128)(4,1)}), s8[4194304]{0:T(1024)(128)(4,1)S(1)}, s32[]{:S(2)}) async-start(s8[4718592]{0:T(1024)(128)(4,1)} %bitcast.14), calls=%async_computation | async-start | bytes 8388608
  64.4 13.4 %slice-start.1 = ((s8[4718592]{0:T(1024)(128)(4,1)}), s8[524288]{0:T(1024)(128)(4,1)S(1)}, s32[]{:S(2)}) async-start(s8[4718592]{0:T(1024)(128)(4,1)} %bitcast.14), calls=%async_computation.1 | async-start | bytes 1048576
  64.5 13.3 %collective-permute-start.18 = (s16[144,384]{1,0:T(8,128)(2,1)S(1)}, s16[144,384]{1,0:T(8,128)(2,1)S(1)}, u32[]{:S(2)}, u32[]{:S(2)}) collective-permute-start(s16[144,384]{1,0:T(8,128)(2,1)S(1)} %add_coded.1.one_ref), channel_id=1, source_target_pairs={{0,16},{8,24},{16,0},{24,8},{1,17},{9,25},{17,1},{25,9},{2,18},{10... | collective-permute-start | bytes 331784 | tf_op jit(solution)/shard_map/ppermute | solution.py:569
  66.7 19.4 %collective-permute-start.19 = (s16[272,768]{1,0:T(8,128)(2,1)S(1)}, s16[272,768]{1,0:T(8,128)(2,1)S(1)}, u32[]{:S(2)}, u32[]{:S(2)}) collective-permute-start(s16[272,768]{1,0:T(8,128)(2,1)S(1)} %get-tuple-element.76), channel_id=1, source_target_pairs={{0,8},{8,0},{16,24},{24,16},{1,9},{9,1},{17,25},{25,17},{2,10},{10... | collective-permute-start | bytes 1253384 | tf_op jit(solution)/shard_map/ppermute | solution.py:569
  76.4 22.1 %collective-permute-start.13 = (s16[144,768]{1,0:T(8,128)(2,1)S(1)}, s16[144,768]{1,0:T(8,128)(2,1)S(1)}, u32[]{:S(2)}, u32[]{:S(2)}) collective-permute-start(s16[144,768]{1,0:T(8,128)(2,1)S(1)} %get-tuple-element.67), channel_id=1, source_target_pairs={{0,16},{1,17},{2,18},{3,19},{4,20},{5,21},{6,22},{7,23},{8,24},{9,... | collective-permute-start | bytes 663560 | tf_op jit(solution)/shard_map/ppermute | solution.py:579
  86.9 15.9 %collective-permute-start.20 = (s16[272,768]{1,0:T(8,128)(2,1)S(1)}, s16[272,768]{1,0:T(8,128)(2,1)S(1)}, u32[]{:S(2)}, u32[]{:S(2)}) collective-permute-start(s16[272,768]{1,0:T(8,128)(2,1)S(1)} %get-tuple-element.80), channel_id=1, source_target_pairs={{0,16},{3,19},{5,21},{6,22},{8,24},{11,27},{13,29},{14,30},{17,1},... | collective-permute-start | bytes 1253384 | tf_op jit(solution)/shard_map/ppermute | solution.py:579
  95.0 4.5 %collective-permute-start.21 = (f32[3,128,128]{2,1,0:T(8,128)S(1)}, f32[3,128,128]{2,1,0:T(8,128)S(1)}, u32[]{:S(2)}, u32[]{:S(2)}) collective-permute-start(f32[3,128,128]{2,1,0:T(8,128)S(1)} %factor.3.refs_6_), channel_id=1, source_target_pairs={{0,4},{4,0},{1,5},{5,1},{2,6},{6,2},{3,7},{7,3},{8,12},{12,8},{9,1... | collective-permute-start | bytes 589832 | tf_op jit(solution)/shard_map/ppermute | solution.py:623

commit v10 on v9

--- a/solution.py
+++ b/solution.py
@@ -17,8 +17,8 @@
 EXP_ROWS = 16
 HALF_STEPS = 48
 LU = 10
-NEAR = 10
-FAR = 10
+NEAR = 2
+FAR = 2
 
 
 def cost(micros):
@@ -90,22 +90,16 @@
     )(blocks)
 
 
-def set_numbers(group, blocks):
-    return range(blocks - 1) if group == 0 else range(blocks - 1, blocks)
-
-
-def halves_kernel(group, layers, blocks, lt_ref, one_ref, two_ref, sems):
+def halves_kernel(number, layers, blocks, lt_ref, one_ref, two_ref, sems):
     half = one_ref.shape[0]
-    numbers = set_numbers(group, blocks)
-    size = len(numbers) * BLK
     copies = []
     for h, ref in enumerate((one_ref, two_ref)):
         for t in range(layers):
-            begin = (t * blocks + numbers[0]) * BLK
+            begin = (t * blocks + number) * BLK
             copies.append(
                 pltpu.make_async_copy(
-                    lt_ref.at[h * half : (h + 1) * half, :, begin : begin + size],
-                    ref.at[:, :, t * size : (t + 1) * size],
+                    lt_ref.at[h * half : (h + 1) * half, :, begin : begin + BLK],
+                    ref.at[:, :, t * BLK : (t + 1) * BLK],
                     sems.at[h, t],
                 )
             )
@@ -115,12 +109,11 @@
         copy.wait()
 
 
-def halves(lt, group, layers, blocks):
+def halves(lt, number, layers, blocks):
     supers, depth, _ = lt.shape
-    size = layers * len(set_numbers(group, blocks)) * BLK
-    one = jax.ShapeDtypeStruct((supers // 2, depth, size), lt.dtype)
-    return pl.pallas_call(
-        functools.partial(halves_kernel, group, layers, blocks),
+    one = jax.ShapeDtypeStruct((supers // 2, depth, layers * BLK), lt.dtype)
+    return pl.pallas_call(
+        functools.partial(halves_kernel, number, layers, blocks),
         out_shape=[one, one],
         in_specs=[ANY],
         out_specs=[ANY, ANY],
@@ -136,29 +129,22 @@
     return 2 * half + part
 
 
-def group_of(spot, blocks):
-    return 0 if spot[1] < blocks - 1 else 1
-
-
-def used_sets(sets, chunk, blocks):
-    groups = sorted({group_of(spot, blocks) for spot in chunk})
-    return [ref for group in groups for ref in sets[group]]
-
-
-def place(where_ref, chunk, spot, part, blocks, flip=0):
-    groups = sorted({group_of(other, blocks) for other in chunk})
-    group = group_of(spot, blocks)
-    numbers = set_numbers(group, blocks)
-    begin = share_at(where_ref, spot, part, flip) * len(numbers) + spot[1] - numbers[0]
-    return 4 * groups.index(group), pl.ds(pl.multiple_of(begin * BLK, BLK), BLK)
-
-
-def split_kernel(chunk, blocks, where_ref, *refs):
+def used_sets(sets, chunk):
+    return [ref for number in sorted({spot[1] for spot in chunk}) for ref in sets[number]]
+
+
+def place(where_ref, chunk, spot, part, flip=0):
+    numbers = sorted({other[1] for other in chunk})
+    begin = pl.multiple_of(share_at(where_ref, spot, part, flip) * BLK, BLK)
+    return 4 * numbers.index(spot[1]), pl.ds(begin, BLK)
+
+
+def split_kernel(chunk, where_ref, *refs):
     sources, (one_ref, two_ref, sems) = refs[:-3], refs[-3:]
     copies = []
     for part in range(2):
         for m, spot in enumerate(chunk):
-            first, lanes = place(where_ref, chunk, spot, part, blocks, flip=1)
+            first, lanes = place(where_ref, chunk, spot, part, flip=1)
             at = (part * len(chunk) + m) * BLK
             for n in range(4):
                 copies.append(
@@ -174,13 +160,13 @@
         copy.wait()
 
 
-def split(where, sets, chunk, blocks):
-    sources = used_sets(sets, chunk, blocks)
+def split(where, sets, chunk):
+    sources = used_sets(sets, chunk)
     half, depth, _ = sources[0].shape
     count = len(chunk)
     one = jax.ShapeDtypeStruct((2, half, depth, 2 * count * BLK), sources[0].dtype)
     return pl.pallas_call(
-        functools.partial(split_kernel, chunk, blocks),
+        functools.partial(split_kernel, chunk),
         out_shape=[one, one],
         in_specs=[SMEM] + [ANY] * len(sources),
         out_specs=[ANY, ANY],
@@ -259,7 +245,7 @@
     sources, (right_ref, acc_ref, left) = refs[:-3], refs[-3:]
 
     def pieces(part, m, h, n, i):
-        first, lanes = place(where_ref, chunk, chunk[m], part, blocks)
+        first, lanes = place(where_ref, chunk, chunk[m], part)
         return sources[first + 2 * h + n][i, :, lanes]
 
     total = product(chunk, blocks, where_ref, lpat_ref, pieces, right_ref, left)
@@ -267,7 +253,7 @@
 
 
 def near_update(where, lpat, sets, right, chunk, blocks):
-    sources = used_sets(sets, chunk, blocks)
+    sources = used_sets(sets, chunk)
     supers, kdim, cols = right.shape
     count = 2 * len(chunk)
     return pl.pallas_call(
@@ -583,49 +569,59 @@
 
     lt = jnp.swapaxes(lpanel[0], 1, 2)
     u = upanel[0]
-    a, b = halves(lt, 0, layers, blocks)
     uo = lax.ppermute(u, "row", xor_perm(rows, 1))
-    sets = [(a, over(a, 1), b, over(b, 2))]
-    a, b = halves(after(lt, a), 1, layers, blocks)
-    sets.append((a, over(a, 1), b, over(b, 2)))
     near_right, far_right = masked_right(where, upat[0], u, uo)
-    rounds = [(phase, number) for phase in range(2) for number in range(blocks)]
-    chunks = [rounds[n : n + 2] for n in range(0, len(rounds), 2)]
-    given = to_other_core(later_blocks(where, after(anc, a), blocks))
-    sides = []
-    for chunk in chunks:
-        before = sides[-1] if sides else [given, near_right]
-        sides.append(split(after(where, *before), sets, chunk, blocks))
-    others = [(over(one, 2), over(two, 1)) for one, two in sides]
     masks = lpat[0]
-    parts = [near_update(where, masks, sets, near_right, chunk, blocks) for chunk in chunks]
-    known = []
-
-    def far_part(j, *waits):
-        part = after(parts[j], *waits) if waits else parts[j]
+    chunks = []
+    for phase in range(2):
+        cut = 1 if phase == 0 else blocks - 1
+        spots_here = [(phase, number) for number in range(blocks)]
+        chunks += [spots_here[:cut], spots_here[cut:]]
+    sets, sides, others = [], [], []
+
+    def first_step(number, *waits):
+        a, b = halves(after(lt, *waits) if waits else lt, number, layers, blocks)
+        sets.append((a, over(a, 1), b, over(b, 2)))
+
+    def second_step(*waits):
+        chunk = chunks[len(sides)]
+        sides.append(split(after(where, *waits), sets, chunk))
+        others.append((over(sides[-1][0], 2), over(sides[-1][1], 1)))
+
+    def far_part(j, known, *waits):
+        part = near_update(where, masks, sets, near_right, chunks[j], blocks)
+        part = after(part, *waits) if waits else part
         return far_update(where, masks, others[j], far_right, part, known, chunks[j], blocks)
 
-    kept0, coded0, *diag = far_part(0)
-    known = diag
-    kept1, coded1, *diag = far_part(1, kept0, parts[2])
-    sum0, sent0 = halve(where, after(kept0, kept1), over_layers(coded0, 1), chunks[0])
-    known = []
+    first_step(0)
+    first_step(1, sets[0][0])
+    given = to_other_core(later_blocks(where, after(anc, sets[0][0]), blocks))
+    second_step(near_right)
+    for number in range(2, blocks):
+        first_step(number, sides[0][0])
+    second_step(sides[0][0], given)
+    kept0, coded0, *diag = far_part(0, [], sides[1][0])
+    sum0, sent0 = halve(where, kept0, over_layers(coded0, 1), chunks[0])
+    got0 = far_layers(sent0, chunks[0])
+    second_step(sides[1][0], kept0)
+    kept1, coded1, *diag = far_part(1, diag, kept0, sent0)
     mine = pick(where, diag[0], to_other_core(diag[1]))
-    got0 = far_layers(sent0, chunks[0])
-    near = add_coded(after(mine, got0), over_layers(mine, 1))
+    near = add_coded(mine, over_layers(mine, 1))
+    sum1, sent1 = halve(where, kept1, over_layers(coded1, 1), chunks[1])
+    got1 = far_layers(sent1, chunks[1])
     far = over_layers(near, 2)
     own = pivots(where, anc, given, near, far)
-    kept2, coded2 = far_part(2, mine, sent0)
-    sum1, sent1 = halve(where, kept1, over_layers(coded1, 1), chunks[1])
-    half_lu = factor(after(own, sent1, coded2), 0, HALF_STEPS)
-    sum2, sent2 = halve(where, after(kept2, half_lu), over_layers(coded2, 1), chunks[2])
-    lu = factor(after(half_lu, sent2), HALF_STEPS, BLK)
+    second_step(sides[2][0], mine)
+    kept2, coded2 = far_part(2, [], kept1, mine, got0)
+    kept3, coded3 = far_part(3, [], kept2, near)
+    sum2, sent2 = halve(where, after(kept2, kept3), over_layers(coded2, 1), chunks[2])
+    got2 = far_layers(sent2, chunks[2])
+    half_lu = factor(after(own, sent2, coded3), 0, HALF_STEPS)
+    sum3, sent3 = halve(where, after(kept3, half_lu), over_layers(coded3, 1), chunks[3])
+    got3 = far_layers(sent3, chunks[3])
+    lu = factor(after(half_lu, sent3), HALF_STEPS, BLK)
     lu_got = lax.ppermute(lu, "row", xor_perm(rows, 1))
-    pairs = [
-        (sum0, got0),
-        (sum1, far_layers(sent1, chunks[1])),
-        (sum2, far_layers(sent2, chunks[2])),
-    ]
+    pairs = [(sum0, got0), (sum1, got1), (sum2, got2), (sum3, got3)]
     return tuple(combine(where, anc, pairs, lu, lu_got, chunks, share))
 
 

time: 107 us -> 114 us (1.065)
  the two profiles are of different devices: /device:TPU:2 before, /device:TPU:7 now
where the time goes in v10:
time: 114 us
  Pallas kernels  43.2 us (38%)
  starting transfers between devices  38.4 us (34%)
  waiting for transfers between devices  26.4 us (23%)
  local copies, waits for them, and re-layouts  4.63 us (4%)
  between operations  1.21 us (1%)
    pallas_call x2, Pallas kernels, factor(): pl.pallas_call(functools.partial(lu_kernel, begin, end), out_shape=jax.Sh...  11.4 us
    ppermute x6, waiting for transfers between devices, over_layers(): return lax.ppermute(value, 'layer', xor_perm(layers, bit))  11.4 us
    ppermute x14, starting transfers between devices, over(): return lax.ppermute(value, 'col', xor_perm(cols, bit))  10.3 us
    ppermute x6, starting transfers between devices, over_layers(): return lax.ppermute(value, 'layer', xor_perm(layers, bit))  8.81 us
    ppermute x4, starting transfers between devices, far_layers(): return lax.ppermute(value, everyone, perm)  8.46 us
    ppermute x14, waiting for transfers between devices, over(): return lax.ppermute(value, 'col', xor_perm(cols, bit))  8.3 us
    pallas_call x4, Pallas kernels, near_update(): pl.pallas_call(functools.partial(near_kernel, chunk, blocks), out_shape=j...  7.88 us
    pallas_call x4, Pallas kernels, far_update(): pl.pallas_call(functools.partial(far_kernel, chunk, blocks, len(earlier))...  7.11 us
  transfers between devices with their start and end apart: 28, of which 8 were waited for; matrix products, arithmetic and copies ran while one was open for 0% of the time, Pallas kernels for 36%

profile of v10, /device:TPU:7, one launch (start us, length us, event | category | flops | bytes accessed | tf_op | source)
XLA Modules:
  0.0 113.9 jit_solution(17874695638587756585)
XLA Ops:
  0.6 0.7 collective-permute-start
  1.4 1.4 %copy-done.1 = bf16[1,8,1536,64]{2,3,1,0:T(8,128)(2,1)S(1)} copy-done((bf16[1,8,1536,64]{2,3,1,0:T(8,128)(2,1)S(1)}, bf16[1,8,1536,64]{2,3,1,0:T(8,128)(2,1)}, u32[]{:S(2)}) %copy-start.1) | copy-done | bytes 1572888
  2.8 0.8 halves.3
  4.9 1.4 %collective-permute-start.6 = (bf16[4,64,512]{2,1,0:T(8,128)(2,1)S(1)}, bf16[4,64,512]{2,1,0:T(8,128)(2,1)}, u32[]{:S(2)}, u32[]{:S(2)}) collective-permute-start(bf16[4,64,512]{2,1,0:T(8,128)(2,1)S(1)} %get-tuple-element.63.refs_0_.refs_4_), channel_id=1, source_target_pairs={{0,1},{1,0},{2,3},{3,2},{4,5},{5,4},{6,7},{7,6},{8,9},{9,8},{10,11... | collective-permute-start | bytes 786440 | tf_op jit(solution)/shard_map/ppermute | solution.py:568
  6.4 2.3 %copy-done = f32[1536,768]{1,0:T(8,128)S(1)} copy-done((f32[1536,768]{1,0:T(8,128)S(1)}, f32[1536,768]{1,0:T(8,128)}, u32[]{:S(2)}) %copy-start) | copy-done | bytes 4718616
  8.7 1.3 %later_blocks.1 = f32[3,128,128]{2,1,0:T(8,128)} custom-call(s32[8]{0:T(128)S(1)} %stack.35.where_ref, f32[1536,768]{1,0:T(8,128)S(1)} %copy-done), custom_call_target="tpu_custom_call" | custom-call | flops 1000 | bytes 1000 | tf_op jit(solution)/shard_map/later_blocks/pallas_call | solution.py:480
  10.0 3.4 %collective-permute-start.5 = (f32[3,128,128]{2,1,0:T(8,128)}, f32[3,128,128]{2,1,0:T(8,128)}, u32[]{:S(2)}, u32[]{:S(2)}) collective-permute-start(f32[3,128,128]{2,1,0:T(8,128)} %later_blocks.1), channel_id=1, source_target_pairs={{0,4},{1,5},{6,2},{7,3},{8,12},{9,13},{14,10},{15,11},{16,20},{17,... | collective-permute-start | bytes 589832 | tf_op jit(solution)/shard_map/ppermute | solution.py:552
  13.5 1.4 %masked_right.1 = (bf16[8,128,768]{2,1,0:T(8,128)(2,1)S(1)}, bf16[8,128,768]{2,1,0:T(8,128)(2,1)S(1)}) custom-call(s32[8]{0:T(128)S(1)} %stack.35.where_ref, s32[8,6]{1,0:T(8,128)S(1)} %bitcast.21, bf16[8,128,768]{2,1,0:T(8,128)(2,1)S(1)} %bitcast.20, bf16[8,128,768]{2,1,0:T(8,128)(2,1)S(1)} %collective-permute-done.uo_ref), custom_call_target="tpu_custom_call" | custom-call | flops 1000 | bytes 1000 | tf_op jit(solution)/shard_map/masked_right/pallas_call | solution.py:212
  15.0 1.7 %split.4 = (bf16[2,4,64,256]{3,2,1,0:T(8,128)(2,1)S(1)}, bf16[2,4,64,256]{3,2,1,0:T(8,128)(2,1)S(1)}) custom-call(s32[8]{0:T(128)S(1)} %stack.35.where_ref, bf16[4,64,512]{2,1,0:T(8,128)(2,1)} %get-tuple-element.55.refs_0_, bf16[4,64,512]{2,1,0:T(8,128)(2,1)} %collective-permute-done.1.refs_1_, bf16[4,64,512]{2,1,0:T(8,128)(2,1)} %get-tuple-element.56.refs_2_, ...), custom_call_target="tpu_custom_call" | custom-call | flops 1000 | bytes 1000 | tf_op jit(solution)/shard_map/split/pallas_call | solution.py:168
  16.9 1.5 %collective-permute-start.9 = (bf16[4,64,512]{2,1,0:T(8,128)(2,1)S(1)}, bf16[4,64,512]{2,1,0:T(8,128)(2,1)S(1)}, u32[]{:S(2)}, u32[]{:S(2)}) collective-permute-start(bf16[4,64,512]{2,1,0:T(8,128)(2,1)S(1)} %get-tuple-element.67.refs_6_.refs_2_), channel_id=1, source_target_pairs={{0,2},{1,3},{2,0},{3,1},{4,6},{5,7},{6,4},{7,5},{8,10},{9,11},{10,... | collective-permute-start | bytes 786440 | tf_op jit(solution)/shard_map/ppermute | solution.py:568
  18.5 1.4 %collective-permute-start.4 = (bf16[2,4,64,256]{3,2,1,0:T(8,128)(2,1)S(1)}, bf16[2,4,64,256]{3,2,1,0:T(8,128)(2,1)S(1)}, u32[]{:S(2)}, u32[]{:S(2)}) collective-permute-start(bf16[2,4,64,256]{3,2,1,0:T(8,128)(2,1)S(1)} %get-tuple-element.58), channel_id=1, source_target_pairs={{0,1},{1,0},{2,3},{3,2},{4,5},{5,4},{6,7},{7,6},{8,9},{9,8},{10,11... | collective-permute-start | bytes 786440 | tf_op jit(solution)/shard_map/ppermute | solution.py:568
  19.9 1.7 %collective-permute-done.7.refs_3_.refs_7_ = bf16[4,64,512]{2,1,0:T(8,128)(2,1)S(1)} collective-permute-done((bf16[4,64,512]{2,1,0:T(8,128)(2,1)}, bf16[4,64,512]{2,1,0:T(8,128)(2,1)S(1)}, u32[]{:S(2)}, u32[]{:S(2)}) %collective-permute-start.7) | collective-permute-done | bytes 262176 | tf_op jit(solution)/shard_map/ppermute | solution.py:568
  21.7 1.9 %collective-permute-done.8.refs_5_.refs_1_ = bf16[4,64,512]{2,1,0:T(8,128)(2,1)S(1)} collective-permute-done((bf16[4,64,512]{2,1,0:T(8,128)(2,1)S(1)}, bf16[4,64,512]{2,1,0:T(8,128)(2,1)S(1)}, u32[]{:S(2)}, u32[]{:S(2)}) %collective-permute-start.8) | collective-permute-done | bytes 262176 | tf_op jit(solution)/shard_map/ppermute | solution.py:568
  23.6 3.5 %collective-permute-done.9.refs_7_.refs_3_ = bf16[4,64,512]{2,1,0:T(8,128)(2,1)S(1)} collective-permute-done((bf16[4,64,512]{2,1,0:T(8,128)(2,1)S(1)}, bf16[4,64,512]{2,1,0:T(8,128)(2,1)S(1)}, u32[]{:S(2)}, u32[]{:S(2)}) %collective-permute-start.9) | collective-permute-done | bytes 262176 | tf_op jit(solution)/shard_map/ppermute | solution.py:568
  27.1 1.6 %split.5 = (bf16[2,4,64,512]{3,2,1,0:T(8,128)(2,1)S(1)}, bf16[2,4,64,512]{3,2,1,0:T(8,128)(2,1)S(1)}) custom-call(s32[8]{0:T(128)S(1)} %stack.35.where_ref, bf16[4,64,512]{2,1,0:T(8,128)(2,1)S(1)} %get-tuple-element.63.refs_0_.refs_4_, bf16[4,64,512]{2,1,0:T(8,128)(2,1)} %collective-permute-done.6.refs_1_.refs_5_, bf16[4,64,512]{2,1,0:T(8,128)(2,1)S(1)} %copy-done.5, ...), custom_call_target="tpu_custom_call" | custom-call | flops 1000 | bytes 1000 | tf_op jit(solution)/shard_map/split/pallas_call | solution.py:168
  28.8 0.9 collective-permute-start.13
  29.7 1.9 %near_update.4.refs_1_ = f32[2,128,768]{2,1,0:T(8,128)S(1)} custom-call(s32[8]{0:T(128)S(1)} %stack.35.where_ref, s32[8,12]{1,0:T(8,128)S(1)} %bitcast.22, bf16[4,64,512]{2,1,0:T(8,128)(2,1)} %get-tuple-element.55.refs_0_, bf16[4,64,512]{2,1,0:T(8,128)(2,1)} %collective-permute-done.1.refs_1_, bf16[4,64,512]{2,1,0:T(8,128)(2,1)} %get-tuple-element.56.refs_2_, ...), custom_call_target="tpu_custom_call" | custom-call | flops 2000001024 | bytes 1000 | tf_op jit(solution)/shard_map/near_update/pallas_call | solution.py:259
  31.6 1.1 collective-permute-done.3.a_ref
  32.7 1.5 %far_update.4 = (f32[1,128,768]{2,1,0:T(8,128)S(1)}, s16[144,768]{1,0:T(8,128)(2,1)S(1)}, s16[144,384]{1,0:T(8,128)(2,1)S(1)}, s16[144,384]{1,0:T(8,128)(2,1)S(1)}) custom-call(s32[8]{0:T(128)S(1)} %stack.35.where_ref, s32[8,12]{1,0:T(8,128)S(1)} %bitcast.23, bf16[2,4,64,256]{3,2,1,0:T(8,128)(2,1)S(1)} %collective-permute-done.3.a_ref, ...), custom_call_target="tpu_custom_call" | custom-call | flops 2000001024 | bytes 1000 | tf_op jit(solution)/shard_map/far_update/pallas_call | solution.py:308
  34.2 1.4 %collective-permute-start.10 = (s16[144,768]{1,0:T(8,128)(2,1)S(1)}, s16[144,768]{1,0:T(8,128)(2,1)S(1)}, u32[]{:S(2)}, u32[]{:S(2)}) collective-permute-start(s16[144,768]{1,0:T(8,128)(2,1)S(1)} %get-tuple-element.71), channel_id=1, source_target_pairs={{0,8},{8,0},{16,24},{24,16},{1,9},{9,1},{17,25},{25,17},{2,10},{10... | collective-permute-start | bytes 663560 | tf_op jit(solution)/shard_map/ppermute | solution.py:555
  35.5 1.8 %split.6 = (bf16[2,4,64,512]{3,2,1,0:T(8,128)(2,1)S(1)}, bf16[2,4,64,512]{3,2,1,0:T(8,128)(2,1)S(1)}) custom-call(s32[8]{0:T(128)S(1)} %stack.35.where_ref, bf16[4,64,512]{2,1,0:T(8,128)(2,1)} %get-tuple-element.55.refs_0_, bf16[4,64,512]{2,1,0:T(8,128)(2,1)} %collective-permute-done.1.refs_1_, bf16[4,64,512]{2,1,0:T(8,128)(2,1)} %get-tuple-element.56.refs_2_, ...), custom_call_target="tpu_custom_call" | custom-call | flops 1000 | bytes 1000 | tf_op jit(solution)/shard_map/split/pallas_call | solution.py:168
  37.5 1.0 collective-permute-start.17
  38.4 2.2 %near_update.5.refs_1_ = f32[4,128,768]{2,1,0:T(8,128)S(1)} custom-call(s32[8]{0:T(128)S(1)} %stack.35.where_ref, s32[8,12]{1,0:T(8,128)S(1)} %bitcast.24, bf16[4,64,512]{2,1,0:T(8,128)(2,1)S(1)} %get-tuple-element.63.refs_0_.refs_4_, bf16[4,64,512]{2,1,0:T(8,128)(2,1)} %collective-permute-done.6.refs_1_.refs_5_, bf16[4,64,512]{2,1,0:T(8,128)(2,1)S(1)} %copy-done.5, ...), custom_call_target="tpu_custom_call" | custom-call | flops 2000001024 | bytes 1000 | tf_op jit(solution)/shard_map/near_update/pallas_call | solution.py:259
  41.3 4.2 %collective-permute-start.11 = (s16[144,768]{1,0:T(8,128)(2,1)S(1)}, s16[144,768]{1,0:T(8,128)(2,1)S(1)}, u32[]{:S(2)}, u32[]{:S(2)}) collective-permute-start(s16[144,768]{1,0:T(8,128)(2,1)S(1)} %get-tuple-element.73), channel_id=1, source_target_pairs={{1,17},{2,18},{4,20},{7,23},{9,25},{10,26},{12,28},{15,31},{16,0},... | collective-permute-start | bytes 663560 | tf_op jit(solution)/shard_map/ppermute | solution.py:565
  45.5 2.0 %far_update.5 = (f32[2,128,768]{2,1,0:T(8,128)S(1)}, s16[272,768]{1,0:T(8,128)(2,1)S(1)}, s16[144,384]{1,0:T(8,128)(2,1)S(1)}, s16[144,384]{1,0:T(8,128)(2,1)S(1)}) custom-call(s32[8]{0:T(128)S(1)} %stack.35.where_ref, s32[8,12]{1,0:T(8,128)S(1)} %bitcast.25, bf16[2,4,64,512]{3,2,1,0:T(8,128)(2,1)S(1)} %collective-permute-done.12.a_ref, ...), custom_call_target="tpu_custom_call" | custom-call | flops 2000001024 | bytes 1000 | tf_op jit(solution)/shard_map/far_update/pallas_call | solution.py:308
  47.6 2.1 %collective-permute-start.18 = (s16[144,384]{1,0:T(8,128)(2,1)S(1)}, s16[144,384]{1,0:T(8,128)(2,1)S(1)}, u32[]{:S(2)}, u32[]{:S(2)}) collective-permute-start(s16[144,384]{1,0:T(8,128)(2,1)S(1)} %get-tuple-element.86), channel_id=1, source_target_pairs={{0,4},{1,5},{6,2},{7,3},{8,12},{9,13},{14,10},{15,11},{16,20},{17,... | collective-permute-start | bytes 331784 | tf_op jit(solution)/shard_map/ppermute | solution.py:552
  49.7 2.5 %near_update.6.refs_1_ = f32[4,128,768]{2,1,0:T(8,128)S(1)} custom-call(s32[8]{0:T(128)S(1)} %stack.35.where_ref, s32[8,12]{1,0:T(8,128)S(1)} %bitcast.26, bf16[4,64,512]{2,1,0:T(8,128)(2,1)} %get-tuple-element.55.refs_0_, bf16[4,64,512]{2,1,0:T(8,128)(2,1)} %collective-permute-done.1.refs_1_, bf16[4,64,512]{2,1,0:T(8,128)(2,1)} %get-tuple-element.56.refs_2_, ...), custom_call_target="tpu_custom_call" | custom-call | flops 2000001024 | bytes 1000 | tf_op jit(solution)/shard_map/near_update/pallas_call | solution.py:259
  52.2 1.2 %collective-permute-start.14 = (s16[272,768]{1,0:T(8,128)(2,1)S(1)}, s16[272,768]{1,0:T(8,128)(2,1)S(1)}, u32[]{:S(2)}, u32[]{:S(2)}) collective-permute-start(s16[272,768]{1,0:T(8,128)(2,1)S(1)} %get-tuple-element.79), channel_id=1, source_target_pairs={{0,8},{8,0},{16,24},{24,16},{1,9},{9,1},{17,25},{25,17},{2,10},{10... | collective-permute-start | bytes 1253384 | tf_op jit(solution)/shard_map/ppermute | solution.py:555
  55.4 3.5 %collective-permute-start.20 = (bf16[2,4,64,256]{3,2,1,0:T(8,128)(2,1)S(1)}, bf16[2,4,64,256]{3,2,1,0:T(8,128)(2,1)S(1)}, u32[]{:S(2)}, u32[]{:S(2)}) collective-permute-start(bf16[2,4,64,256]{3,2,1,0:T(8,128)(2,1)S(1)} %get-tuple-element.91), channel_id=1, source_target_pairs={{0,1},{1,0},{2,3},{3,2},{4,5},{5,4},{6,7},{7,6},{8,9},{9,8},{10,11... | collective-permute-start | bytes 786440 | tf_op jit(solution)/shard_map/ppermute | solution.py:568
  58.9 2.1 %far_update.6 = (f32[2,128,768]{2,1,0:T(8,128)S(1)}, s16[272,768]{1,0:T(8,128)(2,1)S(1)}) custom-call(s32[8]{0:T(128)S(1)} %stack.35.where_ref, s32[8,12]{1,0:T(8,128)S(1)} %bitcast.27, bf16[2,4,64,512]{3,2,1,0:T(8,128)(2,1)S(1)} %collective-permute-done.16.a_ref, bf16[2,4,64,512]{3,2,1,0:T(8,128)(2,1)S(1)} %collective-permute-done.17.b_ref, ...), custom_call_target="tpu_custom_call" | custom-call | flops 2000001024 | bytes 1000 | tf_op jit(solution)/shard_map/far_update/pallas_call | solution.py:308
  61.3 5.1 %collective-permute-done.21.got_ref = s16[144,384]{1,0:T(8,128)(2,1)S(1)} collective-permute-done((s16[144,384]{1,0:T(8,128)(2,1)S(1)}, s16[144,384]{1,0:T(8,128)(2,1)S(1)}, u32[]{:S(2)}, u32[]{:S(2)}) %collective-permute-start.21) | collective-permute-done | bytes 110624 | tf_op jit(solution)/shard_map/ppermute | solution.py:555
  66.4 2.4 %collective-permute-start.24 = (s16[144,384]{1,0:T(8,128)(2,1)S(1)}, s16[144,384]{1,0:T(8,128)(2,1)S(1)}, u32[]{:S(2)}, u32[]{:S(2)}) collective-permute-start(s16[144,384]{1,0:T(8,128)(2,1)S(1)} %add_coded.1.one_ref), channel_id=1, source_target_pairs={{0,16},{8,24},{16,0},{24,8},{1,17},{9,25},{17,1},{25,9},{2,18},{10... | collective-permute-start | bytes 331784 | tf_op jit(solution)/shard_map/ppermute | solution.py:555
  68.8 1.3 %near_update.7.refs_1_ = f32[2,128,768]{2,1,0:T(8,128)S(1)} custom-call(s32[8]{0:T(128)S(1)} %stack.35.where_ref, s32[8,12]{1,0:T(8,128)S(1)} %bitcast.28, bf16[4,64,512]{2,1,0:T(8,128)(2,1)S(1)} %get-tuple-element.66.refs_4_.refs_0_, bf16[4,64,512]{2,1,0:T(8,128)(2,1)S(1)} %collective-permute-done.8.refs_5_.refs_1_, ...), custom_call_target="tpu_custom_call" | custom-call | flops 2000001024 | bytes 1000 | tf_op jit(solution)/shard_map/near_update/pallas_call | solution.py:259
  70.1 6.3 %collective-permute-done.24.two_ref = s16[144,384]{1,0:T(8,128)(2,1)S(1)} collective-permute-done((s16[144,384]{1,0:T(8,128)(2,1)S(1)}, s16[144,384]{1,0:T(8,128)(2,1)S(1)}, u32[]{:S(2)}, u32[]{:S(2)}) %collective-permute-start.24) | collective-permute-done | bytes 110624 | tf_op jit(solution)/shard_map/ppermute | solution.py:555
  76.4 1.1 pivots.1.in_ref
  77.5 1.5 %far_update.7 = (f32[1,128,768]{2,1,0:T(8,128)S(1)}, s16[144,768]{1,0:T(8,128)(2,1)S(1)}) custom-call(s32[8]{0:T(128)S(1)} %stack.35.where_ref, s32[8,12]{1,0:T(8,128)S(1)} %bitcast.29, bf16[2,4,64,256]{3,2,1,0:T(8,128)(2,1)S(1)} %collective-permute-done.19.a_ref, bf16[2,4,64,256]{3,2,1,0:T(8,128)(2,1)S(1)} %collective-permute-done.20.b_ref, ...), custom_call_target="tpu_custom_call" | custom-call | flops 2000001024 | bytes 1000 | tf_op jit(solution)/shard_map/far_update/pallas_call | solution.py:308
  79.0 3.2 %collective-permute-start.25 = (s16[144,768]{1,0:T(8,128)(2,1)S(1)}, s16[144,768]{1,0:T(8,128)(2,1)S(1)}, u32[]{:S(2)}, u32[]{:S(2)}) collective-permute-start(s16[144,768]{1,0:T(8,128)(2,1)S(1)} %get-tuple-element.98), channel_id=1, source_target_pairs={{0,8},{8,0},{16,24},{24,16},{1,9},{9,1},{17,25},{25,17},{2,10},{10... | collective-permute-start | bytes 663560 | tf_op jit(solution)/shard_map/ppermute | solution.py:555
  82.3 0.8 halve.5
  83.1 1.6 %collective-permute-start.15 = (s16[272,768]{1,0:T(8,128)(2,1)S(1)}, s16[272,768]{1,0:T(8,128)(2,1)S(1)}, u32[]{:S(2)}, u32[]{:S(2)}) collective-permute-start(s16[272,768]{1,0:T(8,128)(2,1)S(1)} %get-tuple-element.81), channel_id=1, source_target_pairs={{1,17},{2,18},{4,20},{7,23},{9,25},{10,26},{12,28},{15,31},{16,0},... | collective-permute-start | bytes 1253384 | tf_op jit(solution)/shard_map/ppermute | solution.py:565
  84.7 0.8 halve.6
  85.5 1.3 %collective-permute-start.23 = (s16[272,768]{1,0:T(8,128)(2,1)S(1)}, s16[272,768]{1,0:T(8,128)(2,1)S(1)}, u32[]{:S(2)}, u32[]{:S(2)}) collective-permute-start(s16[272,768]{1,0:T(8,128)(2,1)S(1)} %get-tuple-element.97), channel_id=1, source_target_pairs={{0,16},{3,19},{5,21},{6,22},{8,24},{11,27},{13,29},{14,30},{17,1},... | collective-permute-start | bytes 1253384 | tf_op jit(solution)/shard_map/ppermute | solution.py:565
  86.8 4.6 %factor.2.in_ref = f32[3,128,128]{2,1,0:T(8,128)S(1)} custom-call(f32[3,128,128]{2,1,0:T(8,128)S(1)} %pivots.1.in_ref), custom_call_target="tpu_custom_call" | custom-call | flops 10000001024 | bytes 1000 | tf_op jit(solution)/shard_map/factor/pallas_call | solution.py:82
  92.1 1.3 %collective-permute-start.26 = (s16[144,768]{1,0:T(8,128)(2,1)S(1)}, s16[144,768]{1,0:T(8,128)(2,1)S(1)}, u32[]{:S(2)}, u32[]{:S(2)}) collective-permute-start(s16[144,768]{1,0:T(8,128)(2,1)S(1)} %get-tuple-element.102), channel_id=1, source_target_pairs={{0,16},{3,19},{5,21},{6,22},{8,24},{11,27},{13,29},{14,30},{17,1},... | collective-permute-start | bytes 663560 | tf_op jit(solution)/shard_map/ppermute | solution.py:565
  93.4 6.8 %factor.3.refs_8_ = f32[3,128,128]{2,1,0:T(8,128)S(1)} custom-call(f32[3,128,128]{2,1,0:T(8,128)S(1)} %factor.2.in_ref), custom_call_target="tpu_custom_call" | custom-call | flops 10000001024 | bytes 1000 | tf_op jit(solution)/shard_map/factor/pallas_call | solution.py:82
  100.2 4.5 %collective-permute-start.27 = (f32[3,128,128]{2,1,0:T(8,128)S(1)}, f32[3,128,128]{2,1,0:T(8,128)S(1)}, u32[]{:S(2)}, u32[]{:S(2)}) collective-permute-start(f32[3,128,128]{2,1,0:T(8,128)S(1)} %factor.3.refs_8_), channel_id=1, source_target_pairs={{0,4},{4,0},{1,5},{5,1},{2,6},{6,2},{3,7},{7,3},{8,12},{12,8},{9,1... | collective-permute-start | bytes 589832 | tf_op jit(solution)/shard_map/ppermute | solution.py:623
  104.8 1.1 collective-permute-done.27.refs_9_
  105.9 5.7 %collective-permute-done.26.refs_7_ = s16[144,768]{1,0:T(8,128)(2,1)S(1)} collective-permute-done((s16[144,768]{1,0:T(8,128)(2,1)S(1)}, s16[144,768]{1,0:T(8,128)(2,1)S(1)}, u32[]{:S(2)}, u32[]{:S(2)}) %collective-permute-start.26) | collective-permute-done | bytes 221216 | tf_op jit(solution)/shard_map/ppermute | solution.py:565
  111.5 2.2 %combine.1 = (f32[384,768]{1,0:T(8,128)}, f32[6,128,128]{2,1,0:T(8,128)}) custom-call(s32[8]{0:T(128)S(1)} %stack.35.where_ref, f32[1536,768]{1,0:T(8,128)S(1)} %bitcast.15, f32[1,128,768]{2,1,0:T(8,128)S(1)} %get-tuple-element.72.refs_0_, s16[144,768]{1,0:T(8,128)(2,1)S(1)} %collective-permute-done.11.refs_1_, ...), custom_call_target="tpu_custom_call" | custom-call | flops 1000 | bytes 1000 | tf_op jit(solution)/shard_map/combine/pallas_call | solution.py:443
  (58 shorter events, 5.6 us)
Async XLA Ops:
  0.6 12.9 %collective-permute-start = (bf16[8,128,768]{2,1,0:T(8,128)(2,1)}, bf16[8,128,768]{2,1,0:T(8,128)(2,1)S(1)}, u32[]{:S(2)}, u32[]{:S(2)}) collective-permute-start(bf16[8,128,768]{2,1,0:T(8,128)(2,1)} %bitcast.19), channel_id=1, source_target_pairs={{0,4},{4,0},{1,5},{5,1},{2,6},{6,2},{3,7},{7,3},{8,12},{12,8},{9,1... | collective-permute-start | bytes 4718600 | tf_op jit(solution)/shard_map/ppermute | solution.py:572
  1.4 1.4 %copy-start.1 = (bf16[1,8,1536,64]{2,3,1,0:T(8,128)(2,1)S(1)}, bf16[1,8,1536,64]{2,3,1,0:T(8,128)(2,1)}, u32[]{:S(2)}) copy-start(bf16[1,8,1536,64]{2,3,1,0:T(8,128)(2,1)} %param.5) | copy-start | bytes 4718596
  3.6 11.3 %collective-permute-start.1 = (bf16[4,64,512]{2,1,0:T(8,128)(2,1)}, bf16[4,64,512]{2,1,0:T(8,128)(2,1)}, u32[]{:S(2)}, u32[]{:S(2)}) collective-permute-start(bf16[4,64,512]{2,1,0:T(8,128)(2,1)} %get-tuple-element.55.refs_0_), channel_id=1, source_target_pairs={{0,1},{1,0},{2,3},{3,2},{4,5},{5,4},{6,7},{7,6},{8,9},{9,8},{10,11... | collective-permute-start | bytes 786440 | tf_op jit(solution)/shard_map/ppermute | solution.py:568
  4.0 11.0 %collective-permute-start.2 = (bf16[4,64,512]{2,1,0:T(8,128)(2,1)}, bf16[4,64,512]{2,1,0:T(8,128)(2,1)}, u32[]{:S(2)}, u32[]{:S(2)}) collective-permute-start(bf16[4,64,512]{2,1,0:T(8,128)(2,1)} %get-tuple-element.56.refs_2_), channel_id=1, source_target_pairs={{0,2},{1,3},{2,0},{3,1},{4,6},{5,7},{6,4},{7,5},{8,10},{9,11},{10,... | collective-permute-start | bytes 786440 | tf_op jit(solution)/shard_map/ppermute | solution.py:568
  4.2 0.7 copy-start.4
  4.9 13.7 %collective-permute-start.6 = (bf16[4,64,512]{2,1,0:T(8,128)(2,1)S(1)}, bf16[4,64,512]{2,1,0:T(8,128)(2,1)}, u32[]{:S(2)}, u32[]{:S(2)}) collective-permute-start(bf16[4,64,512]{2,1,0:T(8,128)(2,1)S(1)} %get-tuple-element.63.refs_0_.refs_4_), channel_id=1, source_target_pairs={{0,1},{1,0},{2,3},{3,2},{4,5},{5,4},{6,7},{7,6},{8,9},{9,8},{10,11... | collective-permute-start | bytes 786440 | tf_op jit(solution)/shard_map/ppermute | solution.py:568
  6.3 2.3 %copy-start = (f32[1536,768]{1,0:T(8,128)S(1)}, f32[1536,768]{1,0:T(8,128)}, u32[]{:S(2)}) copy-start(f32[1536,768]{1,0:T(8,128)} %anc_ref.4) | copy-start | bytes 14155780
  8.7 4.7 %copy-start.7 = (s32[1,8,6]{1,0,2:T(1,128)S(1)}, s32[1,8,6]{1,0,2:T(1,128)}, u32[]{:S(2)}) copy-start(s32[1,8,6]{1,0,2:T(1,128)} %param.8) | copy-start | bytes 580
  8.7 4.8 %copy-start.3 = (bf16[1,8,128,768]{3,2,1,0:T(8,128)(2,1)S(1)}, bf16[1,8,128,768]{3,2,1,0:T(8,128)(2,1)}, u32[]{:S(2)}) copy-start(bf16[1,8,128,768]{3,2,1,0:T(8,128)(2,1)} %param.6) | copy-start | bytes 4718596
  10.0 8.5 %collective-permute-start.5 = (f32[3,128,128]{2,1,0:T(8,128)}, f32[3,128,128]{2,1,0:T(8,128)}, u32[]{:S(2)}, u32[]{:S(2)}) collective-permute-start(f32[3,128,128]{2,1,0:T(8,128)} %later_blocks.1), channel_id=1, source_target_pairs={{0,4},{1,5},{6,2},{7,3},{8,12},{9,13},{14,10},{15,11},{16,20},{17,... | collective-permute-start | bytes 589832 | tf_op jit(solution)/shard_map/ppermute | solution.py:552
  13.5 8.1 %collective-permute-start.7 = (bf16[4,64,512]{2,1,0:T(8,128)(2,1)}, bf16[4,64,512]{2,1,0:T(8,128)(2,1)S(1)}, u32[]{:S(2)}, u32[]{:S(2)}) collective-permute-start(bf16[4,64,512]{2,1,0:T(8,128)(2,1)} %copy-done.4), channel_id=1, source_target_pairs={{0,2},{1,3},{2,0},{3,1},{4,6},{5,7},{6,4},{7,5},{8,10},{9,11},{10,... | collective-permute-start | bytes 786440 | tf_op jit(solution)/shard_map/ppermute | solution.py:568
  13.5 3.1 %copy-start.2 = (bf16[1,8,1536,64]{2,3,1,0:T(8,128)(2,1)S(1)}, bf16[1,8,1536,64]{2,3,1,0:T(8,128)(2,1)}, u32[]{:S(2)}) copy-start(bf16[1,8,1536,64]{2,3,1,0:T(8,128)(2,1)} %param.5) | copy-start | bytes 4718596
  14.9 12.2 %copy-start.5 = (bf16[4,64,512]{2,1,0:T(8,128)(2,1)S(1)}, bf16[4,64,512]{2,1,0:T(8,128)(2,1)}, u32[]{:S(2)}) copy-start(bf16[4,64,512]{2,1,0:T(8,128)(2,1)} %copy-done.4) | copy-start | bytes 786436
  16.7 13.0 %copy-start.6 = (s32[1,8,12]{2,1,0:T(8,128)S(1)}, s32[1,8,12]{2,1,0:T(8,128)}, u32[]{:S(2)}) copy-start(s32[1,8,12]{2,1,0:T(8,128)} %param.7) | copy-start | bytes 1156
  16.9 6.7 %collective-permute-start.8 = (bf16[4,64,512]{2,1,0:T(8,128)(2,1)S(1)}, bf16[4,64,512]{2,1,0:T(8,128)(2,1)S(1)}, u32[]{:S(2)}, u32[]{:S(2)}) collective-permute-start(bf16[4,64,512]{2,1,0:T(8,128)(2,1)S(1)} %get-tuple-element.66.refs_4_.refs_0_), channel_id=1, source_target_pairs={{0,1},{1,0},{2,3},{3,2},{4,5},{5,4},{6,7},{7,6},{8,9},{9,8},{10,11... | collective-permute-start | bytes 786440 | tf_op jit(solution)/shard_map/ppermute | solution.py:568
  16.9 10.1 %collective-permute-start.9 = (bf16[4,64,512]{2,1,0:T(8,128)(2,1)S(1)}, bf16[4,64,512]{2,1,0:T(8,128)(2,1)S(1)}, u32[]{:S(2)}, u32[]{:S(2)}) collective-permute-start(bf16[4,64,512]{2,1,0:T(8,128)(2,1)S(1)} %get-tuple-element.67.refs_6_.refs_2_), channel_id=1, source_target_pairs={{0,2},{1,3},{2,0},{3,1},{4,6},{5,7},{6,4},{7,5},{8,10},{9,11},{10,... | collective-permute-start | bytes 786440 | tf_op jit(solution)/shard_map/ppermute | solution.py:568
  18.4 14.3 %collective-permute-start.3 = (bf16[2,4,64,256]{3,2,1,0:T(8,128)(2,1)S(1)}, bf16[2,4,64,256]{3,2,1,0:T(8,128)(2,1)S(1)}, u32[]{:S(2)}, u32[]{:S(2)}) collective-permute-start(bf16[2,4,64,256]{3,2,1,0:T(8,128)(2,1)S(1)} %get-tuple-element.57), channel_id=1, source_target_pairs={{0,2},{1,3},{2,0},{3,1},{4,6},{5,7},{6,4},{7,5},{8,10},{9,11},{10,... | collective-permute-start | bytes 786440 | tf_op jit(solution)/shard_map/ppermute | solution.py:568
  18.5 14.2 %collective-permute-start.4 = (bf16[2,4,64,256]{3,2,1,0:T(8,128)(2,1)S(1)}, bf16[2,4,64,256]{3,2,1,0:T(8,128)(2,1)S(1)}, u32[]{:S(2)}, u32[]{:S(2)}) collective-permute-start(bf16[2,4,64,256]{3,2,1,0:T(8,128)(2,1)S(1)} %get-tuple-element.58), channel_id=1, source_target_pairs={{0,1},{1,0},{2,3},{3,2},{4,5},{5,4},{6,7},{7,6},{8,9},{9,8},{10,11... | collective-permute-start | bytes 786440 | tf_op jit(solution)/shard_map/ppermute | solution.py:568
  28.7 16.8 %collective-permute-start.12 = (bf16[2,4,64,512]{3,2,1,0:T(8,128)(2,1)S(1)}, bf16[2,4,64,512]{3,2,1,0:T(8,128)(2,1)S(1)}, u32[]{:S(2)}, u32[]{:S(2)}) collective-permute-start(bf16[2,4,64,512]{3,2,1,0:T(8,128)(2,1)S(1)} %get-tuple-element.68), channel_id=1, source_target_pairs={{0,2},{1,3},{2,0},{3,1},{4,6},{5,7},{6,4},{7,5},{8,10},{9,11},{10,... | collective-permute-start | bytes 1572872 | tf_op jit(solution)/shard_map/ppermute | solution.py:568
  28.8 16.7 %collective-permute-start.13 = (bf16[2,4,64,512]{3,2,1,0:T(8,128)(2,1)S(1)}, bf16[2,4,64,512]{3,2,1,0:T(8,128)(2,1)S(1)}, u32[]{:S(2)}, u32[]{:S(2)}) collective-permute-start(bf16[2,4,64,512]{3,2,1,0:T(8,128)(2,1)S(1)} %get-tuple-element.74), channel_id=1, source_target_pairs={{0,1},{1,0},{2,3},{3,2},{4,5},{5,4},{6,7},{7,6},{8,9},{9,8},{10,11... | collective-permute-start | bytes 1572872 | tf_op jit(solution)/shard_map/ppermute | solution.py:568
  34.2 6.4 %collective-permute-start.10 = (s16[144,768]{1,0:T(8,128)(2,1)S(1)}, s16[144,768]{1,0:T(8,128)(2,1)S(1)}, u32[]{:S(2)}, u32[]{:S(2)}) collective-permute-start(s16[144,768]{1,0:T(8,128)(2,1)S(1)} %get-tuple-element.71), channel_id=1, source_target_pairs={{0,8},{8,0},{16,24},{24,16},{1,9},{9,1},{17,25},{25,17},{2,10},{10... | collective-permute-start | bytes 663560 | tf_op jit(solution)/shard_map/ppermute | solution.py:555
  37.4 18.0 %collective-permute-start.16 = (bf16[2,4,64,512]{3,2,1,0:T(8,128)(2,1)S(1)}, bf16[2,4,64,512]{3,2,1,0:T(8,128)(2,1)S(1)}, u32[]{:S(2)}, u32[]{:S(2)}) collective-permute-start(bf16[2,4,64,512]{3,2,1,0:T(8,128)(2,1)S(1)} %get-tuple-element.83), channel_id=1, source_target_pairs={{0,2},{1,3},{2,0},{3,1},{4,6},{5,7},{6,4},{7,5},{8,10},{9,11},{10,... | collective-permute-start | bytes 1572872 | tf_op jit(solution)/shard_map/ppermute | solution.py:568
  37.5 21.4 %collective-permute-start.17 = (bf16[2,4,64,512]{3,2,1,0:T(8,128)(2,1)S(1)}, bf16[2,4,64,512]{3,2,1,0:T(8,128)(2,1)S(1)}, u32[]{:S(2)}, u32[]{:S(2)}) collective-permute-start(bf16[2,4,64,512]{3,2,1,0:T(8,128)(2,1)S(1)} %get-tuple-element.84), channel_id=1, source_target_pairs={{0,1},{1,0},{2,3},{3,2},{4,5},{5,4},{6,7},{7,6},{8,9},{9,8},{10,11... | collective-permute-start | bytes 1572872 | tf_op jit(solution)/shard_map/ppermute | solution.py:568
  41.3 14.0 %collective-permute-start.11 = (s16[144,768]{1,0:T(8,128)(2,1)S(1)}, s16[144,768]{1,0:T(8,128)(2,1)S(1)}, u32[]{:S(2)}, u32[]{:S(2)}) collective-permute-start(s16[144,768]{1,0:T(8,128)(2,1)S(1)} %get-tuple-element.73), channel_id=1, source_target_pairs={{1,17},{2,18},{4,20},{7,23},{9,25},{10,26},{12,28},{15,31},{16,0},... | collective-permute-start | bytes 663560 | tf_op jit(solution)/shard_map/ppermute | solution.py:565
  47.6 5.8 %collective-permute-start.18 = (s16[144,384]{1,0:T(8,128)(2,1)S(1)}, s16[144,384]{1,0:T(8,128)(2,1)S(1)}, u32[]{:S(2)}, u32[]{:S(2)}) collective-permute-start(s16[144,384]{1,0:T(8,128)(2,1)S(1)} %get-tuple-element.86), channel_id=1, source_target_pairs={{0,4},{1,5},{6,2},{7,3},{8,12},{9,13},{14,10},{15,11},{16,20},{17,... | collective-permute-start | bytes 331784 | tf_op jit(solution)/shard_map/ppermute | solution.py:552
  52.2 30.1 %collective-permute-start.14 = (s16[272,768]{1,0:T(8,128)(2,1)S(1)}, s16[272,768]{1,0:T(8,128)(2,1)S(1)}, u32[]{:S(2)}, u32[]{:S(2)}) collective-permute-start(s16[272,768]{1,0:T(8,128)(2,1)S(1)} %get-tuple-element.79), channel_id=1, source_target_pairs={{0,8},{8,0},{16,24},{24,16},{1,9},{9,1},{17,25},{25,17},{2,10},{10... | collective-permute-start | bytes 1253384 | tf_op jit(solution)/shard_map/ppermute | solution.py:555
  54.2 12.1 %collective-permute-start.21 = (s16[144,384]{1,0:T(8,128)(2,1)S(1)}, s16[144,384]{1,0:T(8,128)(2,1)S(1)}, u32[]{:S(2)}, u32[]{:S(2)}) collective-permute-start(s16[144,384]{1,0:T(8,128)(2,1)S(1)} %pick.1.mine_ref), channel_id=1, source_target_pairs={{0,8},{8,0},{16,24},{24,16},{1,9},{9,1},{17,25},{25,17},{2,10},{10... | collective-permute-start | bytes 331784 | tf_op jit(solution)/shard_map/ppermute | solution.py:555
  55.3 22.2 %collective-permute-start.19 = (bf16[2,4,64,256]{3,2,1,0:T(8,128)(2,1)S(1)}, bf16[2,4,64,256]{3,2,1,0:T(8,128)(2,1)S(1)}, u32[]{:S(2)}, u32[]{:S(2)}) collective-permute-start(bf16[2,4,64,256]{3,2,1,0:T(8,128)(2,1)S(1)} %get-tuple-element.90), channel_id=1, source_target_pairs={{0,2},{1,3},{2,0},{3,1},{4,6},{5,7},{6,4},{7,5},{8,10},{9,11},{10,... | collective-permute-start | bytes 786440 | tf_op jit(solution)/shard_map/ppermute | solution.py:568
  55.4 22.1 %collective-permute-start.20 = (bf16[2,4,64,256]{3,2,1,0:T(8,128)(2,1)S(1)}, bf16[2,4,64,256]{3,2,1,0:T(8,128)(2,1)S(1)}, u32[]{:S(2)}, u32[]{:S(2)}) collective-permute-start(bf16[2,4,64,256]{3,2,1,0:T(8,128)(2,1)S(1)} %get-tuple-element.91), channel_id=1, source_target_pairs={{0,1},{1,0},{2,3},{3,2},{4,5},{5,4},{6,7},{7,6},{8,9},{9,8},{10,11... | collective-permute-start | bytes 786440 | tf_op jit(solution)/shard_map/ppermute | solution.py:568
  58.9 17.5 %slice-start = ((s8[4718592]{0:T(1024)(128)(4,1)}), s8[4194304]{0:T(1024)(128)(4,1)S(1)}, s32[]{:S(2)}) async-start(s8[4718592]{0:T(1024)(128)(4,1)} %bitcast.14), calls=%async_computation | async-start | bytes 8388608
  61.0 15.4 %slice-start.1 = ((s8[4718592]{0:T(1024)(128)(4,1)}), s8[524288]{0:T(1024)(128)(4,1)S(1)}, s32[]{:S(2)}) async-start(s8[4718592]{0:T(1024)(128)(4,1)} %bitcast.14), calls=%async_computation.1 | async-start | bytes 1048576
  61.0 23.7 %collective-permute-start.22 = (s16[272,768]{1,0:T(8,128)(2,1)S(1)}, s16[272,768]{1,0:T(8,128)(2,1)S(1)}, u32[]{:S(2)}, u32[]{:S(2)}) collective-permute-start(s16[272,768]{1,0:T(8,128)(2,1)S(1)} %get-tuple-element.95), channel_id=1, source_target_pairs={{0,8},{8,0},{16,24},{24,16},{1,9},{9,1},{17,25},{25,17},{2,10},{10... | collective-permute-start | bytes 1253384 | tf_op jit(solution)/shard_map/ppermute | solution.py:555
  66.4 10.0 %collective-permute-start.24 = (s16[144,384]{1,0:T(8,128)(2,1)S(1)}, s16[144,384]{1,0:T(8,128)(2,1)S(1)}, u32[]{:S(2)}, u32[]{:S(2)}) collective-permute-start(s16[144,384]{1,0:T(8,128)(2,1)S(1)} %add_coded.1.one_ref), channel_id=1, source_target_pairs={{0,16},{8,24},{16,0},{24,8},{1,17},{9,25},{17,1},{25,9},{2,18},{10... | collective-permute-start | bytes 331784 | tf_op jit(solution)/shard_map/ppermute | solution.py:555
  79.0 12.4 %collective-permute-start.25 = (s16[144,768]{1,0:T(8,128)(2,1)S(1)}, s16[144,768]{1,0:T(8,128)(2,1)S(1)}, u32[]{:S(2)}, u32[]{:S(2)}) collective-permute-start(s16[144,768]{1,0:T(8,128)(2,1)S(1)} %get-tuple-element.98), channel_id=1, source_target_pairs={{0,8},{8,0},{16,24},{24,16},{1,9},{9,1},{17,25},{25,17},{2,10},{10... | collective-permute-start | bytes 663560 | tf_op jit(solution)/shard_map/ppermute | solution.py:555
  83.1 28.4 %collective-permute-start.15 = (s16[272,768]{1,0:T(8,128)(2,1)S(1)}, s16[272,768]{1,0:T(8,128)(2,1)S(1)}, u32[]{:S(2)}, u32[]{:S(2)}) collective-permute-start(s16[272,768]{1,0:T(8,128)(2,1)S(1)} %get-tuple-element.81), channel_id=1, source_target_pairs={{1,17},{2,18},{4,20},{7,23},{9,25},{10,26},{12,28},{15,31},{16,0},... | collective-permute-start | bytes 1253384 | tf_op jit(solution)/shard_map/ppermute | solution.py:565
  85.5 26.0 %collective-permute-start.23 = (s16[272,768]{1,0:T(8,128)(2,1)S(1)}, s16[272,768]{1,0:T(8,128)(2,1)S(1)}, u32[]{:S(2)}, u32[]{:S(2)}) collective-permute-start(s16[272,768]{1,0:T(8,128)(2,1)S(1)} %get-tuple-element.97), channel_id=1, source_target_pairs={{0,16},{3,19},{5,21},{6,22},{8,24},{11,27},{13,29},{14,30},{17,1},... | collective-permute-start | bytes 1253384 | tf_op jit(solution)/shard_map/ppermute | solution.py:565
  92.1 19.4 %collective-permute-start.26 = (s16[144,768]{1,0:T(8,128)(2,1)S(1)}, s16[144,768]{1,0:T(8,128)(2,1)S(1)}, u32[]{:S(2)}, u32[]{:S(2)}) collective-permute-start(s16[144,768]{1,0:T(8,128)(2,1)S(1)} %get-tuple-element.102), channel_id=1, source_target_pairs={{0,16},{3,19},{5,21},{6,22},{8,24},{11,27},{13,29},{14,30},{17,1},... | collective-permute-start | bytes 663560 | tf_op jit(solution)/shard_map/ppermute | solution.py:565
  100.2 5.6 %collective-permute-start.27 = (f32[3,128,128]{2,1,0:T(8,128)S(1)}, f32[3,128,128]{2,1,0:T(8,128)S(1)}, u32[]{:S(2)}, u32[]{:S(2)}) collective-permute-start(f32[3,128,128]{2,1,0:T(8,128)S(1)} %factor.3.refs_8_), channel_id=1, source_target_pairs={{0,4},{4,0},{1,5},{5,1},{2,6},{6,2},{3,7},{7,3},{8,12},{12,8},{9,1... | collective-permute-start | bytes 589832 | tf_op jit(solution)/shard_map/ppermute | solution.py:623

commit v11 on v10

--- a/solution.py
+++ b/solution.py
@@ -18,7 +18,7 @@
 HALF_STEPS = 48
 LU = 10
 NEAR = 2
-FAR = 2
+FAR = 6
 
 
 def cost(micros):
@@ -610,13 +610,13 @@
     sum1, sent1 = halve(where, kept1, over_layers(coded1, 1), chunks[1])
     got1 = far_layers(sent1, chunks[1])
     far = over_layers(near, 2)
-    own = pivots(where, anc, given, near, far)
     second_step(sides[2][0], mine)
     kept2, coded2 = far_part(2, [], kept1, mine, got0)
-    kept3, coded3 = far_part(3, [], kept2, near)
+    kept3, coded3 = far_part(3, [], kept2, sent1, mine)
     sum2, sent2 = halve(where, after(kept2, kept3), over_layers(coded2, 1), chunks[2])
     got2 = far_layers(sent2, chunks[2])
-    half_lu = factor(after(own, sent2, coded3), 0, HALF_STEPS)
+    own = pivots(where, anc, given, near, after(far, sent2, coded3))
+    half_lu = factor(own, 0, HALF_STEPS)
     sum3, sent3 = halve(where, after(kept3, half_lu), over_layers(coded3, 1), chunks[3])
     got3 = far_layers(sent3, chunks[3])
     lu = factor(after(half_lu, sent3), HALF_STEPS, BLK)

time: 114 us -> 107 us (0.939)
  the two profiles are of different devices: /device:TPU:7 before, /device:TPU:9 now
where the time goes in v11:
time: 107 us
  Pallas kernels  43.1 us (40%)
  starting transfers between devices  42.8 us (40%)
  waiting for transfers between devices  14.8 us (14%)
  local copies, waits for them, and re-layouts  4.63 us (4%)
  between operations  1.21 us (1%)
    ppermute x14, starting transfers between devices, over(): return lax.ppermute(value, 'col', xor_perm(cols, bit))  15.5 us
    pallas_call x2, Pallas kernels, factor(): pl.pallas_call(functools.partial(lu_kernel, begin, end), out_shape=jax.Sh...  11.4 us
    ppermute x4, starting transfers between devices, far_layers(): return lax.ppermute(value, everyone, perm)  10.9 us
    pallas_call x4, Pallas kernels, near_update(): pl.pallas_call(functools.partial(near_kernel, chunk, blocks), out_shape=j...  7.93 us
    ppermute x6, waiting for transfers between devices, over_layers(): return lax.ppermute(value, 'layer', xor_perm(layers, bit))  7.46 us
    pallas_call x4, Pallas kernels, far_update(): pl.pallas_call(functools.partial(far_kernel, chunk, blocks, len(earlier))...  7.13 us
    ppermute x1, starting transfers between devices, planned(): lu_got = lax.ppermute(lu, 'row', xor_perm(rows, 1))  6.84 us
    ppermute x14, waiting for transfers between devices, over(): return lax.ppermute(value, 'col', xor_perm(cols, bit))  6.28 us
  transfers between devices with their start and end apart: 28, of which 7 were waited for; matrix products, arithmetic and copies ran while one was open for 0% of the time, Pallas kernels for 38%

profile of v11, /device:TPU:9, one launch (start us, length us, event | category | flops | bytes accessed | tf_op | source)
XLA Modules:
  0.0 106.6 jit_solution(1122855702066679915)
XLA Ops:
  0.6 0.7 collective-permute-start
  1.4 1.4 %copy-done.1 = bf16[1,8,1536,64]{2,3,1,0:T(8,128)(2,1)S(1)} copy-done((bf16[1,8,1536,64]{2,3,1,0:T(8,128)(2,1)S(1)}, bf16[1,8,1536,64]{2,3,1,0:T(8,128)(2,1)}, u32[]{:S(2)}) %copy-start.1) | copy-done | bytes 1572888
  2.8 0.8 halves.3
  3.6 1.3 %collective-permute-start.1 = (bf16[4,64,512]{2,1,0:T(8,128)(2,1)}, bf16[4,64,512]{2,1,0:T(8,128)(2,1)}, u32[]{:S(2)}, u32[]{:S(2)}) collective-permute-start(bf16[4,64,512]{2,1,0:T(8,128)(2,1)} %get-tuple-element.55.refs_0_), channel_id=1, source_target_pairs={{0,1},{1,0},{2,3},{3,2},{4,5},{5,4},{6,7},{7,6},{8,9},{9,8},{10,11... | collective-permute-start | bytes 786440 | tf_op jit(solution)/shard_map/ppermute | solution.py:568
  4.9 1.2 %collective-permute-start.2 = (bf16[4,64,512]{2,1,0:T(8,128)(2,1)}, bf16[4,64,512]{2,1,0:T(8,128)(2,1)}, u32[]{:S(2)}, u32[]{:S(2)}) collective-permute-start(bf16[4,64,512]{2,1,0:T(8,128)(2,1)} %get-tuple-element.56.refs_2_), channel_id=1, source_target_pairs={{0,2},{1,3},{2,0},{3,1},{4,6},{5,7},{6,4},{7,5},{8,10},{9,11},{10,... | collective-permute-start | bytes 786440 | tf_op jit(solution)/shard_map/ppermute | solution.py:568
  7.4 2.3 %copy-done = f32[1536,768]{1,0:T(8,128)S(1)} copy-done((f32[1536,768]{1,0:T(8,128)S(1)}, f32[1536,768]{1,0:T(8,128)}, u32[]{:S(2)}) %copy-start) | copy-done | bytes 4718616
  9.7 1.3 %later_blocks.1 = f32[3,128,128]{2,1,0:T(8,128)} custom-call(s32[8]{0:T(128)S(1)} %stack.35.where_ref, f32[1536,768]{1,0:T(8,128)S(1)} %copy-done), custom_call_target="tpu_custom_call" | custom-call | flops 1000 | bytes 1000 | tf_op jit(solution)/shard_map/later_blocks/pallas_call | solution.py:480
  11.0 1.3 %collective-permute-start.5 = (f32[3,128,128]{2,1,0:T(8,128)}, f32[3,128,128]{2,1,0:T(8,128)}, u32[]{:S(2)}, u32[]{:S(2)}) collective-permute-start(f32[3,128,128]{2,1,0:T(8,128)} %later_blocks.1), channel_id=1, source_target_pairs={{0,4},{1,5},{6,2},{7,3},{8,12},{9,13},{14,10},{15,11},{16,20},{17,... | collective-permute-start | bytes 589832 | tf_op jit(solution)/shard_map/ppermute | solution.py:552
  12.4 2.4 %collective-permute-start.7 = (bf16[4,64,512]{2,1,0:T(8,128)(2,1)}, bf16[4,64,512]{2,1,0:T(8,128)(2,1)S(1)}, u32[]{:S(2)}, u32[]{:S(2)}) collective-permute-start(bf16[4,64,512]{2,1,0:T(8,128)(2,1)} %copy-done.4), channel_id=1, source_target_pairs={{0,2},{1,3},{2,0},{3,1},{4,6},{5,7},{6,4},{7,5},{8,10},{9,11},{10,... | collective-permute-start | bytes 786440 | tf_op jit(solution)/shard_map/ppermute | solution.py:568
  14.8 1.4 %masked_right.1 = (bf16[8,128,768]{2,1,0:T(8,128)(2,1)S(1)}, bf16[8,128,768]{2,1,0:T(8,128)(2,1)S(1)}) custom-call(s32[8]{0:T(128)S(1)} %stack.35.where_ref, s32[8,6]{1,0:T(8,128)S(1)} %bitcast.21, bf16[8,128,768]{2,1,0:T(8,128)(2,1)S(1)} %bitcast.20, bf16[8,128,768]{2,1,0:T(8,128)(2,1)S(1)} %collective-permute-done.uo_ref), custom_call_target="tpu_custom_call" | custom-call | flops 1000 | bytes 1000 | tf_op jit(solution)/shard_map/masked_right/pallas_call | solution.py:212
  16.2 1.7 %split.4 = (bf16[2,4,64,256]{3,2,1,0:T(8,128)(2,1)S(1)}, bf16[2,4,64,256]{3,2,1,0:T(8,128)(2,1)S(1)}) custom-call(s32[8]{0:T(128)S(1)} %stack.35.where_ref, bf16[4,64,512]{2,1,0:T(8,128)(2,1)} %get-tuple-element.55.refs_0_, bf16[4,64,512]{2,1,0:T(8,128)(2,1)} %collective-permute-done.1.refs_1_, bf16[4,64,512]{2,1,0:T(8,128)(2,1)} %get-tuple-element.56.refs_2_, ...), custom_call_target="tpu_custom_call" | custom-call | flops 1000 | bytes 1000 | tf_op jit(solution)/shard_map/split/pallas_call | solution.py:168
  18.1 1.3 %collective-permute-start.8 = (bf16[4,64,512]{2,1,0:T(8,128)(2,1)S(1)}, bf16[4,64,512]{2,1,0:T(8,128)(2,1)S(1)}, u32[]{:S(2)}, u32[]{:S(2)}) collective-permute-start(bf16[4,64,512]{2,1,0:T(8,128)(2,1)S(1)} %get-tuple-element.66.refs_4_.refs_0_), channel_id=1, source_target_pairs={{0,1},{1,0},{2,3},{3,2},{4,5},{5,4},{6,7},{7,6},{8,9},{9,8},{10,11... | collective-permute-start | bytes 786440 | tf_op jit(solution)/shard_map/ppermute | solution.py:568
  19.4 1.4 %collective-permute-start.3 = (bf16[2,4,64,256]{3,2,1,0:T(8,128)(2,1)S(1)}, bf16[2,4,64,256]{3,2,1,0:T(8,128)(2,1)S(1)}, u32[]{:S(2)}, u32[]{:S(2)}) collective-permute-start(bf16[2,4,64,256]{3,2,1,0:T(8,128)(2,1)S(1)} %get-tuple-element.57), channel_id=1, source_target_pairs={{0,2},{1,3},{2,0},{3,1},{4,6},{5,7},{6,4},{7,5},{8,10},{9,11},{10,... | collective-permute-start | bytes 786440 | tf_op jit(solution)/shard_map/ppermute | solution.py:568
  21.1 2.0 %near_update.4.refs_1_ = f32[2,128,768]{2,1,0:T(8,128)S(1)} custom-call(s32[8]{0:T(128)S(1)} %stack.35.where_ref, s32[8,12]{1,0:T(8,128)S(1)} %bitcast.22, bf16[4,64,512]{2,1,0:T(8,128)(2,1)} %get-tuple-element.55.refs_0_, bf16[4,64,512]{2,1,0:T(8,128)(2,1)} %collective-permute-done.1.refs_1_, bf16[4,64,512]{2,1,0:T(8,128)(2,1)} %get-tuple-element.56.refs_2_, ...), custom_call_target="tpu_custom_call" | custom-call | flops 2000001024 | bytes 1000 | tf_op jit(solution)/shard_map/near_update/pallas_call | solution.py:259
  23.1 3.4 %collective-permute-done.8.refs_5_.refs_1_ = bf16[4,64,512]{2,1,0:T(8,128)(2,1)S(1)} collective-permute-done((bf16[4,64,512]{2,1,0:T(8,128)(2,1)S(1)}, bf16[4,64,512]{2,1,0:T(8,128)(2,1)S(1)}, u32[]{:S(2)}, u32[]{:S(2)}) %collective-permute-start.8) | collective-permute-done | bytes 262176 | tf_op jit(solution)/shard_map/ppermute | solution.py:568
  26.5 1.0 collective-permute-done.9.refs_7_.refs_3_
  27.5 1.6 %split.5 = (bf16[2,4,64,512]{3,2,1,0:T(8,128)(2,1)S(1)}, bf16[2,4,64,512]{3,2,1,0:T(8,128)(2,1)S(1)}) custom-call(s32[8]{0:T(128)S(1)} %stack.35.where_ref, bf16[4,64,512]{2,1,0:T(8,128)(2,1)S(1)} %get-tuple-element.63.refs_0_.refs_4_, bf16[4,64,512]{2,1,0:T(8,128)(2,1)} %collective-permute-done.6.refs_1_.refs_5_, bf16[4,64,512]{2,1,0:T(8,128)(2,1)S(1)} %copy-done.5, ...), custom_call_target="tpu_custom_call" | custom-call | flops 1000 | bytes 1000 | tf_op jit(solution)/shard_map/split/pallas_call | solution.py:168
  29.2 2.1 %collective-permute-start.13 = (bf16[2,4,64,512]{3,2,1,0:T(8,128)(2,1)S(1)}, bf16[2,4,64,512]{3,2,1,0:T(8,128)(2,1)S(1)}, u32[]{:S(2)}, u32[]{:S(2)}) collective-permute-start(bf16[2,4,64,512]{3,2,1,0:T(8,128)(2,1)S(1)} %get-tuple-element.74), channel_id=1, source_target_pairs={{0,1},{1,0},{2,3},{3,2},{4,5},{5,4},{6,7},{7,6},{8,9},{9,8},{10,11... | collective-permute-start | bytes 1572872 | tf_op jit(solution)/shard_map/ppermute | solution.py:568
  31.3 1.8 %collective-permute-done.3.a_ref = bf16[2,4,64,256]{3,2,1,0:T(8,128)(2,1)S(1)} collective-permute-done((bf16[2,4,64,256]{3,2,1,0:T(8,128)(2,1)S(1)}, bf16[2,4,64,256]{3,2,1,0:T(8,128)(2,1)S(1)}, u32[]{:S(2)}, u32[]{:S(2)}) %collective-permute-start.3) | collective-permute-done | bytes 262176 | tf_op jit(solution)/shard_map/ppermute | solution.py:568
  33.1 1.5 %far_update.4 = (f32[1,128,768]{2,1,0:T(8,128)S(1)}, s16[144,768]{1,0:T(8,128)(2,1)S(1)}, s16[144,384]{1,0:T(8,128)(2,1)S(1)}, s16[144,384]{1,0:T(8,128)(2,1)S(1)}) custom-call(s32[8]{0:T(128)S(1)} %stack.35.where_ref, s32[8,12]{1,0:T(8,128)S(1)} %bitcast.23, bf16[2,4,64,256]{3,2,1,0:T(8,128)(2,1)S(1)} %collective-permute-done.3.a_ref, ...), custom_call_target="tpu_custom_call" | custom-call | flops 6000001024 | bytes 1000 | tf_op jit(solution)/shard_map/far_update/pallas_call | solution.py:308
  34.8 2.5 %near_update.6.refs_1_ = f32[4,128,768]{2,1,0:T(8,128)S(1)} custom-call(s32[8]{0:T(128)S(1)} %stack.35.where_ref, s32[8,12]{1,0:T(8,128)S(1)} %bitcast.24, bf16[4,64,512]{2,1,0:T(8,128)(2,1)} %get-tuple-element.55.refs_0_, bf16[4,64,512]{2,1,0:T(8,128)(2,1)} %collective-permute-done.1.refs_1_, bf16[4,64,512]{2,1,0:T(8,128)(2,1)} %get-tuple-element.56.refs_2_, ...), custom_call_target="tpu_custom_call" | custom-call | flops 2000001024 | bytes 1000 | tf_op jit(solution)/shard_map/near_update/pallas_call | solution.py:259
  37.3 1.8 %split.6 = (bf16[2,4,64,512]{3,2,1,0:T(8,128)(2,1)S(1)}, bf16[2,4,64,512]{3,2,1,0:T(8,128)(2,1)S(1)}) custom-call(s32[8]{0:T(128)S(1)} %stack.35.where_ref, bf16[4,64,512]{2,1,0:T(8,128)(2,1)} %get-tuple-element.55.refs_0_, bf16[4,64,512]{2,1,0:T(8,128)(2,1)} %collective-permute-done.1.refs_1_, bf16[4,64,512]{2,1,0:T(8,128)(2,1)} %get-tuple-element.56.refs_2_, ...), custom_call_target="tpu_custom_call" | custom-call | flops 1000 | bytes 1000 | tf_op jit(solution)/shard_map/split/pallas_call | solution.py:168
  39.2 2.0 %collective-permute-start.17 = (bf16[2,4,64,512]{3,2,1,0:T(8,128)(2,1)S(1)}, bf16[2,4,64,512]{3,2,1,0:T(8,128)(2,1)S(1)}, u32[]{:S(2)}, u32[]{:S(2)}) collective-permute-start(bf16[2,4,64,512]{3,2,1,0:T(8,128)(2,1)S(1)} %get-tuple-element.84), channel_id=1, source_target_pairs={{0,1},{1,0},{2,3},{3,2},{4,5},{5,4},{6,7},{7,6},{8,9},{9,8},{10,11... | collective-permute-start | bytes 1572872 | tf_op jit(solution)/shard_map/ppermute | solution.py:568
  41.3 2.1 %near_update.5.refs_1_ = f32[4,128,768]{2,1,0:T(8,128)S(1)} custom-call(s32[8]{0:T(128)S(1)} %stack.35.where_ref, s32[8,12]{1,0:T(8,128)S(1)} %bitcast.25, bf16[4,64,512]{2,1,0:T(8,128)(2,1)S(1)} %get-tuple-element.63.refs_0_.refs_4_, bf16[4,64,512]{2,1,0:T(8,128)(2,1)} %collective-permute-done.6.refs_1_.refs_5_, bf16[4,64,512]{2,1,0:T(8,128)(2,1)S(1)} %copy-done.5, ...), custom_call_target="tpu_custom_call" | custom-call | flops 2000001024 | bytes 1000 | tf_op jit(solution)/shard_map/near_update/pallas_call | solution.py:259
  44.1 4.2 %collective-permute-start.11 = (s16[144,768]{1,0:T(8,128)(2,1)S(1)}, s16[144,768]{1,0:T(8,128)(2,1)S(1)}, u32[]{:S(2)}, u32[]{:S(2)}) collective-permute-start(s16[144,768]{1,0:T(8,128)(2,1)S(1)} %get-tuple-element.73), channel_id=1, source_target_pairs={{1,17},{2,18},{4,20},{7,23},{9,25},{10,26},{12,28},{15,31},{16,0},... | collective-permute-start | bytes 663560 | tf_op jit(solution)/shard_map/ppermute | solution.py:565
  48.4 2.1 %far_update.5 = (f32[2,128,768]{2,1,0:T(8,128)S(1)}, s16[272,768]{1,0:T(8,128)(2,1)S(1)}, s16[144,384]{1,0:T(8,128)(2,1)S(1)}, s16[144,384]{1,0:T(8,128)(2,1)S(1)}) custom-call(s32[8]{0:T(128)S(1)} %stack.35.where_ref, s32[8,12]{1,0:T(8,128)S(1)} %bitcast.26, bf16[2,4,64,512]{3,2,1,0:T(8,128)(2,1)S(1)} %collective-permute-done.12.a_ref, ...), custom_call_target="tpu_custom_call" | custom-call | flops 6000001024 | bytes 1000 | tf_op jit(solution)/shard_map/far_update/pallas_call | solution.py:308
  50.5 1.3 %collective-permute-start.18 = (s16[144,384]{1,0:T(8,128)(2,1)S(1)}, s16[144,384]{1,0:T(8,128)(2,1)S(1)}, u32[]{:S(2)}, u32[]{:S(2)}) collective-permute-start(s16[144,384]{1,0:T(8,128)(2,1)S(1)} %get-tuple-element.86), channel_id=1, source_target_pairs={{0,4},{1,5},{6,2},{7,3},{8,12},{9,13},{14,10},{15,11},{16,20},{17,... | collective-permute-start | bytes 331784 | tf_op jit(solution)/shard_map/ppermute | solution.py:552
  51.8 1.3 %near_update.7.refs_1_ = f32[2,128,768]{2,1,0:T(8,128)S(1)} custom-call(s32[8]{0:T(128)S(1)} %stack.35.where_ref, s32[8,12]{1,0:T(8,128)S(1)} %bitcast.27, bf16[4,64,512]{2,1,0:T(8,128)(2,1)S(1)} %get-tuple-element.66.refs_4_.refs_0_, bf16[4,64,512]{2,1,0:T(8,128)(2,1)S(1)} %collective-permute-done.8.refs_5_.refs_1_, ...), custom_call_target="tpu_custom_call" | custom-call | flops 2000001024 | bytes 1000 | tf_op jit(solution)/shard_map/near_update/pallas_call | solution.py:259
  53.1 1.4 %collective-permute-start.14 = (s16[272,768]{1,0:T(8,128)(2,1)S(1)}, s16[272,768]{1,0:T(8,128)(2,1)S(1)}, u32[]{:S(2)}, u32[]{:S(2)}) collective-permute-start(s16[272,768]{1,0:T(8,128)(2,1)S(1)} %get-tuple-element.79), channel_id=1, source_target_pairs={{0,8},{8,0},{16,24},{24,16},{1,9},{9,1},{17,25},{25,17},{2,10},{10... | collective-permute-start | bytes 1253384 | tf_op jit(solution)/shard_map/ppermute | solution.py:555
  55.6 0.7 split.7
  56.3 3.1 %collective-permute-start.19 = (bf16[2,4,64,256]{3,2,1,0:T(8,128)(2,1)S(1)}, bf16[2,4,64,256]{3,2,1,0:T(8,128)(2,1)S(1)}, u32[]{:S(2)}, u32[]{:S(2)}) collective-permute-start(bf16[2,4,64,256]{3,2,1,0:T(8,128)(2,1)S(1)} %get-tuple-element.90), channel_id=1, source_target_pairs={{0,2},{1,3},{2,0},{3,1},{4,6},{5,7},{6,4},{7,5},{8,10},{9,11},{10,... | collective-permute-start | bytes 786440 | tf_op jit(solution)/shard_map/ppermute | solution.py:568
  59.4 2.1 %far_update.6 = (f32[2,128,768]{2,1,0:T(8,128)S(1)}, s16[272,768]{1,0:T(8,128)(2,1)S(1)}) custom-call(s32[8]{0:T(128)S(1)} %stack.35.where_ref, s32[8,12]{1,0:T(8,128)S(1)} %bitcast.28, bf16[2,4,64,512]{3,2,1,0:T(8,128)(2,1)S(1)} %collective-permute-done.16.a_ref, bf16[2,4,64,512]{3,2,1,0:T(8,128)(2,1)S(1)} %collective-permute-done.17.b_ref, ...), custom_call_target="tpu_custom_call" | custom-call | flops 6000001024 | bytes 1000 | tf_op jit(solution)/shard_map/far_update/pallas_call | solution.py:308
  61.6 1.4 %collective-permute-start.21 = (s16[272,768]{1,0:T(8,128)(2,1)S(1)}, s16[272,768]{1,0:T(8,128)(2,1)S(1)}, u32[]{:S(2)}, u32[]{:S(2)}) collective-permute-start(s16[272,768]{1,0:T(8,128)(2,1)S(1)} %get-tuple-element.95), channel_id=1, source_target_pairs={{0,8},{8,0},{16,24},{24,16},{1,9},{9,1},{17,25},{25,17},{2,10},{10... | collective-permute-start | bytes 1253384 | tf_op jit(solution)/shard_map/ppermute | solution.py:555
  62.9 2.6 %collective-permute-done.23.got_ref = s16[144,384]{1,0:T(8,128)(2,1)S(1)} collective-permute-done((s16[144,384]{1,0:T(8,128)(2,1)S(1)}, s16[144,384]{1,0:T(8,128)(2,1)S(1)}, u32[]{:S(2)}, u32[]{:S(2)}) %collective-permute-start.23) | collective-permute-done | bytes 110624 | tf_op jit(solution)/shard_map/ppermute | solution.py:555
  66.1 0.8 halve.5
  66.9 4.1 %collective-permute-start.15 = (s16[272,768]{1,0:T(8,128)(2,1)S(1)}, s16[272,768]{1,0:T(8,128)(2,1)S(1)}, u32[]{:S(2)}, u32[]{:S(2)}) collective-permute-start(s16[272,768]{1,0:T(8,128)(2,1)S(1)} %get-tuple-element.81), channel_id=1, source_target_pairs={{1,17},{2,18},{4,20},{7,23},{9,25},{10,26},{12,28},{15,31},{16,0},... | collective-permute-start | bytes 1253384 | tf_op jit(solution)/shard_map/ppermute | solution.py:565
  71.1 1.5 %far_update.7 = (f32[1,128,768]{2,1,0:T(8,128)S(1)}, s16[144,768]{1,0:T(8,128)(2,1)S(1)}) custom-call(s32[8]{0:T(128)S(1)} %stack.35.where_ref, s32[8,12]{1,0:T(8,128)S(1)} %bitcast.29, bf16[2,4,64,256]{3,2,1,0:T(8,128)(2,1)S(1)} %collective-permute-done.19.a_ref, bf16[2,4,64,256]{3,2,1,0:T(8,128)(2,1)S(1)} %collective-permute-done.20.b_ref, ...), custom_call_target="tpu_custom_call" | custom-call | flops 6000001024 | bytes 1000 | tf_op jit(solution)/shard_map/far_update/pallas_call | solution.py:308
  72.6 2.3 %collective-permute-start.25 = (s16[144,768]{1,0:T(8,128)(2,1)S(1)}, s16[144,768]{1,0:T(8,128)(2,1)S(1)}, u32[]{:S(2)}, u32[]{:S(2)}) collective-permute-start(s16[144,768]{1,0:T(8,128)(2,1)S(1)} %get-tuple-element.98), channel_id=1, source_target_pairs={{0,8},{8,0},{16,24},{24,16},{1,9},{9,1},{17,25},{25,17},{2,10},{10... | collective-permute-start | bytes 663560 | tf_op jit(solution)/shard_map/ppermute | solution.py:555
  74.8 4.2 %collective-permute-done.21.got_ref = s16[272,768]{1,0:T(8,128)(2,1)S(1)} collective-permute-done((s16[272,768]{1,0:T(8,128)(2,1)S(1)}, s16[272,768]{1,0:T(8,128)(2,1)S(1)}, u32[]{:S(2)}, u32[]{:S(2)}) %collective-permute-start.21) | collective-permute-done | bytes 417824 | tf_op jit(solution)/shard_map/ppermute | solution.py:555
  79.0 0.8 halve.6
  79.8 1.3 %collective-permute-start.22 = (s16[272,768]{1,0:T(8,128)(2,1)S(1)}, s16[272,768]{1,0:T(8,128)(2,1)S(1)}, u32[]{:S(2)}, u32[]{:S(2)}) collective-permute-start(s16[272,768]{1,0:T(8,128)(2,1)S(1)} %get-tuple-element.97), channel_id=1, source_target_pairs={{0,16},{3,19},{5,21},{6,22},{8,24},{11,27},{13,29},{14,30},{17,1},... | collective-permute-start | bytes 1253384 | tf_op jit(solution)/shard_map/ppermute | solution.py:565
  81.2 1.1 %pivots.1.in_ref = f32[3,128,128]{2,1,0:T(8,128)S(1)} custom-call(s32[8]{0:T(128)S(1)} %stack.35.where_ref, f32[1536,768]{1,0:T(8,128)S(1)} %bitcast.15, f32[3,128,128]{2,1,0:T(8,128)} %collective-permute-done.5.given_ref, s16[144,384]{1,0:T(8,128)(2,1)S(1)} %add_coded.1.one_ref, s16[144,384]{1,0:T(8,128)(2,1)S(1)} %collective-permute-done.24.two_ref), custom_call_target="tpu_custom_call" | custom-call | flops 1000 | bytes 1000 | tf_op jit(solution)/shard_map/pivots/pallas_call | solution.py:507
  82.2 4.6 %factor.2.in_ref = f32[3,128,128]{2,1,0:T(8,128)S(1)} custom-call(f32[3,128,128]{2,1,0:T(8,128)S(1)} %pivots.1.in_ref), custom_call_target="tpu_custom_call" | custom-call | flops 10000001024 | bytes 1000 | tf_op jit(solution)/shard_map/factor/pallas_call | solution.py:82
  88.1 1.3 %collective-permute-start.26 = (s16[144,768]{1,0:T(8,128)(2,1)S(1)}, s16[144,768]{1,0:T(8,128)(2,1)S(1)}, u32[]{:S(2)}, u32[]{:S(2)}) collective-permute-start(s16[144,768]{1,0:T(8,128)(2,1)S(1)} %get-tuple-element.102), channel_id=1, source_target_pairs={{0,16},{3,19},{5,21},{6,22},{8,24},{11,27},{13,29},{14,30},{17,1},... | collective-permute-start | bytes 663560 | tf_op jit(solution)/shard_map/ppermute | solution.py:565
  89.4 6.8 %factor.3.refs_8_ = f32[3,128,128]{2,1,0:T(8,128)S(1)} custom-call(f32[3,128,128]{2,1,0:T(8,128)S(1)} %factor.2.in_ref), custom_call_target="tpu_custom_call" | custom-call | flops 10000001024 | bytes 1000 | tf_op jit(solution)/shard_map/factor/pallas_call | solution.py:82
  96.3 6.8 %collective-permute-start.27 = (f32[3,128,128]{2,1,0:T(8,128)S(1)}, f32[3,128,128]{2,1,0:T(8,128)S(1)}, u32[]{:S(2)}, u32[]{:S(2)}) collective-permute-start(f32[3,128,128]{2,1,0:T(8,128)S(1)} %factor.3.refs_8_), channel_id=1, source_target_pairs={{0,4},{4,0},{1,5},{5,1},{2,6},{6,2},{3,7},{7,3},{8,12},{12,8},{9,1... | collective-permute-start | bytes 589832 | tf_op jit(solution)/shard_map/ppermute | solution.py:623
  103.1 1.1 %collective-permute-done.27.refs_9_ = f32[3,128,128]{2,1,0:T(8,128)S(1)} collective-permute-done((f32[3,128,128]{2,1,0:T(8,128)S(1)}, f32[3,128,128]{2,1,0:T(8,128)S(1)}, u32[]{:S(2)}, u32[]{:S(2)}) %collective-permute-start.27) | collective-permute-done | bytes 196640 | tf_op jit(solution)/shard_map/ppermute | solution.py:623
  104.2 2.2 %combine.1 = (f32[384,768]{1,0:T(8,128)}, f32[6,128,128]{2,1,0:T(8,128)}) custom-call(s32[8]{0:T(128)S(1)} %stack.35.where_ref, f32[1536,768]{1,0:T(8,128)S(1)} %bitcast.15, f32[1,128,768]{2,1,0:T(8,128)S(1)} %get-tuple-element.72.refs_0_, s16[144,768]{1,0:T(8,128)(2,1)S(1)} %collective-permute-done.11.refs_1_, ...), custom_call_target="tpu_custom_call" | custom-call | flops 1000 | bytes 1000 | tf_op jit(solution)/shard_map/combine/pallas_call | solution.py:443
  (58 shorter events, 5.9 us)
Async XLA Ops:
  0.6 11.8 %collective-permute-start = (bf16[8,128,768]{2,1,0:T(8,128)(2,1)}, bf16[8,128,768]{2,1,0:T(8,128)(2,1)S(1)}, u32[]{:S(2)}, u32[]{:S(2)}) collective-permute-start(bf16[8,128,768]{2,1,0:T(8,128)(2,1)} %bitcast.19), channel_id=1, source_target_pairs={{0,4},{4,0},{1,5},{5,1},{2,6},{6,2},{3,7},{7,3},{8,12},{12,8},{9,1... | collective-permute-start | bytes 4718600 | tf_op jit(solution)/shard_map/ppermute | solution.py:572
  1.4 1.4 %copy-start.1 = (bf16[1,8,1536,64]{2,3,1,0:T(8,128)(2,1)S(1)}, bf16[1,8,1536,64]{2,3,1,0:T(8,128)(2,1)}, u32[]{:S(2)}) copy-start(bf16[1,8,1536,64]{2,3,1,0:T(8,128)(2,1)} %param.5) | copy-start | bytes 4718596
  3.6 12.5 %collective-permute-start.1 = (bf16[4,64,512]{2,1,0:T(8,128)(2,1)}, bf16[4,64,512]{2,1,0:T(8,128)(2,1)}, u32[]{:S(2)}, u32[]{:S(2)}) collective-permute-start(bf16[4,64,512]{2,1,0:T(8,128)(2,1)} %get-tuple-element.55.refs_0_), channel_id=1, source_target_pairs={{0,1},{1,0},{2,3},{3,2},{4,5},{5,4},{6,7},{7,6},{8,9},{9,8},{10,11... | collective-permute-start | bytes 786440 | tf_op jit(solution)/shard_map/ppermute | solution.py:568
  4.9 11.3 %collective-permute-start.2 = (bf16[4,64,512]{2,1,0:T(8,128)(2,1)}, bf16[4,64,512]{2,1,0:T(8,128)(2,1)}, u32[]{:S(2)}, u32[]{:S(2)}) collective-permute-start(bf16[4,64,512]{2,1,0:T(8,128)(2,1)} %get-tuple-element.56.refs_2_), channel_id=1, source_target_pairs={{0,2},{1,3},{2,0},{3,1},{4,6},{5,7},{6,4},{7,5},{8,10},{9,11},{10,... | collective-permute-start | bytes 786440 | tf_op jit(solution)/shard_map/ppermute | solution.py:568
  6.3 0.7 copy-start.4
  7.0 13.8 %collective-permute-start.6 = (bf16[4,64,512]{2,1,0:T(8,128)(2,1)S(1)}, bf16[4,64,512]{2,1,0:T(8,128)(2,1)}, u32[]{:S(2)}, u32[]{:S(2)}) collective-permute-start(bf16[4,64,512]{2,1,0:T(8,128)(2,1)S(1)} %get-tuple-element.63.refs_0_.refs_4_), channel_id=1, source_target_pairs={{0,1},{1,0},{2,3},{3,2},{4,5},{5,4},{6,7},{7,6},{8,9},{9,8},{10,11... | collective-permute-start | bytes 786440 | tf_op jit(solution)/shard_map/ppermute | solution.py:568
  7.4 2.3 %copy-start = (f32[1536,768]{1,0:T(8,128)S(1)}, f32[1536,768]{1,0:T(8,128)}, u32[]{:S(2)}) copy-start(f32[1536,768]{1,0:T(8,128)} %anc_ref.4) | copy-start | bytes 14155780
  9.7 2.6 %copy-start.7 = (s32[1,8,6]{1,0,2:T(1,128)S(1)}, s32[1,8,6]{1,0,2:T(1,128)}, u32[]{:S(2)}) copy-start(s32[1,8,6]{1,0,2:T(1,128)} %param.8) | copy-start | bytes 580
  9.7 5.0 %copy-start.3 = (bf16[1,8,128,768]{3,2,1,0:T(8,128)(2,1)S(1)}, bf16[1,8,128,768]{3,2,1,0:T(8,128)(2,1)}, u32[]{:S(2)}) copy-start(bf16[1,8,128,768]{3,2,1,0:T(8,128)(2,1)} %param.6) | copy-start | bytes 4718596
  11.0 8.4 %collective-permute-start.5 = (f32[3,128,128]{2,1,0:T(8,128)}, f32[3,128,128]{2,1,0:T(8,128)}, u32[]{:S(2)}, u32[]{:S(2)}) collective-permute-start(f32[3,128,128]{2,1,0:T(8,128)} %later_blocks.1), channel_id=1, source_target_pairs={{0,4},{1,5},{6,2},{7,3},{8,12},{9,13},{14,10},{15,11},{16,20},{17,... | collective-permute-start | bytes 589832 | tf_op jit(solution)/shard_map/ppermute | solution.py:552
  12.4 10.7 %collective-permute-start.7 = (bf16[4,64,512]{2,1,0:T(8,128)(2,1)}, bf16[4,64,512]{2,1,0:T(8,128)(2,1)S(1)}, u32[]{:S(2)}, u32[]{:S(2)}) collective-permute-start(bf16[4,64,512]{2,1,0:T(8,128)(2,1)} %copy-done.4), channel_id=1, source_target_pairs={{0,2},{1,3},{2,0},{3,1},{4,6},{5,7},{6,4},{7,5},{8,10},{9,11},{10,... | collective-permute-start | bytes 786440 | tf_op jit(solution)/shard_map/ppermute | solution.py:568
  14.8 3.1 %copy-start.2 = (bf16[1,8,1536,64]{2,3,1,0:T(8,128)(2,1)S(1)}, bf16[1,8,1536,64]{2,3,1,0:T(8,128)(2,1)}, u32[]{:S(2)}) copy-start(bf16[1,8,1536,64]{2,3,1,0:T(8,128)(2,1)} %param.5) | copy-start | bytes 4718596
  16.1 4.9 %copy-start.6 = (s32[1,8,12]{2,1,0:T(8,128)S(1)}, s32[1,8,12]{2,1,0:T(8,128)}, u32[]{:S(2)}) copy-start(s32[1,8,12]{2,1,0:T(8,128)} %param.7) | copy-start | bytes 1156
  18.1 8.4 %collective-permute-start.8 = (bf16[4,64,512]{2,1,0:T(8,128)(2,1)S(1)}, bf16[4,64,512]{2,1,0:T(8,128)(2,1)S(1)}, u32[]{:S(2)}, u32[]{:S(2)}) collective-permute-start(bf16[4,64,512]{2,1,0:T(8,128)(2,1)S(1)} %get-tuple-element.66.refs_4_.refs_0_), channel_id=1, source_target_pairs={{0,1},{1,0},{2,3},{3,2},{4,5},{5,4},{6,7},{7,6},{8,9},{9,8},{10,11... | collective-permute-start | bytes 786440 | tf_op jit(solution)/shard_map/ppermute | solution.py:568
  19.3 8.1 %collective-permute-start.9 = (bf16[4,64,512]{2,1,0:T(8,128)(2,1)S(1)}, bf16[4,64,512]{2,1,0:T(8,128)(2,1)S(1)}, u32[]{:S(2)}, u32[]{:S(2)}) collective-permute-start(bf16[4,64,512]{2,1,0:T(8,128)(2,1)S(1)} %get-tuple-element.67.refs_6_.refs_2_), channel_id=1, source_target_pairs={{0,2},{1,3},{2,0},{3,1},{4,6},{5,7},{6,4},{7,5},{8,10},{9,11},{10,... | collective-permute-start | bytes 786440 | tf_op jit(solution)/shard_map/ppermute | solution.py:568
  19.4 13.7 %collective-permute-start.3 = (bf16[2,4,64,256]{3,2,1,0:T(8,128)(2,1)S(1)}, bf16[2,4,64,256]{3,2,1,0:T(8,128)(2,1)S(1)}, u32[]{:S(2)}, u32[]{:S(2)}) collective-permute-start(bf16[2,4,64,256]{3,2,1,0:T(8,128)(2,1)S(1)} %get-tuple-element.57), channel_id=1, source_target_pairs={{0,2},{1,3},{2,0},{3,1},{4,6},{5,7},{6,4},{7,5},{8,10},{9,11},{10,... | collective-permute-start | bytes 786440 | tf_op jit(solution)/shard_map/ppermute | solution.py:568
  20.8 12.3 %collective-permute-start.4 = (bf16[2,4,64,256]{3,2,1,0:T(8,128)(2,1)S(1)}, bf16[2,4,64,256]{3,2,1,0:T(8,128)(2,1)S(1)}, u32[]{:S(2)}, u32[]{:S(2)}) collective-permute-start(bf16[2,4,64,256]{3,2,1,0:T(8,128)(2,1)S(1)} %get-tuple-element.58), channel_id=1, source_target_pairs={{0,1},{1,0},{2,3},{3,2},{4,5},{5,4},{6,7},{7,6},{8,9},{9,8},{10,11... | collective-permute-start | bytes 786440 | tf_op jit(solution)/shard_map/ppermute | solution.py:568
  21.1 6.4 %copy-start.5 = (bf16[4,64,512]{2,1,0:T(8,128)(2,1)S(1)}, bf16[4,64,512]{2,1,0:T(8,128)(2,1)}, u32[]{:S(2)}) copy-start(bf16[4,64,512]{2,1,0:T(8,128)(2,1)} %copy-done.4) | copy-start | bytes 786436
  29.1 19.2 %collective-permute-start.12 = (bf16[2,4,64,512]{3,2,1,0:T(8,128)(2,1)S(1)}, bf16[2,4,64,512]{3,2,1,0:T(8,128)(2,1)S(1)}, u32[]{:S(2)}, u32[]{:S(2)}) collective-permute-start(bf16[2,4,64,512]{3,2,1,0:T(8,128)(2,1)S(1)} %get-tuple-element.68), channel_id=1, source_target_pairs={{0,2},{1,3},{2,0},{3,1},{4,6},{5,7},{6,4},{7,5},{8,10},{9,11},{10,... | collective-permute-start | bytes 1572872 | tf_op jit(solution)/shard_map/ppermute | solution.py:568
  29.2 19.2 %collective-permute-start.13 = (bf16[2,4,64,512]{3,2,1,0:T(8,128)(2,1)S(1)}, bf16[2,4,64,512]{3,2,1,0:T(8,128)(2,1)S(1)}, u32[]{:S(2)}, u32[]{:S(2)}) collective-permute-start(bf16[2,4,64,512]{3,2,1,0:T(8,128)(2,1)S(1)} %get-tuple-element.74), channel_id=1, source_target_pairs={{0,1},{1,0},{2,3},{3,2},{4,5},{5,4},{6,7},{7,6},{8,9},{9,8},{10,11... | collective-permute-start | bytes 1572872 | tf_op jit(solution)/shard_map/ppermute | solution.py:568
  34.6 8.9 %collective-permute-start.10 = (s16[144,768]{1,0:T(8,128)(2,1)S(1)}, s16[144,768]{1,0:T(8,128)(2,1)S(1)}, u32[]{:S(2)}, u32[]{:S(2)}) collective-permute-start(s16[144,768]{1,0:T(8,128)(2,1)S(1)} %get-tuple-element.71), channel_id=1, source_target_pairs={{0,8},{8,0},{16,24},{24,16},{1,9},{9,1},{17,25},{25,17},{2,10},{10... | collective-permute-start | bytes 663560 | tf_op jit(solution)/shard_map/ppermute | solution.py:555
  39.2 20.3 %collective-permute-start.16 = (bf16[2,4,64,512]{3,2,1,0:T(8,128)(2,1)S(1)}, bf16[2,4,64,512]{3,2,1,0:T(8,128)(2,1)S(1)}, u32[]{:S(2)}, u32[]{:S(2)}) collective-permute-start(bf16[2,4,64,512]{3,2,1,0:T(8,128)(2,1)S(1)} %get-tuple-element.83), channel_id=1, source_target_pairs={{0,2},{1,3},{2,0},{3,1},{4,6},{5,7},{6,4},{7,5},{8,10},{9,11},{10,... | collective-permute-start | bytes 1572872 | tf_op jit(solution)/shard_map/ppermute | solution.py:568
  39.2 20.2 %collective-permute-start.17 = (bf16[2,4,64,512]{3,2,1,0:T(8,128)(2,1)S(1)}, bf16[2,4,64,512]{3,2,1,0:T(8,128)(2,1)S(1)}, u32[]{:S(2)}, u32[]{:S(2)}) collective-permute-start(bf16[2,4,64,512]{3,2,1,0:T(8,128)(2,1)S(1)} %get-tuple-element.84), channel_id=1, source_target_pairs={{0,1},{1,0},{2,3},{3,2},{4,5},{5,4},{6,7},{7,6},{8,9},{9,8},{10,11... | collective-permute-start | bytes 1572872 | tf_op jit(solution)/shard_map/ppermute | solution.py:568
  44.1 12.2 %collective-permute-start.11 = (s16[144,768]{1,0:T(8,128)(2,1)S(1)}, s16[144,768]{1,0:T(8,128)(2,1)S(1)}, u32[]{:S(2)}, u32[]{:S(2)}) collective-permute-start(s16[144,768]{1,0:T(8,128)(2,1)S(1)} %get-tuple-element.73), channel_id=1, source_target_pairs={{1,17},{2,18},{4,20},{7,23},{9,25},{10,26},{12,28},{15,31},{16,0},... | collective-permute-start | bytes 663560 | tf_op jit(solution)/shard_map/ppermute | solution.py:565
  50.5 4.0 %collective-permute-start.18 = (s16[144,384]{1,0:T(8,128)(2,1)S(1)}, s16[144,384]{1,0:T(8,128)(2,1)S(1)}, u32[]{:S(2)}, u32[]{:S(2)}) collective-permute-start(s16[144,384]{1,0:T(8,128)(2,1)S(1)} %get-tuple-element.86), channel_id=1, source_target_pairs={{0,4},{1,5},{6,2},{7,3},{8,12},{9,13},{14,10},{15,11},{16,20},{17,... | collective-permute-start | bytes 331784 | tf_op jit(solution)/shard_map/ppermute | solution.py:552
  53.1 13.0 %collective-permute-start.14 = (s16[272,768]{1,0:T(8,128)(2,1)S(1)}, s16[272,768]{1,0:T(8,128)(2,1)S(1)}, u32[]{:S(2)}, u32[]{:S(2)}) collective-permute-start(s16[272,768]{1,0:T(8,128)(2,1)S(1)} %get-tuple-element.79), channel_id=1, source_target_pairs={{0,8},{8,0},{16,24},{24,16},{1,9},{9,1},{17,25},{25,17},{2,10},{10... | collective-permute-start | bytes 1253384 | tf_op jit(solution)/shard_map/ppermute | solution.py:555
  55.0 10.6 %collective-permute-start.23 = (s16[144,384]{1,0:T(8,128)(2,1)S(1)}, s16[144,384]{1,0:T(8,128)(2,1)S(1)}, u32[]{:S(2)}, u32[]{:S(2)}) collective-permute-start(s16[144,384]{1,0:T(8,128)(2,1)S(1)} %pick.1.mine_ref), channel_id=1, source_target_pairs={{0,8},{8,0},{16,24},{24,16},{1,9},{9,1},{17,25},{25,17},{2,10},{10... | collective-permute-start | bytes 331784 | tf_op jit(solution)/shard_map/ppermute | solution.py:555
  56.3 14.7 %collective-permute-start.19 = (bf16[2,4,64,256]{3,2,1,0:T(8,128)(2,1)S(1)}, bf16[2,4,64,256]{3,2,1,0:T(8,128)(2,1)S(1)}, u32[]{:S(2)}, u32[]{:S(2)}) collective-permute-start(bf16[2,4,64,256]{3,2,1,0:T(8,128)(2,1)S(1)} %get-tuple-element.90), channel_id=1, source_target_pairs={{0,2},{1,3},{2,0},{3,1},{4,6},{5,7},{6,4},{7,5},{8,10},{9,11},{10,... | collective-permute-start | bytes 786440 | tf_op jit(solution)/shard_map/ppermute | solution.py:568
  59.4 11.6 %collective-permute-start.20 = (bf16[2,4,64,256]{3,2,1,0:T(8,128)(2,1)S(1)}, bf16[2,4,64,256]{3,2,1,0:T(8,128)(2,1)S(1)}, u32[]{:S(2)}, u32[]{:S(2)}) collective-permute-start(bf16[2,4,64,256]{3,2,1,0:T(8,128)(2,1)S(1)} %get-tuple-element.91), channel_id=1, source_target_pairs={{0,1},{1,0},{2,3},{3,2},{4,5},{5,4},{6,7},{7,6},{8,9},{9,8},{10,11... | collective-permute-start | bytes 786440 | tf_op jit(solution)/shard_map/ppermute | solution.py:568
  61.6 17.4 %collective-permute-start.21 = (s16[272,768]{1,0:T(8,128)(2,1)S(1)}, s16[272,768]{1,0:T(8,128)(2,1)S(1)}, u32[]{:S(2)}, u32[]{:S(2)}) collective-permute-start(s16[272,768]{1,0:T(8,128)(2,1)S(1)} %get-tuple-element.95), channel_id=1, source_target_pairs={{0,8},{8,0},{16,24},{24,16},{1,9},{9,1},{17,25},{25,17},{2,10},{10... | collective-permute-start | bytes 1253384 | tf_op jit(solution)/shard_map/ppermute | solution.py:555
  65.7 15.4 %collective-permute-start.24 = (s16[144,384]{1,0:T(8,128)(2,1)S(1)}, s16[144,384]{1,0:T(8,128)(2,1)S(1)}, u32[]{:S(2)}, u32[]{:S(2)}) collective-permute-start(s16[144,384]{1,0:T(8,128)(2,1)S(1)} %add_coded.1.one_ref), channel_id=1, source_target_pairs={{0,16},{8,24},{16,0},{24,8},{1,17},{9,25},{17,1},{25,9},{2,18},{10... | collective-permute-start | bytes 331784 | tf_op jit(solution)/shard_map/ppermute | solution.py:555
  66.9 36.2 %collective-permute-start.15 = (s16[272,768]{1,0:T(8,128)(2,1)S(1)}, s16[272,768]{1,0:T(8,128)(2,1)S(1)}, u32[]{:S(2)}, u32[]{:S(2)}) collective-permute-start(s16[272,768]{1,0:T(8,128)(2,1)S(1)} %get-tuple-element.81), channel_id=1, source_target_pairs={{1,17},{2,18},{4,20},{7,23},{9,25},{10,26},{12,28},{15,31},{16,0},... | collective-permute-start | bytes 1253384 | tf_op jit(solution)/shard_map/ppermute | solution.py:565
  71.0 10.1 %slice-start = ((s8[4718592]{0:T(1024)(128)(4,1)}), s8[4194304]{0:T(1024)(128)(4,1)S(1)}, s32[]{:S(2)}) async-start(s8[4718592]{0:T(1024)(128)(4,1)} %bitcast.14), calls=%async_computation | async-start | bytes 8388608
  71.0 10.1 %slice-start.1 = ((s8[4718592]{0:T(1024)(128)(4,1)}), s8[524288]{0:T(1024)(128)(4,1)S(1)}, s32[]{:S(2)}) async-start(s8[4718592]{0:T(1024)(128)(4,1)} %bitcast.14), calls=%async_computation.1 | async-start | bytes 1048576
  72.6 14.9 %collective-permute-start.25 = (s16[144,768]{1,0:T(8,128)(2,1)S(1)}, s16[144,768]{1,0:T(8,128)(2,1)S(1)}, u32[]{:S(2)}, u32[]{:S(2)}) collective-permute-start(s16[144,768]{1,0:T(8,128)(2,1)S(1)} %get-tuple-element.98), channel_id=1, source_target_pairs={{0,8},{8,0},{16,24},{24,16},{1,9},{9,1},{17,25},{25,17},{2,10},{10... | collective-permute-start | bytes 663560 | tf_op jit(solution)/shard_map/ppermute | solution.py:555
  79.8 24.4 %collective-permute-start.22 = (s16[272,768]{1,0:T(8,128)(2,1)S(1)}, s16[272,768]{1,0:T(8,128)(2,1)S(1)}, u32[]{:S(2)}, u32[]{:S(2)}) collective-permute-start(s16[272,768]{1,0:T(8,128)(2,1)S(1)} %get-tuple-element.97), channel_id=1, source_target_pairs={{0,16},{3,19},{5,21},{6,22},{8,24},{11,27},{13,29},{14,30},{17,1},... | collective-permute-start | bytes 1253384 | tf_op jit(solution)/shard_map/ppermute | solution.py:565
  88.1 16.0 %collective-permute-start.26 = (s16[144,768]{1,0:T(8,128)(2,1)S(1)}, s16[144,768]{1,0:T(8,128)(2,1)S(1)}, u32[]{:S(2)}, u32[]{:S(2)}) collective-permute-start(s16[144,768]{1,0:T(8,128)(2,1)S(1)} %get-tuple-element.102), channel_id=1, source_target_pairs={{0,16},{3,19},{5,21},{6,22},{8,24},{11,27},{13,29},{14,30},{17,1},... | collective-permute-start | bytes 663560 | tf_op jit(solution)/shard_map/ppermute | solution.py:565
  96.3 7.9 %collective-permute-start.27 = (f32[3,128,128]{2,1,0:T(8,128)S(1)}, f32[3,128,128]{2,1,0:T(8,128)S(1)}, u32[]{:S(2)}, u32[]{:S(2)}) collective-permute-start(f32[3,128,128]{2,1,0:T(8,128)S(1)} %factor.3.refs_8_), channel_id=1, source_target_pairs={{0,4},{4,0},{1,5},{5,1},{2,6},{6,2},{3,7},{7,3},{8,12},{12,8},{9,1... | collective-permute-start | bytes 589832 | tf_op jit(solution)/shard_map/ppermute | solution.py:623

commit v12 on v11

--- a/solution.py
+++ b/solution.py
@@ -15,7 +15,8 @@
 CODE_TOP = 32500.0
 EXP_STEPS = 128.0
 EXP_ROWS = 16
-HALF_STEPS = 48
+HALF_STEPS = 40
+MORE_STEPS = 80
 LU = 10
 NEAR = 2
 FAR = 6
@@ -607,19 +608,20 @@
     kept1, coded1, *diag = far_part(1, diag, kept0, sent0)
     mine = pick(where, diag[0], to_other_core(diag[1]))
     near = add_coded(mine, over_layers(mine, 1))
-    sum1, sent1 = halve(where, kept1, over_layers(coded1, 1), chunks[1])
+    sum1, sent1 = halve(where, kept1, over_layers(after(coded1, mine), 1), chunks[1])
     got1 = far_layers(sent1, chunks[1])
     far = over_layers(near, 2)
     second_step(sides[2][0], mine)
     kept2, coded2 = far_part(2, [], kept1, mine, got0)
     kept3, coded3 = far_part(3, [], kept2, sent1, mine)
+    own = pivots(where, anc, given, near, after(far, coded3))
+    half_lu = factor(own, 0, HALF_STEPS)
     sum2, sent2 = halve(where, after(kept2, kept3), over_layers(coded2, 1), chunks[2])
     got2 = far_layers(sent2, chunks[2])
-    own = pivots(where, anc, given, near, after(far, sent2, coded3))
-    half_lu = factor(own, 0, HALF_STEPS)
-    sum3, sent3 = halve(where, after(kept3, half_lu), over_layers(coded3, 1), chunks[3])
+    more_lu = factor(after(half_lu, sent2), HALF_STEPS, MORE_STEPS)
+    sum3, sent3 = halve(where, after(kept3, more_lu), over_layers(coded3, 1), chunks[3])
     got3 = far_layers(sent3, chunks[3])
-    lu = factor(after(half_lu, sent3), HALF_STEPS, BLK)
+    lu = factor(after(more_lu, sent3), MORE_STEPS, BLK)
     lu_got = lax.ppermute(lu, "row", xor_perm(rows, 1))
     pairs = [(sum0, got0), (sum1, got1), (sum2, got2), (sum3, got3)]
     return tuple(combine(where, anc, pairs, lu, lu_got, chunks, share))

time: 107 us -> 109 us (1.019)
  the two profiles are of different devices: /device:TPU:9 before, /device:TPU:2 now
where the time goes in v12:
time: 109 us; the launch traced here: 108 us
  Pallas kernels  43.1 us (40%)
  starting transfers between devices  37 us (34%)
  waiting for transfers between devices  22.5 us (21%)
  local copies, waits for them, and re-layouts  4.62 us (4%)
  between operations  1.22 us (1%)
    ppermute x14, starting transfers between devices, over(): return lax.ppermute(value, 'col', xor_perm(cols, bit))  14.8 us
    pallas_call x3, Pallas kernels, factor(): pl.pallas_call(functools.partial(lu_kernel, begin, end), out_shape=jax.Sh...  11.4 us
    ppermute x4, starting transfers between devices, far_layers(): return lax.ppermute(value, everyone, perm)  8.8 us
    ppermute x6, waiting for transfers between devices, over_layers(): return lax.ppermute(value, 'layer', xor_perm(layers, bit))  8.33 us
    ppermute x6, starting transfers between devices, over_layers(): return lax.ppermute(value, 'layer', xor_perm(layers, bit))  8.01 us
    pallas_call x4, Pallas kernels, near_update(): pl.pallas_call(functools.partial(near_kernel, chunk, blocks), out_shape=j...  7.94 us
    pallas_call x4, Pallas kernels, far_update(): pl.pallas_call(functools.partial(far_kernel, chunk, blocks, len(earlier))...  7.11 us
    ppermute x14, waiting for transfers between devices, over(): return lax.ppermute(value, 'col', xor_perm(cols, bit))  6.76 us
  transfers between devices with their start and end apart: 28, of which 8 were waited for; matrix products, arithmetic and copies ran while one was open for 0% of the time, Pallas kernels for 38%

profile of v12, /device:TPU:2, one launch (start us, length us, event | category | flops | bytes accessed | tf_op | source)
XLA Modules:
  0.0 108.4 jit_solution(13093297633844339021)
XLA Ops:
  0.7 1.4 %copy-done.1 = bf16[1,8,1536,64]{2,3,1,0:T(8,128)(2,1)S(1)} copy-done((bf16[1,8,1536,64]{2,3,1,0:T(8,128)(2,1)S(1)}, bf16[1,8,1536,64]{2,3,1,0:T(8,128)(2,1)}, u32[]{:S(2)}) %copy-start.1) | copy-done | bytes 1572888
  2.1 0.8 halves.3
  3.1 2.0 %collective-permute-start.2 = (bf16[4,64,512]{2,1,0:T(8,128)(2,1)}, bf16[4,64,512]{2,1,0:T(8,128)(2,1)}, u32[]{:S(2)}, u32[]{:S(2)}) collective-permute-start(bf16[4,64,512]{2,1,0:T(8,128)(2,1)} %get-tuple-element.58.refs_2_), channel_id=1, source_target_pairs={{0,2},{1,3},{2,0},{3,1},{4,6},{5,7},{6,4},{7,5},{8,10},{9,11},{10,... | collective-permute-start | bytes 786440 | tf_op jit(solution)/shard_map/ppermute | solution.py:569
  6.0 1.5 %collective-permute-start.6 = (bf16[4,64,512]{2,1,0:T(8,128)(2,1)S(1)}, bf16[4,64,512]{2,1,0:T(8,128)(2,1)}, u32[]{:S(2)}, u32[]{:S(2)}) collective-permute-start(bf16[4,64,512]{2,1,0:T(8,128)(2,1)S(1)} %get-tuple-element.65.refs_0_.refs_4_), channel_id=1, source_target_pairs={{0,1},{1,0},{2,3},{3,2},{4,5},{5,4},{6,7},{7,6},{8,9},{9,8},{10,11... | collective-permute-start | bytes 786440 | tf_op jit(solution)/shard_map/ppermute | solution.py:569
  7.5 2.3 %copy-done = f32[1536,768]{1,0:T(8,128)S(1)} copy-done((f32[1536,768]{1,0:T(8,128)S(1)}, f32[1536,768]{1,0:T(8,128)}, u32[]{:S(2)}) %copy-start) | copy-done | bytes 4718616
  9.9 1.3 %later_blocks.1 = f32[3,128,128]{2,1,0:T(8,128)} custom-call(s32[8]{0:T(128)S(1)} %stack.35.where_ref, f32[1536,768]{1,0:T(8,128)S(1)} %copy-done), custom_call_target="tpu_custom_call" | custom-call | flops 1000 | bytes 1000 | tf_op jit(solution)/shard_map/later_blocks/pallas_call | solution.py:481
  11.2 2.2 %collective-permute-start.5 = (f32[3,128,128]{2,1,0:T(8,128)}, f32[3,128,128]{2,1,0:T(8,128)}, u32[]{:S(2)}, u32[]{:S(2)}) collective-permute-start(f32[3,128,128]{2,1,0:T(8,128)} %later_blocks.1), channel_id=1, source_target_pairs={{0,4},{1,5},{6,2},{7,3},{8,12},{9,13},{14,10},{15,11},{16,20},{17,... | collective-permute-start | bytes 589832 | tf_op jit(solution)/shard_map/ppermute | solution.py:553
  13.5 1.4 %masked_right.1 = (bf16[8,128,768]{2,1,0:T(8,128)(2,1)S(1)}, bf16[8,128,768]{2,1,0:T(8,128)(2,1)S(1)}) custom-call(s32[8]{0:T(128)S(1)} %stack.35.where_ref, s32[8,6]{1,0:T(8,128)S(1)} %bitcast.21, bf16[8,128,768]{2,1,0:T(8,128)(2,1)S(1)} %bitcast.20, bf16[8,128,768]{2,1,0:T(8,128)(2,1)S(1)} %collective-permute-done.uo_ref), custom_call_target="tpu_custom_call" | custom-call | flops 1000 | bytes 1000 | tf_op jit(solution)/shard_map/masked_right/pallas_call | solution.py:213
  14.9 1.7 %split.4 = (bf16[2,4,64,256]{3,2,1,0:T(8,128)(2,1)S(1)}, bf16[2,4,64,256]{3,2,1,0:T(8,128)(2,1)S(1)}) custom-call(s32[8]{0:T(128)S(1)} %stack.35.where_ref, bf16[4,64,512]{2,1,0:T(8,128)(2,1)} %get-tuple-element.57.refs_0_, bf16[4,64,512]{2,1,0:T(8,128)(2,1)} %collective-permute-done.1.refs_1_, bf16[4,64,512]{2,1,0:T(8,128)(2,1)} %get-tuple-element.58.refs_2_, ...), custom_call_target="tpu_custom_call" | custom-call | flops 1000 | bytes 1000 | tf_op jit(solution)/shard_map/split/pallas_call | solution.py:169
  17.4 2.0 %collective-permute-start.9 = (bf16[4,64,512]{2,1,0:T(8,128)(2,1)S(1)}, bf16[4,64,512]{2,1,0:T(8,128)(2,1)S(1)}, u32[]{:S(2)}, u32[]{:S(2)}) collective-permute-start(bf16[4,64,512]{2,1,0:T(8,128)(2,1)S(1)} %get-tuple-element.69.refs_6_.refs_2_), channel_id=1, source_target_pairs={{0,2},{1,3},{2,0},{3,1},{4,6},{5,7},{6,4},{7,5},{8,10},{9,11},{10,... | collective-permute-start | bytes 786440 | tf_op jit(solution)/shard_map/ppermute | solution.py:569
  19.5 1.5 %collective-permute-start.4 = (bf16[2,4,64,256]{3,2,1,0:T(8,128)(2,1)S(1)}, bf16[2,4,64,256]{3,2,1,0:T(8,128)(2,1)S(1)}, u32[]{:S(2)}, u32[]{:S(2)}) collective-permute-start(bf16[2,4,64,256]{3,2,1,0:T(8,128)(2,1)S(1)} %get-tuple-element.60), channel_id=1, source_target_pairs={{0,1},{1,0},{2,3},{3,2},{4,5},{5,4},{6,7},{7,6},{8,9},{9,8},{10,11... | collective-permute-start | bytes 786440 | tf_op jit(solution)/shard_map/ppermute | solution.py:569
  21.0 2.0 %near_update.4.refs_1_ = f32[2,128,768]{2,1,0:T(8,128)S(1)} custom-call(s32[8]{0:T(128)S(1)} %stack.35.where_ref, s32[8,12]{1,0:T(8,128)S(1)} %bitcast.22, bf16[4,64,512]{2,1,0:T(8,128)(2,1)} %get-tuple-element.57.refs_0_, bf16[4,64,512]{2,1,0:T(8,128)(2,1)} %collective-permute-done.1.refs_1_, bf16[4,64,512]{2,1,0:T(8,128)(2,1)} %get-tuple-element.58.refs_2_, ...), custom_call_target="tpu_custom_call" | custom-call | flops 2000001024 | bytes 1000 | tf_op jit(solution)/shard_map/near_update/pallas_call | solution.py:260
  23.0 3.0 %collective-permute-done.8.refs_5_.refs_1_ = bf16[4,64,512]{2,1,0:T(8,128)(2,1)S(1)} collective-permute-done((bf16[4,64,512]{2,1,0:T(8,128)(2,1)S(1)}, bf16[4,64,512]{2,1,0:T(8,128)(2,1)S(1)}, u32[]{:S(2)}, u32[]{:S(2)}) %collective-permute-start.8) | collective-permute-done | bytes 262176 | tf_op jit(solution)/shard_map/ppermute | solution.py:569
  26.0 2.0 %collective-permute-done.9.refs_7_.refs_3_ = bf16[4,64,512]{2,1,0:T(8,128)(2,1)S(1)} collective-permute-done((bf16[4,64,512]{2,1,0:T(8,128)(2,1)S(1)}, bf16[4,64,512]{2,1,0:T(8,128)(2,1)S(1)}, u32[]{:S(2)}, u32[]{:S(2)}) %collective-permute-start.9) | collective-permute-done | bytes 262176 | tf_op jit(solution)/shard_map/ppermute | solution.py:569
  28.0 1.6 %split.5 = (bf16[2,4,64,512]{3,2,1,0:T(8,128)(2,1)S(1)}, bf16[2,4,64,512]{3,2,1,0:T(8,128)(2,1)S(1)}) custom-call(s32[8]{0:T(128)S(1)} %stack.35.where_ref, bf16[4,64,512]{2,1,0:T(8,128)(2,1)S(1)} %get-tuple-element.65.refs_0_.refs_4_, bf16[4,64,512]{2,1,0:T(8,128)(2,1)} %collective-permute-done.6.refs_1_.refs_5_, bf16[4,64,512]{2,1,0:T(8,128)(2,1)S(1)} %copy-done.5, ...), custom_call_target="tpu_custom_call" | custom-call | flops 1000 | bytes 1000 | tf_op jit(solution)/shard_map/split/pallas_call | solution.py:169
  30.4 1.5 %collective-permute-start.13 = (bf16[2,4,64,512]{3,2,1,0:T(8,128)(2,1)S(1)}, bf16[2,4,64,512]{3,2,1,0:T(8,128)(2,1)S(1)}, u32[]{:S(2)}, u32[]{:S(2)}) collective-permute-start(bf16[2,4,64,512]{3,2,1,0:T(8,128)(2,1)S(1)} %get-tuple-element.76), channel_id=1, source_target_pairs={{0,1},{1,0},{2,3},{3,2},{4,5},{5,4},{6,7},{7,6},{8,9},{9,8},{10,11... | collective-permute-start | bytes 1572872 | tf_op jit(solution)/shard_map/ppermute | solution.py:569
  31.9 1.7 %collective-permute-done.3.a_ref = bf16[2,4,64,256]{3,2,1,0:T(8,128)(2,1)S(1)} collective-permute-done((bf16[2,4,64,256]{3,2,1,0:T(8,128)(2,1)S(1)}, bf16[2,4,64,256]{3,2,1,0:T(8,128)(2,1)S(1)}, u32[]{:S(2)}, u32[]{:S(2)}) %collective-permute-start.3) | collective-permute-done | bytes 262176 | tf_op jit(solution)/shard_map/ppermute | solution.py:569
  33.6 1.5 %far_update.4 = (f32[1,128,768]{2,1,0:T(8,128)S(1)}, s16[144,768]{1,0:T(8,128)(2,1)S(1)}, s16[144,384]{1,0:T(8,128)(2,1)S(1)}, s16[144,384]{1,0:T(8,128)(2,1)S(1)}) custom-call(s32[8]{0:T(128)S(1)} %stack.35.where_ref, s32[8,12]{1,0:T(8,128)S(1)} %bitcast.23, bf16[2,4,64,256]{3,2,1,0:T(8,128)(2,1)S(1)} %collective-permute-done.3.a_ref, ...), custom_call_target="tpu_custom_call" | custom-call | flops 6000001024 | bytes 1000 | tf_op jit(solution)/shard_map/far_update/pallas_call | solution.py:309
  35.1 1.5 %collective-permute-start.10 = (s16[144,768]{1,0:T(8,128)(2,1)S(1)}, s16[144,768]{1,0:T(8,128)(2,1)S(1)}, u32[]{:S(2)}, u32[]{:S(2)}) collective-permute-start(s16[144,768]{1,0:T(8,128)(2,1)S(1)} %get-tuple-element.73), channel_id=1, source_target_pairs={{0,8},{8,0},{16,24},{24,16},{1,9},{9,1},{17,25},{25,17},{2,10},{10... | collective-permute-start | bytes 663560 | tf_op jit(solution)/shard_map/ppermute | solution.py:556
  36.6 2.5 %near_update.6.refs_1_ = f32[4,128,768]{2,1,0:T(8,128)S(1)} custom-call(s32[8]{0:T(128)S(1)} %stack.35.where_ref, s32[8,12]{1,0:T(8,128)S(1)} %bitcast.24, bf16[4,64,512]{2,1,0:T(8,128)(2,1)} %get-tuple-element.57.refs_0_, bf16[4,64,512]{2,1,0:T(8,128)(2,1)} %collective-permute-done.1.refs_1_, bf16[4,64,512]{2,1,0:T(8,128)(2,1)} %get-tuple-element.58.refs_2_, ...), custom_call_target="tpu_custom_call" | custom-call | flops 2000001024 | bytes 1000 | tf_op jit(solution)/shard_map/near_update/pallas_call | solution.py:260
  39.1 1.8 %split.6 = (bf16[2,4,64,512]{3,2,1,0:T(8,128)(2,1)S(1)}, bf16[2,4,64,512]{3,2,1,0:T(8,128)(2,1)S(1)}) custom-call(s32[8]{0:T(128)S(1)} %stack.35.where_ref, bf16[4,64,512]{2,1,0:T(8,128)(2,1)} %get-tuple-element.57.refs_0_, bf16[4,64,512]{2,1,0:T(8,128)(2,1)} %collective-permute-done.1.refs_1_, bf16[4,64,512]{2,1,0:T(8,128)(2,1)} %get-tuple-element.58.refs_2_, ...), custom_call_target="tpu_custom_call" | custom-call | flops 1000 | bytes 1000 | tf_op jit(solution)/shard_map/split/pallas_call | solution.py:169
  40.9 0.9 collective-permute-start.17
  41.8 1.5 %collective-permute-start.18 = (bf16[2,4,64,512]{3,2,1,0:T(8,128)(2,1)S(1)}, bf16[2,4,64,512]{3,2,1,0:T(8,128)(2,1)S(1)}, u32[]{:S(2)}, u32[]{:S(2)}) collective-permute-start(bf16[2,4,64,512]{3,2,1,0:T(8,128)(2,1)S(1)} %get-tuple-element.89), channel_id=1, source_target_pairs={{0,1},{1,0},{2,3},{3,2},{4,5},{5,4},{6,7},{7,6},{8,9},{9,8},{10,11... | collective-permute-start | bytes 1572872 | tf_op jit(solution)/shard_map/ppermute | solution.py:569
  43.3 2.1 %near_update.5.refs_1_ = f32[4,128,768]{2,1,0:T(8,128)S(1)} custom-call(s32[8]{0:T(128)S(1)} %stack.35.where_ref, s32[8,12]{1,0:T(8,128)S(1)} %bitcast.25, bf16[4,64,512]{2,1,0:T(8,128)(2,1)S(1)} %get-tuple-element.65.refs_0_.refs_4_, bf16[4,64,512]{2,1,0:T(8,128)(2,1)} %collective-permute-done.6.refs_1_.refs_5_, bf16[4,64,512]{2,1,0:T(8,128)(2,1)S(1)} %copy-done.5, ...), custom_call_target="tpu_custom_call" | custom-call | flops 2000001024 | bytes 1000 | tf_op jit(solution)/shard_map/near_update/pallas_call | solution.py:260
  46.2 4.5 %collective-permute-start.11 = (s16[144,768]{1,0:T(8,128)(2,1)S(1)}, s16[144,768]{1,0:T(8,128)(2,1)S(1)}, u32[]{:S(2)}, u32[]{:S(2)}) collective-permute-start(s16[144,768]{1,0:T(8,128)(2,1)S(1)} %get-tuple-element.75), channel_id=1, source_target_pairs={{1,17},{2,18},{4,20},{7,23},{9,25},{10,26},{12,28},{15,31},{16,0},... | collective-permute-start | bytes 663560 | tf_op jit(solution)/shard_map/ppermute | solution.py:566
  50.7 2.0 %far_update.5 = (f32[2,128,768]{2,1,0:T(8,128)S(1)}, s16[272,768]{1,0:T(8,128)(2,1)S(1)}, s16[144,384]{1,0:T(8,128)(2,1)S(1)}, s16[144,384]{1,0:T(8,128)(2,1)S(1)}) custom-call(s32[8]{0:T(128)S(1)} %stack.35.where_ref, s32[8,12]{1,0:T(8,128)S(1)} %bitcast.26, bf16[2,4,64,512]{3,2,1,0:T(8,128)(2,1)S(1)} %collective-permute-done.12.a_ref, ...), custom_call_target="tpu_custom_call" | custom-call | flops 6000001024 | bytes 1000 | tf_op jit(solution)/shard_map/far_update/pallas_call | solution.py:309
  52.8 1.3 %collective-permute-start.14 = (s16[144,384]{1,0:T(8,128)(2,1)S(1)}, s16[144,384]{1,0:T(8,128)(2,1)S(1)}, u32[]{:S(2)}, u32[]{:S(2)}) collective-permute-start(s16[144,384]{1,0:T(8,128)(2,1)S(1)} %get-tuple-element.83), channel_id=1, source_target_pairs={{0,4},{1,5},{6,2},{7,3},{8,12},{9,13},{14,10},{15,11},{16,20},{17,... | collective-permute-start | bytes 331784 | tf_op jit(solution)/shard_map/ppermute | solution.py:553
  54.1 1.3 %near_update.7.refs_1_ = f32[2,128,768]{2,1,0:T(8,128)S(1)} custom-call(s32[8]{0:T(128)S(1)} %stack.35.where_ref, s32[8,12]{1,0:T(8,128)S(1)} %bitcast.27, bf16[4,64,512]{2,1,0:T(8,128)(2,1)S(1)} %get-tuple-element.68.refs_4_.refs_0_, bf16[4,64,512]{2,1,0:T(8,128)(2,1)S(1)} %collective-permute-done.8.refs_5_.refs_1_, ...), custom_call_target="tpu_custom_call" | custom-call | flops 2000001024 | bytes 1000 | tf_op jit(solution)/shard_map/near_update/pallas_call | solution.py:260
  56.5 1.6 %collective-permute-start.15 = (s16[272,768]{1,0:T(8,128)(2,1)S(1)}, s16[272,768]{1,0:T(8,128)(2,1)S(1)}, u32[]{:S(2)}, u32[]{:S(2)}) collective-permute-start(s16[272,768]{1,0:T(8,128)(2,1)S(1)} %get-tuple-element.84), channel_id=1, source_target_pairs={{0,8},{8,0},{16,24},{24,16},{1,9},{9,1},{17,25},{25,17},{2,10},{10... | collective-permute-start | bytes 1253384 | tf_op jit(solution)/shard_map/ppermute | solution.py:556
  58.9 2.3 %collective-permute-start.20 = (bf16[2,4,64,256]{3,2,1,0:T(8,128)(2,1)S(1)}, bf16[2,4,64,256]{3,2,1,0:T(8,128)(2,1)S(1)}, u32[]{:S(2)}, u32[]{:S(2)}) collective-permute-start(bf16[2,4,64,256]{3,2,1,0:T(8,128)(2,1)S(1)} %get-tuple-element.94), channel_id=1, source_target_pairs={{0,1},{1,0},{2,3},{3,2},{4,5},{5,4},{6,7},{7,6},{8,9},{9,8},{10,11... | collective-permute-start | bytes 786440 | tf_op jit(solution)/shard_map/ppermute | solution.py:569
  61.2 2.1 %far_update.6 = (f32[2,128,768]{2,1,0:T(8,128)S(1)}, s16[272,768]{1,0:T(8,128)(2,1)S(1)}) custom-call(s32[8]{0:T(128)S(1)} %stack.35.where_ref, s32[8,12]{1,0:T(8,128)S(1)} %bitcast.28, bf16[2,4,64,512]{3,2,1,0:T(8,128)(2,1)S(1)} %collective-permute-done.17.a_ref, bf16[2,4,64,512]{3,2,1,0:T(8,128)(2,1)S(1)} %collective-permute-done.18.b_ref, ...), custom_call_target="tpu_custom_call" | custom-call | flops 6000001024 | bytes 1000 | tf_op jit(solution)/shard_map/far_update/pallas_call | solution.py:309
  63.9 1.4 %collective-permute-start.24 = (s16[144,384]{1,0:T(8,128)(2,1)S(1)}, s16[144,384]{1,0:T(8,128)(2,1)S(1)}, u32[]{:S(2)}, u32[]{:S(2)}) collective-permute-start(s16[144,384]{1,0:T(8,128)(2,1)S(1)} %add_coded.1.one_ref), channel_id=1, source_target_pairs={{0,16},{8,24},{16,0},{24,8},{1,17},{9,25},{17,1},{25,9},{2,18},{10... | collective-permute-start | bytes 331784 | tf_op jit(solution)/shard_map/ppermute | solution.py:556
  65.3 8.0 %collective-permute-done.15.got_ref = s16[272,768]{1,0:T(8,128)(2,1)S(1)} collective-permute-done((s16[272,768]{1,0:T(8,128)(2,1)S(1)}, s16[272,768]{1,0:T(8,128)(2,1)S(1)}, u32[]{:S(2)}, u32[]{:S(2)}) %collective-permute-start.15) | collective-permute-done | bytes 417824 | tf_op jit(solution)/shard_map/ppermute | solution.py:556
  74.1 1.7 %collective-permute-start.16 = (s16[272,768]{1,0:T(8,128)(2,1)S(1)}, s16[272,768]{1,0:T(8,128)(2,1)S(1)}, u32[]{:S(2)}, u32[]{:S(2)}) collective-permute-start(s16[272,768]{1,0:T(8,128)(2,1)S(1)} %get-tuple-element.86), channel_id=1, source_target_pairs={{1,17},{2,18},{4,20},{7,23},{9,25},{10,26},{12,28},{15,31},{16,0},... | collective-permute-start | bytes 1253384 | tf_op jit(solution)/shard_map/ppermute | solution.py:566
  75.8 1.5 %far_update.7 = (f32[1,128,768]{2,1,0:T(8,128)S(1)}, s16[144,768]{1,0:T(8,128)(2,1)S(1)}) custom-call(s32[8]{0:T(128)S(1)} %stack.35.where_ref, s32[8,12]{1,0:T(8,128)S(1)} %bitcast.29, bf16[2,4,64,256]{3,2,1,0:T(8,128)(2,1)S(1)} %collective-permute-done.19.a_ref, bf16[2,4,64,256]{3,2,1,0:T(8,128)(2,1)S(1)} %collective-permute-done.20.b_ref, ...), custom_call_target="tpu_custom_call" | custom-call | flops 6000001024 | bytes 1000 | tf_op jit(solution)/shard_map/far_update/pallas_call | solution.py:309
  77.3 2.5 %collective-permute-start.25 = (s16[144,768]{1,0:T(8,128)(2,1)S(1)}, s16[144,768]{1,0:T(8,128)(2,1)S(1)}, u32[]{:S(2)}, u32[]{:S(2)}) collective-permute-start(s16[144,768]{1,0:T(8,128)(2,1)S(1)} %get-tuple-element.101), channel_id=1, source_target_pairs={{0,8},{8,0},{16,24},{24,16},{1,9},{9,1},{17,25},{25,17},{2,10},{10... | collective-permute-start | bytes 663560 | tf_op jit(solution)/shard_map/ppermute | solution.py:556
  80.2 1.1 pivots.1.in_ref
  81.3 3.9 %factor.3.in_ref = f32[3,128,128]{2,1,0:T(8,128)S(1)} custom-call(f32[3,128,128]{2,1,0:T(8,128)S(1)} %pivots.1.in_ref), custom_call_target="tpu_custom_call" | custom-call | flops 10000001024 | bytes 1000 | tf_op jit(solution)/shard_map/factor/pallas_call | solution.py:83
  85.2 0.8 halve.6
  86.0 1.3 %collective-permute-start.22 = (s16[272,768]{1,0:T(8,128)(2,1)S(1)}, s16[272,768]{1,0:T(8,128)(2,1)S(1)}, u32[]{:S(2)}, u32[]{:S(2)}) collective-permute-start(s16[272,768]{1,0:T(8,128)(2,1)S(1)} %get-tuple-element.100), channel_id=1, source_target_pairs={{0,16},{3,19},{5,21},{6,22},{8,24},{11,27},{13,29},{14,30},{17,1},... | collective-permute-start | bytes 1253384 | tf_op jit(solution)/shard_map/ppermute | solution.py:566
  87.3 3.5 %factor.4.in_ref = f32[3,128,128]{2,1,0:T(8,128)S(1)} custom-call(f32[3,128,128]{2,1,0:T(8,128)S(1)} %factor.3.in_ref), custom_call_target="tpu_custom_call" | custom-call | flops 10000001024 | bytes 1000 | tf_op jit(solution)/shard_map/factor/pallas_call | solution.py:83
  91.5 1.3 %collective-permute-start.26 = (s16[144,768]{1,0:T(8,128)(2,1)S(1)}, s16[144,768]{1,0:T(8,128)(2,1)S(1)}, u32[]{:S(2)}, u32[]{:S(2)}) collective-permute-start(s16[144,768]{1,0:T(8,128)(2,1)S(1)} %get-tuple-element.106), channel_id=1, source_target_pairs={{0,16},{3,19},{5,21},{6,22},{8,24},{11,27},{13,29},{14,30},{17,1},... | collective-permute-start | bytes 663560 | tf_op jit(solution)/shard_map/ppermute | solution.py:566
  92.8 4.1 %factor.5.refs_8_ = f32[3,128,128]{2,1,0:T(8,128)S(1)} custom-call(f32[3,128,128]{2,1,0:T(8,128)S(1)} %factor.4.in_ref), custom_call_target="tpu_custom_call" | custom-call | flops 10000001024 | bytes 1000 | tf_op jit(solution)/shard_map/factor/pallas_call | solution.py:83
  96.8 1.9 %collective-permute-start.27 = (f32[3,128,128]{2,1,0:T(8,128)S(1)}, f32[3,128,128]{2,1,0:T(8,128)S(1)}, u32[]{:S(2)}, u32[]{:S(2)}) collective-permute-start(f32[3,128,128]{2,1,0:T(8,128)S(1)} %factor.5.refs_8_), channel_id=1, source_target_pairs={{0,4},{4,0},{1,5},{5,1},{2,6},{6,2},{3,7},{7,3},{8,12},{12,8},{9,1... | collective-permute-start | bytes 589832 | tf_op jit(solution)/shard_map/ppermute | solution.py:625
  98.7 1.1 collective-permute-done.27.refs_9_
  99.8 3.9 %collective-permute-done.22.refs_5_ = s16[272,768]{1,0:T(8,128)(2,1)S(1)} collective-permute-done((s16[272,768]{1,0:T(8,128)(2,1)S(1)}, s16[272,768]{1,0:T(8,128)(2,1)S(1)}, u32[]{:S(2)}, u32[]{:S(2)}) %collective-permute-start.22) | collective-permute-done | bytes 417824 | tf_op jit(solution)/shard_map/ppermute | solution.py:566
  103.7 2.4 %collective-permute-done.26.refs_7_ = s16[144,768]{1,0:T(8,128)(2,1)S(1)} collective-permute-done((s16[144,768]{1,0:T(8,128)(2,1)S(1)}, s16[144,768]{1,0:T(8,128)(2,1)S(1)}, u32[]{:S(2)}, u32[]{:S(2)}) %collective-permute-start.26) | collective-permute-done | bytes 221216 | tf_op jit(solution)/shard_map/ppermute | solution.py:566
  106.1 2.2 %combine.1 = (f32[384,768]{1,0:T(8,128)}, f32[6,128,128]{2,1,0:T(8,128)}) custom-call(s32[8]{0:T(128)S(1)} %stack.35.where_ref, f32[1536,768]{1,0:T(8,128)S(1)} %bitcast.15, f32[1,128,768]{2,1,0:T(8,128)S(1)} %get-tuple-element.74.refs_0_, s16[144,768]{1,0:T(8,128)(2,1)S(1)} %collective-permute-done.11.refs_1_, ...), custom_call_target="tpu_custom_call" | custom-call | flops 1000 | bytes 1000 | tf_op jit(solution)/shard_map/combine/pallas_call | solution.py:444
  (59 shorter events, 7.8 us)
Async XLA Ops:
  0.6 12.9 %collective-permute-start = (bf16[8,128,768]{2,1,0:T(8,128)(2,1)}, bf16[8,128,768]{2,1,0:T(8,128)(2,1)S(1)}, u32[]{:S(2)}, u32[]{:S(2)}) collective-permute-start(bf16[8,128,768]{2,1,0:T(8,128)(2,1)} %bitcast.19), channel_id=1, source_target_pairs={{0,4},{4,0},{1,5},{5,1},{2,6},{6,2},{3,7},{7,3},{8,12},{12,8},{9,1... | collective-permute-start | bytes 4718600 | tf_op jit(solution)/shard_map/ppermute | solution.py:573
  0.7 1.4 %copy-start.1 = (bf16[1,8,1536,64]{2,3,1,0:T(8,128)(2,1)S(1)}, bf16[1,8,1536,64]{2,3,1,0:T(8,128)(2,1)}, u32[]{:S(2)}) copy-start(bf16[1,8,1536,64]{2,3,1,0:T(8,128)(2,1)} %param.5) | copy-start | bytes 4718596
  3.0 11.9 %collective-permute-start.1 = (bf16[4,64,512]{2,1,0:T(8,128)(2,1)}, bf16[4,64,512]{2,1,0:T(8,128)(2,1)}, u32[]{:S(2)}, u32[]{:S(2)}) collective-permute-start(bf16[4,64,512]{2,1,0:T(8,128)(2,1)} %get-tuple-element.57.refs_0_), channel_id=1, source_target_pairs={{0,1},{1,0},{2,3},{3,2},{4,5},{5,4},{6,7},{7,6},{8,9},{9,8},{10,11... | collective-permute-start | bytes 786440 | tf_op jit(solution)/shard_map/ppermute | solution.py:569
  3.1 11.9 %collective-permute-start.2 = (bf16[4,64,512]{2,1,0:T(8,128)(2,1)}, bf16[4,64,512]{2,1,0:T(8,128)(2,1)}, u32[]{:S(2)}, u32[]{:S(2)}) collective-permute-start(bf16[4,64,512]{2,1,0:T(8,128)(2,1)} %get-tuple-element.58.refs_2_), channel_id=1, source_target_pairs={{0,2},{1,3},{2,0},{3,1},{4,6},{5,7},{6,4},{7,5},{8,10},{9,11},{10,... | collective-permute-start | bytes 786440 | tf_op jit(solution)/shard_map/ppermute | solution.py:569
  5.3 0.7 copy-start.4
  6.0 13.5 %collective-permute-start.6 = (bf16[4,64,512]{2,1,0:T(8,128)(2,1)S(1)}, bf16[4,64,512]{2,1,0:T(8,128)(2,1)}, u32[]{:S(2)}, u32[]{:S(2)}) collective-permute-start(bf16[4,64,512]{2,1,0:T(8,128)(2,1)S(1)} %get-tuple-element.65.refs_0_.refs_4_), channel_id=1, source_target_pairs={{0,1},{1,0},{2,3},{3,2},{4,5},{5,4},{6,7},{7,6},{8,9},{9,8},{10,11... | collective-permute-start | bytes 786440 | tf_op jit(solution)/shard_map/ppermute | solution.py:569
  7.5 2.3 %copy-start = (f32[1536,768]{1,0:T(8,128)S(1)}, f32[1536,768]{1,0:T(8,128)}, u32[]{:S(2)}) copy-start(f32[1536,768]{1,0:T(8,128)} %anc_ref.4) | copy-start | bytes 14155780
  9.9 3.5 %copy-start.7 = (s32[1,8,6]{1,0,2:T(1,128)S(1)}, s32[1,8,6]{1,0,2:T(1,128)}, u32[]{:S(2)}) copy-start(s32[1,8,6]{1,0,2:T(1,128)} %param.8) | copy-start | bytes 580
  9.9 3.6 %copy-start.3 = (bf16[1,8,128,768]{3,2,1,0:T(8,128)(2,1)S(1)}, bf16[1,8,128,768]{3,2,1,0:T(8,128)(2,1)}, u32[]{:S(2)}) copy-start(bf16[1,8,128,768]{3,2,1,0:T(8,128)(2,1)} %param.6) | copy-start | bytes 4718596
  11.2 8.3 %collective-permute-start.5 = (f32[3,128,128]{2,1,0:T(8,128)}, f32[3,128,128]{2,1,0:T(8,128)}, u32[]{:S(2)}, u32[]{:S(2)}) collective-permute-start(f32[3,128,128]{2,1,0:T(8,128)} %later_blocks.1), channel_id=1, source_target_pairs={{0,4},{1,5},{6,2},{7,3},{8,12},{9,13},{14,10},{15,11},{16,20},{17,... | collective-permute-start | bytes 589832 | tf_op jit(solution)/shard_map/ppermute | solution.py:553
  13.5 9.5 %collective-permute-start.7 = (bf16[4,64,512]{2,1,0:T(8,128)(2,1)}, bf16[4,64,512]{2,1,0:T(8,128)(2,1)S(1)}, u32[]{:S(2)}, u32[]{:S(2)}) collective-permute-start(bf16[4,64,512]{2,1,0:T(8,128)(2,1)} %copy-done.4), channel_id=1, source_target_pairs={{0,2},{1,3},{2,0},{3,1},{4,6},{5,7},{6,4},{7,5},{8,10},{9,11},{10,... | collective-permute-start | bytes 786440 | tf_op jit(solution)/shard_map/ppermute | solution.py:569
  13.5 3.1 %copy-start.2 = (bf16[1,8,1536,64]{2,3,1,0:T(8,128)(2,1)S(1)}, bf16[1,8,1536,64]{2,3,1,0:T(8,128)(2,1)}, u32[]{:S(2)}) copy-start(bf16[1,8,1536,64]{2,3,1,0:T(8,128)(2,1)} %param.5) | copy-start | bytes 4718596
  14.9 6.1 %copy-start.6 = (s32[1,8,12]{2,1,0:T(8,128)S(1)}, s32[1,8,12]{2,1,0:T(8,128)}, u32[]{:S(2)}) copy-start(s32[1,8,12]{2,1,0:T(8,128)} %param.7) | copy-start | bytes 1156
  16.8 9.2 %collective-permute-start.8 = (bf16[4,64,512]{2,1,0:T(8,128)(2,1)S(1)}, bf16[4,64,512]{2,1,0:T(8,128)(2,1)S(1)}, u32[]{:S(2)}, u32[]{:S(2)}) collective-permute-start(bf16[4,64,512]{2,1,0:T(8,128)(2,1)S(1)} %get-tuple-element.68.refs_4_.refs_0_), channel_id=1, source_target_pairs={{0,1},{1,0},{2,3},{3,2},{4,5},{5,4},{6,7},{7,6},{8,9},{9,8},{10,11... | collective-permute-start | bytes 786440 | tf_op jit(solution)/shard_map/ppermute | solution.py:569
  17.4 10.6 %collective-permute-start.9 = (bf16[4,64,512]{2,1,0:T(8,128)(2,1)S(1)}, bf16[4,64,512]{2,1,0:T(8,128)(2,1)S(1)}, u32[]{:S(2)}, u32[]{:S(2)}) collective-permute-start(bf16[4,64,512]{2,1,0:T(8,128)(2,1)S(1)} %get-tuple-element.69.refs_6_.refs_2_), channel_id=1, source_target_pairs={{0,2},{1,3},{2,0},{3,1},{4,6},{5,7},{6,4},{7,5},{8,10},{9,11},{10,... | collective-permute-start | bytes 786440 | tf_op jit(solution)/shard_map/ppermute | solution.py:569
  19.4 14.2 %collective-permute-start.3 = (bf16[2,4,64,256]{3,2,1,0:T(8,128)(2,1)S(1)}, bf16[2,4,64,256]{3,2,1,0:T(8,128)(2,1)S(1)}, u32[]{:S(2)}, u32[]{:S(2)}) collective-permute-start(bf16[2,4,64,256]{3,2,1,0:T(8,128)(2,1)S(1)} %get-tuple-element.59), channel_id=1, source_target_pairs={{0,2},{1,3},{2,0},{3,1},{4,6},{5,7},{6,4},{7,5},{8,10},{9,11},{10,... | collective-permute-start | bytes 786440 | tf_op jit(solution)/shard_map/ppermute | solution.py:569
  19.5 14.1 %collective-permute-start.4 = (bf16[2,4,64,256]{3,2,1,0:T(8,128)(2,1)S(1)}, bf16[2,4,64,256]{3,2,1,0:T(8,128)(2,1)S(1)}, u32[]{:S(2)}, u32[]{:S(2)}) collective-permute-start(bf16[2,4,64,256]{3,2,1,0:T(8,128)(2,1)S(1)} %get-tuple-element.60), channel_id=1, source_target_pairs={{0,1},{1,0},{2,3},{3,2},{4,5},{5,4},{6,7},{7,6},{8,9},{9,8},{10,11... | collective-permute-start | bytes 786440 | tf_op jit(solution)/shard_map/ppermute | solution.py:569
  21.0 7.0 %copy-start.5 = (bf16[4,64,512]{2,1,0:T(8,128)(2,1)S(1)}, bf16[4,64,512]{2,1,0:T(8,128)(2,1)}, u32[]{:S(2)}) copy-start(bf16[4,64,512]{2,1,0:T(8,128)(2,1)} %copy-done.4) | copy-start | bytes 786436
  29.7 21.0 %collective-permute-start.12 = (bf16[2,4,64,512]{3,2,1,0:T(8,128)(2,1)S(1)}, bf16[2,4,64,512]{3,2,1,0:T(8,128)(2,1)S(1)}, u32[]{:S(2)}, u32[]{:S(2)}) collective-permute-start(bf16[2,4,64,512]{3,2,1,0:T(8,128)(2,1)S(1)} %get-tuple-element.70), channel_id=1, source_target_pairs={{0,2},{1,3},{2,0},{3,1},{4,6},{5,7},{6,4},{7,5},{8,10},{9,11},{10,... | collective-permute-start | bytes 1572872 | tf_op jit(solution)/shard_map/ppermute | solution.py:569
  30.4 20.3 %collective-permute-start.13 = (bf16[2,4,64,512]{3,2,1,0:T(8,128)(2,1)S(1)}, bf16[2,4,64,512]{3,2,1,0:T(8,128)(2,1)S(1)}, u32[]{:S(2)}, u32[]{:S(2)}) collective-permute-start(bf16[2,4,64,512]{3,2,1,0:T(8,128)(2,1)S(1)} %get-tuple-element.76), channel_id=1, source_target_pairs={{0,1},{1,0},{2,3},{3,2},{4,5},{5,4},{6,7},{7,6},{8,9},{9,8},{10,11... | collective-permute-start | bytes 1572872 | tf_op jit(solution)/shard_map/ppermute | solution.py:569
  35.1 10.4 %collective-permute-start.10 = (s16[144,768]{1,0:T(8,128)(2,1)S(1)}, s16[144,768]{1,0:T(8,128)(2,1)S(1)}, u32[]{:S(2)}, u32[]{:S(2)}) collective-permute-start(s16[144,768]{1,0:T(8,128)(2,1)S(1)} %get-tuple-element.73), channel_id=1, source_target_pairs={{0,8},{8,0},{16,24},{24,16},{1,9},{9,1},{17,25},{25,17},{2,10},{10... | collective-permute-start | bytes 663560 | tf_op jit(solution)/shard_map/ppermute | solution.py:556
  40.9 18.0 %collective-permute-start.17 = (bf16[2,4,64,512]{3,2,1,0:T(8,128)(2,1)S(1)}, bf16[2,4,64,512]{3,2,1,0:T(8,128)(2,1)S(1)}, u32[]{:S(2)}, u32[]{:S(2)}) collective-permute-start(bf16[2,4,64,512]{3,2,1,0:T(8,128)(2,1)S(1)} %get-tuple-element.88), channel_id=1, source_target_pairs={{0,2},{1,3},{2,0},{3,1},{4,6},{5,7},{6,4},{7,5},{8,10},{9,11},{10,... | collective-permute-start | bytes 1572872 | tf_op jit(solution)/shard_map/ppermute | solution.py:569
  41.8 19.3 %collective-permute-start.18 = (bf16[2,4,64,512]{3,2,1,0:T(8,128)(2,1)S(1)}, bf16[2,4,64,512]{3,2,1,0:T(8,128)(2,1)S(1)}, u32[]{:S(2)}, u32[]{:S(2)}) collective-permute-start(bf16[2,4,64,512]{3,2,1,0:T(8,128)(2,1)S(1)} %get-tuple-element.89), channel_id=1, source_target_pairs={{0,1},{1,0},{2,3},{3,2},{4,5},{5,4},{6,7},{7,6},{8,9},{9,8},{10,11... | collective-permute-start | bytes 1572872 | tf_op jit(solution)/shard_map/ppermute | solution.py:569
  46.2 10.3 %collective-permute-start.11 = (s16[144,768]{1,0:T(8,128)(2,1)S(1)}, s16[144,768]{1,0:T(8,128)(2,1)S(1)}, u32[]{:S(2)}, u32[]{:S(2)}) collective-permute-start(s16[144,768]{1,0:T(8,128)(2,1)S(1)} %get-tuple-element.75), channel_id=1, source_target_pairs={{1,17},{2,18},{4,20},{7,23},{9,25},{10,26},{12,28},{15,31},{16,0},... | collective-permute-start | bytes 663560 | tf_op jit(solution)/shard_map/ppermute | solution.py:566
  52.8 2.6 %collective-permute-start.14 = (s16[144,384]{1,0:T(8,128)(2,1)S(1)}, s16[144,384]{1,0:T(8,128)(2,1)S(1)}, u32[]{:S(2)}, u32[]{:S(2)}) collective-permute-start(s16[144,384]{1,0:T(8,128)(2,1)S(1)} %get-tuple-element.83), channel_id=1, source_target_pairs={{0,4},{1,5},{6,2},{7,3},{8,12},{9,13},{14,10},{15,11},{16,20},{17,... | collective-permute-start | bytes 331784 | tf_op jit(solution)/shard_map/ppermute | solution.py:553
  56.0 7.9 %collective-permute-start.23 = (s16[144,384]{1,0:T(8,128)(2,1)S(1)}, s16[144,384]{1,0:T(8,128)(2,1)S(1)}, u32[]{:S(2)}, u32[]{:S(2)}) collective-permute-start(s16[144,384]{1,0:T(8,128)(2,1)S(1)} %pick.1.mine_ref), channel_id=1, source_target_pairs={{0,8},{8,0},{16,24},{24,16},{1,9},{9,1},{17,25},{25,17},{2,10},{10... | collective-permute-start | bytes 331784 | tf_op jit(solution)/shard_map/ppermute | solution.py:556
  56.5 16.8 %collective-permute-start.15 = (s16[272,768]{1,0:T(8,128)(2,1)S(1)}, s16[272,768]{1,0:T(8,128)(2,1)S(1)}, u32[]{:S(2)}, u32[]{:S(2)}) collective-permute-start(s16[272,768]{1,0:T(8,128)(2,1)S(1)} %get-tuple-element.84), channel_id=1, source_target_pairs={{0,8},{8,0},{16,24},{24,16},{1,9},{9,1},{17,25},{25,17},{2,10},{10... | collective-permute-start | bytes 1253384 | tf_op jit(solution)/shard_map/ppermute | solution.py:556
  58.8 17.0 %collective-permute-start.19 = (bf16[2,4,64,256]{3,2,1,0:T(8,128)(2,1)S(1)}, bf16[2,4,64,256]{3,2,1,0:T(8,128)(2,1)S(1)}, u32[]{:S(2)}, u32[]{:S(2)}) collective-permute-start(bf16[2,4,64,256]{3,2,1,0:T(8,128)(2,1)S(1)} %get-tuple-element.93), channel_id=1, source_target_pairs={{0,2},{1,3},{2,0},{3,1},{4,6},{5,7},{6,4},{7,5},{8,10},{9,11},{10,... | collective-permute-start | bytes 786440 | tf_op jit(solution)/shard_map/ppermute | solution.py:569
  58.9 16.9 %collective-permute-start.20 = (bf16[2,4,64,256]{3,2,1,0:T(8,128)(2,1)S(1)}, bf16[2,4,64,256]{3,2,1,0:T(8,128)(2,1)S(1)}, u32[]{:S(2)}, u32[]{:S(2)}) collective-permute-start(bf16[2,4,64,256]{3,2,1,0:T(8,128)(2,1)S(1)} %get-tuple-element.94), channel_id=1, source_target_pairs={{0,1},{1,0},{2,3},{3,2},{4,5},{5,4},{6,7},{7,6},{8,9},{9,8},{10,11... | collective-permute-start | bytes 786440 | tf_op jit(solution)/shard_map/ppermute | solution.py:569
  63.3 21.9 %collective-permute-start.21 = (s16[272,768]{1,0:T(8,128)(2,1)S(1)}, s16[272,768]{1,0:T(8,128)(2,1)S(1)}, u32[]{:S(2)}, u32[]{:S(2)}) collective-permute-start(s16[272,768]{1,0:T(8,128)(2,1)S(1)} %get-tuple-element.98), channel_id=1, source_target_pairs={{0,8},{8,0},{16,24},{24,16},{1,9},{9,1},{17,25},{25,17},{2,10},{10... | collective-permute-start | bytes 1253384 | tf_op jit(solution)/shard_map/ppermute | solution.py:556
  63.8 16.4 %slice-start = ((s8[4718592]{0:T(1024)(128)(4,1)}), s8[4194304]{0:T(1024)(128)(4,1)S(1)}, s32[]{:S(2)}) async-start(s8[4718592]{0:T(1024)(128)(4,1)} %bitcast.14), calls=%async_computation | async-start | bytes 8388608
  63.9 16.3 %collective-permute-start.24 = (s16[144,384]{1,0:T(8,128)(2,1)S(1)}, s16[144,384]{1,0:T(8,128)(2,1)S(1)}, u32[]{:S(2)}, u32[]{:S(2)}) collective-permute-start(s16[144,384]{1,0:T(8,128)(2,1)S(1)} %add_coded.1.one_ref), channel_id=1, source_target_pairs={{0,16},{8,24},{16,0},{24,8},{1,17},{9,25},{17,1},{25,9},{2,18},{10... | collective-permute-start | bytes 331784 | tf_op jit(solution)/shard_map/ppermute | solution.py:556
  74.1 29.6 %collective-permute-start.16 = (s16[272,768]{1,0:T(8,128)(2,1)S(1)}, s16[272,768]{1,0:T(8,128)(2,1)S(1)}, u32[]{:S(2)}, u32[]{:S(2)}) collective-permute-start(s16[272,768]{1,0:T(8,128)(2,1)S(1)} %get-tuple-element.86), channel_id=1, source_target_pairs={{1,17},{2,18},{4,20},{7,23},{9,25},{10,26},{12,28},{15,31},{16,0},... | collective-permute-start | bytes 1253384 | tf_op jit(solution)/shard_map/ppermute | solution.py:566
  75.8 4.4 %slice-start.1 = ((s8[4718592]{0:T(1024)(128)(4,1)}), s8[524288]{0:T(1024)(128)(4,1)S(1)}, s32[]{:S(2)}) async-start(s8[4718592]{0:T(1024)(128)(4,1)} %bitcast.14), calls=%async_computation.1 | async-start | bytes 1048576
  77.3 13.5 %collective-permute-start.25 = (s16[144,768]{1,0:T(8,128)(2,1)S(1)}, s16[144,768]{1,0:T(8,128)(2,1)S(1)}, u32[]{:S(2)}, u32[]{:S(2)}) collective-permute-start(s16[144,768]{1,0:T(8,128)(2,1)S(1)} %get-tuple-element.101), channel_id=1, source_target_pairs={{0,8},{8,0},{16,24},{24,16},{1,9},{9,1},{17,25},{25,17},{2,10},{10... | collective-permute-start | bytes 663560 | tf_op jit(solution)/shard_map/ppermute | solution.py:556
  86.0 17.7 %collective-permute-start.22 = (s16[272,768]{1,0:T(8,128)(2,1)S(1)}, s16[272,768]{1,0:T(8,128)(2,1)S(1)}, u32[]{:S(2)}, u32[]{:S(2)}) collective-permute-start(s16[272,768]{1,0:T(8,128)(2,1)S(1)} %get-tuple-element.100), channel_id=1, source_target_pairs={{0,16},{3,19},{5,21},{6,22},{8,24},{11,27},{13,29},{14,30},{17,1},... | collective-permute-start | bytes 1253384 | tf_op jit(solution)/shard_map/ppermute | solution.py:566
  91.5 14.6 %collective-permute-start.26 = (s16[144,768]{1,0:T(8,128)(2,1)S(1)}, s16[144,768]{1,0:T(8,128)(2,1)S(1)}, u32[]{:S(2)}, u32[]{:S(2)}) collective-permute-start(s16[144,768]{1,0:T(8,128)(2,1)S(1)} %get-tuple-element.106), channel_id=1, source_target_pairs={{0,16},{3,19},{5,21},{6,22},{8,24},{11,27},{13,29},{14,30},{17,1},... | collective-permute-start | bytes 663560 | tf_op jit(solution)/shard_map/ppermute | solution.py:566
  96.8 2.9 %collective-permute-start.27 = (f32[3,128,128]{2,1,0:T(8,128)S(1)}, f32[3,128,128]{2,1,0:T(8,128)S(1)}, u32[]{:S(2)}, u32[]{:S(2)}) collective-permute-start(f32[3,128,128]{2,1,0:T(8,128)S(1)} %factor.5.refs_8_), channel_id=1, source_target_pairs={{0,4},{4,0},{1,5},{5,1},{2,6},{6,2},{3,7},{7,3},{8,12},{12,8},{9,1... | collective-permute-start | bytes 589832 | tf_op jit(solution)/shard_map/ppermute | solution.py:625

commit v13 on v9

--- a/solution.py
+++ b/solution.py
@@ -18,7 +18,7 @@
 HALF_STEPS = 48
 LU = 10
 NEAR = 10
-FAR = 10
+FAR = 4
 
 
 def cost(micros):
@@ -612,9 +612,9 @@
     known = []
     mine = pick(where, diag[0], to_other_core(diag[1]))
     got0 = far_layers(sent0, chunks[0])
-    near = add_coded(after(mine, got0), over_layers(mine, 1))
+    near = add_coded(mine, over_layers(mine, 1))
     far = over_layers(near, 2)
-    own = pivots(where, anc, given, near, far)
+    own = pivots(where, anc, given, near, after(far, got0))
     kept2, coded2 = far_part(2, mine, sent0)
     sum1, sent1 = halve(where, kept1, over_layers(coded1, 1), chunks[1])
     half_lu = factor(after(own, sent1, coded2), 0, HALF_STEPS)

time: 107 us -> 106 us (level)
  starting transfers between devices: 35.9 us -> 31.7 us
  waiting for transfers between devices: 27.4 us -> 31.2 us
    ppermute x5, waiting for transfers between devices: 11.2 us -> 14.6 us  [over_layers(): return lax.ppermute(value, 'layer', xor_perm(layers, bit))]
    ppermute x5, starting transfers between devices: 9.07 us -> 6.4 us  [over_layers(): return lax.ppermute(value, 'layer', xor_perm(layers, bit))]
    ppermute x1, starting transfers between devices: 3.45 us -> 1.4 us  [planned(): lu_got = lax.ppermute(lu, 'row', xor_perm(rows, 1))]
  transfers between devices with their start and end apart: 22 -> 22, of which waited for: 13 -> 12; matrix products, arithmetic and copies ran while one was open for 0% -> 0% of each run, Pallas kernels for 32% -> 32%
where the time goes in v13:
time: 106 us; the launch traced here: 105 us
  Pallas kernels  35.2 us (33%)
  starting transfers between devices  31.7 us (30%)
  waiting for transfers between devices  31.2 us (29%)
  local copies, waits for them, and re-layouts  5.34 us (5%)
  between operations  1.07 us (1%)
    ppermute x5, waiting for transfers between devices, over_layers(): return lax.ppermute(value, 'layer', xor_perm(layers, bit))  14.6 us
    ppermute x10, starting transfers between devices, over(): return lax.ppermute(value, 'col', xor_perm(cols, bit))  13.5 us
    pallas_call x2, Pallas kernels, factor(): pl.pallas_call(functools.partial(lu_kernel, begin, end), out_shape=jax.Sh...  11.4 us
    ppermute x10, waiting for transfers between devices, over(): return lax.ppermute(value, 'col', xor_perm(cols, bit))  10.1 us
    ppermute x3, starting transfers between devices, far_layers(): return lax.ppermute(value, everyone, perm)  7.74 us
    ppermute x5, starting transfers between devices, over_layers(): return lax.ppermute(value, 'layer', xor_perm(layers, bit))  6.4 us
    pallas_call x3, Pallas kernels, far_update(): pl.pallas_call(functools.partial(far_kernel, chunk, blocks, len(earlier))...  6.35 us
    pallas_call x3, Pallas kernels, near_update(): pl.pallas_call(functools.partial(near_kernel, chunk, blocks), out_shape=j...  5.49 us
  transfers between devices with their start and end apart: 22, of which 12 were waited for; matrix products, arithmetic and copies ran while one was open for 0% of the time, Pallas kernels for 32%

profile of v13, /device:TPU:2, one launch (start us, length us, event | category | flops | bytes accessed | tf_op | source)
XLA Modules:
  0.0 104.6 jit_solution(3267055363787303092)
XLA Ops:
  0.7 1.4 %copy-done.1 = bf16[1,8,1536,64]{2,3,1,0:T(8,128)(2,1)S(1)} copy-done((bf16[1,8,1536,64]{2,3,1,0:T(8,128)(2,1)S(1)}, bf16[1,8,1536,64]{2,3,1,0:T(8,128)(2,1)}, u32[]{:S(2)}) %copy-start.1) | copy-done | bytes 1572888
  2.4 2.0 %collective-permute-start.3 = (bf16[4,64,1024]{2,1,0:T(8,128)(2,1)S(1)}, bf16[4,64,1024]{2,1,0:T(8,128)(2,1)S(1)}, u32[]{:S(2)}, u32[]{:S(2)}) collective-permute-start(bf16[4,64,1024]{2,1,0:T(8,128)(2,1)S(1)} %get-tuple-element.48.refs_2_), channel_id=1, source_target_pairs={{0,2},{1,3},{2,0},{3,1},{4,6},{5,7},{6,4},{7,5},{8,10},{9,11},{10,... | collective-permute-start | bytes 1572872 | tf_op jit(solution)/shard_map/ppermute | solution.py:582
  4.7 1.6 %collective-permute-start.6 = (bf16[4,64,512]{2,1,0:T(8,128)(2,1)S(1)}, bf16[4,64,512]{2,1,0:T(8,128)(2,1)S(1)}, u32[]{:S(2)}, u32[]{:S(2)}) collective-permute-start(bf16[4,64,512]{2,1,0:T(8,128)(2,1)S(1)} %get-tuple-element.44.refs_4_), channel_id=1, source_target_pairs={{0,1},{1,0},{2,3},{3,2},{4,5},{5,4},{6,7},{7,6},{8,9},{9,8},{10,11... | collective-permute-start | bytes 786440 | tf_op jit(solution)/shard_map/ppermute | solution.py:582
  6.8 2.3 %copy-done = f32[1536,768]{1,0:T(8,128)S(1)} copy-done((f32[1536,768]{1,0:T(8,128)S(1)}, f32[1536,768]{1,0:T(8,128)}, u32[]{:S(2)}) %copy-start) | copy-done | bytes 4718616
  9.2 0.6 later_blocks.1
  9.8 1.3 %collective-permute-start = (f32[3,128,128]{2,1,0:T(8,128)S(1)}, f32[3,128,128]{2,1,0:T(8,128)S(1)}, u32[]{:S(2)}, u32[]{:S(2)}) collective-permute-start(f32[3,128,128]{2,1,0:T(8,128)S(1)} %later_blocks.1), channel_id=1, source_target_pairs={{0,4},{1,5},{6,2},{7,3},{8,12},{9,13},{14,10},{15,11},{16,20},{17,... | collective-permute-start | bytes 589832 | tf_op jit(solution)/shard_map/ppermute | solution.py:566
  11.2 1.4 %copy-done.2 = bf16[1,8,128,768]{3,2,1,0:T(8,128)(2,1)S(1)} copy-done((bf16[1,8,128,768]{3,2,1,0:T(8,128)(2,1)S(1)}, bf16[1,8,128,768]{3,2,1,0:T(8,128)(2,1)}, u32[]{:S(2)}) %copy-start.2) | copy-done | bytes 1572888
  12.6 2.2 %masked_right.1 = (bf16[8,128,768]{2,1,0:T(8,128)(2,1)S(1)}, bf16[8,128,768]{2,1,0:T(8,128)(2,1)S(1)}) custom-call(s32[8]{0:T(128)S(1)} %stack.35.where_ref, s32[8,6]{1,0:T(8,128)S(1)} %bitcast.20, bf16[8,128,768]{2,1,0:T(8,128)(2,1)S(1)} %bitcast.19, bf16[8,128,768]{2,1,0:T(8,128)(2,1)} %collective-permute-done.1.uo_ref), custom_call_target="tpu_custom_call" | custom-call | flops 1000 | bytes 1000 | tf_op jit(solution)/shard_map/masked_right/pallas_call | solution.py:226
  14.8 2.4 %collective-permute-done.2.refs_1_ = bf16[4,64,1024]{2,1,0:T(8,128)(2,1)S(1)} collective-permute-done((bf16[4,64,1024]{2,1,0:T(8,128)(2,1)S(1)}, bf16[4,64,1024]{2,1,0:T(8,128)(2,1)S(1)}, u32[]{:S(2)}, u32[]{:S(2)}) %collective-permute-start.2) | collective-permute-done | bytes 524320 | tf_op jit(solution)/shard_map/ppermute | solution.py:582
  17.2 1.0 split.3
  18.2 2.1 %collective-permute-start.4 = (bf16[2,4,64,512]{3,2,1,0:T(8,128)(2,1)S(1)}, bf16[2,4,64,512]{3,2,1,0:T(8,128)(2,1)S(1)}, u32[]{:S(2)}, u32[]{:S(2)}) collective-permute-start(bf16[2,4,64,512]{3,2,1,0:T(8,128)(2,1)S(1)} %get-tuple-element.49), channel_id=1, source_target_pairs={{0,2},{1,3},{2,0},{3,1},{4,6},{5,7},{6,4},{7,5},{8,10},{9,11},{10,... | collective-permute-start | bytes 1572872 | tf_op jit(solution)/shard_map/ppermute | solution.py:582
  20.3 1.5 %collective-permute-start.5 = (bf16[2,4,64,512]{3,2,1,0:T(8,128)(2,1)S(1)}, bf16[2,4,64,512]{3,2,1,0:T(8,128)(2,1)S(1)}, u32[]{:S(2)}, u32[]{:S(2)}) collective-permute-start(bf16[2,4,64,512]{3,2,1,0:T(8,128)(2,1)S(1)} %get-tuple-element.50), channel_id=1, source_target_pairs={{0,1},{1,0},{2,3},{3,2},{4,5},{5,4},{6,7},{7,6},{8,9},{9,8},{10,11... | collective-permute-start | bytes 1572872 | tf_op jit(solution)/shard_map/ppermute | solution.py:582
  21.8 1.0 collective-permute-done.6.refs_5_
  22.8 1.0 split.4
  23.8 2.1 %collective-permute-start.8 = (bf16[2,4,64,512]{3,2,1,0:T(8,128)(2,1)S(1)}, bf16[2,4,64,512]{3,2,1,0:T(8,128)(2,1)S(1)}, u32[]{:S(2)}, u32[]{:S(2)}) collective-permute-start(bf16[2,4,64,512]{3,2,1,0:T(8,128)(2,1)S(1)} %get-tuple-element.55), channel_id=1, source_target_pairs={{0,2},{1,3},{2,0},{3,1},{4,6},{5,7},{6,4},{7,5},{8,10},{9,11},{10,... | collective-permute-start | bytes 1572872 | tf_op jit(solution)/shard_map/ppermute | solution.py:582
  25.9 1.5 %collective-permute-start.9 = (bf16[2,4,64,512]{3,2,1,0:T(8,128)(2,1)S(1)}, bf16[2,4,64,512]{3,2,1,0:T(8,128)(2,1)S(1)}, u32[]{:S(2)}, u32[]{:S(2)}) collective-permute-start(bf16[2,4,64,512]{3,2,1,0:T(8,128)(2,1)S(1)} %get-tuple-element.56), channel_id=1, source_target_pairs={{0,1},{1,0},{2,3},{3,2},{4,5},{5,4},{6,7},{7,6},{8,9},{9,8},{10,11... | collective-permute-start | bytes 1572872 | tf_op jit(solution)/shard_map/ppermute | solution.py:582
  27.4 1.0 split.5
  28.9 1.8 %near_update.5.refs_1_ = f32[4,128,768]{2,1,0:T(8,128)S(1)} custom-call(s32[8]{0:T(128)S(1)} %stack.35.where_ref, s32[8,12]{1,0:T(8,128)S(1)} %bitcast.21, bf16[4,64,1024]{2,1,0:T(8,128)(2,1)S(1)} %get-tuple-element.42.refs_0_, bf16[4,64,1024]{2,1,0:T(8,128)(2,1)S(1)} %collective-permute-done.2.refs_1_, bf16[4,64,1024]{2,1,0:T(8,128)(2,1)S(1)} %get-tuple-element.48.refs_2_, ...), custom_call_target="tpu_custom_call" | custom-call | flops 10000001024 | bytes 1000 | tf_op jit(solution)/shard_map/near_update/pallas_call | solution.py:273
  30.7 1.8 %near_update.4.refs_1_ = f32[4,128,768]{2,1,0:T(8,128)S(1)} custom-call(s32[8]{0:T(128)S(1)} %stack.35.where_ref, s32[8,12]{1,0:T(8,128)S(1)} %bitcast.22, bf16[4,64,1024]{2,1,0:T(8,128)(2,1)S(1)} %get-tuple-element.42.refs_0_, bf16[4,64,1024]{2,1,0:T(8,128)(2,1)S(1)} %collective-permute-done.2.refs_1_, bf16[4,64,1024]{2,1,0:T(8,128)(2,1)S(1)} %get-tuple-element.48.refs_2_, ...), custom_call_target="tpu_custom_call" | custom-call | flops 10000001024 | bytes 1000 | tf_op jit(solution)/shard_map/near_update/pallas_call | solution.py:273
  32.6 1.9 %near_update.3.refs_1_ = f32[4,128,768]{2,1,0:T(8,128)S(1)} custom-call(s32[8]{0:T(128)S(1)} %stack.35.where_ref, s32[8,12]{1,0:T(8,128)S(1)} %bitcast.23, bf16[4,64,1024]{2,1,0:T(8,128)(2,1)S(1)} %get-tuple-element.42.refs_0_, bf16[4,64,1024]{2,1,0:T(8,128)(2,1)S(1)} %collective-permute-done.2.refs_1_, bf16[4,64,1024]{2,1,0:T(8,128)(2,1)S(1)} %get-tuple-element.48.refs_2_, ...), custom_call_target="tpu_custom_call" | custom-call | flops 10000001024 | bytes 1000 | tf_op jit(solution)/shard_map/near_update/pallas_call | solution.py:273
  34.4 1.6 %collective-permute-start.15 = (bf16[2,4,64,512]{3,2,1,0:T(8,128)(2,1)S(1)}, bf16[2,4,64,512]{3,2,1,0:T(8,128)(2,1)S(1)}, u32[]{:S(2)}, u32[]{:S(2)}) collective-permute-start(bf16[2,4,64,512]{3,2,1,0:T(8,128)(2,1)S(1)} %get-tuple-element.70), channel_id=1, source_target_pairs={{0,1},{1,0},{2,3},{3,2},{4,5},{5,4},{6,7},{7,6},{8,9},{9,8},{10,11... | collective-permute-start | bytes 1572872 | tf_op jit(solution)/shard_map/ppermute | solution.py:582
  36.1 2.1 %far_update.3 = (f32[2,128,768]{2,1,0:T(8,128)S(1)}, s16[272,768]{1,0:T(8,128)(2,1)S(1)}, s16[144,384]{1,0:T(8,128)(2,1)S(1)}, s16[144,384]{1,0:T(8,128)(2,1)S(1)}) custom-call(s32[8]{0:T(128)S(1)} %stack.35.where_ref, s32[8,12]{1,0:T(8,128)S(1)} %bitcast.24, bf16[2,4,64,512]{3,2,1,0:T(8,128)(2,1)S(1)} %collective-permute-done.4.a_ref, ...), custom_call_target="tpu_custom_call" | custom-call | flops 4000001024 | bytes 1000 | tf_op jit(solution)/shard_map/far_update/pallas_call | solution.py:322
  38.2 1.7 %collective-permute-start.10 = (s16[272,768]{1,0:T(8,128)(2,1)S(1)}, s16[272,768]{1,0:T(8,128)(2,1)S(1)}, u32[]{:S(2)}, u32[]{:S(2)}) collective-permute-start(s16[272,768]{1,0:T(8,128)(2,1)S(1)} %get-tuple-element.62), channel_id=1, source_target_pairs={{0,8},{8,0},{16,24},{24,16},{1,9},{9,1},{17,25},{25,17},{2,10},{10... | collective-permute-start | bytes 1253384 | tf_op jit(solution)/shard_map/ppermute | solution.py:569
  39.8 5.5 %collective-permute-done.8.a_ref = bf16[2,4,64,512]{3,2,1,0:T(8,128)(2,1)S(1)} collective-permute-done((bf16[2,4,64,512]{3,2,1,0:T(8,128)(2,1)S(1)}, bf16[2,4,64,512]{3,2,1,0:T(8,128)(2,1)S(1)}, u32[]{:S(2)}, u32[]{:S(2)}) %collective-permute-start.8) | collective-permute-done | bytes 524320 | tf_op jit(solution)/shard_map/ppermute | solution.py:582
  45.3 1.1 %collective-permute-done.9.b_ref = bf16[2,4,64,512]{3,2,1,0:T(8,128)(2,1)S(1)} collective-permute-done((bf16[2,4,64,512]{3,2,1,0:T(8,128)(2,1)S(1)}, bf16[2,4,64,512]{3,2,1,0:T(8,128)(2,1)S(1)}, u32[]{:S(2)}, u32[]{:S(2)}) %collective-permute-start.9) | collective-permute-done | bytes 524320 | tf_op jit(solution)/shard_map/ppermute | solution.py:582
  46.4 2.1 %far_update.4 = (f32[2,128,768]{2,1,0:T(8,128)S(1)}, s16[272,768]{1,0:T(8,128)(2,1)S(1)}, s16[144,384]{1,0:T(8,128)(2,1)S(1)}, s16[144,384]{1,0:T(8,128)(2,1)S(1)}) custom-call(s32[8]{0:T(128)S(1)} %stack.35.where_ref, s32[8,12]{1,0:T(8,128)S(1)} %bitcast.25, bf16[2,4,64,512]{3,2,1,0:T(8,128)(2,1)S(1)} %collective-permute-done.8.a_ref, ...), custom_call_target="tpu_custom_call" | custom-call | flops 4000001024 | bytes 1000 | tf_op jit(solution)/shard_map/far_update/pallas_call | solution.py:322
  48.6 1.3 %collective-permute-start.16 = (s16[144,384]{1,0:T(8,128)(2,1)S(1)}, s16[144,384]{1,0:T(8,128)(2,1)S(1)}, u32[]{:S(2)}, u32[]{:S(2)}) collective-permute-start(s16[144,384]{1,0:T(8,128)(2,1)S(1)} %get-tuple-element.72), channel_id=1, source_target_pairs={{0,4},{1,5},{6,2},{7,3},{8,12},{9,13},{14,10},{15,11},{16,20},{17,... | collective-permute-start | bytes 331784 | tf_op jit(solution)/shard_map/ppermute | solution.py:566
  49.9 0.9 collective-permute-done.16.got_ref
  51.4 1.7 %collective-permute-start.17 = (s16[144,384]{1,0:T(8,128)(2,1)S(1)}, s16[144,384]{1,0:T(8,128)(2,1)S(1)}, u32[]{:S(2)}, u32[]{:S(2)}) collective-permute-start(s16[144,384]{1,0:T(8,128)(2,1)S(1)} %pick.1.mine_ref), channel_id=1, source_target_pairs={{0,8},{8,0},{16,24},{24,16},{1,9},{9,1},{17,25},{25,17},{2,10},{10... | collective-permute-start | bytes 331784 | tf_op jit(solution)/shard_map/ppermute | solution.py:569
  53.5 0.8 halve.3
  54.3 4.7 %collective-permute-start.11 = (s16[272,768]{1,0:T(8,128)(2,1)S(1)}, s16[272,768]{1,0:T(8,128)(2,1)S(1)}, u32[]{:S(2)}, u32[]{:S(2)}) collective-permute-start(s16[272,768]{1,0:T(8,128)(2,1)S(1)} %get-tuple-element.64), channel_id=1, source_target_pairs={{1,17},{2,18},{4,20},{7,23},{9,25},{10,26},{12,28},{15,31},{16,0},... | collective-permute-start | bytes 1253384 | tf_op jit(solution)/shard_map/ppermute | solution.py:579
  59.1 1.0 collective-permute-start.18
  60.1 2.1 %far_update.5 = (f32[2,128,768]{2,1,0:T(8,128)S(1)}, s16[272,768]{1,0:T(8,128)(2,1)S(1)}) custom-call(s32[8]{0:T(128)S(1)} %stack.35.where_ref, s32[8,12]{1,0:T(8,128)S(1)} %bitcast.26, bf16[2,4,64,512]{3,2,1,0:T(8,128)(2,1)S(1)} %collective-permute-done.14.a_ref, bf16[2,4,64,512]{3,2,1,0:T(8,128)(2,1)S(1)} %collective-permute-done.15.b_ref, ...), custom_call_target="tpu_custom_call" | custom-call | flops 4000001024 | bytes 1000 | tf_op jit(solution)/shard_map/far_update/pallas_call | solution.py:322
  62.2 1.7 %collective-permute-start.19 = (s16[272,768]{1,0:T(8,128)(2,1)S(1)}, s16[272,768]{1,0:T(8,128)(2,1)S(1)}, u32[]{:S(2)}, u32[]{:S(2)}) collective-permute-start(s16[272,768]{1,0:T(8,128)(2,1)S(1)} %get-tuple-element.76), channel_id=1, source_target_pairs={{0,8},{8,0},{16,24},{24,16},{1,9},{9,1},{17,25},{25,17},{2,10},{10... | collective-permute-start | bytes 1253384 | tf_op jit(solution)/shard_map/ppermute | solution.py:569
  63.9 9.2 %collective-permute-done.12.got_ref = s16[272,768]{1,0:T(8,128)(2,1)S(1)} collective-permute-done((s16[272,768]{1,0:T(8,128)(2,1)S(1)}, s16[272,768]{1,0:T(8,128)(2,1)S(1)}, u32[]{:S(2)}, u32[]{:S(2)}) %collective-permute-start.12) | collective-permute-done | bytes 417824 | tf_op jit(solution)/shard_map/ppermute | solution.py:569
  73.1 0.7 halve.4
  73.9 1.8 %collective-permute-start.13 = (s16[144,768]{1,0:T(8,128)(2,1)S(1)}, s16[144,768]{1,0:T(8,128)(2,1)S(1)}, u32[]{:S(2)}, u32[]{:S(2)}) collective-permute-start(s16[144,768]{1,0:T(8,128)(2,1)S(1)} %get-tuple-element.67), channel_id=1, source_target_pairs={{0,16},{1,17},{2,18},{3,19},{4,20},{5,21},{6,22},{7,23},{8,24},{9,... | collective-permute-start | bytes 663560 | tf_op jit(solution)/shard_map/ppermute | solution.py:579
  75.6 1.1 %collective-permute-done.18.two_ref = s16[144,384]{1,0:T(8,128)(2,1)S(1)} collective-permute-done((s16[144,384]{1,0:T(8,128)(2,1)S(1)}, s16[144,384]{1,0:T(8,128)(2,1)S(1)}, u32[]{:S(2)}, u32[]{:S(2)}) %collective-permute-start.18) | collective-permute-done | bytes 110624 | tf_op jit(solution)/shard_map/ppermute | solution.py:569
  76.8 0.7 pivots.1.in_ref
  77.4 4.6 %factor.2.in_ref = f32[3,128,128]{2,1,0:T(8,128)S(1)} custom-call(f32[3,128,128]{2,1,0:T(8,128)S(1)} %pivots.1.in_ref), custom_call_target="tpu_custom_call" | custom-call | flops 10000001024 | bytes 1000 | tf_op jit(solution)/shard_map/factor/pallas_call | solution.py:82
  82.0 4.2 %collective-permute-done.19.got_ref = s16[272,768]{1,0:T(8,128)(2,1)S(1)} collective-permute-done((s16[272,768]{1,0:T(8,128)(2,1)S(1)}, s16[272,768]{1,0:T(8,128)(2,1)S(1)}, u32[]{:S(2)}, u32[]{:S(2)}) %collective-permute-start.19) | collective-permute-done | bytes 417824 | tf_op jit(solution)/shard_map/ppermute | solution.py:569
  86.2 0.8 halve.5
  87.0 1.3 %collective-permute-start.20 = (s16[272,768]{1,0:T(8,128)(2,1)S(1)}, s16[272,768]{1,0:T(8,128)(2,1)S(1)}, u32[]{:S(2)}, u32[]{:S(2)}) collective-permute-start(s16[272,768]{1,0:T(8,128)(2,1)S(1)} %get-tuple-element.80), channel_id=1, source_target_pairs={{0,16},{3,19},{5,21},{6,22},{8,24},{11,27},{13,29},{14,30},{17,1},... | collective-permute-start | bytes 1253384 | tf_op jit(solution)/shard_map/ppermute | solution.py:579
  88.3 6.8 %factor.3.refs_6_ = f32[3,128,128]{2,1,0:T(8,128)S(1)} custom-call(f32[3,128,128]{2,1,0:T(8,128)S(1)} %factor.2.in_ref), custom_call_target="tpu_custom_call" | custom-call | flops 10000001024 | bytes 1000 | tf_op jit(solution)/shard_map/factor/pallas_call | solution.py:82
  95.2 1.4 %collective-permute-start.21 = (f32[3,128,128]{2,1,0:T(8,128)S(1)}, f32[3,128,128]{2,1,0:T(8,128)S(1)}, u32[]{:S(2)}, u32[]{:S(2)}) collective-permute-start(f32[3,128,128]{2,1,0:T(8,128)S(1)} %factor.3.refs_6_), channel_id=1, source_target_pairs={{0,4},{4,0},{1,5},{5,1},{2,6},{6,2},{3,7},{7,3},{8,12},{12,8},{9,1... | collective-permute-start | bytes 589832 | tf_op jit(solution)/shard_map/ppermute | solution.py:623
  96.6 1.1 %collective-permute-done.21.refs_7_ = f32[3,128,128]{2,1,0:T(8,128)S(1)} collective-permute-done((f32[3,128,128]{2,1,0:T(8,128)S(1)}, f32[3,128,128]{2,1,0:T(8,128)S(1)}, u32[]{:S(2)}, u32[]{:S(2)}) %collective-permute-start.21) | collective-permute-done | bytes 196640 | tf_op jit(solution)/shard_map/ppermute | solution.py:623
  97.6 4.6 %collective-permute-done.20.refs_5_ = s16[272,768]{1,0:T(8,128)(2,1)S(1)} collective-permute-done((s16[272,768]{1,0:T(8,128)(2,1)S(1)}, s16[272,768]{1,0:T(8,128)(2,1)S(1)}, u32[]{:S(2)}, u32[]{:S(2)}) %collective-permute-start.20) | collective-permute-done | bytes 417824 | tf_op jit(solution)/shard_map/ppermute | solution.py:579
  102.2 2.2 %combine.1 = (f32[384,768]{1,0:T(8,128)}, f32[6,128,128]{2,1,0:T(8,128)}) custom-call(s32[8]{0:T(128)S(1)} %stack.35.where_ref, f32[1536,768]{1,0:T(8,128)S(1)} %bitcast.15, f32[2,128,768]{2,1,0:T(8,128)S(1)} %get-tuple-element.63.refs_0_, s16[272,768]{1,0:T(8,128)(2,1)S(1)} %collective-permute-done.11.refs_1_, ...), custom_call_target="tpu_custom_call" | custom-call | flops 1000 | bytes 1000 | tf_op jit(solution)/shard_map/combine/pallas_call | solution.py:457
  (35 shorter events, 3.1 us)
Async XLA Ops:
  0.6 9.1 %collective-permute-start.1 = (bf16[8,128,768]{2,1,0:T(8,128)(2,1)}, bf16[8,128,768]{2,1,0:T(8,128)(2,1)}, u32[]{:S(2)}, u32[]{:S(2)}) collective-permute-start(bf16[8,128,768]{2,1,0:T(8,128)(2,1)} %bitcast.18), channel_id=1, source_target_pairs={{0,4},{4,0},{1,5},{5,1},{2,6},{6,2},{3,7},{7,3},{8,12},{12,8},{9,1... | collective-permute-start | bytes 4718600 | tf_op jit(solution)/shard_map/ppermute | solution.py:587
  0.7 1.4 %copy-start.1 = (bf16[1,8,1536,64]{2,3,1,0:T(8,128)(2,1)S(1)}, bf16[1,8,1536,64]{2,3,1,0:T(8,128)(2,1)}, u32[]{:S(2)}) copy-start(bf16[1,8,1536,64]{2,3,1,0:T(8,128)(2,1)} %param.5) | copy-start | bytes 4718596
  2.4 14.8 %collective-permute-start.2 = (bf16[4,64,1024]{2,1,0:T(8,128)(2,1)S(1)}, bf16[4,64,1024]{2,1,0:T(8,128)(2,1)S(1)}, u32[]{:S(2)}, u32[]{:S(2)}) collective-permute-start(bf16[4,64,1024]{2,1,0:T(8,128)(2,1)S(1)} %get-tuple-element.42.refs_0_), channel_id=1, source_target_pairs={{0,1},{1,0},{2,3},{3,2},{4,5},{5,4},{6,7},{7,6},{8,9},{9,8},{10,11... | collective-permute-start | bytes 1572872 | tf_op jit(solution)/shard_map/ppermute | solution.py:582
  2.4 14.8 %collective-permute-start.3 = (bf16[4,64,1024]{2,1,0:T(8,128)(2,1)S(1)}, bf16[4,64,1024]{2,1,0:T(8,128)(2,1)S(1)}, u32[]{:S(2)}, u32[]{:S(2)}) collective-permute-start(bf16[4,64,1024]{2,1,0:T(8,128)(2,1)S(1)} %get-tuple-element.48.refs_2_), channel_id=1, source_target_pairs={{0,2},{1,3},{2,0},{3,1},{4,6},{5,7},{6,4},{7,5},{8,10},{9,11},{10,... | collective-permute-start | bytes 1572872 | tf_op jit(solution)/shard_map/ppermute | solution.py:582
  4.7 18.1 %collective-permute-start.6 = (bf16[4,64,512]{2,1,0:T(8,128)(2,1)S(1)}, bf16[4,64,512]{2,1,0:T(8,128)(2,1)S(1)}, u32[]{:S(2)}, u32[]{:S(2)}) collective-permute-start(bf16[4,64,512]{2,1,0:T(8,128)(2,1)S(1)} %get-tuple-element.44.refs_4_), channel_id=1, source_target_pairs={{0,1},{1,0},{2,3},{3,2},{4,5},{5,4},{6,7},{7,6},{8,9},{9,8},{10,11... | collective-permute-start | bytes 786440 | tf_op jit(solution)/shard_map/ppermute | solution.py:582
  6.2 16.6 %collective-permute-start.7 = (bf16[4,64,512]{2,1,0:T(8,128)(2,1)S(1)}, bf16[4,64,512]{2,1,0:T(8,128)(2,1)S(1)}, u32[]{:S(2)}, u32[]{:S(2)}) collective-permute-start(bf16[4,64,512]{2,1,0:T(8,128)(2,1)S(1)} %get-tuple-element.54.refs_6_), channel_id=1, source_target_pairs={{0,2},{1,3},{2,0},{3,1},{4,6},{5,7},{6,4},{7,5},{8,10},{9,11},{10,... | collective-permute-start | bytes 786440 | tf_op jit(solution)/shard_map/ppermute | solution.py:582
  6.8 2.3 %copy-start = (f32[1536,768]{1,0:T(8,128)S(1)}, f32[1536,768]{1,0:T(8,128)}, u32[]{:S(2)}) copy-start(f32[1536,768]{1,0:T(8,128)} %anc_ref.4) | copy-start | bytes 14155780
  9.1 1.9 %copy-start.4 = (s32[1,8,6]{1,0,2:T(1,128)S(1)}, s32[1,8,6]{1,0,2:T(1,128)}, u32[]{:S(2)}) copy-start(s32[1,8,6]{1,0,2:T(1,128)} %param.8) | copy-start | bytes 580
  9.8 5.0 %collective-permute-start = (f32[3,128,128]{2,1,0:T(8,128)S(1)}, f32[3,128,128]{2,1,0:T(8,128)S(1)}, u32[]{:S(2)}, u32[]{:S(2)}) collective-permute-start(f32[3,128,128]{2,1,0:T(8,128)S(1)} %later_blocks.1), channel_id=1, source_target_pairs={{0,4},{1,5},{6,2},{7,3},{8,12},{9,13},{14,10},{15,11},{16,20},{17,... | collective-permute-start | bytes 589832 | tf_op jit(solution)/shard_map/ppermute | solution.py:566
  11.2 1.4 %copy-start.2 = (bf16[1,8,128,768]{3,2,1,0:T(8,128)(2,1)S(1)}, bf16[1,8,128,768]{3,2,1,0:T(8,128)(2,1)}, u32[]{:S(2)}) copy-start(bf16[1,8,128,768]{3,2,1,0:T(8,128)(2,1)} %param.6) | copy-start | bytes 4718596
  18.2 16.2 %collective-permute-start.4 = (bf16[2,4,64,512]{3,2,1,0:T(8,128)(2,1)S(1)}, bf16[2,4,64,512]{3,2,1,0:T(8,128)(2,1)S(1)}, u32[]{:S(2)}, u32[]{:S(2)}) collective-permute-start(bf16[2,4,64,512]{3,2,1,0:T(8,128)(2,1)S(1)} %get-tuple-element.49), channel_id=1, source_target_pairs={{0,2},{1,3},{2,0},{3,1},{4,6},{5,7},{6,4},{7,5},{8,10},{9,11},{10,... | collective-permute-start | bytes 1572872 | tf_op jit(solution)/shard_map/ppermute | solution.py:582
  20.3 15.8 %collective-permute-start.5 = (bf16[2,4,64,512]{3,2,1,0:T(8,128)(2,1)S(1)}, bf16[2,4,64,512]{3,2,1,0:T(8,128)(2,1)S(1)}, u32[]{:S(2)}, u32[]{:S(2)}) collective-permute-start(bf16[2,4,64,512]{3,2,1,0:T(8,128)(2,1)S(1)} %get-tuple-element.50), channel_id=1, source_target_pairs={{0,1},{1,0},{2,3},{3,2},{4,5},{5,4},{6,7},{7,6},{8,9},{9,8},{10,11... | collective-permute-start | bytes 1572872 | tf_op jit(solution)/shard_map/ppermute | solution.py:582
  23.8 21.5 %collective-permute-start.8 = (bf16[2,4,64,512]{3,2,1,0:T(8,128)(2,1)S(1)}, bf16[2,4,64,512]{3,2,1,0:T(8,128)(2,1)S(1)}, u32[]{:S(2)}, u32[]{:S(2)}) collective-permute-start(bf16[2,4,64,512]{3,2,1,0:T(8,128)(2,1)S(1)} %get-tuple-element.55), channel_id=1, source_target_pairs={{0,2},{1,3},{2,0},{3,1},{4,6},{5,7},{6,4},{7,5},{8,10},{9,11},{10,... | collective-permute-start | bytes 1572872 | tf_op jit(solution)/shard_map/ppermute | solution.py:582
  25.9 3.0 %copy-start.3 = (s32[1,8,12]{2,1,0:T(8,128)S(1)}, s32[1,8,12]{2,1,0:T(8,128)}, u32[]{:S(2)}) copy-start(s32[1,8,12]{2,1,0:T(8,128)} %param.7) | copy-start | bytes 1156
  25.9 20.5 %collective-permute-start.9 = (bf16[2,4,64,512]{3,2,1,0:T(8,128)(2,1)S(1)}, bf16[2,4,64,512]{3,2,1,0:T(8,128)(2,1)S(1)}, u32[]{:S(2)}, u32[]{:S(2)}) collective-permute-start(bf16[2,4,64,512]{3,2,1,0:T(8,128)(2,1)S(1)} %get-tuple-element.56), channel_id=1, source_target_pairs={{0,1},{1,0},{2,3},{3,2},{4,5},{5,4},{6,7},{7,6},{8,9},{9,8},{10,11... | collective-permute-start | bytes 1572872 | tf_op jit(solution)/shard_map/ppermute | solution.py:582
  28.3 31.7 %collective-permute-start.14 = (bf16[2,4,64,512]{3,2,1,0:T(8,128)(2,1)S(1)}, bf16[2,4,64,512]{3,2,1,0:T(8,128)(2,1)S(1)}, u32[]{:S(2)}, u32[]{:S(2)}) collective-permute-start(bf16[2,4,64,512]{3,2,1,0:T(8,128)(2,1)S(1)} %get-tuple-element.69), channel_id=1, source_target_pairs={{0,2},{1,3},{2,0},{3,1},{4,6},{5,7},{6,4},{7,5},{8,10},{9,11},{10,... | collective-permute-start | bytes 1572872 | tf_op jit(solution)/shard_map/ppermute | solution.py:582
  34.4 25.6 %collective-permute-start.15 = (bf16[2,4,64,512]{3,2,1,0:T(8,128)(2,1)S(1)}, bf16[2,4,64,512]{3,2,1,0:T(8,128)(2,1)S(1)}, u32[]{:S(2)}, u32[]{:S(2)}) collective-permute-start(bf16[2,4,64,512]{3,2,1,0:T(8,128)(2,1)S(1)} %get-tuple-element.70), channel_id=1, source_target_pairs={{0,1},{1,0},{2,3},{3,2},{4,5},{5,4},{6,7},{7,6},{8,9},{9,8},{10,11... | collective-permute-start | bytes 1572872 | tf_op jit(solution)/shard_map/ppermute | solution.py:582
  38.2 15.3 %collective-permute-start.10 = (s16[272,768]{1,0:T(8,128)(2,1)S(1)}, s16[272,768]{1,0:T(8,128)(2,1)S(1)}, u32[]{:S(2)}, u32[]{:S(2)}) collective-permute-start(s16[272,768]{1,0:T(8,128)(2,1)S(1)} %get-tuple-element.62), channel_id=1, source_target_pairs={{0,8},{8,0},{16,24},{24,16},{1,9},{9,1},{17,25},{25,17},{2,10},{10... | collective-permute-start | bytes 1253384 | tf_op jit(solution)/shard_map/ppermute | solution.py:569
  48.6 2.2 %collective-permute-start.16 = (s16[144,384]{1,0:T(8,128)(2,1)S(1)}, s16[144,384]{1,0:T(8,128)(2,1)S(1)}, u32[]{:S(2)}, u32[]{:S(2)}) collective-permute-start(s16[144,384]{1,0:T(8,128)(2,1)S(1)} %get-tuple-element.72), channel_id=1, source_target_pairs={{0,4},{1,5},{6,2},{7,3},{8,12},{9,13},{14,10},{15,11},{16,20},{17,... | collective-permute-start | bytes 331784 | tf_op jit(solution)/shard_map/ppermute | solution.py:566
  51.4 7.6 %collective-permute-start.17 = (s16[144,384]{1,0:T(8,128)(2,1)S(1)}, s16[144,384]{1,0:T(8,128)(2,1)S(1)}, u32[]{:S(2)}, u32[]{:S(2)}) collective-permute-start(s16[144,384]{1,0:T(8,128)(2,1)S(1)} %pick.1.mine_ref), channel_id=1, source_target_pairs={{0,8},{8,0},{16,24},{24,16},{1,9},{9,1},{17,25},{25,17},{2,10},{10... | collective-permute-start | bytes 331784 | tf_op jit(solution)/shard_map/ppermute | solution.py:569
  53.0 20.1 %collective-permute-start.12 = (s16[272,768]{1,0:T(8,128)(2,1)S(1)}, s16[272,768]{1,0:T(8,128)(2,1)S(1)}, u32[]{:S(2)}, u32[]{:S(2)}) collective-permute-start(s16[272,768]{1,0:T(8,128)(2,1)S(1)} %get-tuple-element.65), channel_id=1, source_target_pairs={{0,8},{8,0},{16,24},{24,16},{1,9},{9,1},{17,25},{25,17},{2,10},{10... | collective-permute-start | bytes 1253384 | tf_op jit(solution)/shard_map/ppermute | solution.py:569
  54.3 22.5 %collective-permute-start.11 = (s16[272,768]{1,0:T(8,128)(2,1)S(1)}, s16[272,768]{1,0:T(8,128)(2,1)S(1)}, u32[]{:S(2)}, u32[]{:S(2)}) collective-permute-start(s16[272,768]{1,0:T(8,128)(2,1)S(1)} %get-tuple-element.64), channel_id=1, source_target_pairs={{1,17},{2,18},{4,20},{7,23},{9,25},{10,26},{12,28},{15,31},{16,0},... | collective-permute-start | bytes 1253384 | tf_op jit(solution)/shard_map/ppermute | solution.py:579
  59.0 17.8 %slice-start = ((s8[4718592]{0:T(1024)(128)(4,1)}), s8[4194304]{0:T(1024)(128)(4,1)S(1)}, s32[]{:S(2)}) async-start(s8[4718592]{0:T(1024)(128)(4,1)} %bitcast.14), calls=%async_computation | async-start | bytes 8388608
  59.1 17.7 %slice-start.1 = ((s8[4718592]{0:T(1024)(128)(4,1)}), s8[524288]{0:T(1024)(128)(4,1)S(1)}, s32[]{:S(2)}) async-start(s8[4718592]{0:T(1024)(128)(4,1)} %bitcast.14), calls=%async_computation.1 | async-start | bytes 1048576
  59.1 17.6 %collective-permute-start.18 = (s16[144,384]{1,0:T(8,128)(2,1)S(1)}, s16[144,384]{1,0:T(8,128)(2,1)S(1)}, u32[]{:S(2)}, u32[]{:S(2)}) collective-permute-start(s16[144,384]{1,0:T(8,128)(2,1)S(1)} %add_coded.1.one_ref), channel_id=1, source_target_pairs={{0,16},{8,24},{16,0},{24,8},{1,17},{9,25},{17,1},{25,9},{2,18},{10... | collective-permute-start | bytes 331784 | tf_op jit(solution)/shard_map/ppermute | solution.py:569
  62.2 24.0 %collective-permute-start.19 = (s16[272,768]{1,0:T(8,128)(2,1)S(1)}, s16[272,768]{1,0:T(8,128)(2,1)S(1)}, u32[]{:S(2)}, u32[]{:S(2)}) collective-permute-start(s16[272,768]{1,0:T(8,128)(2,1)S(1)} %get-tuple-element.76), channel_id=1, source_target_pairs={{0,8},{8,0},{16,24},{24,16},{1,9},{9,1},{17,25},{25,17},{2,10},{10... | collective-permute-start | bytes 1253384 | tf_op jit(solution)/shard_map/ppermute | solution.py:569
  73.9 22.7 %collective-permute-start.13 = (s16[144,768]{1,0:T(8,128)(2,1)S(1)}, s16[144,768]{1,0:T(8,128)(2,1)S(1)}, u32[]{:S(2)}, u32[]{:S(2)}) collective-permute-start(s16[144,768]{1,0:T(8,128)(2,1)S(1)} %get-tuple-element.67), channel_id=1, source_target_pairs={{0,16},{1,17},{2,18},{3,19},{4,20},{5,21},{6,22},{7,23},{8,24},{9,... | collective-permute-start | bytes 663560 | tf_op jit(solution)/shard_map/ppermute | solution.py:579
  87.0 15.2 %collective-permute-start.20 = (s16[272,768]{1,0:T(8,128)(2,1)S(1)}, s16[272,768]{1,0:T(8,128)(2,1)S(1)}, u32[]{:S(2)}, u32[]{:S(2)}) collective-permute-start(s16[272,768]{1,0:T(8,128)(2,1)S(1)} %get-tuple-element.80), channel_id=1, source_target_pairs={{0,16},{3,19},{5,21},{6,22},{8,24},{11,27},{13,29},{14,30},{17,1},... | collective-permute-start | bytes 1253384 | tf_op jit(solution)/shard_map/ppermute | solution.py:579
  95.2 2.5 %collective-permute-start.21 = (f32[3,128,128]{2,1,0:T(8,128)S(1)}, f32[3,128,128]{2,1,0:T(8,128)S(1)}, u32[]{:S(2)}, u32[]{:S(2)}) collective-permute-start(f32[3,128,128]{2,1,0:T(8,128)S(1)} %factor.3.refs_6_), channel_id=1, source_target_pairs={{0,4},{4,0},{1,5},{5,1},{2,6},{6,2},{3,7},{7,3},{8,12},{12,8},{9,1... | collective-permute-start | bytes 589832 | tf_op jit(solution)/shard_map/ppermute | solution.py:623

commit v14 on v13

--- a/solution.py
+++ b/solution.py
@@ -18,7 +18,7 @@
 HALF_STEPS = 48
 LU = 10
 NEAR = 10
-FAR = 4
+FAR = 1
 
 
 def cost(micros):

time: 106 us -> 105 us (level)
    ppermute x1, starting transfers between devices: 1.4 us -> 0.15 us  [planned(): lu_got = lax.ppermute(lu, 'row', xor_perm(rows, 1))]
where the time goes in v14:
time: 105 us; the launch traced here: 104 us
  Pallas kernels  35.5 us (34%)
  starting transfers between devices  31 us (30%)
  waiting for transfers between devices  30.9 us (29%)
  local copies, waits for them, and re-layouts  5.33 us (5%)
  between operations  1.06 us (1%)
    ppermute x5, waiting for transfers between devices, over_layers(): return lax.ppermute(value, 'layer', xor_perm(layers, bit))  14.2 us
    ppermute x10, starting transfers between devices, over(): return lax.ppermute(value, 'col', xor_perm(cols, bit))  13.9 us
    pallas_call x2, Pallas kernels, factor(): pl.pallas_call(functools.partial(lu_kernel, begin, end), out_shape=jax.Sh...  11.4 us
    ppermute x10, waiting for transfers between devices, over(): return lax.ppermute(value, 'col', xor_perm(cols, bit))  9.67 us
    ppermute x3, starting transfers between devices, far_layers(): return lax.ppermute(value, everyone, perm)  7.75 us
    ppermute x5, starting transfers between devices, over_layers(): return lax.ppermute(value, 'layer', xor_perm(layers, bit))  6.52 us
    pallas_call x3, Pallas kernels, far_update(): pl.pallas_call(functools.partial(far_kernel, chunk, blocks, len(earlier))...  6.37 us
    pallas_call x3, Pallas kernels, near_update(): pl.pallas_call(functools.partial(near_kernel, chunk, blocks), out_shape=j...  5.5 us
  transfers between devices with their start and end apart: 22, of which 12 were waited for; matrix products, arithmetic and copies ran while one was open for 0% of the time, Pallas kernels for 32%

profile of v14, /device:TPU:2, one launch (start us, length us, event | category | flops | bytes accessed | tf_op | source)
XLA Modules:
  0.0 103.7 jit_solution(14107469857783299732)
XLA Ops:
  0.7 1.4 %copy-done.1 = bf16[1,8,1536,64]{2,3,1,0:T(8,128)(2,1)S(1)} copy-done((bf16[1,8,1536,64]{2,3,1,0:T(8,128)(2,1)S(1)}, bf16[1,8,1536,64]{2,3,1,0:T(8,128)(2,1)}, u32[]{:S(2)}) %copy-start.1) | copy-done | bytes 1572888
  2.4 2.0 %collective-permute-start.3 = (bf16[4,64,1024]{2,1,0:T(8,128)(2,1)S(1)}, bf16[4,64,1024]{2,1,0:T(8,128)(2,1)S(1)}, u32[]{:S(2)}, u32[]{:S(2)}) collective-permute-start(bf16[4,64,1024]{2,1,0:T(8,128)(2,1)S(1)} %get-tuple-element.48.refs_2_), channel_id=1, source_target_pairs={{0,2},{1,3},{2,0},{3,1},{4,6},{5,7},{6,4},{7,5},{8,10},{9,11},{10,... | collective-permute-start | bytes 1572872 | tf_op jit(solution)/shard_map/ppermute | solution.py:582
  4.7 1.6 %collective-permute-start.6 = (bf16[4,64,512]{2,1,0:T(8,128)(2,1)S(1)}, bf16[4,64,512]{2,1,0:T(8,128)(2,1)S(1)}, u32[]{:S(2)}, u32[]{:S(2)}) collective-permute-start(bf16[4,64,512]{2,1,0:T(8,128)(2,1)S(1)} %get-tuple-element.44.refs_4_), channel_id=1, source_target_pairs={{0,1},{1,0},{2,3},{3,2},{4,5},{5,4},{6,7},{7,6},{8,9},{9,8},{10,11... | collective-permute-start | bytes 786440 | tf_op jit(solution)/shard_map/ppermute | solution.py:582
  6.8 2.3 %copy-done = f32[1536,768]{1,0:T(8,128)S(1)} copy-done((f32[1536,768]{1,0:T(8,128)S(1)}, f32[1536,768]{1,0:T(8,128)}, u32[]{:S(2)}) %copy-start) | copy-done | bytes 4718616
  9.2 0.6 later_blocks.1
  9.8 1.3 %collective-permute-start = (f32[3,128,128]{2,1,0:T(8,128)S(1)}, f32[3,128,128]{2,1,0:T(8,128)S(1)}, u32[]{:S(2)}, u32[]{:S(2)}) collective-permute-start(f32[3,128,128]{2,1,0:T(8,128)S(1)} %later_blocks.1), channel_id=1, source_target_pairs={{0,4},{1,5},{6,2},{7,3},{8,12},{9,13},{14,10},{15,11},{16,20},{17,... | collective-permute-start | bytes 589832 | tf_op jit(solution)/shard_map/ppermute | solution.py:566
  11.2 1.4 %copy-done.2 = bf16[1,8,128,768]{3,2,1,0:T(8,128)(2,1)S(1)} copy-done((bf16[1,8,128,768]{3,2,1,0:T(8,128)(2,1)S(1)}, bf16[1,8,128,768]{3,2,1,0:T(8,128)(2,1)}, u32[]{:S(2)}) %copy-start.2) | copy-done | bytes 1572888
  12.6 2.2 %masked_right.1 = (bf16[8,128,768]{2,1,0:T(8,128)(2,1)S(1)}, bf16[8,128,768]{2,1,0:T(8,128)(2,1)S(1)}) custom-call(s32[8]{0:T(128)S(1)} %stack.35.where_ref, s32[8,6]{1,0:T(8,128)S(1)} %bitcast.26, bf16[8,128,768]{2,1,0:T(8,128)(2,1)S(1)} %bitcast.19, bf16[8,128,768]{2,1,0:T(8,128)(2,1)} %collective-permute-done.1.uo_ref), custom_call_target="tpu_custom_call" | custom-call | flops 1000 | bytes 1000 | tf_op jit(solution)/shard_map/masked_right/pallas_call | solution.py:226
  14.8 2.4 %collective-permute-done.2.refs_1_ = bf16[4,64,1024]{2,1,0:T(8,128)(2,1)S(1)} collective-permute-done((bf16[4,64,1024]{2,1,0:T(8,128)(2,1)S(1)}, bf16[4,64,1024]{2,1,0:T(8,128)(2,1)S(1)}, u32[]{:S(2)}, u32[]{:S(2)}) %collective-permute-start.2) | collective-permute-done | bytes 524320 | tf_op jit(solution)/shard_map/ppermute | solution.py:582
  17.2 1.0 split.3
  18.2 2.1 %collective-permute-start.4 = (bf16[2,4,64,512]{3,2,1,0:T(8,128)(2,1)S(1)}, bf16[2,4,64,512]{3,2,1,0:T(8,128)(2,1)S(1)}, u32[]{:S(2)}, u32[]{:S(2)}) collective-permute-start(bf16[2,4,64,512]{3,2,1,0:T(8,128)(2,1)S(1)} %get-tuple-element.49), channel_id=1, source_target_pairs={{0,2},{1,3},{2,0},{3,1},{4,6},{5,7},{6,4},{7,5},{8,10},{9,11},{10,... | collective-permute-start | bytes 1572872 | tf_op jit(solution)/shard_map/ppermute | solution.py:582
  20.3 1.5 %collective-permute-start.5 = (bf16[2,4,64,512]{3,2,1,0:T(8,128)(2,1)S(1)}, bf16[2,4,64,512]{3,2,1,0:T(8,128)(2,1)S(1)}, u32[]{:S(2)}, u32[]{:S(2)}) collective-permute-start(bf16[2,4,64,512]{3,2,1,0:T(8,128)(2,1)S(1)} %get-tuple-element.50), channel_id=1, source_target_pairs={{0,1},{1,0},{2,3},{3,2},{4,5},{5,4},{6,7},{7,6},{8,9},{9,8},{10,11... | collective-permute-start | bytes 1572872 | tf_op jit(solution)/shard_map/ppermute | solution.py:582
  21.8 1.0 collective-permute-done.6.refs_5_
  22.8 1.0 split.4
  23.8 2.1 %collective-permute-start.8 = (bf16[2,4,64,512]{3,2,1,0:T(8,128)(2,1)S(1)}, bf16[2,4,64,512]{3,2,1,0:T(8,128)(2,1)S(1)}, u32[]{:S(2)}, u32[]{:S(2)}) collective-permute-start(bf16[2,4,64,512]{3,2,1,0:T(8,128)(2,1)S(1)} %get-tuple-element.55), channel_id=1, source_target_pairs={{0,2},{1,3},{2,0},{3,1},{4,6},{5,7},{6,4},{7,5},{8,10},{9,11},{10,... | collective-permute-start | bytes 1572872 | tf_op jit(solution)/shard_map/ppermute | solution.py:582
  25.9 1.5 %collective-permute-start.9 = (bf16[2,4,64,512]{3,2,1,0:T(8,128)(2,1)S(1)}, bf16[2,4,64,512]{3,2,1,0:T(8,128)(2,1)S(1)}, u32[]{:S(2)}, u32[]{:S(2)}) collective-permute-start(bf16[2,4,64,512]{3,2,1,0:T(8,128)(2,1)S(1)} %get-tuple-element.56), channel_id=1, source_target_pairs={{0,1},{1,0},{2,3},{3,2},{4,5},{5,4},{6,7},{7,6},{8,9},{9,8},{10,11... | collective-permute-start | bytes 1572872 | tf_op jit(solution)/shard_map/ppermute | solution.py:582
  27.4 1.0 split.5
  28.9 1.8 %near_update.5.refs_1_ = f32[4,128,768]{2,1,0:T(8,128)S(1)} custom-call(s32[8]{0:T(128)S(1)} %stack.35.where_ref, s32[8,12]{1,0:T(8,128)S(1)} %bitcast.20, bf16[4,64,1024]{2,1,0:T(8,128)(2,1)S(1)} %get-tuple-element.42.refs_0_, bf16[4,64,1024]{2,1,0:T(8,128)(2,1)S(1)} %collective-permute-done.2.refs_1_, bf16[4,64,1024]{2,1,0:T(8,128)(2,1)S(1)} %get-tuple-element.48.refs_2_, ...), custom_call_target="tpu_custom_call" | custom-call | flops 10000001024 | bytes 1000 | tf_op jit(solution)/shard_map/near_update/pallas_call | solution.py:273
  30.7 1.9 %near_update.3.refs_1_ = f32[4,128,768]{2,1,0:T(8,128)S(1)} custom-call(s32[8]{0:T(128)S(1)} %stack.35.where_ref, s32[8,12]{1,0:T(8,128)S(1)} %bitcast.21, bf16[4,64,1024]{2,1,0:T(8,128)(2,1)S(1)} %get-tuple-element.42.refs_0_, bf16[4,64,1024]{2,1,0:T(8,128)(2,1)S(1)} %collective-permute-done.2.refs_1_, bf16[4,64,1024]{2,1,0:T(8,128)(2,1)S(1)} %get-tuple-element.48.refs_2_, ...), custom_call_target="tpu_custom_call" | custom-call | flops 10000001024 | bytes 1000 | tf_op jit(solution)/shard_map/near_update/pallas_call | solution.py:273
  32.6 1.5 %collective-permute-done.4.a_ref = bf16[2,4,64,512]{3,2,1,0:T(8,128)(2,1)S(1)} collective-permute-done((bf16[2,4,64,512]{3,2,1,0:T(8,128)(2,1)S(1)}, bf16[2,4,64,512]{3,2,1,0:T(8,128)(2,1)S(1)}, u32[]{:S(2)}, u32[]{:S(2)}) %collective-permute-start.4) | collective-permute-done | bytes 524320 | tf_op jit(solution)/shard_map/ppermute | solution.py:582
  34.1 2.0 %collective-permute-start.15 = (bf16[2,4,64,512]{3,2,1,0:T(8,128)(2,1)S(1)}, bf16[2,4,64,512]{3,2,1,0:T(8,128)(2,1)S(1)}, u32[]{:S(2)}, u32[]{:S(2)}) collective-permute-start(bf16[2,4,64,512]{3,2,1,0:T(8,128)(2,1)S(1)} %get-tuple-element.70), channel_id=1, source_target_pairs={{0,1},{1,0},{2,3},{3,2},{4,5},{5,4},{6,7},{7,6},{8,9},{9,8},{10,11... | collective-permute-start | bytes 1572872 | tf_op jit(solution)/shard_map/ppermute | solution.py:582
  36.1 2.1 %far_update.3 = (f32[2,128,768]{2,1,0:T(8,128)S(1)}, s16[272,768]{1,0:T(8,128)(2,1)S(1)}, s16[144,384]{1,0:T(8,128)(2,1)S(1)}, s16[144,384]{1,0:T(8,128)(2,1)S(1)}) custom-call(s32[8]{0:T(128)S(1)} %stack.35.where_ref, s32[8,12]{1,0:T(8,128)S(1)} %bitcast.22, bf16[2,4,64,512]{3,2,1,0:T(8,128)(2,1)S(1)} %collective-permute-done.4.a_ref, ...), custom_call_target="tpu_custom_call" | custom-call | flops 1000001024 | bytes 1000 | tf_op jit(solution)/shard_map/far_update/pallas_call | solution.py:322
  38.2 1.7 %collective-permute-start.10 = (s16[272,768]{1,0:T(8,128)(2,1)S(1)}, s16[272,768]{1,0:T(8,128)(2,1)S(1)}, u32[]{:S(2)}, u32[]{:S(2)}) collective-permute-start(s16[272,768]{1,0:T(8,128)(2,1)S(1)} %get-tuple-element.62), channel_id=1, source_target_pairs={{0,8},{8,0},{16,24},{24,16},{1,9},{9,1},{17,25},{25,17},{2,10},{10... | collective-permute-start | bytes 1253384 | tf_op jit(solution)/shard_map/ppermute | solution.py:569
  39.8 1.8 %near_update.4.refs_1_ = f32[4,128,768]{2,1,0:T(8,128)S(1)} custom-call(s32[8]{0:T(128)S(1)} %stack.35.where_ref, s32[8,12]{1,0:T(8,128)S(1)} %bitcast.23, bf16[4,64,1024]{2,1,0:T(8,128)(2,1)S(1)} %get-tuple-element.42.refs_0_, bf16[4,64,1024]{2,1,0:T(8,128)(2,1)S(1)} %collective-permute-done.2.refs_1_, bf16[4,64,1024]{2,1,0:T(8,128)(2,1)S(1)} %get-tuple-element.48.refs_2_, ...), custom_call_target="tpu_custom_call" | custom-call | flops 10000001024 | bytes 1000 | tf_op jit(solution)/shard_map/near_update/pallas_call | solution.py:273
  41.7 3.6 %collective-permute-done.8.a_ref = bf16[2,4,64,512]{3,2,1,0:T(8,128)(2,1)S(1)} collective-permute-done((bf16[2,4,64,512]{3,2,1,0:T(8,128)(2,1)S(1)}, bf16[2,4,64,512]{3,2,1,0:T(8,128)(2,1)S(1)}, u32[]{:S(2)}, u32[]{:S(2)}) %collective-permute-start.8) | collective-permute-done | bytes 524320 | tf_op jit(solution)/shard_map/ppermute | solution.py:582
  45.3 1.1 %collective-permute-done.9.b_ref = bf16[2,4,64,512]{3,2,1,0:T(8,128)(2,1)S(1)} collective-permute-done((bf16[2,4,64,512]{3,2,1,0:T(8,128)(2,1)S(1)}, bf16[2,4,64,512]{3,2,1,0:T(8,128)(2,1)S(1)}, u32[]{:S(2)}, u32[]{:S(2)}) %collective-permute-start.9) | collective-permute-done | bytes 524320 | tf_op jit(solution)/shard_map/ppermute | solution.py:582
  46.4 2.1 %far_update.4 = (f32[2,128,768]{2,1,0:T(8,128)S(1)}, s16[272,768]{1,0:T(8,128)(2,1)S(1)}, s16[144,384]{1,0:T(8,128)(2,1)S(1)}, s16[144,384]{1,0:T(8,128)(2,1)S(1)}) custom-call(s32[8]{0:T(128)S(1)} %stack.35.where_ref, s32[8,12]{1,0:T(8,128)S(1)} %bitcast.24, bf16[2,4,64,512]{3,2,1,0:T(8,128)(2,1)S(1)} %collective-permute-done.8.a_ref, ...), custom_call_target="tpu_custom_call" | custom-call | flops 1000001024 | bytes 1000 | tf_op jit(solution)/shard_map/far_update/pallas_call | solution.py:322
  48.6 1.7 %collective-permute-start.12 = (s16[272,768]{1,0:T(8,128)(2,1)S(1)}, s16[272,768]{1,0:T(8,128)(2,1)S(1)}, u32[]{:S(2)}, u32[]{:S(2)}) collective-permute-start(s16[272,768]{1,0:T(8,128)(2,1)S(1)} %get-tuple-element.65), channel_id=1, source_target_pairs={{0,8},{8,0},{16,24},{24,16},{1,9},{9,1},{17,25},{25,17},{2,10},{10... | collective-permute-start | bytes 1253384 | tf_op jit(solution)/shard_map/ppermute | solution.py:569
  50.2 0.8 halve.3
  51.0 4.5 %collective-permute-start.11 = (s16[272,768]{1,0:T(8,128)(2,1)S(1)}, s16[272,768]{1,0:T(8,128)(2,1)S(1)}, u32[]{:S(2)}, u32[]{:S(2)}) collective-permute-start(s16[272,768]{1,0:T(8,128)(2,1)S(1)} %get-tuple-element.64), channel_id=1, source_target_pairs={{1,17},{2,18},{4,20},{7,23},{9,25},{10,26},{12,28},{15,31},{16,0},... | collective-permute-start | bytes 1253384 | tf_op jit(solution)/shard_map/ppermute | solution.py:579
  55.6 1.3 %collective-permute-start.16 = (s16[144,384]{1,0:T(8,128)(2,1)S(1)}, s16[144,384]{1,0:T(8,128)(2,1)S(1)}, u32[]{:S(2)}, u32[]{:S(2)}) collective-permute-start(s16[144,384]{1,0:T(8,128)(2,1)S(1)} %get-tuple-element.72), channel_id=1, source_target_pairs={{0,4},{1,5},{6,2},{7,3},{8,12},{9,13},{14,10},{15,11},{16,20},{17,... | collective-permute-start | bytes 331784 | tf_op jit(solution)/shard_map/ppermute | solution.py:566
  56.9 0.9 collective-permute-done.16.got_ref
  57.8 0.7 pick.1.mine_ref
  59.1 6.2 %collective-permute-done.17.got_ref = s16[144,384]{1,0:T(8,128)(2,1)S(1)} collective-permute-done((s16[144,384]{1,0:T(8,128)(2,1)S(1)}, s16[144,384]{1,0:T(8,128)(2,1)S(1)}, u32[]{:S(2)}, u32[]{:S(2)}) %collective-permute-start.17) | collective-permute-done | bytes 110624 | tf_op jit(solution)/shard_map/ppermute | solution.py:569
  65.3 1.0 collective-permute-start.18
  66.3 2.1 %far_update.5 = (f32[2,128,768]{2,1,0:T(8,128)S(1)}, s16[272,768]{1,0:T(8,128)(2,1)S(1)}) custom-call(s32[8]{0:T(128)S(1)} %stack.35.where_ref, s32[8,12]{1,0:T(8,128)S(1)} %bitcast.25, bf16[2,4,64,512]{3,2,1,0:T(8,128)(2,1)S(1)} %collective-permute-done.14.a_ref, bf16[2,4,64,512]{3,2,1,0:T(8,128)(2,1)S(1)} %collective-permute-done.15.b_ref, ...), custom_call_target="tpu_custom_call" | custom-call | flops 1000001024 | bytes 1000 | tf_op jit(solution)/shard_map/far_update/pallas_call | solution.py:322
  68.5 1.7 %collective-permute-start.19 = (s16[272,768]{1,0:T(8,128)(2,1)S(1)}, s16[272,768]{1,0:T(8,128)(2,1)S(1)}, u32[]{:S(2)}, u32[]{:S(2)}) collective-permute-start(s16[272,768]{1,0:T(8,128)(2,1)S(1)} %get-tuple-element.76), channel_id=1, source_target_pairs={{0,8},{8,0},{16,24},{24,16},{1,9},{9,1},{17,25},{25,17},{2,10},{10... | collective-permute-start | bytes 1253384 | tf_op jit(solution)/shard_map/ppermute | solution.py:569
  70.2 0.7 halve.4
  70.9 1.9 %collective-permute-start.13 = (s16[144,768]{1,0:T(8,128)(2,1)S(1)}, s16[144,768]{1,0:T(8,128)(2,1)S(1)}, u32[]{:S(2)}, u32[]{:S(2)}) collective-permute-start(s16[144,768]{1,0:T(8,128)(2,1)S(1)} %get-tuple-element.67), channel_id=1, source_target_pairs={{0,16},{1,17},{2,18},{3,19},{4,20},{5,21},{6,22},{7,23},{8,24},{9,... | collective-permute-start | bytes 663560 | tf_op jit(solution)/shard_map/ppermute | solution.py:579
  72.9 0.7 pivots.1.in_ref
  73.6 4.6 %factor.2.in_ref = f32[3,128,128]{2,1,0:T(8,128)S(1)} custom-call(f32[3,128,128]{2,1,0:T(8,128)S(1)} %pivots.1.in_ref), custom_call_target="tpu_custom_call" | custom-call | flops 10000001024 | bytes 1000 | tf_op jit(solution)/shard_map/factor/pallas_call | solution.py:82
  78.2 8.1 %collective-permute-done.19.got_ref = s16[272,768]{1,0:T(8,128)(2,1)S(1)} collective-permute-done((s16[272,768]{1,0:T(8,128)(2,1)S(1)}, s16[272,768]{1,0:T(8,128)(2,1)S(1)}, u32[]{:S(2)}, u32[]{:S(2)}) %collective-permute-start.19) | collective-permute-done | bytes 417824 | tf_op jit(solution)/shard_map/ppermute | solution.py:569
  86.2 0.8 halve.5
  87.0 1.3 %collective-permute-start.20 = (s16[272,768]{1,0:T(8,128)(2,1)S(1)}, s16[272,768]{1,0:T(8,128)(2,1)S(1)}, u32[]{:S(2)}, u32[]{:S(2)}) collective-permute-start(s16[272,768]{1,0:T(8,128)(2,1)S(1)} %get-tuple-element.80), channel_id=1, source_target_pairs={{0,16},{3,19},{5,21},{6,22},{8,24},{11,27},{13,29},{14,30},{17,1},... | collective-permute-start | bytes 1253384 | tf_op jit(solution)/shard_map/ppermute | solution.py:579
  88.3 6.8 %factor.3.refs_6_ = f32[3,128,128]{2,1,0:T(8,128)S(1)} custom-call(f32[3,128,128]{2,1,0:T(8,128)S(1)} %factor.2.in_ref), custom_call_target="tpu_custom_call" | custom-call | flops 10000001024 | bytes 1000 | tf_op jit(solution)/shard_map/factor/pallas_call | solution.py:82
  95.3 1.3 %collective-permute-done.21.refs_7_ = f32[3,128,128]{2,1,0:T(8,128)S(1)} collective-permute-done((f32[3,128,128]{2,1,0:T(8,128)S(1)}, f32[3,128,128]{2,1,0:T(8,128)S(1)}, u32[]{:S(2)}, u32[]{:S(2)}) %collective-permute-start.21) | collective-permute-done | bytes 196640 | tf_op jit(solution)/shard_map/ppermute | solution.py:623
  96.6 4.7 %collective-permute-done.20.refs_5_ = s16[272,768]{1,0:T(8,128)(2,1)S(1)} collective-permute-done((s16[272,768]{1,0:T(8,128)(2,1)S(1)}, s16[272,768]{1,0:T(8,128)(2,1)S(1)}, u32[]{:S(2)}, u32[]{:S(2)}) %collective-permute-start.20) | collective-permute-done | bytes 417824 | tf_op jit(solution)/shard_map/ppermute | solution.py:579
  101.3 2.2 %combine.1 = (f32[384,768]{1,0:T(8,128)}, f32[6,128,128]{2,1,0:T(8,128)}) custom-call(s32[8]{0:T(128)S(1)} %stack.35.where_ref, f32[1536,768]{1,0:T(8,128)S(1)} %bitcast.15, f32[2,128,768]{2,1,0:T(8,128)S(1)} %get-tuple-element.63.refs_0_, s16[272,768]{1,0:T(8,128)(2,1)S(1)} %collective-permute-done.11.refs_1_, ...), custom_call_target="tpu_custom_call" | custom-call | flops 1000 | bytes 1000 | tf_op jit(solution)/shard_map/combine/pallas_call | solution.py:457
  (35 shorter events, 2.8 us)
Async XLA Ops:
  0.6 9.1 %collective-permute-start.1 = (bf16[8,128,768]{2,1,0:T(8,128)(2,1)}, bf16[8,128,768]{2,1,0:T(8,128)(2,1)}, u32[]{:S(2)}, u32[]{:S(2)}) collective-permute-start(bf16[8,128,768]{2,1,0:T(8,128)(2,1)} %bitcast.18), channel_id=1, source_target_pairs={{0,4},{4,0},{1,5},{5,1},{2,6},{6,2},{3,7},{7,3},{8,12},{12,8},{9,1... | collective-permute-start | bytes 4718600 | tf_op jit(solution)/shard_map/ppermute | solution.py:587
  0.7 1.4 %copy-start.1 = (bf16[1,8,1536,64]{2,3,1,0:T(8,128)(2,1)S(1)}, bf16[1,8,1536,64]{2,3,1,0:T(8,128)(2,1)}, u32[]{:S(2)}) copy-start(bf16[1,8,1536,64]{2,3,1,0:T(8,128)(2,1)} %param.5) | copy-start | bytes 4718596
  2.4 14.8 %collective-permute-start.2 = (bf16[4,64,1024]{2,1,0:T(8,128)(2,1)S(1)}, bf16[4,64,1024]{2,1,0:T(8,128)(2,1)S(1)}, u32[]{:S(2)}, u32[]{:S(2)}) collective-permute-start(bf16[4,64,1024]{2,1,0:T(8,128)(2,1)S(1)} %get-tuple-element.42.refs_0_), channel_id=1, source_target_pairs={{0,1},{1,0},{2,3},{3,2},{4,5},{5,4},{6,7},{7,6},{8,9},{9,8},{10,11... | collective-permute-start | bytes 1572872 | tf_op jit(solution)/shard_map/ppermute | solution.py:582
  2.4 14.8 %collective-permute-start.3 = (bf16[4,64,1024]{2,1,0:T(8,128)(2,1)S(1)}, bf16[4,64,1024]{2,1,0:T(8,128)(2,1)S(1)}, u32[]{:S(2)}, u32[]{:S(2)}) collective-permute-start(bf16[4,64,1024]{2,1,0:T(8,128)(2,1)S(1)} %get-tuple-element.48.refs_2_), channel_id=1, source_target_pairs={{0,2},{1,3},{2,0},{3,1},{4,6},{5,7},{6,4},{7,5},{8,10},{9,11},{10,... | collective-permute-start | bytes 1572872 | tf_op jit(solution)/shard_map/ppermute | solution.py:582
  4.7 18.1 %collective-permute-start.6 = (bf16[4,64,512]{2,1,0:T(8,128)(2,1)S(1)}, bf16[4,64,512]{2,1,0:T(8,128)(2,1)S(1)}, u32[]{:S(2)}, u32[]{:S(2)}) collective-permute-start(bf16[4,64,512]{2,1,0:T(8,128)(2,1)S(1)} %get-tuple-element.44.refs_4_), channel_id=1, source_target_pairs={{0,1},{1,0},{2,3},{3,2},{4,5},{5,4},{6,7},{7,6},{8,9},{9,8},{10,11... | collective-permute-start | bytes 786440 | tf_op jit(solution)/shard_map/ppermute | solution.py:582
  6.2 16.6 %collective-permute-start.7 = (bf16[4,64,512]{2,1,0:T(8,128)(2,1)S(1)}, bf16[4,64,512]{2,1,0:T(8,128)(2,1)S(1)}, u32[]{:S(2)}, u32[]{:S(2)}) collective-permute-start(bf16[4,64,512]{2,1,0:T(8,128)(2,1)S(1)} %get-tuple-element.54.refs_6_), channel_id=1, source_target_pairs={{0,2},{1,3},{2,0},{3,1},{4,6},{5,7},{6,4},{7,5},{8,10},{9,11},{10,... | collective-permute-start | bytes 786440 | tf_op jit(solution)/shard_map/ppermute | solution.py:582
  6.8 2.3 %copy-start = (f32[1536,768]{1,0:T(8,128)S(1)}, f32[1536,768]{1,0:T(8,128)}, u32[]{:S(2)}) copy-start(f32[1536,768]{1,0:T(8,128)} %anc_ref.4) | copy-start | bytes 14155780
  9.1 1.9 %copy-start.4 = (s32[1,8,6]{1,0,2:T(1,128)S(1)}, s32[1,8,6]{1,0,2:T(1,128)}, u32[]{:S(2)}) copy-start(s32[1,8,6]{1,0,2:T(1,128)} %param.8) | copy-start | bytes 580
  9.8 5.0 %collective-permute-start = (f32[3,128,128]{2,1,0:T(8,128)S(1)}, f32[3,128,128]{2,1,0:T(8,128)S(1)}, u32[]{:S(2)}, u32[]{:S(2)}) collective-permute-start(f32[3,128,128]{2,1,0:T(8,128)S(1)} %later_blocks.1), channel_id=1, source_target_pairs={{0,4},{1,5},{6,2},{7,3},{8,12},{9,13},{14,10},{15,11},{16,20},{17,... | collective-permute-start | bytes 589832 | tf_op jit(solution)/shard_map/ppermute | solution.py:566
  11.2 1.4 %copy-start.2 = (bf16[1,8,128,768]{3,2,1,0:T(8,128)(2,1)S(1)}, bf16[1,8,128,768]{3,2,1,0:T(8,128)(2,1)}, u32[]{:S(2)}) copy-start(bf16[1,8,128,768]{3,2,1,0:T(8,128)(2,1)} %param.6) | copy-start | bytes 4718596
  18.2 15.8 %collective-permute-start.4 = (bf16[2,4,64,512]{3,2,1,0:T(8,128)(2,1)S(1)}, bf16[2,4,64,512]{3,2,1,0:T(8,128)(2,1)S(1)}, u32[]{:S(2)}, u32[]{:S(2)}) collective-permute-start(bf16[2,4,64,512]{3,2,1,0:T(8,128)(2,1)S(1)} %get-tuple-element.49), channel_id=1, source_target_pairs={{0,2},{1,3},{2,0},{3,1},{4,6},{5,7},{6,4},{7,5},{8,10},{9,11},{10,... | collective-permute-start | bytes 1572872 | tf_op jit(solution)/shard_map/ppermute | solution.py:582
  20.3 15.8 %collective-permute-start.5 = (bf16[2,4,64,512]{3,2,1,0:T(8,128)(2,1)S(1)}, bf16[2,4,64,512]{3,2,1,0:T(8,128)(2,1)S(1)}, u32[]{:S(2)}, u32[]{:S(2)}) collective-permute-start(bf16[2,4,64,512]{3,2,1,0:T(8,128)(2,1)S(1)} %get-tuple-element.50), channel_id=1, source_target_pairs={{0,1},{1,0},{2,3},{3,2},{4,5},{5,4},{6,7},{7,6},{8,9},{9,8},{10,11... | collective-permute-start | bytes 1572872 | tf_op jit(solution)/shard_map/ppermute | solution.py:582
  23.8 21.5 %collective-permute-start.8 = (bf16[2,4,64,512]{3,2,1,0:T(8,128)(2,1)S(1)}, bf16[2,4,64,512]{3,2,1,0:T(8,128)(2,1)S(1)}, u32[]{:S(2)}, u32[]{:S(2)}) collective-permute-start(bf16[2,4,64,512]{3,2,1,0:T(8,128)(2,1)S(1)} %get-tuple-element.55), channel_id=1, source_target_pairs={{0,2},{1,3},{2,0},{3,1},{4,6},{5,7},{6,4},{7,5},{8,10},{9,11},{10,... | collective-permute-start | bytes 1572872 | tf_op jit(solution)/shard_map/ppermute | solution.py:582
  25.9 3.0 %copy-start.3 = (s32[1,8,12]{2,1,0:T(8,128)S(1)}, s32[1,8,12]{2,1,0:T(8,128)}, u32[]{:S(2)}) copy-start(s32[1,8,12]{2,1,0:T(8,128)} %param.7) | copy-start | bytes 1156
  25.9 20.5 %collective-permute-start.9 = (bf16[2,4,64,512]{3,2,1,0:T(8,128)(2,1)S(1)}, bf16[2,4,64,512]{3,2,1,0:T(8,128)(2,1)S(1)}, u32[]{:S(2)}, u32[]{:S(2)}) collective-permute-start(bf16[2,4,64,512]{3,2,1,0:T(8,128)(2,1)S(1)} %get-tuple-element.56), channel_id=1, source_target_pairs={{0,1},{1,0},{2,3},{3,2},{4,5},{5,4},{6,7},{7,6},{8,9},{9,8},{10,11... | collective-permute-start | bytes 1572872 | tf_op jit(solution)/shard_map/ppermute | solution.py:582
  28.3 38.0 %collective-permute-start.14 = (bf16[2,4,64,512]{3,2,1,0:T(8,128)(2,1)S(1)}, bf16[2,4,64,512]{3,2,1,0:T(8,128)(2,1)S(1)}, u32[]{:S(2)}, u32[]{:S(2)}) collective-permute-start(bf16[2,4,64,512]{3,2,1,0:T(8,128)(2,1)S(1)} %get-tuple-element.69), channel_id=1, source_target_pairs={{0,2},{1,3},{2,0},{3,1},{4,6},{5,7},{6,4},{7,5},{8,10},{9,11},{10,... | collective-permute-start | bytes 1572872 | tf_op jit(solution)/shard_map/ppermute | solution.py:582
  34.1 32.3 %collective-permute-start.15 = (bf16[2,4,64,512]{3,2,1,0:T(8,128)(2,1)S(1)}, bf16[2,4,64,512]{3,2,1,0:T(8,128)(2,1)S(1)}, u32[]{:S(2)}, u32[]{:S(2)}) collective-permute-start(bf16[2,4,64,512]{3,2,1,0:T(8,128)(2,1)S(1)} %get-tuple-element.70), channel_id=1, source_target_pairs={{0,1},{1,0},{2,3},{3,2},{4,5},{5,4},{6,7},{7,6},{8,9},{9,8},{10,11... | collective-permute-start | bytes 1572872 | tf_op jit(solution)/shard_map/ppermute | solution.py:582
  36.1 36.8 %slice-start = ((s8[4718592]{0:T(1024)(128)(4,1)}), s8[4194304]{0:T(1024)(128)(4,1)S(1)}, s32[]{:S(2)}) async-start(s8[4718592]{0:T(1024)(128)(4,1)} %bitcast.14), calls=%async_computation | async-start | bytes 8388608
  38.2 34.7 %slice-start.1 = ((s8[4718592]{0:T(1024)(128)(4,1)}), s8[524288]{0:T(1024)(128)(4,1)S(1)}, s32[]{:S(2)}) async-start(s8[4718592]{0:T(1024)(128)(4,1)} %bitcast.14), calls=%async_computation.1 | async-start | bytes 1048576
  38.2 12.0 %collective-permute-start.10 = (s16[272,768]{1,0:T(8,128)(2,1)S(1)}, s16[272,768]{1,0:T(8,128)(2,1)S(1)}, u32[]{:S(2)}, u32[]{:S(2)}) collective-permute-start(s16[272,768]{1,0:T(8,128)(2,1)S(1)} %get-tuple-element.62), channel_id=1, source_target_pairs={{0,8},{8,0},{16,24},{24,16},{1,9},{9,1},{17,25},{25,17},{2,10},{10... | collective-permute-start | bytes 1253384 | tf_op jit(solution)/shard_map/ppermute | solution.py:569
  48.6 21.6 %collective-permute-start.12 = (s16[272,768]{1,0:T(8,128)(2,1)S(1)}, s16[272,768]{1,0:T(8,128)(2,1)S(1)}, u32[]{:S(2)}, u32[]{:S(2)}) collective-permute-start(s16[272,768]{1,0:T(8,128)(2,1)S(1)} %get-tuple-element.65), channel_id=1, source_target_pairs={{0,8},{8,0},{16,24},{24,16},{1,9},{9,1},{17,25},{25,17},{2,10},{10... | collective-permute-start | bytes 1253384 | tf_op jit(solution)/shard_map/ppermute | solution.py:569
  51.0 21.8 %collective-permute-start.11 = (s16[272,768]{1,0:T(8,128)(2,1)S(1)}, s16[272,768]{1,0:T(8,128)(2,1)S(1)}, u32[]{:S(2)}, u32[]{:S(2)}) collective-permute-start(s16[272,768]{1,0:T(8,128)(2,1)S(1)} %get-tuple-element.64), channel_id=1, source_target_pairs={{1,17},{2,18},{4,20},{7,23},{9,25},{10,26},{12,28},{15,31},{16,0},... | collective-permute-start | bytes 1253384 | tf_op jit(solution)/shard_map/ppermute | solution.py:579
  55.6 2.2 %collective-permute-start.16 = (s16[144,384]{1,0:T(8,128)(2,1)S(1)}, s16[144,384]{1,0:T(8,128)(2,1)S(1)}, u32[]{:S(2)}, u32[]{:S(2)}) collective-permute-start(s16[144,384]{1,0:T(8,128)(2,1)S(1)} %get-tuple-element.72), channel_id=1, source_target_pairs={{0,4},{1,5},{6,2},{7,3},{8,12},{9,13},{14,10},{15,11},{16,20},{17,... | collective-permute-start | bytes 331784 | tf_op jit(solution)/shard_map/ppermute | solution.py:566
  58.5 6.7 %collective-permute-start.17 = (s16[144,384]{1,0:T(8,128)(2,1)S(1)}, s16[144,384]{1,0:T(8,128)(2,1)S(1)}, u32[]{:S(2)}, u32[]{:S(2)}) collective-permute-start(s16[144,384]{1,0:T(8,128)(2,1)S(1)} %pick.1.mine_ref), channel_id=1, source_target_pairs={{0,8},{8,0},{16,24},{24,16},{1,9},{9,1},{17,25},{25,17},{2,10},{10... | collective-permute-start | bytes 331784 | tf_op jit(solution)/shard_map/ppermute | solution.py:569
  65.3 7.5 %collective-permute-start.18 = (s16[144,384]{1,0:T(8,128)(2,1)S(1)}, s16[144,384]{1,0:T(8,128)(2,1)S(1)}, u32[]{:S(2)}, u32[]{:S(2)}) collective-permute-start(s16[144,384]{1,0:T(8,128)(2,1)S(1)} %add_coded.1.one_ref), channel_id=1, source_target_pairs={{0,16},{8,24},{16,0},{24,8},{1,17},{9,25},{17,1},{25,9},{2,18},{10... | collective-permute-start | bytes 331784 | tf_op jit(solution)/shard_map/ppermute | solution.py:569
  68.5 17.7 %collective-permute-start.19 = (s16[272,768]{1,0:T(8,128)(2,1)S(1)}, s16[272,768]{1,0:T(8,128)(2,1)S(1)}, u32[]{:S(2)}, u32[]{:S(2)}) collective-permute-start(s16[272,768]{1,0:T(8,128)(2,1)S(1)} %get-tuple-element.76), channel_id=1, source_target_pairs={{0,8},{8,0},{16,24},{24,16},{1,9},{9,1},{17,25},{25,17},{2,10},{10... | collective-permute-start | bytes 1253384 | tf_op jit(solution)/shard_map/ppermute | solution.py:569
  70.9 24.4 %collective-permute-start.13 = (s16[144,768]{1,0:T(8,128)(2,1)S(1)}, s16[144,768]{1,0:T(8,128)(2,1)S(1)}, u32[]{:S(2)}, u32[]{:S(2)}) collective-permute-start(s16[144,768]{1,0:T(8,128)(2,1)S(1)} %get-tuple-element.67), channel_id=1, source_target_pairs={{0,16},{1,17},{2,18},{3,19},{4,20},{5,21},{6,22},{7,23},{8,24},{9,... | collective-permute-start | bytes 663560 | tf_op jit(solution)/shard_map/ppermute | solution.py:579
  87.0 14.3 %collective-permute-start.20 = (s16[272,768]{1,0:T(8,128)(2,1)S(1)}, s16[272,768]{1,0:T(8,128)(2,1)S(1)}, u32[]{:S(2)}, u32[]{:S(2)}) collective-permute-start(s16[272,768]{1,0:T(8,128)(2,1)S(1)} %get-tuple-element.80), channel_id=1, source_target_pairs={{0,16},{3,19},{5,21},{6,22},{8,24},{11,27},{13,29},{14,30},{17,1},... | collective-permute-start | bytes 1253384 | tf_op jit(solution)/shard_map/ppermute | solution.py:579
  95.1 1.5 %collective-permute-start.21 = (f32[3,128,128]{2,1,0:T(8,128)S(1)}, f32[3,128,128]{2,1,0:T(8,128)S(1)}, u32[]{:S(2)}, u32[]{:S(2)}) collective-permute-start(f32[3,128,128]{2,1,0:T(8,128)S(1)} %factor.3.refs_6_), channel_id=1, source_target_pairs={{0,4},{4,0},{1,5},{5,1},{2,6},{6,2},{3,7},{7,3},{8,12},{12,8},{9,1... | collective-permute-start | bytes 589832 | tf_op jit(solution)/shard_map/ppermute | solution.py:623

commit v15 on v14

--- a/solution.py
+++ b/solution.py
@@ -612,10 +612,10 @@
     known = []
     mine = pick(where, diag[0], to_other_core(diag[1]))
     got0 = far_layers(sent0, chunks[0])
-    near = add_coded(mine, over_layers(mine, 1))
+    kept2, coded2 = far_part(2, mine, sent0)
+    near = add_coded(after(mine, coded2), over_layers(mine, 1))
     far = over_layers(near, 2)
     own = pivots(where, anc, given, near, after(far, got0))
-    kept2, coded2 = far_part(2, mine, sent0)
     sum1, sent1 = halve(where, kept1, over_layers(coded1, 1), chunks[1])
     half_lu = factor(after(own, sent1, coded2), 0, HALF_STEPS)
     sum2, sent2 = halve(where, after(kept2, half_lu), over_layers(coded2, 1), chunks[2])

time: 105 us -> 104 us (level)
  waiting for transfers between devices: 30.9 us -> 29.8 us
    ppermute x5, waiting for transfers between devices: 14.2 us -> 13.2 us  [over_layers(): return lax.ppermute(value, 'layer', xor_perm(layers, bit))]
  transfers between devices with their start and end apart: 22 -> 22, of which waited for: 12 -> 13; matrix products, arithmetic and copies ran while one was open for 0% -> 0% of each run, Pallas kernels for 32% -> 32%
where the time goes in v15:
time: 104 us; the launch traced here: 103 us
  Pallas kernels  35.5 us (34%)
  starting transfers between devices  30.9 us (30%)
  waiting for transfers between devices  29.8 us (29%)
  local copies, waits for them, and re-layouts  5.33 us (5%)
  between operations  1.06 us (1%)
    ppermute x10, starting transfers between devices, over(): return lax.ppermute(value, 'col', xor_perm(cols, bit))  13.9 us
    ppermute x5, waiting for transfers between devices, over_layers(): return lax.ppermute(value, 'layer', xor_perm(layers, bit))  13.2 us
    pallas_call x2, Pallas kernels, factor(): pl.pallas_call(functools.partial(lu_kernel, begin, end), out_shape=jax.Sh...  11.4 us
    ppermute x10, waiting for transfers between devices, over(): return lax.ppermute(value, 'col', xor_perm(cols, bit))  9.67 us
    ppermute x3, starting transfers between devices, far_layers(): return lax.ppermute(value, everyone, perm)  7.74 us
    ppermute x5, starting transfers between devices, over_layers(): return lax.ppermute(value, 'layer', xor_perm(layers, bit))  6.44 us
    pallas_call x3, Pallas kernels, far_update(): pl.pallas_call(functools.partial(far_kernel, chunk, blocks, len(earlier))...  6.37 us
    pallas_call x3, Pallas kernels, near_update(): pl.pallas_call(functools.partial(near_kernel, chunk, blocks), out_shape=j...  5.5 us
  transfers between devices with their start and end apart: 22, of which 13 were waited for; matrix products, arithmetic and copies ran while one was open for 0% of the time, Pallas kernels for 32%

profile of v15, /device:TPU:2, one launch (start us, length us, event | category | flops | bytes accessed | tf_op | source)
XLA Modules:
  0.0 102.5 jit_solution(8938768178096165950)
XLA Ops:
  0.7 1.4 %copy-done.1 = bf16[1,8,1536,64]{2,3,1,0:T(8,128)(2,1)S(1)} copy-done((bf16[1,8,1536,64]{2,3,1,0:T(8,128)(2,1)S(1)}, bf16[1,8,1536,64]{2,3,1,0:T(8,128)(2,1)}, u32[]{:S(2)}) %copy-start.1) | copy-done | bytes 1572888
  2.4 2.0 %collective-permute-start.3 = (bf16[4,64,1024]{2,1,0:T(8,128)(2,1)S(1)}, bf16[4,64,1024]{2,1,0:T(8,128)(2,1)S(1)}, u32[]{:S(2)}, u32[]{:S(2)}) collective-permute-start(bf16[4,64,1024]{2,1,0:T(8,128)(2,1)S(1)} %get-tuple-element.49.refs_2_), channel_id=1, source_target_pairs={{0,2},{1,3},{2,0},{3,1},{4,6},{5,7},{6,4},{7,5},{8,10},{9,11},{10,... | collective-permute-start | bytes 1572872 | tf_op jit(solution)/shard_map/ppermute | solution.py:582
  4.7 1.6 %collective-permute-start.6 = (bf16[4,64,512]{2,1,0:T(8,128)(2,1)S(1)}, bf16[4,64,512]{2,1,0:T(8,128)(2,1)S(1)}, u32[]{:S(2)}, u32[]{:S(2)}) collective-permute-start(bf16[4,64,512]{2,1,0:T(8,128)(2,1)S(1)} %get-tuple-element.45.refs_4_), channel_id=1, source_target_pairs={{0,1},{1,0},{2,3},{3,2},{4,5},{5,4},{6,7},{7,6},{8,9},{9,8},{10,11... | collective-permute-start | bytes 786440 | tf_op jit(solution)/shard_map/ppermute | solution.py:582
  6.8 2.3 %copy-done = f32[1536,768]{1,0:T(8,128)S(1)} copy-done((f32[1536,768]{1,0:T(8,128)S(1)}, f32[1536,768]{1,0:T(8,128)}, u32[]{:S(2)}) %copy-start) | copy-done | bytes 4718616
  9.8 1.3 %collective-permute-start = (f32[3,128,128]{2,1,0:T(8,128)S(1)}, f32[3,128,128]{2,1,0:T(8,128)S(1)}, u32[]{:S(2)}, u32[]{:S(2)}) collective-permute-start(f32[3,128,128]{2,1,0:T(8,128)S(1)} %later_blocks.1), channel_id=1, source_target_pairs={{0,4},{1,5},{6,2},{7,3},{8,12},{9,13},{14,10},{15,11},{16,20},{17,... | collective-permute-start | bytes 589832 | tf_op jit(solution)/shard_map/ppermute | solution.py:566
  11.2 1.4 %copy-done.2 = bf16[1,8,128,768]{3,2,1,0:T(8,128)(2,1)S(1)} copy-done((bf16[1,8,128,768]{3,2,1,0:T(8,128)(2,1)S(1)}, bf16[1,8,128,768]{3,2,1,0:T(8,128)(2,1)}, u32[]{:S(2)}) %copy-start.2) | copy-done | bytes 1572888
  12.6 2.2 %masked_right.1 = (bf16[8,128,768]{2,1,0:T(8,128)(2,1)S(1)}, bf16[8,128,768]{2,1,0:T(8,128)(2,1)S(1)}) custom-call(s32[8]{0:T(128)S(1)} %stack.35.where_ref, s32[8,6]{1,0:T(8,128)S(1)} %bitcast.26, bf16[8,128,768]{2,1,0:T(8,128)(2,1)S(1)} %bitcast.19, bf16[8,128,768]{2,1,0:T(8,128)(2,1)} %collective-permute-done.1.uo_ref), custom_call_target="tpu_custom_call" | custom-call | flops 1000 | bytes 1000 | tf_op jit(solution)/shard_map/masked_right/pallas_call | solution.py:226
  14.8 2.4 %collective-permute-done.2.refs_1_ = bf16[4,64,1024]{2,1,0:T(8,128)(2,1)S(1)} collective-permute-done((bf16[4,64,1024]{2,1,0:T(8,128)(2,1)S(1)}, bf16[4,64,1024]{2,1,0:T(8,128)(2,1)S(1)}, u32[]{:S(2)}, u32[]{:S(2)}) %collective-permute-start.2) | collective-permute-done | bytes 524320 | tf_op jit(solution)/shard_map/ppermute | solution.py:582
  17.2 1.0 split.3
  18.2 2.1 %collective-permute-start.4 = (bf16[2,4,64,512]{3,2,1,0:T(8,128)(2,1)S(1)}, bf16[2,4,64,512]{3,2,1,0:T(8,128)(2,1)S(1)}, u32[]{:S(2)}, u32[]{:S(2)}) collective-permute-start(bf16[2,4,64,512]{3,2,1,0:T(8,128)(2,1)S(1)} %get-tuple-element.50), channel_id=1, source_target_pairs={{0,2},{1,3},{2,0},{3,1},{4,6},{5,7},{6,4},{7,5},{8,10},{9,11},{10,... | collective-permute-start | bytes 1572872 | tf_op jit(solution)/shard_map/ppermute | solution.py:582
  20.3 1.5 %collective-permute-start.5 = (bf16[2,4,64,512]{3,2,1,0:T(8,128)(2,1)S(1)}, bf16[2,4,64,512]{3,2,1,0:T(8,128)(2,1)S(1)}, u32[]{:S(2)}, u32[]{:S(2)}) collective-permute-start(bf16[2,4,64,512]{3,2,1,0:T(8,128)(2,1)S(1)} %get-tuple-element.51), channel_id=1, source_target_pairs={{0,1},{1,0},{2,3},{3,2},{4,5},{5,4},{6,7},{7,6},{8,9},{9,8},{10,11... | collective-permute-start | bytes 1572872 | tf_op jit(solution)/shard_map/ppermute | solution.py:582
  21.8 1.0 collective-permute-done.6.refs_5_
  22.8 1.0 split.4
  23.8 2.1 %collective-permute-start.8 = (bf16[2,4,64,512]{3,2,1,0:T(8,128)(2,1)S(1)}, bf16[2,4,64,512]{3,2,1,0:T(8,128)(2,1)S(1)}, u32[]{:S(2)}, u32[]{:S(2)}) collective-permute-start(bf16[2,4,64,512]{3,2,1,0:T(8,128)(2,1)S(1)} %get-tuple-element.56), channel_id=1, source_target_pairs={{0,2},{1,3},{2,0},{3,1},{4,6},{5,7},{6,4},{7,5},{8,10},{9,11},{10,... | collective-permute-start | bytes 1572872 | tf_op jit(solution)/shard_map/ppermute | solution.py:582
  25.9 1.5 %collective-permute-start.9 = (bf16[2,4,64,512]{3,2,1,0:T(8,128)(2,1)S(1)}, bf16[2,4,64,512]{3,2,1,0:T(8,128)(2,1)S(1)}, u32[]{:S(2)}, u32[]{:S(2)}) collective-permute-start(bf16[2,4,64,512]{3,2,1,0:T(8,128)(2,1)S(1)} %get-tuple-element.57), channel_id=1, source_target_pairs={{0,1},{1,0},{2,3},{3,2},{4,5},{5,4},{6,7},{7,6},{8,9},{9,8},{10,11... | collective-permute-start | bytes 1572872 | tf_op jit(solution)/shard_map/ppermute | solution.py:582
  27.4 1.0 split.5
  28.9 1.8 %near_update.5.refs_1_ = f32[4,128,768]{2,1,0:T(8,128)S(1)} custom-call(s32[8]{0:T(128)S(1)} %stack.35.where_ref, s32[8,12]{1,0:T(8,128)S(1)} %bitcast.20, bf16[4,64,1024]{2,1,0:T(8,128)(2,1)S(1)} %get-tuple-element.43.refs_0_, bf16[4,64,1024]{2,1,0:T(8,128)(2,1)S(1)} %collective-permute-done.2.refs_1_, bf16[4,64,1024]{2,1,0:T(8,128)(2,1)S(1)} %get-tuple-element.49.refs_2_, ...), custom_call_target="tpu_custom_call" | custom-call | flops 10000001024 | bytes 1000 | tf_op jit(solution)/shard_map/near_update/pallas_call | solution.py:273
  30.7 1.9 %near_update.3.refs_1_ = f32[4,128,768]{2,1,0:T(8,128)S(1)} custom-call(s32[8]{0:T(128)S(1)} %stack.35.where_ref, s32[8,12]{1,0:T(8,128)S(1)} %bitcast.21, bf16[4,64,1024]{2,1,0:T(8,128)(2,1)S(1)} %get-tuple-element.43.refs_0_, bf16[4,64,1024]{2,1,0:T(8,128)(2,1)S(1)} %collective-permute-done.2.refs_1_, bf16[4,64,1024]{2,1,0:T(8,128)(2,1)S(1)} %get-tuple-element.49.refs_2_, ...), custom_call_target="tpu_custom_call" | custom-call | flops 10000001024 | bytes 1000 | tf_op jit(solution)/shard_map/near_update/pallas_call | solution.py:273
  32.6 1.5 %collective-permute-done.4.a_ref = bf16[2,4,64,512]{3,2,1,0:T(8,128)(2,1)S(1)} collective-permute-done((bf16[2,4,64,512]{3,2,1,0:T(8,128)(2,1)S(1)}, bf16[2,4,64,512]{3,2,1,0:T(8,128)(2,1)S(1)}, u32[]{:S(2)}, u32[]{:S(2)}) %collective-permute-start.4) | collective-permute-done | bytes 524320 | tf_op jit(solution)/shard_map/ppermute | solution.py:582
  34.1 2.0 %collective-permute-start.15 = (bf16[2,4,64,512]{3,2,1,0:T(8,128)(2,1)S(1)}, bf16[2,4,64,512]{3,2,1,0:T(8,128)(2,1)S(1)}, u32[]{:S(2)}, u32[]{:S(2)}) collective-permute-start(bf16[2,4,64,512]{3,2,1,0:T(8,128)(2,1)S(1)} %get-tuple-element.71), channel_id=1, source_target_pairs={{0,1},{1,0},{2,3},{3,2},{4,5},{5,4},{6,7},{7,6},{8,9},{9,8},{10,11... | collective-permute-start | bytes 1572872 | tf_op jit(solution)/shard_map/ppermute | solution.py:582
  36.1 2.1 %far_update.3 = (f32[2,128,768]{2,1,0:T(8,128)S(1)}, s16[272,768]{1,0:T(8,128)(2,1)S(1)}, s16[144,384]{1,0:T(8,128)(2,1)S(1)}, s16[144,384]{1,0:T(8,128)(2,1)S(1)}) custom-call(s32[8]{0:T(128)S(1)} %stack.35.where_ref, s32[8,12]{1,0:T(8,128)S(1)} %bitcast.22, bf16[2,4,64,512]{3,2,1,0:T(8,128)(2,1)S(1)} %collective-permute-done.4.a_ref, ...), custom_call_target="tpu_custom_call" | custom-call | flops 1000001024 | bytes 1000 | tf_op jit(solution)/shard_map/far_update/pallas_call | solution.py:322
  38.2 1.7 %collective-permute-start.10 = (s16[272,768]{1,0:T(8,128)(2,1)S(1)}, s16[272,768]{1,0:T(8,128)(2,1)S(1)}, u32[]{:S(2)}, u32[]{:S(2)}) collective-permute-start(s16[272,768]{1,0:T(8,128)(2,1)S(1)} %get-tuple-element.63), channel_id=1, source_target_pairs={{0,8},{8,0},{16,24},{24,16},{1,9},{9,1},{17,25},{25,17},{2,10},{10... | collective-permute-start | bytes 1253384 | tf_op jit(solution)/shard_map/ppermute | solution.py:569
  39.8 1.8 %near_update.4.refs_1_ = f32[4,128,768]{2,1,0:T(8,128)S(1)} custom-call(s32[8]{0:T(128)S(1)} %stack.35.where_ref, s32[8,12]{1,0:T(8,128)S(1)} %bitcast.23, bf16[4,64,1024]{2,1,0:T(8,128)(2,1)S(1)} %get-tuple-element.43.refs_0_, bf16[4,64,1024]{2,1,0:T(8,128)(2,1)S(1)} %collective-permute-done.2.refs_1_, bf16[4,64,1024]{2,1,0:T(8,128)(2,1)S(1)} %get-tuple-element.49.refs_2_, ...), custom_call_target="tpu_custom_call" | custom-call | flops 10000001024 | bytes 1000 | tf_op jit(solution)/shard_map/near_update/pallas_call | solution.py:273
  41.7 3.6 %collective-permute-done.8.a_ref = bf16[2,4,64,512]{3,2,1,0:T(8,128)(2,1)S(1)} collective-permute-done((bf16[2,4,64,512]{3,2,1,0:T(8,128)(2,1)S(1)}, bf16[2,4,64,512]{3,2,1,0:T(8,128)(2,1)S(1)}, u32[]{:S(2)}, u32[]{:S(2)}) %collective-permute-start.8) | collective-permute-done | bytes 524320 | tf_op jit(solution)/shard_map/ppermute | solution.py:582
  45.3 1.1 %collective-permute-done.9.b_ref = bf16[2,4,64,512]{3,2,1,0:T(8,128)(2,1)S(1)} collective-permute-done((bf16[2,4,64,512]{3,2,1,0:T(8,128)(2,1)S(1)}, bf16[2,4,64,512]{3,2,1,0:T(8,128)(2,1)S(1)}, u32[]{:S(2)}, u32[]{:S(2)}) %collective-permute-start.9) | collective-permute-done | bytes 524320 | tf_op jit(solution)/shard_map/ppermute | solution.py:582
  46.4 2.1 %far_update.4 = (f32[2,128,768]{2,1,0:T(8,128)S(1)}, s16[272,768]{1,0:T(8,128)(2,1)S(1)}, s16[144,384]{1,0:T(8,128)(2,1)S(1)}, s16[144,384]{1,0:T(8,128)(2,1)S(1)}) custom-call(s32[8]{0:T(128)S(1)} %stack.35.where_ref, s32[8,12]{1,0:T(8,128)S(1)} %bitcast.24, bf16[2,4,64,512]{3,2,1,0:T(8,128)(2,1)S(1)} %collective-permute-done.8.a_ref, ...), custom_call_target="tpu_custom_call" | custom-call | flops 1000001024 | bytes 1000 | tf_op jit(solution)/shard_map/far_update/pallas_call | solution.py:322
  48.6 1.7 %collective-permute-start.12 = (s16[272,768]{1,0:T(8,128)(2,1)S(1)}, s16[272,768]{1,0:T(8,128)(2,1)S(1)}, u32[]{:S(2)}, u32[]{:S(2)}) collective-permute-start(s16[272,768]{1,0:T(8,128)(2,1)S(1)} %get-tuple-element.66), channel_id=1, source_target_pairs={{0,8},{8,0},{16,24},{24,16},{1,9},{9,1},{17,25},{25,17},{2,10},{10... | collective-permute-start | bytes 1253384 | tf_op jit(solution)/shard_map/ppermute | solution.py:569
  50.2 0.8 halve.3
  51.0 4.5 %collective-permute-start.11 = (s16[272,768]{1,0:T(8,128)(2,1)S(1)}, s16[272,768]{1,0:T(8,128)(2,1)S(1)}, u32[]{:S(2)}, u32[]{:S(2)}) collective-permute-start(s16[272,768]{1,0:T(8,128)(2,1)S(1)} %get-tuple-element.65), channel_id=1, source_target_pairs={{1,17},{2,18},{4,20},{7,23},{9,25},{10,26},{12,28},{15,31},{16,0},... | collective-permute-start | bytes 1253384 | tf_op jit(solution)/shard_map/ppermute | solution.py:579
  55.6 1.3 %collective-permute-start.16 = (s16[144,384]{1,0:T(8,128)(2,1)S(1)}, s16[144,384]{1,0:T(8,128)(2,1)S(1)}, u32[]{:S(2)}, u32[]{:S(2)}) collective-permute-start(s16[144,384]{1,0:T(8,128)(2,1)S(1)} %get-tuple-element.73), channel_id=1, source_target_pairs={{0,4},{1,5},{6,2},{7,3},{8,12},{9,13},{14,10},{15,11},{16,20},{17,... | collective-permute-start | bytes 331784 | tf_op jit(solution)/shard_map/ppermute | solution.py:566
  56.9 0.9 collective-permute-done.16.got_ref
  57.8 0.7 pick.1.mine_ref
  59.1 2.1 %far_update.5 = (f32[2,128,768]{2,1,0:T(8,128)S(1)}, s16[272,768]{1,0:T(8,128)(2,1)S(1)}) custom-call(s32[8]{0:T(128)S(1)} %stack.35.where_ref, s32[8,12]{1,0:T(8,128)S(1)} %bitcast.25, bf16[2,4,64,512]{3,2,1,0:T(8,128)(2,1)S(1)} %collective-permute-done.14.a_ref, bf16[2,4,64,512]{3,2,1,0:T(8,128)(2,1)S(1)} %collective-permute-done.15.b_ref, ...), custom_call_target="tpu_custom_call" | custom-call | flops 1000001024 | bytes 1000 | tf_op jit(solution)/shard_map/far_update/pallas_call | solution.py:322
  61.2 4.0 %collective-permute-done.17.got_ref = s16[144,384]{1,0:T(8,128)(2,1)S(1)} collective-permute-done((s16[144,384]{1,0:T(8,128)(2,1)S(1)}, s16[144,384]{1,0:T(8,128)(2,1)S(1)}, u32[]{:S(2)}, u32[]{:S(2)}) %collective-permute-start.17) | collective-permute-done | bytes 110624 | tf_op jit(solution)/shard_map/ppermute | solution.py:569
  65.3 1.0 collective-permute-start.18
  66.3 1.6 %collective-permute-start.19 = (s16[272,768]{1,0:T(8,128)(2,1)S(1)}, s16[272,768]{1,0:T(8,128)(2,1)S(1)}, u32[]{:S(2)}, u32[]{:S(2)}) collective-permute-start(s16[272,768]{1,0:T(8,128)(2,1)S(1)} %get-tuple-element.76), channel_id=1, source_target_pairs={{0,8},{8,0},{16,24},{24,16},{1,9},{9,1},{17,25},{25,17},{2,10},{10... | collective-permute-start | bytes 1253384 | tf_op jit(solution)/shard_map/ppermute | solution.py:569
  68.0 0.7 halve.4
  68.7 1.9 %collective-permute-start.13 = (s16[144,768]{1,0:T(8,128)(2,1)S(1)}, s16[144,768]{1,0:T(8,128)(2,1)S(1)}, u32[]{:S(2)}, u32[]{:S(2)}) collective-permute-start(s16[144,768]{1,0:T(8,128)(2,1)S(1)} %get-tuple-element.68), channel_id=1, source_target_pairs={{0,16},{1,17},{2,18},{3,19},{4,20},{5,21},{6,22},{7,23},{8,24},{9,... | collective-permute-start | bytes 663560 | tf_op jit(solution)/shard_map/ppermute | solution.py:579
  70.6 1.3 %collective-permute-done.18.two_ref = s16[144,384]{1,0:T(8,128)(2,1)S(1)} collective-permute-done((s16[144,384]{1,0:T(8,128)(2,1)S(1)}, s16[144,384]{1,0:T(8,128)(2,1)S(1)}, u32[]{:S(2)}, u32[]{:S(2)}) %collective-permute-start.18) | collective-permute-done | bytes 110624 | tf_op jit(solution)/shard_map/ppermute | solution.py:569
  72.0 0.7 pivots.1.in_ref
  72.7 4.6 %factor.2.in_ref = f32[3,128,128]{2,1,0:T(8,128)S(1)} custom-call(f32[3,128,128]{2,1,0:T(8,128)S(1)} %pivots.1.in_ref), custom_call_target="tpu_custom_call" | custom-call | flops 10000001024 | bytes 1000 | tf_op jit(solution)/shard_map/factor/pallas_call | solution.py:82
  77.3 7.8 %collective-permute-done.19.got_ref = s16[272,768]{1,0:T(8,128)(2,1)S(1)} collective-permute-done((s16[272,768]{1,0:T(8,128)(2,1)S(1)}, s16[272,768]{1,0:T(8,128)(2,1)S(1)}, u32[]{:S(2)}, u32[]{:S(2)}) %collective-permute-start.19) | collective-permute-done | bytes 417824 | tf_op jit(solution)/shard_map/ppermute | solution.py:569
  85.0 0.8 halve.5
  85.8 1.3 %collective-permute-start.20 = (s16[272,768]{1,0:T(8,128)(2,1)S(1)}, s16[272,768]{1,0:T(8,128)(2,1)S(1)}, u32[]{:S(2)}, u32[]{:S(2)}) collective-permute-start(s16[272,768]{1,0:T(8,128)(2,1)S(1)} %get-tuple-element.82), channel_id=1, source_target_pairs={{0,16},{3,19},{5,21},{6,22},{8,24},{11,27},{13,29},{14,30},{17,1},... | collective-permute-start | bytes 1253384 | tf_op jit(solution)/shard_map/ppermute | solution.py:579
  87.1 6.8 %factor.3.refs_6_ = f32[3,128,128]{2,1,0:T(8,128)S(1)} custom-call(f32[3,128,128]{2,1,0:T(8,128)S(1)} %factor.2.in_ref), custom_call_target="tpu_custom_call" | custom-call | flops 10000001024 | bytes 1000 | tf_op jit(solution)/shard_map/factor/pallas_call | solution.py:82
  94.1 1.3 %collective-permute-done.21.refs_7_ = f32[3,128,128]{2,1,0:T(8,128)S(1)} collective-permute-done((f32[3,128,128]{2,1,0:T(8,128)S(1)}, f32[3,128,128]{2,1,0:T(8,128)S(1)}, u32[]{:S(2)}, u32[]{:S(2)}) %collective-permute-start.21) | collective-permute-done | bytes 196640 | tf_op jit(solution)/shard_map/ppermute | solution.py:623
  95.4 4.7 %collective-permute-done.20.refs_5_ = s16[272,768]{1,0:T(8,128)(2,1)S(1)} collective-permute-done((s16[272,768]{1,0:T(8,128)(2,1)S(1)}, s16[272,768]{1,0:T(8,128)(2,1)S(1)}, u32[]{:S(2)}, u32[]{:S(2)}) %collective-permute-start.20) | collective-permute-done | bytes 417824 | tf_op jit(solution)/shard_map/ppermute | solution.py:579
  100.1 2.2 %combine.1 = (f32[384,768]{1,0:T(8,128)}, f32[6,128,128]{2,1,0:T(8,128)}) custom-call(s32[8]{0:T(128)S(1)} %stack.35.where_ref, f32[1536,768]{1,0:T(8,128)S(1)} %bitcast.15, f32[2,128,768]{2,1,0:T(8,128)S(1)} %get-tuple-element.64.refs_0_, s16[272,768]{1,0:T(8,128)(2,1)S(1)} %collective-permute-done.11.refs_1_, ...), custom_call_target="tpu_custom_call" | custom-call | flops 1000 | bytes 1000 | tf_op jit(solution)/shard_map/combine/pallas_call | solution.py:457
  (35 shorter events, 3.4 us)
Async XLA Ops:
  0.6 9.1 %collective-permute-start.1 = (bf16[8,128,768]{2,1,0:T(8,128)(2,1)}, bf16[8,128,768]{2,1,0:T(8,128)(2,1)}, u32[]{:S(2)}, u32[]{:S(2)}) collective-permute-start(bf16[8,128,768]{2,1,0:T(8,128)(2,1)} %bitcast.18), channel_id=1, source_target_pairs={{0,4},{4,0},{1,5},{5,1},{2,6},{6,2},{3,7},{7,3},{8,12},{12,8},{9,1... | collective-permute-start | bytes 4718600 | tf_op jit(solution)/shard_map/ppermute | solution.py:587
  0.7 1.4 %copy-start.1 = (bf16[1,8,1536,64]{2,3,1,0:T(8,128)(2,1)S(1)}, bf16[1,8,1536,64]{2,3,1,0:T(8,128)(2,1)}, u32[]{:S(2)}) copy-start(bf16[1,8,1536,64]{2,3,1,0:T(8,128)(2,1)} %param.5) | copy-start | bytes 4718596
  2.4 14.8 %collective-permute-start.2 = (bf16[4,64,1024]{2,1,0:T(8,128)(2,1)S(1)}, bf16[4,64,1024]{2,1,0:T(8,128)(2,1)S(1)}, u32[]{:S(2)}, u32[]{:S(2)}) collective-permute-start(bf16[4,64,1024]{2,1,0:T(8,128)(2,1)S(1)} %get-tuple-element.43.refs_0_), channel_id=1, source_target_pairs={{0,1},{1,0},{2,3},{3,2},{4,5},{5,4},{6,7},{7,6},{8,9},{9,8},{10,11... | collective-permute-start | bytes 1572872 | tf_op jit(solution)/shard_map/ppermute | solution.py:582
  2.4 14.8 %collective-permute-start.3 = (bf16[4,64,1024]{2,1,0:T(8,128)(2,1)S(1)}, bf16[4,64,1024]{2,1,0:T(8,128)(2,1)S(1)}, u32[]{:S(2)}, u32[]{:S(2)}) collective-permute-start(bf16[4,64,1024]{2,1,0:T(8,128)(2,1)S(1)} %get-tuple-element.49.refs_2_), channel_id=1, source_target_pairs={{0,2},{1,3},{2,0},{3,1},{4,6},{5,7},{6,4},{7,5},{8,10},{9,11},{10,... | collective-permute-start | bytes 1572872 | tf_op jit(solution)/shard_map/ppermute | solution.py:582
  4.7 18.1 %collective-permute-start.6 = (bf16[4,64,512]{2,1,0:T(8,128)(2,1)S(1)}, bf16[4,64,512]{2,1,0:T(8,128)(2,1)S(1)}, u32[]{:S(2)}, u32[]{:S(2)}) collective-permute-start(bf16[4,64,512]{2,1,0:T(8,128)(2,1)S(1)} %get-tuple-element.45.refs_4_), channel_id=1, source_target_pairs={{0,1},{1,0},{2,3},{3,2},{4,5},{5,4},{6,7},{7,6},{8,9},{9,8},{10,11... | collective-permute-start | bytes 786440 | tf_op jit(solution)/shard_map/ppermute | solution.py:582
  6.2 16.6 %collective-permute-start.7 = (bf16[4,64,512]{2,1,0:T(8,128)(2,1)S(1)}, bf16[4,64,512]{2,1,0:T(8,128)(2,1)S(1)}, u32[]{:S(2)}, u32[]{:S(2)}) collective-permute-start(bf16[4,64,512]{2,1,0:T(8,128)(2,1)S(1)} %get-tuple-element.55.refs_6_), channel_id=1, source_target_pairs={{0,2},{1,3},{2,0},{3,1},{4,6},{5,7},{6,4},{7,5},{8,10},{9,11},{10,... | collective-permute-start | bytes 786440 | tf_op jit(solution)/shard_map/ppermute | solution.py:582
  6.8 2.3 %copy-start = (f32[1536,768]{1,0:T(8,128)S(1)}, f32[1536,768]{1,0:T(8,128)}, u32[]{:S(2)}) copy-start(f32[1536,768]{1,0:T(8,128)} %anc_ref.4) | copy-start | bytes 14155780
  9.1 1.9 %copy-start.4 = (s32[1,8,6]{1,0,2:T(1,128)S(1)}, s32[1,8,6]{1,0,2:T(1,128)}, u32[]{:S(2)}) copy-start(s32[1,8,6]{1,0,2:T(1,128)} %param.8) | copy-start | bytes 580
  9.8 5.0 %collective-permute-start = (f32[3,128,128]{2,1,0:T(8,128)S(1)}, f32[3,128,128]{2,1,0:T(8,128)S(1)}, u32[]{:S(2)}, u32[]{:S(2)}) collective-permute-start(f32[3,128,128]{2,1,0:T(8,128)S(1)} %later_blocks.1), channel_id=1, source_target_pairs={{0,4},{1,5},{6,2},{7,3},{8,12},{9,13},{14,10},{15,11},{16,20},{17,... | collective-permute-start | bytes 589832 | tf_op jit(solution)/shard_map/ppermute | solution.py:566
  11.2 1.4 %copy-start.2 = (bf16[1,8,128,768]{3,2,1,0:T(8,128)(2,1)S(1)}, bf16[1,8,128,768]{3,2,1,0:T(8,128)(2,1)}, u32[]{:S(2)}) copy-start(bf16[1,8,128,768]{3,2,1,0:T(8,128)(2,1)} %param.6) | copy-start | bytes 4718596
  18.2 15.8 %collective-permute-start.4 = (bf16[2,4,64,512]{3,2,1,0:T(8,128)(2,1)S(1)}, bf16[2,4,64,512]{3,2,1,0:T(8,128)(2,1)S(1)}, u32[]{:S(2)}, u32[]{:S(2)}) collective-permute-start(bf16[2,4,64,512]{3,2,1,0:T(8,128)(2,1)S(1)} %get-tuple-element.50), channel_id=1, source_target_pairs={{0,2},{1,3},{2,0},{3,1},{4,6},{5,7},{6,4},{7,5},{8,10},{9,11},{10,... | collective-permute-start | bytes 1572872 | tf_op jit(solution)/shard_map/ppermute | solution.py:582
  20.3 15.8 %collective-permute-start.5 = (bf16[2,4,64,512]{3,2,1,0:T(8,128)(2,1)S(1)}, bf16[2,4,64,512]{3,2,1,0:T(8,128)(2,1)S(1)}, u32[]{:S(2)}, u32[]{:S(2)}) collective-permute-start(bf16[2,4,64,512]{3,2,1,0:T(8,128)(2,1)S(1)} %get-tuple-element.51), channel_id=1, source_target_pairs={{0,1},{1,0},{2,3},{3,2},{4,5},{5,4},{6,7},{7,6},{8,9},{9,8},{10,11... | collective-permute-start | bytes 1572872 | tf_op jit(solution)/shard_map/ppermute | solution.py:582
  23.8 21.5 %collective-permute-start.8 = (bf16[2,4,64,512]{3,2,1,0:T(8,128)(2,1)S(1)}, bf16[2,4,64,512]{3,2,1,0:T(8,128)(2,1)S(1)}, u32[]{:S(2)}, u32[]{:S(2)}) collective-permute-start(bf16[2,4,64,512]{3,2,1,0:T(8,128)(2,1)S(1)} %get-tuple-element.56), channel_id=1, source_target_pairs={{0,2},{1,3},{2,0},{3,1},{4,6},{5,7},{6,4},{7,5},{8,10},{9,11},{10,... | collective-permute-start | bytes 1572872 | tf_op jit(solution)/shard_map/ppermute | solution.py:582
  25.9 3.0 %copy-start.3 = (s32[1,8,12]{2,1,0:T(8,128)S(1)}, s32[1,8,12]{2,1,0:T(8,128)}, u32[]{:S(2)}) copy-start(s32[1,8,12]{2,1,0:T(8,128)} %param.7) | copy-start | bytes 1156
  25.9 20.5 %collective-permute-start.9 = (bf16[2,4,64,512]{3,2,1,0:T(8,128)(2,1)S(1)}, bf16[2,4,64,512]{3,2,1,0:T(8,128)(2,1)S(1)}, u32[]{:S(2)}, u32[]{:S(2)}) collective-permute-start(bf16[2,4,64,512]{3,2,1,0:T(8,128)(2,1)S(1)} %get-tuple-element.57), channel_id=1, source_target_pairs={{0,1},{1,0},{2,3},{3,2},{4,5},{5,4},{6,7},{7,6},{8,9},{9,8},{10,11... | collective-permute-start | bytes 1572872 | tf_op jit(solution)/shard_map/ppermute | solution.py:582
  28.3 30.7 %collective-permute-start.14 = (bf16[2,4,64,512]{3,2,1,0:T(8,128)(2,1)S(1)}, bf16[2,4,64,512]{3,2,1,0:T(8,128)(2,1)S(1)}, u32[]{:S(2)}, u32[]{:S(2)}) collective-permute-start(bf16[2,4,64,512]{3,2,1,0:T(8,128)(2,1)S(1)} %get-tuple-element.70), channel_id=1, source_target_pairs={{0,2},{1,3},{2,0},{3,1},{4,6},{5,7},{6,4},{7,5},{8,10},{9,11},{10,... | collective-permute-start | bytes 1572872 | tf_op jit(solution)/shard_map/ppermute | solution.py:582
  34.1 25.0 %collective-permute-start.15 = (bf16[2,4,64,512]{3,2,1,0:T(8,128)(2,1)S(1)}, bf16[2,4,64,512]{3,2,1,0:T(8,128)(2,1)S(1)}, u32[]{:S(2)}, u32[]{:S(2)}) collective-permute-start(bf16[2,4,64,512]{3,2,1,0:T(8,128)(2,1)S(1)} %get-tuple-element.71), channel_id=1, source_target_pairs={{0,1},{1,0},{2,3},{3,2},{4,5},{5,4},{6,7},{7,6},{8,9},{9,8},{10,11... | collective-permute-start | bytes 1572872 | tf_op jit(solution)/shard_map/ppermute | solution.py:582
  36.1 35.9 %slice-start = ((s8[4718592]{0:T(1024)(128)(4,1)}), s8[4194304]{0:T(1024)(128)(4,1)S(1)}, s32[]{:S(2)}) async-start(s8[4718592]{0:T(1024)(128)(4,1)} %bitcast.14), calls=%async_computation | async-start | bytes 8388608
  38.2 33.8 %slice-start.1 = ((s8[4718592]{0:T(1024)(128)(4,1)}), s8[524288]{0:T(1024)(128)(4,1)S(1)}, s32[]{:S(2)}) async-start(s8[4718592]{0:T(1024)(128)(4,1)} %bitcast.14), calls=%async_computation.1 | async-start | bytes 1048576
  38.2 12.0 %collective-permute-start.10 = (s16[272,768]{1,0:T(8,128)(2,1)S(1)}, s16[272,768]{1,0:T(8,128)(2,1)S(1)}, u32[]{:S(2)}, u32[]{:S(2)}) collective-permute-start(s16[272,768]{1,0:T(8,128)(2,1)S(1)} %get-tuple-element.63), channel_id=1, source_target_pairs={{0,8},{8,0},{16,24},{24,16},{1,9},{9,1},{17,25},{25,17},{2,10},{10... | collective-permute-start | bytes 1253384 | tf_op jit(solution)/shard_map/ppermute | solution.py:569
  48.6 19.4 %collective-permute-start.12 = (s16[272,768]{1,0:T(8,128)(2,1)S(1)}, s16[272,768]{1,0:T(8,128)(2,1)S(1)}, u32[]{:S(2)}, u32[]{:S(2)}) collective-permute-start(s16[272,768]{1,0:T(8,128)(2,1)S(1)} %get-tuple-element.66), channel_id=1, source_target_pairs={{0,8},{8,0},{16,24},{24,16},{1,9},{9,1},{17,25},{25,17},{2,10},{10... | collective-permute-start | bytes 1253384 | tf_op jit(solution)/shard_map/ppermute | solution.py:569
  51.0 21.0 %collective-permute-start.11 = (s16[272,768]{1,0:T(8,128)(2,1)S(1)}, s16[272,768]{1,0:T(8,128)(2,1)S(1)}, u32[]{:S(2)}, u32[]{:S(2)}) collective-permute-start(s16[272,768]{1,0:T(8,128)(2,1)S(1)} %get-tuple-element.65), channel_id=1, source_target_pairs={{1,17},{2,18},{4,20},{7,23},{9,25},{10,26},{12,28},{15,31},{16,0},... | collective-permute-start | bytes 1253384 | tf_op jit(solution)/shard_map/ppermute | solution.py:579
  55.6 2.2 %collective-permute-start.16 = (s16[144,384]{1,0:T(8,128)(2,1)S(1)}, s16[144,384]{1,0:T(8,128)(2,1)S(1)}, u32[]{:S(2)}, u32[]{:S(2)}) collective-permute-start(s16[144,384]{1,0:T(8,128)(2,1)S(1)} %get-tuple-element.73), channel_id=1, source_target_pairs={{0,4},{1,5},{6,2},{7,3},{8,12},{9,13},{14,10},{15,11},{16,20},{17,... | collective-permute-start | bytes 331784 | tf_op jit(solution)/shard_map/ppermute | solution.py:566
  58.5 6.7 %collective-permute-start.17 = (s16[144,384]{1,0:T(8,128)(2,1)S(1)}, s16[144,384]{1,0:T(8,128)(2,1)S(1)}, u32[]{:S(2)}, u32[]{:S(2)}) collective-permute-start(s16[144,384]{1,0:T(8,128)(2,1)S(1)} %pick.1.mine_ref), channel_id=1, source_target_pairs={{0,8},{8,0},{16,24},{24,16},{1,9},{9,1},{17,25},{25,17},{2,10},{10... | collective-permute-start | bytes 331784 | tf_op jit(solution)/shard_map/ppermute | solution.py:569
  65.3 6.6 %collective-permute-start.18 = (s16[144,384]{1,0:T(8,128)(2,1)S(1)}, s16[144,384]{1,0:T(8,128)(2,1)S(1)}, u32[]{:S(2)}, u32[]{:S(2)}) collective-permute-start(s16[144,384]{1,0:T(8,128)(2,1)S(1)} %add_coded.1.one_ref), channel_id=1, source_target_pairs={{0,16},{8,24},{16,0},{24,8},{1,17},{9,25},{17,1},{25,9},{2,18},{10... | collective-permute-start | bytes 331784 | tf_op jit(solution)/shard_map/ppermute | solution.py:569
  66.3 18.7 %collective-permute-start.19 = (s16[272,768]{1,0:T(8,128)(2,1)S(1)}, s16[272,768]{1,0:T(8,128)(2,1)S(1)}, u32[]{:S(2)}, u32[]{:S(2)}) collective-permute-start(s16[272,768]{1,0:T(8,128)(2,1)S(1)} %get-tuple-element.76), channel_id=1, source_target_pairs={{0,8},{8,0},{16,24},{24,16},{1,9},{9,1},{17,25},{25,17},{2,10},{10... | collective-permute-start | bytes 1253384 | tf_op jit(solution)/shard_map/ppermute | solution.py:569
  68.7 25.4 %collective-permute-start.13 = (s16[144,768]{1,0:T(8,128)(2,1)S(1)}, s16[144,768]{1,0:T(8,128)(2,1)S(1)}, u32[]{:S(2)}, u32[]{:S(2)}) collective-permute-start(s16[144,768]{1,0:T(8,128)(2,1)S(1)} %get-tuple-element.68), channel_id=1, source_target_pairs={{0,16},{1,17},{2,18},{3,19},{4,20},{5,21},{6,22},{7,23},{8,24},{9,... | collective-permute-start | bytes 663560 | tf_op jit(solution)/shard_map/ppermute | solution.py:579
  85.8 14.3 %collective-permute-start.20 = (s16[272,768]{1,0:T(8,128)(2,1)S(1)}, s16[272,768]{1,0:T(8,128)(2,1)S(1)}, u32[]{:S(2)}, u32[]{:S(2)}) collective-permute-start(s16[272,768]{1,0:T(8,128)(2,1)S(1)} %get-tuple-element.82), channel_id=1, source_target_pairs={{0,16},{3,19},{5,21},{6,22},{8,24},{11,27},{13,29},{14,30},{17,1},... | collective-permute-start | bytes 1253384 | tf_op jit(solution)/shard_map/ppermute | solution.py:579
  94.0 1.5 %collective-permute-start.21 = (f32[3,128,128]{2,1,0:T(8,128)S(1)}, f32[3,128,128]{2,1,0:T(8,128)S(1)}, u32[]{:S(2)}, u32[]{:S(2)}) collective-permute-start(f32[3,128,128]{2,1,0:T(8,128)S(1)} %factor.3.refs_6_), channel_id=1, source_target_pairs={{0,4},{4,0},{1,5},{5,1},{2,6},{6,2},{3,7},{7,3},{8,12},{12,8},{9,1... | collective-permute-start | bytes 589832 | tf_op jit(solution)/shard_map/ppermute | solution.py:623
